TPU v7x, 32 devices: a whole 2x2x4 slice. The times are simulated.
32 devices in a mesh: hst: 8 (over z, y), grp: 4 (over x, core).
Axes of the slice: x: 2, y: 2, z: 4, core: 2. Of those that a mesh axis runs over, the one named last changes fastest.
Arguments:
- queries: bfloat16 [16384, 1536], P(('hst', 'grp')), may hold values from -5 to 5
- keys_values: bfloat16 [2, 16384, 1536], P(None, ('hst', 'grp')), may hold values from -5 to 5
- token_ids: int32 [16384], replicated, may hold values from 0 to 4095
- lengths: int32 [32], replicated, may hold values from 1 to 512, 12288 in all
- suffix_queries: bfloat16 [1024, 1536], P('hst', 'grp'), may hold values from -5 to 5
- suffix_kv: bfloat16 [2, 1024, 1536], P(None, 'hst', 'grp'), may hold values from -5 to 5
Outputs:
- context_out: bfloat16 [16384, 1536], P(('hst', 'grp'))
- suffix_out: bfloat16 [1024, 1536], P('hst', 'grp')
All inputs are finite; a program needn't handle non-finite values.
Results may differ from a plain program's by a relative error of at most 0.0029.
Values may be sent and summed in bfloat16 or wider, within the bound.
No kernel may reach another device: no remote copies, remote signals or barrier semaphores. Data moves between devices by JAX's collectives and lax.ppermute only.
A program may use at most 128 MiB of HBM per device.

v0:
```python
import math

import jax
import jax.numpy as jnp
from jax import lax
from jax.sharding import PartitionSpec as P

HSZ = 128
NAMB = 512


NEG = -1e30


def broadcast(block, axis, owner):
    block = jnp.where(lax.axis_index(axis) == owner, block, jnp.zeros_like(block))
    return lax.psum(block, axis)


def attend(q, keys, values, valid):
    scale = 1.0 / math.sqrt(HSZ)
    s = jnp.einsum("qhd,khd->hqk", q, keys, preferred_element_type=jnp.float32) * scale
    masked = jnp.where(valid[None], s, NEG)
    top = jnp.max(masked, axis=-1)
    weights = jnp.where(valid[None], jnp.exp(masked - top[..., None]), 0.0)
    total = jnp.sum(weights, axis=-1)
    mixed = jnp.einsum(
        "hqk,khd->qhd", weights.astype(jnp.bfloat16), values, preferred_element_type=jnp.float32
    )
    return (top.T, total.T, mixed)


def per_device(queries, keys_values, token_ids, lengths, suffix_queries, suffix_kv):
    groups = lax.axis_size("grp")
    host = lax.axis_index("hst")
    block = host * groups + lax.axis_index("grp")
    rows = queries.shape[0]
    heads = queries.shape[1] // HSZ
    places = jnp.arange(rows)
    clear = token_ids >= NAMB
    swapped = lax.all_to_all(keys_values, "grp", split_axis=2, concat_axis=1, tiled=True)
    anchor = broadcast(keys_values, ("hst", "grp"), 0)
    gathered = lax.all_gather(suffix_queries, "hst", axis=0, tiled=True)
    anchor_ok = clear[:rows] & (places < lengths[0]) & (block > 0)
    own_len = lengths[block]
    own_ok = lax.dynamic_slice_in_dim(clear, block * rows, rows, 0) & (places < own_len)
    causal = places[None, :] <= places[:, None]
    own_valid = causal & (own_ok[None, :] | (places[None, :] == places[:, None]))
    valid = jnp.concatenate([jnp.broadcast_to(anchor_ok[None, :], (rows, rows)), own_valid], axis=1)
    both = jnp.concatenate([anchor, keys_values], axis=1).reshape(2, 2 * rows, heads, HSZ)
    top, total, mixed = attend(queries.reshape(rows, heads, HSZ), both[0], both[1], valid)
    context = mixed / total[:, :, None]
    context = jnp.where((places < own_len)[:, None, None], context, 0.0)
    context_out = context.astype(jnp.bfloat16).reshape(rows, heads * HSZ)
    local_width = suffix_queries.shape[1]
    local_heads = local_width // HSZ
    share = suffix_queries.shape[0]
    span = swapped.shape[1]
    lens = lax.dynamic_slice_in_dim(lengths, host * groups, groups, 0)
    ctx_ok = lax.dynamic_slice_in_dim(clear, host * span, span, 0) & (
        jnp.arange(span) % rows < jnp.repeat(lens, rows, total_repeat_length=span)
    )
    spos = host * share + jnp.arange(share)
    suffix_keys = jnp.concatenate([swapped, suffix_kv], axis=1).reshape(
        2, span + share, local_heads, HSZ
    )
    total_q = gathered.shape[0]
    width_q = min(512, total_q)

    def one_piece(index):
        q = lax.dynamic_slice_in_dim(gathered, index * width_q, width_q, 0).reshape(
            width_q, local_heads, HSZ
        )
        qpos = index * width_q + jnp.arange(width_q)
        seen = jnp.concatenate(
            [jnp.broadcast_to(ctx_ok[None, :], (width_q, span)), spos[None, :] <= qpos[:, None]],
            axis=1,
        )
        return attend(q, suffix_keys[0], suffix_keys[1], seen)

    tops, totals, parts = lax.map(one_piece, jnp.arange(total_q // width_q))
    tops = tops.reshape(total_q, local_heads)
    totals = totals.reshape(total_q, local_heads)
    parts = parts.reshape(total_q, local_heads, HSZ)
    upper = lax.pmax(tops, "hst")
    factor = jnp.exp(tops - upper)
    scaled_parts = parts * factor[..., None]
    scaled_totals = totals * factor
    acc, summed = lax.psum((scaled_parts, scaled_totals), "hst")
    mine_acc = lax.dynamic_slice_in_dim(acc, host * share, share, 0)
    mine_sum = lax.dynamic_slice_in_dim(summed, host * share, share, 0)
    suffix = mine_acc / mine_sum[..., None]
    suffix_out = suffix.astype(jnp.bfloat16).reshape(share, local_width)
    return (context_out, suffix_out)


def solution(mesh):
    return jax.shard_map(
        per_device,
        mesh=mesh,
        in_specs=(
            P(("hst", "grp"), None),
            P(None, ("hst", "grp"), None),
            P(),
            P(),
            P("hst", "grp"),
            P(None, "hst", "grp"),
        ),
        out_specs=(P(("hst", "grp"), None), P("hst", "grp")),
        check_vma=False,
    )
```

profile of v0, /device:TPU:0, one launch (start us, length us, event | category | flops | bytes accessed | tf_op | source)
XLA Modules:
  0.0 378.3 jit_solution(14179699135018119275)
XLA Ops:
  8.0 8.6 %copy.38 = bf16[2,512,1536]{1,0,2:T(2,128)(2,1)} copy(bf16[2,512,1536]{2,1,0:T(8,128)(2,1)} %param.11) | data formatting | bytes 6291456 | tf_op args[1]
  16.6 4.7 %all-to-all-start = ((bf16[2,512,1536]{1,0,2:T(2,128)(2,1)}), bf16[2,512,1536]{1,0,2:T(2,128)(2,1)}, u32[]{:S(2)}, u32[]{:S(2)}) async-start(bf16[2,512,1536]{1,0,2:T(2,128)(2,1)} %copy.38), calls=%async_computation | async-start | bytes 6291456 | tf_op jit(solution)/shard_map/all_to_all | solution.py:41
  21.3 3.2 copy.31
  24.6 1.9 broadcast_select_fusion
  26.5 0.0 all-reduce.5.cloned.1.call-start
  26.6 0.2 copy.40
  26.8 1.0 copy.37
  27.8 2.6 copy.33
  30.4 0.1 dynamic_slice.28
  30.5 0.6 fusion.53
  31.1 1.3 fusion.48
  32.3 1.1 iota_compare_fusion.3
  33.5 0.7 fusion.52
  34.2 2.5 fusion.45
  36.7 0.2 fusion.40
  36.8 1.1 pad_add_fusion.1
  38.0 36.9 %all_gather.3 = bf16[1024,384]{0,1:T(8,128)(2,1)} all-gather(bf16[128,384]{0,1:T(8,128)(2,1)S(1)} %copy.37), channel_id=1, replica_groups=mesh['hst'=8,'grp'=4] {'hst'}, dimensions={0}, use_global_device_ids=true | all-gather | bytes 884736 | tf_op jit(solution)/shard_map/all_gather | solution.py:43
  74.8 99.3 %all-reduce.3.cloned.1.call-done = bf16[2,512,1536]{1,2,0:T(8,128)(2,1)} async-done(((bf16[2,512,1536]{1,2,0:T(8,128)(2,1)}), bf16[2,512,1536]{1,2,0:T(8,128)(2,1)}) %all-reduce.3.cloned.1.call-update) | async-done | bytes 3145744 | tf_op jit(solution)/shard_map/psum | solution.py:17
  174.2 4.5 %pad_maximum_fusion.1 = (bf16[1,1024,1536]{1,2,0:T(8,128)(2,1)}, bf16[1,1024,1536]{1,2,0:T(8,128)(2,1)}) fusion(bf16[2,512,1536]{1,2,0:T(8,128)(2,1)S(1)} %copy.31, bf16[2,512,1536]{1,2,0:T(8,128)(2,1)} %all-reduce.3.cloned.1.call-done), kind=kLoop, calls=%fused_computation.39 | loop fusion | flops 12582912 | bytes 12582912 | tf_op jit(solution)/shard_map/concatenate | solution.py:50
  178.7 4.3 %copy.54 = bf16[2,512,4,384]{1,2,3,0:T(4,128)(2,1)S(1)} copy(bf16[2,512,4,384]{1,0,3,2:T(2,128)(2,1)} %bitcast.13) | data formatting | bytes 6291456 | tf_op jit(solution)/shard_map/all_to_all | solution.py:41
  183.0 4.0 %concatenate.23 = bf16[2,2048,3,128]{1,3,2,0:T(8,128)(2,1)} reshape(bf16[2,4,512,384]{2,1,3,0:T(4,128)(2,1)S(1)} %bitcast.91) | data formatting | bytes 6291456 | tf_op jit(solution)/shard_map/concatenate | solution.py:64
  187.0 2.2 pad_maximum_fusion
  189.2 3.6 copy.41
  192.8 51.7 %while.16 = (s32[]{:T(128)}, f32[2,512,3]{1,2,0:T(4,128)S(1)}, f32[2,512,3]{1,2,0:T(4,128)S(1)}, f32[2,512,3,128]{3,1,0,2:T(8,128)}, pred[2048]{0:T(1024)(128)(4...) while((s32[]{:T(128)}, f32[2,512,3]{1,2,0:T(4,128)S(1)}, ...), condition=%wide.region_6.7_spmd.clone, body=%wide.region_3.6_spmd.clone.sunk | while | flops 1755903616 | bytes 76027424 | solution.py:81
  192.8 0.6 dynamic_slice.42
  194.1 1.0 constant_dynamic-slice_fusion.3
  195.1 0.1 broadcast_compare_fusion.3
  195.3 0.3 pad_add_fusion.3
  195.6 8.1 %fusion.71 = (f32[3,512]{1,0:T(4,128)S(1)}, f32[3,512,2176]{2,1,0:T(8,128)}) fusion(pred[512,2176]{1,0:T(8,128)(4,1)S(1)} %pad_add_fusion.3, bf16[512,3,128]{0,2,1:T(8,128)(2,1)S(1)} %bitcast.92, bf16[2,2176,3,128]{3,1,2,0:T(8,128)(2,1)} %get-tuple-element.256), kind=kOutput, calls=%fused_computation.3.clone.1 | convolution fusion | flops 865663488 | bytes 16553984 | tf_op jit(solution)/shard_map/while/body/eval_jaxpr/qhd,khd->hqk/dot_general | solution.py:22
  203.7 7.0 %fusion.73 = f32[2,512,3,128]{3,1,0,2:T(8,128)S(1)} fusion(f32[2,512,3,128]{3,1,0,2:T(8,128)S(1)} %copy-done.2, s32[]{:T(128)} %get-tuple-element.235, bf16[2,2176,3,128]{3,1,2,0:T(8,128)(2,1)S(1)} %copy-done, f32[3,512,2176]{2,1,0:T(8,128)} %get-tuple-element.217, f32[3,512]{1,0:T(4,128)S(1)} %get-tuple-element.218, ...), kind=kOutput, calls=%fused_computation.15.clone.1 | convolution fusion | flops 872349696 | bytes 16949252 | tf_op jit(solution)/shard_map/while/body/eval_jaxpr/hqk,khd->qhd/dot_general | solution.py:27
  210.8 7.9 %fusion.72 = f32[3,512]{1,0:T(4,128)S(1)} fusion(f32[3,512,2176]{2,1,0:T(8,128)} %get-tuple-element.217, f32[3,512]{1,0:T(4,128)S(1)} %get-tuple-element.218, pred[512,2176]{1,0:T(8,128)(4,1)S(1)} %pad_add_fusion.3), kind=kLoop, calls=%fused_computation.5.clone.1 | loop fusion | flops 16710144 | bytes 14495744 | tf_op jit(solution)/shard_map/while/body/eval_jaxpr/reduce_sum | solution.py:26
  218.7 0.6 dynamic_slice.42
  219.9 1.0 constant_dynamic-slice_fusion.3
  221.0 0.1 broadcast_compare_fusion.3
  221.1 0.3 pad_add_fusion.3
  221.5 8.1 %fusion.71 = (f32[3,512]{1,0:T(4,128)S(1)}, f32[3,512,2176]{2,1,0:T(8,128)}) fusion(pred[512,2176]{1,0:T(8,128)(4,1)S(1)} %pad_add_fusion.3, bf16[512,3,128]{0,2,1:T(8,128)(2,1)S(1)} %bitcast.92, bf16[2,2176,3,128]{3,1,2,0:T(8,128)(2,1)} %get-tuple-element.256), kind=kOutput, calls=%fused_computation.3.clone.1 | convolution fusion | flops 865663488 | bytes 16553984 | tf_op jit(solution)/shard_map/while/body/eval_jaxpr/qhd,khd->hqk/dot_general | solution.py:22
  229.6 7.0 %fusion.73 = f32[2,512,3,128]{3,1,0,2:T(8,128)S(1)} fusion(f32[2,512,3,128]{3,1,0,2:T(8,128)S(1)} %copy-done.2, s32[]{:T(128)} %get-tuple-element.235, bf16[2,2176,3,128]{3,1,2,0:T(8,128)(2,1)S(1)} %copy-done, f32[3,512,2176]{2,1,0:T(8,128)} %get-tuple-element.217, f32[3,512]{1,0:T(4,128)S(1)} %get-tuple-element.218, ...), kind=kOutput, calls=%fused_computation.15.clone.1 | convolution fusion | flops 872349696 | bytes 16949252 | tf_op jit(solution)/shard_map/while/body/eval_jaxpr/hqk,khd->qhd/dot_general | solution.py:27
  236.6 7.9 %fusion.72 = f32[3,512]{1,0:T(4,128)S(1)} fusion(f32[3,512,2176]{2,1,0:T(8,128)} %get-tuple-element.217, f32[3,512]{1,0:T(4,128)S(1)} %get-tuple-element.218, pred[512,2176]{1,0:T(8,128)(4,1)S(1)} %pad_add_fusion.3), kind=kLoop, calls=%fused_computation.5.clone.1 | loop fusion | flops 16710144 | bytes 14495744 | tf_op jit(solution)/shard_map/while/body/eval_jaxpr/reduce_sum | solution.py:26
  244.5 35.9 %pmax.7 = f32[1024,3]{0,1:T(4,128)S(1)} all-reduce(f32[1024,3]{0,1:T(4,128)S(1)} %bitcast.99), channel_id=1, replica_groups=mesh['hst'=8,'grp'=4] {'hst'}, use_global_device_ids=true, to_apply=%region_7.8 | all-reduce | flops 3072 | bytes 24576 | tf_op jit(solution)/shard_map/pmax | solution.py:85
  280.4 3.1 bitcast_multiply_fusion
  283.5 18.0 %fusion.54 = (f32[12,512]{1,0:T(8,128)S(1)}, bf16[12,512,1024]{1,2,0:T(8,128)(2,1)}) fusion(pred[512,1024]{0,1:T(8,128)(4,1)} %pad_add_fusion.1, bf16[1024,12,128]{0,2,1:T(8,128)(2,1)} %bitcast.94, bf16[512,12,128]{0,2,1:T(8,128)(2,1)} %bitcast.95), kind=kOutput, calls=%fused_computation.72 | convolution fusion | flops 1648362496 | bytes 17850368 | tf_op jit(solution)/shard_map/sub | solution.py:25
  301.5 7.6 %fusion.37 = bf16[512,12,128]{0,2,1:T(8,128)(2,1)} fusion(bf16[1024,12,128]{0,2,1:T(8,128)(2,1)S(1)} %bitcast.93, bf16[12,512,1024]{1,2,0:T(8,128)(2,1)} %get-tuple-element.155, f32[512,12]{0,1:T(8,128)S(1)} %bitcast.102, pred[512]{0:T(512)(128)(4,1)S(1)} %copy-done.12), kind=kOutput, calls=%fused_computation.42 | convolution fusion | flops 1612972032 | bytes 17326592 | tf_op jit(solution)/shard_map/hqk,khd->qhd/dot_general | solution.py:27
  309.2 2.6 copy.44
  311.7 33.2 %psum.23 = f32[1024,3]{0,1:T(4,128)S(1)} all-reduce(f32[1024,3]{0,1:T(4,128)S(1)} %get-tuple-element.138), channel_id=1, replica_groups=mesh['hst'=8,'grp'=4] {'hst'}, use_global_device_ids=true, to_apply=%region_9.10 | all-reduce | flops 3072 | bytes 24576 | tf_op jit(solution)/shard_map/psum | solution.py:89
  344.9 24.0 %all-reduce.5.cloned.1.call-done = f32[1024,3,128]{2,0,1:T(8,128)} async-done(((f32[1024,3,128]{2,0,1:T(8,128)}), f32[1024,3,128]{2,0,1:T(8,128)}) %all-reduce.5.cloned.1.call-update) | async-done | bytes 1572880 | tf_op jit(solution)/shard_map/psum | solution.py:89
  368.9 1.0 divide_convert_fusion
  370.0 0.1 copy.43
  370.1 0.8 copy.45
  (52 shorter events, 0.2 us)
Async XLA Ops:
  16.6 162.0 %all-to-all-start = ((bf16[2,512,1536]{1,0,2:T(2,128)(2,1)}), bf16[2,512,1536]{1,0,2:T(2,128)(2,1)}, u32[]{:S(2)}, u32[]{:S(2)}) async-start(bf16[2,512,1536]{1,0,2:T(2,128)(2,1)} %copy.38), calls=%async_computation | async-start | bytes 6291456 | tf_op jit(solution)/shard_map/all_to_all | solution.py:41
  21.3 152.9 %all-reduce.3.cloned.1.call-start = ((), (), s32[]{:S(2)}) async-start(), calls=%async_computation.1 | async-start | bytes 6291456 | tf_op jit(solution)/shard_map/psum | solution.py:17
  24.6 2.0 copy-start.4
  26.4 4.0 %copy-start.11 = (s32[32]{0:T(128)S(1)}, s32[32]{0:T(128)}, u32[]{:S(2)}) copy-start(s32[32]{0:T(128)} %param.13) | copy-start | bytes 388
  26.4 7.7 %copy-start.8 = (pred[2048]{0:T(1024)(128)(4,1)S(1)}, pred[2048]{0:T(1024)(128)(4,1)}, u32[]{:S(2)}) copy-start(pred[2048]{0:T(1024)(128)(4,1)} %constant.176) | copy-start | bytes 6148
  26.4 7.7 %copy-start.9 = (pred[2048]{0:T(1024)(128)(4,1)S(1)}, pred[2048]{0:T(1024)(128)(4,1)}, u32[]{:S(2)}) copy-start(pred[2048]{0:T(1024)(128)(4,1)} %constant.177) | copy-start | bytes 6148
  26.4 7.7 %copy-start.10 = (pred[2048]{0:T(1024)(128)(4,1)S(1)}, pred[2048]{0:T(1024)(128)(4,1)}, u32[]{:S(2)}) copy-start(pred[2048]{0:T(1024)(128)(4,1)} %constant.178) | copy-start | bytes 6148
  26.5 342.4 %all-reduce.5.cloned.1.call-start = ((), (), s32[]{:S(2)}) async-start(), calls=%async_computation.2 | async-start | bytes 3145728 | tf_op jit(solution)/shard_map/psum | solution.py:89
  26.7 3.7 copy-start.5
  189.2 3.6 copy-start.6
  189.2 3.6 copy-start.7
  195.6 8.2 %copy-start = (bf16[2,2176,3,128]{3,1,2,0:T(8,128)(2,1)S(1)}, bf16[2,2176,3,128]{3,1,2,0:T(8,128)(2,1)}, u32[]{:S(2)}) copy-start(bf16[2,2176,3,128]{3,1,2,0:T(8,128)(2,1)} %get-tuple-element.256) | copy-start | bytes 10027012 | tf_op jit(solution)/shard_map/while
  195.6 8.2 %copy-start.2 = (f32[2,512,3,128]{3,1,0,2:T(8,128)S(1)}, f32[2,512,3,128]{3,1,0,2:T(8,128)}, u32[]{:S(2)}) copy-start(f32[2,512,3,128]{3,1,0,2:T(8,128)} %get-tuple-element.238) | copy-start | bytes 4718596 | tf_op jit(solution)/shard_map/while
  210.8 7.9 %copy-start.3 = (f32[2,512,3,128]{3,1,0,2:T(8,128)}, f32[2,512,3,128]{3,1,0,2:T(8,128)S(1)}, u32[]{:S(2)}) copy-start(f32[2,512,3,128]{3,1,0,2:T(8,128)S(1)} %fusion.73) | copy-start | bytes 4718596 | tf_op jit(solution)/shard_map/while
  221.4 8.2 %copy-start = (bf16[2,2176,3,128]{3,1,2,0:T(8,128)(2,1)S(1)}, bf16[2,2176,3,128]{3,1,2,0:T(8,128)(2,1)}, u32[]{:S(2)}) copy-start(bf16[2,2176,3,128]{3,1,2,0:T(8,128)(2,1)} %get-tuple-element.256) | copy-start | bytes 10027012 | tf_op jit(solution)/shard_map/while
  221.4 8.2 %copy-start.2 = (f32[2,512,3,128]{3,1,0,2:T(8,128)S(1)}, f32[2,512,3,128]{3,1,0,2:T(8,128)}, u32[]{:S(2)}) copy-start(f32[2,512,3,128]{3,1,0,2:T(8,128)} %get-tuple-element.238) | copy-start | bytes 4718596 | tf_op jit(solution)/shard_map/while
  236.6 7.9 %copy-start.3 = (f32[2,512,3,128]{3,1,0,2:T(8,128)}, f32[2,512,3,128]{3,1,0,2:T(8,128)S(1)}, u32[]{:S(2)}) copy-start(f32[2,512,3,128]{3,1,0,2:T(8,128)S(1)} %fusion.73) | copy-start | bytes 4718596 | tf_op jit(solution)/shard_map/while
  283.5 18.0 %copy-start.1 = (bf16[1,1024,1536]{1,2,0:T(8,128)(2,1)S(1)}, bf16[1,1024,1536]{1,2,0:T(8,128)(2,1)}, u32[]{:S(2)}) copy-start(bf16[1,1024,1536]{1,2,0:T(8,128)(2,1)} %get-tuple-element.145) | copy-start | bytes 9437188
  283.5 18.0 %copy-start.12 = (pred[512]{0:T(512)(128)(4,1)S(1)}, pred[512]{0:T(512)(128)(4,1)}, u32[]{:S(2)}) copy-start(pred[512]{0:T(512)(128)(4,1)} %iota_compare_fusion.3) | copy-start | bytes 1540
Sparse Core Ops, SparseCore 0:
  27.6 146.5 all-reduce.2
Sparse Core Ops, SparseCore 1:
  283.6 85.3 all-reduce.4
where the time goes:
time: 379 us; the launch traced here: 378 us
  waiting for transfers between devices  123 us (32%)
  blocking collectives  106 us (28%)
  matrix products  55.9 us (15%)
  local copies, waits for them, and re-layouts  35.6 us (9%)
  other arithmetic  35.6 us (9%)
  between operations  15.7 us (4%)
  starting transfers between devices  4.74 us (1%)
    psum x1, waiting for transfers between devices, broadcast(): return lax.psum(block, axis)  99.3 us
    all_gather x1, blocking collectives, per_device(): gathered = lax.all_gather(suffix_queries, 'hst', axis=0, tiled=True)  36.9 us
    pmax x1, blocking collectives, per_device(): upper = lax.pmax(tops, 'hst')  35.9 us
    psum x1, blocking collectives, per_device(): acc, summed = lax.psum((scaled_parts, scaled_totals), 'hst')  33.2 us
    psum x1, waiting for transfers between devices, per_device(): acc, summed = lax.psum((scaled_parts, scaled_totals), 'hst')  24 us
    unnamed x28, local copies, waits for them, and re-layouts  22.6 us
    dot_general x3, matrix products, attend(): jnp.einsum('hqk,khd->qhd', weights.astype(jnp.bfloat16), values, preferre...  21.6 us
    sub x1, matrix products, attend(): weights = jnp.where(valid[None], jnp.exp(masked - top[..., None]), 0.0)  18 us
  transfers between devices with their start and end apart: 3, of which 2 were waited for; matrix products, arithmetic and copies ran while one was open for 13% of the time, Pallas kernels for 0%

commit v1 on v0

v1 whole, which is shorter than its diff:
```python
import functools
import math

import jax
import jax.numpy as jnp
from jax import lax
from jax.experimental import pallas as pl
from jax.experimental.pallas import tpu as pltpu
from jax.sharding import PartitionSpec as P

HSZ = 128
NAMB = 512
NEG = -1e30
FLOOR = -1e4
SCALE = 1.0 / math.sqrt(HSZ)
C2 = SCALE * math.log2(math.e)
BOTH = ("hst", "grp")


def dot_t(a, b):
    return lax.dot_general(a, b, (((1,), (1,)), ((), ())), preferred_element_type=jnp.float32)


def dot(a, b):
    return lax.dot_general(a, b, (((1,), (0,)), ((), ())), preferred_element_type=jnp.float32)


def softmax_mix(scores, values):
    top = functools.reduce(jnp.maximum, [jnp.max(s, axis=-1, keepdims=True) for s in scores])
    base = top * C2
    total = 0.0
    mixed = 0.0
    for s, v in zip(scores, values):
        w = jnp.exp2(s * C2 - base)
        total = total + jnp.sum(w, axis=-1, keepdims=True)
        mixed = mixed + dot(w.astype(jnp.bfloat16), v)
    return top, total, mixed


def pack_kernel(kv_ref, out_ref):
    out_ref[0, 0] = kv_ref[0]


def pack(kv, groups):
    _, rows, width = kv.shape
    part = width // groups
    return pl.pallas_call(
        pack_kernel,
        grid=(groups, 2),
        in_specs=[pl.BlockSpec((1, rows, part), lambda g, s: (s, 0, g))],
        out_specs=pl.BlockSpec((1, 1, rows, part), lambda g, s: (g, s, 0, 0)),
        out_shape=jax.ShapeDtypeStruct((groups, 2, rows, part), kv.dtype),
        cost_estimate=pl.CostEstimate(flops=0, bytes_accessed=4 * kv.size, transcendentals=0),
        name="pack_heads",
    )(kv)


def suffix_kernel(groups, sub, share, at_ref, q_ref, kv_ref, sk_ref, bias_ref, n_ref, st_ref):
    host = at_ref[0]
    step, head = pl.program_id(0), pl.program_id(1)
    tile = q_ref.shape[0]

    @pl.when(head == 0)
    def _():
        st_ref[...] = jnp.zeros_like(st_ref)

    for first in range(0, tile, sub):
        q = q_ref[first : first + sub, :]
        scores = []
        values = []
        for g in range(groups):
            bias = bias_ref[pl.ds(host * groups + g, 1), :]
            scores.append(dot_t(q, kv_ref[g, 0]) + bias)
            values.append(kv_ref[g, 1])
        s = dot_t(q, sk_ref[0])
        qpos = step * tile + first + lax.broadcasted_iota(jnp.int32, s.shape, 0)
        spos = host * share + lax.broadcasted_iota(jnp.int32, s.shape, 1)
        scores.append(jnp.where(spos <= qpos, s, NEG))
        values.append(sk_ref[1])
        top, total, mixed = softmax_mix(scores, values)
        n = mixed / total
        size = jnp.max(jnp.abs(n), axis=-1, keepdims=True)
        size = jnp.where(size > 0.0, size, 1.0)
        n_ref[first : first + sub, :] = n / size
        lse = jnp.maximum(top * SCALE + jnp.log(total), FLOOR)
        lane = lax.broadcasted_iota(jnp.int32, (sub, 128), 1)
        turned = jnp.where(lane == 0, lse, size).T
        for c in range(sub // share):
            chunk = first // share + c
            st_ref[chunk, pl.ds(2 * head, 2), :] = turned[0:2, c * share : (c + 1) * share]


def suffix_attend(at, q, kv, sk, bias):
    groups, _, rows, width = kv.shape
    total_q = q.shape[0]
    share = sk.shape[1]
    heads = width // HSZ
    tile, sub = min(512, total_q), min(256, total_q)
    seen = groups * rows + share
    return pl.pallas_call(
        functools.partial(suffix_kernel, groups, sub, share),
        grid_spec=pltpu.PrefetchScalarGridSpec(
            num_scalar_prefetch=1,
            grid=(total_q // tile, heads),
            in_specs=[
                pl.BlockSpec((tile, HSZ), lambda i, h, at: (i, h)),
                pl.BlockSpec((groups, 2, rows, HSZ), lambda i, h, at: (0, 0, 0, h)),
                pl.BlockSpec((2, share, HSZ), lambda i, h, at: (0, 0, h)),
                pl.BlockSpec(bias.shape, lambda i, h, at: (0, 0)),
            ],
            out_specs=[
                pl.BlockSpec((tile, HSZ), lambda i, h, at: (i, h)),
                pl.BlockSpec((tile // share, 8, share), lambda i, h, at: (i, 0, 0)),
            ],
        ),
        out_shape=[
            jax.ShapeDtypeStruct((total_q, width), jnp.float32),
            jax.ShapeDtypeStruct((total_q // share, 8, share), jnp.float32),
        ],
        compiler_params=pltpu.CompilerParams(vmem_limit_bytes=48 * 1024 * 1024),
        cost_estimate=pl.CostEstimate(
            flops=8 * total_q * seen * width,
            bytes_accessed=2 * kv.size + 2 * q.size + 4 * q.size,
            transcendentals=total_q * seen * heads,
        ),
        name="suffix_attend",
    )(at, q, kv, sk, bias)


def context_kernel(pieces, at_ref, len_ref, q_ref, kv_ref, bias_ref, *rest):
    piece_refs, (out_ref, diag_ref, anchor_ref) = rest[:pieces], rest[pieces:]
    block, mine = at_ref[2], at_ref[3]
    rows = q_ref.shape[0]
    half = rows // 2
    part = rows // pieces
    own = bias_ref[pl.ds(block, 1), :]

    @pl.when(pl.program_id(0) == 0)
    def _():
        row = lax.broadcasted_iota(jnp.int32, (half, half), 0)
        col = lax.broadcasted_iota(jnp.int32, (half, half), 1)
        for t in range(2):
            ok = own[:, t * half : (t + 1) * half]
            diag_ref[t] = jnp.where(col == row, 0.0, jnp.where(col < row, ok, NEG))

    for k in range(pieces):
        place = pl.multiple_of(jnp.bitwise_xor(mine, k) * part, part)
        anchor_ref[:, pl.ds(place, part), :] = piece_refs[k][...]
    anchor_bias = jnp.where(block > 0, bias_ref[0:1, :], NEG)
    keys, values = kv_ref[0], kv_ref[1]
    for t in range(2):
        q = q_ref[t * half : (t + 1) * half, :]
        scores = [dot_t(q, anchor_ref[0]) + anchor_bias]
        mix = [anchor_ref[1]]
        if t == 1:
            scores.append(dot_t(q, keys[:half]) + own[:, :half])
            mix.append(values[:half])
        scores.append(dot_t(q, keys[t * half : (t + 1) * half]) + diag_ref[t])
        mix.append(values[t * half : (t + 1) * half])
        _, total, mixed = softmax_mix(scores, mix)
        place = t * half + lax.broadcasted_iota(jnp.int32, mixed.shape, 0)
        out = jnp.where(place < len_ref[block], mixed / total, 0.0)
        out_ref[t * half : (t + 1) * half, :] = out.astype(out_ref.dtype)


def context_attend(at, lengths, q, kv, bias, anchor):
    rows, width = q.shape
    heads = width // HSZ
    pieces = len(anchor)
    part = rows // pieces
    half = rows // 2
    column = lambda h, *_: (0, h)
    return pl.pallas_call(
        functools.partial(context_kernel, pieces),
        grid_spec=pltpu.PrefetchScalarGridSpec(
            num_scalar_prefetch=2,
            grid=(heads,),
            in_specs=[
                pl.BlockSpec((rows, HSZ), column),
                pl.BlockSpec((2, rows, HSZ), lambda h, *_: (0, 0, h)),
                pl.BlockSpec(bias.shape, lambda h, *_: (0, 0)),
            ]
            + [pl.BlockSpec((2, part, HSZ), lambda h, *_: (0, 0, h))] * pieces,
            out_specs=pl.BlockSpec((rows, HSZ), column),
            scratch_shapes=[
                pltpu.VMEM((2, half, half), jnp.float32),
                pltpu.VMEM((2, rows, HSZ), jnp.bfloat16),
            ],
        ),
        out_shape=jax.ShapeDtypeStruct((rows, width), q.dtype),
        compiler_params=pltpu.CompilerParams(vmem_limit_bytes=48 * 1024 * 1024),
        cost_estimate=pl.CostEstimate(
            flops=8 * rows * rows * width,
            bytes_accessed=12 * q.size,
            transcendentals=2 * rows * rows * heads,
        ),
        name="context_attend",
    )(at, lengths, q, kv, bias, *anchor)


def spread_anchor(kv, hosts, groups):
    count = 2 * groups
    part = kv.shape[1] // count
    first = (lax.axis_index("hst") == 0) & (lax.axis_index("grp") == 0)
    piece = jnp.where(first, kv[:, :part], 0.0)
    for p in range(1, count):
        piece = piece + lax.ppermute(kv[:, p * part : (p + 1) * part], BOTH, [(0, p)])
    far = hosts // 2
    while far >= 2:
        pairs = [(h, h + far) for h in range(hosts) if h % (2 * far) < 2]
        piece = piece + lax.ppermute(piece, "hst", pairs)
        far //= 2
    swap = lambda x, axis, n, k: lax.ppermute(x, axis, [(i, i ^ k) for i in range(n)])
    held = {0: piece}
    held[groups] = swap(piece, "hst", hosts, 1)
    k = groups // 2
    while k >= 1:
        for have in list(held):
            held[have ^ k] = swap(held[have], "grp", groups, k)
        k //= 2
    return [held[k] for k in range(count)]


def combine(parts, stats, share):
    hosts, _, width = parts.shape
    heads = width // HSZ
    lse, size = stats[:, 0 : 2 * heads : 2, :], stats[:, 1 : 2 * heads : 2, :]
    factor = jnp.exp(lse - jnp.max(lse, axis=0, keepdims=True))
    factor = factor / jnp.sum(factor, axis=0, keepdims=True) * size
    factor = factor.transpose(0, 2, 1)[..., None]
    out = jnp.sum(parts.astype(jnp.float32).reshape(hosts, share, heads, HSZ) * factor, axis=0)
    return out.astype(jnp.bfloat16).reshape(share, width)


def per_device(queries, keys_values, token_ids, lengths, suffix_queries, suffix_kv):
    hosts, groups = lax.axis_size("hst"), lax.axis_size("grp")
    host, group = lax.axis_index("hst"), lax.axis_index("grp")
    rows = queries.shape[0]
    share = suffix_queries.shape[0]
    at = jnp.stack([host, group, host * groups + group, (host % 2) * groups + group]).astype(jnp.int32)
    swapped = lax.all_to_all(pack(keys_values, groups), "grp", split_axis=0, concat_axis=0, tiled=True)
    gathered = lax.all_gather(suffix_queries, "hst", axis=0, tiled=True)
    anchor = spread_anchor(keys_values, hosts, groups)
    seen = (token_ids.reshape(-1, rows) >= NAMB) & (jnp.arange(rows)[None, :] < lengths[:, None])
    bias = jnp.where(seen, 0.0, NEG).astype(jnp.float32)
    parts, stats = suffix_attend(at, gathered, swapped, suffix_kv, bias)
    parts = parts.astype(jnp.float16).reshape(hosts, share, -1)
    parts = lax.all_to_all(parts, "hst", split_axis=0, concat_axis=0, tiled=True)
    stats = lax.all_to_all(stats, "hst", split_axis=0, concat_axis=0, tiled=True)
    context_out = context_attend(at, lengths, queries, keys_values, bias, anchor)
    return (context_out, combine(parts, stats, share))


def solution(mesh):
    return jax.shard_map(
        per_device,
        mesh=mesh,
        in_specs=(
            P(("hst", "grp"), None),
            P(None, ("hst", "grp"), None),
            P(),
            P(),
            P("hst", "grp"),
            P(None, "hst", "grp"),
        ),
        out_specs=(P(("hst", "grp"), None), P("hst", "grp")),
        check_vma=False,
    )
```

time: 379 us -> 181 us (0.48)
  waiting for transfers between devices: 123 us -> 41 us
  blocking collectives: 106 us -> 33.9 us
  matrix products: 55.9 us -> 0 us
  Pallas kernels: 0 us -> 39.7 us
  starting transfers between devices: 4.74 us -> 39.6 us
  other arithmetic: 35.6 us -> 9.12 us
  local copies, waits for them, and re-layouts: 35.6 us -> 16.2 us
  between operations: 15.7 us -> 0.75 us
    psum x2 -> x0, waiting for transfers between devices: 123 us -> none  [the longest x1 99.3 us: broadcast(): return lax.psum(block, axis)]
    ppermute x0 -> x16, waiting for transfers between devices: none -> 41 us  [the longest x7 35 us: spread_anchor(): piece = piece + lax.ppermute(kv[:, p * part:(p + 1) * part], BOTH, [(0, p)])]
    pallas_call x0 -> x3, Pallas kernels: none -> 39.7 us  [the longest x1 17.4 us: context_attend(): pl.pallas_call(functools.partial(context_kernel, pieces), grid_spec=pltpu...]
    dot_general x5 -> x0, matrix products: 37.9 us -> none  [the longest x3 21.6 us: attend(): jnp.einsum('hqk,khd->qhd', weights.astype(jnp.bfloat16), values, preferre...]
    pmax x1 -> x0, blocking collectives: 35.9 us -> none  [per_device(): upper = lax.pmax(tops, 'hst')]
    psum x1 -> x0, blocking collectives: 33.2 us -> none  [per_device(): acc, summed = lax.psum((scaled_parts, scaled_totals), 'hst')]
    ppermute x0 -> x16, starting transfers between devices: none -> 25.4 us  [the longest x7 18.8 us: spread_anchor(): piece = piece + lax.ppermute(kv[:, p * part:(p + 1) * part], BOTH, [(0, p)])]
    sub x1 -> x0, matrix products: 18 us -> none  [attend(): weights = jnp.where(valid[None], jnp.exp(masked - top[..., None]), 0.0)]
  transfers between devices with their start and end apart: 3 -> 19, of which waited for: 2 -> 6; matrix products, arithmetic and copies ran while one was open for 13% -> 7% of each run, Pallas kernels for 0% -> 22%
where the time goes in v1:
time: 181 us; the launch traced here: 180 us
  waiting for transfers between devices  41 us (23%)
  Pallas kernels  39.7 us (22%)
  starting transfers between devices  39.6 us (22%)
  blocking collectives  33.9 us (19%)
  local copies, waits for them, and re-layouts  16.2 us (9%)
  other arithmetic  9.12 us (5%)
    ppermute x7, waiting for transfers between devices, spread_anchor(): piece = piece + lax.ppermute(kv[:, p * part:(p + 1) * part], BOTH, [(0, p)])  35 us
    all_gather x1, blocking collectives, per_device(): gathered = lax.all_gather(suffix_queries, 'hst', axis=0, tiled=True)  33.9 us
    ppermute x7, starting transfers between devices, spread_anchor(): piece = piece + lax.ppermute(kv[:, p * part:(p + 1) * part], BOTH, [(0, p)])  18.8 us
    pallas_call x1, Pallas kernels, context_attend(): pl.pallas_call(functools.partial(context_kernel, pieces), grid_spec=pltpu...  17.4 us
    pallas_call x1, Pallas kernels, suffix_attend(): pl.pallas_call(functools.partial(suffix_kernel, groups, sub, share), grid...  16.2 us
    unnamed x29, local copies, waits for them, and re-layouts  8.93 us
    pallas_call x1, Pallas kernels, pack(): pl.pallas_call(pack_kernel, grid=(groups, 2), in_specs=[pl.BlockSpec((1,...  6.17 us
    all_to_all x1, starting transfers between devices, per_device(): lax.all_to_all(parts, 'hst', split_axis=0, concat_axis=0, tiled=True)  6 us
  transfers between devices with their start and end apart: 19, of which 6 were waited for; matrix products, arithmetic and copies ran while one was open for 7% of the time, Pallas kernels for 22%

profile of v1, /device:TPU:0, one launch (start us, length us, event | category | flops | bytes accessed | tf_op | source)
XLA Modules:
  0.0 180.3 jit_solution(1209302260903983680)
XLA Ops:
  0.6 3.3 %fusion.5 = (bf16[2,64,1536]{2,1,0:T(8,128)(2,1)}, bf16[2,64,1536]{2,1,0:T(8,128)(2,1)}, bf16[2,64,1536]{2,1,0:T(8,128)(2,1)}, bf16[2,64,1536]{2,1,0:T(8,128)(2,...) fusion(bf16[2,512,1536]{2,1,0:T(8,128)(2,1)} %kv_ref.3), kind=kLoop, calls=%fused_computation.12 | loop fusion | bytes 5505024 | tf_op jit(solution)/shard_map/slice | solution.py:207
  3.9 2.4 %collective-permute-start = (bf16[2,64,1536]{2,1,0:T(8,128)(2,1)}, bf16[2,64,1536]{2,1,0:T(8,128)(2,1)S(1)}, u32[]{:S(2)}, u32[]{:S(2)}) collective-permute-start(bf16[2,64,1536]{2,1,0:T(8,128)(2,1)} %get-tuple-element.8), channel_id=1, source_target_pairs={{0,1}} | collective-permute-start | bytes 1179656 | tf_op jit(solution)/shard_map/ppermute | solution.py:207
  6.3 3.9 %collective-permute-start.1 = (bf16[2,64,1536]{2,1,0:T(8,128)(2,1)}, bf16[2,64,1536]{2,1,0:T(8,128)(2,1)}, u32[]{:S(2)}, u32[]{:S(2)}) collective-permute-start(bf16[2,64,1536]{2,1,0:T(8,128)(2,1)} %get-tuple-element.14), channel_id=1, source_target_pairs={{0,2}} | collective-permute-start | bytes 1179656 | tf_op jit(solution)/shard_map/ppermute | solution.py:207
  10.2 6.2 %pack_heads.1 = bf16[4,2,512,384]{3,2,1,0:T(8,128)(2,1)} custom-call(bf16[2,512,1536]{2,1,0:T(8,128)(2,1)} %kv_ref.3), custom_call_target="tpu_custom_call" | custom-call | bytes 6291456 | tf_op jit(solution)/shard_map/pack_heads/pallas_call | solution.py:47
  16.3 3.7 %all-to-all-start = ((bf16[4,2,512,384]{3,2,1,0:T(8,128)(2,1)}), bf16[4,2,512,384]{3,2,1,0:T(8,128)(2,1)S(1)}, u32[]{:S(2)}, u32[]{:S(2)}) async-start(bf16[4,2,512,384]{3,2,1,0:T(8,128)(2,1)} %pack_heads.1), calls=%async_computation | async-start | bytes 6291456 | tf_op jit(solution)/shard_map/all_to_all | solution.py:241
  20.1 4.4 %collective-permute-start.2 = (bf16[2,64,1536]{2,1,0:T(8,128)(2,1)}, bf16[2,64,1536]{2,1,0:T(8,128)(2,1)}, u32[]{:S(2)}, u32[]{:S(2)}) collective-permute-start(bf16[2,64,1536]{2,1,0:T(8,128)(2,1)} %get-tuple-element.13), channel_id=1, source_target_pairs={{0,3}} | collective-permute-start | bytes 1179656 | tf_op jit(solution)/shard_map/ppermute | solution.py:207
  24.4 2.0 %collective-permute-start.3 = (bf16[2,64,1536]{2,1,0:T(8,128)(2,1)}, bf16[2,64,1536]{2,1,0:T(8,128)(2,1)}, u32[]{:S(2)}, u32[]{:S(2)}) collective-permute-start(bf16[2,64,1536]{2,1,0:T(8,128)(2,1)} %get-tuple-element.12), channel_id=1, source_target_pairs={{0,4}} | collective-permute-start | bytes 1179656 | tf_op jit(solution)/shard_map/ppermute | solution.py:207
  26.5 2.0 %collective-permute-start.4 = (bf16[2,64,1536]{2,1,0:T(8,128)(2,1)}, bf16[2,64,1536]{2,1,0:T(8,128)(2,1)}, u32[]{:S(2)}, u32[]{:S(2)}) collective-permute-start(bf16[2,64,1536]{2,1,0:T(8,128)(2,1)} %get-tuple-element.11), channel_id=1, source_target_pairs={{0,5}} | collective-permute-start | bytes 1179656 | tf_op jit(solution)/shard_map/ppermute | solution.py:207
  28.5 2.0 %collective-permute-start.5 = (bf16[2,64,1536]{2,1,0:T(8,128)(2,1)}, bf16[2,64,1536]{2,1,0:T(8,128)(2,1)}, u32[]{:S(2)}, u32[]{:S(2)}) collective-permute-start(bf16[2,64,1536]{2,1,0:T(8,128)(2,1)} %get-tuple-element.10), channel_id=1, source_target_pairs={{0,6}} | collective-permute-start | bytes 1179656 | tf_op jit(solution)/shard_map/ppermute | solution.py:207
  30.5 2.0 %collective-permute-start.6 = (bf16[2,64,1536]{2,1,0:T(8,128)(2,1)}, bf16[2,64,1536]{2,1,0:T(8,128)(2,1)}, u32[]{:S(2)}, u32[]{:S(2)}) collective-permute-start(bf16[2,64,1536]{2,1,0:T(8,128)(2,1)} %get-tuple-element.9), channel_id=1, source_target_pairs={{0,7}} | collective-permute-start | bytes 1179656 | tf_op jit(solution)/shard_map/ppermute | solution.py:207
  32.6 26.6 %collective-permute-done.2 = bf16[2,64,1536]{2,1,0:T(8,128)(2,1)} collective-permute-done((bf16[2,64,1536]{2,1,0:T(8,128)(2,1)}, bf16[2,64,1536]{2,1,0:T(8,128)(2,1)}, u32[]{:S(2)}, u32[]{:S(2)}) %collective-permute-start.2) | collective-permute-done | bytes 393248 | tf_op jit(solution)/shard_map/ppermute | solution.py:207
  59.2 4.2 %collective-permute-done.5 = bf16[2,64,1536]{2,1,0:T(8,128)(2,1)} collective-permute-done((bf16[2,64,1536]{2,1,0:T(8,128)(2,1)}, bf16[2,64,1536]{2,1,0:T(8,128)(2,1)}, u32[]{:S(2)}, u32[]{:S(2)}) %collective-permute-start.5) | collective-permute-done | bytes 393248 | tf_op jit(solution)/shard_map/ppermute | solution.py:207
  63.4 4.2 %collective-permute-done.6 = bf16[2,64,1536]{2,1,0:T(8,128)(2,1)} collective-permute-done((bf16[2,64,1536]{2,1,0:T(8,128)(2,1)}, bf16[2,64,1536]{2,1,0:T(8,128)(2,1)}, u32[]{:S(2)}, u32[]{:S(2)}) %collective-permute-start.6) | collective-permute-done | bytes 393248 | tf_op jit(solution)/shard_map/ppermute | solution.py:207
  67.6 2.0 %add_add_fusion = bf16[2,64,1536]{2,1,0:T(8,128)(2,1)S(1)} fusion(bf16[2,64,1536]{2,1,0:T(8,128)(2,1)} %collective-permute-done.6, bf16[2,64,1536]{2,1,0:T(8,128)(2,1)} %collective-permute-done.5, bf16[2,64,1536]{2,1,0:T(8,128)(2,1)} %collective-permute-done.4, bf16[2,64,1536]{2,1,0:T(8,128)(2,1)} %collective-permute-done.3, ...), kind=kLoop, calls=%fused_computation.2 | loop fusion | flops 1572864 | bytes 3538945 | tf_op jit(solution)/shard_map/add | solution.py:207
  69.6 2.0 %collective-permute-start.7 = (bf16[2,64,1536]{2,1,0:T(8,128)(2,1)S(1)}, bf16[2,64,1536]{2,1,0:T(8,128)(2,1)}, u32[]{:S(2)}, u32[]{:S(2)}) collective-permute-start(bf16[2,64,1536]{2,1,0:T(8,128)(2,1)S(1)} %add_add_fusion), channel_id=1, source_target_pairs={{0,16},{4,20},{1,17},{5,21},{2,18},{6,22},{3,19},{7,23}} | collective-permute-start | bytes 1179656 | tf_op jit(solution)/shard_map/ppermute | solution.py:211
  71.6 0.6 broadcast_compare_fusion
  72.2 1.4 ge.11
  73.6 1.4 fusion.2.bias_ref
  75.0 1.7 collective-permute-done.7
  76.7 1.1 add.47
  77.8 1.3 collective-permute-start.8
  79.1 0.1 pad_add_fusion.at_ref
  79.2 33.9 %all_gather.3.q_ref = bf16[1024,384]{1,0:T(8,128)(2,1)} all-gather(bf16[128,384]{1,0:T(8,128)(2,1)} %param.10), channel_id=1, replica_groups=mesh['hst'=8,'grp'=4] {'hst'}, dimensions={0}, use_global_device_ids=true | all-gather | bytes 884736 | tf_op jit(solution)/shard_map/all_gather | solution.py:242
  113.0 0.1 add.48.rest_0_
  113.1 0.7 collective-permute-start.12
  113.8 1.1 copy-done.1
  115.0 0.8 copy-done.2
  115.8 0.9 copy-done.11
  116.7 16.2 %suffix_attend.1 = (f32[1024,384]{1,0:T(8,128)S(1)}, f32[8,8,128]{2,1,0:T(8,128)S(1)}) custom-call(s32[4]{0:T(128)S(1)} %pad_add_fusion.at_ref, bf16[1024,384]{1,0:T(8,128)(2,1)S(1)} %copy-done.1, bf16[4,2,512,384]{3,2,1,0:T(8,128)(2,1)S(1)} %all-to-all-done.kv_ref, bf16[2,128,384]{2,1,0:T(8,128)(2,1)S(1)} %copy-done.11, f32[32,512]{1,0:T(8,128)S(1)} %copy-done.2), custom_call_target="tpu_custom_call" | custom-call | flops 6845104128 | bytes 5505024 | tf_op jit(solution)/shard_map/suffix_attend/pallas_call | solution.py:100
  132.9 1.1 copy-done
  134.1 0.6 copy-done.4
  134.7 4.5 %all-to-all-start.2 = ((f32[8,8,128]{2,1,0:T(8,128)}), f32[8,8,128]{2,1,0:T(8,128)S(1)}, u32[]{:S(2)}, u32[]{:S(2)}) async-start(f32[8,8,128]{2,1,0:T(8,128)} %copy-done.4), calls=%async_computation.2 | async-start | bytes 65536 | tf_op jit(solution)/shard_map/all_to_all | solution.py:249
  139.2 0.3 collective-permute-start.10
  139.5 1.8 collective-permute-start.14
  141.2 2.5 %convert_element_type.12 = f16[1024,384]{1,0:T(8,128)(2,1)} convert(f32[1024,384]{1,0:T(8,128)} %copy-done) | non-fusion elementwise | flops 393216 | bytes 2359296 | tf_op jit(solution)/shard_map/convert_element_type | solution.py:247
  143.7 2.6 %copy.10 = f16[8,128,384]{1,2,0:T(8,128)(2,1)} copy(f16[8,128,384]{2,1,0:T(8,128)(2,1)} %bitcast.11) | data formatting | bytes 1572864 | tf_op jit(solution)/shard_map/reshape | solution.py:247
  146.3 6.0 %all-to-all-start.1 = ((f16[8,128,384]{1,2,0:T(8,128)(2,1)}), f16[8,128,384]{1,2,0:T(8,128)(2,1)}, u32[]{:S(2)}, u32[]{:S(2)}) async-start(f16[8,128,384]{1,2,0:T(8,128)(2,1)} %copy.10), calls=%async_computation.1 | async-start | bytes 1572864 | tf_op jit(solution)/shard_map/all_to_all | solution.py:248
  152.3 0.5 collective-permute-start.13
  152.8 0.1 collective-permute-start.11
  152.9 0.7 copy-done.7
  153.7 3.4 %collective-permute-done.14.rest_6_ = bf16[2,64,1536]{2,1,0:T(8,128)(2,1)S(1)} collective-permute-done((bf16[2,64,1536]{2,1,0:T(8,128)(2,1)}, bf16[2,64,1536]{2,1,0:T(8,128)(2,1)S(1)}, u32[]{:S(2)}, u32[]{:S(2)}) %collective-permute-start.14) | collective-permute-done | bytes 393248 | tf_op jit(solution)/shard_map/ppermute | solution.py:213
  157.0 0.8 copy-done.9
  157.8 0.9 collective-permute-done.15.rest_7_
  158.8 1.0 copy-done.8
  159.8 1.0 copy-done.10
  160.8 17.4 %context_attend.1 = bf16[512,1536]{1,0:T(8,128)(2,1)} custom-call(s32[4]{0:T(128)S(1)} %pad_add_fusion.at_ref, s32[32]{0:T(128)S(1)} %copy-done.5, bf16[512,1536]{1,0:T(8,128)(2,1)S(1)} %copy-done.6, bf16[2,512,1536]{2,1,0:T(8,128)(2,1)} %kv_ref.3, f32[32,512]{1,0:T(8,128)S(1)} %copy-done.3, bf16[2,64,1536]{2,1,0:T(8,128)(2,1)S(1)} %add.48.rest_0_, ...), custom_call_target="tpu_custom_call" | custom-call | flops 3221225472 | bytes 9437184 | tf_op jit(solution)/shard_map/context_attend/pallas_call | solution.py:173
  178.3 1.3 fusion
  179.5 0.8 copy.11
  (39 shorter events, 0.2 us)
Async XLA Ops:
  3.9 24.6 %collective-permute-start = (bf16[2,64,1536]{2,1,0:T(8,128)(2,1)}, bf16[2,64,1536]{2,1,0:T(8,128)(2,1)S(1)}, u32[]{:S(2)}, u32[]{:S(2)}) collective-permute-start(bf16[2,64,1536]{2,1,0:T(8,128)(2,1)} %get-tuple-element.8), channel_id=1, source_target_pairs={{0,1}} | collective-permute-start | bytes 1179656 | tf_op jit(solution)/shard_map/ppermute | solution.py:207
  6.3 24.3 %collective-permute-start.1 = (bf16[2,64,1536]{2,1,0:T(8,128)(2,1)}, bf16[2,64,1536]{2,1,0:T(8,128)(2,1)}, u32[]{:S(2)}, u32[]{:S(2)}) collective-permute-start(bf16[2,64,1536]{2,1,0:T(8,128)(2,1)} %get-tuple-element.14), channel_id=1, source_target_pairs={{0,2}} | collective-permute-start | bytes 1179656 | tf_op jit(solution)/shard_map/ppermute | solution.py:207
  16.3 97.5 %all-to-all-start = ((bf16[4,2,512,384]{3,2,1,0:T(8,128)(2,1)}), bf16[4,2,512,384]{3,2,1,0:T(8,128)(2,1)S(1)}, u32[]{:S(2)}, u32[]{:S(2)}) async-start(bf16[4,2,512,384]{3,2,1,0:T(8,128)(2,1)} %pack_heads.1), calls=%async_computation | async-start | bytes 6291456 | tf_op jit(solution)/shard_map/all_to_all | solution.py:241
  20.1 39.1 %collective-permute-start.2 = (bf16[2,64,1536]{2,1,0:T(8,128)(2,1)}, bf16[2,64,1536]{2,1,0:T(8,128)(2,1)}, u32[]{:S(2)}, u32[]{:S(2)}) collective-permute-start(bf16[2,64,1536]{2,1,0:T(8,128)(2,1)} %get-tuple-element.13), channel_id=1, source_target_pairs={{0,3}} | collective-permute-start | bytes 1179656 | tf_op jit(solution)/shard_map/ppermute | solution.py:207
  24.4 34.7 %collective-permute-start.3 = (bf16[2,64,1536]{2,1,0:T(8,128)(2,1)}, bf16[2,64,1536]{2,1,0:T(8,128)(2,1)}, u32[]{:S(2)}, u32[]{:S(2)}) collective-permute-start(bf16[2,64,1536]{2,1,0:T(8,128)(2,1)} %get-tuple-element.12), channel_id=1, source_target_pairs={{0,4}} | collective-permute-start | bytes 1179656 | tf_op jit(solution)/shard_map/ppermute | solution.py:207
  26.5 32.7 %collective-permute-start.4 = (bf16[2,64,1536]{2,1,0:T(8,128)(2,1)}, bf16[2,64,1536]{2,1,0:T(8,128)(2,1)}, u32[]{:S(2)}, u32[]{:S(2)}) collective-permute-start(bf16[2,64,1536]{2,1,0:T(8,128)(2,1)} %get-tuple-element.11), channel_id=1, source_target_pairs={{0,5}} | collective-permute-start | bytes 1179656 | tf_op jit(solution)/shard_map/ppermute | solution.py:207
  28.5 34.9 %copy-start.12 = (bf16[2,64,1536]{2,1,0:T(8,128)(2,1)}, bf16[2,64,1536]{2,1,0:T(8,128)(2,1)S(1)}, u32[]{:S(2)}) copy-start(bf16[2,64,1536]{2,1,0:T(8,128)(2,1)S(1)} %collective-permute-done) | copy-start | bytes 1179652
  28.5 34.9 %collective-permute-start.5 = (bf16[2,64,1536]{2,1,0:T(8,128)(2,1)}, bf16[2,64,1536]{2,1,0:T(8,128)(2,1)}, u32[]{:S(2)}, u32[]{:S(2)}) collective-permute-start(bf16[2,64,1536]{2,1,0:T(8,128)(2,1)} %get-tuple-element.10), channel_id=1, source_target_pairs={{0,6}} | collective-permute-start | bytes 1179656 | tf_op jit(solution)/shard_map/ppermute | solution.py:207
  30.5 37.0 %collective-permute-start.6 = (bf16[2,64,1536]{2,1,0:T(8,128)(2,1)}, bf16[2,64,1536]{2,1,0:T(8,128)(2,1)}, u32[]{:S(2)}, u32[]{:S(2)}) collective-permute-start(bf16[2,64,1536]{2,1,0:T(8,128)(2,1)} %get-tuple-element.9), channel_id=1, source_target_pairs={{0,7}} | collective-permute-start | bytes 1179656 | tf_op jit(solution)/shard_map/ppermute | solution.py:207
  32.5 39.0 %copy-start.13 = (s32[16384]{0:T(1024)S(1)}, s32[16384]{0:T(1024)}, u32[]{:S(2)}) copy-start(s32[16384]{0:T(1024)} %param.8) | copy-start | bytes 196612
  32.6 41.0 %copy-start.5 = (s32[32]{0:T(128)S(1)}, s32[32]{0:T(128)}, u32[]{:S(2)}) copy-start(s32[32]{0:T(128)} %len_ref.1) | copy-start | bytes 388
  69.6 7.1 %collective-permute-start.7 = (bf16[2,64,1536]{2,1,0:T(8,128)(2,1)S(1)}, bf16[2,64,1536]{2,1,0:T(8,128)(2,1)}, u32[]{:S(2)}, u32[]{:S(2)}) collective-permute-start(bf16[2,64,1536]{2,1,0:T(8,128)(2,1)S(1)} %add_add_fusion), channel_id=1, source_target_pairs={{0,16},{4,20},{1,17},{5,21},{2,18},{6,22},{3,19},{7,23}} | collective-permute-start | bytes 1179656 | tf_op jit(solution)/shard_map/ppermute | solution.py:211
  77.8 35.3 %collective-permute-start.8 = (bf16[2,64,1536]{2,1,0:T(8,128)(2,1)S(1)}, bf16[2,64,1536]{2,1,0:T(8,128)(2,1)S(1)}, u32[]{:S(2)}, u32[]{:S(2)}) collective-permute-start(bf16[2,64,1536]{2,1,0:T(8,128)(2,1)S(1)} %add.47), channel_id=1, source_target_pairs={{0,8},{4,12},{16,24},{20,28},{1,9},{5,13},{17,25},{21,29},{2,10},{... | collective-permute-start | bytes 1179656 | tf_op jit(solution)/shard_map/ppermute | solution.py:211
  113.1 26.3 %collective-permute-start.12 = (bf16[2,64,1536]{2,1,0:T(8,128)(2,1)S(1)}, bf16[2,64,1536]{2,1,0:T(8,128)(2,1)}, u32[]{:S(2)}, u32[]{:S(2)}) collective-permute-start(bf16[2,64,1536]{2,1,0:T(8,128)(2,1)S(1)} %add.48.rest_0_), channel_id=1, source_target_pairs={{0,4},{4,0},{8,12},{12,8},{16,20},{20,16},{24,28},{28,24},{1,5},{5... | collective-permute-start | bytes 1179656 | tf_op jit(solution)/shard_map/ppermute | solution.py:213
  113.8 1.1 copy-start.1
  115.0 0.8 copy-start.2
  115.8 0.9 copy-start.11
  132.9 1.1 copy-start
  134.1 0.6 copy-start.4
  134.7 11.6 %all-to-all-start.2 = ((f32[8,8,128]{2,1,0:T(8,128)}), f32[8,8,128]{2,1,0:T(8,128)S(1)}, u32[]{:S(2)}, u32[]{:S(2)}) async-start(f32[8,8,128]{2,1,0:T(8,128)} %copy-done.4), calls=%async_computation.2 | async-start | bytes 65536 | tf_op jit(solution)/shard_map/all_to_all | solution.py:249
  139.2 13.6 %collective-permute-start.10 = (bf16[2,64,1536]{2,1,0:T(8,128)(2,1)S(1)}, bf16[2,64,1536]{2,1,0:T(8,128)(2,1)S(1)}, u32[]{:S(2)}, u32[]{:S(2)}) collective-permute-start(bf16[2,64,1536]{2,1,0:T(8,128)(2,1)S(1)} %add.48.rest_0_), channel_id=1, source_target_pairs={{0,2},{1,3},{2,0},{3,1},{4,6},{5,7},{6,4},{7,5},{8,10},{9,11},{10,... | collective-permute-start | bytes 1179656 | tf_op jit(solution)/shard_map/ppermute | solution.py:213
  139.5 17.5 %collective-permute-start.14 = (bf16[2,64,1536]{2,1,0:T(8,128)(2,1)}, bf16[2,64,1536]{2,1,0:T(8,128)(2,1)S(1)}, u32[]{:S(2)}, u32[]{:S(2)}) collective-permute-start(bf16[2,64,1536]{2,1,0:T(8,128)(2,1)} %collective-permute-done.12.rest_4_), channel_id=1, source_target_pairs={{0,2},{1,3},{2,0},{3,1},{4,6},{5,7},{6,4},{7,5},{8,10},{9,11},{10,... | collective-permute-start | bytes 1179656 | tf_op jit(solution)/shard_map/ppermute | solution.py:213
  143.7 15.1 %copy-start.3 = (f32[32,512]{1,0:T(8,128)S(1)}, f32[32,512]{1,0:T(8,128)}, u32[]{:S(2)}) copy-start(f32[32,512]{1,0:T(8,128)} %fusion.2.bias_ref) | copy-start | bytes 196612
  143.7 15.1 %copy-start.6 = (bf16[512,1536]{1,0:T(8,128)(2,1)S(1)}, bf16[512,1536]{1,0:T(8,128)(2,1)}, u32[]{:S(2)}) copy-start(bf16[512,1536]{1,0:T(8,128)(2,1)} %q_ref.1) | copy-start | bytes 4718596
  146.3 31.9 %all-to-all-start.1 = ((f16[8,128,384]{1,2,0:T(8,128)(2,1)}), f16[8,128,384]{1,2,0:T(8,128)(2,1)}, u32[]{:S(2)}, u32[]{:S(2)}) async-start(f16[8,128,384]{1,2,0:T(8,128)(2,1)} %copy.10), calls=%async_computation.1 | async-start | bytes 1572864 | tf_op jit(solution)/shard_map/all_to_all | solution.py:248
  152.3 5.5 %collective-permute-start.9 = (bf16[2,64,1536]{2,1,0:T(8,128)(2,1)S(1)}, bf16[2,64,1536]{2,1,0:T(8,128)(2,1)S(1)}, u32[]{:S(2)}, u32[]{:S(2)}) collective-permute-start(bf16[2,64,1536]{2,1,0:T(8,128)(2,1)S(1)} %add.48.rest_0_), channel_id=1, source_target_pairs={{0,1},{1,0},{2,3},{3,2},{4,5},{5,4},{6,7},{7,6},{8,9},{9,8},{10,11... | collective-permute-start | bytes 1179656 | tf_op jit(solution)/shard_map/ppermute | solution.py:213
  152.3 5.5 %collective-permute-start.13 = (bf16[2,64,1536]{2,1,0:T(8,128)(2,1)}, bf16[2,64,1536]{2,1,0:T(8,128)(2,1)S(1)}, u32[]{:S(2)}, u32[]{:S(2)}) collective-permute-start(bf16[2,64,1536]{2,1,0:T(8,128)(2,1)} %collective-permute-done.12.rest_4_), channel_id=1, source_target_pairs={{0,1},{1,0},{2,3},{3,2},{4,5},{5,4},{6,7},{7,6},{8,9},{9,8},{10,11... | collective-permute-start | bytes 1179656 | tf_op jit(solution)/shard_map/ppermute | solution.py:213
  152.8 5.0 %collective-permute-start.11 = (bf16[2,64,1536]{2,1,0:T(8,128)(2,1)S(1)}, bf16[2,64,1536]{2,1,0:T(8,128)(2,1)S(1)}, u32[]{:S(2)}, u32[]{:S(2)}) collective-permute-start(bf16[2,64,1536]{2,1,0:T(8,128)(2,1)S(1)} %collective-permute-done.10.rest_2_), channel_id=1, source_target_pairs={{0,1},{1,0},{2,3},{3,2},{4,5},{5,4},{6,7},{7,6},{8,9},{9,8},{10,11... | collective-permute-start | bytes 1179656 | tf_op jit(solution)/shard_map/ppermute | solution.py:213
  152.9 0.7 copy-start.7
  157.0 1.7 collective-permute-start.15
  157.0 0.8 copy-start.9
  158.8 1.0 copy-start.8
  159.8 1.0 copy-start.10

commit v2 on v1

v2 whole, which is shorter than its diff:
```python
import functools
import math

import jax
import jax.numpy as jnp
from jax import lax
from jax.experimental import pallas as pl
from jax.experimental.pallas import tpu as pltpu
from jax.sharding import PartitionSpec as P

HSZ = 128
NAMB = 512
NEG = -1e30
FLOOR = -2000.0
EXTRA = 16
C2 = math.log2(math.e) / math.sqrt(HSZ)
BOTH = ("hst", "grp")


def dot_t(a, b):
    return lax.dot_general(a, b, (((1,), (1,)), ((), ())), preferred_element_type=jnp.float32)


def dot(a, b):
    return lax.dot_general(a, b, (((1,), (0,)), ((), ())), preferred_element_type=jnp.float32)


def softmax_mix(tiles):
    results = []
    for scores, values in tiles:
        top = functools.reduce(jnp.maximum, [jnp.max(s, axis=-1, keepdims=True) for s in scores])
        base = top * C2
        weights = [jnp.exp2(s * C2 - base) for s in scores]
        total = functools.reduce(jnp.add, [jnp.sum(w, axis=-1, keepdims=True) for w in weights])
        mixed = functools.reduce(jnp.add, [dot(w.astype(jnp.bfloat16), v) for w, v in zip(weights, values)])
        results.append((base, total, mixed))
    return results


def pack_kernel(groups, kv_ref, out_ref, sems):
    part = out_ref.shape[3]
    copies = [
        pltpu.make_async_copy(kv_ref.at[s, :, pl.ds(g * part, part)], out_ref.at[g, s], sems.at[g, s])
        for g in range(groups)
        for s in range(2)
    ]
    for copy in copies:
        copy.start()
    for copy in copies:
        copy.wait()


def pack(kv, groups):
    _, rows, width = kv.shape
    return pl.pallas_call(
        functools.partial(pack_kernel, groups),
        in_specs=[pl.BlockSpec(memory_space=pl.ANY)],
        out_specs=pl.BlockSpec(memory_space=pl.ANY),
        out_shape=jax.ShapeDtypeStruct((groups, 2, rows, width // groups), kv.dtype),
        scratch_shapes=[pltpu.SemaphoreType.DMA((groups, 2))],
        cost_estimate=pl.CostEstimate(flops=0, bytes_accessed=4 * kv.size, transcendentals=0),
        name="pack_heads",
    )(kv)


def suffix_kernel(groups, sub, share, at_ref, q_ref, kv_ref, sk_ref, bias_ref, out_ref):
    host = at_ref[0]
    step = pl.program_id(0)
    tile = q_ref.shape[0]
    bias = [bias_ref[pl.ds(host * groups + g, 1), :] for g in range(groups)]
    tiles = []
    for first in range(0, tile, sub):
        q = q_ref[first : first + sub, :]
        scores = [dot_t(q, kv_ref[g, 0]) + bias[g] for g in range(groups)]
        s = dot_t(q, sk_ref[0])
        qpos = step * tile + first + lax.broadcasted_iota(jnp.int32, s.shape, 0)
        spos = host * share + lax.broadcasted_iota(jnp.int32, s.shape, 1)
        scores.append(jnp.where(spos <= qpos, s, NEG))
        tiles.append((scores, [kv_ref[g, 1] for g in range(groups)] + [sk_ref[1]]))
    for number, (base, total, mixed) in enumerate(softmax_mix(tiles)):
        first = number * sub
        n = mixed / total
        size = jnp.max(jnp.abs(n), axis=-1, keepdims=True)
        shift = jnp.clip(jnp.floor(jnp.log2(size)), -100.0, 100.0)
        n = n * jnp.exp2(-shift)
        level = jnp.maximum(base + jnp.log2(total), FLOOR)
        whole = jnp.floor(level)
        rest = jnp.exp2(level - whole)
        coarse = jnp.round(rest * 512.0) * (1.0 / 512.0)
        fine = (rest - coarse) * 1024.0
        lane = lax.broadcasted_iota(jnp.int32, (sub, HSZ), 1)
        stats = jnp.where(lane == 0, whole, jnp.where(lane == 1, coarse, jnp.where(lane == 2, fine, shift)))
        turned = stats.T
        for c in range(sub // share):
            chunk = first // share + c
            out_ref[chunk, :share, :] = n[c * share : (c + 1) * share, :]
            out_ref[chunk, share : share + EXTRA, :share] = turned[:EXTRA, c * share : (c + 1) * share]


def suffix_attend(at, q, kv, sk, bias):
    groups, _, rows, width = kv.shape
    total_q = q.shape[0]
    share = sk.shape[1]
    heads = width // HSZ
    tile, sub = min(512, total_q), min(256, total_q)
    seen = groups * rows + share
    return pl.pallas_call(
        functools.partial(suffix_kernel, groups, sub, share),
        grid_spec=pltpu.PrefetchScalarGridSpec(
            num_scalar_prefetch=1,
            grid=(total_q // tile, heads),
            in_specs=[
                pl.BlockSpec((tile, HSZ), lambda i, h, at: (i, h)),
                pl.BlockSpec((groups, 2, rows, HSZ), lambda i, h, at: (0, 0, 0, h)),
                pl.BlockSpec((2, share, HSZ), lambda i, h, at: (0, 0, h)),
                pl.BlockSpec(bias.shape, lambda i, h, at: (0, 0)),
            ],
            out_specs=pl.BlockSpec((tile // share, share + EXTRA, HSZ), lambda i, h, at: (i, 0, h)),
        ),
        out_shape=jax.ShapeDtypeStruct((total_q // share, share + EXTRA, width), jnp.float32),
        compiler_params=pltpu.CompilerParams(vmem_limit_bytes=48 * 1024 * 1024),
        cost_estimate=pl.CostEstimate(
            flops=8 * total_q * seen * width,
            bytes_accessed=2 * kv.size + 2 * q.size + 4 * q.size,
            transcendentals=total_q * seen * heads,
        ),
        name="suffix_attend",
    )(at, q, kv, sk, bias)


def combine_kernel(in_ref, out_ref):
    hosts, tall, _ = in_ref.shape
    share = tall - EXTRA
    stats = in_ref[:, share:, :].reshape(hosts * EXTRA, HSZ).T[:share, :]
    column = lambda g, k: stats[:, g * EXTRA + k : g * EXTRA + k + 1]
    highest = functools.reduce(jnp.maximum, [column(g, 0) for g in range(hosts)])
    total = 0.0
    mixed = 0.0
    for g in range(hosts):
        weight = jnp.exp2(column(g, 0) - highest) * (column(g, 1) + column(g, 2) * (1.0 / 1024.0))
        total = total + weight
        mixed = mixed + (weight * jnp.exp2(column(g, 3))) * in_ref[g, :share, :]
    out_ref[...] = (mixed / total).astype(out_ref.dtype)


def combine(parts):
    hosts, tall, width = parts.shape
    return pl.pallas_call(
        combine_kernel,
        grid=(width // HSZ,),
        in_specs=[pl.BlockSpec((hosts, tall, HSZ), lambda h: (0, 0, h))],
        out_specs=pl.BlockSpec((tall - EXTRA, HSZ), lambda h: (0, h)),
        out_shape=jax.ShapeDtypeStruct((tall - EXTRA, width), jnp.bfloat16),
        cost_estimate=pl.CostEstimate(flops=2 * parts.size, bytes_accessed=4 * parts.size, transcendentals=0),
        name="combine_groups",
    )(parts)


def context_kernel(at_ref, len_ref, q_ref, kv_ref, bias_ref, anchor_ref, *rest):
    out_ref, diag_ref = rest[-2:]
    block = at_ref[0]
    rows = q_ref.shape[0]
    half = rows // 2
    own = bias_ref[pl.ds(block, 1), :]

    @pl.when(pl.program_id(0) == 0)
    def _():
        row = lax.broadcasted_iota(jnp.int32, (half, half), 0)
        col = lax.broadcasted_iota(jnp.int32, (half, half), 1)
        for t in range(2):
            ok = own[:, t * half : (t + 1) * half]
            diag_ref[t] = jnp.where(col == row, 0.0, jnp.where(col < row, ok, NEG))

    anchor_keys = anchor_ref[:, 0].reshape(rows, HSZ)
    anchor_values = anchor_ref[:, 1].reshape(rows, HSZ)
    anchor_bias = jnp.where(block > 0, bias_ref[0:1, :], NEG)
    keys, values = kv_ref[0], kv_ref[1]
    tiles = []
    for t in range(2):
        q = q_ref[t * half : (t + 1) * half, :]
        scores = [dot_t(q, anchor_keys) + anchor_bias]
        mix = [anchor_values]
        if t == 1:
            scores.append(dot_t(q, keys[:half]) + own[:, :half])
            mix.append(values[:half])
        scores.append(dot_t(q, keys[t * half : (t + 1) * half]) + diag_ref[t])
        mix.append(values[t * half : (t + 1) * half])
        tiles.append((scores, mix))
    for t, (_, total, mixed) in enumerate(softmax_mix(tiles)):
        place = t * half + lax.broadcasted_iota(jnp.int32, mixed.shape, 0)
        out = jnp.where(place < len_ref[block], mixed / total, 0.0)
        out_ref[t * half : (t + 1) * half, :] = out.astype(out_ref.dtype)


def context_attend(at, lengths, q, kv, bias, anchor, before):
    rows, width = q.shape
    hosts, _, part, group_width = anchor.shape
    heads = group_width // HSZ
    half = rows // 2
    column = lambda h, at, n: (0, at[1] * heads + h)
    both = lambda h, at, n: (0, 0, at[1] * heads + h)
    more = [] if before is None else [before]
    return pl.pallas_call(
        context_kernel,
        grid_spec=pltpu.PrefetchScalarGridSpec(
            num_scalar_prefetch=2,
            grid=(heads,),
            in_specs=[
                pl.BlockSpec((rows, HSZ), column),
                pl.BlockSpec((2, rows, HSZ), both),
                pl.BlockSpec(bias.shape, lambda h, *_: (0, 0)),
                pl.BlockSpec((hosts, 2, part, HSZ), lambda h, *_: (0, 0, 0, h)),
            ]
            + [pl.BlockSpec(memory_space=pl.ANY) for _ in more],
            out_specs=pl.BlockSpec((rows, HSZ), column),
            scratch_shapes=[pltpu.VMEM((2, half, half), jnp.float32)],
        ),
        out_shape=jax.ShapeDtypeStruct((rows, width), q.dtype),
        input_output_aliases={6: 0} if more else {},
        compiler_params=pltpu.CompilerParams(vmem_limit_bytes=48 * 1024 * 1024),
        cost_estimate=pl.CostEstimate(
            flops=8 * rows * rows * group_width,
            bytes_accessed=12 * rows * group_width,
            transcendentals=2 * rows * rows * heads,
        ),
        name="context_attend",
    )(at, lengths, q, kv, bias, anchor, *more)


def gather_rows(x, axis, n):
    return lax.all_to_all(jnp.broadcast_to(x[None], (n, *x.shape)), axis, split_axis=0, concat_axis=0, tiled=True)


def spread_anchor(kv, hosts, groups):
    _, rows, width = kv.shape
    part, wide = rows // hosts, width // groups
    first = (lax.axis_index("hst") == 0) & (lax.axis_index("grp") == 0)
    slab = jnp.where(first, kv[:, :part], 0.0)
    for h in range(1, hosts):
        slab = slab + lax.ppermute(kv[:, h * part : (h + 1) * part], BOTH, [(0, h * groups)])
    piece = slab[:, :, :wide]
    for g in range(1, groups):
        piece = piece + lax.ppermute(slab[:, :, g * wide : (g + 1) * wide], "grp", [(0, g)])
    return gather_rows(piece, "hst", hosts)


def per_device(queries, keys_values, token_ids, lengths, suffix_queries, suffix_kv):
    hosts, groups = lax.axis_size("hst"), lax.axis_size("grp")
    host, group = lax.axis_index("hst"), lax.axis_index("grp")
    rows = queries.shape[0]
    swapped = lax.all_to_all(pack(keys_values, groups), "grp", split_axis=0, concat_axis=0, tiled=True)
    gathered = gather_rows(suffix_queries, "hst", hosts).reshape(-1, suffix_queries.shape[1])
    held = {0: spread_anchor(keys_values, hosts, groups)}
    k = groups // 2
    while k >= 1:
        for have in list(held):
            held[have ^ k] = lax.ppermute(held[have], "grp", [(g, g ^ k) for g in range(groups)])
        k //= 2
    seen = (token_ids.reshape(-1, rows) >= NAMB) & (jnp.arange(rows)[None, :] < lengths[:, None])
    bias = jnp.where(seen, 0.0, NEG).astype(jnp.float32)
    parts = suffix_attend(jnp.stack([host]).astype(jnp.int32), gathered, swapped, suffix_kv, bias)
    parts = lax.all_to_all(parts.astype(jnp.float16), "hst", split_axis=0, concat_axis=0, tiled=True)
    context_out = None
    for k in range(groups):
        at = jnp.stack([host * groups + group, group ^ k]).astype(jnp.int32)
        context_out = context_attend(at, lengths, queries, keys_values, bias, held[k], context_out)
    return (context_out, combine(parts.astype(jnp.float32)))


def solution(mesh):
    return jax.shard_map(
        per_device,
        mesh=mesh,
        in_specs=(
            P(("hst", "grp"), None),
            P(None, ("hst", "grp"), None),
            P(),
            P(),
            P("hst", "grp"),
            P(None, "hst", "grp"),
        ),
        out_specs=(P(("hst", "grp"), None), P("hst", "grp")),
        check_vma=False,
    )
```

time: 181 us -> 251 us (1.39)
  Pallas kernels: 39.7 us -> 135 us
  blocking collectives: 33.9 us -> 0 us
  waiting for transfers between devices: 41 us -> 59.6 us
  local copies, waits for them, and re-layouts: 16.2 us -> 9.83 us
  other arithmetic: 9.12 us -> 5.15 us
    pallas_call x2 -> x6, Pallas kernels: 23.5 us -> 121 us  [the longest x1 96.5 us: pack(): pl.pallas_call(functools.partial(pack_kernel, groups), in_specs=[pl.Block...]
    all_to_all x1, waiting for transfers between devices: 0.01 us -> 35.2 us  [per_device(): lax.all_to_all(pack(keys_values, groups), 'grp', split_axis=0, concat_axi...]
    all_gather x1 -> x0, blocking collectives: 33.9 us -> none  [per_device(): gathered = lax.all_gather(suffix_queries, 'hst', axis=0, tiled=True)]
    ppermute x16 -> x13, waiting for transfers between devices: 41 us -> 24.4 us  [the longest x7 22.2 us: spread_anchor(): lax.ppermute(kv[:, h * part:(h + 1) * part], BOTH, [(0, h * groups)])]
    ppermute x16 -> x13, starting transfers between devices: 25.4 us -> 19.2 us  [the longest x7 12.8 us: spread_anchor(): lax.ppermute(kv[:, h * part:(h + 1) * part], BOTH, [(0, h * groups)])]
    all_to_all x2 -> x3, starting transfers between devices: 10.5 us -> 16 us  [the longest x2 9.9 us: gather_rows(): lax.all_to_all(jnp.broadcast_to(x[None], (n, *x.shape)), axis, split_axis...]
    unnamed x29 -> x20, local copies, waits for them, and re-layouts: 8.93 us -> 4.65 us
    reshape x1 -> x0, local copies, waits for them, and re-layouts: 2.62 us -> none  [per_device(): parts = parts.astype(jnp.float16).reshape(hosts, share, -1)]
  transfers between devices with their start and end apart: 19 -> 17, of which waited for: 6 -> 8; matrix products, arithmetic and copies ran while one was open for 7% -> 1% of each run, Pallas kernels for 22% -> 52%
where the time goes in v2:
time: 251 us; the launch traced here: 250 us
  Pallas kernels  135 us (54%)
  waiting for transfers between devices  59.6 us (24%)
  starting transfers between devices  38.9 us (15%)
  local copies, waits for them, and re-layouts  9.83 us (4%)
  other arithmetic  5.15 us (2%)
    pallas_call x1, Pallas kernels, pack(): pl.pallas_call(functools.partial(pack_kernel, groups), in_specs=[pl.Block...  96.5 us
    all_to_all x1, waiting for transfers between devices, per_device(): lax.all_to_all(pack(keys_values, groups), 'grp', split_axis=0, concat_axi...  35.2 us
    ppermute x7, waiting for transfers between devices, spread_anchor(): lax.ppermute(kv[:, h * part:(h + 1) * part], BOTH, [(0, h * groups)])  22.2 us
    pallas_call x4, Pallas kernels, context_attend(): pl.pallas_call(context_kernel, grid_spec=pltpu.PrefetchScalarGridSpec(num...  19.5 us
    pallas_call x1, Pallas kernels, suffix_attend(): pl.pallas_call(functools.partial(suffix_kernel, groups, sub, share), grid...  14 us
    ppermute x7, starting transfers between devices, spread_anchor(): lax.ppermute(kv[:, h * part:(h + 1) * part], BOTH, [(0, h * groups)])  12.8 us
    all_to_all x2, starting transfers between devices, gather_rows(): lax.all_to_all(jnp.broadcast_to(x[None], (n, *x.shape)), axis, split_axis...  9.9 us
    all_to_all x1, starting transfers between devices, per_device(): lax.all_to_all(parts.astype(jnp.float16), 'hst', split_axis=0, concat_axi...  6.13 us
  transfers between devices with their start and end apart: 17, of which 8 were waited for; matrix products, arithmetic and copies ran while one was open for 1% of the time, Pallas kernels for 52%

profile of v2, /device:TPU:0, one launch (start us, length us, event | category | flops | bytes accessed | tf_op | source)
XLA Modules:
  0.0 249.7 jit_solution(16462925629019143303)
XLA Ops:
  0.6 3.1 %fusion.4 = (bf16[2,64,1536]{2,1,0:T(8,128)(2,1)S(1)}, bf16[2,64,1536]{2,1,0:T(8,128)(2,1)}, bf16[2,64,1536]{2,1,0:T(8,128)(2,1)}, bf16[2,64,1536]{2,1,0:T(8,128...) fusion(bf16[2,512,1536]{2,1,0:T(8,128)(2,1)} %kv_ref.9), kind=kLoop, calls=%fused_computation.12 | loop fusion | bytes 5505024 | tf_op jit(solution)/shard_map/slice | solution.py:240
  3.7 4.9 %collective-permute-start = (bf16[2,64,1536]{2,1,0:T(8,128)(2,1)S(1)}, bf16[2,64,1536]{2,1,0:T(8,128)(2,1)S(1)}, u32[]{:S(2)}, u32[]{:S(2)}) collective-permute-start(bf16[2,64,1536]{2,1,0:T(8,128)(2,1)S(1)} %get-tuple-element.2), channel_id=1, source_target_pairs={{0,4}} | collective-permute-start | bytes 1179656 | tf_op jit(solution)/shard_map/ppermute | solution.py:240
  8.6 1.3 collective-permute-start.1
  9.9 1.3 collective-permute-start.2
  11.2 1.3 collective-permute-start.3
  12.5 1.3 collective-permute-start.4
  13.9 1.3 collective-permute-start.5
  15.2 1.3 collective-permute-start.6
  16.5 1.0 broadcast_in_dim.30
  17.5 3.5 %all-to-all-start.1 = ((bf16[8,128,384]{2,1,0:T(8,128)(2,1)}), bf16[8,128,384]{2,1,0:T(8,128)(2,1)S(1)}, u32[]{:S(2)}, u32[]{:S(2)}) async-start(bf16[8,128,384]{2,1,0:T(8,128)(2,1)} %broadcast_in_dim.30), calls=%async_computation.1 | async-start | bytes 1572864 | tf_op jit(solution)/shard_map/all_to_all | solution.py:231
  21.1 1.4 collective-permute-done.2
  22.4 8.2 %collective-permute-done.3 = bf16[2,64,1536]{2,1,0:T(8,128)(2,1)S(1)} collective-permute-done((bf16[2,64,1536]{2,1,0:T(8,128)(2,1)}, bf16[2,64,1536]{2,1,0:T(8,128)(2,1)S(1)}, u32[]{:S(2)}, u32[]{:S(2)}) %collective-permute-start.3) | collective-permute-done | bytes 393248 | tf_op jit(solution)/shard_map/ppermute | solution.py:240
  30.7 4.2 %collective-permute-done.4 = bf16[2,64,1536]{2,1,0:T(8,128)(2,1)S(1)} collective-permute-done((bf16[2,64,1536]{2,1,0:T(8,128)(2,1)}, bf16[2,64,1536]{2,1,0:T(8,128)(2,1)S(1)}, u32[]{:S(2)}, u32[]{:S(2)}) %collective-permute-start.4) | collective-permute-done | bytes 393248 | tf_op jit(solution)/shard_map/ppermute | solution.py:240
  34.9 4.2 %collective-permute-done.5 = bf16[2,64,1536]{2,1,0:T(8,128)(2,1)S(1)} collective-permute-done((bf16[2,64,1536]{2,1,0:T(8,128)(2,1)}, bf16[2,64,1536]{2,1,0:T(8,128)(2,1)S(1)}, u32[]{:S(2)}, u32[]{:S(2)}) %collective-permute-start.5) | collective-permute-done | bytes 393248 | tf_op jit(solution)/shard_map/ppermute | solution.py:240
  39.1 4.2 %collective-permute-done.6 = bf16[2,64,1536]{2,1,0:T(8,128)(2,1)S(1)} collective-permute-done((bf16[2,64,1536]{2,1,0:T(8,128)(2,1)}, bf16[2,64,1536]{2,1,0:T(8,128)(2,1)S(1)}, u32[]{:S(2)}, u32[]{:S(2)}) %collective-permute-start.6) | collective-permute-done | bytes 393248 | tf_op jit(solution)/shard_map/ppermute | solution.py:240
  43.3 1.1 add_add_fusion
  44.5 1.3 collective-permute-start.7
  45.8 1.3 collective-permute-start.8
  47.1 1.3 collective-permute-start.9
  48.4 0.9 collective-permute-done.8
  49.3 1.3 collective-permute-done.9
  50.6 1.1 broadcast_in_dim.29
  51.7 0.1 copy-done.4
  51.8 6.4 %all-to-all-start = ((bf16[8,2,64,384]{3,2,1,0:T(8,128)(2,1)}), bf16[8,2,64,384]{3,2,1,0:T(8,128)(2,1)S(1)}, u32[]{:S(2)}, u32[]{:S(2)}) async-start(bf16[8,2,64,384]{3,2,1,0:T(8,128)(2,1)} %broadcast_in_dim.29), calls=%async_computation | async-start | bytes 1572864 | tf_op jit(solution)/shard_map/all_to_all | solution.py:231
  58.2 96.5 %pack_heads.1 = bf16[4,2,512,384]{3,2,1,0:T(8,128)(2,1)} custom-call(bf16[2,512,1536]{2,1,0:T(8,128)(2,1)} %kv_ref.9), custom_call_target="tpu_custom_call" | custom-call | bytes 6291456 | tf_op jit(solution)/shard_map/pack_heads/pallas_call | solution.py:55
  154.6 0.0 copy-start.9
  154.7 0.9 copy-done.2
  155.6 3.7 %all-to-all-start.2 = ((bf16[4,2,512,384]{3,2,1,0:T(8,128)(2,1)}), bf16[4,2,512,384]{3,2,1,0:T(8,128)(2,1)S(1)}, u32[]{:S(2)}, u32[]{:S(2)}) async-start(bf16[4,2,512,384]{3,2,1,0:T(8,128)(2,1)} %pack_heads.1), calls=%async_computation.2 | async-start | bytes 6291456 | tf_op jit(solution)/shard_map/all_to_all | solution.py:251
  159.4 0.1 fusion.3.bias_ref
  159.4 2.0 collective-permute-start.10
  161.5 35.2 %all-to-all-done.2.kv_ref = bf16[4,2,512,384]{3,2,1,0:T(8,128)(2,1)S(1)} async-done(((bf16[4,2,512,384]{3,2,1,0:T(8,128)(2,1)}), bf16[4,2,512,384]{3,2,1,0:T(8,128)(2,1)S(1)}, u32[]{:S(2)}, u32[]{:S(2)}) %all-to-all-start.2) | async-done | bytes 3145760 | tf_op jit(solution)/shard_map/all_to_all | solution.py:251
  196.6 1.1 copy-done.5
  197.8 14.0 %suffix_attend.1 = f32[8,144,384]{2,1,0:T(8,128)S(1)} custom-call(s32[1]{0:T(128)} %bitcast.5.at_ref, bf16[1024,384]{1,0:T(8,128)(2,1)S(1)} %bitcast.7, bf16[4,2,512,384]{3,2,1,0:T(8,128)(2,1)S(1)} %all-to-all-done.2.kv_ref, bf16[2,128,384]{2,1,0:T(8,128)(2,1)S(1)} %copy-done.7, f32[32,512]{1,0:T(8,128)S(1)} %fusion.3.bias_ref), custom_call_target="tpu_custom_call" | custom-call | flops 6845104128 | bytes 5505024 | tf_op jit(solution)/shard_map/suffix_attend/pallas_call | solution.py:107
  211.8 1.1 convert_element_type.8
  212.8 6.1 %all-to-all-start.3 = ((f16[8,144,384]{2,1,0:T(8,128)(2,1)}), f16[8,144,384]{2,1,0:T(8,128)(2,1)}, u32[]{:S(2)}, u32[]{:S(2)}) async-start(f16[8,144,384]{2,1,0:T(8,128)(2,1)} %convert_element_type.8), calls=%async_computation.3 | async-start | bytes 1769472 | tf_op jit(solution)/shard_map/all_to_all | solution.py:262
  219.0 0.5 collective-permute-start.11
  219.5 0.1 pad_add_fusion.3.at_ref
  219.6 0.1 pad_add_fusion.2.at_ref
  219.6 0.1 pad_add_fusion.1.at_ref
  219.7 0.1 pad_add_fusion.at_ref
  219.8 1.4 copy-done.1
  221.2 1.1 copy-done.3
  222.3 4.3 %context_attend.4.rest_0_ = bf16[512,1536]{1,0:T(8,128)(2,1)} custom-call(s32[2]{0:T(128)S(1)} %pad_add_fusion.3.at_ref, s32[32]{0:T(128)S(1)} %copy-done.6, bf16[512,1536]{1,0:T(8,128)(2,1)S(1)} %copy-done.1, bf16[2,512,1536]{2,1,0:T(8,128)(2,1)S(1)} %copy-done, f32[32,512]{1,0:T(8,128)S(1)} %fusion.3.bias_ref, bf16[8,2,64,384]{3,2,1,0:T(8,128)(2,1)S(1)} %copy-done.3), custom_call_target="tpu_custom_call" | custom-call | flops 805306368 | bytes 2359296 | tf_op jit(solution)/shard_map/context_attend/pallas_call | solution.py:203
  226.6 5.1 %context_attend.5.rest_0_ = bf16[512,1536]{1,0:T(8,128)(2,1)} custom-call(s32[2]{0:T(128)S(1)} %pad_add_fusion.2.at_ref, s32[32]{0:T(128)S(1)} %copy-done.6, bf16[512,1536]{1,0:T(8,128)(2,1)S(1)} %copy-done.1, bf16[2,512,1536]{2,1,0:T(8,128)(2,1)S(1)} %copy-done, f32[32,512]{1,0:T(8,128)S(1)} %fusion.3.bias_ref, ...), custom_call_target="tpu_custom_call", output_to_operand_aliasing={{}: (6, {})} | custom-call | flops 805306368 | bytes 2359296 | tf_op jit(solution)/shard_map/context_attend/pallas_call | solution.py:203
  231.7 5.1 %context_attend.6.rest_0_ = bf16[512,1536]{1,0:T(8,128)(2,1)} custom-call(s32[2]{0:T(128)S(1)} %pad_add_fusion.1.at_ref, s32[32]{0:T(128)S(1)} %copy-done.6, bf16[512,1536]{1,0:T(8,128)(2,1)S(1)} %copy-done.1, bf16[2,512,1536]{2,1,0:T(8,128)(2,1)S(1)} %copy-done, f32[32,512]{1,0:T(8,128)S(1)} %fusion.3.bias_ref, ...), custom_call_target="tpu_custom_call", output_to_operand_aliasing={{}: (6, {})} | custom-call | flops 805306368 | bytes 2359296 | tf_op jit(solution)/shard_map/context_attend/pallas_call | solution.py:203
  236.8 5.1 %context_attend.7 = bf16[512,1536]{1,0:T(8,128)(2,1)} custom-call(s32[2]{0:T(128)S(1)} %pad_add_fusion.at_ref, s32[32]{0:T(128)S(1)} %copy-done.6, bf16[512,1536]{1,0:T(8,128)(2,1)S(1)} %copy-done.1, bf16[2,512,1536]{2,1,0:T(8,128)(2,1)S(1)} %copy-done, f32[32,512]{1,0:T(8,128)S(1)} %fusion.3.bias_ref, ...), custom_call_target="tpu_custom_call", output_to_operand_aliasing={{}: (6, {})} | custom-call | flops 805306368 | bytes 2359296 | tf_op jit(solution)/shard_map/context_attend/pallas_call | solution.py:203
  241.8 2.5 %convert_element_type.9.in_ref = f32[8,144,384]{2,1,0:T(8,128)} convert(f16[8,144,384]{2,1,0:T(8,128)(2,1)} %all-to-all-done.3) | non-fusion elementwise | flops 442368 | bytes 2654208 | tf_op jit(solution)/shard_map/convert_element_type | solution.py:267
  244.3 5.4 %combine_groups.1 = bf16[128,384]{1,0:T(8,128)(2,1)} custom-call(f32[8,144,384]{2,1,0:T(8,128)} %convert_element_type.9.in_ref), custom_call_target="tpu_custom_call" | custom-call | flops 884736 | bytes 1769472 | tf_op jit(solution)/shard_map/combine_groups/pallas_call | solution.py:148
  (28 shorter events, 0.2 us)
Async XLA Ops:
  0.6 15.9 %copy-start.8 = (bf16[128,384]{1,0:T(8,128)(2,1)S(1)}, bf16[128,384]{1,0:T(8,128)(2,1)}, u32[]{:S(2)}) copy-start(bf16[128,384]{1,0:T(8,128)(2,1)} %param.10) | copy-start | bytes 294916
  3.7 10.2 %collective-permute-start = (bf16[2,64,1536]{2,1,0:T(8,128)(2,1)S(1)}, bf16[2,64,1536]{2,1,0:T(8,128)(2,1)S(1)}, u32[]{:S(2)}, u32[]{:S(2)}) collective-permute-start(bf16[2,64,1536]{2,1,0:T(8,128)(2,1)S(1)} %get-tuple-element.2), channel_id=1, source_target_pairs={{0,4}} | collective-permute-start | bytes 1179656 | tf_op jit(solution)/shard_map/ppermute | solution.py:240
  8.6 6.6 %collective-permute-start.1 = (bf16[2,64,1536]{2,1,0:T(8,128)(2,1)S(1)}, bf16[2,64,1536]{2,1,0:T(8,128)(2,1)S(1)}, u32[]{:S(2)}, u32[]{:S(2)}) collective-permute-start(bf16[2,64,1536]{2,1,0:T(8,128)(2,1)S(1)} %get-tuple-element.8), channel_id=1, source_target_pairs={{0,8}} | collective-permute-start | bytes 1179656 | tf_op jit(solution)/shard_map/ppermute | solution.py:240
  9.9 12.5 %collective-permute-start.2 = (bf16[2,64,1536]{2,1,0:T(8,128)(2,1)}, bf16[2,64,1536]{2,1,0:T(8,128)(2,1)S(1)}, u32[]{:S(2)}, u32[]{:S(2)}) collective-permute-start(bf16[2,64,1536]{2,1,0:T(8,128)(2,1)} %get-tuple-element.7), channel_id=1, source_target_pairs={{0,12}} | collective-permute-start | bytes 1179656 | tf_op jit(solution)/shard_map/ppermute | solution.py:240
  11.2 19.4 %collective-permute-start.3 = (bf16[2,64,1536]{2,1,0:T(8,128)(2,1)}, bf16[2,64,1536]{2,1,0:T(8,128)(2,1)S(1)}, u32[]{:S(2)}, u32[]{:S(2)}) collective-permute-start(bf16[2,64,1536]{2,1,0:T(8,128)(2,1)} %get-tuple-element.6), channel_id=1, source_target_pairs={{0,16}} | collective-permute-start | bytes 1179656 | tf_op jit(solution)/shard_map/ppermute | solution.py:240
  12.5 22.3 %collective-permute-start.4 = (bf16[2,64,1536]{2,1,0:T(8,128)(2,1)}, bf16[2,64,1536]{2,1,0:T(8,128)(2,1)S(1)}, u32[]{:S(2)}, u32[]{:S(2)}) collective-permute-start(bf16[2,64,1536]{2,1,0:T(8,128)(2,1)} %get-tuple-element.5), channel_id=1, source_target_pairs={{0,20}} | collective-permute-start | bytes 1179656 | tf_op jit(solution)/shard_map/ppermute | solution.py:240
  13.9 25.2 %collective-permute-start.5 = (bf16[2,64,1536]{2,1,0:T(8,128)(2,1)}, bf16[2,64,1536]{2,1,0:T(8,128)(2,1)S(1)}, u32[]{:S(2)}, u32[]{:S(2)}) collective-permute-start(bf16[2,64,1536]{2,1,0:T(8,128)(2,1)} %get-tuple-element.4), channel_id=1, source_target_pairs={{0,24}} | collective-permute-start | bytes 1179656 | tf_op jit(solution)/shard_map/ppermute | solution.py:240
  15.2 28.1 %collective-permute-start.6 = (bf16[2,64,1536]{2,1,0:T(8,128)(2,1)}, bf16[2,64,1536]{2,1,0:T(8,128)(2,1)S(1)}, u32[]{:S(2)}, u32[]{:S(2)}) collective-permute-start(bf16[2,64,1536]{2,1,0:T(8,128)(2,1)} %get-tuple-element.3), channel_id=1, source_target_pairs={{0,28}} | collective-permute-start | bytes 1179656 | tf_op jit(solution)/shard_map/ppermute | solution.py:240
  17.5 33.1 %all-to-all-start.1 = ((bf16[8,128,384]{2,1,0:T(8,128)(2,1)}), bf16[8,128,384]{2,1,0:T(8,128)(2,1)S(1)}, u32[]{:S(2)}, u32[]{:S(2)}) async-start(bf16[8,128,384]{2,1,0:T(8,128)(2,1)} %broadcast_in_dim.30), calls=%async_computation.1 | async-start | bytes 1572864 | tf_op jit(solution)/shard_map/all_to_all | solution.py:231
  44.5 3.9 %collective-permute-start.7 = (bf16[2,64,384]{2,1,0:T(8,128)(2,1)S(1)}, bf16[2,64,384]{2,1,0:T(8,128)(2,1)S(1)}, u32[]{:S(2)}, u32[]{:S(2)}) collective-permute-start(bf16[2,64,384]{2,1,0:T(8,128)(2,1)S(1)} %get-tuple-element.9), channel_id=1, source_target_pairs={{0,1},{4,5},{8,9},{12,13},{16,17},{20,21},{24,25},{28,29}} | collective-permute-start | bytes 294920 | tf_op jit(solution)/shard_map/ppermute | solution.py:243
  45.8 3.5 %collective-permute-start.8 = (bf16[2,64,384]{2,1,0:T(8,128)(2,1)S(1)}, bf16[2,64,384]{2,1,0:T(8,128)(2,1)S(1)}, u32[]{:S(2)}, u32[]{:S(2)}) collective-permute-start(bf16[2,64,384]{2,1,0:T(8,128)(2,1)S(1)} %get-tuple-element.11), channel_id=1, source_target_pairs={{0,2},{4,6},{8,10},{12,14},{16,18},{20,22},{24,26},{28,30}} | collective-permute-start | bytes 294920 | tf_op jit(solution)/shard_map/ppermute | solution.py:243
  47.1 3.5 %collective-permute-start.9 = (bf16[2,64,384]{2,1,0:T(8,128)(2,1)S(1)}, bf16[2,64,384]{2,1,0:T(8,128)(2,1)S(1)}, u32[]{:S(2)}, u32[]{:S(2)}) collective-permute-start(bf16[2,64,384]{2,1,0:T(8,128)(2,1)S(1)} %get-tuple-element.10), channel_id=1, source_target_pairs={{0,3},{4,7},{8,11},{12,15},{16,19},{20,23},{24,27},{28,31}} | collective-permute-start | bytes 294920 | tf_op jit(solution)/shard_map/ppermute | solution.py:243
  50.6 1.2 copy-start.4
  51.8 102.9 %all-to-all-start = ((bf16[8,2,64,384]{3,2,1,0:T(8,128)(2,1)}), bf16[8,2,64,384]{3,2,1,0:T(8,128)(2,1)S(1)}, u32[]{:S(2)}, u32[]{:S(2)}) async-start(bf16[8,2,64,384]{3,2,1,0:T(8,128)(2,1)} %broadcast_in_dim.29), calls=%async_computation | async-start | bytes 1572864 | tf_op jit(solution)/shard_map/all_to_all | solution.py:231
  154.6 4.6 %copy-start.9 = (s32[16384]{0:T(1024)S(1)}, s32[16384]{0:T(1024)}, u32[]{:S(2)}) copy-start(s32[16384]{0:T(1024)} %param.8) | copy-start | bytes 196612
  154.6 4.7 %copy-start.6 = (s32[32]{0:T(128)S(1)}, s32[32]{0:T(128)}, u32[]{:S(2)}) copy-start(s32[32]{0:T(128)} %len_ref.7) | copy-start | bytes 388
  154.7 42.0 %copy-start.7 = (bf16[2,128,384]{2,1,0:T(8,128)(2,1)S(1)}, bf16[2,128,384]{2,1,0:T(8,128)(2,1)}, u32[]{:S(2)}) copy-start(bf16[2,128,384]{2,1,0:T(8,128)(2,1)} %sk_ref.1) | copy-start | bytes 589828
  154.7 0.9 copy-start.2
  155.6 41.1 %all-to-all-start.2 = ((bf16[4,2,512,384]{3,2,1,0:T(8,128)(2,1)}), bf16[4,2,512,384]{3,2,1,0:T(8,128)(2,1)S(1)}, u32[]{:S(2)}, u32[]{:S(2)}) async-start(bf16[4,2,512,384]{3,2,1,0:T(8,128)(2,1)} %pack_heads.1), calls=%async_computation.2 | async-start | bytes 6291456 | tf_op jit(solution)/shard_map/all_to_all | solution.py:251
  159.4 59.5 %collective-permute-start.10 = (bf16[8,2,64,384]{3,2,1,0:T(8,128)(2,1)}, bf16[8,2,64,384]{3,2,1,0:T(8,128)(2,1)}, u32[]{:S(2)}, u32[]{:S(2)}) collective-permute-start(bf16[8,2,64,384]{3,2,1,0:T(8,128)(2,1)} %copy-done.2), channel_id=1, source_target_pairs={{0,2},{1,3},{2,0},{3,1},{4,6},{5,7},{6,4},{7,5},{8,10},{9,11},{10,... | collective-permute-start | bytes 2359304 | tf_op jit(solution)/shard_map/ppermute | solution.py:257
  196.6 1.1 copy-start.5
  211.8 8.0 %copy-start = (bf16[2,512,1536]{2,1,0:T(8,128)(2,1)S(1)}, bf16[2,512,1536]{2,1,0:T(8,128)(2,1)}, u32[]{:S(2)}) copy-start(bf16[2,512,1536]{2,1,0:T(8,128)(2,1)} %kv_ref.9) | copy-start | bytes 9437188
  212.8 29.0 %all-to-all-start.3 = ((f16[8,144,384]{2,1,0:T(8,128)(2,1)}), f16[8,144,384]{2,1,0:T(8,128)(2,1)}, u32[]{:S(2)}, u32[]{:S(2)}) async-start(f16[8,144,384]{2,1,0:T(8,128)(2,1)} %convert_element_type.8), calls=%async_computation.3 | async-start | bytes 1769472 | tf_op jit(solution)/shard_map/all_to_all | solution.py:262
  219.0 7.7 %collective-permute-start.12 = (bf16[8,2,64,384]{3,2,1,0:T(8,128)(2,1)}, bf16[8,2,64,384]{3,2,1,0:T(8,128)(2,1)}, u32[]{:S(2)}, u32[]{:S(2)}) collective-permute-start(bf16[8,2,64,384]{3,2,1,0:T(8,128)(2,1)} %copy-done.2), channel_id=1, source_target_pairs={{0,1},{1,0},{2,3},{3,2},{4,5},{5,4},{6,7},{7,6},{8,9},{9,8},{10,11... | collective-permute-start | bytes 2359304 | tf_op jit(solution)/shard_map/ppermute | solution.py:257
  219.0 17.8 %collective-permute-start.11 = (bf16[8,2,64,384]{3,2,1,0:T(8,128)(2,1)}, bf16[8,2,64,384]{3,2,1,0:T(8,128)(2,1)}, u32[]{:S(2)}, u32[]{:S(2)}) collective-permute-start(bf16[8,2,64,384]{3,2,1,0:T(8,128)(2,1)} %collective-permute-done.10.anchor_ref), channel_id=1, source_target_pairs={{0,1},{1,0},{2,3},{3,2},{4,5},{5,4},{6,7},{7,6},{8,9},{9,8},{10,11... | collective-permute-start | bytes 2359304 | tf_op jit(solution)/shard_map/ppermute | solution.py:257
  219.8 1.4 copy-start.1
  221.2 1.1 copy-start.3

commit v3 on v2

v3 whole, which is shorter than its diff:
```python
import functools
import math

import jax
import jax.numpy as jnp
from jax import lax
from jax.experimental import pallas as pl
from jax.experimental.pallas import tpu as pltpu
from jax.sharding import PartitionSpec as P

HSZ = 128
NAMB = 512
NEG = -1e30
FLOOR = -2000.0
EXTRA = 16
C2 = math.log2(math.e) / math.sqrt(HSZ)
BOTH = ("hst", "grp")


def dot_t(a, b):
    return lax.dot_general(a, b, (((1,), (1,)), ((), ())), preferred_element_type=jnp.float32)


def dot(a, b):
    return lax.dot_general(a, b, (((1,), (0,)), ((), ())), preferred_element_type=jnp.float32)


def softmax(scores):
    top = functools.reduce(jnp.maximum, [jnp.max(s, axis=-1, keepdims=True) for s in scores])
    base = top * C2
    weights = [jnp.exp2(s * C2 - base) for s in scores]
    total = functools.reduce(jnp.add, [jnp.sum(w, axis=-1, keepdims=True) for w in weights])
    return base, total, [w.astype(jnp.bfloat16) for w in weights]


def pack_kernel(kv_ref, out_ref):
    out_ref[0] = kv_ref[...]


def pack(kv, groups):
    _, rows, width = kv.shape
    part = width // groups
    return pl.pallas_call(
        pack_kernel,
        grid=(groups, 2),
        in_specs=[pl.BlockSpec((1, rows, part), lambda g, s: (s, 0, g))],
        out_specs=pl.BlockSpec((1, 1, rows, part), lambda g, s: (g, s, 0, 0)),
        out_shape=jax.ShapeDtypeStruct((groups, 2, rows, part), kv.dtype),
        cost_estimate=pl.CostEstimate(flops=0, bytes_accessed=4 * kv.size, transcendentals=0),
        name="pack_heads",
    )(kv)


def suffix_kernel(at_ref, q_ref, kv_ref, sk_ref, bias_ref, *rest):
    out_ref = rest[-1]
    host = at_ref[0]
    groups = kv_ref.shape[0]
    chunks, share, _ = q_ref.shape
    odd = pl.program_id(0)
    bias = [bias_ref[pl.ds(host * groups + g, 1), :] for g in range(groups)]
    values = [kv_ref[g, 1] for g in range(groups)] + [sk_ref[1]]

    def score(k):
        q = q_ref[k]
        s = dot_t(q, sk_ref[0])
        qpos = jnp.bitwise_xor(host, 2 * k + odd) * share + lax.broadcasted_iota(jnp.int32, s.shape, 0)
        spos = host * share + lax.broadcasted_iota(jnp.int32, s.shape, 1)
        return [dot_t(q, kv_ref[g, 0]) + bias[g] for g in range(groups)] + [jnp.where(spos <= qpos, s, NEG)]

    ahead = score(0)
    for k in range(chunks):
        scores = ahead
        if k + 1 < chunks:
            ahead = score(k + 1)
        base, total, weights = softmax(scores)
        mixed = functools.reduce(jnp.add, [dot(w, v) for w, v in zip(weights, values)])
        n = mixed / total
        size = jnp.max(jnp.abs(n), axis=-1, keepdims=True)
        shift = jnp.clip(jnp.floor(jnp.log2(size)), -100.0, 100.0)
        level = jnp.maximum(base + jnp.log2(total), FLOOR)
        whole = jnp.floor(level)
        rest = jnp.exp2(level - whole)
        coarse = jnp.round(rest * 512.0) * (1.0 / 512.0)
        fine = (rest - coarse) * 1024.0
        lane = lax.broadcasted_iota(jnp.int32, (share, HSZ), 1)
        stats = jnp.where(lane == 0, whole, jnp.where(lane == 1, coarse, jnp.where(lane == 2, fine, shift)))
        to = jnp.bitwise_xor(host, 2 * k + odd)
        out_ref[to, :share, :] = n * jnp.exp2(-shift)
        out_ref[to, share : share + EXTRA, :share] = stats.T[:EXTRA, :]


def suffix_attend(host, q, kv, sk, bias, head, before):
    hosts, share, width = q.shape
    groups, _, rows, _ = kv.shape
    seen = groups * rows + share
    more = [] if before is None else [before]
    chunks = hosts // 2
    return pl.pallas_call(
        suffix_kernel,
        grid_spec=pltpu.PrefetchScalarGridSpec(
            num_scalar_prefetch=1,
            grid=(2,),
            in_specs=[
                pl.BlockSpec((chunks, share, HSZ), lambda i, at: (i, 0, head)),
                pl.BlockSpec((groups, 2, rows, HSZ), lambda i, at: (0, 0, 0, head)),
                pl.BlockSpec((2, share, HSZ), lambda i, at: (0, 0, head)),
                pl.BlockSpec(bias.shape, lambda i, at: (0, 0)),
            ]
            + [pl.BlockSpec(memory_space=pl.ANY) for _ in more],
            out_specs=pl.BlockSpec((hosts, share + EXTRA, HSZ), lambda i, at: (0, 0, head)),
        ),
        out_shape=jax.ShapeDtypeStruct((hosts, share + EXTRA, width), jnp.float32),
        input_output_aliases={5: 0} if more else {},
        compiler_params=pltpu.CompilerParams(vmem_limit_bytes=48 * 1024 * 1024),
        cost_estimate=pl.CostEstimate(
            flops=8 * hosts * share * seen * HSZ,
            bytes_accessed=4 * (groups * rows + 3 * hosts * share) * HSZ,
            transcendentals=hosts * share * seen,
        ),
        name="suffix_attend",
    )(host, q, kv, sk, bias, *more)


def combine_kernel(in_ref, out_ref):
    hosts, tall, _ = in_ref.shape
    share = tall - EXTRA
    whole, coarse, fine, shift = [in_ref[:, share + k, :] for k in range(4)]
    weight = jnp.exp2(whole - jnp.max(whole, axis=0, keepdims=True)) * (coarse + fine * (1.0 / 1024.0))
    factor = weight * jnp.exp2(shift) / jnp.sum(weight, axis=0, keepdims=True)
    factor = jnp.concatenate([factor, jnp.zeros((HSZ - hosts, HSZ), jnp.float32)], axis=0).T[:share, :]
    mixed = 0.0
    for g in range(hosts):
        mixed = mixed + factor[:, g : g + 1] * in_ref[g, :share, :]
    out_ref[...] = mixed.astype(out_ref.dtype)


def combine(parts):
    hosts, tall, width = parts.shape
    return pl.pallas_call(
        combine_kernel,
        grid=(width // HSZ,),
        in_specs=[pl.BlockSpec((hosts, tall, HSZ), lambda h: (0, 0, h))],
        out_specs=pl.BlockSpec((tall - EXTRA, HSZ), lambda h: (0, h)),
        out_shape=jax.ShapeDtypeStruct((tall - EXTRA, width), jnp.bfloat16),
        cost_estimate=pl.CostEstimate(flops=2 * parts.size, bytes_accessed=4 * parts.size, transcendentals=0),
        name="combine_groups",
    )(parts)


def context_kernel(at_ref, len_ref, q_ref, kv_ref, bias_ref, anchor_ref, *rest):
    out_ref, diag_ref = rest[-2:]
    block = at_ref[0]
    rows = q_ref.shape[0]
    half = rows // 2
    own = bias_ref[pl.ds(block, 1), :]

    @pl.when(pl.program_id(0) == 0)
    def _():
        row = lax.broadcasted_iota(jnp.int32, (half, half), 0)
        col = lax.broadcasted_iota(jnp.int32, (half, half), 1)
        for t in range(2):
            ok = own[:, t * half : (t + 1) * half]
            diag_ref[t] = jnp.where(col == row, 0.0, jnp.where(col < row, ok, NEG))

    hosts = anchor_ref.shape[0]
    apart = [jnp.bitwise_xor(at_ref[2], h) for h in range(hosts)]
    order = [jnp.bitwise_and(k, 1) * (hosts // 2) + lax.shift_right_logical(k, 1) for k in apart]
    anchor_keys = jnp.concatenate([anchor_ref[k, 0] for k in order], axis=0)
    anchor_values = jnp.concatenate([anchor_ref[k, 1] for k in order], axis=0)
    anchor_bias = jnp.where(block > 0, bias_ref[0:1, :], NEG)
    keys, values = kv_ref[0], kv_ref[1]
    tiles = []
    for t in range(2):
        q = q_ref[t * half : (t + 1) * half, :]
        scores = [dot_t(q, anchor_keys) + anchor_bias]
        mix = [anchor_values]
        if t == 1:
            scores.append(dot_t(q, keys[:half]) + own[:, :half])
            mix.append(values[:half])
        scores.append(dot_t(q, keys[t * half : (t + 1) * half]) + diag_ref[t])
        mix.append(values[t * half : (t + 1) * half])
        tiles.append((scores, mix))
    for t, (scores, mix) in enumerate(tiles):
        _, total, weights = softmax(scores)
        mixed = functools.reduce(jnp.add, [dot(w, v) for w, v in zip(weights, mix)])
        place = t * half + lax.broadcasted_iota(jnp.int32, mixed.shape, 0)
        out = jnp.where(place < len_ref[block], mixed / total, 0.0)
        out_ref[t * half : (t + 1) * half, :] = out.astype(out_ref.dtype)


def context_attend(at, lengths, q, kv, bias, anchor, before):
    rows, width = q.shape
    hosts, _, part, group_width = anchor.shape
    heads = group_width // HSZ
    half = rows // 2
    column = lambda h, at, n: (0, at[1] * heads + h)
    both = lambda h, at, n: (0, 0, at[1] * heads + h)
    more = [] if before is None else [before]
    return pl.pallas_call(
        context_kernel,
        grid_spec=pltpu.PrefetchScalarGridSpec(
            num_scalar_prefetch=2,
            grid=(heads,),
            in_specs=[
                pl.BlockSpec((rows, HSZ), column),
                pl.BlockSpec((2, rows, HSZ), both),
                pl.BlockSpec(bias.shape, lambda h, *_: (0, 0)),
                pl.BlockSpec((hosts, 2, part, HSZ), lambda h, *_: (0, 0, 0, h)),
            ]
            + [pl.BlockSpec(memory_space=pl.ANY) for _ in more],
            out_specs=pl.BlockSpec((rows, HSZ), column),
            scratch_shapes=[pltpu.VMEM((2, half, half), jnp.float32)],
        ),
        out_shape=jax.ShapeDtypeStruct((rows, width), q.dtype),
        input_output_aliases={6: 0} if more else {},
        compiler_params=pltpu.CompilerParams(vmem_limit_bytes=48 * 1024 * 1024),
        cost_estimate=pl.CostEstimate(
            flops=8 * rows * rows * group_width,
            bytes_accessed=12 * rows * group_width,
            transcendentals=2 * rows * rows * heads,
        ),
        name="context_attend",
    )(at, lengths, q, kv, bias, anchor, *more)


def swap(x, axis, k):
    return lax.ppermute(x, axis, [(i, i ^ k) for i in range(lax.axis_size(axis))])


def scatter_rows(kv, hosts, groups):
    part = kv.shape[1] // hosts
    rows = lambda h: kv[:, h * part : (h + 1) * part]
    send = lambda x, a, b: lax.ppermute(x, BOTH, [(a * groups, b * groups)])
    first = (lax.axis_index("hst") == 0) & (lax.axis_index("grp") == 0)
    pieces = [jnp.where(first, rows(0), 0.0)]
    for h in range(hosts - 1, 0, -2):
        near = send(rows(h), 0, 1)
        pieces.append(near if h == 1 else send(near, 1, h))
        if h > 1:
            pieces.append(send(rows(h - 1), 0, h - 1))
    return functools.reduce(jnp.add, pieces)


def gather_hosts(x, hosts):
    near = jnp.stack([x] + [swap(x, "hst", k) for k in range(2, hosts, 2)], axis=0)
    far = swap(near, "hst", 1)
    return jnp.concatenate([near, far], axis=0)


def spread_anchor(kv, hosts, groups):
    wide = kv.shape[2] // groups
    slab = scatter_rows(kv, hosts, groups)
    piece = slab[:, :, :wide]
    for g in range(1, groups):
        piece = piece + lax.ppermute(slab[:, :, g * wide : (g + 1) * wide], "grp", [(0, g)])
    return gather_hosts(piece, hosts)


def per_device(queries, keys_values, token_ids, lengths, suffix_queries, suffix_kv):
    hosts, groups = lax.axis_size("hst"), lax.axis_size("grp")
    host, group = lax.axis_index("hst"), lax.axis_index("grp")
    rows = queries.shape[0]
    packed, keys_values = lax.optimization_barrier((pack(keys_values, groups), keys_values))
    swapped = lax.all_to_all(packed, "grp", split_axis=0, concat_axis=0, tiled=True)
    gathered = gather_hosts(suffix_queries, hosts)
    held = {0: spread_anchor(keys_values, hosts, groups)}
    k = groups // 2
    while k >= 1:
        for have in list(held):
            held[have ^ k] = swap(held[have], "grp", k)
        k //= 2
    seen = (token_ids.reshape(-1, rows) >= NAMB) & (jnp.arange(rows)[None, :] < lengths[:, None])
    bias = jnp.where(seen, 0.0, NEG).astype(jnp.float32)
    parts = None
    for head in range(suffix_queries.shape[1] // HSZ):
        parts = suffix_attend(jnp.stack([host]), gathered, swapped, suffix_kv, bias, head, parts)
    coded = lax.all_to_all(parts.astype(jnp.float16), "hst", split_axis=0, concat_axis=0, tiled=True)
    context_out = None
    for k in range(groups):
        at = jnp.stack([host * groups + group, group ^ k, host])
        context_out = context_attend(at, lengths, queries, keys_values, bias, held[k], context_out)
    return (context_out, combine(coded.astype(jnp.float32)))


def solution(mesh):
    return jax.shard_map(
        per_device,
        mesh=mesh,
        in_specs=(
            P(("hst", "grp"), None),
            P(None, ("hst", "grp"), None),
            P(),
            P(),
            P("hst", "grp"),
            P(None, "hst", "grp"),
        ),
        out_specs=(P(("hst", "grp"), None), P("hst", "grp")),
        check_vma=False,
    )
```

time: 251 us -> 139 us (0.55)
  Pallas kernels: 135 us -> 47.4 us
  waiting for transfers between devices: 59.6 us -> 19.7 us
  starting transfers between devices: 38.9 us -> 53.8 us
    pallas_call x2 -> x4, Pallas kernels: 110 us -> 23.5 us  [the longest x3 17.3 us: suffix_attend(): pl.pallas_call(suffix_kernel, grid_spec=pltpu.PrefetchScalarGridSpec(num_...]
    all_to_all x3 -> x1, waiting for transfers between devices: 35.2 us -> 0.01 us  [per_device(): lax.all_to_all(packed, 'grp', split_axis=0, concat_axis=0, tiled=True)]
    ppermute x10 -> x21, starting transfers between devices: 15.3 us -> 39.9 us  [the longest x11 25.1 us: swap(): lax.ppermute(x, axis, [(i, i ^ k) for i in range(lax.axis_size(axis))])]
    all_to_all x3 -> x1, starting transfers between devices: 13.6 us -> 4.91 us  [per_device(): lax.all_to_all(packed, 'grp', split_axis=0, concat_axis=0, tiled=True)]
    ppermute x10 -> x21, waiting for transfers between devices: 22.2 us -> 17.5 us  [the longest x10 11.4 us: scatter_rows(): send = lambda x, a, b: lax.ppermute(x, BOTH, [(a * groups, b * groups)])]
    unnamed x20 -> x23, local copies, waits for them, and re-layouts: 4.65 us -> 6.36 us
  transfers between devices with their start and end apart: 17 -> 26, of which waited for: 8 -> 8; matrix products, arithmetic and copies ran while one was open for 1% -> 7% of each run, Pallas kernels for 52% -> 32%
where the time goes in v3:
time: 139 us; the launch traced here: 138 us
  starting transfers between devices  53.8 us (39%)
  Pallas kernels  47.4 us (34%)
  waiting for transfers between devices  19.7 us (14%)
  local copies, waits for them, and re-layouts  8.88 us (6%)
  other arithmetic  6.84 us (5%)
    ppermute x11, starting transfers between devices, swap(): lax.ppermute(x, axis, [(i, i ^ k) for i in range(lax.axis_size(axis))])  25.1 us
    pallas_call x4, Pallas kernels, context_attend(): pl.pallas_call(context_kernel, grid_spec=pltpu.PrefetchScalarGridSpec(num...  20.4 us
    pallas_call x3, Pallas kernels, suffix_attend(): pl.pallas_call(suffix_kernel, grid_spec=pltpu.PrefetchScalarGridSpec(num_...  17.3 us
    ppermute x10, starting transfers between devices, scatter_rows(): send = lambda x, a, b: lax.ppermute(x, BOTH, [(a * groups, b * groups)])  14.8 us
    ppermute x10, waiting for transfers between devices, scatter_rows(): send = lambda x, a, b: lax.ppermute(x, BOTH, [(a * groups, b * groups)])  11.4 us
    unnamed x23, local copies, waits for them, and re-layouts  6.36 us
    pallas_call x1, Pallas kernels, pack(): pl.pallas_call(pack_kernel, grid=(groups, 2), in_specs=[pl.BlockSpec((1,...  6.19 us
    ppermute x11, waiting for transfers between devices, swap(): lax.ppermute(x, axis, [(i, i ^ k) for i in range(lax.axis_size(axis))])  6.12 us
  transfers between devices with their start and end apart: 26, of which 8 were waited for; matrix products, arithmetic and copies ran while one was open for 7% of the time, Pallas kernels for 32%

profile of v3, /device:TPU:0, one launch (start us, length us, event | category | flops | bytes accessed | tf_op | source)
XLA Modules:
  0.0 137.6 jit_solution(13820779801887011507)
XLA Ops:
  0.6 3.1 %collective-permute-start.20 = (bf16[128,384]{1,0:T(8,128)(2,1)}, bf16[128,384]{1,0:T(8,128)(2,1)S(1)}, u32[]{:S(2)}, u32[]{:S(2)}) collective-permute-start(bf16[128,384]{1,0:T(8,128)(2,1)} %param.10), channel_id=1, source_target_pairs={{0,8},{4,12},{8,0},{12,4},{16,24},{20,28},{24,16},{28,20},{1,9},{5... | collective-permute-start | bytes 294920 | tf_op jit(solution)/shard_map/ppermute | solution.py:227
  3.7 2.5 %collective-permute-start.22 = (bf16[128,384]{1,0:T(8,128)(2,1)}, bf16[128,384]{1,0:T(8,128)(2,1)S(1)}, u32[]{:S(2)}, u32[]{:S(2)}) collective-permute-start(bf16[128,384]{1,0:T(8,128)(2,1)} %param.10), channel_id=1, source_target_pairs={{0,24},{4,28},{8,16},{12,20},{16,8},{20,12},{24,0},{28,4},{1,25},{... | collective-permute-start | bytes 294920 | tf_op jit(solution)/shard_map/ppermute | solution.py:227
  6.3 6.2 %pack_heads.1 = bf16[4,2,512,384]{3,2,1,0:T(8,128)(2,1)} custom-call(bf16[2,512,1536]{2,1,0:T(8,128)(2,1)} %kv_ref.5), custom_call_target="tpu_custom_call" | custom-call | bytes 6291456 | tf_op jit(solution)/shard_map/pack_heads/pallas_call | solution.py:43
  12.5 4.9 %all-to-all-start = ((bf16[4,2,512,384]{3,2,1,0:T(8,128)(2,1)}), bf16[4,2,512,384]{3,2,1,0:T(8,128)(2,1)}, u32[]{:S(2)}, u32[]{:S(2)}) async-start(bf16[4,2,512,384]{3,2,1,0:T(8,128)(2,1)} %pack_heads.1), calls=%async_computation | async-start | bytes 6291456 | tf_op jit(solution)/shard_map/all_to_all | solution.py:264
  17.5 1.6 %fusion.5 = (bf16[2,64,1536]{2,1,0:T(8,128)(2,1)}, bf16[2,64,1536]{2,1,0:T(8,128)(2,1)}, bf16[2,64,1536]{2,1,0:T(8,128)(2,1)}, bf16[2,64,1536]{2,1,0:T(8,128)(2,...) fusion(bf16[2,512,1536]{2,1,0:T(8,128)(2,1)S(1)} %copy-done), kind=kLoop, calls=%fused_computation.24 | loop fusion | bytes 5505024 | tf_op jit(solution)/shard_map/slice | solution.py:232
  19.0 4.2 %collective-permute-start = (bf16[2,64,1536]{2,1,0:T(8,128)(2,1)}, bf16[2,64,1536]{2,1,0:T(8,128)(2,1)}, u32[]{:S(2)}, u32[]{:S(2)}) collective-permute-start(bf16[2,64,1536]{2,1,0:T(8,128)(2,1)} %get-tuple-element.8), channel_id=1, source_target_pairs={{0,4}} | collective-permute-start | bytes 1179656 | tf_op jit(solution)/shard_map/ppermute | solution.py:233
  23.2 2.0 %collective-permute-start.9 = (bf16[2,64,1536]{2,1,0:T(8,128)(2,1)}, bf16[2,64,1536]{2,1,0:T(8,128)(2,1)}, u32[]{:S(2)}, u32[]{:S(2)}) collective-permute-start(bf16[2,64,1536]{2,1,0:T(8,128)(2,1)} %get-tuple-element.9), channel_id=1, source_target_pairs={{0,4}} | collective-permute-start | bytes 1179656 | tf_op jit(solution)/shard_map/ppermute | solution.py:233
  25.4 1.3 collective-permute-start.8
  26.7 1.3 collective-permute-start.6
  28.0 1.3 collective-permute-start.3
  29.5 1.3 collective-permute-start.5
  30.8 1.8 %collective-permute-done.9 = bf16[2,64,1536]{2,1,0:T(8,128)(2,1)} collective-permute-done((bf16[2,64,1536]{2,1,0:T(8,128)(2,1)}, bf16[2,64,1536]{2,1,0:T(8,128)(2,1)}, u32[]{:S(2)}, u32[]{:S(2)}) %collective-permute-start.9) | collective-permute-done | bytes 393248 | tf_op jit(solution)/shard_map/ppermute | solution.py:233
  32.6 1.3 collective-permute-start.2
  33.9 0.7 collective-permute-start.1
  34.6 6.1 %collective-permute-done.6 = bf16[2,64,1536]{2,1,0:T(8,128)(2,1)S(1)} collective-permute-done((bf16[2,64,1536]{2,1,0:T(8,128)(2,1)}, bf16[2,64,1536]{2,1,0:T(8,128)(2,1)S(1)}, u32[]{:S(2)}, u32[]{:S(2)}) %collective-permute-start.6) | collective-permute-done | bytes 393248 | tf_op jit(solution)/shard_map/ppermute | solution.py:233
  40.7 0.7 collective-permute-start.7
  41.4 3.5 %collective-permute-done.3 = bf16[2,64,1536]{2,1,0:T(8,128)(2,1)S(1)} collective-permute-done((bf16[2,64,1536]{2,1,0:T(8,128)(2,1)}, bf16[2,64,1536]{2,1,0:T(8,128)(2,1)S(1)}, u32[]{:S(2)}, u32[]{:S(2)}) %collective-permute-start.3) | collective-permute-done | bytes 393248 | tf_op jit(solution)/shard_map/ppermute | solution.py:233
  45.6 0.9 constant_dynamic-update-slice_fusion.7
  46.5 1.0 pad_maximum_fusion.1
  47.5 3.1 %collective-permute-start.23 = (bf16[4,128,384]{2,1,0:T(8,128)(2,1)S(1)}, bf16[4,128,384]{2,1,0:T(8,128)(2,1)S(1)}, u32[]{:S(2)}, u32[]{:S(2)}) collective-permute-start(bf16[4,128,384]{2,1,0:T(8,128)(2,1)S(1)} %pad_maximum_fusion.1), channel_id=1, source_target_pairs={{0,4},{4,0},{8,12},{12,8},{16,20},{20,16},{24,28},{28,24},{1,5},{5... | collective-permute-start | bytes 1179656 | tf_op jit(solution)/shard_map/ppermute | solution.py:227
  50.6 1.2 add_add_fusion
  51.8 1.3 collective-permute-start.10
  53.1 1.3 collective-permute-start.12
  54.4 1.3 collective-permute-start.11
  55.7 0.8 collective-permute-done.12
  56.6 1.3 collective-permute-done.11
  57.9 0.7 constant_dynamic-update-slice_fusion.4
  58.6 4.4 %collective-permute-start.13 = (bf16[2,64,384]{2,1,0:T(8,128)(2,1)S(1)}, bf16[2,64,384]{2,1,0:T(8,128)(2,1)S(1)}, u32[]{:S(2)}, u32[]{:S(2)}) collective-permute-start(bf16[2,64,384]{2,1,0:T(8,128)(2,1)S(1)} %get-tuple-element.7), channel_id=1, source_target_pairs={{0,8},{4,12},{8,0},{12,4},{16,24},{20,28},{24,16},{28,20},{1,9},{5... | collective-permute-start | bytes 294920 | tf_op jit(solution)/shard_map/ppermute | solution.py:227
  63.0 0.9 copy-done.3
  63.9 1.2 collective-permute-done.15
  65.1 1.0 collective-permute-done.14
  66.2 4.8 %collective-permute-start.16 = (bf16[4,2,64,384]{3,2,1,0:T(8,128)(2,1)S(1)}, bf16[4,2,64,384]{3,2,1,0:T(8,128)(2,1)S(1)}, u32[]{:S(2)}, u32[]{:S(2)}) collective-permute-start(bf16[4,2,64,384]{3,2,1,0:T(8,128)(2,1)S(1)} %pad_maximum_fusion), channel_id=1, source_target_pairs={{0,4},{4,0},{8,12},{12,8},{16,20},{20,16},{24,28},{28,24},{1,5},{5... | collective-permute-start | bytes 1179656 | tf_op jit(solution)/shard_map/ppermute | solution.py:227
  73.0 3.8 %collective-permute-done.16 = bf16[4,2,64,384]{3,2,1,0:T(8,128)(2,1)S(1)} collective-permute-done((bf16[4,2,64,384]{3,2,1,0:T(8,128)(2,1)S(1)}, bf16[4,2,64,384]{3,2,1,0:T(8,128)(2,1)S(1)}, u32[]{:S(2)}, u32[]{:S(2)}) %collective-permute-start.16) | collective-permute-done | bytes 393248 | tf_op jit(solution)/shard_map/ppermute | solution.py:227
  76.8 0.8 constant_dynamic-update-slice_fusion.anchor_ref
  77.7 6.6 %collective-permute-start.17 = (bf16[8,2,64,384]{3,2,1,0:T(8,128)(2,1)}, bf16[8,2,64,384]{3,2,1,0:T(8,128)(2,1)}, u32[]{:S(2)}, u32[]{:S(2)}) collective-permute-start(bf16[8,2,64,384]{3,2,1,0:T(8,128)(2,1)} %constant_dynamic-update-slice_fusion.anchor_ref), channel_id=1, source_target_pairs={{0,2},{1,3},{2,0},{3,1},{4,6},{5,7},{6,4},{7,5},{8,10},{9,11},{10,... | collective-permute-start | bytes 2359304 | tf_op jit(solution)/shard_map/ppermute | solution.py:227
  84.3 1.1 copy-done.4
  85.4 5.7 %suffix_attend.3.rest_0_ = f32[8,144,384]{2,1,0:T(8,128)S(1)} custom-call(s32[1]{0:T(128)} %bitcast.2.at_ref, bf16[8,128,384]{2,1,0:T(8,128)(2,1)S(1)} %copy-done.4, bf16[4,2,512,384]{3,2,1,0:T(8,128)(2,1)} %all-to-all-done.kv_ref, bf16[2,128,384]{2,1,0:T(8,128)(2,1)S(1)} %copy-done.5, f32[32,512]{1,0:T(8,128)S(1)} %fusion.3.bias_ref), custom_call_target="tpu_custom_call" | custom-call | flops 2281701376 | bytes 2621440 | tf_op jit(solution)/shard_map/suffix_attend/pallas_call | solution.py:98
  91.2 5.8 %suffix_attend.4.rest_0_ = f32[8,144,384]{2,1,0:T(8,128)S(1)} custom-call(s32[1]{0:T(128)} %bitcast.2.at_ref, bf16[8,128,384]{2,1,0:T(8,128)(2,1)S(1)} %copy-done.4, bf16[4,2,512,384]{3,2,1,0:T(8,128)(2,1)} %all-to-all-done.kv_ref, bf16[2,128,384]{2,1,0:T(8,128)(2,1)S(1)} %copy-done.5, ...), custom_call_target="tpu_custom_call", output_to_operand_aliasing={{}: (5, {})} | custom-call | flops 2281701376 | bytes 2621440 | tf_op jit(solution)/shard_map/suffix_attend/pallas_call | solution.py:98
  96.9 5.8 %suffix_attend.5 = f32[8,144,384]{2,1,0:T(8,128)S(1)} custom-call(s32[1]{0:T(128)} %bitcast.2.at_ref, bf16[8,128,384]{2,1,0:T(8,128)(2,1)S(1)} %copy-done.4, bf16[4,2,512,384]{3,2,1,0:T(8,128)(2,1)} %all-to-all-done.kv_ref, bf16[2,128,384]{2,1,0:T(8,128)(2,1)S(1)} %copy-done.5, f32[32,512]{1,0:T(8,128)S(1)} %fusion.3.bias_ref, ...), custom_call_target="tpu_custom_call", output_to_operand_aliasing={{}: (5, {})} | custom-call | flops 2281701376 | bytes 2621440 | tf_op jit(solution)/shard_map/suffix_attend/pallas_call | solution.py:98
  102.7 1.1 convert_element_type.8
  103.8 5.1 %all-to-all-start.1 = ((f16[8,144,384]{2,1,0:T(8,128)(2,1)}), f16[8,144,384]{2,1,0:T(8,128)(2,1)}, u32[]{:S(2)}, u32[]{:S(2)}) async-start(f16[8,144,384]{2,1,0:T(8,128)(2,1)} %convert_element_type.8), calls=%async_computation.1 | async-start | bytes 1769472 | tf_op jit(solution)/shard_map/all_to_all | solution.py:277
  109.7 1.4 %copy-done.1 = bf16[512,1536]{1,0:T(8,128)(2,1)S(1)} copy-done((bf16[512,1536]{1,0:T(8,128)(2,1)S(1)}, bf16[512,1536]{1,0:T(8,128)(2,1)}, u32[]{:S(2)}) %copy-start.1) | copy-done | bytes 1572888
  111.1 5.1 %context_attend.4.rest_0_ = bf16[512,1536]{1,0:T(8,128)(2,1)} custom-call(s32[3]{0:T(128)S(1)} %add_add_fusion.4.at_ref, s32[32]{0:T(128)S(1)} %copy-done.2, bf16[512,1536]{1,0:T(8,128)(2,1)S(1)} %copy-done.1, bf16[2,512,1536]{2,1,0:T(8,128)(2,1)S(1)} %copy-done, f32[32,512]{1,0:T(8,128)S(1)} %fusion.3.bias_ref, ...), custom_call_target="tpu_custom_call" | custom-call | flops 805306368 | bytes 2359296 | tf_op jit(solution)/shard_map/context_attend/pallas_call | solution.py:199
  116.2 5.1 %context_attend.5.rest_0_ = bf16[512,1536]{1,0:T(8,128)(2,1)} custom-call(s32[3]{0:T(128)S(1)} %add_add_fusion.3.at_ref, s32[32]{0:T(128)S(1)} %copy-done.2, bf16[512,1536]{1,0:T(8,128)(2,1)S(1)} %copy-done.1, bf16[2,512,1536]{2,1,0:T(8,128)(2,1)S(1)} %copy-done, f32[32,512]{1,0:T(8,128)S(1)} %fusion.3.bias_ref, ...), custom_call_target="tpu_custom_call", output_to_operand_aliasing={{}: (6, {})} | custom-call | flops 805306368 | bytes 2359296 | tf_op jit(solution)/shard_map/context_attend/pallas_call | solution.py:199
  121.3 5.1 %context_attend.6.rest_0_ = bf16[512,1536]{1,0:T(8,128)(2,1)} custom-call(s32[3]{0:T(128)S(1)} %add_add_fusion.2.at_ref, s32[32]{0:T(128)S(1)} %copy-done.2, bf16[512,1536]{1,0:T(8,128)(2,1)S(1)} %copy-done.1, bf16[2,512,1536]{2,1,0:T(8,128)(2,1)S(1)} %copy-done, f32[32,512]{1,0:T(8,128)S(1)} %fusion.3.bias_ref, ...), custom_call_target="tpu_custom_call", output_to_operand_aliasing={{}: (6, {})} | custom-call | flops 805306368 | bytes 2359296 | tf_op jit(solution)/shard_map/context_attend/pallas_call | solution.py:199
  126.4 5.1 %context_attend.7 = bf16[512,1536]{1,0:T(8,128)(2,1)} custom-call(s32[3]{0:T(128)S(1)} %add_add_fusion.1.at_ref, s32[32]{0:T(128)S(1)} %copy-done.2, bf16[512,1536]{1,0:T(8,128)(2,1)S(1)} %copy-done.1, bf16[2,512,1536]{2,1,0:T(8,128)(2,1)S(1)} %copy-done, f32[32,512]{1,0:T(8,128)S(1)} %fusion.3.bias_ref, ...), custom_call_target="tpu_custom_call", output_to_operand_aliasing={{}: (6, {})} | custom-call | flops 805306368 | bytes 2359296 | tf_op jit(solution)/shard_map/context_attend/pallas_call | solution.py:199
  131.5 2.5 %convert_element_type.9.in_ref = f32[8,144,384]{2,1,0:T(8,128)} convert(f16[8,144,384]{2,1,0:T(8,128)(2,1)} %all-to-all-done.1) | non-fusion elementwise | flops 442368 | bytes 2654208 | tf_op jit(solution)/shard_map/convert_element_type | solution.py:282
  134.1 3.5 %combine_groups.1 = bf16[128,384]{1,0:T(8,128)(2,1)} custom-call(f32[8,144,384]{2,1,0:T(8,128)} %convert_element_type.9.in_ref), custom_call_target="tpu_custom_call" | custom-call | flops 884736 | bytes 1769472 | tf_op jit(solution)/shard_map/combine_groups/pallas_call | solution.py:139
  (53 shorter events, 4.0 us)
Async XLA Ops:
  0.6 24.7 %collective-permute-start.20 = (bf16[128,384]{1,0:T(8,128)(2,1)}, bf16[128,384]{1,0:T(8,128)(2,1)S(1)}, u32[]{:S(2)}, u32[]{:S(2)}) collective-permute-start(bf16[128,384]{1,0:T(8,128)(2,1)} %param.10), channel_id=1, source_target_pairs={{0,8},{4,12},{8,0},{12,4},{16,24},{20,28},{24,16},{28,20},{1,9},{5... | collective-permute-start | bytes 294920 | tf_op jit(solution)/shard_map/ppermute | solution.py:227
  3.7 23.0 %collective-permute-start.22 = (bf16[128,384]{1,0:T(8,128)(2,1)}, bf16[128,384]{1,0:T(8,128)(2,1)S(1)}, u32[]{:S(2)}, u32[]{:S(2)}) collective-permute-start(bf16[128,384]{1,0:T(8,128)(2,1)} %param.10), channel_id=1, source_target_pairs={{0,24},{4,28},{8,16},{12,20},{16,8},{20,12},{24,0},{28,4},{1,25},{... | collective-permute-start | bytes 294920 | tf_op jit(solution)/shard_map/ppermute | solution.py:227
  6.2 21.8 %collective-permute-start.21 = (bf16[128,384]{1,0:T(8,128)(2,1)}, bf16[128,384]{1,0:T(8,128)(2,1)}, u32[]{:S(2)}, u32[]{:S(2)}) collective-permute-start(bf16[128,384]{1,0:T(8,128)(2,1)} %param.10), channel_id=1, source_target_pairs={{0,16},{4,20},{8,24},{12,28},{16,0},{20,4},{24,8},{28,12},{1,17},{... | collective-permute-start | bytes 294920 | tf_op jit(solution)/shard_map/ppermute | solution.py:227
  12.5 4.9 %copy-start = (bf16[2,512,1536]{2,1,0:T(8,128)(2,1)S(1)}, bf16[2,512,1536]{2,1,0:T(8,128)(2,1)}, u32[]{:S(2)}) copy-start(bf16[2,512,1536]{2,1,0:T(8,128)(2,1)} %kv_ref.5) | copy-start | bytes 9437188
  12.5 71.8 %all-to-all-start = ((bf16[4,2,512,384]{3,2,1,0:T(8,128)(2,1)}), bf16[4,2,512,384]{3,2,1,0:T(8,128)(2,1)}, u32[]{:S(2)}, u32[]{:S(2)}) async-start(bf16[4,2,512,384]{3,2,1,0:T(8,128)(2,1)} %pack_heads.1), calls=%async_computation | async-start | bytes 6291456 | tf_op jit(solution)/shard_map/all_to_all | solution.py:264
  17.4 7.8 %copy-start.7 = (s32[16384]{0:T(1024)S(1)}, s32[16384]{0:T(1024)}, u32[]{:S(2)}) copy-start(s32[16384]{0:T(1024)} %param.8) | copy-start | bytes 196612
  17.4 11.9 %copy-start.2 = (s32[32]{0:T(128)S(1)}, s32[32]{0:T(128)}, u32[]{:S(2)}) copy-start(s32[32]{0:T(128)} %len_ref.7) | copy-start | bytes 388
  17.5 12.0 %copy-start.6 = (bf16[128,384]{1,0:T(8,128)(2,1)S(1)}, bf16[128,384]{1,0:T(8,128)(2,1)}, u32[]{:S(2)}) copy-start(bf16[128,384]{1,0:T(8,128)(2,1)} %param.10) | copy-start | bytes 294916
  19.0 10.5 %collective-permute-start = (bf16[2,64,1536]{2,1,0:T(8,128)(2,1)}, bf16[2,64,1536]{2,1,0:T(8,128)(2,1)}, u32[]{:S(2)}, u32[]{:S(2)}) collective-permute-start(bf16[2,64,1536]{2,1,0:T(8,128)(2,1)} %get-tuple-element.8), channel_id=1, source_target_pairs={{0,4}} | collective-permute-start | bytes 1179656 | tf_op jit(solution)/shard_map/ppermute | solution.py:233
  23.2 9.3 %collective-permute-start.9 = (bf16[2,64,1536]{2,1,0:T(8,128)(2,1)}, bf16[2,64,1536]{2,1,0:T(8,128)(2,1)}, u32[]{:S(2)}, u32[]{:S(2)}) collective-permute-start(bf16[2,64,1536]{2,1,0:T(8,128)(2,1)} %get-tuple-element.9), channel_id=1, source_target_pairs={{0,4}} | collective-permute-start | bytes 1179656 | tf_op jit(solution)/shard_map/ppermute | solution.py:233
  25.4 8.5 %collective-permute-start.8 = (bf16[2,64,1536]{2,1,0:T(8,128)(2,1)}, bf16[2,64,1536]{2,1,0:T(8,128)(2,1)S(1)}, u32[]{:S(2)}, u32[]{:S(2)}) collective-permute-start(bf16[2,64,1536]{2,1,0:T(8,128)(2,1)} %get-tuple-element.10), channel_id=1, source_target_pairs={{0,8}} | collective-permute-start | bytes 1179656 | tf_op jit(solution)/shard_map/ppermute | solution.py:233
  26.7 14.0 %collective-permute-start.6 = (bf16[2,64,1536]{2,1,0:T(8,128)(2,1)}, bf16[2,64,1536]{2,1,0:T(8,128)(2,1)S(1)}, u32[]{:S(2)}, u32[]{:S(2)}) collective-permute-start(bf16[2,64,1536]{2,1,0:T(8,128)(2,1)} %get-tuple-element.11), channel_id=1, source_target_pairs={{0,4}} | collective-permute-start | bytes 1179656 | tf_op jit(solution)/shard_map/ppermute | solution.py:233
  28.0 16.9 %collective-permute-start.3 = (bf16[2,64,1536]{2,1,0:T(8,128)(2,1)}, bf16[2,64,1536]{2,1,0:T(8,128)(2,1)S(1)}, u32[]{:S(2)}, u32[]{:S(2)}) collective-permute-start(bf16[2,64,1536]{2,1,0:T(8,128)(2,1)} %get-tuple-element.13), channel_id=1, source_target_pairs={{0,4}} | collective-permute-start | bytes 1179656 | tf_op jit(solution)/shard_map/ppermute | solution.py:233
  29.5 18.0 %collective-permute-start.5 = (bf16[2,64,1536]{2,1,0:T(8,128)(2,1)}, bf16[2,64,1536]{2,1,0:T(8,128)(2,1)S(1)}, u32[]{:S(2)}, u32[]{:S(2)}) collective-permute-start(bf16[2,64,1536]{2,1,0:T(8,128)(2,1)} %get-tuple-element.12), channel_id=1, source_target_pairs={{0,16}} | collective-permute-start | bytes 1179656 | tf_op jit(solution)/shard_map/ppermute | solution.py:233
  32.6 18.0 %collective-permute-start.2 = (bf16[2,64,1536]{2,1,0:T(8,128)(2,1)}, bf16[2,64,1536]{2,1,0:T(8,128)(2,1)S(1)}, u32[]{:S(2)}, u32[]{:S(2)}) collective-permute-start(bf16[2,64,1536]{2,1,0:T(8,128)(2,1)} %get-tuple-element.14), channel_id=1, source_target_pairs={{0,24}} | collective-permute-start | bytes 1179656 | tf_op jit(solution)/shard_map/ppermute | solution.py:233
  33.9 16.7 %collective-permute-start.1 = (bf16[2,64,1536]{2,1,0:T(8,128)(2,1)}, bf16[2,64,1536]{2,1,0:T(8,128)(2,1)S(1)}, u32[]{:S(2)}, u32[]{:S(2)}) collective-permute-start(bf16[2,64,1536]{2,1,0:T(8,128)(2,1)} %collective-permute-done), channel_id=1, source_target_pairs={{4,28}} | collective-permute-start | bytes 1179656 | tf_op jit(solution)/shard_map/ppermute | solution.py:233
  40.7 9.9 %collective-permute-start.7 = (bf16[2,64,1536]{2,1,0:T(8,128)(2,1)S(1)}, bf16[2,64,1536]{2,1,0:T(8,128)(2,1)S(1)}, u32[]{:S(2)}, u32[]{:S(2)}) collective-permute-start(bf16[2,64,1536]{2,1,0:T(8,128)(2,1)S(1)} %collective-permute-done.6), channel_id=1, source_target_pairs={{4,12}} | collective-permute-start | bytes 1179656 | tf_op jit(solution)/shard_map/ppermute | solution.py:233
  44.9 5.7 %collective-permute-start.4 = (bf16[2,64,1536]{2,1,0:T(8,128)(2,1)S(1)}, bf16[2,64,1536]{2,1,0:T(8,128)(2,1)S(1)}, u32[]{:S(2)}, u32[]{:S(2)}) collective-permute-start(bf16[2,64,1536]{2,1,0:T(8,128)(2,1)S(1)} %collective-permute-done.3), channel_id=1, source_target_pairs={{4,20}} | collective-permute-start | bytes 1179656 | tf_op jit(solution)/shard_map/ppermute | solution.py:233
  47.5 15.5 %collective-permute-start.23 = (bf16[4,128,384]{2,1,0:T(8,128)(2,1)S(1)}, bf16[4,128,384]{2,1,0:T(8,128)(2,1)S(1)}, u32[]{:S(2)}, u32[]{:S(2)}) collective-permute-start(bf16[4,128,384]{2,1,0:T(8,128)(2,1)S(1)} %pad_maximum_fusion.1), channel_id=1, source_target_pairs={{0,4},{4,0},{8,12},{12,8},{16,20},{20,16},{24,28},{28,24},{1,5},{5... | collective-permute-start | bytes 1179656 | tf_op jit(solution)/shard_map/ppermute | solution.py:227
  51.8 4.0 %collective-permute-start.10 = (bf16[2,64,384]{2,1,0:T(8,128)(2,1)S(1)}, bf16[2,64,384]{2,1,0:T(8,128)(2,1)S(1)}, u32[]{:S(2)}, u32[]{:S(2)}) collective-permute-start(bf16[2,64,384]{2,1,0:T(8,128)(2,1)S(1)} %get-tuple-element.15), channel_id=1, source_target_pairs={{0,1},{4,5},{8,9},{12,13},{16,17},{20,21},{24,25},{28,29}} | collective-permute-start | bytes 294920 | tf_op jit(solution)/shard_map/ppermute | solution.py:255
  53.1 3.5 %collective-permute-start.12 = (bf16[2,64,384]{2,1,0:T(8,128)(2,1)S(1)}, bf16[2,64,384]{2,1,0:T(8,128)(2,1)S(1)}, u32[]{:S(2)}, u32[]{:S(2)}) collective-permute-start(bf16[2,64,384]{2,1,0:T(8,128)(2,1)S(1)} %get-tuple-element.16), channel_id=1, source_target_pairs={{0,3},{4,7},{8,11},{12,15},{16,19},{20,23},{24,27},{28,31}} | collective-permute-start | bytes 294920 | tf_op jit(solution)/shard_map/ppermute | solution.py:255
  54.4 3.5 %collective-permute-start.11 = (bf16[2,64,384]{2,1,0:T(8,128)(2,1)S(1)}, bf16[2,64,384]{2,1,0:T(8,128)(2,1)S(1)}, u32[]{:S(2)}, u32[]{:S(2)}) collective-permute-start(bf16[2,64,384]{2,1,0:T(8,128)(2,1)S(1)} %get-tuple-element.17), channel_id=1, source_target_pairs={{0,2},{4,6},{8,10},{12,14},{16,18},{20,22},{24,26},{28,30}} | collective-permute-start | bytes 294920 | tf_op jit(solution)/shard_map/ppermute | solution.py:255
  55.7 28.6 %copy-start.5 = (bf16[2,128,384]{2,1,0:T(8,128)(2,1)S(1)}, bf16[2,128,384]{2,1,0:T(8,128)(2,1)}, u32[]{:S(2)}) copy-start(bf16[2,128,384]{2,1,0:T(8,128)(2,1)} %sk_ref.5) | copy-start | bytes 589828
  58.6 6.6 %collective-permute-start.15 = (bf16[2,64,384]{2,1,0:T(8,128)(2,1)S(1)}, bf16[2,64,384]{2,1,0:T(8,128)(2,1)S(1)}, u32[]{:S(2)}, u32[]{:S(2)}) collective-permute-start(bf16[2,64,384]{2,1,0:T(8,128)(2,1)S(1)} %get-tuple-element.7), channel_id=1, source_target_pairs={{0,24},{4,28},{8,16},{12,20},{16,8},{20,12},{24,0},{28,4},{1,25},{... | collective-permute-start | bytes 294920 | tf_op jit(solution)/shard_map/ppermute | solution.py:227
  58.6 7.6 %collective-permute-start.14 = (bf16[2,64,384]{2,1,0:T(8,128)(2,1)S(1)}, bf16[2,64,384]{2,1,0:T(8,128)(2,1)S(1)}, u32[]{:S(2)}, u32[]{:S(2)}) collective-permute-start(bf16[2,64,384]{2,1,0:T(8,128)(2,1)S(1)} %get-tuple-element.7), channel_id=1, source_target_pairs={{0,16},{4,20},{8,24},{12,28},{16,0},{20,4},{24,8},{28,12},{1,17},{... | collective-permute-start | bytes 294920 | tf_op jit(solution)/shard_map/ppermute | solution.py:227
  58.6 7.6 %collective-permute-start.13 = (bf16[2,64,384]{2,1,0:T(8,128)(2,1)S(1)}, bf16[2,64,384]{2,1,0:T(8,128)(2,1)S(1)}, u32[]{:S(2)}, u32[]{:S(2)}) collective-permute-start(bf16[2,64,384]{2,1,0:T(8,128)(2,1)S(1)} %get-tuple-element.7), channel_id=1, source_target_pairs={{0,8},{4,12},{8,0},{12,4},{16,24},{20,28},{24,16},{28,20},{1,9},{5... | collective-permute-start | bytes 294920 | tf_op jit(solution)/shard_map/ppermute | solution.py:227
  63.0 0.9 copy-start.3
  66.2 10.6 %collective-permute-start.16 = (bf16[4,2,64,384]{3,2,1,0:T(8,128)(2,1)S(1)}, bf16[4,2,64,384]{3,2,1,0:T(8,128)(2,1)S(1)}, u32[]{:S(2)}, u32[]{:S(2)}) collective-permute-start(bf16[4,2,64,384]{3,2,1,0:T(8,128)(2,1)S(1)} %pad_maximum_fusion), channel_id=1, source_target_pairs={{0,4},{4,0},{8,12},{12,8},{16,20},{20,16},{24,28},{28,24},{1,5},{5... | collective-permute-start | bytes 1179656 | tf_op jit(solution)/shard_map/ppermute | solution.py:227
  77.7 31.2 %collective-permute-start.17 = (bf16[8,2,64,384]{3,2,1,0:T(8,128)(2,1)}, bf16[8,2,64,384]{3,2,1,0:T(8,128)(2,1)}, u32[]{:S(2)}, u32[]{:S(2)}) collective-permute-start(bf16[8,2,64,384]{3,2,1,0:T(8,128)(2,1)} %constant_dynamic-update-slice_fusion.anchor_ref), channel_id=1, source_target_pairs={{0,2},{1,3},{2,0},{3,1},{4,6},{5,7},{6,4},{7,5},{8,10},{9,11},{10,... | collective-permute-start | bytes 2359304 | tf_op jit(solution)/shard_map/ppermute | solution.py:227
  84.3 1.1 copy-start.4
  103.8 27.7 %all-to-all-start.1 = ((f16[8,144,384]{2,1,0:T(8,128)(2,1)}), f16[8,144,384]{2,1,0:T(8,128)(2,1)}, u32[]{:S(2)}, u32[]{:S(2)}) async-start(f16[8,144,384]{2,1,0:T(8,128)(2,1)} %convert_element_type.8), calls=%async_computation.1 | async-start | bytes 1769472 | tf_op jit(solution)/shard_map/all_to_all | solution.py:277
  108.9 7.3 %collective-permute-start.19 = (bf16[8,2,64,384]{3,2,1,0:T(8,128)(2,1)}, bf16[8,2,64,384]{3,2,1,0:T(8,128)(2,1)}, u32[]{:S(2)}, u32[]{:S(2)}) collective-permute-start(bf16[8,2,64,384]{3,2,1,0:T(8,128)(2,1)} %constant_dynamic-update-slice_fusion.anchor_ref), channel_id=1, source_target_pairs={{0,1},{1,0},{2,3},{3,2},{4,5},{5,4},{6,7},{7,6},{8,9},{9,8},{10,11... | collective-permute-start | bytes 2359304 | tf_op jit(solution)/shard_map/ppermute | solution.py:227
  108.9 17.5 %collective-permute-start.18 = (bf16[8,2,64,384]{3,2,1,0:T(8,128)(2,1)}, bf16[8,2,64,384]{3,2,1,0:T(8,128)(2,1)}, u32[]{:S(2)}, u32[]{:S(2)}) collective-permute-start(bf16[8,2,64,384]{3,2,1,0:T(8,128)(2,1)} %collective-permute-done.17.anchor_ref), channel_id=1, source_target_pairs={{0,1},{1,0},{2,3},{3,2},{4,5},{5,4},{6,7},{7,6},{8,9},{9,8},{10,11... | collective-permute-start | bytes 2359304 | tf_op jit(solution)/shard_map/ppermute | solution.py:227
  109.7 1.4 %copy-start.1 = (bf16[512,1536]{1,0:T(8,128)(2,1)S(1)}, bf16[512,1536]{1,0:T(8,128)(2,1)}, u32[]{:S(2)}) copy-start(bf16[512,1536]{1,0:T(8,128)(2,1)} %q_ref.7) | copy-start | bytes 4718596

commit v4 on v3

v4 whole, which is shorter than its diff:
```python
import functools
import math

import jax
import jax.numpy as jnp
from jax import lax
from jax.experimental import pallas as pl
from jax.experimental.pallas import tpu as pltpu
from jax.sharding import PartitionSpec as P

HSZ = 128
NAMB = 512
NEG = -1e30
FLOOR = -2000.0
EXTRA = 16
TILE = 256
C2 = math.log2(math.e) / math.sqrt(HSZ)
BOTH = ("hst", "grp")


def dot_t(a, b):
    return lax.dot_general(a, b, (((1,), (1,)), ((), ())), preferred_element_type=jnp.float32)


def dot(a, b):
    return lax.dot_general(a, b, (((1,), (0,)), ((), ())), preferred_element_type=jnp.float32)


def softmax(scores):
    top = functools.reduce(jnp.maximum, [jnp.max(s, axis=-1, keepdims=True) for s in scores])
    base = top * C2
    weights = [jnp.exp2(s * C2 - base) for s in scores]
    total = functools.reduce(jnp.add, [jnp.sum(w, axis=-1, keepdims=True) for w in weights])
    return base, total, [w.astype(jnp.bfloat16) for w in weights]


def pack_kernel(kv_ref, out_ref):
    groups, _, _, part = out_ref.shape
    for g in range(groups):
        out_ref[g, 0] = kv_ref[0, :, g * part : (g + 1) * part]


def pack(kv, groups):
    _, rows, width = kv.shape
    part = width // groups
    few = rows // 4
    return pl.pallas_call(
        pack_kernel,
        grid=(2, 4),
        in_specs=[pl.BlockSpec((1, few, width), lambda s, i: (s, i, 0))],
        out_specs=pl.BlockSpec((groups, 1, few, part), lambda s, i: (0, s, i, 0)),
        out_shape=jax.ShapeDtypeStruct((groups, 2, rows, part), kv.dtype),
        cost_estimate=pl.CostEstimate(flops=0, bytes_accessed=4 * kv.size, transcendentals=0),
        name="pack_heads",
    )(kv)


def pipelined(tasks, score, finish):
    ahead = score(tasks[0])
    for n, task in enumerate(tasks):
        scores = ahead
        if n + 1 < len(tasks):
            ahead = score(tasks[n + 1])
        finish(task, scores)


def suffix_kernel(at_ref, q_ref, kv_ref, sk_ref, bias_ref, *rest):
    out_ref = rest[-1]
    host = at_ref[0]
    groups = kv_ref.shape[0]
    hosts, share, _ = q_ref.shape
    apart = list(range(0, hosts, 2)) + list(range(1, hosts, 2))
    chunks = min(hosts, max(1, TILE // share))
    bias = [bias_ref[pl.ds(host * groups + g, 1), :] for g in range(groups)]
    values = [kv_ref[g, 1] for g in range(groups)] + [sk_ref[1]]

    def score(first):
        q = jnp.concatenate([q_ref[first + c] for c in range(chunks)], axis=0)
        s = dot_t(q, sk_ref[0])
        row = lax.broadcasted_iota(jnp.int32, (share, share), 0)
        spos = host * share + lax.broadcasted_iota(jnp.int32, (share, share), 1)
        late = []
        for c in range(chunks):
            qpos = jnp.bitwise_xor(host, apart[first + c]) * share + row
            late.append(jnp.where(spos <= qpos, s[c * share : (c + 1) * share], NEG))
        return [dot_t(q, kv_ref[g, 0]) + bias[g] for g in range(groups)] + [jnp.concatenate(late, axis=0)]

    def finish(first, scores):
        base, total, weights = softmax(scores)
        mixed = functools.reduce(jnp.add, [dot(w, v) for w, v in zip(weights, values)])
        n = mixed / total
        size = jnp.max(jnp.abs(n), axis=-1, keepdims=True)
        shift = jnp.clip(jnp.floor(jnp.log2(size)), -100.0, 100.0)
        level = jnp.maximum(base + jnp.log2(total), FLOOR)
        whole = jnp.floor(level)
        rest = jnp.exp2(level - whole)
        coarse = jnp.round(rest * 512.0) * (1.0 / 512.0)
        fine = (rest - coarse) * 1024.0
        lane = lax.broadcasted_iota(jnp.int32, (chunks * share, HSZ), 1)
        stats = jnp.where(lane == 0, whole, jnp.where(lane == 1, coarse, jnp.where(lane == 2, fine, shift)))
        turned = stats.T
        n = n * jnp.exp2(-shift)
        for c in range(chunks):
            to = jnp.bitwise_xor(host, apart[first + c])
            out_ref[to, :share, :] = n[c * share : (c + 1) * share]
            out_ref[to, share : share + EXTRA, :share] = turned[:EXTRA, c * share : (c + 1) * share]

    pipelined(list(range(0, hosts, chunks)), score, finish)


def suffix_attend(host, q, kv, sk, bias, head, before):
    hosts, share, width = q.shape
    groups, _, rows, _ = kv.shape
    seen = groups * rows + share
    more = [] if before is None else [before]
    return pl.pallas_call(
        suffix_kernel,
        grid_spec=pltpu.PrefetchScalarGridSpec(
            num_scalar_prefetch=1,
            grid=(1,),
            in_specs=[
                pl.BlockSpec((hosts, share, HSZ), lambda i, at: (0, 0, head)),
                pl.BlockSpec((groups, 2, rows, HSZ), lambda i, at: (0, 0, 0, head)),
                pl.BlockSpec((2, share, HSZ), lambda i, at: (0, 0, head)),
                pl.BlockSpec(bias.shape, lambda i, at: (0, 0)),
            ]
            + [pl.BlockSpec(memory_space=pl.ANY) for _ in more],
            out_specs=pl.BlockSpec((hosts, share + EXTRA, HSZ), lambda i, at: (0, 0, head)),
        ),
        out_shape=jax.ShapeDtypeStruct((hosts, share + EXTRA, width), jnp.float32),
        input_output_aliases={5: 0} if more else {},
        compiler_params=pltpu.CompilerParams(vmem_limit_bytes=48 * 1024 * 1024),
        cost_estimate=pl.CostEstimate(
            flops=8 * hosts * share * seen * HSZ,
            bytes_accessed=4 * (groups * rows + 3 * hosts * share) * HSZ,
            transcendentals=hosts * share * seen,
        ),
        name="suffix_attend",
    )(host, q, kv, sk, bias, *more)


def combine_kernel(in_ref, out_ref):
    hosts, tall, _ = in_ref.shape
    share = tall - EXTRA
    whole, coarse, fine, shift = [in_ref[:, share + k, :] for k in range(4)]
    weight = jnp.exp2(whole - jnp.max(whole, axis=0, keepdims=True)) * (coarse + fine * (1.0 / 1024.0))
    factor = weight * jnp.exp2(shift) / jnp.sum(weight, axis=0, keepdims=True)
    factor = jnp.concatenate([factor, jnp.zeros((HSZ - hosts, HSZ), jnp.float32)], axis=0).T[:share, :]
    mixed = 0.0
    for g in range(hosts):
        mixed = mixed + factor[:, g : g + 1] * in_ref[g, :share, :]
    out_ref[...] = mixed.astype(out_ref.dtype)


def combine(parts):
    hosts, tall, width = parts.shape
    return pl.pallas_call(
        combine_kernel,
        grid=(width // HSZ,),
        in_specs=[pl.BlockSpec((hosts, tall, HSZ), lambda h: (0, 0, h))],
        out_specs=pl.BlockSpec((tall - EXTRA, HSZ), lambda h: (0, h)),
        out_shape=jax.ShapeDtypeStruct((tall - EXTRA, width), jnp.bfloat16),
        cost_estimate=pl.CostEstimate(flops=2 * parts.size, bytes_accessed=4 * parts.size, transcendentals=0),
        name="combine_groups",
    )(parts)


def context_kernel(at_ref, len_ref, q_ref, kv_ref, bias_ref, near_ref, far_ref, *rest):
    out_ref, diag_ref = rest[-2:]
    block, odd = at_ref[0], at_ref[2]
    rows, width = q_ref.shape
    half = rows // 2
    own = bias_ref[pl.ds(block, 1), :]
    row = lax.broadcasted_iota(jnp.int32, (half, half), 0)
    col = lax.broadcasted_iota(jnp.int32, (half, half), 1)
    for t in range(2):
        ok = own[:, t * half : (t + 1) * half]
        diag_ref[t] = jnp.where(col == row, 0.0, jnp.where(col < row, ok, NEG))
    low, high = bias_ref[0:1, :half], bias_ref[0:1, half:]
    near_bias = jnp.where(block > 0, jnp.where(odd == 0, low, high), NEG)
    far_bias = jnp.where(block > 0, jnp.where(odd == 0, high, low), NEG)

    def score(task):
        first, t = task
        head = slice(first, first + HSZ)
        q = q_ref[t * half : (t + 1) * half, head]
        scores = [dot_t(q, near_ref[0, :, head]) + near_bias, dot_t(q, far_ref[0, :, head]) + far_bias]
        if t == 1:
            scores.append(dot_t(q, kv_ref[0, :half, head]) + own[:, :half])
        scores.append(dot_t(q, kv_ref[0, t * half : (t + 1) * half, head]) + diag_ref[t])
        return scores

    def finish(task, scores):
        first, t = task
        head = slice(first, first + HSZ)
        _, total, weights = softmax(scores)
        values = [near_ref[1, :, head], far_ref[1, :, head]]
        values += [kv_ref[1, u * half : (u + 1) * half, head] for u in range(t + 1)]
        mixed = functools.reduce(jnp.add, [dot(w, v) for w, v in zip(weights, values)])
        place = t * half + lax.broadcasted_iota(jnp.int32, mixed.shape, 0)
        out = jnp.where(place < len_ref[block], mixed / total, 0.0)
        out_ref[t * half : (t + 1) * half, head] = out.astype(out_ref.dtype)

    pipelined([(first, t) for first in range(0, width, HSZ) for t in range(2)], score, finish)


def context_attend(at, lengths, q, kv, bias, near, far, before):
    rows, width = q.shape
    _, half, wide = near.shape
    heads = wide // HSZ
    both = lambda i, at, n: (0, 0, at[1])
    more = [] if before is None else [before]
    return pl.pallas_call(
        context_kernel,
        grid_spec=pltpu.PrefetchScalarGridSpec(
            num_scalar_prefetch=2,
            grid=(1,),
            in_specs=[
                pl.BlockSpec((rows, wide), lambda i, at, n: (0, at[1])),
                pl.BlockSpec((2, rows, wide), both),
                pl.BlockSpec(bias.shape, lambda i, *_: (0, 0)),
                pl.BlockSpec((2, half, wide), lambda i, *_: (0, 0, 0)),
                pl.BlockSpec((2, half, wide), lambda i, *_: (0, 0, 0)),
            ]
            + [pl.BlockSpec(memory_space=pl.ANY) for _ in more],
            out_specs=pl.BlockSpec((rows, wide), lambda i, at, n: (0, at[1])),
            scratch_shapes=[pltpu.VMEM((2, half, half), jnp.float32)],
        ),
        out_shape=jax.ShapeDtypeStruct((rows, width), q.dtype),
        input_output_aliases={7: 0} if more else {},
        compiler_params=pltpu.CompilerParams(vmem_limit_bytes=48 * 1024 * 1024),
        cost_estimate=pl.CostEstimate(
            flops=8 * rows * rows * wide,
            bytes_accessed=12 * rows * wide,
            transcendentals=2 * rows * rows * heads,
        ),
        name="context_attend",
    )(at, lengths, q, kv, bias, near, far, *more)


def swap(x, axis, k):
    return lax.ppermute(x, axis, [(i, i ^ k) for i in range(lax.axis_size(axis))])


def gather_hosts(x, hosts):
    near = jnp.stack([x] + [swap(x, "hst", k) for k in range(2, hosts, 2)], axis=0)
    far = swap(near, "hst", 1)
    return jnp.concatenate([near, far], axis=0)


def after(x, done):
    return lax.optimization_barrier((x, done))[0]


def anchor_quarters(kv):
    _, rows, width = kv.shape
    tall, wide = rows // 2, width // 2
    quarter = lambda y, x: kv[:, y * tall : (y + 1) * tall, x * wide : (x + 1) * wide]
    return [quarter(1, 1), quarter(0, 1), quarter(1, 0), quarter(0, 0)]


def spread_anchor(quarters, hosts, groups):
    cores = groups // 2
    first = (lax.axis_index("hst") == 0) & (lax.axis_index("grp") == 0)
    slab = jnp.where(first, quarters[3], 0.0)
    for quarter, to in zip(quarters, [groups + cores, cores, groups]):
        slab = slab + lax.ppermute(quarter, BOTH, [(0, to)])
    wide = slab.shape[2] // cores
    piece = slab[:, :, :wide]
    for c in range(1, cores):
        pairs = [(x, x + c) for x in (0, cores)]
        piece = piece + lax.ppermute(slab[:, :, c * wide : (c + 1) * wide], "grp", pairs)
    far = hosts // 2
    while far >= 2:
        pairs = [(h, h + far) for h in range(hosts) if h % (2 * far) < 2]
        piece = piece + lax.ppermute(piece, "hst", pairs)
        far //= 2
    return piece


def per_device(queries, keys_values, token_ids, lengths, suffix_queries, suffix_kv):
    hosts, groups = lax.axis_size("hst"), lax.axis_size("grp")
    host, group = lax.axis_index("hst"), lax.axis_index("grp")
    rows = queries.shape[0]
    heads = suffix_queries.shape[1] // HSZ
    quarters, keys_values = lax.optimization_barrier((anchor_quarters(keys_values), keys_values))
    swapped = lax.all_to_all(pack(keys_values, groups), "grp", split_axis=0, concat_axis=0, tiled=True)
    near = spread_anchor(quarters, hosts, groups)
    gathered = gather_hosts(suffix_queries, hosts)
    seen = (token_ids.reshape(-1, rows) >= NAMB) & (jnp.arange(rows)[None, :] < lengths[:, None])
    bias = jnp.where(seen, 0.0, NEG).astype(jnp.float32)
    cores = groups // 2
    far = swap(near, "hst", 1)
    other_near = swap(near, "grp", cores)
    parts = None
    for head in range(heads):
        parts = suffix_attend(jnp.stack([host]), gathered, swapped, suffix_kv, bias, head, parts)
        if head == 0:
            far = after(far, parts)
    held = {0: [near, far], cores: [other_near, swap(far, "grp", cores)]}
    for k in range(1, cores):
        held[k] = [swap(x, "grp", k) for x in held[0]]
    for k in range(1, cores):
        held[cores ^ k] = [swap(after(x, parts), "grp", k) for x in held[cores]]
    coded = lax.all_to_all(parts.astype(jnp.float16), "hst", split_axis=0, concat_axis=0, tiled=True)
    context_out = None
    for k in range(groups):
        at = jnp.stack([host * groups + group, group ^ k, host % 2])
        context_out = context_attend(at, lengths, queries, keys_values, bias, *held[k], context_out)
    return (context_out, combine(coded.astype(jnp.float32)))


def solution(mesh):
    return jax.shard_map(
        per_device,
        mesh=mesh,
        in_specs=(
            P(("hst", "grp"), None),
            P(None, ("hst", "grp"), None),
            P(),
            P(),
            P("hst", "grp"),
            P(None, "hst", "grp"),
        ),
        out_specs=(P(("hst", "grp"), None), P("hst", "grp")),
        check_vma=False,
    )
```

time: 139 us -> 134 us (0.964)
  starting transfers between devices: 53.8 us -> 33.5 us
  waiting for transfers between devices: 19.7 us -> 39.3 us
  Pallas kernels: 47.4 us -> 39.8 us
  other arithmetic: 6.84 us -> 9.77 us
    ppermute x11, starting transfers between devices: 25.1 us -> 8.25 us  [swap(): lax.ppermute(x, axis, [(i, i ^ k) for i in range(lax.axis_size(axis))])]
    ppermute x11, waiting for transfers between devices: 6.12 us -> 18.9 us  [swap(): lax.ppermute(x, axis, [(i, i ^ k) for i in range(lax.axis_size(axis))])]
    ppermute x13 -> x6, waiting for transfers between devices: 13.6 us -> 19.7 us  [the longest x2 13.8 us: spread_anchor(): piece = piece + lax.ppermute(piece, 'hst', pairs)]
    pallas_call x3, Pallas kernels: 17.3 us -> 12.8 us  [suffix_attend(): pl.pallas_call(suffix_kernel, grid_spec=pltpu.PrefetchScalarGridSpec(num_...]
    ppermute x13 -> x6, starting transfers between devices: 18.7 us -> 14.8 us  [the longest x3 10.1 us: spread_anchor(): slab = slab + lax.ppermute(quarter, BOTH, [(0, to)])]
    add x1 -> x4, other arithmetic: 1.15 us -> 4.82 us  [the longest x2 2.05 us: spread_anchor(): piece = piece + lax.ppermute(piece, 'hst', pairs)]
    pallas_call x4, Pallas kernels: 20.4 us -> 17.3 us  [context_attend(): pl.pallas_call(context_kernel, grid_spec=pltpu.PrefetchScalarGridSpec(num...]
    slice x2, local copies, waits for them, and re-layouts: 1.59 us -> 3.68 us  [the longest x1 3.64 us: anchor_quarters(): kv[:, y * tall:(y + 1) * tall, x * wide:(x + 1) * wide]]
  transfers between devices with their start and end apart: 26 -> 19, of which waited for: 8 -> 8; matrix products, arithmetic and copies ran while one was open for 7% -> 6% of each run, Pallas kernels for 32% -> 21%
where the time goes in v4:
time: 134 us; the launch traced here: 133 us
  Pallas kernels  39.8 us (30%)
  waiting for transfers between devices  39.3 us (29%)
  starting transfers between devices  33.5 us (25%)
  other arithmetic  9.77 us (7%)
  local copies, waits for them, and re-layouts  9.47 us (7%)
    ppermute x11, waiting for transfers between devices, swap(): lax.ppermute(x, axis, [(i, i ^ k) for i in range(lax.axis_size(axis))])  18.9 us
    pallas_call x4, Pallas kernels, context_attend(): pl.pallas_call(context_kernel, grid_spec=pltpu.PrefetchScalarGridSpec(num...  17.3 us
    ppermute x2, waiting for transfers between devices, spread_anchor(): piece = piece + lax.ppermute(piece, 'hst', pairs)  13.8 us
    pallas_call x3, Pallas kernels, suffix_attend(): pl.pallas_call(suffix_kernel, grid_spec=pltpu.PrefetchScalarGridSpec(num_...  12.8 us
    ppermute x3, starting transfers between devices, spread_anchor(): slab = slab + lax.ppermute(quarter, BOTH, [(0, to)])  10.1 us
    ppermute x11, starting transfers between devices, swap(): lax.ppermute(x, axis, [(i, i ^ k) for i in range(lax.axis_size(axis))])  8.25 us
    all_to_all x1, starting transfers between devices, per_device(): lax.all_to_all(parts.astype(jnp.float16), 'hst', split_axis=0, concat_axi...  6.72 us
    pallas_call x1, Pallas kernels, pack(): pl.pallas_call(pack_kernel, grid=(2, 4), in_specs=[pl.BlockSpec((1, few,...  6.19 us
  transfers between devices with their start and end apart: 19, of which 8 were waited for; matrix products, arithmetic and copies ran while one was open for 6% of the time, Pallas kernels for 21%

profile of v4, /device:TPU:0, one launch (start us, length us, event | category | flops | bytes accessed | tf_op | source)
XLA Modules:
  0.0 132.7 jit_solution(17117332750649704482)
XLA Ops:
  0.6 3.6 %fusion.2 = (bf16[2,256,768]{2,1,0:T(8,128)(2,1)}, bf16[2,256,768]{2,1,0:T(8,128)(2,1)}, bf16[2,256,768]{2,1,0:T(8,128)(2,1)}, bf16[2,256,768]{2,1,0:T(8,128)(2,1)}) fusion(bf16[2,512,1536]{2,1,0:T(8,128)(2,1)} %kv_ref.4), kind=kLoop, calls=%fused_computation.16 | loop fusion | bytes 6291456 | tf_op jit(solution)/shard_map/slice | solution.py:258
  4.3 5.8 %collective-permute-start.2 = (bf16[2,256,768]{2,1,0:T(8,128)(2,1)}, bf16[2,256,768]{2,1,0:T(8,128)(2,1)}, u32[]{:S(2)}, u32[]{:S(2)}) collective-permute-start(bf16[2,256,768]{2,1,0:T(8,128)(2,1)} %get-tuple-element.14), channel_id=1, source_target_pairs={{0,4}} | collective-permute-start | bytes 2359304 | tf_op jit(solution)/shard_map/ppermute | solution.py:267
  10.0 2.2 %collective-permute-start.1 = (bf16[2,256,768]{2,1,0:T(8,128)(2,1)}, bf16[2,256,768]{2,1,0:T(8,128)(2,1)}, u32[]{:S(2)}, u32[]{:S(2)}) collective-permute-start(bf16[2,256,768]{2,1,0:T(8,128)(2,1)} %get-tuple-element.13), channel_id=1, source_target_pairs={{0,2}} | collective-permute-start | bytes 2359304 | tf_op jit(solution)/shard_map/ppermute | solution.py:267
  12.2 2.2 %collective-permute-start = (bf16[2,256,768]{2,1,0:T(8,128)(2,1)}, bf16[2,256,768]{2,1,0:T(8,128)(2,1)}, u32[]{:S(2)}, u32[]{:S(2)}) collective-permute-start(bf16[2,256,768]{2,1,0:T(8,128)(2,1)} %get-tuple-element.12), channel_id=1, source_target_pairs={{0,6}} | collective-permute-start | bytes 2359304 | tf_op jit(solution)/shard_map/ppermute | solution.py:267
  14.4 0.1 collective-permute-start.8
  14.6 6.2 %pack_heads.1 = bf16[4,2,512,384]{3,2,1,0:T(8,128)(2,1)} custom-call(bf16[2,512,1536]{2,1,0:T(8,128)(2,1)} %kv_ref.4), custom_call_target="tpu_custom_call" | custom-call | bytes 6291456 | tf_op jit(solution)/shard_map/pack_heads/pallas_call | solution.py:47
  20.7 3.7 %all-to-all-start = ((bf16[4,2,512,384]{3,2,1,0:T(8,128)(2,1)}), bf16[4,2,512,384]{3,2,1,0:T(8,128)(2,1)S(1)}, u32[]{:S(2)}, u32[]{:S(2)}) async-start(bf16[4,2,512,384]{3,2,1,0:T(8,128)(2,1)} %pack_heads.1), calls=%async_computation | async-start | bytes 6291456 | tf_op jit(solution)/shard_map/all_to_all | solution.py:287
  24.5 4.3 %collective-permute-start.9 = (bf16[128,384]{1,0:T(8,128)(2,1)S(1)}, bf16[128,384]{1,0:T(8,128)(2,1)S(1)}, u32[]{:S(2)}, u32[]{:S(2)}) collective-permute-start(bf16[128,384]{1,0:T(8,128)(2,1)S(1)} %copy-done.7), channel_id=1, source_target_pairs={{0,24},{4,28},{8,16},{12,20},{16,8},{20,12},{24,0},{28,4},{1,25},{... | collective-permute-start | bytes 294920 | tf_op jit(solution)/shard_map/ppermute | solution.py:242
  28.8 4.6 %collective-permute-done = bf16[2,256,768]{2,1,0:T(8,128)(2,1)} collective-permute-done((bf16[2,256,768]{2,1,0:T(8,128)(2,1)}, bf16[2,256,768]{2,1,0:T(8,128)(2,1)}, u32[]{:S(2)}, u32[]{:S(2)}) %collective-permute-start) | collective-permute-done | bytes 786464 | tf_op jit(solution)/shard_map/ppermute | solution.py:267
  33.4 2.0 %add_add_fusion = bf16[2,256,768]{2,1,0:T(8,128)(2,1)S(1)} fusion(bf16[2,256,768]{2,1,0:T(8,128)(2,1)} %collective-permute-done.2, bf16[2,256,768]{2,1,0:T(8,128)(2,1)} %collective-permute-done.1, bf16[2,256,768]{2,1,0:T(8,128)(2,1)} %collective-permute-done, bf16[2,256,768]{2,1,0:T(8,128)(2,1)} %get-tuple-element.11, pred[]{:T(512)S(6)} %and.18), kind=kLoop, calls=%fused_computation | loop fusion | flops 1572864 | bytes 3932161 | tf_op jit(solution)/shard_map/add | solution.py:267
  35.5 1.3 collective-permute-start.3
  36.8 1.3 collective-permute-done.3
  38.1 0.8 slice_add_fusion
  38.9 2.0 %collective-permute-start.4 = (bf16[2,256,384]{2,1,0:T(8,128)(2,1)}, bf16[2,256,384]{2,1,0:T(8,128)(2,1)}, u32[]{:S(2)}, u32[]{:S(2)}) collective-permute-start(bf16[2,256,384]{2,1,0:T(8,128)(2,1)} %slice_add_fusion), channel_id=1, source_target_pairs={{0,16},{4,20},{1,17},{5,21},{2,18},{6,22},{3,19},{7,23}} | collective-permute-start | bytes 1179656 | tf_op jit(solution)/shard_map/ppermute | solution.py:276
  40.9 0.7 constant_dynamic-update-slice_fusion.4
  41.6 0.1 fusion.1.bias_ref
  41.8 0.6 copy-done.8
  42.4 1.0 pad_maximum_fusion
  43.5 6.2 %collective-permute-done.4 = bf16[2,256,384]{2,1,0:T(8,128)(2,1)} collective-permute-done((bf16[2,256,384]{2,1,0:T(8,128)(2,1)}, bf16[2,256,384]{2,1,0:T(8,128)(2,1)}, u32[]{:S(2)}, u32[]{:S(2)}) %collective-permute-start.4) | collective-permute-done | bytes 393248 | tf_op jit(solution)/shard_map/ppermute | solution.py:276
  49.7 1.2 add.37
  50.9 1.3 collective-permute-start.5
  52.2 0.9 constant_dynamic-update-slice_fusion.2
  53.2 7.6 %collective-permute-done.5 = bf16[2,256,384]{2,1,0:T(8,128)(2,1)S(1)} collective-permute-done((bf16[2,256,384]{2,1,0:T(8,128)(2,1)S(1)}, bf16[2,256,384]{2,1,0:T(8,128)(2,1)S(1)}, u32[]{:S(2)}, u32[]{:S(2)}) %collective-permute-start.5) | collective-permute-done | bytes 393248 | tf_op jit(solution)/shard_map/ppermute | solution.py:276
  60.8 0.8 add.38.near_ref
  61.7 0.9 copy-done.4
  62.6 0.7 all-to-all-done.kv_ref
  63.3 1.1 copy-done.5
  64.4 4.2 %suffix_attend.3.rest_0_ = f32[8,144,384]{2,1,0:T(8,128)S(1)} custom-call(s32[1]{0:T(128)} %bitcast.3.at_ref, bf16[8,128,384]{2,1,0:T(8,128)(2,1)S(1)} %copy-done.5, bf16[4,2,512,384]{3,2,1,0:T(8,128)(2,1)S(1)} %all-to-all-done.kv_ref, bf16[2,128,384]{2,1,0:T(8,128)(2,1)S(1)} %copy-done.6, f32[32,512]{1,0:T(8,128)S(1)} %fusion.1.bias_ref), custom_call_target="tpu_custom_call" | custom-call | flops 2281701376 | bytes 2621440 | tf_op jit(solution)/shard_map/suffix_attend/pallas_call | solution.py:116
  68.6 3.6 %collective-permute-done.12.far_ref = bf16[2,256,384]{2,1,0:T(8,128)(2,1)} collective-permute-done((bf16[2,256,384]{2,1,0:T(8,128)(2,1)}, bf16[2,256,384]{2,1,0:T(8,128)(2,1)}, u32[]{:S(2)}, u32[]{:S(2)}) %collective-permute-start.12) | collective-permute-done | bytes 393248 | tf_op jit(solution)/shard_map/ppermute | solution.py:242
  72.2 4.2 %suffix_attend.4.rest_0_ = f32[8,144,384]{2,1,0:T(8,128)S(1)} custom-call(s32[1]{0:T(128)} %bitcast.3.at_ref, bf16[8,128,384]{2,1,0:T(8,128)(2,1)S(1)} %copy-done.5, bf16[4,2,512,384]{3,2,1,0:T(8,128)(2,1)S(1)} %all-to-all-done.kv_ref, bf16[2,128,384]{2,1,0:T(8,128)(2,1)S(1)} %copy-done.6, ...), custom_call_target="tpu_custom_call", output_to_operand_aliasing={{}: (5, {})} | custom-call | flops 2281701376 | bytes 2621440 | tf_op jit(solution)/shard_map/suffix_attend/pallas_call | solution.py:116
  76.4 4.4 %suffix_attend.5 = f32[8,144,384]{2,1,0:T(8,128)S(1)} custom-call(s32[1]{0:T(128)} %bitcast.3.at_ref, bf16[8,128,384]{2,1,0:T(8,128)(2,1)S(1)} %copy-done.5, bf16[4,2,512,384]{3,2,1,0:T(8,128)(2,1)S(1)} %all-to-all-done.kv_ref, bf16[2,128,384]{2,1,0:T(8,128)(2,1)S(1)} %copy-done.6, f32[32,512]{1,0:T(8,128)S(1)} %fusion.1.bias_ref, ...), custom_call_target="tpu_custom_call", output_to_operand_aliasing={{}: (5, {})} | custom-call | flops 2281701376 | bytes 2621440 | tf_op jit(solution)/shard_map/suffix_attend/pallas_call | solution.py:116
  80.8 1.1 convert_element_type.8
  81.9 6.7 %all-to-all-start.1 = ((f16[8,144,384]{2,1,0:T(8,128)(2,1)}), f16[8,144,384]{2,1,0:T(8,128)(2,1)}, u32[]{:S(2)}, u32[]{:S(2)}) async-start(f16[8,144,384]{2,1,0:T(8,128)(2,1)} %convert_element_type.8), calls=%async_computation.1 | async-start | bytes 1769472 | tf_op jit(solution)/shard_map/all_to_all | solution.py:305
  88.6 3.1 %collective-permute-start.6 = (bf16[2,256,384]{2,1,0:T(8,128)(2,1)}, bf16[2,256,384]{2,1,0:T(8,128)(2,1)}, u32[]{:S(2)}, u32[]{:S(2)}) collective-permute-start(bf16[2,256,384]{2,1,0:T(8,128)(2,1)} %add.38.near_ref), channel_id=1, source_target_pairs={{0,2},{1,3},{2,0},{3,1},{4,6},{5,7},{6,4},{7,5},{8,10},{9,11},{10,... | collective-permute-start | bytes 1179656 | tf_op jit(solution)/shard_map/ppermute | solution.py:242
  91.8 0.1 add_add_fusion.1.at_ref
  91.9 0.5 collective-permute-start.16
  92.4 0.1 add_add_fusion.2.at_ref
  92.5 9.6 %collective-permute-done.6.near_ref = bf16[2,256,384]{2,1,0:T(8,128)(2,1)} collective-permute-done((bf16[2,256,384]{2,1,0:T(8,128)(2,1)}, bf16[2,256,384]{2,1,0:T(8,128)(2,1)}, u32[]{:S(2)}, u32[]{:S(2)}) %collective-permute-start.6) | collective-permute-done | bytes 393248 | tf_op jit(solution)/shard_map/ppermute | solution.py:242
  102.1 5.7 %collective-permute-done.13.far_ref = bf16[2,256,384]{2,1,0:T(8,128)(2,1)} collective-permute-done((bf16[2,256,384]{2,1,0:T(8,128)(2,1)}, bf16[2,256,384]{2,1,0:T(8,128)(2,1)}, u32[]{:S(2)}, u32[]{:S(2)}) %collective-permute-start.13) | collective-permute-done | bytes 393248 | tf_op jit(solution)/shard_map/ppermute | solution.py:242
  107.8 0.1 add_add_fusion.3.at_ref
  107.9 0.1 add_add_fusion.4.at_ref
  108.0 1.4 %copy-done.1 = bf16[512,1536]{1,0:T(8,128)(2,1)S(1)} copy-done((bf16[512,1536]{1,0:T(8,128)(2,1)S(1)}, bf16[512,1536]{1,0:T(8,128)(2,1)}, u32[]{:S(2)}) %copy-start.1) | copy-done | bytes 1572888
  109.4 4.8 %context_attend.4.rest_0_ = bf16[512,1536]{1,0:T(8,128)(2,1)} custom-call(s32[3]{0:T(128)S(1)} %add_add_fusion.4.at_ref, s32[32]{0:T(128)S(1)} %copy-done.2, bf16[512,1536]{1,0:T(8,128)(2,1)S(1)} %copy-done.1, bf16[2,512,1536]{2,1,0:T(8,128)(2,1)S(1)} %copy-done, f32[32,512]{1,0:T(8,128)S(1)} %fusion.1.bias_ref, bf16[2,256,384]{2,1,0:T(8,128)(2,1)} %add.38.near_ref, ...), custom_call_target="tpu_custom_call" | custom-call | flops 805306368 | bytes 2359296 | tf_op jit(solution)/shard_map/context_attend/pallas_call | solution.py:213
  114.2 3.8 %context_attend.5.rest_0_ = bf16[512,1536]{1,0:T(8,128)(2,1)} custom-call(s32[3]{0:T(128)S(1)} %add_add_fusion.3.at_ref, s32[32]{0:T(128)S(1)} %copy-done.2, bf16[512,1536]{1,0:T(8,128)(2,1)S(1)} %copy-done.1, bf16[2,512,1536]{2,1,0:T(8,128)(2,1)S(1)} %copy-done, f32[32,512]{1,0:T(8,128)S(1)} %fusion.1.bias_ref, ...), custom_call_target="tpu_custom_call", output_to_operand_aliasing={{}: (7, {})} | custom-call | flops 805306368 | bytes 2359296 | tf_op jit(solution)/shard_map/context_attend/pallas_call | solution.py:213
  118.0 4.8 %context_attend.6.rest_0_ = bf16[512,1536]{1,0:T(8,128)(2,1)} custom-call(s32[3]{0:T(128)S(1)} %add_add_fusion.2.at_ref, s32[32]{0:T(128)S(1)} %copy-done.2, bf16[512,1536]{1,0:T(8,128)(2,1)S(1)} %copy-done.1, bf16[2,512,1536]{2,1,0:T(8,128)(2,1)S(1)} %copy-done, f32[32,512]{1,0:T(8,128)S(1)} %fusion.1.bias_ref, ...), custom_call_target="tpu_custom_call", output_to_operand_aliasing={{}: (7, {})} | custom-call | flops 805306368 | bytes 2359296 | tf_op jit(solution)/shard_map/context_attend/pallas_call | solution.py:213
  122.9 3.9 %context_attend.7 = bf16[512,1536]{1,0:T(8,128)(2,1)} custom-call(s32[3]{0:T(128)S(1)} %add_add_fusion.1.at_ref, s32[32]{0:T(128)S(1)} %copy-done.2, bf16[512,1536]{1,0:T(8,128)(2,1)S(1)} %copy-done.1, bf16[2,512,1536]{2,1,0:T(8,128)(2,1)S(1)} %copy-done, f32[32,512]{1,0:T(8,128)S(1)} %fusion.1.bias_ref, ...), custom_call_target="tpu_custom_call", output_to_operand_aliasing={{}: (7, {})} | custom-call | flops 805306368 | bytes 2359296 | tf_op jit(solution)/shard_map/context_attend/pallas_call | solution.py:213
  126.7 2.5 %convert_element_type.9.in_ref = f32[8,144,384]{2,1,0:T(8,128)} convert(f16[8,144,384]{2,1,0:T(8,128)(2,1)} %all-to-all-done.1) | non-fusion elementwise | flops 442368 | bytes 2654208 | tf_op jit(solution)/shard_map/convert_element_type | solution.py:310
  129.2 3.5 %combine_groups.1 = bf16[128,384]{1,0:T(8,128)(2,1)} custom-call(f32[8,144,384]{2,1,0:T(8,128)} %convert_element_type.9.in_ref), custom_call_target="tpu_custom_call" | custom-call | flops 884736 | bytes 1769472 | tf_op jit(solution)/shard_map/combine_groups/pallas_call | solution.py:157
  (42 shorter events, 0.4 us)
Async XLA Ops:
  0.6 13.8 %copy-start.7 = (bf16[128,384]{1,0:T(8,128)(2,1)S(1)}, bf16[128,384]{1,0:T(8,128)(2,1)}, u32[]{:S(2)}) copy-start(bf16[128,384]{1,0:T(8,128)(2,1)} %param.10) | copy-start | bytes 294916
  4.3 20.2 %collective-permute-start.2 = (bf16[2,256,768]{2,1,0:T(8,128)(2,1)}, bf16[2,256,768]{2,1,0:T(8,128)(2,1)}, u32[]{:S(2)}, u32[]{:S(2)}) collective-permute-start(bf16[2,256,768]{2,1,0:T(8,128)(2,1)} %get-tuple-element.14), channel_id=1, source_target_pairs={{0,4}} | collective-permute-start | bytes 2359304 | tf_op jit(solution)/shard_map/ppermute | solution.py:267
  10.0 18.8 %collective-permute-start.1 = (bf16[2,256,768]{2,1,0:T(8,128)(2,1)}, bf16[2,256,768]{2,1,0:T(8,128)(2,1)}, u32[]{:S(2)}, u32[]{:S(2)}) collective-permute-start(bf16[2,256,768]{2,1,0:T(8,128)(2,1)} %get-tuple-element.13), channel_id=1, source_target_pairs={{0,2}} | collective-permute-start | bytes 2359304 | tf_op jit(solution)/shard_map/ppermute | solution.py:267
  12.2 21.2 %collective-permute-start = (bf16[2,256,768]{2,1,0:T(8,128)(2,1)}, bf16[2,256,768]{2,1,0:T(8,128)(2,1)}, u32[]{:S(2)}, u32[]{:S(2)}) collective-permute-start(bf16[2,256,768]{2,1,0:T(8,128)(2,1)} %get-tuple-element.12), channel_id=1, source_target_pairs={{0,6}} | collective-permute-start | bytes 2359304 | tf_op jit(solution)/shard_map/ppermute | solution.py:267
  14.4 27.3 %collective-permute-start.7 = (bf16[128,384]{1,0:T(8,128)(2,1)S(1)}, bf16[128,384]{1,0:T(8,128)(2,1)S(1)}, u32[]{:S(2)}, u32[]{:S(2)}) collective-permute-start(bf16[128,384]{1,0:T(8,128)(2,1)S(1)} %copy-done.7), channel_id=1, source_target_pairs={{0,8},{4,12},{8,0},{12,4},{16,24},{20,28},{24,16},{28,20},{1,9},{5... | collective-permute-start | bytes 294920 | tf_op jit(solution)/shard_map/ppermute | solution.py:242
  14.4 27.3 %collective-permute-start.8 = (bf16[128,384]{1,0:T(8,128)(2,1)S(1)}, bf16[128,384]{1,0:T(8,128)(2,1)}, u32[]{:S(2)}, u32[]{:S(2)}) collective-permute-start(bf16[128,384]{1,0:T(8,128)(2,1)S(1)} %copy-done.7), channel_id=1, source_target_pairs={{0,16},{4,20},{8,24},{12,28},{16,0},{20,4},{24,8},{28,12},{1,17},{... | collective-permute-start | bytes 294920 | tf_op jit(solution)/shard_map/ppermute | solution.py:242
  20.7 42.5 %all-to-all-start = ((bf16[4,2,512,384]{3,2,1,0:T(8,128)(2,1)}), bf16[4,2,512,384]{3,2,1,0:T(8,128)(2,1)S(1)}, u32[]{:S(2)}, u32[]{:S(2)}) async-start(bf16[4,2,512,384]{3,2,1,0:T(8,128)(2,1)} %pack_heads.1), calls=%async_computation | async-start | bytes 6291456 | tf_op jit(solution)/shard_map/all_to_all | solution.py:287
  24.5 12.3 %copy-start.10 = (s32[16384]{0:T(1024)S(1)}, s32[16384]{0:T(1024)}, u32[]{:S(2)}) copy-start(s32[16384]{0:T(1024)} %param.8) | copy-start | bytes 196612
  24.5 17.3 %collective-permute-start.9 = (bf16[128,384]{1,0:T(8,128)(2,1)S(1)}, bf16[128,384]{1,0:T(8,128)(2,1)S(1)}, u32[]{:S(2)}, u32[]{:S(2)}) collective-permute-start(bf16[128,384]{1,0:T(8,128)(2,1)S(1)} %copy-done.7), channel_id=1, source_target_pairs={{0,24},{4,28},{8,16},{12,20},{16,8},{20,12},{24,0},{28,4},{1,25},{... | collective-permute-start | bytes 294920 | tf_op jit(solution)/shard_map/ppermute | solution.py:242
  35.4 6.2 %copy-start.2 = (s32[32]{0:T(128)S(1)}, s32[32]{0:T(128)}, u32[]{:S(2)}) copy-start(s32[32]{0:T(128)} %len_ref.7) | copy-start | bytes 388
  35.5 2.6 %collective-permute-start.3 = (bf16[2,256,384]{2,1,0:T(8,128)(2,1)S(1)}, bf16[2,256,384]{2,1,0:T(8,128)(2,1)S(1)}, u32[]{:S(2)}, u32[]{:S(2)}) collective-permute-start(bf16[2,256,384]{2,1,0:T(8,128)(2,1)S(1)} %slice.25), channel_id=1, source_target_pairs={{0,1},{2,3},{4,5},{6,7},{8,9},{10,11},{12,13},{14,15},{16,17},{18,... | collective-permute-start | bytes 1179656 | tf_op jit(solution)/shard_map/ppermute | solution.py:272
  38.9 10.8 %collective-permute-start.4 = (bf16[2,256,384]{2,1,0:T(8,128)(2,1)}, bf16[2,256,384]{2,1,0:T(8,128)(2,1)}, u32[]{:S(2)}, u32[]{:S(2)}) collective-permute-start(bf16[2,256,384]{2,1,0:T(8,128)(2,1)} %slice_add_fusion), channel_id=1, source_target_pairs={{0,16},{4,20},{1,17},{5,21},{2,18},{6,22},{3,19},{7,23}} | collective-permute-start | bytes 1179656 | tf_op jit(solution)/shard_map/ppermute | solution.py:276
  41.6 10.6 %copy-start.3 = (bf16[8,128,384]{2,1,0:T(8,128)(2,1)S(1)}, bf16[8,128,384]{2,1,0:T(8,128)(2,1)}, u32[]{:S(2)}) copy-start(bf16[8,128,384]{2,1,0:T(8,128)(2,1)} %constant_dynamic-update-slice_fusion.4) | copy-start | bytes 2359300
  41.8 0.6 copy-start.8
  43.4 18.3 %copy-start.9 = (bf16[128,384]{1,0:T(8,128)(2,1)S(1)}, bf16[128,384]{1,0:T(8,128)(2,1)}, u32[]{:S(2)}) copy-start(bf16[128,384]{1,0:T(8,128)(2,1)} %copy-done.8) | copy-start | bytes 294916
  43.4 19.9 %copy-start.6 = (bf16[2,128,384]{2,1,0:T(8,128)(2,1)S(1)}, bf16[2,128,384]{2,1,0:T(8,128)(2,1)}, u32[]{:S(2)}) copy-start(bf16[2,128,384]{2,1,0:T(8,128)(2,1)} %sk_ref.5) | copy-start | bytes 589828
  43.4 18.3 %collective-permute-start.10 = (bf16[4,128,384]{2,1,0:T(8,128)(2,1)S(1)}, bf16[4,128,384]{2,1,0:T(8,128)(2,1)S(1)}, u32[]{:S(2)}, u32[]{:S(2)}) collective-permute-start(bf16[4,128,384]{2,1,0:T(8,128)(2,1)S(1)} %pad_maximum_fusion), channel_id=1, source_target_pairs={{0,4},{4,0},{8,12},{12,8},{16,20},{20,16},{24,28},{28,24},{1,5},{5... | collective-permute-start | bytes 1179656 | tf_op jit(solution)/shard_map/ppermute | solution.py:242
  50.9 9.9 %collective-permute-start.5 = (bf16[2,256,384]{2,1,0:T(8,128)(2,1)S(1)}, bf16[2,256,384]{2,1,0:T(8,128)(2,1)S(1)}, u32[]{:S(2)}, u32[]{:S(2)}) collective-permute-start(bf16[2,256,384]{2,1,0:T(8,128)(2,1)S(1)} %add.37), channel_id=1, source_target_pairs={{0,8},{4,12},{16,24},{20,28},{1,9},{5,13},{17,25},{21,29},{2,10},{... | collective-permute-start | bytes 1179656 | tf_op jit(solution)/shard_map/ppermute | solution.py:276
  61.6 10.6 %collective-permute-start.12 = (bf16[2,256,384]{2,1,0:T(8,128)(2,1)}, bf16[2,256,384]{2,1,0:T(8,128)(2,1)}, u32[]{:S(2)}, u32[]{:S(2)}) collective-permute-start(bf16[2,256,384]{2,1,0:T(8,128)(2,1)} %add.38.near_ref), channel_id=1, source_target_pairs={{0,4},{4,0},{8,12},{12,8},{16,20},{20,16},{24,28},{28,24},{1,5},{5... | collective-permute-start | bytes 1179656 | tf_op jit(solution)/shard_map/ppermute | solution.py:242
  61.7 0.9 copy-start.4
  63.3 1.1 copy-start.5
  80.8 27.2 %copy-start = (bf16[2,512,1536]{2,1,0:T(8,128)(2,1)S(1)}, bf16[2,512,1536]{2,1,0:T(8,128)(2,1)}, u32[]{:S(2)}) copy-start(bf16[2,512,1536]{2,1,0:T(8,128)(2,1)} %kv_ref.4) | copy-start | bytes 9437188
  81.9 44.8 %all-to-all-start.1 = ((f16[8,144,384]{2,1,0:T(8,128)(2,1)}), f16[8,144,384]{2,1,0:T(8,128)(2,1)}, u32[]{:S(2)}, u32[]{:S(2)}) async-start(f16[8,144,384]{2,1,0:T(8,128)(2,1)} %convert_element_type.8), calls=%async_computation.1 | async-start | bytes 1769472 | tf_op jit(solution)/shard_map/all_to_all | solution.py:305
  88.6 13.5 %collective-permute-start.6 = (bf16[2,256,384]{2,1,0:T(8,128)(2,1)}, bf16[2,256,384]{2,1,0:T(8,128)(2,1)}, u32[]{:S(2)}, u32[]{:S(2)}) collective-permute-start(bf16[2,256,384]{2,1,0:T(8,128)(2,1)} %add.38.near_ref), channel_id=1, source_target_pairs={{0,2},{1,3},{2,0},{3,1},{4,6},{5,7},{6,4},{7,5},{8,10},{9,11},{10,... | collective-permute-start | bytes 1179656 | tf_op jit(solution)/shard_map/ppermute | solution.py:242
  91.7 16.1 %collective-permute-start.13 = (bf16[2,256,384]{2,1,0:T(8,128)(2,1)}, bf16[2,256,384]{2,1,0:T(8,128)(2,1)}, u32[]{:S(2)}, u32[]{:S(2)}) collective-permute-start(bf16[2,256,384]{2,1,0:T(8,128)(2,1)} %collective-permute-done.12.far_ref), channel_id=1, source_target_pairs={{0,2},{1,3},{2,0},{3,1},{4,6},{5,7},{6,4},{7,5},{8,10},{9,11},{10,... | collective-permute-start | bytes 1179656 | tf_op jit(solution)/shard_map/ppermute | solution.py:242
  91.9 22.3 %collective-permute-start.15 = (bf16[2,256,384]{2,1,0:T(8,128)(2,1)}, bf16[2,256,384]{2,1,0:T(8,128)(2,1)S(1)}, u32[]{:S(2)}, u32[]{:S(2)}) collective-permute-start(bf16[2,256,384]{2,1,0:T(8,128)(2,1)} %add.38.near_ref), channel_id=1, source_target_pairs={{0,1},{1,0},{2,3},{3,2},{4,5},{5,4},{6,7},{7,6},{8,9},{9,8},{10,11... | collective-permute-start | bytes 1179656 | tf_op jit(solution)/shard_map/ppermute | solution.py:242
  91.9 22.3 %collective-permute-start.16 = (bf16[2,256,384]{2,1,0:T(8,128)(2,1)}, bf16[2,256,384]{2,1,0:T(8,128)(2,1)S(1)}, u32[]{:S(2)}, u32[]{:S(2)}) collective-permute-start(bf16[2,256,384]{2,1,0:T(8,128)(2,1)} %collective-permute-done.12.far_ref), channel_id=1, source_target_pairs={{0,1},{1,0},{2,3},{3,2},{4,5},{5,4},{6,7},{7,6},{8,9},{9,8},{10,11... | collective-permute-start | bytes 1179656 | tf_op jit(solution)/shard_map/ppermute | solution.py:242
  102.1 20.8 %collective-permute-start.11 = (bf16[2,256,384]{2,1,0:T(8,128)(2,1)}, bf16[2,256,384]{2,1,0:T(8,128)(2,1)S(1)}, u32[]{:S(2)}, u32[]{:S(2)}) collective-permute-start(bf16[2,256,384]{2,1,0:T(8,128)(2,1)} %collective-permute-done.6.near_ref), channel_id=1, source_target_pairs={{0,1},{1,0},{2,3},{3,2},{4,5},{5,4},{6,7},{7,6},{8,9},{9,8},{10,11... | collective-permute-start | bytes 1179656 | tf_op jit(solution)/shard_map/ppermute | solution.py:242
  107.8 15.1 %collective-permute-start.14 = (bf16[2,256,384]{2,1,0:T(8,128)(2,1)}, bf16[2,256,384]{2,1,0:T(8,128)(2,1)S(1)}, u32[]{:S(2)}, u32[]{:S(2)}) collective-permute-start(bf16[2,256,384]{2,1,0:T(8,128)(2,1)} %collective-permute-done.13.far_ref), channel_id=1, source_target_pairs={{0,1},{1,0},{2,3},{3,2},{4,5},{5,4},{6,7},{7,6},{8,9},{9,8},{10,11... | collective-permute-start | bytes 1179656 | tf_op jit(solution)/shard_map/ppermute | solution.py:242
  108.0 1.4 %copy-start.1 = (bf16[512,1536]{1,0:T(8,128)(2,1)S(1)}, bf16[512,1536]{1,0:T(8,128)(2,1)}, u32[]{:S(2)}) copy-start(bf16[512,1536]{1,0:T(8,128)(2,1)} %q_ref.7) | copy-start | bytes 4718596

commit v5 on v4

--- a/solution.py
+++ b/solution.py
@@ -108,7 +108,7 @@
     pipelined(list(range(0, hosts, chunks)), score, finish)
 
 
-def suffix_attend(host, q, kv, sk, bias, head, before):
+def suffix_attend(host, q, kv, sk, bias, first, count, before):
     hosts, share, width = q.shape
     groups, _, rows, _ = kv.shape
     seen = groups * rows + share
@@ -117,23 +117,23 @@
         suffix_kernel,
         grid_spec=pltpu.PrefetchScalarGridSpec(
             num_scalar_prefetch=1,
-            grid=(1,),
+            grid=(count,),
             in_specs=[
-                pl.BlockSpec((hosts, share, HSZ), lambda i, at: (0, 0, head)),
-                pl.BlockSpec((groups, 2, rows, HSZ), lambda i, at: (0, 0, 0, head)),
-                pl.BlockSpec((2, share, HSZ), lambda i, at: (0, 0, head)),
+                pl.BlockSpec((hosts, share, HSZ), lambda i, at: (0, 0, first + i)),
+                pl.BlockSpec((groups, 2, rows, HSZ), lambda i, at: (0, 0, 0, first + i)),
+                pl.BlockSpec((2, share, HSZ), lambda i, at: (0, 0, first + i)),
                 pl.BlockSpec(bias.shape, lambda i, at: (0, 0)),
             ]
             + [pl.BlockSpec(memory_space=pl.ANY) for _ in more],
-            out_specs=pl.BlockSpec((hosts, share + EXTRA, HSZ), lambda i, at: (0, 0, head)),
+            out_specs=pl.BlockSpec((hosts, share + EXTRA, HSZ), lambda i, at: (0, 0, first + i)),
         ),
         out_shape=jax.ShapeDtypeStruct((hosts, share + EXTRA, width), jnp.float32),
         input_output_aliases={5: 0} if more else {},
         compiler_params=pltpu.CompilerParams(vmem_limit_bytes=48 * 1024 * 1024),
         cost_estimate=pl.CostEstimate(
-            flops=8 * hosts * share * seen * HSZ,
-            bytes_accessed=4 * (groups * rows + 3 * hosts * share) * HSZ,
-            transcendentals=hosts * share * seen,
+            flops=8 * count * hosts * share * seen * HSZ,
+            bytes_accessed=4 * count * (groups * rows + 3 * hosts * share) * HSZ,
+            transcendentals=count * hosts * share * seen,
         ),
         name="suffix_attend",
     )(host, q, kv, sk, bias, *more)
@@ -248,14 +248,10 @@
     return jnp.concatenate([near, far], axis=0)
 
 
-def after(x, done):
-    return lax.optimization_barrier((x, done))[0]
-
-
-def anchor_quarters(kv):
-    _, rows, width = kv.shape
+def anchor_quarters(block):
+    rows, width = block.shape
     tall, wide = rows // 2, width // 2
-    quarter = lambda y, x: kv[:, y * tall : (y + 1) * tall, x * wide : (x + 1) * wide]
+    quarter = lambda y, x: block[y * tall : (y + 1) * tall, x * wide : (x + 1) * wide]
     return [quarter(1, 1), quarter(0, 1), quarter(1, 0), quarter(0, 0)]
 
 
@@ -265,11 +261,11 @@
     slab = jnp.where(first, quarters[3], 0.0)
     for quarter, to in zip(quarters, [groups + cores, cores, groups]):
         slab = slab + lax.ppermute(quarter, BOTH, [(0, to)])
-    wide = slab.shape[2] // cores
-    piece = slab[:, :, :wide]
+    wide = slab.shape[1] // cores
+    piece = slab[:, :wide]
     for c in range(1, cores):
         pairs = [(x, x + c) for x in (0, cores)]
-        piece = piece + lax.ppermute(slab[:, :, c * wide : (c + 1) * wide], "grp", pairs)
+        piece = piece + lax.ppermute(slab[:, c * wide : (c + 1) * wide], "grp", pairs)
     far = hosts // 2
     while far >= 2:
         pairs = [(h, h + far) for h in range(hosts) if h % (2 * far) < 2]
@@ -283,25 +279,27 @@
     host, group = lax.axis_index("hst"), lax.axis_index("grp")
     rows = queries.shape[0]
     heads = suffix_queries.shape[1] // HSZ
-    quarters, keys_values = lax.optimization_barrier((anchor_quarters(keys_values), keys_values))
-    swapped = lax.all_to_all(pack(keys_values, groups), "grp", split_axis=0, concat_axis=0, tiled=True)
-    near = spread_anchor(quarters, hosts, groups)
+    quarters, keys_values = lax.optimization_barrier(([anchor_quarters(x) for x in keys_values], keys_values))
+    packed, suffix_queries = lax.optimization_barrier((pack(keys_values, groups), suffix_queries))
+    swapped = lax.all_to_all(packed, "grp", split_axis=0, concat_axis=0, tiled=True)
+    near = jnp.stack([spread_anchor(x, hosts, groups) for x in quarters])
     gathered = gather_hosts(suffix_queries, hosts)
     seen = (token_ids.reshape(-1, rows) >= NAMB) & (jnp.arange(rows)[None, :] < lengths[:, None])
     bias = jnp.where(seen, 0.0, NEG).astype(jnp.float32)
     cores = groups // 2
-    far = swap(near, "hst", 1)
-    other_near = swap(near, "grp", cores)
-    parts = None
-    for head in range(heads):
-        parts = suffix_attend(jnp.stack([host]), gathered, swapped, suffix_kv, bias, head, parts)
-        if head == 0:
-            far = after(far, parts)
-    held = {0: [near, far], cores: [other_near, swap(far, "grp", cores)]}
+    suffix = functools.partial(suffix_attend, jnp.stack([host]), gathered, swapped, suffix_kv, bias)
+    parts = suffix(0, 1, None)
+    held = {0: [near, swap(near, "hst", 1)], cores: [swap(near, "grp", cores)]}
+    held, parts = lax.optimization_barrier((held, parts))
+    held[cores].append(swap(held[0][1], "grp", cores))
     for k in range(1, cores):
         held[k] = [swap(x, "grp", k) for x in held[0]]
+        held[cores ^ k] = [swap(held[cores][0], "grp", k)]
+    if heads > 1:
+        parts = suffix(1, heads - 1, parts)
+    held, parts = lax.optimization_barrier((held, parts))
     for k in range(1, cores):
-        held[cores ^ k] = [swap(after(x, parts), "grp", k) for x in held[cores]]
+        held[cores ^ k].append(swap(held[cores][1], "grp", k))
     coded = lax.all_to_all(parts.astype(jnp.float16), "hst", split_axis=0, concat_axis=0, tiled=True)
     context_out = None
     for k in range(groups):

time: 134 us -> 152 us (1.13)
  waiting for transfers between devices: 39.3 us -> 48 us
  starting transfers between devices: 33.5 us -> 40.8 us
  local copies, waits for them, and re-layouts: 9.47 us -> 12.7 us
  other arithmetic: 9.77 us -> 7.43 us
    ppermute x3 -> x6, waiting for transfers between devices: 4.61 us -> 27.6 us  [spread_anchor(): slab = slab + lax.ppermute(quarter, BOTH, [(0, to)])]
    ppermute x11, waiting for transfers between devices: 18.9 us -> 6.62 us  [swap(): lax.ppermute(x, axis, [(i, i ^ k) for i in range(lax.axis_size(axis))])]
    ppermute x3 -> x6, starting transfers between devices: 10.1 us -> 15.4 us  [spread_anchor(): slab = slab + lax.ppermute(quarter, BOTH, [(0, to)])]
    unnamed x26 -> x42, local copies, waits for them, and re-layouts: 5.69 us -> 8.77 us
    ppermute x2 -> x4, waiting for transfers between devices: 13.8 us -> 11.3 us  [spread_anchor(): piece = piece + lax.ppermute(piece, 'hst', pairs)]
    all_to_all x1, waiting for transfers between devices: 0.01 us -> 2.47 us  [per_device(): lax.all_to_all(parts.astype(jnp.float16), 'hst', split_axis=0, concat_axi...]
    ppermute x2 -> x4, starting transfers between devices: 3.35 us -> 5.52 us  [spread_anchor(): piece = piece + lax.ppermute(piece, 'hst', pairs)]
    all_to_all x1, starting transfers between devices: 6.72 us -> 4.56 us  [per_device(): lax.all_to_all(parts.astype(jnp.float16), 'hst', split_axis=0, concat_axi...]
  transfers between devices with their start and end apart: 19 -> 25, of which waited for: 8 -> 10; matrix products, arithmetic and copies ran while one was open for 6% -> 4% of each run, Pallas kernels for 21% -> 21%
where the time goes in v5:
time: 152 us; the launch traced here: 151 us
  waiting for transfers between devices  48 us (32%)
  starting transfers between devices  40.8 us (27%)
  Pallas kernels  40.7 us (27%)
  local copies, waits for them, and re-layouts  12.7 us (8%)
  other arithmetic  7.43 us (5%)
    ppermute x6, waiting for transfers between devices, spread_anchor(): slab = slab + lax.ppermute(quarter, BOTH, [(0, to)])  27.6 us
    pallas_call x4, Pallas kernels, context_attend(): pl.pallas_call(context_kernel, grid_spec=pltpu.PrefetchScalarGridSpec(num...  18.3 us
    ppermute x6, starting transfers between devices, spread_anchor(): slab = slab + lax.ppermute(quarter, BOTH, [(0, to)])  15.4 us
    pallas_call x2, Pallas kernels, suffix_attend(): pl.pallas_call(suffix_kernel, grid_spec=pltpu.PrefetchScalarGridSpec(num_...  12.7 us
    ppermute x4, waiting for transfers between devices, spread_anchor(): piece = piece + lax.ppermute(piece, 'hst', pairs)  11.3 us
    ppermute x11, starting transfers between devices, swap(): lax.ppermute(x, axis, [(i, i ^ k) for i in range(lax.axis_size(axis))])  8.95 us
    unnamed x42, local copies, waits for them, and re-layouts  8.77 us
    ppermute x11, waiting for transfers between devices, swap(): lax.ppermute(x, axis, [(i, i ^ k) for i in range(lax.axis_size(axis))])  6.62 us
  transfers between devices with their start and end apart: 25, of which 10 were waited for; matrix products, arithmetic and copies ran while one was open for 4% of the time, Pallas kernels for 21%

profile of v5, /device:TPU:0, one launch (start us, length us, event | category | flops | bytes accessed | tf_op | source)
XLA Modules:
  0.0 150.8 jit_solution(3173126365362443722)
XLA Ops:
  0.6 2.1 %slice_bitcast_fusion = (bf16[512,1536]{1,0:T(8,128)(2,1)S(1)}, bf16[512,1536]{1,0:T(8,128)(2,1)S(1)}) fusion(bf16[2,512,1536]{2,1,0:T(8,128)(2,1)} %kv_ref.4), kind=kLoop, calls=%fused_computation | loop fusion | bytes 6291456 | tf_op jit(solution)/shard_map/unstack | solution.py:282
  2.7 1.7 %fusion.2 = (bf16[256,768]{1,0:T(8,128)(2,1)}, bf16[256,768]{1,0:T(8,128)(2,1)}, bf16[256,768]{1,0:T(8,128)(2,1)}, bf16[256,768]{1,0:T(8,128)(2,1)}, bf16[256,76...) fusion(bf16[512,1536]{1,0:T(8,128)(2,1)S(1)} %get-tuple-element.48, ...), kind=kLoop, calls=%fused_computation.23 | loop fusion | bytes 6291456 | tf_op jit(solution)/shard_map/slice | solution.py:254
  4.4 6.2 %pack_heads.1 = bf16[4,2,512,384]{3,2,1,0:T(8,128)(2,1)} custom-call(bf16[2,512,1536]{2,1,0:T(8,128)(2,1)} %kv_ref.4), custom_call_target="tpu_custom_call" | custom-call | bytes 6291456 | tf_op jit(solution)/shard_map/pack_heads/pallas_call | solution.py:47
  10.6 5.1 %collective-permute-start.16 = (bf16[128,384]{1,0:T(8,128)(2,1)S(1)}, bf16[128,384]{1,0:T(8,128)(2,1)S(1)}, u32[]{:S(2)}, u32[]{:S(2)}) collective-permute-start(bf16[128,384]{1,0:T(8,128)(2,1)S(1)} %copy-done.17), channel_id=1, source_target_pairs={{0,24},{4,28},{8,16},{12,20},{16,8},{20,12},{24,0},{28,4},{1,25},{... | collective-permute-start | bytes 294920 | tf_op jit(solution)/shard_map/ppermute | solution.py:242
  15.8 5.1 %collective-permute-start = (bf16[256,768]{1,0:T(8,128)(2,1)}, bf16[256,768]{1,0:T(8,128)(2,1)}, u32[]{:S(2)}, u32[]{:S(2)}) collective-permute-start(bf16[256,768]{1,0:T(8,128)(2,1)} %get-tuple-element.27), channel_id=1, source_target_pairs={{0,6}} | collective-permute-start | bytes 1179656 | tf_op jit(solution)/shard_map/ppermute | solution.py:263
  20.9 2.0 %collective-permute-start.1 = (bf16[256,768]{1,0:T(8,128)(2,1)}, bf16[256,768]{1,0:T(8,128)(2,1)}, u32[]{:S(2)}, u32[]{:S(2)}) collective-permute-start(bf16[256,768]{1,0:T(8,128)(2,1)} %get-tuple-element.28), channel_id=1, source_target_pairs={{0,2}} | collective-permute-start | bytes 1179656 | tf_op jit(solution)/shard_map/ppermute | solution.py:263
  22.9 2.1 %collective-permute-start.2 = (bf16[256,768]{1,0:T(8,128)(2,1)}, bf16[256,768]{1,0:T(8,128)(2,1)}, u32[]{:S(2)}, u32[]{:S(2)}) collective-permute-start(bf16[256,768]{1,0:T(8,128)(2,1)} %get-tuple-element.29), channel_id=1, source_target_pairs={{0,4}} | collective-permute-start | bytes 1179656 | tf_op jit(solution)/shard_map/ppermute | solution.py:263
  24.9 3.7 %all-to-all-start = ((bf16[4,2,512,384]{3,2,1,0:T(8,128)(2,1)}), bf16[4,2,512,384]{3,2,1,0:T(8,128)(2,1)S(1)}, u32[]{:S(2)}, u32[]{:S(2)}) async-start(bf16[4,2,512,384]{3,2,1,0:T(8,128)(2,1)} %pack_heads.1), calls=%async_computation | async-start | bytes 6291456 | tf_op jit(solution)/shard_map/all_to_all | solution.py:284
  29.6 1.5 %constant_dynamic-update-slice_fusion.3 = bf16[8,128,384]{2,1,0:T(8,128)(2,1)} fusion(bf16[8,128,384]{2,1,0:T(8,128)(2,1)} %constant_dynamic-update-slice_fusion.4, bf16[128,384]{1,0:T(8,128)(2,1)} %collective-permute-done.14), kind=kLoop, calls=%fused_computation.17 | loop fusion | bytes 196608
  31.1 1.3 collective-permute-start.6
  32.4 3.2 %collective-permute-done.15 = bf16[128,384]{1,0:T(8,128)(2,1)S(1)} collective-permute-done((bf16[128,384]{1,0:T(8,128)(2,1)S(1)}, bf16[128,384]{1,0:T(8,128)(2,1)S(1)}, u32[]{:S(2)}, u32[]{:S(2)}) %collective-permute-start.15) | collective-permute-done | bytes 98336 | tf_op jit(solution)/shard_map/ppermute | solution.py:242
  35.6 3.6 %collective-permute-start.7 = (bf16[256,768]{1,0:T(8,128)(2,1)}, bf16[256,768]{1,0:T(8,128)(2,1)S(1)}, u32[]{:S(2)}, u32[]{:S(2)}) collective-permute-start(bf16[256,768]{1,0:T(8,128)(2,1)} %get-tuple-element.32), channel_id=1, source_target_pairs={{0,2}} | collective-permute-start | bytes 1179656 | tf_op jit(solution)/shard_map/ppermute | solution.py:263
  39.2 1.3 collective-permute-start.8
  40.5 1.0 pad_maximum_fusion.1
  41.7 1.4 add_add_fusion.1
  43.1 1.3 collective-permute-start.3
  44.4 23.4 %collective-permute-done.6 = bf16[256,768]{1,0:T(8,128)(2,1)S(1)} collective-permute-done((bf16[256,768]{1,0:T(8,128)(2,1)}, bf16[256,768]{1,0:T(8,128)(2,1)S(1)}, u32[]{:S(2)}, u32[]{:S(2)}) %collective-permute-start.6) | collective-permute-done | bytes 393248 | tf_op jit(solution)/shard_map/ppermute | solution.py:263
  67.8 4.2 %collective-permute-done.7 = bf16[256,768]{1,0:T(8,128)(2,1)S(1)} collective-permute-done((bf16[256,768]{1,0:T(8,128)(2,1)}, bf16[256,768]{1,0:T(8,128)(2,1)S(1)}, u32[]{:S(2)}, u32[]{:S(2)}) %collective-permute-start.7) | collective-permute-done | bytes 393248 | tf_op jit(solution)/shard_map/ppermute | solution.py:263
  72.2 1.4 collective-permute-start.9
  73.7 1.3 collective-permute-start.4
  75.0 1.3 collective-permute-start.10
  76.3 3.2 %collective-permute-done.4 = bf16[256,384]{1,0:T(8,128)(2,1)S(1)} collective-permute-done((bf16[256,384]{1,0:T(8,128)(2,1)S(1)}, bf16[256,384]{1,0:T(8,128)(2,1)S(1)}, u32[]{:S(2)}, u32[]{:S(2)}) %collective-permute-start.4) | collective-permute-done | bytes 196640 | tf_op jit(solution)/shard_map/ppermute | solution.py:272
  79.6 1.3 collective-permute-start.5
  81.0 2.8 %collective-permute-done.10 = bf16[256,384]{1,0:T(8,128)(2,1)S(1)} collective-permute-done((bf16[256,384]{1,0:T(8,128)(2,1)S(1)}, bf16[256,384]{1,0:T(8,128)(2,1)S(1)}, u32[]{:S(2)}, u32[]{:S(2)}) %collective-permute-start.10) | collective-permute-done | bytes 196640 | tf_op jit(solution)/shard_map/ppermute | solution.py:272
  83.8 1.6 %collective-permute-start.11 = (bf16[256,384]{1,0:T(8,128)(2,1)S(1)}, bf16[256,384]{1,0:T(8,128)(2,1)S(1)}, u32[]{:S(2)}, u32[]{:S(2)}) collective-permute-start(bf16[256,384]{1,0:T(8,128)(2,1)S(1)} %add.61), channel_id=1, source_target_pairs={{0,8},{4,12},{16,24},{20,28},{1,9},{5,13},{17,25},{21,29},{2,10},{... | collective-permute-start | bytes 589832 | tf_op jit(solution)/shard_map/ppermute | solution.py:272
  85.5 2.5 %collective-permute-done.5 = bf16[256,384]{1,0:T(8,128)(2,1)S(1)} collective-permute-done((bf16[256,384]{1,0:T(8,128)(2,1)S(1)}, bf16[256,384]{1,0:T(8,128)(2,1)S(1)}, u32[]{:S(2)}, u32[]{:S(2)}) %collective-permute-start.5) | collective-permute-done | bytes 196640 | tf_op jit(solution)/shard_map/ppermute | solution.py:272
  88.0 2.7 %collective-permute-done.11 = bf16[256,384]{1,0:T(8,128)(2,1)S(1)} collective-permute-done((bf16[256,384]{1,0:T(8,128)(2,1)S(1)}, bf16[256,384]{1,0:T(8,128)(2,1)S(1)}, u32[]{:S(2)}, u32[]{:S(2)}) %collective-permute-start.11) | collective-permute-done | bytes 196640 | tf_op jit(solution)/shard_map/ppermute | solution.py:272
  90.8 0.8 pad_maximum_fusion.near_ref
  91.6 2.4 %collective-permute-start.13 = (bf16[2,256,384]{2,1,0:T(8,128)(2,1)}, bf16[2,256,384]{2,1,0:T(8,128)(2,1)}, u32[]{:S(2)}, u32[]{:S(2)}) collective-permute-start(bf16[2,256,384]{2,1,0:T(8,128)(2,1)} %pad_maximum_fusion.near_ref), channel_id=1, source_target_pairs={{0,2},{1,3},{2,0},{3,1},{4,6},{5,7},{6,4},{7,5},{8,10},{9,11},{10,... | collective-permute-start | bytes 1179656 | tf_op jit(solution)/shard_map/ppermute | solution.py:242
  94.1 0.9 copy-done.12
  95.0 1.1 copy-done.13
  96.1 4.2 %suffix_attend.2.rest_0_ = f32[8,144,384]{2,1,0:T(8,128)S(1)} custom-call(s32[1]{0:T(128)} %bitcast.7.at_ref, bf16[8,128,384]{2,1,0:T(8,128)(2,1)S(1)} %copy-done.13, bf16[4,2,512,384]{3,2,1,0:T(8,128)(2,1)S(1)} %all-to-all-done.kv_ref, bf16[2,128,384]{2,1,0:T(8,128)(2,1)S(1)} %copy-done.15, f32[32,512]{1,0:T(8,128)S(1)} %fusion.1.bias_ref), custom_call_target="tpu_custom_call" | custom-call | flops 2281701376 | bytes 2621440 | tf_op jit(solution)/shard_map/suffix_attend/pallas_call | solution.py:116
  100.3 1.9 %collective-permute-done.13.near_ref = bf16[2,256,384]{2,1,0:T(8,128)(2,1)} collective-permute-done((bf16[2,256,384]{2,1,0:T(8,128)(2,1)}, bf16[2,256,384]{2,1,0:T(8,128)(2,1)}, u32[]{:S(2)}, u32[]{:S(2)}) %collective-permute-start.13) | collective-permute-done | bytes 393248 | tf_op jit(solution)/shard_map/ppermute | solution.py:242
  102.2 1.5 collective-permute-done.12.far_ref
  104.5 8.5 %suffix_attend.3 = f32[8,144,384]{2,1,0:T(8,128)S(1)} custom-call(s32[1]{0:T(128)} %bitcast.7.at_ref, bf16[8,128,384]{2,1,0:T(8,128)(2,1)S(1)} %copy-done.14, bf16[4,2,512,384]{3,2,1,0:T(8,128)(2,1)S(1)} %all-to-all-done.kv_ref, bf16[2,128,384]{2,1,0:T(8,128)(2,1)S(1)} %copy-done.15, f32[32,512]{1,0:T(8,128)S(1)} %fusion.1.bias_ref, ...), custom_call_target="tpu_custom_call", output_to_operand_aliasing={{}: (5, {})} | custom-call | flops 4563402752 | bytes 5242880 | tf_op jit(solution)/shard_map/suffix_attend/pallas_call | solution.py:116
  113.0 0.8 copy-done.8
  113.8 0.8 copy-done.4
  114.6 0.8 copy-done.2
  116.1 1.1 convert_element_type.9
  117.2 4.6 %all-to-all-start.1 = ((f16[8,144,384]{2,1,0:T(8,128)(2,1)}), f16[8,144,384]{2,1,0:T(8,128)(2,1)}, u32[]{:S(2)}, u32[]{:S(2)}) async-start(f16[8,144,384]{2,1,0:T(8,128)(2,1)} %convert_element_type.9), calls=%async_computation.1 | async-start | bytes 1769472 | tf_op jit(solution)/shard_map/all_to_all | solution.py:303
  122.5 1.4 copy-done.1
  123.9 4.8 %context_attend.4.rest_0_ = bf16[512,1536]{1,0:T(8,128)(2,1)} custom-call(s32[3]{0:T(128)S(1)} %get-tuple-element.59.at_ref, s32[32]{0:T(128)S(1)} %copy-done.10, bf16[512,1536]{1,0:T(8,128)(2,1)S(1)} %copy-done.1, bf16[2,512,1536]{2,1,0:T(8,128)(2,1)S(1)} %copy-done, f32[32,512]{1,0:T(8,128)S(1)} %fusion.1.bias_ref, ...), custom_call_target="tpu_custom_call" | custom-call | flops 805306368 | bytes 2359296 | tf_op jit(solution)/shard_map/context_attend/pallas_call | solution.py:213
  128.8 3.8 %context_attend.5.rest_0_ = bf16[512,1536]{1,0:T(8,128)(2,1)} custom-call(s32[3]{0:T(128)S(1)} %get-tuple-element.58.at_ref, s32[32]{0:T(128)S(1)} %copy-done.10, bf16[512,1536]{1,0:T(8,128)(2,1)S(1)} %copy-done.1, bf16[2,512,1536]{2,1,0:T(8,128)(2,1)S(1)} %copy-done, f32[32,512]{1,0:T(8,128)S(1)} %fusion.1.bias_ref, ...), custom_call_target="tpu_custom_call", output_to_operand_aliasing={{}: (7, {})} | custom-call | flops 805306368 | bytes 2359296 | tf_op jit(solution)/shard_map/context_attend/pallas_call | solution.py:213
  132.6 4.8 %context_attend.6.rest_0_ = bf16[512,1536]{1,0:T(8,128)(2,1)} custom-call(s32[3]{0:T(128)S(1)} %add_add_fusion.3.at_ref, s32[32]{0:T(128)S(1)} %copy-done.10, bf16[512,1536]{1,0:T(8,128)(2,1)S(1)} %copy-done.1, bf16[2,512,1536]{2,1,0:T(8,128)(2,1)S(1)} %copy-done, f32[32,512]{1,0:T(8,128)S(1)} %fusion.1.bias_ref, ...), custom_call_target="tpu_custom_call", output_to_operand_aliasing={{}: (7, {})} | custom-call | flops 805306368 | bytes 2359296 | tf_op jit(solution)/shard_map/context_attend/pallas_call | solution.py:213
  137.5 4.8 %context_attend.7 = bf16[512,1536]{1,0:T(8,128)(2,1)} custom-call(s32[3]{0:T(128)S(1)} %add_add_fusion.2.at_ref, s32[32]{0:T(128)S(1)} %copy-done.10, bf16[512,1536]{1,0:T(8,128)(2,1)S(1)} %copy-done.1, bf16[2,512,1536]{2,1,0:T(8,128)(2,1)S(1)} %copy-done, f32[32,512]{1,0:T(8,128)S(1)} %fusion.1.bias_ref, ...), custom_call_target="tpu_custom_call", output_to_operand_aliasing={{}: (7, {})} | custom-call | flops 805306368 | bytes 2359296 | tf_op jit(solution)/shard_map/context_attend/pallas_call | solution.py:213
  142.3 2.5 %all-to-all-done.1 = f16[8,144,384]{2,1,0:T(8,128)(2,1)} async-done(((f16[8,144,384]{2,1,0:T(8,128)(2,1)}), f16[8,144,384]{2,1,0:T(8,128)(2,1)}, u32[]{:S(2)}, u32[]{:S(2)}) %all-to-all-start.1) | async-done | bytes 884768 | tf_op jit(solution)/shard_map/all_to_all | solution.py:303
  144.8 2.5 %convert_element_type.10.in_ref = f32[8,144,384]{2,1,0:T(8,128)} convert(f16[8,144,384]{2,1,0:T(8,128)(2,1)} %all-to-all-done.1) | non-fusion elementwise | flops 442368 | bytes 2654208 | tf_op jit(solution)/shard_map/convert_element_type | solution.py:308
  147.3 3.5 %combine_groups.1 = bf16[128,384]{1,0:T(8,128)(2,1)} custom-call(f32[8,144,384]{2,1,0:T(8,128)} %convert_element_type.10.in_ref), custom_call_target="tpu_custom_call" | custom-call | flops 884736 | bytes 1769472 | tf_op jit(solution)/shard_map/combine_groups/pallas_call | solution.py:157
  (75 shorter events, 3.8 us)
Async XLA Ops:
  4.4 6.2 %copy-start.17 = (bf16[128,384]{1,0:T(8,128)(2,1)S(1)}, bf16[128,384]{1,0:T(8,128)(2,1)}, u32[]{:S(2)}) copy-start(bf16[128,384]{1,0:T(8,128)(2,1)} %param.10) | copy-start | bytes 294916
  10.6 18.7 %copy-start.18 = (s32[16384]{0:T(1024)S(1)}, s32[16384]{0:T(1024)}, u32[]{:S(2)}) copy-start(s32[16384]{0:T(1024)} %param.8) | copy-start | bytes 196612
  10.6 18.7 %copy-start.10 = (s32[32]{0:T(128)S(1)}, s32[32]{0:T(128)}, u32[]{:S(2)}) copy-start(s32[32]{0:T(128)} %len_ref.7) | copy-start | bytes 388
  10.6 20.5 %collective-permute-start.16 = (bf16[128,384]{1,0:T(8,128)(2,1)S(1)}, bf16[128,384]{1,0:T(8,128)(2,1)S(1)}, u32[]{:S(2)}, u32[]{:S(2)}) collective-permute-start(bf16[128,384]{1,0:T(8,128)(2,1)S(1)} %copy-done.17), channel_id=1, source_target_pairs={{0,24},{4,28},{8,16},{12,20},{16,8},{20,12},{24,0},{28,4},{1,25},{... | collective-permute-start | bytes 294920 | tf_op jit(solution)/shard_map/ppermute | solution.py:242
  15.8 13.7 %collective-permute-start.14 = (bf16[128,384]{1,0:T(8,128)(2,1)S(1)}, bf16[128,384]{1,0:T(8,128)(2,1)}, u32[]{:S(2)}, u32[]{:S(2)}) collective-permute-start(bf16[128,384]{1,0:T(8,128)(2,1)S(1)} %copy-done.17), channel_id=1, source_target_pairs={{0,8},{4,12},{8,0},{12,4},{16,24},{20,28},{24,16},{28,20},{1,9},{5... | collective-permute-start | bytes 294920 | tf_op jit(solution)/shard_map/ppermute | solution.py:242
  15.8 23.5 %collective-permute-start = (bf16[256,768]{1,0:T(8,128)(2,1)}, bf16[256,768]{1,0:T(8,128)(2,1)}, u32[]{:S(2)}, u32[]{:S(2)}) collective-permute-start(bf16[256,768]{1,0:T(8,128)(2,1)} %get-tuple-element.27), channel_id=1, source_target_pairs={{0,6}} | collective-permute-start | bytes 1179656 | tf_op jit(solution)/shard_map/ppermute | solution.py:263
  20.9 20.7 %collective-permute-start.1 = (bf16[256,768]{1,0:T(8,128)(2,1)}, bf16[256,768]{1,0:T(8,128)(2,1)}, u32[]{:S(2)}, u32[]{:S(2)}) collective-permute-start(bf16[256,768]{1,0:T(8,128)(2,1)} %get-tuple-element.28), channel_id=1, source_target_pairs={{0,2}} | collective-permute-start | bytes 1179656 | tf_op jit(solution)/shard_map/ppermute | solution.py:263
  22.9 18.8 %collective-permute-start.2 = (bf16[256,768]{1,0:T(8,128)(2,1)}, bf16[256,768]{1,0:T(8,128)(2,1)}, u32[]{:S(2)}, u32[]{:S(2)}) collective-permute-start(bf16[256,768]{1,0:T(8,128)(2,1)} %get-tuple-element.29), channel_id=1, source_target_pairs={{0,4}} | collective-permute-start | bytes 1179656 | tf_op jit(solution)/shard_map/ppermute | solution.py:263
  24.9 70.0 %all-to-all-start = ((bf16[4,2,512,384]{3,2,1,0:T(8,128)(2,1)}), bf16[4,2,512,384]{3,2,1,0:T(8,128)(2,1)S(1)}, u32[]{:S(2)}, u32[]{:S(2)}) async-start(bf16[4,2,512,384]{3,2,1,0:T(8,128)(2,1)} %pack_heads.1), calls=%async_computation | async-start | bytes 6291456 | tf_op jit(solution)/shard_map/all_to_all | solution.py:284
  29.5 6.1 %collective-permute-start.15 = (bf16[128,384]{1,0:T(8,128)(2,1)S(1)}, bf16[128,384]{1,0:T(8,128)(2,1)S(1)}, u32[]{:S(2)}, u32[]{:S(2)}) collective-permute-start(bf16[128,384]{1,0:T(8,128)(2,1)S(1)} %copy-done.17), channel_id=1, source_target_pairs={{0,16},{4,20},{8,24},{12,28},{16,0},{20,4},{24,8},{28,12},{1,17},{... | collective-permute-start | bytes 294920 | tf_op jit(solution)/shard_map/ppermute | solution.py:242
  31.1 36.7 %collective-permute-start.6 = (bf16[256,768]{1,0:T(8,128)(2,1)}, bf16[256,768]{1,0:T(8,128)(2,1)S(1)}, u32[]{:S(2)}, u32[]{:S(2)}) collective-permute-start(bf16[256,768]{1,0:T(8,128)(2,1)} %get-tuple-element.31), channel_id=1, source_target_pairs={{0,6}} | collective-permute-start | bytes 1179656 | tf_op jit(solution)/shard_map/ppermute | solution.py:263
  35.6 36.4 %collective-permute-start.7 = (bf16[256,768]{1,0:T(8,128)(2,1)}, bf16[256,768]{1,0:T(8,128)(2,1)S(1)}, u32[]{:S(2)}, u32[]{:S(2)}) collective-permute-start(bf16[256,768]{1,0:T(8,128)(2,1)} %get-tuple-element.32), channel_id=1, source_target_pairs={{0,2}} | collective-permute-start | bytes 1179656 | tf_op jit(solution)/shard_map/ppermute | solution.py:263
  39.2 32.8 %collective-permute-start.8 = (bf16[256,768]{1,0:T(8,128)(2,1)}, bf16[256,768]{1,0:T(8,128)(2,1)S(1)}, u32[]{:S(2)}, u32[]{:S(2)}) collective-permute-start(bf16[256,768]{1,0:T(8,128)(2,1)} %get-tuple-element.33), channel_id=1, source_target_pairs={{0,4}} | collective-permute-start | bytes 1179656 | tf_op jit(solution)/shard_map/ppermute | solution.py:263
  40.5 31.5 %copy-start.16 = (bf16[256,768]{1,0:T(8,128)(2,1)S(1)}, bf16[256,768]{1,0:T(8,128)(2,1)}, u32[]{:S(2)}) copy-start(bf16[256,768]{1,0:T(8,128)(2,1)} %get-tuple-element.30) | copy-start | bytes 1179652
  41.6 52.4 %collective-permute-start.17 = (bf16[4,128,384]{2,1,0:T(8,128)(2,1)S(1)}, bf16[4,128,384]{2,1,0:T(8,128)(2,1)S(1)}, u32[]{:S(2)}, u32[]{:S(2)}) collective-permute-start(bf16[4,128,384]{2,1,0:T(8,128)(2,1)S(1)} %pad_maximum_fusion.1), channel_id=1, source_target_pairs={{0,4},{4,0},{8,12},{12,8},{16,20},{20,16},{24,28},{28,24},{1,5},{5... | collective-permute-start | bytes 1179656 | tf_op jit(solution)/shard_map/ppermute | solution.py:242
  43.1 30.5 %collective-permute-start.3 = (bf16[256,384]{1,0:T(8,128)(2,1)S(1)}, bf16[256,384]{1,0:T(8,128)(2,1)S(1)}, u32[]{:S(2)}, u32[]{:S(2)}) collective-permute-start(bf16[256,384]{1,0:T(8,128)(2,1)S(1)} %slice.57), channel_id=1, source_target_pairs={{0,1},{2,3},{4,5},{6,7},{8,9},{10,11},{12,13},{14,15},{16,17},{18,... | collective-permute-start | bytes 589832 | tf_op jit(solution)/shard_map/ppermute | solution.py:268
  72.1 8.8 %copy-start.11 = (bf16[8,128,384]{2,1,0:T(8,128)(2,1)S(1)}, bf16[8,128,384]{2,1,0:T(8,128)(2,1)}, u32[]{:S(2)}) copy-start(bf16[8,128,384]{2,1,0:T(8,128)(2,1)} %constant_dynamic-update-slice_fusion.3) | copy-start | bytes 2359300
  72.2 2.8 %collective-permute-start.9 = (bf16[256,384]{1,0:T(8,128)(2,1)S(1)}, bf16[256,384]{1,0:T(8,128)(2,1)S(1)}, u32[]{:S(2)}, u32[]{:S(2)}) collective-permute-start(bf16[256,384]{1,0:T(8,128)(2,1)S(1)} %slice.59), channel_id=1, source_target_pairs={{0,1},{2,3},{4,5},{6,7},{8,9},{10,11},{12,13},{14,15},{16,17},{18,... | collective-permute-start | bytes 589832 | tf_op jit(solution)/shard_map/ppermute | solution.py:268
  73.7 5.9 %collective-permute-start.4 = (bf16[256,384]{1,0:T(8,128)(2,1)S(1)}, bf16[256,384]{1,0:T(8,128)(2,1)S(1)}, u32[]{:S(2)}, u32[]{:S(2)}) collective-permute-start(bf16[256,384]{1,0:T(8,128)(2,1)S(1)} %slice_add_fusion.1), channel_id=1, source_target_pairs={{0,16},{4,20},{1,17},{5,21},{2,18},{6,22},{3,19},{7,23}} | collective-permute-start | bytes 589832 | tf_op jit(solution)/shard_map/ppermute | solution.py:272
  75.0 8.8 %collective-permute-start.10 = (bf16[256,384]{1,0:T(8,128)(2,1)S(1)}, bf16[256,384]{1,0:T(8,128)(2,1)S(1)}, u32[]{:S(2)}, u32[]{:S(2)}) collective-permute-start(bf16[256,384]{1,0:T(8,128)(2,1)S(1)} %slice_add_fusion), channel_id=1, source_target_pairs={{0,16},{4,20},{1,17},{5,21},{2,18},{6,22},{3,19},{7,23}} | collective-permute-start | bytes 589832 | tf_op jit(solution)/shard_map/ppermute | solution.py:272
  79.6 8.4 %collective-permute-start.5 = (bf16[256,384]{1,0:T(8,128)(2,1)S(1)}, bf16[256,384]{1,0:T(8,128)(2,1)S(1)}, u32[]{:S(2)}, u32[]{:S(2)}) collective-permute-start(bf16[256,384]{1,0:T(8,128)(2,1)S(1)} %add.55), channel_id=1, source_target_pairs={{0,8},{4,12},{16,24},{20,28},{1,9},{5,13},{17,25},{21,29},{2,10},{... | collective-permute-start | bytes 589832 | tf_op jit(solution)/shard_map/ppermute | solution.py:272
  83.8 11.1 %copy-start.15 = (bf16[2,128,384]{2,1,0:T(8,128)(2,1)S(1)}, bf16[2,128,384]{2,1,0:T(8,128)(2,1)}, u32[]{:S(2)}) copy-start(bf16[2,128,384]{2,1,0:T(8,128)(2,1)} %sk_ref.3) | copy-start | bytes 589828
  83.8 6.9 %collective-permute-start.11 = (bf16[256,384]{1,0:T(8,128)(2,1)S(1)}, bf16[256,384]{1,0:T(8,128)(2,1)S(1)}, u32[]{:S(2)}, u32[]{:S(2)}) collective-permute-start(bf16[256,384]{1,0:T(8,128)(2,1)S(1)} %add.61), channel_id=1, source_target_pairs={{0,8},{4,12},{16,24},{20,28},{1,9},{5,13},{17,25},{21,29},{2,10},{... | collective-permute-start | bytes 589832 | tf_op jit(solution)/shard_map/ppermute | solution.py:272
  91.6 10.6 %collective-permute-start.13 = (bf16[2,256,384]{2,1,0:T(8,128)(2,1)}, bf16[2,256,384]{2,1,0:T(8,128)(2,1)}, u32[]{:S(2)}, u32[]{:S(2)}) collective-permute-start(bf16[2,256,384]{2,1,0:T(8,128)(2,1)} %pad_maximum_fusion.near_ref), channel_id=1, source_target_pairs={{0,2},{1,3},{2,0},{3,1},{4,6},{5,7},{6,4},{7,5},{8,10},{9,11},{10,... | collective-permute-start | bytes 1179656 | tf_op jit(solution)/shard_map/ppermute | solution.py:242
  94.0 9.7 %collective-permute-start.12 = (bf16[2,256,384]{2,1,0:T(8,128)(2,1)}, bf16[2,256,384]{2,1,0:T(8,128)(2,1)}, u32[]{:S(2)}, u32[]{:S(2)}) collective-permute-start(bf16[2,256,384]{2,1,0:T(8,128)(2,1)} %pad_maximum_fusion.near_ref), channel_id=1, source_target_pairs={{0,4},{4,0},{8,12},{12,8},{16,20},{20,16},{24,28},{28,24},{1,5},{5... | collective-permute-start | bytes 1179656 | tf_op jit(solution)/shard_map/ppermute | solution.py:242
  94.1 0.9 copy-start.12
  95.0 1.1 copy-start.13
  96.1 8.4 %copy-start.14 = (bf16[8,128,384]{2,1,0:T(8,128)(2,1)S(1)}, bf16[8,128,384]{2,1,0:T(8,128)(2,1)}, u32[]{:S(2)}) copy-start(bf16[8,128,384]{2,1,0:T(8,128)(2,1)} %copy-done.12) | copy-start | bytes 2359300
  103.7 10.9 %collective-permute-start.20 = (bf16[2,256,384]{2,1,0:T(8,128)(2,1)}, bf16[2,256,384]{2,1,0:T(8,128)(2,1)S(1)}, u32[]{:S(2)}, u32[]{:S(2)}) collective-permute-start(bf16[2,256,384]{2,1,0:T(8,128)(2,1)} %collective-permute-done.12.far_ref), channel_id=1, source_target_pairs={{0,2},{1,3},{2,0},{3,1},{4,6},{5,7},{6,4},{7,5},{8,10},{9,11},{10,... | collective-permute-start | bytes 1179656 | tf_op jit(solution)/shard_map/ppermute | solution.py:242
  104.0 11.4 %collective-permute-start.19 = (bf16[2,256,384]{2,1,0:T(8,128)(2,1)}, bf16[2,256,384]{2,1,0:T(8,128)(2,1)S(1)}, u32[]{:S(2)}, u32[]{:S(2)}) collective-permute-start(bf16[2,256,384]{2,1,0:T(8,128)(2,1)} %collective-permute-done.12.far_ref), channel_id=1, source_target_pairs={{0,1},{1,0},{2,3},{3,2},{4,5},{5,4},{6,7},{7,6},{8,9},{9,8},{10,11... | collective-permute-start | bytes 1179656 | tf_op jit(solution)/shard_map/ppermute | solution.py:242
  104.0 9.1 %collective-permute-start.18 = (bf16[2,256,384]{2,1,0:T(8,128)(2,1)}, bf16[2,256,384]{2,1,0:T(8,128)(2,1)S(1)}, u32[]{:S(2)}, u32[]{:S(2)}) collective-permute-start(bf16[2,256,384]{2,1,0:T(8,128)(2,1)} %pad_maximum_fusion.near_ref), channel_id=1, source_target_pairs={{0,1},{1,0},{2,3},{3,2},{4,5},{5,4},{6,7},{7,6},{8,9},{9,8},{10,11... | collective-permute-start | bytes 1179656 | tf_op jit(solution)/shard_map/ppermute | solution.py:242
  104.5 9.3 %collective-permute-start.21 = (bf16[2,256,384]{2,1,0:T(8,128)(2,1)}, bf16[2,256,384]{2,1,0:T(8,128)(2,1)S(1)}, u32[]{:S(2)}, u32[]{:S(2)}) collective-permute-start(bf16[2,256,384]{2,1,0:T(8,128)(2,1)} %collective-permute-done.13.near_ref), channel_id=1, source_target_pairs={{0,1},{1,0},{2,3},{3,2},{4,5},{5,4},{6,7},{7,6},{8,9},{9,8},{10,11... | collective-permute-start | bytes 1179656 | tf_op jit(solution)/shard_map/ppermute | solution.py:242
  113.0 0.8 copy-start.8
  113.8 0.8 copy-start.4
  114.6 0.8 copy-start.2
  115.4 0.8 copy-start.6
  116.1 6.4 %copy-start = (bf16[2,512,1536]{2,1,0:T(8,128)(2,1)S(1)}, bf16[2,512,1536]{2,1,0:T(8,128)(2,1)}, u32[]{:S(2)}) copy-start(bf16[2,512,1536]{2,1,0:T(8,128)(2,1)} %kv_ref.4) | copy-start | bytes 9437188
  117.2 27.6 %all-to-all-start.1 = ((f16[8,144,384]{2,1,0:T(8,128)(2,1)}), f16[8,144,384]{2,1,0:T(8,128)(2,1)}, u32[]{:S(2)}, u32[]{:S(2)}) async-start(f16[8,144,384]{2,1,0:T(8,128)(2,1)} %convert_element_type.9), calls=%async_computation.1 | async-start | bytes 1769472 | tf_op jit(solution)/shard_map/all_to_all | solution.py:303
  121.9 15.6 %collective-permute-start.22 = (bf16[2,256,384]{2,1,0:T(8,128)(2,1)}, bf16[2,256,384]{2,1,0:T(8,128)(2,1)}, u32[]{:S(2)}, u32[]{:S(2)}) collective-permute-start(bf16[2,256,384]{2,1,0:T(8,128)(2,1)} %copy-done.2), channel_id=1, source_target_pairs={{0,1},{1,0},{2,3},{3,2},{4,5},{5,4},{6,7},{7,6},{8,9},{9,8},{10,11... | collective-permute-start | bytes 1179656 | tf_op jit(solution)/shard_map/ppermute | solution.py:242
  122.5 1.4 copy-start.1
  123.9 4.8 %copy-start.7 = (bf16[2,256,384]{2,1,0:T(8,128)(2,1)S(1)}, bf16[2,256,384]{2,1,0:T(8,128)(2,1)}, u32[]{:S(2)}) copy-start(bf16[2,256,384]{2,1,0:T(8,128)(2,1)} %copy-done.6) | copy-start | bytes 1179652
  123.9 4.8 %copy-start.9 = (bf16[2,256,384]{2,1,0:T(8,128)(2,1)S(1)}, bf16[2,256,384]{2,1,0:T(8,128)(2,1)}, u32[]{:S(2)}) copy-start(bf16[2,256,384]{2,1,0:T(8,128)(2,1)} %copy-done.8) | copy-start | bytes 1179652
  128.8 3.9 %copy-start.3 = (bf16[2,256,384]{2,1,0:T(8,128)(2,1)S(1)}, bf16[2,256,384]{2,1,0:T(8,128)(2,1)}, u32[]{:S(2)}) copy-start(bf16[2,256,384]{2,1,0:T(8,128)(2,1)} %copy-done.2) | copy-start | bytes 1179652
  132.6 4.8 %copy-start.5 = (bf16[2,256,384]{2,1,0:T(8,128)(2,1)S(1)}, bf16[2,256,384]{2,1,0:T(8,128)(2,1)}, u32[]{:S(2)}) copy-start(bf16[2,256,384]{2,1,0:T(8,128)(2,1)} %copy-done.4) | copy-start | bytes 1179652

commit v6 on v5

--- a/solution.py
+++ b/solution.py
@@ -129,7 +129,7 @@
         ),
         out_shape=jax.ShapeDtypeStruct((hosts, share + EXTRA, width), jnp.float32),
         input_output_aliases={5: 0} if more else {},
-        compiler_params=pltpu.CompilerParams(vmem_limit_bytes=48 * 1024 * 1024),
+        compiler_params=pltpu.CompilerParams(vmem_limit_bytes=24 * 1024 * 1024),
         cost_estimate=pl.CostEstimate(
             flops=8 * count * hosts * share * seen * HSZ,
             bytes_accessed=4 * count * (groups * rows + 3 * hosts * share) * HSZ,
@@ -228,7 +228,7 @@
         ),
         out_shape=jax.ShapeDtypeStruct((rows, width), q.dtype),
         input_output_aliases={7: 0} if more else {},
-        compiler_params=pltpu.CompilerParams(vmem_limit_bytes=48 * 1024 * 1024),
+        compiler_params=pltpu.CompilerParams(vmem_limit_bytes=24 * 1024 * 1024),
         cost_estimate=pl.CostEstimate(
             flops=8 * rows * rows * wide,
             bytes_accessed=12 * rows * wide,
@@ -248,19 +248,30 @@
     return jnp.concatenate([near, far], axis=0)
 
 
-def anchor_quarters(block):
-    rows, width = block.shape
+def after(x, done):
+    return lax.optimization_barrier((x, done))[0]
+
+
+def quarter(kv, y, x):
+    _, rows, width = kv.shape
     tall, wide = rows // 2, width // 2
-    quarter = lambda y, x: block[y * tall : (y + 1) * tall, x * wide : (x + 1) * wide]
-    return [quarter(1, 1), quarter(0, 1), quarter(1, 0), quarter(0, 0)]
-
-
-def spread_anchor(quarters, hosts, groups):
+    return kv[:, y * tall : (y + 1) * tall, x * wide : (x + 1) * wide]
+
+
+def scatter_anchor(mine, across, diagonal, below, groups):
     cores = groups // 2
     first = (lax.axis_index("hst") == 0) & (lax.axis_index("grp") == 0)
-    slab = jnp.where(first, quarters[3], 0.0)
-    for quarter, to in zip(quarters, [groups + cores, cores, groups]):
-        slab = slab + lax.ppermute(quarter, BOTH, [(0, to)])
+    send = lambda x, to: lax.ppermute(x, BOTH, [(0, to)])
+    down = send(below, groups)
+    slabs = []
+    for s in range(2):
+        slab = jnp.where(first, mine[s], 0.0) + send(diagonal[s], groups + cores) + send(across[s], cores)
+        slabs.append(slab + (after(down[s], slabs[0]) if s else down[s]))
+    return slabs
+
+
+def spread_anchor(slab, hosts, groups):
+    cores = groups // 2
     wide = slab.shape[1] // cores
     piece = slab[:, :wide]
     for c in range(1, cores):
@@ -279,10 +290,12 @@
     host, group = lax.axis_index("hst"), lax.axis_index("grp")
     rows = queries.shape[0]
     heads = suffix_queries.shape[1] // HSZ
-    quarters, keys_values = lax.optimization_barrier(([anchor_quarters(x) for x in keys_values], keys_values))
-    packed, suffix_queries = lax.optimization_barrier((pack(keys_values, groups), suffix_queries))
-    swapped = lax.all_to_all(packed, "grp", split_axis=0, concat_axis=0, tiled=True)
-    near = jnp.stack([spread_anchor(x, hosts, groups) for x in quarters])
+    quarters = [quarter(keys_values, y, x) for y, x in ((0, 0), (0, 1), (1, 1), (1, 0))]
+    quarters, keys_values = lax.optimization_barrier((quarters, keys_values))
+    swapped = lax.all_to_all(pack(keys_values, groups), "grp", split_axis=0, concat_axis=0, tiled=True)
+    slabs = scatter_anchor(*quarters, groups)
+    near = jnp.stack([spread_anchor(x, hosts, groups) for x in slabs])
+    suffix_queries = after(suffix_queries, slabs[0])
     gathered = gather_hosts(suffix_queries, hosts)
     seen = (token_ids.reshape(-1, rows) >= NAMB) & (jnp.arange(rows)[None, :] < lengths[:, None])
     bias = jnp.where(seen, 0.0, NEG).astype(jnp.float32)

time: 152 us -> 124 us (0.82)
  waiting for transfers between devices: 48 us -> 18.8 us
    ppermute x6 -> x5, waiting for transfers between devices: 27.6 us -> 0.01 us  [scatter_anchor(): send = lambda x, to: lax.ppermute(x, BOTH, [(0, to)])]
    ppermute x11, waiting for transfers between devices: 6.62 us -> 3.47 us  [swap(): lax.ppermute(x, axis, [(i, i ^ k) for i in range(lax.axis_size(axis))])]
    unnamed x42 -> x34, local copies, waits for them, and re-layouts: 8.77 us -> 5.8 us
    squeeze x0 -> x3, local copies, waits for them, and re-layouts: none -> 2.93 us  [the longest x1 1.02 us: scatter_anchor(): slabs.append(slab + (after(down[s], slabs[0]) if s else down[s]))]
    another operation x1 -> x0, local copies, waits for them, and re-layouts: 2.09 us -> none  [per_device(): quarters, keys_values = lax.optimization_barrier(([anchor_quarters(x) for...]
    ppermute x4, starting transfers between devices: 5.52 us -> 7.25 us  [spread_anchor(): piece = piece + lax.ppermute(piece, 'hst', pairs)]
    ppermute x6 -> x5, starting transfers between devices: 15.4 us -> 14.9 us  [scatter_anchor(): send = lambda x, to: lax.ppermute(x, BOTH, [(0, to)])]
  transfers between devices with their start and end apart: 25 -> 24, of which waited for: 10 -> 8; matrix products, arithmetic and copies ran while one was open for 4% -> 5% of each run, Pallas kernels for 21% -> 30%
where the time goes in v6:
time: 124 us; the launch traced here: 123 us
  starting transfers between devices  42.2 us (34%)
  Pallas kernels  40.7 us (33%)
  waiting for transfers between devices  18.8 us (15%)
  local copies, waits for them, and re-layouts  12.1 us (10%)
  other arithmetic  7.75 us (6%)
    pallas_call x4, Pallas kernels, context_attend(): pl.pallas_call(context_kernel, grid_spec=pltpu.PrefetchScalarGridSpec(num...  18.3 us
    ppermute x5, starting transfers between devices, scatter_anchor(): send = lambda x, to: lax.ppermute(x, BOTH, [(0, to)])  14.9 us
    pallas_call x2, Pallas kernels, suffix_attend(): pl.pallas_call(suffix_kernel, grid_spec=pltpu.PrefetchScalarGridSpec(num_...  12.7 us
    ppermute x4, waiting for transfers between devices, spread_anchor(): piece = piece + lax.ppermute(piece, 'hst', pairs)  12.4 us
    ppermute x11, starting transfers between devices, swap(): lax.ppermute(x, axis, [(i, i ^ k) for i in range(lax.axis_size(axis))])  8.95 us
    ppermute x4, starting transfers between devices, spread_anchor(): piece = piece + lax.ppermute(piece, 'hst', pairs)  7.25 us
    pallas_call x1, Pallas kernels, pack(): pl.pallas_call(pack_kernel, grid=(2, 4), in_specs=[pl.BlockSpec((1, few,...  6.18 us
    unnamed x34, local copies, waits for them, and re-layouts  5.8 us
  transfers between devices with their start and end apart: 24, of which 8 were waited for; matrix products, arithmetic and copies ran while one was open for 5% of the time, Pallas kernels for 30%

profile of v6, /device:TPU:0, one launch (start us, length us, event | category | flops | bytes accessed | tf_op | source)
XLA Modules:
  0.0 122.5 jit_solution(3393009161860794921)
XLA Ops:
  0.6 3.2 %fusion.6 = (bf16[2,256,768]{2,1,0:T(8,128)(2,1)}, bf16[2,256,768]{2,1,0:T(8,128)(2,1)S(1)}, bf16[2,256,768]{2,1,0:T(8,128)(2,1)S(1)}, bf16[2,256,768]{2,1,0:T(8,128)(2,1)}) fusion(bf16[2,512,1536]{2,1,0:T(8,128)(2,1)} %kv_ref.4), kind=kLoop, calls=%fused_computation.31 | loop fusion | bytes 6291456 | tf_op jit(solution)/shard_map/slice | solution.py:258
  3.8 1.0 slice_bitcast_fusion.3
  4.8 6.6 %collective-permute-start.6 = (bf16[256,768]{1,0:T(8,128)(2,1)}, bf16[256,768]{1,0:T(8,128)(2,1)}, u32[]{:S(2)}, u32[]{:S(2)}) collective-permute-start(bf16[256,768]{1,0:T(8,128)(2,1)} %get-tuple-element.44), channel_id=1, source_target_pairs={{0,6}} | collective-permute-start | bytes 1179656 | tf_op jit(solution)/shard_map/ppermute | solution.py:264
  11.4 2.0 %collective-permute-start = (bf16[256,768]{1,0:T(8,128)(2,1)}, bf16[256,768]{1,0:T(8,128)(2,1)}, u32[]{:S(2)}, u32[]{:S(2)}) collective-permute-start(bf16[256,768]{1,0:T(8,128)(2,1)} %get-tuple-element.45), channel_id=1, source_target_pairs={{0,6}} | collective-permute-start | bytes 1179656 | tf_op jit(solution)/shard_map/ppermute | solution.py:264
  13.4 2.2 %collective-permute-start.2 = (bf16[2,256,768]{2,1,0:T(8,128)(2,1)}, bf16[2,256,768]{2,1,0:T(8,128)(2,1)}, u32[]{:S(2)}, u32[]{:S(2)}) collective-permute-start(bf16[2,256,768]{2,1,0:T(8,128)(2,1)} %get-tuple-element.25), channel_id=1, source_target_pairs={{0,4}} | collective-permute-start | bytes 2359304 | tf_op jit(solution)/shard_map/ppermute | solution.py:264
  15.6 0.9 slice_bitcast_fusion.2
  16.5 2.0 %collective-permute-start.7 = (bf16[256,768]{1,0:T(8,128)(2,1)}, bf16[256,768]{1,0:T(8,128)(2,1)}, u32[]{:S(2)}, u32[]{:S(2)}) collective-permute-start(bf16[256,768]{1,0:T(8,128)(2,1)} %get-tuple-element.46), channel_id=1, source_target_pairs={{0,2}} | collective-permute-start | bytes 1179656 | tf_op jit(solution)/shard_map/ppermute | solution.py:264
  18.6 2.1 %collective-permute-start.1 = (bf16[256,768]{1,0:T(8,128)(2,1)}, bf16[256,768]{1,0:T(8,128)(2,1)}, u32[]{:S(2)}, u32[]{:S(2)}) collective-permute-start(bf16[256,768]{1,0:T(8,128)(2,1)} %get-tuple-element.47), channel_id=1, source_target_pairs={{0,2}} | collective-permute-start | bytes 1179656 | tf_op jit(solution)/shard_map/ppermute | solution.py:264
  20.6 6.2 %pack_heads.1 = bf16[4,2,512,384]{3,2,1,0:T(8,128)(2,1)} custom-call(bf16[2,512,1536]{2,1,0:T(8,128)(2,1)} %kv_ref.4), custom_call_target="tpu_custom_call" | custom-call | bytes 6291456 | tf_op jit(solution)/shard_map/pack_heads/pallas_call | solution.py:47
  26.8 3.8 %all-to-all-start = ((bf16[4,2,512,384]{3,2,1,0:T(8,128)(2,1)}), bf16[4,2,512,384]{3,2,1,0:T(8,128)(2,1)S(1)}, u32[]{:S(2)}, u32[]{:S(2)}) async-start(bf16[4,2,512,384]{3,2,1,0:T(8,128)(2,1)} %pack_heads.1), calls=%async_computation | async-start | bytes 6291456 | tf_op jit(solution)/shard_map/all_to_all | solution.py:295
  30.9 1.5 %fusion = bf16[256,768]{1,0:T(8,128)(2,1)S(1)} fusion(bf16[2,256,768]{2,1,0:T(8,128)(2,1)} %collective-permute-done.2, bf16[256,768]{1,0:T(8,128)(2,1)} %collective-permute-done.1, bf16[256,768]{1,0:T(8,128)(2,1)} %collective-permute-done, bf16[2,256,768]{2,1,0:T(8,128)(2,1)} %get-tuple-element.22, pred[]{:T(512)S(6)} %and.18), kind=kLoop, calls=%fused_computation.2 | loop fusion | flops 786432 | bytes 1966081 | tf_op jit(solution)/shard_map/add | solution.py:269
  32.6 4.3 %collective-permute-start.13 = (bf16[128,384]{1,0:T(8,128)(2,1)S(1)}, bf16[128,384]{1,0:T(8,128)(2,1)S(1)}, u32[]{:S(2)}, u32[]{:S(2)}) collective-permute-start(bf16[128,384]{1,0:T(8,128)(2,1)S(1)} %copy-done.13), channel_id=1, source_target_pairs={{0,8},{4,12},{8,0},{12,4},{16,24},{20,28},{24,16},{28,20},{1,9},{5... | collective-permute-start | bytes 294920 | tf_op jit(solution)/shard_map/ppermute | solution.py:242
  36.9 1.0 slice_bitcast_fusion
  37.9 1.3 %fusion.2 = bf16[256,768]{1,0:T(8,128)(2,1)S(1)} fusion(bf16[256,768]{1,0:T(8,128)(2,1)S(1)} %slice_bitcast_fusion, bf16[256,768]{1,0:T(8,128)(2,1)} %collective-permute-done.7, bf16[256,768]{1,0:T(8,128)(2,1)} %collective-permute-done.6, bf16[2,256,768]{2,1,0:T(8,128)(2,1)S(1)} %copy-done.12, pred[]{:T(512)S(6)} %and.18), kind=kLoop, calls=%fused_computation.7 | loop fusion | flops 786432 | bytes 1966081 | tf_op jit(solution)/shard_map/add | solution.py:269
  39.3 1.5 %collective-permute-start.3 = (bf16[256,384]{1,0:T(8,128)(2,1)S(1)}, bf16[256,384]{1,0:T(8,128)(2,1)S(1)}, u32[]{:S(2)}, u32[]{:S(2)}) collective-permute-start(bf16[256,384]{1,0:T(8,128)(2,1)S(1)} %slice.66), channel_id=1, source_target_pairs={{0,1},{2,3},{4,5},{6,7},{8,9},{10,11},{12,13},{14,15},{16,17},{18,... | collective-permute-start | bytes 589832 | tf_op jit(solution)/shard_map/ppermute | solution.py:279
  40.8 1.3 %collective-permute-start.8 = (bf16[256,384]{1,0:T(8,128)(2,1)S(1)}, bf16[256,384]{1,0:T(8,128)(2,1)S(1)}, u32[]{:S(2)}, u32[]{:S(2)}) collective-permute-start(bf16[256,384]{1,0:T(8,128)(2,1)S(1)} %slice.69), channel_id=1, source_target_pairs={{0,1},{2,3},{4,5},{6,7},{8,9},{10,11},{12,13},{14,15},{16,17},{18,... | collective-permute-start | bytes 589832 | tf_op jit(solution)/shard_map/ppermute | solution.py:279
  42.1 0.7 collective-permute-done.14
  43.0 3.3 %collective-permute-start.4 = (bf16[256,384]{1,0:T(8,128)(2,1)S(1)}, bf16[256,384]{1,0:T(8,128)(2,1)S(1)}, u32[]{:S(2)}, u32[]{:S(2)}) collective-permute-start(bf16[256,384]{1,0:T(8,128)(2,1)S(1)} %slice_add_fusion.1), channel_id=1, source_target_pairs={{0,16},{4,20},{1,17},{5,21},{2,18},{6,22},{3,19},{7,23}} | collective-permute-start | bytes 589832 | tf_op jit(solution)/shard_map/ppermute | solution.py:283
  46.4 1.3 %collective-permute-start.9 = (bf16[256,384]{1,0:T(8,128)(2,1)S(1)}, bf16[256,384]{1,0:T(8,128)(2,1)S(1)}, u32[]{:S(2)}, u32[]{:S(2)}) collective-permute-start(bf16[256,384]{1,0:T(8,128)(2,1)S(1)} %slice_add_fusion), channel_id=1, source_target_pairs={{0,16},{4,20},{1,17},{5,21},{2,18},{6,22},{3,19},{7,23}} | collective-permute-start | bytes 589832 | tf_op jit(solution)/shard_map/ppermute | solution.py:283
  47.8 3.9 %collective-permute-done.4 = bf16[256,384]{1,0:T(8,128)(2,1)S(1)} collective-permute-done((bf16[256,384]{1,0:T(8,128)(2,1)S(1)}, bf16[256,384]{1,0:T(8,128)(2,1)S(1)}, u32[]{:S(2)}, u32[]{:S(2)}) %collective-permute-start.4) | collective-permute-done | bytes 196640 | tf_op jit(solution)/shard_map/ppermute | solution.py:283
  51.8 1.3 %collective-permute-start.5 = (bf16[256,384]{1,0:T(8,128)(2,1)S(1)}, bf16[256,384]{1,0:T(8,128)(2,1)S(1)}, u32[]{:S(2)}, u32[]{:S(2)}) collective-permute-start(bf16[256,384]{1,0:T(8,128)(2,1)S(1)} %add.55), channel_id=1, source_target_pairs={{0,8},{4,12},{16,24},{20,28},{1,9},{5,13},{17,25},{21,29},{2,10},{... | collective-permute-start | bytes 589832 | tf_op jit(solution)/shard_map/ppermute | solution.py:283
  53.1 2.8 %collective-permute-done.9 = bf16[256,384]{1,0:T(8,128)(2,1)S(1)} collective-permute-done((bf16[256,384]{1,0:T(8,128)(2,1)S(1)}, bf16[256,384]{1,0:T(8,128)(2,1)S(1)}, u32[]{:S(2)}, u32[]{:S(2)}) %collective-permute-start.9) | collective-permute-done | bytes 196640 | tf_op jit(solution)/shard_map/ppermute | solution.py:283
  56.0 1.3 %collective-permute-start.10 = (bf16[256,384]{1,0:T(8,128)(2,1)S(1)}, bf16[256,384]{1,0:T(8,128)(2,1)S(1)}, u32[]{:S(2)}, u32[]{:S(2)}) collective-permute-start(bf16[256,384]{1,0:T(8,128)(2,1)S(1)} %add.61), channel_id=1, source_target_pairs={{0,8},{4,12},{16,24},{20,28},{1,9},{5,13},{17,25},{21,29},{2,10},{... | collective-permute-start | bytes 589832 | tf_op jit(solution)/shard_map/ppermute | solution.py:283
  57.3 2.8 %collective-permute-done.5 = bf16[256,384]{1,0:T(8,128)(2,1)S(1)} collective-permute-done((bf16[256,384]{1,0:T(8,128)(2,1)S(1)}, bf16[256,384]{1,0:T(8,128)(2,1)S(1)}, u32[]{:S(2)}, u32[]{:S(2)}) %collective-permute-start.5) | collective-permute-done | bytes 196640 | tf_op jit(solution)/shard_map/ppermute | solution.py:283
  60.2 2.8 %collective-permute-done.10 = bf16[256,384]{1,0:T(8,128)(2,1)S(1)} collective-permute-done((bf16[256,384]{1,0:T(8,128)(2,1)S(1)}, bf16[256,384]{1,0:T(8,128)(2,1)S(1)}, u32[]{:S(2)}, u32[]{:S(2)}) %collective-permute-start.10) | collective-permute-done | bytes 196640 | tf_op jit(solution)/shard_map/ppermute | solution.py:283
  63.0 0.8 pad_maximum_fusion.near_ref
  63.8 1.3 %collective-permute-start.12 = (bf16[2,256,384]{2,1,0:T(8,128)(2,1)}, bf16[2,256,384]{2,1,0:T(8,128)(2,1)}, u32[]{:S(2)}, u32[]{:S(2)}) collective-permute-start(bf16[2,256,384]{2,1,0:T(8,128)(2,1)} %pad_maximum_fusion.near_ref), channel_id=1, source_target_pairs={{0,2},{1,3},{2,0},{3,1},{4,6},{5,7},{6,4},{7,5},{8,10},{9,11},{10,... | collective-permute-start | bytes 1179656 | tf_op jit(solution)/shard_map/ppermute | solution.py:242
  65.1 1.7 %collective-permute-start.11 = (bf16[2,256,384]{2,1,0:T(8,128)(2,1)}, bf16[2,256,384]{2,1,0:T(8,128)(2,1)}, u32[]{:S(2)}, u32[]{:S(2)}) collective-permute-start(bf16[2,256,384]{2,1,0:T(8,128)(2,1)} %pad_maximum_fusion.near_ref), channel_id=1, source_target_pairs={{0,4},{4,0},{8,12},{12,8},{16,20},{20,16},{24,28},{28,24},{1,5},{5... | collective-permute-start | bytes 1179656 | tf_op jit(solution)/shard_map/ppermute | solution.py:242
  67.0 0.9 copy-done.9
  68.0 1.1 copy-done.10
  69.2 4.2 %suffix_attend.2.rest_0_ = f32[8,144,384]{2,1,0:T(8,128)S(1)} custom-call(s32[1]{0:T(128)} %bitcast.13.at_ref, bf16[8,128,384]{2,1,0:T(8,128)(2,1)S(1)} %copy-done.10, bf16[4,2,512,384]{3,2,1,0:T(8,128)(2,1)S(1)} %all-to-all-done.kv_ref, bf16[2,128,384]{2,1,0:T(8,128)(2,1)S(1)} %copy-done.11, f32[32,512]{1,0:T(8,128)S(1)} %fusion.5.bias_ref), custom_call_target="tpu_custom_call" | custom-call | flops 2281701376 | bytes 2621440 | tf_op jit(solution)/shard_map/suffix_attend/pallas_call | solution.py:116
  73.4 2.7 %collective-permute-done.12.near_ref = bf16[2,256,384]{2,1,0:T(8,128)(2,1)} collective-permute-done((bf16[2,256,384]{2,1,0:T(8,128)(2,1)}, bf16[2,256,384]{2,1,0:T(8,128)(2,1)}, u32[]{:S(2)}, u32[]{:S(2)}) %collective-permute-start.12) | collective-permute-done | bytes 393248 | tf_op jit(solution)/shard_map/ppermute | solution.py:242
  76.5 0.5 collective-permute-start.17
  77.0 8.5 %suffix_attend.3 = f32[8,144,384]{2,1,0:T(8,128)S(1)} custom-call(s32[1]{0:T(128)} %bitcast.13.at_ref, bf16[8,128,384]{2,1,0:T(8,128)(2,1)S(1)} %copy-done.10, bf16[4,2,512,384]{3,2,1,0:T(8,128)(2,1)S(1)} %all-to-all-done.kv_ref, bf16[2,128,384]{2,1,0:T(8,128)(2,1)S(1)} %copy-done.11, f32[32,512]{1,0:T(8,128)S(1)} %fusion.5.bias_ref, ...), custom_call_target="tpu_custom_call", output_to_operand_aliasing={{}: (5, {})} | custom-call | flops 4563402752 | bytes 5242880 | tf_op jit(solution)/shard_map/suffix_attend/pallas_call | solution.py:116
  85.5 0.8 copy-done.6
  86.3 0.8 copy-done.2
  87.1 0.7 copy-done.4
  87.8 1.1 convert_element_type.9
  88.9 4.4 %all-to-all-start.1 = ((f16[8,144,384]{2,1,0:T(8,128)(2,1)}), f16[8,144,384]{2,1,0:T(8,128)(2,1)}, u32[]{:S(2)}, u32[]{:S(2)}) async-start(f16[8,144,384]{2,1,0:T(8,128)(2,1)} %convert_element_type.9), calls=%async_computation.1 | async-start | bytes 1769472 | tf_op jit(solution)/shard_map/all_to_all | solution.py:316
  93.4 0.5 collective-permute-start.21
  94.1 1.4 %copy-done.1 = bf16[512,1536]{1,0:T(8,128)(2,1)S(1)} copy-done((bf16[512,1536]{1,0:T(8,128)(2,1)S(1)}, bf16[512,1536]{1,0:T(8,128)(2,1)}, u32[]{:S(2)}) %copy-start.1) | copy-done | bytes 1572888
  95.5 4.8 %context_attend.4.rest_0_ = bf16[512,1536]{1,0:T(8,128)(2,1)} custom-call(s32[3]{0:T(128)S(1)} %get-tuple-element.49.at_ref, s32[32]{0:T(128)S(1)} %copy-done.8, bf16[512,1536]{1,0:T(8,128)(2,1)S(1)} %copy-done.1, bf16[2,512,1536]{2,1,0:T(8,128)(2,1)S(1)} %copy-done, f32[32,512]{1,0:T(8,128)S(1)} %fusion.5.bias_ref, ...), custom_call_target="tpu_custom_call" | custom-call | flops 805306368 | bytes 2359296 | tf_op jit(solution)/shard_map/context_attend/pallas_call | solution.py:213
  100.3 3.8 %context_attend.5.rest_0_ = bf16[512,1536]{1,0:T(8,128)(2,1)} custom-call(s32[3]{0:T(128)S(1)} %get-tuple-element.48.at_ref, s32[32]{0:T(128)S(1)} %copy-done.8, bf16[512,1536]{1,0:T(8,128)(2,1)S(1)} %copy-done.1, bf16[2,512,1536]{2,1,0:T(8,128)(2,1)S(1)} %copy-done, f32[32,512]{1,0:T(8,128)S(1)} %fusion.5.bias_ref, ...), custom_call_target="tpu_custom_call", output_to_operand_aliasing={{}: (7, {})} | custom-call | flops 805306368 | bytes 2359296 | tf_op jit(solution)/shard_map/context_attend/pallas_call | solution.py:213
  104.2 4.8 %context_attend.6.rest_0_ = bf16[512,1536]{1,0:T(8,128)(2,1)} custom-call(s32[3]{0:T(128)S(1)} %add_add_fusion.1.at_ref, s32[32]{0:T(128)S(1)} %copy-done.8, bf16[512,1536]{1,0:T(8,128)(2,1)S(1)} %copy-done.1, bf16[2,512,1536]{2,1,0:T(8,128)(2,1)S(1)} %copy-done, f32[32,512]{1,0:T(8,128)S(1)} %fusion.5.bias_ref, ...), custom_call_target="tpu_custom_call", output_to_operand_aliasing={{}: (7, {})} | custom-call | flops 805306368 | bytes 2359296 | tf_op jit(solution)/shard_map/context_attend/pallas_call | solution.py:213
  109.0 4.8 %context_attend.7 = bf16[512,1536]{1,0:T(8,128)(2,1)} custom-call(s32[3]{0:T(128)S(1)} %add_add_fusion.at_ref, s32[32]{0:T(128)S(1)} %copy-done.8, bf16[512,1536]{1,0:T(8,128)(2,1)S(1)} %copy-done.1, bf16[2,512,1536]{2,1,0:T(8,128)(2,1)S(1)} %copy-done, f32[32,512]{1,0:T(8,128)S(1)} %fusion.5.bias_ref, ...), custom_call_target="tpu_custom_call", output_to_operand_aliasing={{}: (7, {})} | custom-call | flops 805306368 | bytes 2359296 | tf_op jit(solution)/shard_map/context_attend/pallas_call | solution.py:213
  113.8 2.7 %all-to-all-done.1 = f16[8,144,384]{2,1,0:T(8,128)(2,1)} async-done(((f16[8,144,384]{2,1,0:T(8,128)(2,1)}), f16[8,144,384]{2,1,0:T(8,128)(2,1)}, u32[]{:S(2)}, u32[]{:S(2)}) %all-to-all-start.1) | async-done | bytes 884768 | tf_op jit(solution)/shard_map/all_to_all | solution.py:316
  116.5 2.5 %convert_element_type.10.in_ref = f32[8,144,384]{2,1,0:T(8,128)} convert(f16[8,144,384]{2,1,0:T(8,128)(2,1)} %all-to-all-done.1) | non-fusion elementwise | flops 442368 | bytes 2654208 | tf_op jit(solution)/shard_map/convert_element_type | solution.py:321
  119.0 3.5 %combine_groups.1 = bf16[128,384]{1,0:T(8,128)(2,1)} custom-call(f32[8,144,384]{2,1,0:T(8,128)} %convert_element_type.10.in_ref), custom_call_target="tpu_custom_call" | custom-call | flops 884736 | bytes 1769472 | tf_op jit(solution)/shard_map/combine_groups/pallas_call | solution.py:157
  (67 shorter events, 1.7 us)
Async XLA Ops:
  4.8 33.1 %collective-permute-start.6 = (bf16[256,768]{1,0:T(8,128)(2,1)}, bf16[256,768]{1,0:T(8,128)(2,1)}, u32[]{:S(2)}, u32[]{:S(2)}) collective-permute-start(bf16[256,768]{1,0:T(8,128)(2,1)} %get-tuple-element.44), channel_id=1, source_target_pairs={{0,6}} | collective-permute-start | bytes 1179656 | tf_op jit(solution)/shard_map/ppermute | solution.py:264
  11.4 19.5 %collective-permute-start = (bf16[256,768]{1,0:T(8,128)(2,1)}, bf16[256,768]{1,0:T(8,128)(2,1)}, u32[]{:S(2)}, u32[]{:S(2)}) collective-permute-start(bf16[256,768]{1,0:T(8,128)(2,1)} %get-tuple-element.45), channel_id=1, source_target_pairs={{0,6}} | collective-permute-start | bytes 1179656 | tf_op jit(solution)/shard_map/ppermute | solution.py:264
  13.4 17.5 %collective-permute-start.2 = (bf16[2,256,768]{2,1,0:T(8,128)(2,1)}, bf16[2,256,768]{2,1,0:T(8,128)(2,1)}, u32[]{:S(2)}, u32[]{:S(2)}) collective-permute-start(bf16[2,256,768]{2,1,0:T(8,128)(2,1)} %get-tuple-element.25), channel_id=1, source_target_pairs={{0,4}} | collective-permute-start | bytes 2359304 | tf_op jit(solution)/shard_map/ppermute | solution.py:264
  16.5 21.4 %collective-permute-start.7 = (bf16[256,768]{1,0:T(8,128)(2,1)}, bf16[256,768]{1,0:T(8,128)(2,1)}, u32[]{:S(2)}, u32[]{:S(2)}) collective-permute-start(bf16[256,768]{1,0:T(8,128)(2,1)} %get-tuple-element.46), channel_id=1, source_target_pairs={{0,2}} | collective-permute-start | bytes 1179656 | tf_op jit(solution)/shard_map/ppermute | solution.py:264
  18.6 12.3 %collective-permute-start.1 = (bf16[256,768]{1,0:T(8,128)(2,1)}, bf16[256,768]{1,0:T(8,128)(2,1)}, u32[]{:S(2)}, u32[]{:S(2)}) collective-permute-start(bf16[256,768]{1,0:T(8,128)(2,1)} %get-tuple-element.47), channel_id=1, source_target_pairs={{0,2}} | collective-permute-start | bytes 1179656 | tf_op jit(solution)/shard_map/ppermute | solution.py:264
  26.8 3.8 %copy-start.14 = (s32[16384]{0:T(1024)S(1)}, s32[16384]{0:T(1024)}, u32[]{:S(2)}) copy-start(s32[16384]{0:T(1024)} %param.8) | copy-start | bytes 196612
  26.8 3.9 %copy-start.8 = (s32[32]{0:T(128)S(1)}, s32[32]{0:T(128)}, u32[]{:S(2)}) copy-start(s32[32]{0:T(128)} %len_ref.7) | copy-start | bytes 388
  26.8 41.2 %all-to-all-start = ((bf16[4,2,512,384]{3,2,1,0:T(8,128)(2,1)}), bf16[4,2,512,384]{3,2,1,0:T(8,128)(2,1)S(1)}, u32[]{:S(2)}, u32[]{:S(2)}) async-start(bf16[4,2,512,384]{3,2,1,0:T(8,128)(2,1)} %pack_heads.1), calls=%async_computation | async-start | bytes 6291456 | tf_op jit(solution)/shard_map/all_to_all | solution.py:295
  30.7 1.7 %copy-start.13 = (bf16[128,384]{1,0:T(8,128)(2,1)S(1)}, bf16[128,384]{1,0:T(8,128)(2,1)}, u32[]{:S(2)}) copy-start(bf16[128,384]{1,0:T(8,128)(2,1)} %param.10) | copy-start | bytes 294916
  30.8 7.1 %copy-start.12 = (bf16[2,256,768]{2,1,0:T(8,128)(2,1)S(1)}, bf16[2,256,768]{2,1,0:T(8,128)(2,1)}, u32[]{:S(2)}) copy-start(bf16[2,256,768]{2,1,0:T(8,128)(2,1)} %get-tuple-element.22) | copy-start | bytes 2359300
  32.4 9.7 %collective-permute-start.15 = (bf16[128,384]{1,0:T(8,128)(2,1)S(1)}, bf16[128,384]{1,0:T(8,128)(2,1)S(1)}, u32[]{:S(2)}, u32[]{:S(2)}) collective-permute-start(bf16[128,384]{1,0:T(8,128)(2,1)S(1)} %copy-done.13), channel_id=1, source_target_pairs={{0,24},{4,28},{8,16},{12,20},{16,8},{20,12},{24,0},{28,4},{1,25},{... | collective-permute-start | bytes 294920 | tf_op jit(solution)/shard_map/ppermute | solution.py:242
  32.5 10.3 %collective-permute-start.14 = (bf16[128,384]{1,0:T(8,128)(2,1)S(1)}, bf16[128,384]{1,0:T(8,128)(2,1)S(1)}, u32[]{:S(2)}, u32[]{:S(2)}) collective-permute-start(bf16[128,384]{1,0:T(8,128)(2,1)S(1)} %copy-done.13), channel_id=1, source_target_pairs={{0,16},{4,20},{8,24},{12,28},{16,0},{20,4},{24,8},{28,12},{1,17},{... | collective-permute-start | bytes 294920 | tf_op jit(solution)/shard_map/ppermute | solution.py:242
  32.6 10.2 %collective-permute-start.13 = (bf16[128,384]{1,0:T(8,128)(2,1)S(1)}, bf16[128,384]{1,0:T(8,128)(2,1)S(1)}, u32[]{:S(2)}, u32[]{:S(2)}) collective-permute-start(bf16[128,384]{1,0:T(8,128)(2,1)S(1)} %copy-done.13), channel_id=1, source_target_pairs={{0,8},{4,12},{8,0},{12,4},{16,24},{20,28},{24,16},{28,20},{1,9},{5... | collective-permute-start | bytes 294920 | tf_op jit(solution)/shard_map/ppermute | solution.py:242
  39.3 3.7 %collective-permute-start.3 = (bf16[256,384]{1,0:T(8,128)(2,1)S(1)}, bf16[256,384]{1,0:T(8,128)(2,1)S(1)}, u32[]{:S(2)}, u32[]{:S(2)}) collective-permute-start(bf16[256,384]{1,0:T(8,128)(2,1)S(1)} %slice.66), channel_id=1, source_target_pairs={{0,1},{2,3},{4,5},{6,7},{8,9},{10,11},{12,13},{14,15},{16,17},{18,... | collective-permute-start | bytes 589832 | tf_op jit(solution)/shard_map/ppermute | solution.py:279
  40.8 5.6 %collective-permute-start.8 = (bf16[256,384]{1,0:T(8,128)(2,1)S(1)}, bf16[256,384]{1,0:T(8,128)(2,1)S(1)}, u32[]{:S(2)}, u32[]{:S(2)}) collective-permute-start(bf16[256,384]{1,0:T(8,128)(2,1)S(1)} %slice.69), channel_id=1, source_target_pairs={{0,1},{2,3},{4,5},{6,7},{8,9},{10,11},{12,13},{14,15},{16,17},{18,... | collective-permute-start | bytes 589832 | tf_op jit(solution)/shard_map/ppermute | solution.py:279
  42.9 24.0 %collective-permute-start.16 = (bf16[4,128,384]{2,1,0:T(8,128)(2,1)S(1)}, bf16[4,128,384]{2,1,0:T(8,128)(2,1)S(1)}, u32[]{:S(2)}, u32[]{:S(2)}) collective-permute-start(bf16[4,128,384]{2,1,0:T(8,128)(2,1)S(1)} %pad_maximum_fusion.1), channel_id=1, source_target_pairs={{0,4},{4,0},{8,12},{12,8},{16,20},{20,16},{24,28},{28,24},{1,5},{5... | collective-permute-start | bytes 1179656 | tf_op jit(solution)/shard_map/ppermute | solution.py:242
  43.0 8.6 %collective-permute-start.4 = (bf16[256,384]{1,0:T(8,128)(2,1)S(1)}, bf16[256,384]{1,0:T(8,128)(2,1)S(1)}, u32[]{:S(2)}, u32[]{:S(2)}) collective-permute-start(bf16[256,384]{1,0:T(8,128)(2,1)S(1)} %slice_add_fusion.1), channel_id=1, source_target_pairs={{0,16},{4,20},{1,17},{5,21},{2,18},{6,22},{3,19},{7,23}} | collective-permute-start | bytes 589832 | tf_op jit(solution)/shard_map/ppermute | solution.py:283
  46.4 9.5 %collective-permute-start.9 = (bf16[256,384]{1,0:T(8,128)(2,1)S(1)}, bf16[256,384]{1,0:T(8,128)(2,1)S(1)}, u32[]{:S(2)}, u32[]{:S(2)}) collective-permute-start(bf16[256,384]{1,0:T(8,128)(2,1)S(1)} %slice_add_fusion), channel_id=1, source_target_pairs={{0,16},{4,20},{1,17},{5,21},{2,18},{6,22},{3,19},{7,23}} | collective-permute-start | bytes 589832 | tf_op jit(solution)/shard_map/ppermute | solution.py:283
  51.8 8.4 %collective-permute-start.5 = (bf16[256,384]{1,0:T(8,128)(2,1)S(1)}, bf16[256,384]{1,0:T(8,128)(2,1)S(1)}, u32[]{:S(2)}, u32[]{:S(2)}) collective-permute-start(bf16[256,384]{1,0:T(8,128)(2,1)S(1)} %add.55), channel_id=1, source_target_pairs={{0,8},{4,12},{16,24},{20,28},{1,9},{5,13},{17,25},{21,29},{2,10},{... | collective-permute-start | bytes 589832 | tf_op jit(solution)/shard_map/ppermute | solution.py:283
  53.1 15.0 %copy-start.11 = (bf16[2,128,384]{2,1,0:T(8,128)(2,1)S(1)}, bf16[2,128,384]{2,1,0:T(8,128)(2,1)}, u32[]{:S(2)}) copy-start(bf16[2,128,384]{2,1,0:T(8,128)(2,1)} %sk_ref.3) | copy-start | bytes 589828
  56.0 7.0 %collective-permute-start.10 = (bf16[256,384]{1,0:T(8,128)(2,1)S(1)}, bf16[256,384]{1,0:T(8,128)(2,1)S(1)}, u32[]{:S(2)}, u32[]{:S(2)}) collective-permute-start(bf16[256,384]{1,0:T(8,128)(2,1)S(1)} %add.61), channel_id=1, source_target_pairs={{0,8},{4,12},{16,24},{20,28},{1,9},{5,13},{17,25},{21,29},{2,10},{... | collective-permute-start | bytes 589832 | tf_op jit(solution)/shard_map/ppermute | solution.py:283
  63.8 12.3 %collective-permute-start.12 = (bf16[2,256,384]{2,1,0:T(8,128)(2,1)}, bf16[2,256,384]{2,1,0:T(8,128)(2,1)}, u32[]{:S(2)}, u32[]{:S(2)}) collective-permute-start(bf16[2,256,384]{2,1,0:T(8,128)(2,1)} %pad_maximum_fusion.near_ref), channel_id=1, source_target_pairs={{0,2},{1,3},{2,0},{3,1},{4,6},{5,7},{6,4},{7,5},{8,10},{9,11},{10,... | collective-permute-start | bytes 1179656 | tf_op jit(solution)/shard_map/ppermute | solution.py:242
  65.1 11.0 %collective-permute-start.11 = (bf16[2,256,384]{2,1,0:T(8,128)(2,1)}, bf16[2,256,384]{2,1,0:T(8,128)(2,1)}, u32[]{:S(2)}, u32[]{:S(2)}) collective-permute-start(bf16[2,256,384]{2,1,0:T(8,128)(2,1)} %pad_maximum_fusion.near_ref), channel_id=1, source_target_pairs={{0,4},{4,0},{8,12},{12,8},{16,20},{20,16},{24,28},{28,24},{1,5},{5... | collective-permute-start | bytes 1179656 | tf_op jit(solution)/shard_map/ppermute | solution.py:242
  67.0 0.9 copy-start.9
  68.0 1.1 copy-start.10
  76.1 11.0 %collective-permute-start.19 = (bf16[2,256,384]{2,1,0:T(8,128)(2,1)}, bf16[2,256,384]{2,1,0:T(8,128)(2,1)}, u32[]{:S(2)}, u32[]{:S(2)}) collective-permute-start(bf16[2,256,384]{2,1,0:T(8,128)(2,1)} %collective-permute-done.11.far_ref), channel_id=1, source_target_pairs={{0,2},{1,3},{2,0},{3,1},{4,6},{5,7},{6,4},{7,5},{8,10},{9,11},{10,... | collective-permute-start | bytes 1179656 | tf_op jit(solution)/shard_map/ppermute | solution.py:242
  76.5 10.6 %collective-permute-start.18 = (bf16[2,256,384]{2,1,0:T(8,128)(2,1)}, bf16[2,256,384]{2,1,0:T(8,128)(2,1)S(1)}, u32[]{:S(2)}, u32[]{:S(2)}) collective-permute-start(bf16[2,256,384]{2,1,0:T(8,128)(2,1)} %collective-permute-done.11.far_ref), channel_id=1, source_target_pairs={{0,1},{1,0},{2,3},{3,2},{4,5},{5,4},{6,7},{7,6},{8,9},{9,8},{10,11... | collective-permute-start | bytes 1179656 | tf_op jit(solution)/shard_map/ppermute | solution.py:242
  76.5 9.1 %collective-permute-start.17 = (bf16[2,256,384]{2,1,0:T(8,128)(2,1)}, bf16[2,256,384]{2,1,0:T(8,128)(2,1)S(1)}, u32[]{:S(2)}, u32[]{:S(2)}) collective-permute-start(bf16[2,256,384]{2,1,0:T(8,128)(2,1)} %pad_maximum_fusion.near_ref), channel_id=1, source_target_pairs={{0,1},{1,0},{2,3},{3,2},{4,5},{5,4},{6,7},{7,6},{8,9},{9,8},{10,11... | collective-permute-start | bytes 1179656 | tf_op jit(solution)/shard_map/ppermute | solution.py:242
  77.0 9.3 %collective-permute-start.20 = (bf16[2,256,384]{2,1,0:T(8,128)(2,1)}, bf16[2,256,384]{2,1,0:T(8,128)(2,1)S(1)}, u32[]{:S(2)}, u32[]{:S(2)}) collective-permute-start(bf16[2,256,384]{2,1,0:T(8,128)(2,1)} %collective-permute-done.12.near_ref), channel_id=1, source_target_pairs={{0,1},{1,0},{2,3},{3,2},{4,5},{5,4},{6,7},{7,6},{8,9},{9,8},{10,11... | collective-permute-start | bytes 1179656 | tf_op jit(solution)/shard_map/ppermute | solution.py:242
  85.5 8.6 %copy-start = (bf16[2,512,1536]{2,1,0:T(8,128)(2,1)S(1)}, bf16[2,512,1536]{2,1,0:T(8,128)(2,1)}, u32[]{:S(2)}) copy-start(bf16[2,512,1536]{2,1,0:T(8,128)(2,1)} %kv_ref.4) | copy-start | bytes 9437188
  85.5 0.8 copy-start.6
  86.3 0.8 copy-start.2
  87.1 0.7 copy-start.4
  88.9 27.6 %all-to-all-start.1 = ((f16[8,144,384]{2,1,0:T(8,128)(2,1)}), f16[8,144,384]{2,1,0:T(8,128)(2,1)}, u32[]{:S(2)}, u32[]{:S(2)}) async-start(f16[8,144,384]{2,1,0:T(8,128)(2,1)} %convert_element_type.9), calls=%async_computation.1 | async-start | bytes 1769472 | tf_op jit(solution)/shard_map/all_to_all | solution.py:316
  93.4 15.6 %collective-permute-start.21 = (bf16[2,256,384]{2,1,0:T(8,128)(2,1)}, bf16[2,256,384]{2,1,0:T(8,128)(2,1)}, u32[]{:S(2)}, u32[]{:S(2)}) collective-permute-start(bf16[2,256,384]{2,1,0:T(8,128)(2,1)} %collective-permute-done.19.far_ref), channel_id=1, source_target_pairs={{0,1},{1,0},{2,3},{3,2},{4,5},{5,4},{6,7},{7,6},{8,9},{9,8},{10,11... | collective-permute-start | bytes 1179656 | tf_op jit(solution)/shard_map/ppermute | solution.py:242
  94.1 1.4 %copy-start.1 = (bf16[512,1536]{1,0:T(8,128)(2,1)S(1)}, bf16[512,1536]{1,0:T(8,128)(2,1)}, u32[]{:S(2)}) copy-start(bf16[512,1536]{1,0:T(8,128)(2,1)} %q_ref.7) | copy-start | bytes 4718596
  95.5 4.8 %copy-start.5 = (bf16[2,256,384]{2,1,0:T(8,128)(2,1)S(1)}, bf16[2,256,384]{2,1,0:T(8,128)(2,1)}, u32[]{:S(2)}) copy-start(bf16[2,256,384]{2,1,0:T(8,128)(2,1)} %copy-done.4) | copy-start | bytes 1179652
  95.5 4.8 %copy-start.7 = (bf16[2,256,384]{2,1,0:T(8,128)(2,1)S(1)}, bf16[2,256,384]{2,1,0:T(8,128)(2,1)}, u32[]{:S(2)}) copy-start(bf16[2,256,384]{2,1,0:T(8,128)(2,1)} %copy-done.6) | copy-start | bytes 1179652
  104.2 4.8 %copy-start.3 = (bf16[2,256,384]{2,1,0:T(8,128)(2,1)S(1)}, bf16[2,256,384]{2,1,0:T(8,128)(2,1)}, u32[]{:S(2)}) copy-start(bf16[2,256,384]{2,1,0:T(8,128)(2,1)} %copy-done.2) | copy-start | bytes 1179652

commit v7 on v5

--- a/solution.py
+++ b/solution.py
@@ -129,7 +129,7 @@
         ),
         out_shape=jax.ShapeDtypeStruct((hosts, share + EXTRA, width), jnp.float32),
         input_output_aliases={5: 0} if more else {},
-        compiler_params=pltpu.CompilerParams(vmem_limit_bytes=48 * 1024 * 1024),
+        compiler_params=pltpu.CompilerParams(vmem_limit_bytes=24 * 1024 * 1024),
         cost_estimate=pl.CostEstimate(
             flops=8 * count * hosts * share * seen * HSZ,
             bytes_accessed=4 * count * (groups * rows + 3 * hosts * share) * HSZ,
@@ -167,7 +167,7 @@
 
 def context_kernel(at_ref, len_ref, q_ref, kv_ref, bias_ref, near_ref, far_ref, *rest):
     out_ref, diag_ref = rest[-2:]
-    block, odd = at_ref[0], at_ref[2]
+    block, odd, level = at_ref[0], at_ref[2], at_ref[3]
     rows, width = q_ref.shape
     half = rows // 2
     own = bias_ref[pl.ds(block, 1), :]
@@ -180,11 +180,15 @@
     near_bias = jnp.where(block > 0, jnp.where(odd == 0, low, high), NEG)
     far_bias = jnp.where(block > 0, jnp.where(odd == 0, high, low), NEG)
 
+    def anchor(ref, which, head):
+        order = [jnp.bitwise_xor(level, z) for z in range(ref.shape[0])]
+        return jnp.concatenate([ref[z, which, :, head] for z in order], axis=0)
+
     def score(task):
         first, t = task
         head = slice(first, first + HSZ)
         q = q_ref[t * half : (t + 1) * half, head]
-        scores = [dot_t(q, near_ref[0, :, head]) + near_bias, dot_t(q, far_ref[0, :, head]) + far_bias]
+        scores = [dot_t(q, anchor(near_ref, 0, head)) + near_bias, dot_t(q, anchor(far_ref, 0, head)) + far_bias]
         if t == 1:
             scores.append(dot_t(q, kv_ref[0, :half, head]) + own[:, :half])
         scores.append(dot_t(q, kv_ref[0, t * half : (t + 1) * half, head]) + diag_ref[t])
@@ -194,7 +198,7 @@
         first, t = task
         head = slice(first, first + HSZ)
         _, total, weights = softmax(scores)
-        values = [near_ref[1, :, head], far_ref[1, :, head]]
+        values = [anchor(near_ref, 1, head), anchor(far_ref, 1, head)]
         values += [kv_ref[1, u * half : (u + 1) * half, head] for u in range(t + 1)]
         mixed = functools.reduce(jnp.add, [dot(w, v) for w, v in zip(weights, values)])
         place = t * half + lax.broadcasted_iota(jnp.int32, mixed.shape, 0)
@@ -206,7 +210,8 @@
 
 def context_attend(at, lengths, q, kv, bias, near, far, before):
     rows, width = q.shape
-    _, half, wide = near.shape
+    half = rows // 2
+    wide = near.shape[3]
     heads = wide // HSZ
     both = lambda i, at, n: (0, 0, at[1])
     more = [] if before is None else [before]
@@ -219,8 +224,8 @@
                 pl.BlockSpec((rows, wide), lambda i, at, n: (0, at[1])),
                 pl.BlockSpec((2, rows, wide), both),
                 pl.BlockSpec(bias.shape, lambda i, *_: (0, 0)),
-                pl.BlockSpec((2, half, wide), lambda i, *_: (0, 0, 0)),
-                pl.BlockSpec((2, half, wide), lambda i, *_: (0, 0, 0)),
+                pl.BlockSpec(near.shape, lambda i, *_: (0, 0, 0, 0)),
+                pl.BlockSpec(far.shape, lambda i, *_: (0, 0, 0, 0)),
             ]
             + [pl.BlockSpec(memory_space=pl.ANY) for _ in more],
             out_specs=pl.BlockSpec((rows, wide), lambda i, at, n: (0, at[1])),
@@ -228,7 +233,7 @@
         ),
         out_shape=jax.ShapeDtypeStruct((rows, width), q.dtype),
         input_output_aliases={7: 0} if more else {},
-        compiler_params=pltpu.CompilerParams(vmem_limit_bytes=48 * 1024 * 1024),
+        compiler_params=pltpu.CompilerParams(vmem_limit_bytes=24 * 1024 * 1024),
         cost_estimate=pl.CostEstimate(
             flops=8 * rows * rows * wide,
             bytes_accessed=12 * rows * wide,
@@ -248,63 +253,66 @@
     return jnp.concatenate([near, far], axis=0)
 
 
-def anchor_quarters(block):
-    rows, width = block.shape
-    tall, wide = rows // 2, width // 2
-    quarter = lambda y, x: block[y * tall : (y + 1) * tall, x * wide : (x + 1) * wide]
-    return [quarter(1, 1), quarter(0, 1), quarter(1, 0), quarter(0, 0)]
-
-
-def spread_anchor(quarters, hosts, groups):
-    cores = groups // 2
+def after(x, done):
+    return lax.optimization_barrier((x, done))[0]
+
+
+def scatter_rows(kv, hosts, groups):
+    part = kv.shape[1] // hosts
+    levels = hosts // 2
+    rows = lambda p, count=1: kv[:, p * part : (p + count) * part]
+    send = lambda x, a, b: lax.ppermute(x, BOTH, [(a * groups, b * groups)])
     first = (lax.axis_index("hst") == 0) & (lax.axis_index("grp") == 0)
-    slab = jnp.where(first, quarters[3], 0.0)
-    for quarter, to in zip(quarters, [groups + cores, cores, groups]):
-        slab = slab + lax.ppermute(quarter, BOTH, [(0, to)])
-    wide = slab.shape[1] // cores
-    piece = slab[:, :wide]
-    for c in range(1, cores):
-        pairs = [(x, x + c) for x in (0, cores)]
-        piece = piece + lax.ppermute(slab[:, c * wide : (c + 1) * wide], "grp", pairs)
-    far = hosts // 2
-    while far >= 2:
-        pairs = [(h, h + far) for h in range(hosts) if h % (2 * far) < 2]
-        piece = piece + lax.ppermute(piece, "hst", pairs)
-        far //= 2
+    passing = send(rows(levels + 1, levels - 2), 0, 1)
+    pieces = [jnp.where(first, rows(0), 0.0)]
+    pieces += [send(rows(hosts - 1), 0, hosts - 1)]
+    pieces += [send(rows(z), 0, 2 * z) for z in range(levels - 1, 0, -1)]
+    pieces += [send(rows(levels), 0, 1)]
+    pieces += [send(passing[:, (z - 1) * part : z * part], 1, 2 * z + 1) for z in range(levels - 2, 0, -1)]
+    return functools.reduce(jnp.add, pieces), passing
+
+
+def share_heads(slab, groups):
+    wide = slab.shape[2] // groups
+    piece = slab[:, :, :wide]
+    for g in range(1, groups):
+        piece = piece + lax.ppermute(slab[:, :, g * wide : (g + 1) * wide], "grp", [(0, g)])
     return piece
 
 
 def per_device(queries, keys_values, token_ids, lengths, suffix_queries, suffix_kv):
     hosts, groups = lax.axis_size("hst"), lax.axis_size("grp")
     host, group = lax.axis_index("hst"), lax.axis_index("grp")
+    cores = groups // 2
     rows = queries.shape[0]
     heads = suffix_queries.shape[1] // HSZ
-    quarters, keys_values = lax.optimization_barrier(([anchor_quarters(x) for x in keys_values], keys_values))
-    packed, suffix_queries = lax.optimization_barrier((pack(keys_values, groups), suffix_queries))
+    packed, keys_values = lax.optimization_barrier((pack(keys_values, groups), keys_values))
     swapped = lax.all_to_all(packed, "grp", split_axis=0, concat_axis=0, tiled=True)
-    near = jnp.stack([spread_anchor(x, hosts, groups) for x in quarters])
-    gathered = gather_hosts(suffix_queries, hosts)
+    slab, passing = scatter_rows(keys_values, hosts, groups)
+    gathered = gather_hosts(after(suffix_queries, passing), hosts)
+    piece = share_heads(slab, groups)
+    chunks = [piece] + [swap(piece, "hst", k) for k in range(2, hosts, 2)]
     seen = (token_ids.reshape(-1, rows) >= NAMB) & (jnp.arange(rows)[None, :] < lengths[:, None])
     bias = jnp.where(seen, 0.0, NEG).astype(jnp.float32)
-    cores = groups // 2
-    suffix = functools.partial(suffix_attend, jnp.stack([host]), gathered, swapped, suffix_kv, bias)
-    parts = suffix(0, 1, None)
-    held = {0: [near, swap(near, "hst", 1)], cores: [swap(near, "grp", cores)]}
-    held, parts = lax.optimization_barrier((held, parts))
-    held[cores].append(swap(held[0][1], "grp", cores))
+    parts = suffix_attend(jnp.stack([host]), gathered, swapped, suffix_kv, bias, 0, heads, None)
+    parts = parts.astype(jnp.float16)
+    coded = lax.all_to_all(parts, "hst", split_axis=0, concat_axis=0, tiled=True)
+
+    def context(k, anchor, before):
+        at = jnp.stack([host * groups + group, group ^ k, host % 2, host // 2])
+        return context_attend(at, lengths, queries, keys_values, bias, *anchor, before)
+
+    near = jnp.stack(after(chunks, parts))
+    far = swap(near, "hst", 1)
+    held = {0: [near, far], cores: [swap(near, "grp", cores), swap(far, "grp", cores)]}
     for k in range(1, cores):
         held[k] = [swap(x, "grp", k) for x in held[0]]
-        held[cores ^ k] = [swap(held[cores][0], "grp", k)]
-    if heads > 1:
-        parts = suffix(1, heads - 1, parts)
-    held, parts = lax.optimization_barrier((held, parts))
+    context_out = context(0, held[0], None)
+    other = after(held[cores], context_out)
     for k in range(1, cores):
-        held[cores ^ k].append(swap(held[cores][1], "grp", k))
-    coded = lax.all_to_all(parts.astype(jnp.float16), "hst", split_axis=0, concat_axis=0, tiled=True)
-    context_out = None
-    for k in range(groups):
-        at = jnp.stack([host * groups + group, group ^ k, host % 2])
-        context_out = context_attend(at, lengths, queries, keys_values, bias, *held[k], context_out)
+        held[cores ^ k] = [swap(x, "grp", k) for x in other]
+    for k in range(1, groups):
+        context_out = context(k, held[k], context_out)
     return (context_out, combine(coded.astype(jnp.float32)))
 
 

time: 152 us -> 145 us (0.954)
  waiting for transfers between devices: 48 us -> 35 us
  starting transfers between devices: 40.8 us -> 49.2 us
  local copies, waits for them, and re-layouts: 12.7 us -> 9.29 us
  Pallas kernels: 40.7 us -> 42.6 us
    ppermute x12 -> x11, waiting for transfers between devices: 39 us -> 5.22 us  [the longest x8 5.22 us: scatter_rows(): send = lambda x, a, b: lax.ppermute(x, BOTH, [(a * groups, b * groups)])]
    ppermute x11 -> x14, waiting for transfers between devices: 6.62 us -> 29.7 us  [swap(): lax.ppermute(x, axis, [(i, i ^ k) for i in range(lax.axis_size(axis))])]
    ppermute x12 -> x11, starting transfers between devices: 23.6 us -> 29 us  [the longest x8 23.3 us: scatter_rows(): send = lambda x, a, b: lax.ppermute(x, BOTH, [(a * groups, b * groups)])]
    unnamed x42 -> x28, local copies, waits for them, and re-layouts: 8.77 us -> 4.92 us
    slice x3 -> x4, local copies, waits for them, and re-layouts: 1.76 us -> 4.27 us  [the longest x2 2.3 us: scatter_rows(): rows = lambda p, count=1: kv[:, p * part:(p + count) * part]]
    all_to_all x1, waiting for transfers between devices: 2.47 us -> 0.01 us  [per_device(): lax.all_to_all(parts, 'hst', split_axis=0, concat_axis=0, tiled=True)]
    another operation x1 -> x0, local copies, waits for them, and re-layouts: 2.09 us -> none  [per_device(): quarters, keys_values = lax.optimization_barrier(([anchor_quarters(x) for...]
    ppermute x11 -> x14, starting transfers between devices: 8.95 us -> 9.7 us  [swap(): lax.ppermute(x, axis, [(i, i ^ k) for i in range(lax.axis_size(axis))])]
  transfers between devices with their start and end apart: 25 -> 27, of which waited for: 10 -> 7; matrix products, arithmetic and copies ran while one was open for 4% -> 6% of each run, Pallas kernels for 21% -> 23%
where the time goes in v7:
time: 145 us; the launch traced here: 144 us
  starting transfers between devices  49.2 us (34%)
  Pallas kernels  42.6 us (29%)
  waiting for transfers between devices  35 us (24%)
  local copies, waits for them, and re-layouts  9.29 us (6%)
  other arithmetic  7.24 us (5%)
    ppermute x14, waiting for transfers between devices, swap(): lax.ppermute(x, axis, [(i, i ^ k) for i in range(lax.axis_size(axis))])  29.7 us
    ppermute x8, starting transfers between devices, scatter_rows(): send = lambda x, a, b: lax.ppermute(x, BOTH, [(a * groups, b * groups)])  23.3 us
    pallas_call x4, Pallas kernels, context_attend(): pl.pallas_call(context_kernel, grid_spec=pltpu.PrefetchScalarGridSpec(num...  19.6 us
    pallas_call x1, Pallas kernels, suffix_attend(): pl.pallas_call(suffix_kernel, grid_spec=pltpu.PrefetchScalarGridSpec(num_...  13.3 us
    ppermute x14, starting transfers between devices, swap(): lax.ppermute(x, axis, [(i, i ^ k) for i in range(lax.axis_size(axis))])  9.7 us
    pallas_call x1, Pallas kernels, pack(): pl.pallas_call(pack_kernel, grid=(2, 4), in_specs=[pl.BlockSpec((1, few,...  6.18 us
    ppermute x3, starting transfers between devices, share_heads(): lax.ppermute(slab[:, :, g * wide:(g + 1) * wide], 'grp', [(0, g)])  5.77 us
    all_to_all x1, starting transfers between devices, per_device(): lax.all_to_all(parts, 'hst', split_axis=0, concat_axis=0, tiled=True)  5.56 us
  transfers between devices with their start and end apart: 27, of which 7 were waited for; matrix products, arithmetic and copies ran while one was open for 6% of the time, Pallas kernels for 23%

profile of v7, /device:TPU:0, one launch (start us, length us, event | category | flops | bytes accessed | tf_op | source)
XLA Modules:
  0.0 144.3 jit_solution(3334785754630052687)
XLA Ops:
  0.6 6.2 %pack_heads.1 = bf16[4,2,512,384]{3,2,1,0:T(8,128)(2,1)} custom-call(bf16[2,512,1536]{2,1,0:T(8,128)(2,1)} %kv_ref.5), custom_call_target="tpu_custom_call" | custom-call | bytes 6291456 | tf_op jit(solution)/shard_map/pack_heads/pallas_call | solution.py:47
  6.8 4.9 %all-to-all-start = ((bf16[4,2,512,384]{3,2,1,0:T(8,128)(2,1)}), bf16[4,2,512,384]{3,2,1,0:T(8,128)(2,1)}, u32[]{:S(2)}, u32[]{:S(2)}) async-start(bf16[4,2,512,384]{3,2,1,0:T(8,128)(2,1)} %pack_heads.1), calls=%async_computation | async-start | bytes 6291456 | tf_op jit(solution)/shard_map/all_to_all | solution.py:290
  11.7 0.9 slice.45
  12.7 5.9 %collective-permute-start.5 = (bf16[2,128,1536]{2,1,0:T(8,128)(2,1)}, bf16[2,128,1536]{2,1,0:T(8,128)(2,1)}, u32[]{:S(2)}, u32[]{:S(2)}) collective-permute-start(bf16[2,128,1536]{2,1,0:T(8,128)(2,1)} %slice.45), channel_id=1, source_target_pairs={{0,4}} | collective-permute-start | bytes 2359304 | tf_op jit(solution)/shard_map/ppermute | solution.py:264
  18.6 1.4 fusion.4
  19.9 4.5 %collective-permute-start = (bf16[2,64,1536]{2,1,0:T(8,128)(2,1)}, bf16[2,64,1536]{2,1,0:T(8,128)(2,1)}, u32[]{:S(2)}, u32[]{:S(2)}) collective-permute-start(bf16[2,64,1536]{2,1,0:T(8,128)(2,1)} %get-tuple-element.20), channel_id=1, source_target_pairs={{0,28}} | collective-permute-start | bytes 1179656 | tf_op jit(solution)/shard_map/ppermute | solution.py:264
  24.4 2.1 %collective-permute-start.4 = (bf16[2,64,1536]{2,1,0:T(8,128)(2,1)}, bf16[2,64,1536]{2,1,0:T(8,128)(2,1)}, u32[]{:S(2)}, u32[]{:S(2)}) collective-permute-start(bf16[2,64,1536]{2,1,0:T(8,128)(2,1)} %get-tuple-element.21), channel_id=1, source_target_pairs={{0,4}} | collective-permute-start | bytes 1179656 | tf_op jit(solution)/shard_map/ppermute | solution.py:264
  26.5 2.0 %collective-permute-start.3 = (bf16[2,64,1536]{2,1,0:T(8,128)(2,1)}, bf16[2,64,1536]{2,1,0:T(8,128)(2,1)}, u32[]{:S(2)}, u32[]{:S(2)}) collective-permute-start(bf16[2,64,1536]{2,1,0:T(8,128)(2,1)} %get-tuple-element.22), channel_id=1, source_target_pairs={{0,8}} | collective-permute-start | bytes 1179656 | tf_op jit(solution)/shard_map/ppermute | solution.py:264
  28.6 0.1 fusion.3.bias_ref
  28.8 1.2 fusion.5
  30.0 8.6 %collective-permute-done.14 = bf16[128,384]{1,0:T(8,128)(2,1)S(1)} collective-permute-done((bf16[128,384]{1,0:T(8,128)(2,1)S(1)}, bf16[128,384]{1,0:T(8,128)(2,1)S(1)}, u32[]{:S(2)}, u32[]{:S(2)}) %collective-permute-start.14) | collective-permute-done | bytes 98336 | tf_op jit(solution)/shard_map/ppermute | solution.py:247
  38.7 4.8 %collective-permute-start.2 = (bf16[2,64,1536]{2,1,0:T(8,128)(2,1)S(1)}, bf16[2,64,1536]{2,1,0:T(8,128)(2,1)S(1)}, u32[]{:S(2)}, u32[]{:S(2)}) collective-permute-start(bf16[2,64,1536]{2,1,0:T(8,128)(2,1)S(1)} %copy-done.10), channel_id=1, source_target_pairs={{0,16}} | collective-permute-start | bytes 1179656 | tf_op jit(solution)/shard_map/ppermute | solution.py:264
  43.6 2.6 %collective-permute-start.1 = (bf16[2,64,1536]{2,1,0:T(8,128)(2,1)S(1)}, bf16[2,64,1536]{2,1,0:T(8,128)(2,1)S(1)}, u32[]{:S(2)}, u32[]{:S(2)}) collective-permute-start(bf16[2,64,1536]{2,1,0:T(8,128)(2,1)S(1)} %copy-done.9), channel_id=1, source_target_pairs={{0,24}} | collective-permute-start | bytes 1179656 | tf_op jit(solution)/shard_map/ppermute | solution.py:264
  46.2 0.7 collective-permute-start.6
  46.9 0.7 collective-permute-start.7
  47.8 1.0 collective-permute-done.2
  48.8 4.2 %collective-permute-done.1 = bf16[2,64,1536]{2,1,0:T(8,128)(2,1)S(1)} collective-permute-done((bf16[2,64,1536]{2,1,0:T(8,128)(2,1)S(1)}, bf16[2,64,1536]{2,1,0:T(8,128)(2,1)S(1)}, u32[]{:S(2)}, u32[]{:S(2)}) %collective-permute-start.1) | collective-permute-done | bytes 393248 | tf_op jit(solution)/shard_map/ppermute | solution.py:264
  53.0 1.4 add_add_fusion
  54.4 0.8 fusion.6
  55.2 1.9 %collective-permute-start.8 = (bf16[2,64,384]{2,1,0:T(8,128)(2,1)}, bf16[2,64,384]{2,1,0:T(8,128)(2,1)}, u32[]{:S(2)}, u32[]{:S(2)}) collective-permute-start(bf16[2,64,384]{2,1,0:T(8,128)(2,1)} %get-tuple-element.27), channel_id=1, source_target_pairs={{0,1},{4,5},{8,9},{12,13},{16,17},{20,21},{24,25},{28,29}} | collective-permute-start | bytes 294920 | tf_op jit(solution)/shard_map/ppermute | solution.py:279
  57.1 1.9 %collective-permute-start.10 = (bf16[2,64,384]{2,1,0:T(8,128)(2,1)}, bf16[2,64,384]{2,1,0:T(8,128)(2,1)}, u32[]{:S(2)}, u32[]{:S(2)}) collective-permute-start(bf16[2,64,384]{2,1,0:T(8,128)(2,1)} %get-tuple-element.28), channel_id=1, source_target_pairs={{0,3},{4,7},{8,11},{12,15},{16,19},{20,23},{24,27},{28,31}} | collective-permute-start | bytes 294920 | tf_op jit(solution)/shard_map/ppermute | solution.py:279
  59.1 1.9 %collective-permute-start.9 = (bf16[2,64,384]{2,1,0:T(8,128)(2,1)S(1)}, bf16[2,64,384]{2,1,0:T(8,128)(2,1)}, u32[]{:S(2)}, u32[]{:S(2)}) collective-permute-start(bf16[2,64,384]{2,1,0:T(8,128)(2,1)S(1)} %get-tuple-element.29), channel_id=1, source_target_pairs={{0,2},{4,6},{8,10},{12,14},{16,18},{20,22},{24,26},{28,30}} | collective-permute-start | bytes 294920 | tf_op jit(solution)/shard_map/ppermute | solution.py:279
  61.1 0.9 copy-done.4
  61.9 1.1 copy-done.5
  63.1 13.3 %suffix_attend.1 = f32[8,144,384]{2,1,0:T(8,128)S(1)} custom-call(s32[1]{0:T(128)} %bitcast.4.at_ref, bf16[8,128,384]{2,1,0:T(8,128)(2,1)S(1)} %copy-done.5, bf16[4,2,512,384]{3,2,1,0:T(8,128)(2,1)} %all-to-all-done.kv_ref, bf16[2,128,384]{2,1,0:T(8,128)(2,1)S(1)} %copy-done.6, f32[32,512]{1,0:T(8,128)S(1)} %fusion.3.bias_ref), custom_call_target="tpu_custom_call" | custom-call | flops 6845104128 | bytes 7864320 | tf_op jit(solution)/shard_map/suffix_attend/pallas_call | solution.py:116
  76.4 1.1 convert_element_type.8
  77.5 5.6 %all-to-all-start.1 = ((f16[8,144,384]{2,1,0:T(8,128)(2,1)}), f16[8,144,384]{2,1,0:T(8,128)(2,1)}, u32[]{:S(2)}, u32[]{:S(2)}) async-start(f16[8,144,384]{2,1,0:T(8,128)(2,1)} %convert_element_type.8), calls=%async_computation.1 | async-start | bytes 1769472 | tf_op jit(solution)/shard_map/all_to_all | solution.py:299
  83.1 1.1 fusion.1
  84.1 3.9 %collective-permute-start.13 = (bf16[2,64,384]{2,1,0:T(8,128)(2,1)S(1)}, bf16[2,64,384]{2,1,0:T(8,128)(2,1)S(1)}, u32[]{:S(2)}, u32[]{:S(2)}) collective-permute-start(bf16[2,64,384]{2,1,0:T(8,128)(2,1)S(1)} %fusion.1), channel_id=1, source_target_pairs={{0,24},{4,28},{8,16},{12,20},{16,8},{20,12},{24,0},{28,4},{1,25},{... | collective-permute-start | bytes 294920 | tf_op jit(solution)/shard_map/ppermute | solution.py:247
  88.0 0.6 collective-permute-start.11
  88.7 8.5 %collective-permute-done.13 = bf16[2,64,384]{2,1,0:T(8,128)(2,1)S(1)} collective-permute-done((bf16[2,64,384]{2,1,0:T(8,128)(2,1)S(1)}, bf16[2,64,384]{2,1,0:T(8,128)(2,1)S(1)}, u32[]{:S(2)}, u32[]{:S(2)}) %collective-permute-start.13) | collective-permute-done | bytes 98336 | tf_op jit(solution)/shard_map/ppermute | solution.py:247
  97.2 5.1 %collective-permute-done.12 = bf16[2,64,384]{2,1,0:T(8,128)(2,1)S(1)} collective-permute-done((bf16[2,64,384]{2,1,0:T(8,128)(2,1)S(1)}, bf16[2,64,384]{2,1,0:T(8,128)(2,1)S(1)}, u32[]{:S(2)}, u32[]{:S(2)}) %collective-permute-start.12) | collective-permute-done | bytes 98336 | tf_op jit(solution)/shard_map/ppermute | solution.py:247
  102.3 0.8 pad_maximum_fusion.1.near_ref
  103.1 1.2 collective-permute-start.19
  104.3 0.6 collective-permute-start.18
  104.9 6.3 %collective-permute-done.19.far_ref = bf16[4,2,64,384]{3,2,1,0:T(8,128)(2,1)} collective-permute-done((bf16[4,2,64,384]{3,2,1,0:T(8,128)(2,1)}, bf16[4,2,64,384]{3,2,1,0:T(8,128)(2,1)}, u32[]{:S(2)}, u32[]{:S(2)}) %collective-permute-start.19) | collective-permute-done | bytes 393248 | tf_op jit(solution)/shard_map/ppermute | solution.py:247
  111.2 2.2 %collective-permute-start.20 = (bf16[4,2,64,384]{3,2,1,0:T(8,128)(2,1)}, bf16[4,2,64,384]{3,2,1,0:T(8,128)(2,1)}, u32[]{:S(2)}, u32[]{:S(2)}) collective-permute-start(bf16[4,2,64,384]{3,2,1,0:T(8,128)(2,1)} %collective-permute-done.19.far_ref), channel_id=1, source_target_pairs={{0,2},{1,3},{2,0},{3,1},{4,6},{5,7},{6,4},{7,5},{8,10},{9,11},{10,... | collective-permute-start | bytes 1179656 | tf_op jit(solution)/shard_map/ppermute | solution.py:247
  113.4 0.5 collective-permute-start.24
  114.0 1.4 copy-done.1
  115.4 4.9 %context_attend.4.rest_0_ = bf16[512,1536]{1,0:T(8,128)(2,1)} custom-call(s32[4]{0:T(128)S(1)} %get-tuple-element.30.at_ref, s32[32]{0:T(128)S(1)} %copy-done.3, bf16[512,1536]{1,0:T(8,128)(2,1)S(1)} %copy-done.1, bf16[2,512,1536]{2,1,0:T(8,128)(2,1)S(1)} %copy-done, f32[32,512]{1,0:T(8,128)S(1)} %fusion.3.bias_ref, ...), custom_call_target="tpu_custom_call" | custom-call | flops 805306368 | bytes 2359296 | tf_op jit(solution)/shard_map/context_attend/pallas_call | solution.py:218
  120.3 1.1 collective-permute-done.20.far_ref
  121.4 0.5 collective-permute-start.22
  122.1 1.4 copy-done.2
  123.5 4.9 %context_attend.5.rest_0_ = bf16[512,1536]{1,0:T(8,128)(2,1)} custom-call(s32[4]{0:T(128)S(1)} %get-tuple-element.31.at_ref, s32[32]{0:T(128)S(1)} %copy-done.3, bf16[512,1536]{1,0:T(8,128)(2,1)S(1)} %copy-done.2, bf16[2,512,1536]{2,1,0:T(8,128)(2,1)S(1)} %copy-done, f32[32,512]{1,0:T(8,128)S(1)} %fusion.3.bias_ref, ...), custom_call_target="tpu_custom_call", output_to_operand_aliasing={{}: (7, {})} | custom-call | flops 805306368 | bytes 2359296 | tf_op jit(solution)/shard_map/context_attend/pallas_call | solution.py:218
  128.4 4.9 %context_attend.6.rest_0_ = bf16[512,1536]{1,0:T(8,128)(2,1)} custom-call(s32[4]{0:T(128)S(1)} %add_add_fusion.3.at_ref, s32[32]{0:T(128)S(1)} %copy-done.3, bf16[512,1536]{1,0:T(8,128)(2,1)S(1)} %copy-done.2, bf16[2,512,1536]{2,1,0:T(8,128)(2,1)S(1)} %copy-done, f32[32,512]{1,0:T(8,128)S(1)} %fusion.3.bias_ref, ...), custom_call_target="tpu_custom_call", output_to_operand_aliasing={{}: (7, {})} | custom-call | flops 805306368 | bytes 2359296 | tf_op jit(solution)/shard_map/context_attend/pallas_call | solution.py:218
  133.4 4.9 %context_attend.7 = bf16[512,1536]{1,0:T(8,128)(2,1)} custom-call(s32[4]{0:T(128)S(1)} %add_add_fusion.1.at_ref, s32[32]{0:T(128)S(1)} %copy-done.3, bf16[512,1536]{1,0:T(8,128)(2,1)S(1)} %copy-done.2, bf16[2,512,1536]{2,1,0:T(8,128)(2,1)S(1)} %copy-done, f32[32,512]{1,0:T(8,128)S(1)} %fusion.3.bias_ref, ...), custom_call_target="tpu_custom_call", output_to_operand_aliasing={{}: (7, {})} | custom-call | flops 805306368 | bytes 2359296 | tf_op jit(solution)/shard_map/context_attend/pallas_call | solution.py:218
  138.3 2.5 %convert_element_type.9.in_ref = f32[8,144,384]{2,1,0:T(8,128)} convert(f16[8,144,384]{2,1,0:T(8,128)(2,1)} %all-to-all-done.1) | non-fusion elementwise | flops 442368 | bytes 2654208 | tf_op jit(solution)/shard_map/convert_element_type | solution.py:316
  140.8 3.5 %combine_groups.1 = bf16[128,384]{1,0:T(8,128)(2,1)} custom-call(f32[8,144,384]{2,1,0:T(8,128)} %convert_element_type.9.in_ref), custom_call_target="tpu_custom_call" | custom-call | flops 884736 | bytes 1769472 | tf_op jit(solution)/shard_map/combine_groups/pallas_call | solution.py:157
  (58 shorter events, 0.8 us)
Async XLA Ops:
  6.8 4.9 %copy-start = (bf16[2,512,1536]{2,1,0:T(8,128)(2,1)S(1)}, bf16[2,512,1536]{2,1,0:T(8,128)(2,1)}, u32[]{:S(2)}) copy-start(bf16[2,512,1536]{2,1,0:T(8,128)(2,1)} %kv_ref.5) | copy-start | bytes 9437188
  6.8 55.1 %all-to-all-start = ((bf16[4,2,512,384]{3,2,1,0:T(8,128)(2,1)}), bf16[4,2,512,384]{3,2,1,0:T(8,128)(2,1)}, u32[]{:S(2)}, u32[]{:S(2)}) async-start(bf16[4,2,512,384]{3,2,1,0:T(8,128)(2,1)} %pack_heads.1), calls=%async_computation | async-start | bytes 6291456 | tf_op jit(solution)/shard_map/all_to_all | solution.py:290
  12.7 15.8 %copy-start.11 = (s32[16384]{0:T(1024)S(1)}, s32[16384]{0:T(1024)}, u32[]{:S(2)}) copy-start(s32[16384]{0:T(1024)} %param.8) | copy-start | bytes 196612
  12.7 15.9 %copy-start.3 = (s32[32]{0:T(128)S(1)}, s32[32]{0:T(128)}, u32[]{:S(2)}) copy-start(s32[32]{0:T(128)} %len_ref.7) | copy-start | bytes 388
  12.7 16.0 %copy-start.8 = (bf16[128,384]{1,0:T(8,128)(2,1)S(1)}, bf16[128,384]{1,0:T(8,128)(2,1)}, u32[]{:S(2)}) copy-start(bf16[128,384]{1,0:T(8,128)(2,1)} %param.10) | copy-start | bytes 294916
  12.7 16.0 %collective-permute-start.5 = (bf16[2,128,1536]{2,1,0:T(8,128)(2,1)}, bf16[2,128,1536]{2,1,0:T(8,128)(2,1)}, u32[]{:S(2)}, u32[]{:S(2)}) collective-permute-start(bf16[2,128,1536]{2,1,0:T(8,128)(2,1)} %slice.45), channel_id=1, source_target_pairs={{0,4}} | collective-permute-start | bytes 2359304 | tf_op jit(solution)/shard_map/ppermute | solution.py:264
  19.9 18.7 %collective-permute-start = (bf16[2,64,1536]{2,1,0:T(8,128)(2,1)}, bf16[2,64,1536]{2,1,0:T(8,128)(2,1)}, u32[]{:S(2)}, u32[]{:S(2)}) collective-permute-start(bf16[2,64,1536]{2,1,0:T(8,128)(2,1)} %get-tuple-element.20), channel_id=1, source_target_pairs={{0,28}} | collective-permute-start | bytes 1179656 | tf_op jit(solution)/shard_map/ppermute | solution.py:264
  24.4 19.1 %collective-permute-start.4 = (bf16[2,64,1536]{2,1,0:T(8,128)(2,1)}, bf16[2,64,1536]{2,1,0:T(8,128)(2,1)}, u32[]{:S(2)}, u32[]{:S(2)}) collective-permute-start(bf16[2,64,1536]{2,1,0:T(8,128)(2,1)} %get-tuple-element.21), channel_id=1, source_target_pairs={{0,4}} | collective-permute-start | bytes 1179656 | tf_op jit(solution)/shard_map/ppermute | solution.py:264
  26.5 21.3 %collective-permute-start.3 = (bf16[2,64,1536]{2,1,0:T(8,128)(2,1)}, bf16[2,64,1536]{2,1,0:T(8,128)(2,1)}, u32[]{:S(2)}, u32[]{:S(2)}) collective-permute-start(bf16[2,64,1536]{2,1,0:T(8,128)(2,1)} %get-tuple-element.22), channel_id=1, source_target_pairs={{0,8}} | collective-permute-start | bytes 1179656 | tf_op jit(solution)/shard_map/ppermute | solution.py:264
  28.6 10.1 %copy-start.10 = (bf16[2,64,1536]{2,1,0:T(8,128)(2,1)S(1)}, bf16[2,64,1536]{2,1,0:T(8,128)(2,1)}, u32[]{:S(2)}) copy-start(bf16[2,64,1536]{2,1,0:T(8,128)(2,1)} %get-tuple-element.23) | copy-start | bytes 1179652
  28.6 15.0 %copy-start.9 = (bf16[2,64,1536]{2,1,0:T(8,128)(2,1)S(1)}, bf16[2,64,1536]{2,1,0:T(8,128)(2,1)}, u32[]{:S(2)}) copy-start(bf16[2,64,1536]{2,1,0:T(8,128)(2,1)} %get-tuple-element.24) | copy-start | bytes 1179652
  28.7 17.5 %collective-permute-start.16 = (bf16[128,384]{1,0:T(8,128)(2,1)S(1)}, bf16[128,384]{1,0:T(8,128)(2,1)S(1)}, u32[]{:S(2)}, u32[]{:S(2)}) collective-permute-start(bf16[128,384]{1,0:T(8,128)(2,1)S(1)} %copy-done.8), channel_id=1, source_target_pairs={{0,24},{4,28},{8,16},{12,20},{16,8},{20,12},{24,0},{28,4},{1,25},{... | collective-permute-start | bytes 294920 | tf_op jit(solution)/shard_map/ppermute | solution.py:247
  28.8 9.9 %collective-permute-start.14 = (bf16[128,384]{1,0:T(8,128)(2,1)S(1)}, bf16[128,384]{1,0:T(8,128)(2,1)S(1)}, u32[]{:S(2)}, u32[]{:S(2)}) collective-permute-start(bf16[128,384]{1,0:T(8,128)(2,1)S(1)} %copy-done.8), channel_id=1, source_target_pairs={{0,8},{4,12},{8,0},{12,4},{16,24},{20,28},{24,16},{28,20},{1,9},{5... | collective-permute-start | bytes 294920 | tf_op jit(solution)/shard_map/ppermute | solution.py:247
  38.7 8.2 %collective-permute-start.15 = (bf16[128,384]{1,0:T(8,128)(2,1)S(1)}, bf16[128,384]{1,0:T(8,128)(2,1)S(1)}, u32[]{:S(2)}, u32[]{:S(2)}) collective-permute-start(bf16[128,384]{1,0:T(8,128)(2,1)S(1)} %copy-done.8), channel_id=1, source_target_pairs={{0,16},{4,20},{8,24},{12,28},{16,0},{20,4},{24,8},{28,12},{1,17},{... | collective-permute-start | bytes 294920 | tf_op jit(solution)/shard_map/ppermute | solution.py:247
  38.7 10.1 %collective-permute-start.2 = (bf16[2,64,1536]{2,1,0:T(8,128)(2,1)S(1)}, bf16[2,64,1536]{2,1,0:T(8,128)(2,1)S(1)}, u32[]{:S(2)}, u32[]{:S(2)}) collective-permute-start(bf16[2,64,1536]{2,1,0:T(8,128)(2,1)S(1)} %copy-done.10), channel_id=1, source_target_pairs={{0,16}} | collective-permute-start | bytes 1179656 | tf_op jit(solution)/shard_map/ppermute | solution.py:264
  43.6 9.4 %collective-permute-start.1 = (bf16[2,64,1536]{2,1,0:T(8,128)(2,1)S(1)}, bf16[2,64,1536]{2,1,0:T(8,128)(2,1)S(1)}, u32[]{:S(2)}, u32[]{:S(2)}) collective-permute-start(bf16[2,64,1536]{2,1,0:T(8,128)(2,1)S(1)} %copy-done.9), channel_id=1, source_target_pairs={{0,24}} | collective-permute-start | bytes 1179656 | tf_op jit(solution)/shard_map/ppermute | solution.py:264
  46.2 6.8 %collective-permute-start.6 = (bf16[2,64,1536]{2,1,0:T(8,128)(2,1)S(1)}, bf16[2,64,1536]{2,1,0:T(8,128)(2,1)S(1)}, u32[]{:S(2)}, u32[]{:S(2)}) collective-permute-start(bf16[2,64,1536]{2,1,0:T(8,128)(2,1)S(1)} %get-tuple-element.25), channel_id=1, source_target_pairs={{4,20}} | collective-permute-start | bytes 1179656 | tf_op jit(solution)/shard_map/ppermute | solution.py:264
  46.9 6.1 %collective-permute-start.7 = (bf16[2,64,1536]{2,1,0:T(8,128)(2,1)S(1)}, bf16[2,64,1536]{2,1,0:T(8,128)(2,1)S(1)}, u32[]{:S(2)}, u32[]{:S(2)}) collective-permute-start(bf16[2,64,1536]{2,1,0:T(8,128)(2,1)S(1)} %get-tuple-element.26), channel_id=1, source_target_pairs={{4,12}} | collective-permute-start | bytes 1179656 | tf_op jit(solution)/shard_map/ppermute | solution.py:264
  47.7 14.2 %copy-start.6 = (bf16[2,128,384]{2,1,0:T(8,128)(2,1)S(1)}, bf16[2,128,384]{2,1,0:T(8,128)(2,1)}, u32[]{:S(2)}) copy-start(bf16[2,128,384]{2,1,0:T(8,128)(2,1)} %sk_ref.1) | copy-start | bytes 589828
  47.7 13.2 %collective-permute-start.17 = (bf16[4,128,384]{2,1,0:T(8,128)(2,1)S(1)}, bf16[4,128,384]{2,1,0:T(8,128)(2,1)S(1)}, u32[]{:S(2)}, u32[]{:S(2)}) collective-permute-start(bf16[4,128,384]{2,1,0:T(8,128)(2,1)S(1)} %pad_maximum_fusion), channel_id=1, source_target_pairs={{0,4},{4,0},{8,12},{12,8},{16,20},{20,16},{24,28},{28,24},{1,5},{5... | collective-permute-start | bytes 1179656 | tf_op jit(solution)/shard_map/ppermute | solution.py:247
  54.4 6.6 %copy-start.7 = (bf16[2,64,1536]{2,1,0:T(8,128)(2,1)}, bf16[2,64,1536]{2,1,0:T(8,128)(2,1)S(1)}, u32[]{:S(2)}) copy-start(bf16[2,64,1536]{2,1,0:T(8,128)(2,1)S(1)} %add_add_fusion) | copy-start | bytes 1179652
  55.2 27.8 %collective-permute-start.8 = (bf16[2,64,384]{2,1,0:T(8,128)(2,1)}, bf16[2,64,384]{2,1,0:T(8,128)(2,1)}, u32[]{:S(2)}, u32[]{:S(2)}) collective-permute-start(bf16[2,64,384]{2,1,0:T(8,128)(2,1)} %get-tuple-element.27), channel_id=1, source_target_pairs={{0,1},{4,5},{8,9},{12,13},{16,17},{20,21},{24,25},{28,29}} | collective-permute-start | bytes 294920 | tf_op jit(solution)/shard_map/ppermute | solution.py:279
  57.1 25.9 %collective-permute-start.10 = (bf16[2,64,384]{2,1,0:T(8,128)(2,1)}, bf16[2,64,384]{2,1,0:T(8,128)(2,1)}, u32[]{:S(2)}, u32[]{:S(2)}) collective-permute-start(bf16[2,64,384]{2,1,0:T(8,128)(2,1)} %get-tuple-element.28), channel_id=1, source_target_pairs={{0,3},{4,7},{8,11},{12,15},{16,19},{20,23},{24,27},{28,31}} | collective-permute-start | bytes 294920 | tf_op jit(solution)/shard_map/ppermute | solution.py:279
  59.1 24.0 %collective-permute-start.9 = (bf16[2,64,384]{2,1,0:T(8,128)(2,1)S(1)}, bf16[2,64,384]{2,1,0:T(8,128)(2,1)}, u32[]{:S(2)}, u32[]{:S(2)}) collective-permute-start(bf16[2,64,384]{2,1,0:T(8,128)(2,1)S(1)} %get-tuple-element.29), channel_id=1, source_target_pairs={{0,2},{4,6},{8,10},{12,14},{16,18},{20,22},{24,26},{28,30}} | collective-permute-start | bytes 294920 | tf_op jit(solution)/shard_map/ppermute | solution.py:279
  61.1 0.9 copy-start.4
  61.9 1.1 copy-start.5
  77.5 60.8 %all-to-all-start.1 = ((f16[8,144,384]{2,1,0:T(8,128)(2,1)}), f16[8,144,384]{2,1,0:T(8,128)(2,1)}, u32[]{:S(2)}, u32[]{:S(2)}) async-start(f16[8,144,384]{2,1,0:T(8,128)(2,1)} %convert_element_type.8), calls=%async_computation.1 | async-start | bytes 1769472 | tf_op jit(solution)/shard_map/all_to_all | solution.py:299
  84.1 13.0 %collective-permute-start.13 = (bf16[2,64,384]{2,1,0:T(8,128)(2,1)S(1)}, bf16[2,64,384]{2,1,0:T(8,128)(2,1)S(1)}, u32[]{:S(2)}, u32[]{:S(2)}) collective-permute-start(bf16[2,64,384]{2,1,0:T(8,128)(2,1)S(1)} %fusion.1), channel_id=1, source_target_pairs={{0,24},{4,28},{8,16},{12,20},{16,8},{20,12},{24,0},{28,4},{1,25},{... | collective-permute-start | bytes 294920 | tf_op jit(solution)/shard_map/ppermute | solution.py:247
  88.0 14.3 %collective-permute-start.12 = (bf16[2,64,384]{2,1,0:T(8,128)(2,1)S(1)}, bf16[2,64,384]{2,1,0:T(8,128)(2,1)S(1)}, u32[]{:S(2)}, u32[]{:S(2)}) collective-permute-start(bf16[2,64,384]{2,1,0:T(8,128)(2,1)S(1)} %fusion.1), channel_id=1, source_target_pairs={{0,16},{4,20},{8,24},{12,28},{16,0},{20,4},{24,8},{28,12},{1,17},{... | collective-permute-start | bytes 294920 | tf_op jit(solution)/shard_map/ppermute | solution.py:247
  88.0 14.3 %collective-permute-start.11 = (bf16[2,64,384]{2,1,0:T(8,128)(2,1)S(1)}, bf16[2,64,384]{2,1,0:T(8,128)(2,1)S(1)}, u32[]{:S(2)}, u32[]{:S(2)}) collective-permute-start(bf16[2,64,384]{2,1,0:T(8,128)(2,1)S(1)} %fusion.1), channel_id=1, source_target_pairs={{0,8},{4,12},{8,0},{12,4},{16,24},{20,28},{24,16},{28,20},{1,9},{5... | collective-permute-start | bytes 294920 | tf_op jit(solution)/shard_map/ppermute | solution.py:247
  103.1 8.1 %collective-permute-start.19 = (bf16[4,2,64,384]{3,2,1,0:T(8,128)(2,1)}, bf16[4,2,64,384]{3,2,1,0:T(8,128)(2,1)}, u32[]{:S(2)}, u32[]{:S(2)}) collective-permute-start(bf16[4,2,64,384]{3,2,1,0:T(8,128)(2,1)} %pad_maximum_fusion.1.near_ref), channel_id=1, source_target_pairs={{0,4},{4,0},{8,12},{12,8},{16,20},{20,16},{24,28},{28,24},{1,5},{5... | collective-permute-start | bytes 1179656 | tf_op jit(solution)/shard_map/ppermute | solution.py:247
  104.3 16.0 %collective-permute-start.18 = (bf16[4,2,64,384]{3,2,1,0:T(8,128)(2,1)}, bf16[4,2,64,384]{3,2,1,0:T(8,128)(2,1)}, u32[]{:S(2)}, u32[]{:S(2)}) collective-permute-start(bf16[4,2,64,384]{3,2,1,0:T(8,128)(2,1)} %pad_maximum_fusion.1.near_ref), channel_id=1, source_target_pairs={{0,2},{1,3},{2,0},{3,1},{4,6},{5,7},{6,4},{7,5},{8,10},{9,11},{10,... | collective-permute-start | bytes 1179656 | tf_op jit(solution)/shard_map/ppermute | solution.py:247
  111.2 10.2 %collective-permute-start.20 = (bf16[4,2,64,384]{3,2,1,0:T(8,128)(2,1)}, bf16[4,2,64,384]{3,2,1,0:T(8,128)(2,1)}, u32[]{:S(2)}, u32[]{:S(2)}) collective-permute-start(bf16[4,2,64,384]{3,2,1,0:T(8,128)(2,1)} %collective-permute-done.19.far_ref), channel_id=1, source_target_pairs={{0,2},{1,3},{2,0},{3,1},{4,6},{5,7},{6,4},{7,5},{8,10},{9,11},{10,... | collective-permute-start | bytes 1179656 | tf_op jit(solution)/shard_map/ppermute | solution.py:247
  113.4 8.7 %collective-permute-start.23 = (bf16[4,2,64,384]{3,2,1,0:T(8,128)(2,1)}, bf16[4,2,64,384]{3,2,1,0:T(8,128)(2,1)}, u32[]{:S(2)}, u32[]{:S(2)}) collective-permute-start(bf16[4,2,64,384]{3,2,1,0:T(8,128)(2,1)} %pad_maximum_fusion.1.near_ref), channel_id=1, source_target_pairs={{0,1},{1,0},{2,3},{3,2},{4,5},{5,4},{6,7},{7,6},{8,9},{9,8},{10,11... | collective-permute-start | bytes 1179656 | tf_op jit(solution)/shard_map/ppermute | solution.py:247
  113.4 8.7 %collective-permute-start.24 = (bf16[4,2,64,384]{3,2,1,0:T(8,128)(2,1)}, bf16[4,2,64,384]{3,2,1,0:T(8,128)(2,1)}, u32[]{:S(2)}, u32[]{:S(2)}) collective-permute-start(bf16[4,2,64,384]{3,2,1,0:T(8,128)(2,1)} %collective-permute-done.19.far_ref), channel_id=1, source_target_pairs={{0,1},{1,0},{2,3},{3,2},{4,5},{5,4},{6,7},{7,6},{8,9},{9,8},{10,11... | collective-permute-start | bytes 1179656 | tf_op jit(solution)/shard_map/ppermute | solution.py:247
  114.0 1.4 copy-start.1
  121.4 11.9 %collective-permute-start.21 = (bf16[4,2,64,384]{3,2,1,0:T(8,128)(2,1)}, bf16[4,2,64,384]{3,2,1,0:T(8,128)(2,1)}, u32[]{:S(2)}, u32[]{:S(2)}) collective-permute-start(bf16[4,2,64,384]{3,2,1,0:T(8,128)(2,1)} %collective-permute-done.18.near_ref), channel_id=1, source_target_pairs={{0,1},{1,0},{2,3},{3,2},{4,5},{5,4},{6,7},{7,6},{8,9},{9,8},{10,11... | collective-permute-start | bytes 1179656 | tf_op jit(solution)/shard_map/ppermute | solution.py:247
  121.4 11.9 %collective-permute-start.22 = (bf16[4,2,64,384]{3,2,1,0:T(8,128)(2,1)}, bf16[4,2,64,384]{3,2,1,0:T(8,128)(2,1)}, u32[]{:S(2)}, u32[]{:S(2)}) collective-permute-start(bf16[4,2,64,384]{3,2,1,0:T(8,128)(2,1)} %collective-permute-done.20.far_ref), channel_id=1, source_target_pairs={{0,1},{1,0},{2,3},{3,2},{4,5},{5,4},{6,7},{7,6},{8,9},{9,8},{10,11... | collective-permute-start | bytes 1179656 | tf_op jit(solution)/shard_map/ppermute | solution.py:247
  122.1 1.4 copy-start.2

commit v8 on v6

--- a/solution.py
+++ b/solution.py
@@ -12,7 +12,7 @@
 NAMB = 512
 NEG = -1e30
 FLOOR = -2000.0
-EXTRA = 16
+EXTRA = 8
 TILE = 256
 C2 = math.log2(math.e) / math.sqrt(HSZ)
 BOTH = ("hst", "grp")
@@ -34,25 +34,53 @@
     return base, total, [w.astype(jnp.bfloat16) for w in weights]
 
 
-def pack_kernel(kv_ref, out_ref):
-    groups, _, _, part = out_ref.shape
-    for g in range(groups):
-        out_ref[g, 0] = kv_ref[0, :, g * part : (g + 1) * part]
+def pack_kernel(kv_ref, out_ref, below_ref, *refs):
+    across_refs, diagonal_refs, (held, came, left) = refs[0:2], refs[2:4], refs[4:]
+    groups, _, rows, part = out_ref.shape
+    few, wide, pieces = rows // 4, groups * part // 2, [(s, i) for s in range(2) for i in range(4)]
+    arrive = {}
+    for s, i in pieces:
+        band = pl.ds(i * few, few)
+        arrive[s, i] = pltpu.make_async_copy(kv_ref.at[s, band], held.at[s, band], came.at[s, i])
+        arrive[s, i].start()
+    leave = []
+    for s, i in pieces:
+        arrive[s, i].wait()
+        band, place = pl.ds(i * few, few), pl.ds(i % 2 * few, few)
+        right = held.at[s, band, pl.ds(wide, wide)]
+        moves = [(right, (across_refs if i < 2 else diagonal_refs)[s].at[place])]
+        if i >= 2:
+            moves.append((held.at[s, band, pl.ds(0, wide)], below_ref.at[s, place]))
+        moves += [(held.at[s, band, pl.ds(g * part, part)], out_ref.at[g, s, band]) for g in range(groups)]
+        for n, (source, target) in enumerate(moves):
+            leave.append(pltpu.make_async_copy(source, target, left.at[s, i, n]))
+            leave[-1].start()
+    for copy in leave:
+        copy.wait()
 
 
 def pack(kv, groups):
     _, rows, width = kv.shape
-    part = width // groups
-    few = rows // 4
-    return pl.pallas_call(
+    anywhere = pl.BlockSpec(memory_space=pl.ANY)
+    half = jax.ShapeDtypeStruct((rows // 2, width // 2), kv.dtype)
+    out, below, *others = pl.pallas_call(
         pack_kernel,
-        grid=(2, 4),
-        in_specs=[pl.BlockSpec((1, few, width), lambda s, i: (s, i, 0))],
-        out_specs=pl.BlockSpec((groups, 1, few, part), lambda s, i: (0, s, i, 0)),
-        out_shape=jax.ShapeDtypeStruct((groups, 2, rows, part), kv.dtype),
-        cost_estimate=pl.CostEstimate(flops=0, bytes_accessed=4 * kv.size, transcendentals=0),
+        in_specs=[anywhere],
+        out_specs=[anywhere] * 6,
+        out_shape=[
+            jax.ShapeDtypeStruct((groups, 2, rows, width // groups), kv.dtype),
+            jax.ShapeDtypeStruct((2, rows // 2, width // 2), kv.dtype),
+        ]
+        + [half] * 4,
+        scratch_shapes=[
+            pltpu.VMEM(kv.shape, kv.dtype),
+            pltpu.SemaphoreType.DMA((2, 4)),
+            pltpu.SemaphoreType.DMA((2, 4, groups + 2)),
+        ],
+        cost_estimate=pl.CostEstimate(flops=0, bytes_accessed=6 * kv.size, transcendentals=0),
         name="pack_heads",
     )(kv)
+    return out, below, others[:2], others[2:]
 
 
 def pipelined(tasks, score, finish):
@@ -129,7 +157,7 @@
         ),
         out_shape=jax.ShapeDtypeStruct((hosts, share + EXTRA, width), jnp.float32),
         input_output_aliases={5: 0} if more else {},
-        compiler_params=pltpu.CompilerParams(vmem_limit_bytes=24 * 1024 * 1024),
+        compiler_params=pltpu.CompilerParams(vmem_limit_bytes=60 * 1024 * 1024),
         cost_estimate=pl.CostEstimate(
             flops=8 * count * hosts * share * seen * HSZ,
             bytes_accessed=4 * count * (groups * rows + 3 * hosts * share) * HSZ,
@@ -228,7 +256,7 @@
         ),
         out_shape=jax.ShapeDtypeStruct((rows, width), q.dtype),
         input_output_aliases={7: 0} if more else {},
-        compiler_params=pltpu.CompilerParams(vmem_limit_bytes=24 * 1024 * 1024),
+        compiler_params=pltpu.CompilerParams(vmem_limit_bytes=60 * 1024 * 1024),
         cost_estimate=pl.CostEstimate(
             flops=8 * rows * rows * wide,
             bytes_accessed=12 * rows * wide,
@@ -252,20 +280,15 @@
     return lax.optimization_barrier((x, done))[0]
 
 
-def quarter(kv, y, x):
-    _, rows, width = kv.shape
-    tall, wide = rows // 2, width // 2
-    return kv[:, y * tall : (y + 1) * tall, x * wide : (x + 1) * wide]
-
-
-def scatter_anchor(mine, across, diagonal, below, groups):
+def scatter_anchor(kv, across, diagonal, below, groups):
     cores = groups // 2
     first = (lax.axis_index("hst") == 0) & (lax.axis_index("grp") == 0)
     send = lambda x, to: lax.ppermute(x, BOTH, [(0, to)])
     down = send(below, groups)
+    _, rows, width = kv.shape
     slabs = []
     for s in range(2):
-        slab = jnp.where(first, mine[s], 0.0) + send(diagonal[s], groups + cores) + send(across[s], cores)
+        slab = jnp.where(first, kv[s, : rows // 2, : width // 2], 0.0) + send(diagonal[s], groups + cores) + send(across[s], cores)
         slabs.append(slab + (after(down[s], slabs[0]) if s else down[s]))
     return slabs
 
@@ -290,10 +313,9 @@
     host, group = lax.axis_index("hst"), lax.axis_index("grp")
     rows = queries.shape[0]
     heads = suffix_queries.shape[1] // HSZ
-    quarters = [quarter(keys_values, y, x) for y, x in ((0, 0), (0, 1), (1, 1), (1, 0))]
-    quarters, keys_values = lax.optimization_barrier((quarters, keys_values))
-    swapped = lax.all_to_all(pack(keys_values, groups), "grp", split_axis=0, concat_axis=0, tiled=True)
-    slabs = scatter_anchor(*quarters, groups)
+    packed, below, across, diagonal = pack(keys_values, groups)
+    swapped = lax.all_to_all(packed, "grp", split_axis=0, concat_axis=0, tiled=True)
+    slabs = scatter_anchor(keys_values, across, diagonal, below, groups)
     near = jnp.stack([spread_anchor(x, hosts, groups) for x in slabs])
     suffix_queries = after(suffix_queries, slabs[0])
     gathered = gather_hosts(suffix_queries, hosts)
@@ -301,23 +323,30 @@
     bias = jnp.where(seen, 0.0, NEG).astype(jnp.float32)
     cores = groups // 2
     suffix = functools.partial(suffix_attend, jnp.stack([host]), gathered, swapped, suffix_kv, bias)
-    parts = suffix(0, 1, None)
-    held = {0: [near, swap(near, "hst", 1)], cores: [swap(near, "grp", cores)]}
-    held, parts = lax.optimization_barrier((held, parts))
-    held[cores].append(swap(held[0][1], "grp", cores))
+    early = max(1, heads - 1)
+    parts = suffix(0, early, None)
+    far, other_near, parts = lax.optimization_barrier((swap(near, "hst", 1), swap(near, "grp", cores), parts))
+    other_far = swap(far, "grp", cores)
+    held = {0: [near, far], cores: [other_near, other_far]}
+    by_core = [[swap(x, "grp", k) for x in (near, far, other_near)] for k in range(1, cores)]
+    if heads > early:
+        parts = suffix(early, heads - early, parts)
+    by_core, parts = lax.optimization_barrier((by_core, parts))
+    parts = parts.astype(jnp.float16)
+    held[0], other_far = after((held[0], other_far), parts)
+    coded = lax.all_to_all(parts, "hst", split_axis=0, concat_axis=0, tiled=True)
+
+    def context(k, before):
+        at = jnp.stack([host * groups + group, group ^ k, host % 2])
+        return context_attend(at, lengths, queries, keys_values, bias, *held[k], before)
+
+    context_out = context(0, None)
+    other_far = after(other_far, context_out)
     for k in range(1, cores):
-        held[k] = [swap(x, "grp", k) for x in held[0]]
-        held[cores ^ k] = [swap(held[cores][0], "grp", k)]
-    if heads > 1:
-        parts = suffix(1, heads - 1, parts)
-    held, parts = lax.optimization_barrier((held, parts))
-    for k in range(1, cores):
-        held[cores ^ k].append(swap(held[cores][1], "grp", k))
-    coded = lax.all_to_all(parts.astype(jnp.float16), "hst", split_axis=0, concat_axis=0, tiled=True)
-    context_out = None
-    for k in range(groups):
-        at = jnp.stack([host * groups + group, group ^ k, host % 2])
-        context_out = context_attend(at, lengths, queries, keys_values, bias, *held[k], context_out)
+        held[k] = by_core[k - 1][:2]
+        held[cores ^ k] = [by_core[k - 1][2], swap(other_far, "grp", k)]
+    for k in range(1, groups):
+        context_out = context(k, context_out)
     return (context_out, combine(coded.astype(jnp.float32)))
 
 

time: 124 us -> 159 us (1.28)
  waiting for transfers between devices: 18.8 us -> 57.3 us
  local copies, waits for them, and re-layouts: 12.1 us -> 3.64 us
  Pallas kernels: 40.7 us -> 44.9 us
  other arithmetic: 7.75 us -> 10.4 us
    ppermute x5, waiting for transfers between devices: 0.01 us -> 33.7 us  [scatter_anchor(): send = lambda x, to: lax.ppermute(x, BOTH, [(0, to)])]
    ppermute x11, waiting for transfers between devices: 3.47 us -> 10.7 us  [swap(): lax.ppermute(x, axis, [(i, i ^ k) for i in range(lax.axis_size(axis))])]
    pallas_call x2, Pallas kernels: 12.7 us -> 16.3 us  [suffix_attend(): pl.pallas_call(suffix_kernel, grid_spec=pltpu.PrefetchScalarGridSpec(num_...]
    unnamed x34 -> x24, local copies, waits for them, and re-layouts: 5.8 us -> 2.47 us
    slice x1 -> x0, local copies, waits for them, and re-layouts: 3.2 us -> none  [quarter(): return kv[:, y * tall:(y + 1) * tall, x * wide:(x + 1) * wide]]
    pallas_call x4, Pallas kernels: 18.3 us -> 21.2 us  [context_attend(): pl.pallas_call(context_kernel, grid_spec=pltpu.PrefetchScalarGridSpec(num...]
    all_to_all x2, waiting for transfers between devices: 2.89 us -> 0.01 us  [the longest x1 0.01 us: per_device(): lax.all_to_all(parts, 'hst', split_axis=0, concat_axis=0, tiled=True)]
    another operation x3 -> x4, other arithmetic: 0.23 us -> 2.55 us  [context(): at = jnp.stack([host * groups + group, group ^ k, host % 2])]
  transfers between devices with their start and end apart: 24 -> 24, of which waited for: 8 -> 8; matrix products, arithmetic and copies ran while one was open for 5% -> 5% of each run, Pallas kernels for 30% -> 24%
where the time goes in v8:
time: 159 us; the launch traced here: 158 us
  waiting for transfers between devices  57.3 us (36%)
  Pallas kernels  44.9 us (28%)
  starting transfers between devices  40.7 us (26%)
  other arithmetic  10.4 us (7%)
  local copies, waits for them, and re-layouts  3.64 us (2%)
    ppermute x5, waiting for transfers between devices, scatter_anchor(): send = lambda x, to: lax.ppermute(x, BOTH, [(0, to)])  33.7 us
    pallas_call x4, Pallas kernels, context_attend(): pl.pallas_call(context_kernel, grid_spec=pltpu.PrefetchScalarGridSpec(num...  21.2 us
    pallas_call x2, Pallas kernels, suffix_attend(): pl.pallas_call(suffix_kernel, grid_spec=pltpu.PrefetchScalarGridSpec(num_...  16.3 us
    ppermute x5, starting transfers between devices, scatter_anchor(): send = lambda x, to: lax.ppermute(x, BOTH, [(0, to)])  16 us
    ppermute x4, waiting for transfers between devices, spread_anchor(): piece = piece + lax.ppermute(piece, 'hst', pairs)  12.8 us
    ppermute x11, waiting for transfers between devices, swap(): lax.ppermute(x, axis, [(i, i ^ k) for i in range(lax.axis_size(axis))])  10.7 us
    ppermute x11, starting transfers between devices, swap(): lax.ppermute(x, axis, [(i, i ^ k) for i in range(lax.axis_size(axis))])  7.79 us
    all_to_all x1, starting transfers between devices, per_device(): lax.all_to_all(parts, 'hst', split_axis=0, concat_axis=0, tiled=True)  5.21 us
  transfers between devices with their start and end apart: 24, of which 8 were waited for; matrix products, arithmetic and copies ran while one was open for 5% of the time, Pallas kernels for 24%

profile of v8, /device:TPU:0, one launch (start us, length us, event | category | flops | bytes accessed | tf_op | source)
XLA Modules:
  0.0 157.9 jit_solution(14152477792119301353)
XLA Ops:
  0.6 3.9 %pack_heads.1 = (bf16[4,2,512,384]{3,2,1,0:T(8,128)(2,1)}, bf16[2,256,768]{2,1,0:T(8,128)(2,1)}, bf16[256,768]{1,0:T(8,128)(2,1)}, bf16[256,768]{1,0:T(8,128)(2,...) custom-call(bf16[2,512,1536]{2,1,0:T(8,128)(2,1)} %kv_ref.9), custom_call_target="tpu_custom_call" | custom-call | bytes 9437184 | tf_op jit(solution)/shard_map/pack_heads/pallas_call | solution.py:66
  4.5 5.8 %collective-permute-start.2 = (bf16[2,256,768]{2,1,0:T(8,128)(2,1)}, bf16[2,256,768]{2,1,0:T(8,128)(2,1)}, u32[]{:S(2)}, u32[]{:S(2)}) collective-permute-start(bf16[2,256,768]{2,1,0:T(8,128)(2,1)} %get-tuple-element.23), channel_id=1, source_target_pairs={{0,4}} | collective-permute-start | bytes 2359304 | tf_op jit(solution)/shard_map/ppermute | solution.py:286
  10.3 3.8 %all-to-all-start = ((bf16[4,2,512,384]{3,2,1,0:T(8,128)(2,1)}), bf16[4,2,512,384]{3,2,1,0:T(8,128)(2,1)S(1)}, u32[]{:S(2)}, u32[]{:S(2)}) async-start(bf16[4,2,512,384]{3,2,1,0:T(8,128)(2,1)} %get-tuple-element.28), calls=%async_computation | async-start | bytes 6291456 | tf_op jit(solution)/shard_map/all_to_all | solution.py:317
  14.1 2.7 %collective-permute-start = (bf16[256,768]{1,0:T(8,128)(2,1)}, bf16[256,768]{1,0:T(8,128)(2,1)}, u32[]{:S(2)}, u32[]{:S(2)}) collective-permute-start(bf16[256,768]{1,0:T(8,128)(2,1)} %get-tuple-element.21), channel_id=1, source_target_pairs={{0,6}} | collective-permute-start | bytes 1179656 | tf_op jit(solution)/shard_map/ppermute | solution.py:286
  16.9 3.4 %collective-permute-start.1 = (bf16[256,768]{1,0:T(8,128)(2,1)}, bf16[256,768]{1,0:T(8,128)(2,1)}, u32[]{:S(2)}, u32[]{:S(2)}) collective-permute-start(bf16[256,768]{1,0:T(8,128)(2,1)} %get-tuple-element.22), channel_id=1, source_target_pairs={{0,2}} | collective-permute-start | bytes 1179656 | tf_op jit(solution)/shard_map/ppermute | solution.py:286
  20.3 2.0 %collective-permute-start.6 = (bf16[256,768]{1,0:T(8,128)(2,1)}, bf16[256,768]{1,0:T(8,128)(2,1)}, u32[]{:S(2)}, u32[]{:S(2)}) collective-permute-start(bf16[256,768]{1,0:T(8,128)(2,1)} %get-tuple-element.24), channel_id=1, source_target_pairs={{0,6}} | collective-permute-start | bytes 1179656 | tf_op jit(solution)/shard_map/ppermute | solution.py:286
  22.4 2.0 %collective-permute-start.7 = (bf16[256,768]{1,0:T(8,128)(2,1)}, bf16[256,768]{1,0:T(8,128)(2,1)}, u32[]{:S(2)}, u32[]{:S(2)}) collective-permute-start(bf16[256,768]{1,0:T(8,128)(2,1)} %get-tuple-element.25), channel_id=1, source_target_pairs={{0,2}} | collective-permute-start | bytes 1179656 | tf_op jit(solution)/shard_map/ppermute | solution.py:286
  24.5 0.7 fusion.5.bias_ref
  25.2 28.0 %collective-permute-done = bf16[256,768]{1,0:T(8,128)(2,1)} collective-permute-done((bf16[256,768]{1,0:T(8,128)(2,1)}, bf16[256,768]{1,0:T(8,128)(2,1)}, u32[]{:S(2)}, u32[]{:S(2)}) %collective-permute-start) | collective-permute-done | bytes 393248 | tf_op jit(solution)/shard_map/ppermute | solution.py:286
  53.2 4.2 %collective-permute-done.1 = bf16[256,768]{1,0:T(8,128)(2,1)} collective-permute-done((bf16[256,768]{1,0:T(8,128)(2,1)}, bf16[256,768]{1,0:T(8,128)(2,1)}, u32[]{:S(2)}, u32[]{:S(2)}) %collective-permute-start.1) | collective-permute-done | bytes 393248 | tf_op jit(solution)/shard_map/ppermute | solution.py:286
  57.4 1.4 fusion
  58.9 0.1 collective-permute-start.16
  58.9 0.1 collective-permute-start.15
  59.0 4.3 %collective-permute-start.14 = (bf16[128,384]{1,0:T(8,128)(2,1)S(1)}, bf16[128,384]{1,0:T(8,128)(2,1)S(1)}, u32[]{:S(2)}, u32[]{:S(2)}) collective-permute-start(bf16[128,384]{1,0:T(8,128)(2,1)S(1)} %copy-done.6), channel_id=1, source_target_pairs={{0,8},{4,12},{8,0},{12,4},{16,24},{20,28},{24,16},{28,20},{1,9},{5... | collective-permute-start | bytes 294920 | tf_op jit(solution)/shard_map/ppermute | solution.py:270
  63.3 1.0 slice_bitcast_fusion
  64.4 1.5 collective-permute-done.7
  65.8 1.3 fusion.2
  67.2 1.3 collective-permute-start.3
  68.5 1.3 collective-permute-start.8
  70.1 1.3 collective-permute-start.4
  71.5 1.3 collective-permute-start.9
  72.8 3.9 %collective-permute-done.4 = bf16[256,384]{1,0:T(8,128)(2,1)S(1)} collective-permute-done((bf16[256,384]{1,0:T(8,128)(2,1)S(1)}, bf16[256,384]{1,0:T(8,128)(2,1)S(1)}, u32[]{:S(2)}, u32[]{:S(2)}) %collective-permute-start.4) | collective-permute-done | bytes 196640 | tf_op jit(solution)/shard_map/ppermute | solution.py:306
  76.7 1.3 collective-permute-start.5
  78.1 2.8 %collective-permute-done.9 = bf16[256,384]{1,0:T(8,128)(2,1)S(1)} collective-permute-done((bf16[256,384]{1,0:T(8,128)(2,1)S(1)}, bf16[256,384]{1,0:T(8,128)(2,1)S(1)}, u32[]{:S(2)}, u32[]{:S(2)}) %collective-permute-start.9) | collective-permute-done | bytes 196640 | tf_op jit(solution)/shard_map/ppermute | solution.py:306
  80.9 1.3 collective-permute-start.10
  82.4 2.8 %collective-permute-done.5 = bf16[256,384]{1,0:T(8,128)(2,1)S(1)} collective-permute-done((bf16[256,384]{1,0:T(8,128)(2,1)S(1)}, bf16[256,384]{1,0:T(8,128)(2,1)S(1)}, u32[]{:S(2)}, u32[]{:S(2)}) %collective-permute-start.5) | collective-permute-done | bytes 196640 | tf_op jit(solution)/shard_map/ppermute | solution.py:306
  85.1 3.4 %collective-permute-done.10 = bf16[256,384]{1,0:T(8,128)(2,1)S(1)} collective-permute-done((bf16[256,384]{1,0:T(8,128)(2,1)S(1)}, bf16[256,384]{1,0:T(8,128)(2,1)S(1)}, u32[]{:S(2)}, u32[]{:S(2)}) %collective-permute-start.10) | collective-permute-done | bytes 196640 | tf_op jit(solution)/shard_map/ppermute | solution.py:306
  88.6 2.5 %collective-permute-start.13 = (bf16[2,256,384]{2,1,0:T(8,128)(2,1)S(1)}, bf16[2,256,384]{2,1,0:T(8,128)(2,1)}, u32[]{:S(2)}, u32[]{:S(2)}) collective-permute-start(bf16[2,256,384]{2,1,0:T(8,128)(2,1)S(1)} %pad_maximum_fusion.near_ref), channel_id=1, source_target_pairs={{0,2},{1,3},{2,0},{3,1},{4,6},{5,7},{6,4},{7,5},{8,10},{9,11},{10,... | collective-permute-start | bytes 1179656 | tf_op jit(solution)/shard_map/ppermute | solution.py:270
  91.2 1.6 %copy-done = bf16[4,2,512,384]{3,2,1,0:T(8,128)(2,1)} copy-done((bf16[4,2,512,384]{3,2,1,0:T(8,128)(2,1)}, bf16[4,2,512,384]{3,2,1,0:T(8,128)(2,1)S(1)}, u32[]{:S(2)}) %copy-start) | copy-done | bytes 3145752
  92.8 10.3 %suffix_attend.2.rest_0_ = f32[8,136,384]{2,1,0:T(8,128)} custom-call(s32[1]{0:T(128)} %bitcast.9.at_ref, bf16[8,128,384]{2,1,0:T(8,128)(2,1)} %copy-done.9, bf16[4,2,512,384]{3,2,1,0:T(8,128)(2,1)} %copy-done, bf16[2,128,384]{2,1,0:T(8,128)(2,1)} %sk_ref.3, f32[32,512]{1,0:T(8,128)} %fusion.5.bias_ref), custom_call_target="tpu_custom_call" | custom-call | flops 4563402752 | bytes 5242880 | tf_op jit(solution)/shard_map/suffix_attend/pallas_call | solution.py:144
  103.1 0.6 collective-permute-start.19
  103.7 0.1 collective-permute-start.18
  103.7 6.1 %suffix_attend.3 = f32[8,136,384]{2,1,0:T(8,128)} custom-call(s32[1]{0:T(128)} %bitcast.9.at_ref, bf16[8,128,384]{2,1,0:T(8,128)(2,1)} %copy-done.9, bf16[4,2,512,384]{3,2,1,0:T(8,128)(2,1)} %copy-done, bf16[2,128,384]{2,1,0:T(8,128)(2,1)} %sk_ref.3, f32[32,512]{1,0:T(8,128)} %fusion.5.bias_ref, ...), custom_call_target="tpu_custom_call", output_to_operand_aliasing={{}: (5, {})} | custom-call | flops 2281701376 | bytes 2621440 | tf_op jit(solution)/shard_map/suffix_attend/pallas_call | solution.py:144
  109.8 2.7 %convert_element_type.9 = f16[8,136,384]{2,1,0:T(8,128)(2,1)} convert(f32[8,136,384]{2,1,0:T(8,128)} %suffix_attend.3) | non-fusion elementwise | flops 417792 | bytes 2506752 | tf_op jit(solution)/shard_map/convert_element_type | solution.py:335
  112.6 5.2 %all-to-all-start.1 = ((f16[8,136,384]{2,1,0:T(8,128)(2,1)}), f16[8,136,384]{2,1,0:T(8,128)(2,1)S(1)}, u32[]{:S(2)}, u32[]{:S(2)}) async-start(f16[8,136,384]{2,1,0:T(8,128)(2,1)} %convert_element_type.9), calls=%async_computation.1 | async-start | bytes 1671168 | tf_op jit(solution)/shard_map/all_to_all | solution.py:337
  117.8 0.1 collective-permute-start.20
  117.9 0.6 add_add_fusion.1.at_ref
  118.5 10.7 %collective-permute-done.20.far_ref = bf16[2,256,384]{2,1,0:T(8,128)(2,1)S(1)} collective-permute-done((bf16[2,256,384]{2,1,0:T(8,128)(2,1)}, bf16[2,256,384]{2,1,0:T(8,128)(2,1)S(1)}, u32[]{:S(2)}, u32[]{:S(2)}) %collective-permute-start.20) | collective-permute-done | bytes 393248 | tf_op jit(solution)/shard_map/ppermute | solution.py:270
  129.2 5.3 %context_attend.4.rest_0_ = bf16[512,1536]{1,0:T(8,128)(2,1)} custom-call(s32[3]{0:T(128)} %add_add_fusion.1.at_ref, s32[32]{0:T(128)} %len_ref.7, bf16[512,1536]{1,0:T(8,128)(2,1)} %q_ref.7, bf16[2,512,1536]{2,1,0:T(8,128)(2,1)} %kv_ref.9, f32[32,512]{1,0:T(8,128)} %fusion.5.bias_ref, bf16[2,256,384]{2,1,0:T(8,128)(2,1)} %copy-done.1, ...), custom_call_target="tpu_custom_call" | custom-call | flops 805306368 | bytes 2359296 | tf_op jit(solution)/shard_map/context_attend/pallas_call | solution.py:241
  134.5 0.7 add_add_fusion.2.at_ref
  135.2 0.6 add_add_fusion.3.at_ref
  135.8 0.6 add_add_fusion.at_ref
  136.4 5.3 %context_attend.5.rest_0_ = bf16[512,1536]{1,0:T(8,128)(2,1)} custom-call(s32[3]{0:T(128)} %add_add_fusion.3.at_ref, s32[32]{0:T(128)} %len_ref.7, bf16[512,1536]{1,0:T(8,128)(2,1)} %q_ref.7, bf16[2,512,1536]{2,1,0:T(8,128)(2,1)} %kv_ref.9, f32[32,512]{1,0:T(8,128)} %fusion.5.bias_ref, ...), custom_call_target="tpu_custom_call", output_to_operand_aliasing={{}: (7, {})} | custom-call | flops 805306368 | bytes 2359296 | tf_op jit(solution)/shard_map/context_attend/pallas_call | solution.py:241
  141.7 5.3 %context_attend.6.rest_0_ = bf16[512,1536]{1,0:T(8,128)(2,1)} custom-call(s32[3]{0:T(128)} %add_add_fusion.2.at_ref, s32[32]{0:T(128)} %len_ref.7, bf16[512,1536]{1,0:T(8,128)(2,1)} %q_ref.7, bf16[2,512,1536]{2,1,0:T(8,128)(2,1)} %kv_ref.9, f32[32,512]{1,0:T(8,128)} %fusion.5.bias_ref, ...), custom_call_target="tpu_custom_call", output_to_operand_aliasing={{}: (7, {})} | custom-call | flops 805306368 | bytes 2359296 | tf_op jit(solution)/shard_map/context_attend/pallas_call | solution.py:241
  147.0 0.7 copy-done.5
  147.8 5.3 %context_attend.7 = bf16[512,1536]{1,0:T(8,128)(2,1)} custom-call(s32[3]{0:T(128)} %add_add_fusion.at_ref, s32[32]{0:T(128)} %len_ref.7, bf16[512,1536]{1,0:T(8,128)(2,1)} %q_ref.7, bf16[2,512,1536]{2,1,0:T(8,128)(2,1)} %kv_ref.9, f32[32,512]{1,0:T(8,128)} %fusion.5.bias_ref, bf16[2,256,384]{2,1,0:T(8,128)(2,1)} %copy-done.2, ...), custom_call_target="tpu_custom_call", output_to_operand_aliasing={{}: (7, {})} | custom-call | flops 805306368 | bytes 2359296 | tf_op jit(solution)/shard_map/context_attend/pallas_call | solution.py:241
  153.1 1.3 convert_element_type.10.in_ref
  154.4 3.5 %combine_groups.1 = bf16[128,384]{1,0:T(8,128)(2,1)} custom-call(f32[8,136,384]{2,1,0:T(8,128)} %convert_element_type.10.in_ref), custom_call_target="tpu_custom_call" | custom-call | flops 835584 | bytes 1671168 | tf_op jit(solution)/shard_map/combine_groups/pallas_call | solution.py:185
  (55 shorter events, 0.7 us)
Async XLA Ops:
  4.5 52.9 %collective-permute-start.2 = (bf16[2,256,768]{2,1,0:T(8,128)(2,1)}, bf16[2,256,768]{2,1,0:T(8,128)(2,1)}, u32[]{:S(2)}, u32[]{:S(2)}) collective-permute-start(bf16[2,256,768]{2,1,0:T(8,128)(2,1)} %get-tuple-element.23), channel_id=1, source_target_pairs={{0,4}} | collective-permute-start | bytes 2359304 | tf_op jit(solution)/shard_map/ppermute | solution.py:286
  10.3 14.1 %copy-start.7 = (s32[16384]{0:T(1024)S(1)}, s32[16384]{0:T(1024)}, u32[]{:S(2)}) copy-start(s32[16384]{0:T(1024)} %param.8) | copy-start | bytes 196612
  10.3 14.2 %copy-start.8 = (s32[32]{0:T(128)S(1)}, s32[32]{0:T(128)}, u32[]{:S(2)}) copy-start(s32[32]{0:T(128)} %len_ref.7) | copy-start | bytes 388
  10.3 80.9 %all-to-all-start = ((bf16[4,2,512,384]{3,2,1,0:T(8,128)(2,1)}), bf16[4,2,512,384]{3,2,1,0:T(8,128)(2,1)S(1)}, u32[]{:S(2)}, u32[]{:S(2)}) async-start(bf16[4,2,512,384]{3,2,1,0:T(8,128)(2,1)} %get-tuple-element.28), calls=%async_computation | async-start | bytes 6291456 | tf_op jit(solution)/shard_map/all_to_all | solution.py:317
  14.1 44.7 %copy-start.6 = (bf16[128,384]{1,0:T(8,128)(2,1)S(1)}, bf16[128,384]{1,0:T(8,128)(2,1)}, u32[]{:S(2)}) copy-start(bf16[128,384]{1,0:T(8,128)(2,1)} %param.10) | copy-start | bytes 294916
  14.1 39.1 %collective-permute-start = (bf16[256,768]{1,0:T(8,128)(2,1)}, bf16[256,768]{1,0:T(8,128)(2,1)}, u32[]{:S(2)}, u32[]{:S(2)}) collective-permute-start(bf16[256,768]{1,0:T(8,128)(2,1)} %get-tuple-element.21), channel_id=1, source_target_pairs={{0,6}} | collective-permute-start | bytes 1179656 | tf_op jit(solution)/shard_map/ppermute | solution.py:286
  16.9 40.5 %collective-permute-start.1 = (bf16[256,768]{1,0:T(8,128)(2,1)}, bf16[256,768]{1,0:T(8,128)(2,1)}, u32[]{:S(2)}, u32[]{:S(2)}) collective-permute-start(bf16[256,768]{1,0:T(8,128)(2,1)} %get-tuple-element.22), channel_id=1, source_target_pairs={{0,2}} | collective-permute-start | bytes 1179656 | tf_op jit(solution)/shard_map/ppermute | solution.py:286
  20.3 44.0 %collective-permute-start.6 = (bf16[256,768]{1,0:T(8,128)(2,1)}, bf16[256,768]{1,0:T(8,128)(2,1)}, u32[]{:S(2)}, u32[]{:S(2)}) collective-permute-start(bf16[256,768]{1,0:T(8,128)(2,1)} %get-tuple-element.24), channel_id=1, source_target_pairs={{0,6}} | collective-permute-start | bytes 1179656 | tf_op jit(solution)/shard_map/ppermute | solution.py:286
  22.4 43.5 %collective-permute-start.7 = (bf16[256,768]{1,0:T(8,128)(2,1)}, bf16[256,768]{1,0:T(8,128)(2,1)}, u32[]{:S(2)}, u32[]{:S(2)}) collective-permute-start(bf16[256,768]{1,0:T(8,128)(2,1)} %get-tuple-element.25), channel_id=1, source_target_pairs={{0,2}} | collective-permute-start | bytes 1179656 | tf_op jit(solution)/shard_map/ppermute | solution.py:286
  58.9 11.0 %collective-permute-start.16 = (bf16[128,384]{1,0:T(8,128)(2,1)S(1)}, bf16[128,384]{1,0:T(8,128)(2,1)S(1)}, u32[]{:S(2)}, u32[]{:S(2)}) collective-permute-start(bf16[128,384]{1,0:T(8,128)(2,1)S(1)} %copy-done.6), channel_id=1, source_target_pairs={{0,24},{4,28},{8,16},{12,20},{16,8},{20,12},{24,0},{28,4},{1,25},{... | collective-permute-start | bytes 294920 | tf_op jit(solution)/shard_map/ppermute | solution.py:270
  58.9 10.9 %collective-permute-start.15 = (bf16[128,384]{1,0:T(8,128)(2,1)S(1)}, bf16[128,384]{1,0:T(8,128)(2,1)S(1)}, u32[]{:S(2)}, u32[]{:S(2)}) collective-permute-start(bf16[128,384]{1,0:T(8,128)(2,1)S(1)} %copy-done.6), channel_id=1, source_target_pairs={{0,16},{4,20},{8,24},{12,28},{16,0},{20,4},{24,8},{28,12},{1,17},{... | collective-permute-start | bytes 294920 | tf_op jit(solution)/shard_map/ppermute | solution.py:270
  59.0 10.9 %collective-permute-start.14 = (bf16[128,384]{1,0:T(8,128)(2,1)S(1)}, bf16[128,384]{1,0:T(8,128)(2,1)S(1)}, u32[]{:S(2)}, u32[]{:S(2)}) collective-permute-start(bf16[128,384]{1,0:T(8,128)(2,1)S(1)} %copy-done.6), channel_id=1, source_target_pairs={{0,8},{4,12},{8,0},{12,4},{16,24},{20,28},{24,16},{28,20},{1,9},{5... | collective-permute-start | bytes 294920 | tf_op jit(solution)/shard_map/ppermute | solution.py:270
  67.2 2.9 %collective-permute-start.3 = (bf16[256,384]{1,0:T(8,128)(2,1)S(1)}, bf16[256,384]{1,0:T(8,128)(2,1)S(1)}, u32[]{:S(2)}, u32[]{:S(2)}) collective-permute-start(bf16[256,384]{1,0:T(8,128)(2,1)S(1)} %slice.34), channel_id=1, source_target_pairs={{0,1},{2,3},{4,5},{6,7},{8,9},{10,11},{12,13},{14,15},{16,17},{18,... | collective-permute-start | bytes 589832 | tf_op jit(solution)/shard_map/ppermute | solution.py:302
  68.5 2.9 %collective-permute-start.8 = (bf16[256,384]{1,0:T(8,128)(2,1)S(1)}, bf16[256,384]{1,0:T(8,128)(2,1)S(1)}, u32[]{:S(2)}, u32[]{:S(2)}) collective-permute-start(bf16[256,384]{1,0:T(8,128)(2,1)S(1)} %slice.37), channel_id=1, source_target_pairs={{0,1},{2,3},{4,5},{6,7},{8,9},{10,11},{12,13},{14,15},{16,17},{18,... | collective-permute-start | bytes 589832 | tf_op jit(solution)/shard_map/ppermute | solution.py:302
  70.0 12.3 %collective-permute-start.17 = (bf16[4,128,384]{2,1,0:T(8,128)(2,1)S(1)}, bf16[4,128,384]{2,1,0:T(8,128)(2,1)S(1)}, u32[]{:S(2)}, u32[]{:S(2)}) collective-permute-start(bf16[4,128,384]{2,1,0:T(8,128)(2,1)S(1)} %pad_maximum_fusion.1), channel_id=1, source_target_pairs={{0,4},{4,0},{8,12},{12,8},{16,20},{20,16},{24,28},{28,24},{1,5},{5... | collective-permute-start | bytes 1179656 | tf_op jit(solution)/shard_map/ppermute | solution.py:270
  70.1 6.5 %collective-permute-start.4 = (bf16[256,384]{1,0:T(8,128)(2,1)S(1)}, bf16[256,384]{1,0:T(8,128)(2,1)S(1)}, u32[]{:S(2)}, u32[]{:S(2)}) collective-permute-start(bf16[256,384]{1,0:T(8,128)(2,1)S(1)} %slice_add_fusion.1), channel_id=1, source_target_pairs={{0,16},{4,20},{1,17},{5,21},{2,18},{6,22},{3,19},{7,23}} | collective-permute-start | bytes 589832 | tf_op jit(solution)/shard_map/ppermute | solution.py:306
  71.5 9.4 %collective-permute-start.9 = (bf16[256,384]{1,0:T(8,128)(2,1)S(1)}, bf16[256,384]{1,0:T(8,128)(2,1)S(1)}, u32[]{:S(2)}, u32[]{:S(2)}) collective-permute-start(bf16[256,384]{1,0:T(8,128)(2,1)S(1)} %slice_add_fusion), channel_id=1, source_target_pairs={{0,16},{4,20},{1,17},{5,21},{2,18},{6,22},{3,19},{7,23}} | collective-permute-start | bytes 589832 | tf_op jit(solution)/shard_map/ppermute | solution.py:306
  76.7 8.4 %collective-permute-start.5 = (bf16[256,384]{1,0:T(8,128)(2,1)S(1)}, bf16[256,384]{1,0:T(8,128)(2,1)S(1)}, u32[]{:S(2)}, u32[]{:S(2)}) collective-permute-start(bf16[256,384]{1,0:T(8,128)(2,1)S(1)} %add.55), channel_id=1, source_target_pairs={{0,8},{4,12},{16,24},{20,28},{1,9},{5,13},{17,25},{21,29},{2,10},{... | collective-permute-start | bytes 589832 | tf_op jit(solution)/shard_map/ppermute | solution.py:306
  80.9 7.6 %collective-permute-start.10 = (bf16[256,384]{1,0:T(8,128)(2,1)S(1)}, bf16[256,384]{1,0:T(8,128)(2,1)S(1)}, u32[]{:S(2)}, u32[]{:S(2)}) collective-permute-start(bf16[256,384]{1,0:T(8,128)(2,1)S(1)} %add.61), channel_id=1, source_target_pairs={{0,8},{4,12},{16,24},{20,28},{1,9},{5,13},{17,25},{21,29},{2,10},{... | collective-permute-start | bytes 589832 | tf_op jit(solution)/shard_map/ppermute | solution.py:306
  82.3 8.8 %copy-start.9 = (bf16[8,128,384]{2,1,0:T(8,128)(2,1)}, bf16[8,128,384]{2,1,0:T(8,128)(2,1)S(1)}, u32[]{:S(2)}) copy-start(bf16[8,128,384]{2,1,0:T(8,128)(2,1)S(1)} %constant_dynamic-update-slice_fusion.q_ref) | copy-start | bytes 2359300
  88.6 14.5 %copy-start.1 = (bf16[2,256,384]{2,1,0:T(8,128)(2,1)}, bf16[2,256,384]{2,1,0:T(8,128)(2,1)S(1)}, u32[]{:S(2)}) copy-start(bf16[2,256,384]{2,1,0:T(8,128)(2,1)S(1)} %pad_maximum_fusion.near_ref) | copy-start | bytes 1179652
  88.6 14.5 %collective-permute-start.13 = (bf16[2,256,384]{2,1,0:T(8,128)(2,1)S(1)}, bf16[2,256,384]{2,1,0:T(8,128)(2,1)}, u32[]{:S(2)}, u32[]{:S(2)}) collective-permute-start(bf16[2,256,384]{2,1,0:T(8,128)(2,1)S(1)} %pad_maximum_fusion.near_ref), channel_id=1, source_target_pairs={{0,2},{1,3},{2,0},{3,1},{4,6},{5,7},{6,4},{7,5},{8,10},{9,11},{10,... | collective-permute-start | bytes 1179656 | tf_op jit(solution)/shard_map/ppermute | solution.py:270
  91.2 11.9 %collective-permute-start.12 = (bf16[2,256,384]{2,1,0:T(8,128)(2,1)S(1)}, bf16[2,256,384]{2,1,0:T(8,128)(2,1)}, u32[]{:S(2)}, u32[]{:S(2)}) collective-permute-start(bf16[2,256,384]{2,1,0:T(8,128)(2,1)S(1)} %pad_maximum_fusion.near_ref), channel_id=1, source_target_pairs={{0,4},{4,0},{8,12},{12,8},{16,20},{20,16},{24,28},{28,24},{1,5},{5... | collective-permute-start | bytes 1179656 | tf_op jit(solution)/shard_map/ppermute | solution.py:270
  91.2 18.7 %collective-permute-start.11 = (bf16[2,256,384]{2,1,0:T(8,128)(2,1)S(1)}, bf16[2,256,384]{2,1,0:T(8,128)(2,1)}, u32[]{:S(2)}, u32[]{:S(2)}) collective-permute-start(bf16[2,256,384]{2,1,0:T(8,128)(2,1)S(1)} %pad_maximum_fusion.near_ref), channel_id=1, source_target_pairs={{0,1},{1,0},{2,3},{3,2},{4,5},{5,4},{6,7},{7,6},{8,9},{9,8},{10,11... | collective-permute-start | bytes 1179656 | tf_op jit(solution)/shard_map/ppermute | solution.py:270
  91.2 1.6 %copy-start = (bf16[4,2,512,384]{3,2,1,0:T(8,128)(2,1)}, bf16[4,2,512,384]{3,2,1,0:T(8,128)(2,1)S(1)}, u32[]{:S(2)}) copy-start(bf16[4,2,512,384]{3,2,1,0:T(8,128)(2,1)S(1)} %all-to-all-done.kv_ref) | copy-start | bytes 9437188
  103.1 6.7 %collective-permute-start.19 = (bf16[2,256,384]{2,1,0:T(8,128)(2,1)}, bf16[2,256,384]{2,1,0:T(8,128)(2,1)S(1)}, u32[]{:S(2)}, u32[]{:S(2)}) collective-permute-start(bf16[2,256,384]{2,1,0:T(8,128)(2,1)} %collective-permute-done.13.near_ref), channel_id=1, source_target_pairs={{0,1},{1,0},{2,3},{3,2},{4,5},{5,4},{6,7},{7,6},{8,9},{9,8},{10,11... | collective-permute-start | bytes 1179656 | tf_op jit(solution)/shard_map/ppermute | solution.py:270
  103.7 6.2 %collective-permute-start.18 = (bf16[2,256,384]{2,1,0:T(8,128)(2,1)}, bf16[2,256,384]{2,1,0:T(8,128)(2,1)S(1)}, u32[]{:S(2)}, u32[]{:S(2)}) collective-permute-start(bf16[2,256,384]{2,1,0:T(8,128)(2,1)} %collective-permute-done.12.far_ref), channel_id=1, source_target_pairs={{0,1},{1,0},{2,3},{3,2},{4,5},{5,4},{6,7},{7,6},{8,9},{9,8},{10,11... | collective-permute-start | bytes 1179656 | tf_op jit(solution)/shard_map/ppermute | solution.py:270
  109.8 2.8 %copy-start.2 = (bf16[2,256,384]{2,1,0:T(8,128)(2,1)}, bf16[2,256,384]{2,1,0:T(8,128)(2,1)S(1)}, u32[]{:S(2)}) copy-start(bf16[2,256,384]{2,1,0:T(8,128)(2,1)S(1)} %collective-permute-done.19.near_ref) | copy-start | bytes 1179652
  109.8 2.7 %copy-start.3 = (bf16[2,256,384]{2,1,0:T(8,128)(2,1)}, bf16[2,256,384]{2,1,0:T(8,128)(2,1)S(1)}, u32[]{:S(2)}) copy-start(bf16[2,256,384]{2,1,0:T(8,128)(2,1)S(1)} %collective-permute-done.18.far_ref) | copy-start | bytes 1179652
  112.6 40.5 %all-to-all-start.1 = ((f16[8,136,384]{2,1,0:T(8,128)(2,1)}), f16[8,136,384]{2,1,0:T(8,128)(2,1)S(1)}, u32[]{:S(2)}, u32[]{:S(2)}) async-start(f16[8,136,384]{2,1,0:T(8,128)(2,1)} %convert_element_type.9), calls=%async_computation.1 | async-start | bytes 1671168 | tf_op jit(solution)/shard_map/all_to_all | solution.py:337
  117.8 11.4 %collective-permute-start.20 = (bf16[2,256,384]{2,1,0:T(8,128)(2,1)}, bf16[2,256,384]{2,1,0:T(8,128)(2,1)S(1)}, u32[]{:S(2)}, u32[]{:S(2)}) collective-permute-start(bf16[2,256,384]{2,1,0:T(8,128)(2,1)} %collective-permute-done.12.far_ref), channel_id=1, source_target_pairs={{0,2},{1,3},{2,0},{3,1},{4,6},{5,7},{6,4},{7,5},{8,10},{9,11},{10,... | collective-permute-start | bytes 1179656 | tf_op jit(solution)/shard_map/ppermute | solution.py:270
  129.2 5.3 %copy-start.4 = (bf16[2,256,384]{2,1,0:T(8,128)(2,1)}, bf16[2,256,384]{2,1,0:T(8,128)(2,1)S(1)}, u32[]{:S(2)}) copy-start(bf16[2,256,384]{2,1,0:T(8,128)(2,1)S(1)} %collective-permute-done.20.far_ref) | copy-start | bytes 1179652
  134.5 12.5 %collective-permute-start.21 = (bf16[2,256,384]{2,1,0:T(8,128)(2,1)S(1)}, bf16[2,256,384]{2,1,0:T(8,128)(2,1)S(1)}, u32[]{:S(2)}, u32[]{:S(2)}) collective-permute-start(bf16[2,256,384]{2,1,0:T(8,128)(2,1)S(1)} %collective-permute-done.20.far_ref), channel_id=1, source_target_pairs={{0,1},{1,0},{2,3},{3,2},{4,5},{5,4},{6,7},{7,6},{8,9},{9,8},{10,11... | collective-permute-start | bytes 1179656 | tf_op jit(solution)/shard_map/ppermute | solution.py:270
  147.0 0.7 copy-start.5

commit v9 on v8

--- a/solution.py
+++ b/solution.py
@@ -92,18 +92,19 @@
         finish(task, scores)
 
 
-def suffix_kernel(at_ref, q_ref, kv_ref, sk_ref, bias_ref, *rest):
-    out_ref = rest[-1]
+def suffix_kernel(at_ref, near_ref, far_ref, kv_ref, sk_ref, bias_ref, out_ref):
     host = at_ref[0]
     groups = kv_ref.shape[0]
-    hosts, share, _ = q_ref.shape
+    half, share, _ = near_ref.shape
+    hosts = 2 * half
+    chunk = lambda n: near_ref[n] if n < half else far_ref[n - half]
     apart = list(range(0, hosts, 2)) + list(range(1, hosts, 2))
     chunks = min(hosts, max(1, TILE // share))
     bias = [bias_ref[pl.ds(host * groups + g, 1), :] for g in range(groups)]
     values = [kv_ref[g, 1] for g in range(groups)] + [sk_ref[1]]
 
     def score(first):
-        q = jnp.concatenate([q_ref[first + c] for c in range(chunks)], axis=0)
+        q = jnp.concatenate([chunk(first + c) for c in range(chunks)], axis=0)
         s = dot_t(q, sk_ref[0])
         row = lax.broadcasted_iota(jnp.int32, (share, share), 0)
         spos = host * share + lax.broadcasted_iota(jnp.int32, (share, share), 1)
@@ -136,35 +137,35 @@
     pipelined(list(range(0, hosts, chunks)), score, finish)
 
 
-def suffix_attend(host, q, kv, sk, bias, first, count, before):
-    hosts, share, width = q.shape
+def suffix_attend(host, near, far, kv, sk, bias):
+    half, share, width = near.shape
+    hosts, heads = 2 * half, width // HSZ
     groups, _, rows, _ = kv.shape
     seen = groups * rows + share
-    more = [] if before is None else [before]
+    column = lambda h, at: (0, 0, h)
     return pl.pallas_call(
         suffix_kernel,
         grid_spec=pltpu.PrefetchScalarGridSpec(
             num_scalar_prefetch=1,
-            grid=(count,),
+            grid=(heads,),
             in_specs=[
-                pl.BlockSpec((hosts, share, HSZ), lambda i, at: (0, 0, first + i)),
-                pl.BlockSpec((groups, 2, rows, HSZ), lambda i, at: (0, 0, 0, first + i)),
-                pl.BlockSpec((2, share, HSZ), lambda i, at: (0, 0, first + i)),
-                pl.BlockSpec(bias.shape, lambda i, at: (0, 0)),
-            ]
-            + [pl.BlockSpec(memory_space=pl.ANY) for _ in more],
-            out_specs=pl.BlockSpec((hosts, share + EXTRA, HSZ), lambda i, at: (0, 0, first + i)),
+                pl.BlockSpec((half, share, HSZ), column),
+                pl.BlockSpec((half, share, HSZ), column),
+                pl.BlockSpec((groups, 2, rows, HSZ), lambda h, at: (0, 0, 0, h)),
+                pl.BlockSpec((2, share, HSZ), column),
+                pl.BlockSpec(bias.shape, lambda h, at: (0, 0)),
+            ],
+            out_specs=pl.BlockSpec((hosts, share + EXTRA, HSZ), column),
         ),
         out_shape=jax.ShapeDtypeStruct((hosts, share + EXTRA, width), jnp.float32),
-        input_output_aliases={5: 0} if more else {},
-        compiler_params=pltpu.CompilerParams(vmem_limit_bytes=60 * 1024 * 1024),
+        compiler_params=pltpu.CompilerParams(vmem_limit_bytes=24 * 1024 * 1024),
         cost_estimate=pl.CostEstimate(
-            flops=8 * count * hosts * share * seen * HSZ,
-            bytes_accessed=4 * count * (groups * rows + 3 * hosts * share) * HSZ,
-            transcendentals=count * hosts * share * seen,
+            flops=8 * hosts * share * seen * width,
+            bytes_accessed=4 * (groups * rows + 3 * hosts * share) * width,
+            transcendentals=heads * hosts * share * seen,
         ),
         name="suffix_attend",
-    )(host, q, kv, sk, bias, *more)
+    )(host, near, far, kv, sk, bias)
 
 
 def combine_kernel(in_ref, out_ref):
@@ -256,7 +257,7 @@
         ),
         out_shape=jax.ShapeDtypeStruct((rows, width), q.dtype),
         input_output_aliases={7: 0} if more else {},
-        compiler_params=pltpu.CompilerParams(vmem_limit_bytes=60 * 1024 * 1024),
+        compiler_params=pltpu.CompilerParams(vmem_limit_bytes=24 * 1024 * 1024),
         cost_estimate=pl.CostEstimate(
             flops=8 * rows * rows * wide,
             bytes_accessed=12 * rows * wide,
@@ -272,8 +273,7 @@
 
 def gather_hosts(x, hosts):
     near = jnp.stack([x] + [swap(x, "hst", k) for k in range(2, hosts, 2)], axis=0)
-    far = swap(near, "hst", 1)
-    return jnp.concatenate([near, far], axis=0)
+    return near, swap(near, "hst", 1)
 
 
 def after(x, done):
@@ -312,36 +312,29 @@
     hosts, groups = lax.axis_size("hst"), lax.axis_size("grp")
     host, group = lax.axis_index("hst"), lax.axis_index("grp")
     rows = queries.shape[0]
-    heads = suffix_queries.shape[1] // HSZ
+    cores = groups // 2
     packed, below, across, diagonal = pack(keys_values, groups)
+    slabs = scatter_anchor(keys_values, across, diagonal, below, groups)
+    packed, suffix_queries = after((packed, suffix_queries), slabs[0])
     swapped = lax.all_to_all(packed, "grp", split_axis=0, concat_axis=0, tiled=True)
-    slabs = scatter_anchor(keys_values, across, diagonal, below, groups)
     near = jnp.stack([spread_anchor(x, hosts, groups) for x in slabs])
-    suffix_queries = after(suffix_queries, slabs[0])
     gathered = gather_hosts(suffix_queries, hosts)
     seen = (token_ids.reshape(-1, rows) >= NAMB) & (jnp.arange(rows)[None, :] < lengths[:, None])
     bias = jnp.where(seen, 0.0, NEG).astype(jnp.float32)
-    cores = groups // 2
-    suffix = functools.partial(suffix_attend, jnp.stack([host]), gathered, swapped, suffix_kv, bias)
-    early = max(1, heads - 1)
-    parts = suffix(0, early, None)
-    far, other_near, parts = lax.optimization_barrier((swap(near, "hst", 1), swap(near, "grp", cores), parts))
+    far, other_near, gathered = lax.optimization_barrier((swap(near, "hst", 1), swap(near, "grp", cores), gathered))
     other_far = swap(far, "grp", cores)
-    held = {0: [near, far], cores: [other_near, other_far]}
     by_core = [[swap(x, "grp", k) for x in (near, far, other_near)] for k in range(1, cores)]
-    if heads > early:
-        parts = suffix(early, heads - early, parts)
-    by_core, parts = lax.optimization_barrier((by_core, parts))
+    parts = suffix_attend(jnp.stack([host]), *gathered, swapped, suffix_kv, bias)
+    other_far, by_core, parts = lax.optimization_barrier((other_far, by_core, parts))
     parts = parts.astype(jnp.float16)
-    held[0], other_far = after((held[0], other_far), parts)
     coded = lax.all_to_all(parts, "hst", split_axis=0, concat_axis=0, tiled=True)
+    held = {0: after([near, far], parts), cores: [other_near, other_far]}
 
     def context(k, before):
         at = jnp.stack([host * groups + group, group ^ k, host % 2])
         return context_attend(at, lengths, queries, keys_values, bias, *held[k], before)
 
     context_out = context(0, None)
-    other_far = after(other_far, context_out)
     for k in range(1, cores):
         held[k] = by_core[k - 1][:2]
         held[cores ^ k] = [by_core[k - 1][2], swap(other_far, "grp", k)]

time: 159 us -> 127 us (0.80)
  waiting for transfers between devices: 57.3 us -> 32.7 us
  Pallas kernels: 44.9 us -> 40.4 us
    ppermute x5, waiting for transfers between devices: 33.7 us -> 3.56 us  [scatter_anchor(): send = lambda x, to: lax.ppermute(x, BOTH, [(0, to)])]
    ppermute x11, waiting for transfers between devices: 10.7 us -> 18.5 us  [swap(): lax.ppermute(x, axis, [(i, i ^ k) for i in range(lax.axis_size(axis))])]
    pallas_call x2 -> x1, Pallas kernels: 16.3 us -> 13.3 us  [suffix_attend(): pl.pallas_call(suffix_kernel, grid_spec=pltpu.PrefetchScalarGridSpec(num_...]
    ppermute x4, waiting for transfers between devices: 12.8 us -> 10.2 us  [spread_anchor(): piece = piece + lax.ppermute(piece, 'hst', pairs)]
    ppermute x5, starting transfers between devices: 16 us -> 13.6 us  [scatter_anchor(): send = lambda x, to: lax.ppermute(x, BOTH, [(0, to)])]
    another operation x4, other arithmetic: 2.55 us -> 0.3 us  [context(): at = jnp.stack([host * groups + group, group ^ k, host % 2])]
    pallas_call x4, Pallas kernels: 21.2 us -> 19.3 us  [context_attend(): pl.pallas_call(context_kernel, grid_spec=pltpu.PrefetchScalarGridSpec(num...]
    another operation x1, other arithmetic: 0.06 us -> 1.89 us  [gather_hosts(): jnp.stack([x] + [swap(x, 'hst', k) for k in range(2, hosts, 2)], axis=0)]
  transfers between devices with their start and end apart: 24 -> 24, of which waited for: 8 -> 7; matrix products, arithmetic and copies ran while one was open for 5% -> 6% of each run, Pallas kernels for 24% -> 26%
where the time goes in v9:
time: 127 us; the launch traced here: 126 us
  Pallas kernels  40.4 us (32%)
  starting transfers between devices  39.2 us (31%)
  waiting for transfers between devices  32.7 us (26%)
  other arithmetic  9.29 us (7%)
  local copies, waits for them, and re-layouts  3.22 us (3%)
    pallas_call x4, Pallas kernels, context_attend(): pl.pallas_call(context_kernel, grid_spec=pltpu.PrefetchScalarGridSpec(num...  19.3 us
    ppermute x11, waiting for transfers between devices, swap(): lax.ppermute(x, axis, [(i, i ^ k) for i in range(lax.axis_size(axis))])  18.5 us
    ppermute x5, starting transfers between devices, scatter_anchor(): send = lambda x, to: lax.ppermute(x, BOTH, [(0, to)])  13.6 us
    pallas_call x1, Pallas kernels, suffix_attend(): pl.pallas_call(suffix_kernel, grid_spec=pltpu.PrefetchScalarGridSpec(num_...  13.3 us
    ppermute x4, waiting for transfers between devices, spread_anchor(): piece = piece + lax.ppermute(piece, 'hst', pairs)  10.2 us
    ppermute x11, starting transfers between devices, swap(): lax.ppermute(x, axis, [(i, i ^ k) for i in range(lax.axis_size(axis))])  7.06 us
    ppermute x4, starting transfers between devices, spread_anchor(): piece = piece + lax.ppermute(piece, 'hst', pairs)  5.82 us
    all_to_all x1, starting transfers between devices, per_device(): lax.all_to_all(packed, 'grp', split_axis=0, concat_axis=0, tiled=True)  4.65 us
  transfers between devices with their start and end apart: 24, of which 7 were waited for; matrix products, arithmetic and copies ran while one was open for 6% of the time, Pallas kernels for 26%

profile of v9, /device:TPU:0, one launch (start us, length us, event | category | flops | bytes accessed | tf_op | source)
XLA Modules:
  0.0 125.7 jit_solution(1486908535538718805)
XLA Ops:
  0.6 4.3 %pack_heads.1 = (bf16[4,2,512,384]{3,2,1,0:T(8,128)(2,1)}, bf16[2,256,768]{2,1,0:T(8,128)(2,1)}, bf16[256,768]{1,0:T(8,128)(2,1)}, bf16[256,768]{1,0:T(8,128)(2,...) custom-call(bf16[2,512,1536]{2,1,0:T(8,128)(2,1)} %kv_ref.9), custom_call_target="tpu_custom_call" | custom-call | bytes 9437184 | tf_op jit(solution)/shard_map/pack_heads/pallas_call | solution.py:66
  5.0 5.8 %collective-permute-start.2 = (bf16[2,256,768]{2,1,0:T(8,128)(2,1)}, bf16[2,256,768]{2,1,0:T(8,128)(2,1)}, u32[]{:S(2)}, u32[]{:S(2)}) collective-permute-start(bf16[2,256,768]{2,1,0:T(8,128)(2,1)} %get-tuple-element.24), channel_id=1, source_target_pairs={{0,4}} | collective-permute-start | bytes 2359304 | tf_op jit(solution)/shard_map/ppermute | solution.py:286
  10.7 1.6 %collective-permute-start = (bf16[256,768]{1,0:T(8,128)(2,1)}, bf16[256,768]{1,0:T(8,128)(2,1)S(1)}, u32[]{:S(2)}, u32[]{:S(2)}) collective-permute-start(bf16[256,768]{1,0:T(8,128)(2,1)} %get-tuple-element.22), channel_id=1, source_target_pairs={{0,6}} | collective-permute-start | bytes 1179656 | tf_op jit(solution)/shard_map/ppermute | solution.py:286
  12.3 2.1 %collective-permute-start.1 = (bf16[256,768]{1,0:T(8,128)(2,1)}, bf16[256,768]{1,0:T(8,128)(2,1)}, u32[]{:S(2)}, u32[]{:S(2)}) collective-permute-start(bf16[256,768]{1,0:T(8,128)(2,1)} %get-tuple-element.23), channel_id=1, source_target_pairs={{0,2}} | collective-permute-start | bytes 1179656 | tf_op jit(solution)/shard_map/ppermute | solution.py:286
  14.4 2.1 %collective-permute-start.6 = (bf16[256,768]{1,0:T(8,128)(2,1)}, bf16[256,768]{1,0:T(8,128)(2,1)}, u32[]{:S(2)}, u32[]{:S(2)}) collective-permute-start(bf16[256,768]{1,0:T(8,128)(2,1)} %get-tuple-element.25), channel_id=1, source_target_pairs={{0,6}} | collective-permute-start | bytes 1179656 | tf_op jit(solution)/shard_map/ppermute | solution.py:286
  16.5 2.1 %collective-permute-start.7 = (bf16[256,768]{1,0:T(8,128)(2,1)}, bf16[256,768]{1,0:T(8,128)(2,1)}, u32[]{:S(2)}, u32[]{:S(2)}) collective-permute-start(bf16[256,768]{1,0:T(8,128)(2,1)} %get-tuple-element.26), channel_id=1, source_target_pairs={{0,2}} | collective-permute-start | bytes 1179656 | tf_op jit(solution)/shard_map/ppermute | solution.py:286
  18.6 3.6 %collective-permute-done.1 = bf16[256,768]{1,0:T(8,128)(2,1)} collective-permute-done((bf16[256,768]{1,0:T(8,128)(2,1)}, bf16[256,768]{1,0:T(8,128)(2,1)}, u32[]{:S(2)}, u32[]{:S(2)}) %collective-permute-start.1) | collective-permute-done | bytes 393248 | tf_op jit(solution)/shard_map/ppermute | solution.py:286
  22.1 1.3 %fusion = bf16[256,768]{1,0:T(8,128)(2,1)S(1)} fusion(bf16[2,256,768]{2,1,0:T(8,128)(2,1)} %collective-permute-done.2, bf16[256,768]{1,0:T(8,128)(2,1)} %collective-permute-done.1, bf16[256,768]{1,0:T(8,128)(2,1)} %copy-done.5, bf16[2,512,1536]{2,1,0:T(8,128)(2,1)S(1)} %copy-done, pred[]{:T(512)S(6)} %and.18), kind=kLoop, calls=%fused_computation.2 | loop fusion | flops 786432 | bytes 1966081 | tf_op jit(solution)/shard_map/add | solution.py:292
  23.4 0.1 collective-permute-start.15
  23.5 0.1 collective-permute-start.14
  23.6 4.3 %collective-permute-start.13 = (bf16[128,384]{1,0:T(8,128)(2,1)}, bf16[128,384]{1,0:T(8,128)(2,1)}, u32[]{:S(2)}, u32[]{:S(2)}) collective-permute-start(bf16[128,384]{1,0:T(8,128)(2,1)} %param.10), channel_id=1, source_target_pairs={{0,8},{4,12},{8,0},{12,4},{16,24},{20,28},{24,16},{28,20},{1,9},{5... | collective-permute-start | bytes 294920 | tf_op jit(solution)/shard_map/ppermute | solution.py:271
  27.9 0.7 slice.34
  28.6 4.6 %all-to-all-start = ((bf16[4,2,512,384]{3,2,1,0:T(8,128)(2,1)}), bf16[4,2,512,384]{3,2,1,0:T(8,128)(2,1)}, u32[]{:S(2)}, u32[]{:S(2)}) async-start(bf16[4,2,512,384]{3,2,1,0:T(8,128)(2,1)} %get-tuple-element.34), calls=%async_computation | async-start | bytes 6291456 | tf_op jit(solution)/shard_map/all_to_all | solution.py:319
  33.2 1.0 slice_bitcast_fusion
  34.3 2.4 %collective-permute-start.3 = (bf16[256,384]{1,0:T(8,128)(2,1)}, bf16[256,384]{1,0:T(8,128)(2,1)S(1)}, u32[]{:S(2)}, u32[]{:S(2)}) collective-permute-start(bf16[256,384]{1,0:T(8,128)(2,1)} %slice.34), channel_id=1, source_target_pairs={{0,1},{2,3},{4,5},{6,7},{8,9},{10,11},{12,13},{14,15},{16,17},{18,... | collective-permute-start | bytes 589832 | tf_op jit(solution)/shard_map/ppermute | solution.py:302
  36.7 1.2 fusion.2
  37.9 1.3 %collective-permute-start.8 = (bf16[256,384]{1,0:T(8,128)(2,1)S(1)}, bf16[256,384]{1,0:T(8,128)(2,1)S(1)}, u32[]{:S(2)}, u32[]{:S(2)}) collective-permute-start(bf16[256,384]{1,0:T(8,128)(2,1)S(1)} %slice.37), channel_id=1, source_target_pairs={{0,1},{2,3},{4,5},{6,7},{8,9},{10,11},{12,13},{14,15},{16,17},{18,... | collective-permute-start | bytes 589832 | tf_op jit(solution)/shard_map/ppermute | solution.py:302
  39.2 1.9 %collective-permute-start.4 = (bf16[256,384]{1,0:T(8,128)(2,1)S(1)}, bf16[256,384]{1,0:T(8,128)(2,1)S(1)}, u32[]{:S(2)}, u32[]{:S(2)}) collective-permute-start(bf16[256,384]{1,0:T(8,128)(2,1)S(1)} %slice_add_fusion.1), channel_id=1, source_target_pairs={{0,16},{4,20},{1,17},{5,21},{2,18},{6,22},{3,19},{7,23}} | collective-permute-start | bytes 589832 | tf_op jit(solution)/shard_map/ppermute | solution.py:306
  41.2 1.3 %collective-permute-start.9 = (bf16[256,384]{1,0:T(8,128)(2,1)S(1)}, bf16[256,384]{1,0:T(8,128)(2,1)S(1)}, u32[]{:S(2)}, u32[]{:S(2)}) collective-permute-start(bf16[256,384]{1,0:T(8,128)(2,1)S(1)} %slice_add_fusion), channel_id=1, source_target_pairs={{0,16},{4,20},{1,17},{5,21},{2,18},{6,22},{3,19},{7,23}} | collective-permute-start | bytes 589832 | tf_op jit(solution)/shard_map/ppermute | solution.py:306
  42.5 4.0 %collective-permute-done.4 = bf16[256,384]{1,0:T(8,128)(2,1)S(1)} collective-permute-done((bf16[256,384]{1,0:T(8,128)(2,1)S(1)}, bf16[256,384]{1,0:T(8,128)(2,1)S(1)}, u32[]{:S(2)}, u32[]{:S(2)}) %collective-permute-start.4) | collective-permute-done | bytes 196640 | tf_op jit(solution)/shard_map/ppermute | solution.py:306
  46.6 1.3 %collective-permute-start.5 = (bf16[256,384]{1,0:T(8,128)(2,1)S(1)}, bf16[256,384]{1,0:T(8,128)(2,1)S(1)}, u32[]{:S(2)}, u32[]{:S(2)}) collective-permute-start(bf16[256,384]{1,0:T(8,128)(2,1)S(1)} %add.55), channel_id=1, source_target_pairs={{0,8},{4,12},{16,24},{20,28},{1,9},{5,13},{17,25},{21,29},{2,10},{... | collective-permute-start | bytes 589832 | tf_op jit(solution)/shard_map/ppermute | solution.py:306
  47.9 1.9 %pad_maximum_fusion.1.near_ref = bf16[4,128,384]{2,1,0:T(8,128)(2,1)} fusion(bf16[1,128,384]{2,1,0:T(8,128)(2,1)} %bitcast.12, bf16[1,128,384]{2,1,0:T(8,128)(2,1)} %bitcast.11, bf16[1,128,384]{2,1,0:T(8,128)(2,1)} %bitcast.10, bf16[1,128,384]{2,1,0:T(8,128)(2,1)} %bitcast.9), kind=kLoop, calls=%fused_computation.4 | loop fusion | flops 589824 | bytes 786432 | tf_op jit(solution)/shard_map/stack | solution.py:275
  49.8 0.9 collective-permute-done.9
  50.8 1.3 %collective-permute-start.10 = (bf16[256,384]{1,0:T(8,128)(2,1)S(1)}, bf16[256,384]{1,0:T(8,128)(2,1)S(1)}, u32[]{:S(2)}, u32[]{:S(2)}) collective-permute-start(bf16[256,384]{1,0:T(8,128)(2,1)S(1)} %add.61), channel_id=1, source_target_pairs={{0,8},{4,12},{16,24},{20,28},{1,9},{5,13},{17,25},{21,29},{2,10},{... | collective-permute-start | bytes 589832 | tf_op jit(solution)/shard_map/ppermute | solution.py:306
  52.1 2.8 %collective-permute-done.5 = bf16[256,384]{1,0:T(8,128)(2,1)S(1)} collective-permute-done((bf16[256,384]{1,0:T(8,128)(2,1)S(1)}, bf16[256,384]{1,0:T(8,128)(2,1)S(1)}, u32[]{:S(2)}, u32[]{:S(2)}) %collective-permute-start.5) | collective-permute-done | bytes 196640 | tf_op jit(solution)/shard_map/ppermute | solution.py:306
  55.0 2.5 %collective-permute-done.10 = bf16[256,384]{1,0:T(8,128)(2,1)S(1)} collective-permute-done((bf16[256,384]{1,0:T(8,128)(2,1)S(1)}, bf16[256,384]{1,0:T(8,128)(2,1)S(1)}, u32[]{:S(2)}, u32[]{:S(2)}) %collective-permute-start.10) | collective-permute-done | bytes 196640 | tf_op jit(solution)/shard_map/ppermute | solution.py:306
  57.5 0.8 pad_maximum_fusion.near_ref
  58.3 1.7 %collective-permute-start.12 = (bf16[2,256,384]{2,1,0:T(8,128)(2,1)}, bf16[2,256,384]{2,1,0:T(8,128)(2,1)}, u32[]{:S(2)}, u32[]{:S(2)}) collective-permute-start(bf16[2,256,384]{2,1,0:T(8,128)(2,1)} %pad_maximum_fusion.near_ref), channel_id=1, source_target_pairs={{0,2},{1,3},{2,0},{3,1},{4,6},{5,7},{6,4},{7,5},{8,10},{9,11},{10,... | collective-permute-start | bytes 1179656 | tf_op jit(solution)/shard_map/ppermute | solution.py:271
  60.0 0.1 fusion.5.bias_ref
  60.2 18.4 %collective-permute-done.12.near_ref = bf16[2,256,384]{2,1,0:T(8,128)(2,1)} collective-permute-done((bf16[2,256,384]{2,1,0:T(8,128)(2,1)}, bf16[2,256,384]{2,1,0:T(8,128)(2,1)}, u32[]{:S(2)}, u32[]{:S(2)}) %collective-permute-start.12) | collective-permute-done | bytes 393248 | tf_op jit(solution)/shard_map/ppermute | solution.py:271
  78.7 0.4 collective-permute-start.17
  79.0 0.2 collective-permute-start.20
  79.3 13.3 %suffix_attend.1 = f32[8,136,384]{2,1,0:T(8,128)S(1)} custom-call(s32[1]{0:T(128)} %bitcast.13.at_ref, bf16[4,128,384]{2,1,0:T(8,128)(2,1)} %pad_maximum_fusion.1.near_ref, bf16[4,128,384]{2,1,0:T(8,128)(2,1)} %collective-permute-done.16.far_ref, bf16[4,2,512,384]{3,2,1,0:T(8,128)(2,1)} %all-to-all-done.kv_ref, bf16[2,128,384]{2,1,0:T(8,128)(2,1)S(1)} %copy-done.4, ...), custom_call_target="tpu_custom_call" | custom-call | flops 6845104128 | bytes 7864320 | tf_op jit(solution)/shard_map/suffix_attend/pallas_call | solution.py:146
  92.6 1.0 convert_element_type.9
  93.7 4.4 %all-to-all-start.1 = ((f16[8,136,384]{2,1,0:T(8,128)(2,1)}), f16[8,136,384]{2,1,0:T(8,128)(2,1)}, u32[]{:S(2)}, u32[]{:S(2)}) async-start(f16[8,136,384]{2,1,0:T(8,128)(2,1)} %convert_element_type.9), calls=%async_computation.1 | async-start | bytes 1671168 | tf_op jit(solution)/shard_map/all_to_all | solution.py:330
  98.1 0.1 add_add_fusion.1.at_ref
  98.2 0.1 add_add_fusion.2.at_ref
  98.2 0.3 collective-permute-start.21
  98.5 0.1 add_add_fusion.3.at_ref
  98.6 0.1 add_add_fusion.at_ref
  98.7 1.4 %copy-done.1 = bf16[512,1536]{1,0:T(8,128)(2,1)S(1)} copy-done((bf16[512,1536]{1,0:T(8,128)(2,1)S(1)}, bf16[512,1536]{1,0:T(8,128)(2,1)}, u32[]{:S(2)}) %copy-start.1) | copy-done | bytes 1572888
  100.1 4.8 %context_attend.4.rest_0_ = bf16[512,1536]{1,0:T(8,128)(2,1)} custom-call(s32[3]{0:T(128)S(1)} %add_add_fusion.3.at_ref, s32[32]{0:T(128)S(1)} %copy-done.3, bf16[512,1536]{1,0:T(8,128)(2,1)S(1)} %copy-done.1, bf16[2,512,1536]{2,1,0:T(8,128)(2,1)S(1)} %copy-done, f32[32,512]{1,0:T(8,128)S(1)} %fusion.5.bias_ref, ...), custom_call_target="tpu_custom_call" | custom-call | flops 805306368 | bytes 2359296 | tf_op jit(solution)/shard_map/context_attend/pallas_call | solution.py:242
  104.9 4.8 %context_attend.5.rest_0_ = bf16[512,1536]{1,0:T(8,128)(2,1)} custom-call(s32[3]{0:T(128)S(1)} %add_add_fusion.2.at_ref, s32[32]{0:T(128)S(1)} %copy-done.3, bf16[512,1536]{1,0:T(8,128)(2,1)S(1)} %copy-done.2, bf16[2,512,1536]{2,1,0:T(8,128)(2,1)S(1)} %copy-done, f32[32,512]{1,0:T(8,128)S(1)} %fusion.5.bias_ref, ...), custom_call_target="tpu_custom_call", output_to_operand_aliasing={{}: (7, {})} | custom-call | flops 805306368 | bytes 2359296 | tf_op jit(solution)/shard_map/context_attend/pallas_call | solution.py:242
  109.7 4.8 %context_attend.6.rest_0_ = bf16[512,1536]{1,0:T(8,128)(2,1)} custom-call(s32[3]{0:T(128)S(1)} %add_add_fusion.1.at_ref, s32[32]{0:T(128)S(1)} %copy-done.3, bf16[512,1536]{1,0:T(8,128)(2,1)S(1)} %copy-done.2, bf16[2,512,1536]{2,1,0:T(8,128)(2,1)S(1)} %copy-done, f32[32,512]{1,0:T(8,128)S(1)} %fusion.5.bias_ref, ...), custom_call_target="tpu_custom_call", output_to_operand_aliasing={{}: (7, {})} | custom-call | flops 805306368 | bytes 2359296 | tf_op jit(solution)/shard_map/context_attend/pallas_call | solution.py:242
  114.6 4.8 %context_attend.7 = bf16[512,1536]{1,0:T(8,128)(2,1)} custom-call(s32[3]{0:T(128)S(1)} %add_add_fusion.at_ref, s32[32]{0:T(128)S(1)} %copy-done.3, bf16[512,1536]{1,0:T(8,128)(2,1)S(1)} %copy-done.2, bf16[2,512,1536]{2,1,0:T(8,128)(2,1)S(1)} %copy-done, f32[32,512]{1,0:T(8,128)S(1)} %fusion.5.bias_ref, ...), custom_call_target="tpu_custom_call", output_to_operand_aliasing={{}: (7, {})} | custom-call | flops 805306368 | bytes 2359296 | tf_op jit(solution)/shard_map/context_attend/pallas_call | solution.py:242
  119.4 0.4 all-to-all-done.1
  119.8 2.5 %convert_element_type.10.in_ref = f32[8,136,384]{2,1,0:T(8,128)} convert(f16[8,136,384]{2,1,0:T(8,128)(2,1)} %all-to-all-done.1) | non-fusion elementwise | flops 417792 | bytes 2506752 | tf_op jit(solution)/shard_map/convert_element_type | solution.py:343
  122.3 3.5 %combine_groups.1 = bf16[128,384]{1,0:T(8,128)(2,1)} custom-call(f32[8,136,384]{2,1,0:T(8,128)} %convert_element_type.10.in_ref), custom_call_target="tpu_custom_call" | custom-call | flops 835584 | bytes 1671168 | tf_op jit(solution)/shard_map/combine_groups/pallas_call | solution.py:186
  (43 shorter events, 0.4 us)
Async XLA Ops:
  0.6 21.5 %copy-start = (bf16[2,512,1536]{2,1,0:T(8,128)(2,1)S(1)}, bf16[2,512,1536]{2,1,0:T(8,128)(2,1)}, u32[]{:S(2)}) copy-start(bf16[2,512,1536]{2,1,0:T(8,128)(2,1)} %kv_ref.9) | copy-start | bytes 9437188
  5.0 17.2 %collective-permute-start.2 = (bf16[2,256,768]{2,1,0:T(8,128)(2,1)}, bf16[2,256,768]{2,1,0:T(8,128)(2,1)}, u32[]{:S(2)}, u32[]{:S(2)}) collective-permute-start(bf16[2,256,768]{2,1,0:T(8,128)(2,1)} %get-tuple-element.24), channel_id=1, source_target_pairs={{0,4}} | collective-permute-start | bytes 2359304 | tf_op jit(solution)/shard_map/ppermute | solution.py:286
  10.7 7.8 %collective-permute-start = (bf16[256,768]{1,0:T(8,128)(2,1)}, bf16[256,768]{1,0:T(8,128)(2,1)S(1)}, u32[]{:S(2)}, u32[]{:S(2)}) collective-permute-start(bf16[256,768]{1,0:T(8,128)(2,1)} %get-tuple-element.22), channel_id=1, source_target_pairs={{0,6}} | collective-permute-start | bytes 1179656 | tf_op jit(solution)/shard_map/ppermute | solution.py:286
  12.3 9.8 %collective-permute-start.1 = (bf16[256,768]{1,0:T(8,128)(2,1)}, bf16[256,768]{1,0:T(8,128)(2,1)}, u32[]{:S(2)}, u32[]{:S(2)}) collective-permute-start(bf16[256,768]{1,0:T(8,128)(2,1)} %get-tuple-element.23), channel_id=1, source_target_pairs={{0,2}} | collective-permute-start | bytes 1179656 | tf_op jit(solution)/shard_map/ppermute | solution.py:286
  14.4 19.9 %collective-permute-start.6 = (bf16[256,768]{1,0:T(8,128)(2,1)}, bf16[256,768]{1,0:T(8,128)(2,1)}, u32[]{:S(2)}, u32[]{:S(2)}) collective-permute-start(bf16[256,768]{1,0:T(8,128)(2,1)} %get-tuple-element.25), channel_id=1, source_target_pairs={{0,6}} | collective-permute-start | bytes 1179656 | tf_op jit(solution)/shard_map/ppermute | solution.py:286
  16.5 20.2 %collective-permute-start.7 = (bf16[256,768]{1,0:T(8,128)(2,1)}, bf16[256,768]{1,0:T(8,128)(2,1)}, u32[]{:S(2)}, u32[]{:S(2)}) collective-permute-start(bf16[256,768]{1,0:T(8,128)(2,1)} %get-tuple-element.26), channel_id=1, source_target_pairs={{0,2}} | collective-permute-start | bytes 1179656 | tf_op jit(solution)/shard_map/ppermute | solution.py:286
  18.6 3.6 %copy-start.5 = (bf16[256,768]{1,0:T(8,128)(2,1)}, bf16[256,768]{1,0:T(8,128)(2,1)S(1)}, u32[]{:S(2)}) copy-start(bf16[256,768]{1,0:T(8,128)(2,1)S(1)} %collective-permute-done) | copy-start | bytes 1179652
  23.4 24.4 %collective-permute-start.15 = (bf16[128,384]{1,0:T(8,128)(2,1)}, bf16[128,384]{1,0:T(8,128)(2,1)}, u32[]{:S(2)}, u32[]{:S(2)}) collective-permute-start(bf16[128,384]{1,0:T(8,128)(2,1)} %param.10), channel_id=1, source_target_pairs={{0,24},{4,28},{8,16},{12,20},{16,8},{20,12},{24,0},{28,4},{1,25},{... | collective-permute-start | bytes 294920 | tf_op jit(solution)/shard_map/ppermute | solution.py:271
  23.5 24.4 %collective-permute-start.14 = (bf16[128,384]{1,0:T(8,128)(2,1)}, bf16[128,384]{1,0:T(8,128)(2,1)}, u32[]{:S(2)}, u32[]{:S(2)}) collective-permute-start(bf16[128,384]{1,0:T(8,128)(2,1)} %param.10), channel_id=1, source_target_pairs={{0,16},{4,20},{8,24},{12,28},{16,0},{20,4},{24,8},{28,12},{1,17},{... | collective-permute-start | bytes 294920 | tf_op jit(solution)/shard_map/ppermute | solution.py:271
  23.6 24.3 %collective-permute-start.13 = (bf16[128,384]{1,0:T(8,128)(2,1)}, bf16[128,384]{1,0:T(8,128)(2,1)}, u32[]{:S(2)}, u32[]{:S(2)}) collective-permute-start(bf16[128,384]{1,0:T(8,128)(2,1)} %param.10), channel_id=1, source_target_pairs={{0,8},{4,12},{8,0},{12,4},{16,24},{20,28},{24,16},{28,20},{1,9},{5... | collective-permute-start | bytes 294920 | tf_op jit(solution)/shard_map/ppermute | solution.py:271
  28.6 50.7 %all-to-all-start = ((bf16[4,2,512,384]{3,2,1,0:T(8,128)(2,1)}), bf16[4,2,512,384]{3,2,1,0:T(8,128)(2,1)}, u32[]{:S(2)}, u32[]{:S(2)}) async-start(bf16[4,2,512,384]{3,2,1,0:T(8,128)(2,1)} %get-tuple-element.34), calls=%async_computation | async-start | bytes 6291456 | tf_op jit(solution)/shard_map/all_to_all | solution.py:319
  34.3 4.9 %collective-permute-start.3 = (bf16[256,384]{1,0:T(8,128)(2,1)}, bf16[256,384]{1,0:T(8,128)(2,1)S(1)}, u32[]{:S(2)}, u32[]{:S(2)}) collective-permute-start(bf16[256,384]{1,0:T(8,128)(2,1)} %slice.34), channel_id=1, source_target_pairs={{0,1},{2,3},{4,5},{6,7},{8,9},{10,11},{12,13},{14,15},{16,17},{18,... | collective-permute-start | bytes 589832 | tf_op jit(solution)/shard_map/ppermute | solution.py:302
  37.9 3.3 %collective-permute-start.8 = (bf16[256,384]{1,0:T(8,128)(2,1)S(1)}, bf16[256,384]{1,0:T(8,128)(2,1)S(1)}, u32[]{:S(2)}, u32[]{:S(2)}) collective-permute-start(bf16[256,384]{1,0:T(8,128)(2,1)S(1)} %slice.37), channel_id=1, source_target_pairs={{0,1},{2,3},{4,5},{6,7},{8,9},{10,11},{12,13},{14,15},{16,17},{18,... | collective-permute-start | bytes 589832 | tf_op jit(solution)/shard_map/ppermute | solution.py:302
  39.2 7.3 %collective-permute-start.4 = (bf16[256,384]{1,0:T(8,128)(2,1)S(1)}, bf16[256,384]{1,0:T(8,128)(2,1)S(1)}, u32[]{:S(2)}, u32[]{:S(2)}) collective-permute-start(bf16[256,384]{1,0:T(8,128)(2,1)S(1)} %slice_add_fusion.1), channel_id=1, source_target_pairs={{0,16},{4,20},{1,17},{5,21},{2,18},{6,22},{3,19},{7,23}} | collective-permute-start | bytes 589832 | tf_op jit(solution)/shard_map/ppermute | solution.py:306
  41.2 9.5 %collective-permute-start.9 = (bf16[256,384]{1,0:T(8,128)(2,1)S(1)}, bf16[256,384]{1,0:T(8,128)(2,1)S(1)}, u32[]{:S(2)}, u32[]{:S(2)}) collective-permute-start(bf16[256,384]{1,0:T(8,128)(2,1)S(1)} %slice_add_fusion), channel_id=1, source_target_pairs={{0,16},{4,20},{1,17},{5,21},{2,18},{6,22},{3,19},{7,23}} | collective-permute-start | bytes 589832 | tf_op jit(solution)/shard_map/ppermute | solution.py:306
  46.6 8.4 %collective-permute-start.5 = (bf16[256,384]{1,0:T(8,128)(2,1)S(1)}, bf16[256,384]{1,0:T(8,128)(2,1)S(1)}, u32[]{:S(2)}, u32[]{:S(2)}) collective-permute-start(bf16[256,384]{1,0:T(8,128)(2,1)S(1)} %add.55), channel_id=1, source_target_pairs={{0,8},{4,12},{16,24},{20,28},{1,9},{5,13},{17,25},{21,29},{2,10},{... | collective-permute-start | bytes 589832 | tf_op jit(solution)/shard_map/ppermute | solution.py:306
  47.9 12.1 %copy-start.6 = (s32[16384]{0:T(1024)S(1)}, s32[16384]{0:T(1024)}, u32[]{:S(2)}) copy-start(s32[16384]{0:T(1024)} %param.8) | copy-start | bytes 196612
  47.9 12.1 %copy-start.3 = (s32[32]{0:T(128)S(1)}, s32[32]{0:T(128)}, u32[]{:S(2)}) copy-start(s32[32]{0:T(128)} %len_ref.7) | copy-start | bytes 388
  47.9 31.3 %copy-start.4 = (bf16[2,128,384]{2,1,0:T(8,128)(2,1)S(1)}, bf16[2,128,384]{2,1,0:T(8,128)(2,1)}, u32[]{:S(2)}) copy-start(bf16[2,128,384]{2,1,0:T(8,128)(2,1)} %sk_ref.1) | copy-start | bytes 589828
  49.8 10.4 %collective-permute-start.16 = (bf16[4,128,384]{2,1,0:T(8,128)(2,1)}, bf16[4,128,384]{2,1,0:T(8,128)(2,1)}, u32[]{:S(2)}, u32[]{:S(2)}) collective-permute-start(bf16[4,128,384]{2,1,0:T(8,128)(2,1)} %pad_maximum_fusion.1.near_ref), channel_id=1, source_target_pairs={{0,4},{4,0},{8,12},{12,8},{16,20},{20,16},{24,28},{28,24},{1,5},{5... | collective-permute-start | bytes 1179656 | tf_op jit(solution)/shard_map/ppermute | solution.py:271
  50.8 6.7 %collective-permute-start.10 = (bf16[256,384]{1,0:T(8,128)(2,1)S(1)}, bf16[256,384]{1,0:T(8,128)(2,1)S(1)}, u32[]{:S(2)}, u32[]{:S(2)}) collective-permute-start(bf16[256,384]{1,0:T(8,128)(2,1)S(1)} %add.61), channel_id=1, source_target_pairs={{0,8},{4,12},{16,24},{20,28},{1,9},{5,13},{17,25},{21,29},{2,10},{... | collective-permute-start | bytes 589832 | tf_op jit(solution)/shard_map/ppermute | solution.py:306
  58.3 20.4 %collective-permute-start.12 = (bf16[2,256,384]{2,1,0:T(8,128)(2,1)}, bf16[2,256,384]{2,1,0:T(8,128)(2,1)}, u32[]{:S(2)}, u32[]{:S(2)}) collective-permute-start(bf16[2,256,384]{2,1,0:T(8,128)(2,1)} %pad_maximum_fusion.near_ref), channel_id=1, source_target_pairs={{0,2},{1,3},{2,0},{3,1},{4,6},{5,7},{6,4},{7,5},{8,10},{9,11},{10,... | collective-permute-start | bytes 1179656 | tf_op jit(solution)/shard_map/ppermute | solution.py:271
  60.0 18.7 %collective-permute-start.11 = (bf16[2,256,384]{2,1,0:T(8,128)(2,1)}, bf16[2,256,384]{2,1,0:T(8,128)(2,1)}, u32[]{:S(2)}, u32[]{:S(2)}) collective-permute-start(bf16[2,256,384]{2,1,0:T(8,128)(2,1)} %pad_maximum_fusion.near_ref), channel_id=1, source_target_pairs={{0,4},{4,0},{8,12},{12,8},{16,20},{20,16},{24,28},{28,24},{1,5},{5... | collective-permute-start | bytes 1179656 | tf_op jit(solution)/shard_map/ppermute | solution.py:271
  60.1 32.5 %collective-permute-start.18 = (bf16[2,256,384]{2,1,0:T(8,128)(2,1)}, bf16[2,256,384]{2,1,0:T(8,128)(2,1)}, u32[]{:S(2)}, u32[]{:S(2)}) collective-permute-start(bf16[2,256,384]{2,1,0:T(8,128)(2,1)} %pad_maximum_fusion.near_ref), channel_id=1, source_target_pairs={{0,1},{1,0},{2,3},{3,2},{4,5},{5,4},{6,7},{7,6},{8,9},{9,8},{10,11... | collective-permute-start | bytes 1179656 | tf_op jit(solution)/shard_map/ppermute | solution.py:271
  78.7 13.9 %collective-permute-start.19 = (bf16[2,256,384]{2,1,0:T(8,128)(2,1)}, bf16[2,256,384]{2,1,0:T(8,128)(2,1)}, u32[]{:S(2)}, u32[]{:S(2)}) collective-permute-start(bf16[2,256,384]{2,1,0:T(8,128)(2,1)} %collective-permute-done.11.far_ref), channel_id=1, source_target_pairs={{0,1},{1,0},{2,3},{3,2},{4,5},{5,4},{6,7},{7,6},{8,9},{9,8},{10,11... | collective-permute-start | bytes 1179656 | tf_op jit(solution)/shard_map/ppermute | solution.py:271
  78.7 14.0 %collective-permute-start.17 = (bf16[2,256,384]{2,1,0:T(8,128)(2,1)}, bf16[2,256,384]{2,1,0:T(8,128)(2,1)}, u32[]{:S(2)}, u32[]{:S(2)}) collective-permute-start(bf16[2,256,384]{2,1,0:T(8,128)(2,1)} %collective-permute-done.11.far_ref), channel_id=1, source_target_pairs={{0,2},{1,3},{2,0},{3,1},{4,6},{5,7},{6,4},{7,5},{8,10},{9,11},{10,... | collective-permute-start | bytes 1179656 | tf_op jit(solution)/shard_map/ppermute | solution.py:271
  79.0 13.6 %collective-permute-start.20 = (bf16[2,256,384]{2,1,0:T(8,128)(2,1)}, bf16[2,256,384]{2,1,0:T(8,128)(2,1)}, u32[]{:S(2)}, u32[]{:S(2)}) collective-permute-start(bf16[2,256,384]{2,1,0:T(8,128)(2,1)} %collective-permute-done.12.near_ref), channel_id=1, source_target_pairs={{0,1},{1,0},{2,3},{3,2},{4,5},{5,4},{6,7},{7,6},{8,9},{9,8},{10,11... | collective-permute-start | bytes 1179656 | tf_op jit(solution)/shard_map/ppermute | solution.py:271
  93.7 26.1 %all-to-all-start.1 = ((f16[8,136,384]{2,1,0:T(8,128)(2,1)}), f16[8,136,384]{2,1,0:T(8,128)(2,1)}, u32[]{:S(2)}, u32[]{:S(2)}) async-start(f16[8,136,384]{2,1,0:T(8,128)(2,1)} %convert_element_type.9), calls=%async_computation.1 | async-start | bytes 1671168 | tf_op jit(solution)/shard_map/all_to_all | solution.py:330
  98.2 16.3 %collective-permute-start.21 = (bf16[2,256,384]{2,1,0:T(8,128)(2,1)}, bf16[2,256,384]{2,1,0:T(8,128)(2,1)}, u32[]{:S(2)}, u32[]{:S(2)}) collective-permute-start(bf16[2,256,384]{2,1,0:T(8,128)(2,1)} %collective-permute-done.17.far_ref), channel_id=1, source_target_pairs={{0,1},{1,0},{2,3},{3,2},{4,5},{5,4},{6,7},{7,6},{8,9},{9,8},{10,11... | collective-permute-start | bytes 1179656 | tf_op jit(solution)/shard_map/ppermute | solution.py:271
  98.7 1.4 %copy-start.1 = (bf16[512,1536]{1,0:T(8,128)(2,1)S(1)}, bf16[512,1536]{1,0:T(8,128)(2,1)}, u32[]{:S(2)}) copy-start(bf16[512,1536]{1,0:T(8,128)(2,1)} %q_ref.7) | copy-start | bytes 4718596
  100.1 4.8 %copy-start.2 = (bf16[512,1536]{1,0:T(8,128)(2,1)S(1)}, bf16[512,1536]{1,0:T(8,128)(2,1)}, u32[]{:S(2)}) copy-start(bf16[512,1536]{1,0:T(8,128)(2,1)} %q_ref.7) | copy-start | bytes 4718596

commit v10 on v9

--- a/solution.py
+++ b/solution.py
@@ -92,7 +92,8 @@
         finish(task, scores)
 
 
-def suffix_kernel(at_ref, near_ref, far_ref, kv_ref, sk_ref, bias_ref, out_ref):
+def suffix_kernel(at_ref, near_ref, far_ref, kv_ref, sk_ref, bias_ref, *rest):
+    out_ref = rest[-1]
     host = at_ref[0]
     groups = kv_ref.shape[0]
     half, share, _ = near_ref.shape
@@ -137,57 +138,61 @@
     pipelined(list(range(0, hosts, chunks)), score, finish)
 
 
-def suffix_attend(host, near, far, kv, sk, bias):
+def suffix_attend(host, near, far, kv, sk, bias, first, count, before):
     half, share, width = near.shape
-    hosts, heads = 2 * half, width // HSZ
+    hosts = 2 * half
+    more = [] if before is None else [before]
     groups, _, rows, _ = kv.shape
     seen = groups * rows + share
-    column = lambda h, at: (0, 0, h)
+    column = lambda h, at: (0, 0, first + h)
     return pl.pallas_call(
         suffix_kernel,
         grid_spec=pltpu.PrefetchScalarGridSpec(
             num_scalar_prefetch=1,
-            grid=(heads,),
+            grid=(count,),
             in_specs=[
                 pl.BlockSpec((half, share, HSZ), column),
                 pl.BlockSpec((half, share, HSZ), column),
-                pl.BlockSpec((groups, 2, rows, HSZ), lambda h, at: (0, 0, 0, h)),
+                pl.BlockSpec((groups, 2, rows, HSZ), lambda h, at: (0, 0, 0, first + h)),
                 pl.BlockSpec((2, share, HSZ), column),
                 pl.BlockSpec(bias.shape, lambda h, at: (0, 0)),
-            ],
+            ]
+            + [pl.BlockSpec(memory_space=pl.ANY) for _ in more],
             out_specs=pl.BlockSpec((hosts, share + EXTRA, HSZ), column),
         ),
         out_shape=jax.ShapeDtypeStruct((hosts, share + EXTRA, width), jnp.float32),
+        input_output_aliases={6: 0} if more else {},
         compiler_params=pltpu.CompilerParams(vmem_limit_bytes=24 * 1024 * 1024),
         cost_estimate=pl.CostEstimate(
-            flops=8 * hosts * share * seen * width,
-            bytes_accessed=4 * (groups * rows + 3 * hosts * share) * width,
-            transcendentals=heads * hosts * share * seen,
+            flops=8 * count * hosts * share * seen * HSZ,
+            bytes_accessed=4 * count * (groups * rows + 3 * hosts * share) * HSZ,
+            transcendentals=count * hosts * share * seen,
         ),
         name="suffix_attend",
-    )(host, near, far, kv, sk, bias)
+    )(host, near, far, kv, sk, bias, *more)
 
 
 def combine_kernel(in_ref, out_ref):
-    hosts, tall, _ = in_ref.shape
+    hosts, tall, width = in_ref.shape
     share = tall - EXTRA
-    whole, coarse, fine, shift = [in_ref[:, share + k, :] for k in range(4)]
-    weight = jnp.exp2(whole - jnp.max(whole, axis=0, keepdims=True)) * (coarse + fine * (1.0 / 1024.0))
-    factor = weight * jnp.exp2(shift) / jnp.sum(weight, axis=0, keepdims=True)
-    factor = jnp.concatenate([factor, jnp.zeros((HSZ - hosts, HSZ), jnp.float32)], axis=0).T[:share, :]
-    mixed = 0.0
-    for g in range(hosts):
-        mixed = mixed + factor[:, g : g + 1] * in_ref[g, :share, :]
-    out_ref[...] = mixed.astype(out_ref.dtype)
+    for first in range(0, width, HSZ):
+        head = slice(first, first + HSZ)
+        whole, coarse, fine, shift = [in_ref[:, share + k, head] for k in range(4)]
+        weight = jnp.exp2(whole - jnp.max(whole, axis=0, keepdims=True)) * (coarse + fine * (1.0 / 1024.0))
+        factor = weight * jnp.exp2(shift) / jnp.sum(weight, axis=0, keepdims=True)
+        factor = jnp.concatenate([factor, jnp.zeros((HSZ - hosts, HSZ), jnp.float32)], axis=0).T[:share, :]
+        mixed = 0.0
+        for g in range(hosts):
+            mixed = mixed + factor[:, g : g + 1] * in_ref[g, :share, head]
+        out_ref[:, head] = mixed.astype(out_ref.dtype)
 
 
 def combine(parts):
-    hosts, tall, width = parts.shape
+    _, tall, width = parts.shape
     return pl.pallas_call(
         combine_kernel,
-        grid=(width // HSZ,),
-        in_specs=[pl.BlockSpec((hosts, tall, HSZ), lambda h: (0, 0, h))],
-        out_specs=pl.BlockSpec((tall - EXTRA, HSZ), lambda h: (0, h)),
+        in_specs=[pl.BlockSpec(memory_space=pltpu.VMEM)],
+        out_specs=pl.BlockSpec(memory_space=pltpu.VMEM),
         out_shape=jax.ShapeDtypeStruct((tall - EXTRA, width), jnp.bfloat16),
         cost_estimate=pl.CostEstimate(flops=2 * parts.size, bytes_accessed=4 * parts.size, transcendentals=0),
         name="combine_groups",
@@ -290,7 +295,7 @@
     for s in range(2):
         slab = jnp.where(first, kv[s, : rows // 2, : width // 2], 0.0) + send(diagonal[s], groups + cores) + send(across[s], cores)
         slabs.append(slab + (after(down[s], slabs[0]) if s else down[s]))
-    return slabs
+    return slabs, down
 
 
 def spread_anchor(slab, hosts, groups):
@@ -314,18 +319,22 @@
     rows = queries.shape[0]
     cores = groups // 2
     packed, below, across, diagonal = pack(keys_values, groups)
-    slabs = scatter_anchor(keys_values, across, diagonal, below, groups)
-    packed, suffix_queries = after((packed, suffix_queries), slabs[0])
-    swapped = lax.all_to_all(packed, "grp", split_axis=0, concat_axis=0, tiled=True)
+    slabs, down = scatter_anchor(keys_values, across, diagonal, below, groups)
+    swapped = lax.all_to_all(after(packed, down), "grp", split_axis=0, concat_axis=0, tiled=True)
     near = jnp.stack([spread_anchor(x, hosts, groups) for x in slabs])
-    gathered = gather_hosts(suffix_queries, hosts)
+    gathered = gather_hosts(after(suffix_queries, slabs[1]), hosts)
     seen = (token_ids.reshape(-1, rows) >= NAMB) & (jnp.arange(rows)[None, :] < lengths[:, None])
     bias = jnp.where(seen, 0.0, NEG).astype(jnp.float32)
-    far, other_near, gathered = lax.optimization_barrier((swap(near, "hst", 1), swap(near, "grp", cores), gathered))
+    suffix = functools.partial(suffix_attend, jnp.stack([host]), *gathered, swapped, suffix_kv, bias)
+    heads = suffix_queries.shape[1] // HSZ
+    early = max(1, heads - 1)
+    far, other_near = swap(near, "hst", 1), swap(after(near, swapped), "grp", cores)
+    far, other_near, parts = lax.optimization_barrier((far, other_near, suffix(0, early, None)))
     other_far = swap(far, "grp", cores)
-    by_core = [[swap(x, "grp", k) for x in (near, far, other_near)] for k in range(1, cores)]
-    parts = suffix_attend(jnp.stack([host]), *gathered, swapped, suffix_kv, bias)
-    other_far, by_core, parts = lax.optimization_barrier((other_far, by_core, parts))
+    by_core = [[swap(x, "grp", k) for x in (near, far)] for k in range(1, cores)]
+    if heads > early:
+        parts = suffix(early, heads - early, parts)
+    by_core, parts = lax.optimization_barrier((by_core, parts))
     parts = parts.astype(jnp.float16)
     coded = lax.all_to_all(parts, "hst", split_axis=0, concat_axis=0, tiled=True)
     held = {0: after([near, far], parts), cores: [other_near, other_far]}
@@ -336,9 +345,12 @@
 
     context_out = context(0, None)
     for k in range(1, cores):
-        held[k] = by_core[k - 1][:2]
-        held[cores ^ k] = [by_core[k - 1][2], swap(other_far, "grp", k)]
-    for k in range(1, groups):
+        held[k] = by_core[k - 1]
+        context_out = context(k, context_out)
+    other = after(held[cores], context_out)
+    for k in range(1, cores):
+        held[cores ^ k] = [swap(x, "grp", k) for x in other]
+    for k in range(cores, groups):
         context_out = context(k, context_out)
     return (context_out, combine(coded.astype(jnp.float32)))
 

time: 127 us -> 117 us (0.921)
  waiting for transfers between devices: 32.7 us -> 11.8 us
  starting transfers between devices: 39.2 us -> 47.1 us
  local copies, waits for them, and re-layouts: 3.22 us -> 5.93 us
    ppermute x11, waiting for transfers between devices: 18.5 us -> 0.03 us  [swap(): lax.ppermute(x, axis, [(i, i ^ k) for i in range(lax.axis_size(axis))])]
    ppermute x4, starting transfers between devices: 5.82 us -> 10.3 us  [spread_anchor(): piece = piece + lax.ppermute(piece, 'hst', pairs)]
    ppermute x11, starting transfers between devices: 7.06 us -> 10.9 us  [swap(): lax.ppermute(x, axis, [(i, i ^ k) for i in range(lax.axis_size(axis))])]
    ppermute x4, waiting for transfers between devices: 10.2 us -> 7.1 us  [spread_anchor(): piece = piece + lax.ppermute(piece, 'hst', pairs)]
    unnamed x14 -> x24, local copies, waits for them, and re-layouts: 1.44 us -> 4.52 us
    all_to_all x1, waiting for transfers between devices: 0.01 us -> 2.37 us  [per_device(): lax.all_to_all(after(packed, down), 'grp', split_axis=0, concat_axis=0, t...]
    ge x1, other arithmetic: 0.01 us -> 1.46 us  [per_device(): token_ids.reshape(-1, rows) >= NAMB]
    pallas_call x1 -> x2, Pallas kernels: 13.3 us -> 14.7 us  [suffix_attend(): pl.pallas_call(suffix_kernel, grid_spec=pltpu.PrefetchScalarGridSpec(num_...]
  transfers between devices with their start and end apart: 24 -> 24, of which waited for: 7 -> 5; matrix products, arithmetic and copies ran while one was open for 6% -> 6% of each run, Pallas kernels for 26% -> 29%
where the time goes in v10:
time: 117 us; the launch traced here: 116 us
  starting transfers between devices  47.1 us (40%)
  Pallas kernels  40.6 us (35%)
  waiting for transfers between devices  11.8 us (10%)
  other arithmetic  9.61 us (8%)
  local copies, waits for them, and re-layouts  5.93 us (5%)
    pallas_call x4, Pallas kernels, context_attend(): pl.pallas_call(context_kernel, grid_spec=pltpu.PrefetchScalarGridSpec(num...  19.3 us
    pallas_call x2, Pallas kernels, suffix_attend(): pl.pallas_call(suffix_kernel, grid_spec=pltpu.PrefetchScalarGridSpec(num_...  14.7 us
    ppermute x5, starting transfers between devices, scatter_anchor(): send = lambda x, to: lax.ppermute(x, BOTH, [(0, to)])  12.8 us
    ppermute x11, starting transfers between devices, swap(): lax.ppermute(x, axis, [(i, i ^ k) for i in range(lax.axis_size(axis))])  10.9 us
    ppermute x4, starting transfers between devices, spread_anchor(): piece = piece + lax.ppermute(piece, 'hst', pairs)  10.3 us
    ppermute x4, waiting for transfers between devices, spread_anchor(): piece = piece + lax.ppermute(piece, 'hst', pairs)  7.1 us
    all_to_all x1, starting transfers between devices, per_device(): lax.all_to_all(after(packed, down), 'grp', split_axis=0, concat_axis=0, t...  4.91 us
    unnamed x24, local copies, waits for them, and re-layouts  4.52 us
  transfers between devices with their start and end apart: 24, of which 5 were waited for; matrix products, arithmetic and copies ran while one was open for 6% of the time, Pallas kernels for 29%

profile of v10, /device:TPU:0, one launch (start us, length us, event | category | flops | bytes accessed | tf_op | source)
XLA Modules:
  0.0 116.0 jit_solution(15615147515030308961)
XLA Ops:
  0.6 3.9 %pack_heads.1 = (bf16[4,2,512,384]{3,2,1,0:T(8,128)(2,1)}, bf16[2,256,768]{2,1,0:T(8,128)(2,1)}, bf16[256,768]{1,0:T(8,128)(2,1)}, bf16[256,768]{1,0:T(8,128)(2,...) custom-call(bf16[2,512,1536]{2,1,0:T(8,128)(2,1)} %kv_ref.9), custom_call_target="tpu_custom_call" | custom-call | bytes 9437184 | tf_op jit(solution)/shard_map/pack_heads/pallas_call | solution.py:66
  4.5 4.9 %collective-permute-start.2 = (bf16[2,256,768]{2,1,0:T(8,128)(2,1)}, bf16[2,256,768]{2,1,0:T(8,128)(2,1)S(1)}, u32[]{:S(2)}, u32[]{:S(2)}) collective-permute-start(bf16[2,256,768]{2,1,0:T(8,128)(2,1)} %get-tuple-element.24), channel_id=1, source_target_pairs={{0,4}} | collective-permute-start | bytes 2359304 | tf_op jit(solution)/shard_map/ppermute | solution.py:291
  9.4 2.4 %collective-permute-start = (bf16[256,768]{1,0:T(8,128)(2,1)}, bf16[256,768]{1,0:T(8,128)(2,1)}, u32[]{:S(2)}, u32[]{:S(2)}) collective-permute-start(bf16[256,768]{1,0:T(8,128)(2,1)} %get-tuple-element.22), channel_id=1, source_target_pairs={{0,6}} | collective-permute-start | bytes 1179656 | tf_op jit(solution)/shard_map/ppermute | solution.py:291
  11.8 2.1 %collective-permute-start.1 = (bf16[256,768]{1,0:T(8,128)(2,1)}, bf16[256,768]{1,0:T(8,128)(2,1)}, u32[]{:S(2)}, u32[]{:S(2)}) collective-permute-start(bf16[256,768]{1,0:T(8,128)(2,1)} %get-tuple-element.23), channel_id=1, source_target_pairs={{0,2}} | collective-permute-start | bytes 1179656 | tf_op jit(solution)/shard_map/ppermute | solution.py:291
  13.9 1.3 %collective-permute-start.6 = (bf16[256,768]{1,0:T(8,128)(2,1)}, bf16[256,768]{1,0:T(8,128)(2,1)S(1)}, u32[]{:S(2)}, u32[]{:S(2)}) collective-permute-start(bf16[256,768]{1,0:T(8,128)(2,1)} %get-tuple-element.25), channel_id=1, source_target_pairs={{0,6}} | collective-permute-start | bytes 1179656 | tf_op jit(solution)/shard_map/ppermute | solution.py:291
  15.2 2.1 %collective-permute-start.7 = (bf16[256,768]{1,0:T(8,128)(2,1)}, bf16[256,768]{1,0:T(8,128)(2,1)}, u32[]{:S(2)}, u32[]{:S(2)}) collective-permute-start(bf16[256,768]{1,0:T(8,128)(2,1)} %get-tuple-element.26), channel_id=1, source_target_pairs={{0,2}} | collective-permute-start | bytes 1179656 | tf_op jit(solution)/shard_map/ppermute | solution.py:291
  17.3 1.9 %collective-permute-done.2 = bf16[2,256,768]{2,1,0:T(8,128)(2,1)S(1)} collective-permute-done((bf16[2,256,768]{2,1,0:T(8,128)(2,1)}, bf16[2,256,768]{2,1,0:T(8,128)(2,1)S(1)}, u32[]{:S(2)}, u32[]{:S(2)}) %collective-permute-start.2) | collective-permute-done | bytes 786464 | tf_op jit(solution)/shard_map/ppermute | solution.py:291
  19.2 0.9 copy-done.8
  20.1 4.9 %all-to-all-start = ((bf16[4,2,512,384]{3,2,1,0:T(8,128)(2,1)}), bf16[4,2,512,384]{3,2,1,0:T(8,128)(2,1)}, u32[]{:S(2)}, u32[]{:S(2)}) async-start(bf16[4,2,512,384]{3,2,1,0:T(8,128)(2,1)} %get-tuple-element.29), calls=%async_computation | async-start | bytes 6291456 | tf_op jit(solution)/shard_map/all_to_all | solution.py:323
  25.0 1.5 %broadcast_compare_fusion = pred[16384]{0:T(1024)(128)(4,1)} fusion(s32[16384]{0:T(1024)} %param.8), kind=kLoop, calls=%fused_computation.17 | loop fusion | flops 16384 | bytes 81920 | tf_op jit(solution)/shard_map/ge | solution.py:326
  26.4 1.3 %ge.11 = pred[32,512]{1,0:T(8,128)(4,1)} reshape(pred[16384]{0:T(1024)(128)(4,1)} %broadcast_compare_fusion) | data formatting | bytes 32768 | tf_op jit(solution)/shard_map/ge | solution.py:326
  27.8 1.4 %fusion = bf16[256,768]{1,0:T(8,128)(2,1)S(1)} fusion(bf16[2,256,768]{2,1,0:T(8,128)(2,1)} %copy-done.8, bf16[256,768]{1,0:T(8,128)(2,1)} %collective-permute-done.1, bf16[256,768]{1,0:T(8,128)(2,1)} %collective-permute-done, bf16[2,512,1536]{2,1,0:T(8,128)(2,1)S(1)} %copy-done, pred[]{:T(512)S(6)} %and.18), kind=kLoop, calls=%fused_computation.2 | loop fusion | flops 786432 | bytes 1966081 | tf_op jit(solution)/shard_map/add | solution.py:297
  29.3 2.5 %collective-permute-start.3 = (bf16[256,384]{1,0:T(8,128)(2,1)S(1)}, bf16[256,384]{1,0:T(8,128)(2,1)S(1)}, u32[]{:S(2)}, u32[]{:S(2)}) collective-permute-start(bf16[256,384]{1,0:T(8,128)(2,1)S(1)} %slice.34), channel_id=1, source_target_pairs={{0,1},{2,3},{4,5},{6,7},{8,9},{10,11},{12,13},{14,15},{16,17},{18,... | collective-permute-start | bytes 589832 | tf_op jit(solution)/shard_map/ppermute | solution.py:307
  31.9 0.4 collective-permute-done.7
  32.3 1.1 fusion.2
  33.5 4.3 %collective-permute-start.15 = (bf16[128,384]{1,0:T(8,128)(2,1)S(1)}, bf16[128,384]{1,0:T(8,128)(2,1)S(1)}, u32[]{:S(2)}, u32[]{:S(2)}) collective-permute-start(bf16[128,384]{1,0:T(8,128)(2,1)S(1)} %copy-done.10), channel_id=1, source_target_pairs={{0,24},{4,28},{8,16},{12,20},{16,8},{20,12},{24,0},{28,4},{1,25},{... | collective-permute-start | bytes 294920 | tf_op jit(solution)/shard_map/ppermute | solution.py:276
  37.9 1.3 %collective-permute-start.8 = (bf16[256,384]{1,0:T(8,128)(2,1)S(1)}, bf16[256,384]{1,0:T(8,128)(2,1)S(1)}, u32[]{:S(2)}, u32[]{:S(2)}) collective-permute-start(bf16[256,384]{1,0:T(8,128)(2,1)S(1)} %slice.37), channel_id=1, source_target_pairs={{0,1},{2,3},{4,5},{6,7},{8,9},{10,11},{12,13},{14,15},{16,17},{18,... | collective-permute-start | bytes 589832 | tf_op jit(solution)/shard_map/ppermute | solution.py:307
  39.2 1.3 %collective-permute-start.4 = (bf16[256,384]{1,0:T(8,128)(2,1)S(1)}, bf16[256,384]{1,0:T(8,128)(2,1)S(1)}, u32[]{:S(2)}, u32[]{:S(2)}) collective-permute-start(bf16[256,384]{1,0:T(8,128)(2,1)S(1)} %slice_add_fusion.1), channel_id=1, source_target_pairs={{0,16},{4,20},{1,17},{5,21},{2,18},{6,22},{3,19},{7,23}} | collective-permute-start | bytes 589832 | tf_op jit(solution)/shard_map/ppermute | solution.py:311
  40.6 1.3 %collective-permute-start.9 = (bf16[256,384]{1,0:T(8,128)(2,1)S(1)}, bf16[256,384]{1,0:T(8,128)(2,1)S(1)}, u32[]{:S(2)}, u32[]{:S(2)}) collective-permute-start(bf16[256,384]{1,0:T(8,128)(2,1)S(1)} %slice_add_fusion), channel_id=1, source_target_pairs={{0,16},{4,20},{1,17},{5,21},{2,18},{6,22},{3,19},{7,23}} | collective-permute-start | bytes 589832 | tf_op jit(solution)/shard_map/ppermute | solution.py:311
  41.9 4.0 %collective-permute-done.4 = bf16[256,384]{1,0:T(8,128)(2,1)S(1)} collective-permute-done((bf16[256,384]{1,0:T(8,128)(2,1)S(1)}, bf16[256,384]{1,0:T(8,128)(2,1)S(1)}, u32[]{:S(2)}, u32[]{:S(2)}) %collective-permute-start.4) | collective-permute-done | bytes 196640 | tf_op jit(solution)/shard_map/ppermute | solution.py:311
  45.9 1.3 %collective-permute-start.5 = (bf16[256,384]{1,0:T(8,128)(2,1)S(1)}, bf16[256,384]{1,0:T(8,128)(2,1)S(1)}, u32[]{:S(2)}, u32[]{:S(2)}) collective-permute-start(bf16[256,384]{1,0:T(8,128)(2,1)S(1)} %add.55), channel_id=1, source_target_pairs={{0,8},{4,12},{16,24},{20,28},{1,9},{5,13},{17,25},{21,29},{2,10},{... | collective-permute-start | bytes 589832 | tf_op jit(solution)/shard_map/ppermute | solution.py:311
  47.2 0.1 fusion.5.bias_ref
  47.4 0.8 pad_maximum_fusion.1.near_ref
  48.2 1.9 %collective-permute-start.16 = (bf16[4,128,384]{2,1,0:T(8,128)(2,1)}, bf16[4,128,384]{2,1,0:T(8,128)(2,1)}, u32[]{:S(2)}, u32[]{:S(2)}) collective-permute-start(bf16[4,128,384]{2,1,0:T(8,128)(2,1)} %pad_maximum_fusion.1.near_ref), channel_id=1, source_target_pairs={{0,4},{4,0},{8,12},{12,8},{16,20},{20,16},{24,28},{28,24},{1,5},{5... | collective-permute-start | bytes 1179656 | tf_op jit(solution)/shard_map/ppermute | solution.py:276
  50.2 6.4 %collective-permute-start.10 = (bf16[256,384]{1,0:T(8,128)(2,1)S(1)}, bf16[256,384]{1,0:T(8,128)(2,1)S(1)}, u32[]{:S(2)}, u32[]{:S(2)}) collective-permute-start(bf16[256,384]{1,0:T(8,128)(2,1)S(1)} %add.61), channel_id=1, source_target_pairs={{0,8},{4,12},{16,24},{20,28},{1,9},{5,13},{17,25},{21,29},{2,10},{... | collective-permute-start | bytes 589832 | tf_op jit(solution)/shard_map/ppermute | solution.py:311
  56.6 3.1 %collective-permute-done.10 = bf16[256,384]{1,0:T(8,128)(2,1)S(1)} collective-permute-done((bf16[256,384]{1,0:T(8,128)(2,1)S(1)}, bf16[256,384]{1,0:T(8,128)(2,1)S(1)}, u32[]{:S(2)}, u32[]{:S(2)}) %collective-permute-start.10) | collective-permute-done | bytes 196640 | tf_op jit(solution)/shard_map/ppermute | solution.py:311
  59.8 0.8 pad_maximum_fusion.near_ref
  60.6 2.4 %all-to-all-done.kv_ref = bf16[4,2,512,384]{3,2,1,0:T(8,128)(2,1)} async-done(((bf16[4,2,512,384]{3,2,1,0:T(8,128)(2,1)}), bf16[4,2,512,384]{3,2,1,0:T(8,128)(2,1)}, u32[]{:S(2)}, u32[]{:S(2)}) %all-to-all-start) | async-done | bytes 3145760 | tf_op jit(solution)/shard_map/all_to_all | solution.py:323
  63.0 2.5 %collective-permute-start.12 = (bf16[2,256,384]{2,1,0:T(8,128)(2,1)}, bf16[2,256,384]{2,1,0:T(8,128)(2,1)}, u32[]{:S(2)}, u32[]{:S(2)}) collective-permute-start(bf16[2,256,384]{2,1,0:T(8,128)(2,1)} %pad_maximum_fusion.near_ref), channel_id=1, source_target_pairs={{0,2},{1,3},{2,0},{3,1},{4,6},{5,7},{6,4},{7,5},{8,10},{9,11},{10,... | collective-permute-start | bytes 1179656 | tf_op jit(solution)/shard_map/ppermute | solution.py:276
  65.5 9.3 %suffix_attend.2.rest_0_ = f32[8,136,384]{2,1,0:T(8,128)S(1)} custom-call(s32[1]{0:T(128)} %bitcast.9.at_ref, bf16[4,128,384]{2,1,0:T(8,128)(2,1)} %pad_maximum_fusion.1.near_ref, bf16[4,128,384]{2,1,0:T(8,128)(2,1)} %collective-permute-done.16.far_ref, bf16[4,2,512,384]{3,2,1,0:T(8,128)(2,1)} %all-to-all-done.kv_ref, bf16[2,128,384]{2,1,0:T(8,128)(2,1)S(1)} %copy-done.7, ...), custom_call_target="tpu_custom_call" | custom-call | flops 4563402752 | bytes 5242880 | tf_op jit(solution)/shard_map/suffix_attend/pallas_call | solution.py:148
  74.9 5.4 %suffix_attend.3 = f32[8,136,384]{2,1,0:T(8,128)S(1)} custom-call(s32[1]{0:T(128)} %bitcast.9.at_ref, bf16[4,128,384]{2,1,0:T(8,128)(2,1)} %pad_maximum_fusion.1.near_ref, bf16[4,128,384]{2,1,0:T(8,128)(2,1)} %collective-permute-done.16.far_ref, bf16[4,2,512,384]{3,2,1,0:T(8,128)(2,1)} %all-to-all-done.kv_ref, ...), custom_call_target="tpu_custom_call", output_to_operand_aliasing={{}: (6, {})} | custom-call | flops 2281701376 | bytes 2621440 | tf_op jit(solution)/shard_map/suffix_attend/pallas_call | solution.py:148
  80.3 0.7 copy-done.4
  81.0 1.0 convert_element_type.9
  82.0 4.4 %all-to-all-start.1 = ((f16[8,136,384]{2,1,0:T(8,128)(2,1)}), f16[8,136,384]{2,1,0:T(8,128)(2,1)}, u32[]{:S(2)}, u32[]{:S(2)}) async-start(f16[8,136,384]{2,1,0:T(8,128)(2,1)} %convert_element_type.9), calls=%async_computation.1 | async-start | bytes 1671168 | tf_op jit(solution)/shard_map/all_to_all | solution.py:339
  86.4 1.4 %collective-permute-start.17 = (bf16[2,256,384]{2,1,0:T(8,128)(2,1)}, bf16[2,256,384]{2,1,0:T(8,128)(2,1)}, u32[]{:S(2)}, u32[]{:S(2)}) collective-permute-start(bf16[2,256,384]{2,1,0:T(8,128)(2,1)} %collective-permute-done.11.far_ref), channel_id=1, source_target_pairs={{0,2},{1,3},{2,0},{3,1},{4,6},{5,7},{6,4},{7,5},{8,10},{9,11},{10,... | collective-permute-start | bytes 1179656 | tf_op jit(solution)/shard_map/ppermute | solution.py:276
  87.8 0.1 add_add_fusion.2.at_ref
  87.9 0.1 add_add_fusion.1.at_ref
  88.0 1.4 %copy-done.1 = bf16[512,1536]{1,0:T(8,128)(2,1)S(1)} copy-done((bf16[512,1536]{1,0:T(8,128)(2,1)S(1)}, bf16[512,1536]{1,0:T(8,128)(2,1)}, u32[]{:S(2)}) %copy-start.1) | copy-done | bytes 1572888
  89.4 4.9 %context_attend.4.rest_0_ = bf16[512,1536]{1,0:T(8,128)(2,1)} custom-call(s32[3]{0:T(128)S(1)} %add_add_fusion.2.at_ref, s32[32]{0:T(128)S(1)} %copy-done.6, bf16[512,1536]{1,0:T(8,128)(2,1)S(1)} %copy-done.1, bf16[2,512,1536]{2,1,0:T(8,128)(2,1)S(1)} %copy-done, f32[32,512]{1,0:T(8,128)S(1)} %fusion.5.bias_ref, ...), custom_call_target="tpu_custom_call" | custom-call | flops 805306368 | bytes 2359296 | tf_op jit(solution)/shard_map/context_attend/pallas_call | solution.py:247
  94.3 4.8 %context_attend.5.rest_0_ = bf16[512,1536]{1,0:T(8,128)(2,1)} custom-call(s32[3]{0:T(128)S(1)} %add_add_fusion.1.at_ref, s32[32]{0:T(128)S(1)} %copy-done.6, bf16[512,1536]{1,0:T(8,128)(2,1)S(1)} %copy-done.2, bf16[2,512,1536]{2,1,0:T(8,128)(2,1)S(1)} %copy-done, f32[32,512]{1,0:T(8,128)S(1)} %fusion.5.bias_ref, ...), custom_call_target="tpu_custom_call", output_to_operand_aliasing={{}: (7, {})} | custom-call | flops 805306368 | bytes 2359296 | tf_op jit(solution)/shard_map/context_attend/pallas_call | solution.py:247
  99.1 0.5 collective-permute-start.21
  99.6 0.1 add_add_fusion.3.at_ref
  99.7 0.1 add_add_fusion.at_ref
  99.8 1.4 %copy-done.3 = bf16[512,1536]{1,0:T(8,128)(2,1)S(1)} copy-done((bf16[512,1536]{1,0:T(8,128)(2,1)S(1)}, bf16[512,1536]{1,0:T(8,128)(2,1)}, u32[]{:S(2)}) %copy-start.3) | copy-done | bytes 1572888
  101.2 4.8 %context_attend.6.rest_0_ = bf16[512,1536]{1,0:T(8,128)(2,1)} custom-call(s32[3]{0:T(128)S(1)} %add_add_fusion.3.at_ref, s32[32]{0:T(128)S(1)} %copy-done.6, bf16[512,1536]{1,0:T(8,128)(2,1)S(1)} %copy-done.3, bf16[2,512,1536]{2,1,0:T(8,128)(2,1)S(1)} %copy-done, f32[32,512]{1,0:T(8,128)S(1)} %fusion.5.bias_ref, ...), custom_call_target="tpu_custom_call", output_to_operand_aliasing={{}: (7, {})} | custom-call | flops 805306368 | bytes 2359296 | tf_op jit(solution)/shard_map/context_attend/pallas_call | solution.py:247
  106.0 4.8 %context_attend.7 = bf16[512,1536]{1,0:T(8,128)(2,1)} custom-call(s32[3]{0:T(128)S(1)} %add_add_fusion.at_ref, s32[32]{0:T(128)S(1)} %copy-done.6, bf16[512,1536]{1,0:T(8,128)(2,1)S(1)} %copy-done.3, bf16[2,512,1536]{2,1,0:T(8,128)(2,1)S(1)} %copy-done, f32[32,512]{1,0:T(8,128)S(1)} %fusion.5.bias_ref, ...), custom_call_target="tpu_custom_call", output_to_operand_aliasing={{}: (7, {})} | custom-call | flops 805306368 | bytes 2359296 | tf_op jit(solution)/shard_map/context_attend/pallas_call | solution.py:247
  110.8 2.5 %convert_element_type.10.in_ref = f32[8,136,384]{2,1,0:T(8,128)} convert(f16[8,136,384]{2,1,0:T(8,128)(2,1)} %all-to-all-done.1) | non-fusion elementwise | flops 417792 | bytes 2506752 | tf_op jit(solution)/shard_map/convert_element_type | solution.py:355
  113.3 2.7 %combine_groups.1 = bf16[128,384]{1,0:T(8,128)(2,1)} custom-call(f32[8,136,384]{2,1,0:T(8,128)} %convert_element_type.10.in_ref), custom_call_target="tpu_custom_call" | custom-call | flops 835584 | bytes 1671168 | tf_op jit(solution)/shard_map/combine_groups/pallas_call | solution.py:192
  (54 shorter events, 0.6 us)
Async XLA Ops:
  4.5 14.7 %collective-permute-start.2 = (bf16[2,256,768]{2,1,0:T(8,128)(2,1)}, bf16[2,256,768]{2,1,0:T(8,128)(2,1)S(1)}, u32[]{:S(2)}, u32[]{:S(2)}) collective-permute-start(bf16[2,256,768]{2,1,0:T(8,128)(2,1)} %get-tuple-element.24), channel_id=1, source_target_pairs={{0,4}} | collective-permute-start | bytes 2359304 | tf_op jit(solution)/shard_map/ppermute | solution.py:291
  9.4 18.4 %collective-permute-start = (bf16[256,768]{1,0:T(8,128)(2,1)}, bf16[256,768]{1,0:T(8,128)(2,1)}, u32[]{:S(2)}, u32[]{:S(2)}) collective-permute-start(bf16[256,768]{1,0:T(8,128)(2,1)} %get-tuple-element.22), channel_id=1, source_target_pairs={{0,6}} | collective-permute-start | bytes 1179656 | tf_op jit(solution)/shard_map/ppermute | solution.py:291
  11.8 16.0 %collective-permute-start.1 = (bf16[256,768]{1,0:T(8,128)(2,1)}, bf16[256,768]{1,0:T(8,128)(2,1)}, u32[]{:S(2)}, u32[]{:S(2)}) collective-permute-start(bf16[256,768]{1,0:T(8,128)(2,1)} %get-tuple-element.23), channel_id=1, source_target_pairs={{0,2}} | collective-permute-start | bytes 1179656 | tf_op jit(solution)/shard_map/ppermute | solution.py:291
  13.9 18.0 %collective-permute-start.6 = (bf16[256,768]{1,0:T(8,128)(2,1)}, bf16[256,768]{1,0:T(8,128)(2,1)S(1)}, u32[]{:S(2)}, u32[]{:S(2)}) collective-permute-start(bf16[256,768]{1,0:T(8,128)(2,1)} %get-tuple-element.25), channel_id=1, source_target_pairs={{0,6}} | collective-permute-start | bytes 1179656 | tf_op jit(solution)/shard_map/ppermute | solution.py:291
  15.2 17.1 %collective-permute-start.7 = (bf16[256,768]{1,0:T(8,128)(2,1)}, bf16[256,768]{1,0:T(8,128)(2,1)}, u32[]{:S(2)}, u32[]{:S(2)}) collective-permute-start(bf16[256,768]{1,0:T(8,128)(2,1)} %get-tuple-element.26), channel_id=1, source_target_pairs={{0,2}} | collective-permute-start | bytes 1179656 | tf_op jit(solution)/shard_map/ppermute | solution.py:291
  19.2 0.9 copy-start.8
  20.1 7.7 %copy-start = (bf16[2,512,1536]{2,1,0:T(8,128)(2,1)S(1)}, bf16[2,512,1536]{2,1,0:T(8,128)(2,1)}, u32[]{:S(2)}) copy-start(bf16[2,512,1536]{2,1,0:T(8,128)(2,1)} %kv_ref.9) | copy-start | bytes 9437188
  20.1 42.9 %all-to-all-start = ((bf16[4,2,512,384]{3,2,1,0:T(8,128)(2,1)}), bf16[4,2,512,384]{3,2,1,0:T(8,128)(2,1)}, u32[]{:S(2)}, u32[]{:S(2)}) async-start(bf16[4,2,512,384]{3,2,1,0:T(8,128)(2,1)} %get-tuple-element.29), calls=%async_computation | async-start | bytes 6291456 | tf_op jit(solution)/shard_map/all_to_all | solution.py:323
  27.8 1.5 %copy-start.9 = (bf16[2,256,768]{2,1,0:T(8,128)(2,1)S(1)}, bf16[2,256,768]{2,1,0:T(8,128)(2,1)}, u32[]{:S(2)}) copy-start(bf16[2,256,768]{2,1,0:T(8,128)(2,1)} %copy-done.8) | copy-start | bytes 2359300
  29.2 4.2 %copy-start.10 = (bf16[128,384]{1,0:T(8,128)(2,1)S(1)}, bf16[128,384]{1,0:T(8,128)(2,1)}, u32[]{:S(2)}) copy-start(bf16[128,384]{1,0:T(8,128)(2,1)} %param.10) | copy-start | bytes 294916
  29.3 17.9 %copy-start.6 = (s32[32]{0:T(128)S(1)}, s32[32]{0:T(128)}, u32[]{:S(2)}) copy-start(s32[32]{0:T(128)} %len_ref.7) | copy-start | bytes 388
  29.3 17.9 %copy-start.11 = (pred[32,512]{1,0:T(8,128)(4,1)S(1)}, pred[32,512]{1,0:T(8,128)(4,1)}, u32[]{:S(2)}) copy-start(pred[32,512]{1,0:T(8,128)(4,1)} %ge.11) | copy-start | bytes 49156
  29.3 9.8 %collective-permute-start.3 = (bf16[256,384]{1,0:T(8,128)(2,1)S(1)}, bf16[256,384]{1,0:T(8,128)(2,1)S(1)}, u32[]{:S(2)}, u32[]{:S(2)}) collective-permute-start(bf16[256,384]{1,0:T(8,128)(2,1)S(1)} %slice.34), channel_id=1, source_target_pairs={{0,1},{2,3},{4,5},{6,7},{8,9},{10,11},{12,13},{14,15},{16,17},{18,... | collective-permute-start | bytes 589832 | tf_op jit(solution)/shard_map/ppermute | solution.py:307
  33.4 13.9 %collective-permute-start.13 = (bf16[128,384]{1,0:T(8,128)(2,1)S(1)}, bf16[128,384]{1,0:T(8,128)(2,1)S(1)}, u32[]{:S(2)}, u32[]{:S(2)}) collective-permute-start(bf16[128,384]{1,0:T(8,128)(2,1)S(1)} %copy-done.10), channel_id=1, source_target_pairs={{0,8},{4,12},{8,0},{12,4},{16,24},{20,28},{24,16},{28,20},{1,9},{5... | collective-permute-start | bytes 294920 | tf_op jit(solution)/shard_map/ppermute | solution.py:276
  33.5 13.9 %collective-permute-start.14 = (bf16[128,384]{1,0:T(8,128)(2,1)S(1)}, bf16[128,384]{1,0:T(8,128)(2,1)S(1)}, u32[]{:S(2)}, u32[]{:S(2)}) collective-permute-start(bf16[128,384]{1,0:T(8,128)(2,1)S(1)} %copy-done.10), channel_id=1, source_target_pairs={{0,16},{4,20},{8,24},{12,28},{16,0},{20,4},{24,8},{28,12},{1,17},{... | collective-permute-start | bytes 294920 | tf_op jit(solution)/shard_map/ppermute | solution.py:276
  33.5 13.8 %collective-permute-start.15 = (bf16[128,384]{1,0:T(8,128)(2,1)S(1)}, bf16[128,384]{1,0:T(8,128)(2,1)S(1)}, u32[]{:S(2)}, u32[]{:S(2)}) collective-permute-start(bf16[128,384]{1,0:T(8,128)(2,1)S(1)} %copy-done.10), channel_id=1, source_target_pairs={{0,24},{4,28},{8,16},{12,20},{16,8},{20,12},{24,0},{28,4},{1,25},{... | collective-permute-start | bytes 294920 | tf_op jit(solution)/shard_map/ppermute | solution.py:276
  37.9 2.7 %collective-permute-start.8 = (bf16[256,384]{1,0:T(8,128)(2,1)S(1)}, bf16[256,384]{1,0:T(8,128)(2,1)S(1)}, u32[]{:S(2)}, u32[]{:S(2)}) collective-permute-start(bf16[256,384]{1,0:T(8,128)(2,1)S(1)} %slice.37), channel_id=1, source_target_pairs={{0,1},{2,3},{4,5},{6,7},{8,9},{10,11},{12,13},{14,15},{16,17},{18,... | collective-permute-start | bytes 589832 | tf_op jit(solution)/shard_map/ppermute | solution.py:307
  39.2 6.6 %collective-permute-start.4 = (bf16[256,384]{1,0:T(8,128)(2,1)S(1)}, bf16[256,384]{1,0:T(8,128)(2,1)S(1)}, u32[]{:S(2)}, u32[]{:S(2)}) collective-permute-start(bf16[256,384]{1,0:T(8,128)(2,1)S(1)} %slice_add_fusion.1), channel_id=1, source_target_pairs={{0,16},{4,20},{1,17},{5,21},{2,18},{6,22},{3,19},{7,23}} | collective-permute-start | bytes 589832 | tf_op jit(solution)/shard_map/ppermute | solution.py:311
  40.6 9.6 %collective-permute-start.9 = (bf16[256,384]{1,0:T(8,128)(2,1)S(1)}, bf16[256,384]{1,0:T(8,128)(2,1)S(1)}, u32[]{:S(2)}, u32[]{:S(2)}) collective-permute-start(bf16[256,384]{1,0:T(8,128)(2,1)S(1)} %slice_add_fusion), channel_id=1, source_target_pairs={{0,16},{4,20},{1,17},{5,21},{2,18},{6,22},{3,19},{7,23}} | collective-permute-start | bytes 589832 | tf_op jit(solution)/shard_map/ppermute | solution.py:311
  45.9 10.7 %collective-permute-start.5 = (bf16[256,384]{1,0:T(8,128)(2,1)S(1)}, bf16[256,384]{1,0:T(8,128)(2,1)S(1)}, u32[]{:S(2)}, u32[]{:S(2)}) collective-permute-start(bf16[256,384]{1,0:T(8,128)(2,1)S(1)} %add.55), channel_id=1, source_target_pairs={{0,8},{4,12},{16,24},{20,28},{1,9},{5,13},{17,25},{21,29},{2,10},{... | collective-permute-start | bytes 589832 | tf_op jit(solution)/shard_map/ppermute | solution.py:311
  47.4 18.1 %copy-start.7 = (bf16[2,128,384]{2,1,0:T(8,128)(2,1)S(1)}, bf16[2,128,384]{2,1,0:T(8,128)(2,1)}, u32[]{:S(2)}) copy-start(bf16[2,128,384]{2,1,0:T(8,128)(2,1)} %sk_ref.3) | copy-start | bytes 589828
  48.2 17.3 %collective-permute-start.16 = (bf16[4,128,384]{2,1,0:T(8,128)(2,1)}, bf16[4,128,384]{2,1,0:T(8,128)(2,1)}, u32[]{:S(2)}, u32[]{:S(2)}) collective-permute-start(bf16[4,128,384]{2,1,0:T(8,128)(2,1)} %pad_maximum_fusion.1.near_ref), channel_id=1, source_target_pairs={{0,4},{4,0},{8,12},{12,8},{16,20},{20,16},{24,28},{28,24},{1,5},{5... | collective-permute-start | bytes 1179656 | tf_op jit(solution)/shard_map/ppermute | solution.py:276
  50.2 9.6 %collective-permute-start.10 = (bf16[256,384]{1,0:T(8,128)(2,1)S(1)}, bf16[256,384]{1,0:T(8,128)(2,1)S(1)}, u32[]{:S(2)}, u32[]{:S(2)}) collective-permute-start(bf16[256,384]{1,0:T(8,128)(2,1)S(1)} %add.61), channel_id=1, source_target_pairs={{0,8},{4,12},{16,24},{20,28},{1,9},{5,13},{17,25},{21,29},{2,10},{... | collective-permute-start | bytes 589832 | tf_op jit(solution)/shard_map/ppermute | solution.py:311
  60.6 14.2 %collective-permute-start.11 = (bf16[2,256,384]{2,1,0:T(8,128)(2,1)}, bf16[2,256,384]{2,1,0:T(8,128)(2,1)}, u32[]{:S(2)}, u32[]{:S(2)}) collective-permute-start(bf16[2,256,384]{2,1,0:T(8,128)(2,1)} %pad_maximum_fusion.near_ref), channel_id=1, source_target_pairs={{0,4},{4,0},{8,12},{12,8},{16,20},{20,16},{24,28},{28,24},{1,5},{5... | collective-permute-start | bytes 1179656 | tf_op jit(solution)/shard_map/ppermute | solution.py:276
  60.6 19.6 %collective-permute-start.18 = (bf16[2,256,384]{2,1,0:T(8,128)(2,1)}, bf16[2,256,384]{2,1,0:T(8,128)(2,1)}, u32[]{:S(2)}, u32[]{:S(2)}) collective-permute-start(bf16[2,256,384]{2,1,0:T(8,128)(2,1)} %pad_maximum_fusion.near_ref), channel_id=1, source_target_pairs={{0,1},{1,0},{2,3},{3,2},{4,5},{5,4},{6,7},{7,6},{8,9},{9,8},{10,11... | collective-permute-start | bytes 1179656 | tf_op jit(solution)/shard_map/ppermute | solution.py:276
  63.0 11.8 %collective-permute-start.12 = (bf16[2,256,384]{2,1,0:T(8,128)(2,1)}, bf16[2,256,384]{2,1,0:T(8,128)(2,1)}, u32[]{:S(2)}, u32[]{:S(2)}) collective-permute-start(bf16[2,256,384]{2,1,0:T(8,128)(2,1)} %pad_maximum_fusion.near_ref), channel_id=1, source_target_pairs={{0,2},{1,3},{2,0},{3,1},{4,6},{5,7},{6,4},{7,5},{8,10},{9,11},{10,... | collective-permute-start | bytes 1179656 | tf_op jit(solution)/shard_map/ppermute | solution.py:276
  74.8 5.5 %collective-permute-start.19 = (bf16[2,256,384]{2,1,0:T(8,128)(2,1)}, bf16[2,256,384]{2,1,0:T(8,128)(2,1)S(1)}, u32[]{:S(2)}, u32[]{:S(2)}) collective-permute-start(bf16[2,256,384]{2,1,0:T(8,128)(2,1)} %collective-permute-done.11.far_ref), channel_id=1, source_target_pairs={{0,1},{1,0},{2,3},{3,2},{4,5},{5,4},{6,7},{7,6},{8,9},{9,8},{10,11... | collective-permute-start | bytes 1179656 | tf_op jit(solution)/shard_map/ppermute | solution.py:276
  80.3 0.7 copy-start.4
  82.0 28.8 %all-to-all-start.1 = ((f16[8,136,384]{2,1,0:T(8,128)(2,1)}), f16[8,136,384]{2,1,0:T(8,128)(2,1)}, u32[]{:S(2)}, u32[]{:S(2)}) async-start(f16[8,136,384]{2,1,0:T(8,128)(2,1)} %convert_element_type.9), calls=%async_computation.1 | async-start | bytes 1671168 | tf_op jit(solution)/shard_map/all_to_all | solution.py:339
  86.4 12.7 %collective-permute-start.17 = (bf16[2,256,384]{2,1,0:T(8,128)(2,1)}, bf16[2,256,384]{2,1,0:T(8,128)(2,1)}, u32[]{:S(2)}, u32[]{:S(2)}) collective-permute-start(bf16[2,256,384]{2,1,0:T(8,128)(2,1)} %collective-permute-done.11.far_ref), channel_id=1, source_target_pairs={{0,2},{1,3},{2,0},{3,1},{4,6},{5,7},{6,4},{7,5},{8,10},{9,11},{10,... | collective-permute-start | bytes 1179656 | tf_op jit(solution)/shard_map/ppermute | solution.py:276
  88.0 1.4 %copy-start.1 = (bf16[512,1536]{1,0:T(8,128)(2,1)S(1)}, bf16[512,1536]{1,0:T(8,128)(2,1)}, u32[]{:S(2)}) copy-start(bf16[512,1536]{1,0:T(8,128)(2,1)} %q_ref.7) | copy-start | bytes 4718596
  89.4 4.9 %copy-start.2 = (bf16[512,1536]{1,0:T(8,128)(2,1)S(1)}, bf16[512,1536]{1,0:T(8,128)(2,1)}, u32[]{:S(2)}) copy-start(bf16[512,1536]{1,0:T(8,128)(2,1)} %q_ref.7) | copy-start | bytes 4718596
  89.4 4.9 %copy-start.5 = (bf16[2,256,384]{2,1,0:T(8,128)(2,1)S(1)}, bf16[2,256,384]{2,1,0:T(8,128)(2,1)}, u32[]{:S(2)}) copy-start(bf16[2,256,384]{2,1,0:T(8,128)(2,1)} %copy-done.4) | copy-start | bytes 1179652
  99.1 6.9 %collective-permute-start.20 = (bf16[2,256,384]{2,1,0:T(8,128)(2,1)}, bf16[2,256,384]{2,1,0:T(8,128)(2,1)}, u32[]{:S(2)}, u32[]{:S(2)}) collective-permute-start(bf16[2,256,384]{2,1,0:T(8,128)(2,1)} %collective-permute-done.12.near_ref), channel_id=1, source_target_pairs={{0,1},{1,0},{2,3},{3,2},{4,5},{5,4},{6,7},{7,6},{8,9},{9,8},{10,11... | collective-permute-start | bytes 1179656 | tf_op jit(solution)/shard_map/ppermute | solution.py:276
  99.1 6.9 %collective-permute-start.21 = (bf16[2,256,384]{2,1,0:T(8,128)(2,1)}, bf16[2,256,384]{2,1,0:T(8,128)(2,1)}, u32[]{:S(2)}, u32[]{:S(2)}) collective-permute-start(bf16[2,256,384]{2,1,0:T(8,128)(2,1)} %collective-permute-done.17.far_ref), channel_id=1, source_target_pairs={{0,1},{1,0},{2,3},{3,2},{4,5},{5,4},{6,7},{7,6},{8,9},{9,8},{10,11... | collective-permute-start | bytes 1179656 | tf_op jit(solution)/shard_map/ppermute | solution.py:276
  99.8 1.4 %copy-start.3 = (bf16[512,1536]{1,0:T(8,128)(2,1)S(1)}, bf16[512,1536]{1,0:T(8,128)(2,1)}, u32[]{:S(2)}) copy-start(bf16[512,1536]{1,0:T(8,128)(2,1)} %q_ref.7) | copy-start | bytes 4718596

commit v11 on v10

--- a/solution.py
+++ b/solution.py
@@ -199,11 +199,23 @@
     )(parts)
 
 
-def context_kernel(at_ref, len_ref, q_ref, kv_ref, bias_ref, near_ref, far_ref, *rest):
-    out_ref, diag_ref = rest[-2:]
+def context_kernel(at_ref, len_ref, bias_ref, *refs):
+    sources, (out_ref, diag_ref, *held, came) = refs[:4], refs[-7:]
+    q_ref, kv_ref, near_ref, far_ref = held
     block, odd = at_ref[0], at_ref[2]
     rows, width = q_ref.shape
     half = rows // 2
+    loads = {}
+    for first in range(0, width, HSZ):
+        there = pl.ds(pl.multiple_of(at_ref[1] * width, HSZ) + first, HSZ)
+        here = pl.ds(first, HSZ)
+        places = [(slice(None), there), (slice(None), slice(None), there)] + [(slice(None), slice(None), here)] * 2
+        loads[first] = [
+            pltpu.make_async_copy(source.at[place], to.at[(*place[:-1], here)], came.at[first // HSZ, n])
+            for n, (source, place, to) in enumerate(zip(sources, places, held))
+        ]
+        for load in loads[first]:
+            load.start()
     own = bias_ref[pl.ds(block, 1), :]
     row = lax.broadcasted_iota(jnp.int32, (half, half), 0)
     col = lax.broadcasted_iota(jnp.int32, (half, half), 1)
@@ -217,6 +229,9 @@
     def score(task):
         first, t = task
         head = slice(first, first + HSZ)
+        if t == 0:
+            for load in loads[first]:
+                load.wait()
         q = q_ref[t * half : (t + 1) * half, head]
         scores = [dot_t(q, near_ref[0, :, head]) + near_bias, dot_t(q, far_ref[0, :, head]) + far_bias]
         if t == 1:
@@ -242,23 +257,23 @@
     rows, width = q.shape
     _, half, wide = near.shape
     heads = wide // HSZ
-    both = lambda i, at, n: (0, 0, at[1])
     more = [] if before is None else [before]
+    anywhere = pl.BlockSpec(memory_space=pl.ANY)
     return pl.pallas_call(
         context_kernel,
         grid_spec=pltpu.PrefetchScalarGridSpec(
             num_scalar_prefetch=2,
             grid=(1,),
-            in_specs=[
-                pl.BlockSpec((rows, wide), lambda i, at, n: (0, at[1])),
-                pl.BlockSpec((2, rows, wide), both),
-                pl.BlockSpec(bias.shape, lambda i, *_: (0, 0)),
-                pl.BlockSpec((2, half, wide), lambda i, *_: (0, 0, 0)),
-                pl.BlockSpec((2, half, wide), lambda i, *_: (0, 0, 0)),
-            ]
-            + [pl.BlockSpec(memory_space=pl.ANY) for _ in more],
+            in_specs=[pl.BlockSpec(bias.shape, lambda i, *_: (0, 0))] + [anywhere] * (4 + len(more)),
             out_specs=pl.BlockSpec((rows, wide), lambda i, at, n: (0, at[1])),
-            scratch_shapes=[pltpu.VMEM((2, half, half), jnp.float32)],
+            scratch_shapes=[
+                pltpu.VMEM((2, half, half), jnp.float32),
+                pltpu.VMEM((rows, wide), q.dtype),
+                pltpu.VMEM((2, rows, wide), kv.dtype),
+                pltpu.VMEM((2, half, wide), near.dtype),
+                pltpu.VMEM((2, half, wide), far.dtype),
+                pltpu.SemaphoreType.DMA((heads, 4)),
+            ],
         ),
         out_shape=jax.ShapeDtypeStruct((rows, width), q.dtype),
         input_output_aliases={7: 0} if more else {},
@@ -269,7 +284,7 @@
             transcendentals=2 * rows * rows * heads,
         ),
         name="context_attend",
-    )(at, lengths, q, kv, bias, near, far, *more)
+    )(at, lengths, bias, q, kv, near, far, *more)
 
 
 def swap(x, axis, k):
@@ -326,15 +341,11 @@
     seen = (token_ids.reshape(-1, rows) >= NAMB) & (jnp.arange(rows)[None, :] < lengths[:, None])
     bias = jnp.where(seen, 0.0, NEG).astype(jnp.float32)
     suffix = functools.partial(suffix_attend, jnp.stack([host]), *gathered, swapped, suffix_kv, bias)
-    heads = suffix_queries.shape[1] // HSZ
-    early = max(1, heads - 1)
     far, other_near = swap(near, "hst", 1), swap(after(near, swapped), "grp", cores)
-    far, other_near, parts = lax.optimization_barrier((far, other_near, suffix(0, early, None)))
+    parts = suffix(0, suffix_queries.shape[1] // HSZ, None)
+    far, other_near, parts = lax.optimization_barrier((far, other_near, parts))
     other_far = swap(far, "grp", cores)
     by_core = [[swap(x, "grp", k) for x in (near, far)] for k in range(1, cores)]
-    if heads > early:
-        parts = suffix(early, heads - early, parts)
-    by_core, parts = lax.optimization_barrier((by_core, parts))
     parts = parts.astype(jnp.float16)
     coded = lax.all_to_all(parts, "hst", split_axis=0, concat_axis=0, tiled=True)
     held = {0: after([near, far], parts), cores: [other_near, other_far]}

time: 117 us -> 120 us (1.026)
  waiting for transfers between devices: 11.8 us -> 16.9 us
  starting transfers between devices: 47.1 us -> 43 us
  local copies, waits for them, and re-layouts: 5.93 us -> 7.35 us
    ppermute x4, starting transfers between devices: 10.3 us -> 5.84 us  [spread_anchor(): piece = piece + lax.ppermute(piece, 'hst', pairs)]
    ppermute x5, waiting for transfers between devices: 2.34 us -> 6.75 us  [scatter_anchor(): send = lambda x, to: lax.ppermute(x, BOTH, [(0, to)])]
    ppermute x4, waiting for transfers between devices: 7.1 us -> 10.1 us  [spread_anchor(): piece = piece + lax.ppermute(piece, 'hst', pairs)]
    all_to_all x1, waiting for transfers between devices: 2.37 us -> 0.01 us  [per_device(): lax.all_to_all(after(packed, down), 'grp', split_axis=0, concat_axis=0, t...]
    pallas_call x4, Pallas kernels: 19.3 us -> 20.9 us  [context_attend(): pl.pallas_call(context_kernel, grid_spec=pltpu.PrefetchScalarGridSpec(num...]
    pallas_call x2 -> x1, Pallas kernels: 14.7 us -> 13.3 us  [suffix_attend(): pl.pallas_call(suffix_kernel, grid_spec=pltpu.PrefetchScalarGridSpec(num_...]
    unnamed x24 -> x26, local copies, waits for them, and re-layouts: 4.52 us -> 5.27 us
  transfers between devices with their start and end apart: 24 -> 24, of which waited for: 5 -> 6; matrix products, arithmetic and copies ran while one was open for 6% -> 7% of each run, Pallas kernels for 29% -> 29%
where the time goes in v11:
time: 120 us; the launch traced here: 119 us
  starting transfers between devices  43 us (36%)
  Pallas kernels  40.8 us (34%)
  waiting for transfers between devices  16.9 us (14%)
  other arithmetic  9.81 us (8%)
  local copies, waits for them, and re-layouts  7.35 us (6%)
    pallas_call x4, Pallas kernels, context_attend(): pl.pallas_call(context_kernel, grid_spec=pltpu.PrefetchScalarGridSpec(num...  20.9 us
    pallas_call x1, Pallas kernels, suffix_attend(): pl.pallas_call(suffix_kernel, grid_spec=pltpu.PrefetchScalarGridSpec(num_...  13.3 us
    ppermute x5, starting transfers between devices, scatter_anchor(): send = lambda x, to: lax.ppermute(x, BOTH, [(0, to)])  12.4 us
    ppermute x11, starting transfers between devices, swap(): lax.ppermute(x, axis, [(i, i ^ k) for i in range(lax.axis_size(axis))])  11.3 us
    ppermute x4, waiting for transfers between devices, spread_anchor(): piece = piece + lax.ppermute(piece, 'hst', pairs)  10.1 us
    ppermute x5, waiting for transfers between devices, scatter_anchor(): send = lambda x, to: lax.ppermute(x, BOTH, [(0, to)])  6.75 us
    ppermute x4, starting transfers between devices, spread_anchor(): piece = piece + lax.ppermute(piece, 'hst', pairs)  5.84 us
    all_to_all x1, starting transfers between devices, per_device(): lax.all_to_all(parts, 'hst', split_axis=0, concat_axis=0, tiled=True)  5.32 us
  transfers between devices with their start and end apart: 24, of which 6 were waited for; matrix products, arithmetic and copies ran while one was open for 7% of the time, Pallas kernels for 29%

profile of v11, /device:TPU:0, one launch (start us, length us, event | category | flops | bytes accessed | tf_op | source)
XLA Modules:
  0.0 118.9 jit_solution(8674528008000315639)
XLA Ops:
  0.6 3.9 %pack_heads.1 = (bf16[4,2,512,384]{3,2,1,0:T(8,128)(2,1)}, bf16[2,256,768]{2,1,0:T(8,128)(2,1)}, bf16[256,768]{1,0:T(8,128)(2,1)}, bf16[256,768]{1,0:T(8,128)(2,...) custom-call(bf16[2,512,1536]{2,1,0:T(8,128)(2,1)} %refs_1_.7), custom_call_target="tpu_custom_call" | custom-call | bytes 9437184 | tf_op jit(solution)/shard_map/pack_heads/pallas_call | solution.py:66
  4.5 4.9 %collective-permute-start.2 = (bf16[2,256,768]{2,1,0:T(8,128)(2,1)}, bf16[2,256,768]{2,1,0:T(8,128)(2,1)S(1)}, u32[]{:S(2)}, u32[]{:S(2)}) collective-permute-start(bf16[2,256,768]{2,1,0:T(8,128)(2,1)} %get-tuple-element.21), channel_id=1, source_target_pairs={{0,4}} | collective-permute-start | bytes 2359304 | tf_op jit(solution)/shard_map/ppermute | solution.py:306
  9.4 1.3 %collective-permute-start.1 = (bf16[256,768]{1,0:T(8,128)(2,1)}, bf16[256,768]{1,0:T(8,128)(2,1)S(1)}, u32[]{:S(2)}, u32[]{:S(2)}) collective-permute-start(bf16[256,768]{1,0:T(8,128)(2,1)} %get-tuple-element.20), channel_id=1, source_target_pairs={{0,2}} | collective-permute-start | bytes 1179656 | tf_op jit(solution)/shard_map/ppermute | solution.py:306
  10.7 2.1 %collective-permute-start = (bf16[256,768]{1,0:T(8,128)(2,1)}, bf16[256,768]{1,0:T(8,128)(2,1)}, u32[]{:S(2)}, u32[]{:S(2)}) collective-permute-start(bf16[256,768]{1,0:T(8,128)(2,1)} %get-tuple-element.19), channel_id=1, source_target_pairs={{0,6}} | collective-permute-start | bytes 1179656 | tf_op jit(solution)/shard_map/ppermute | solution.py:306
  12.8 2.1 %collective-permute-start.7 = (bf16[256,768]{1,0:T(8,128)(2,1)}, bf16[256,768]{1,0:T(8,128)(2,1)}, u32[]{:S(2)}, u32[]{:S(2)}) collective-permute-start(bf16[256,768]{1,0:T(8,128)(2,1)} %get-tuple-element.23), channel_id=1, source_target_pairs={{0,2}} | collective-permute-start | bytes 1179656 | tf_op jit(solution)/shard_map/ppermute | solution.py:306
  14.9 2.1 %collective-permute-start.6 = (bf16[256,768]{1,0:T(8,128)(2,1)}, bf16[256,768]{1,0:T(8,128)(2,1)}, u32[]{:S(2)}, u32[]{:S(2)}) collective-permute-start(bf16[256,768]{1,0:T(8,128)(2,1)} %get-tuple-element.22), channel_id=1, source_target_pairs={{0,6}} | collective-permute-start | bytes 1179656 | tf_op jit(solution)/shard_map/ppermute | solution.py:306
  16.9 2.2 %collective-permute-done.2 = bf16[2,256,768]{2,1,0:T(8,128)(2,1)S(1)} collective-permute-done((bf16[2,256,768]{2,1,0:T(8,128)(2,1)}, bf16[2,256,768]{2,1,0:T(8,128)(2,1)S(1)}, u32[]{:S(2)}, u32[]{:S(2)}) %collective-permute-start.2) | collective-permute-done | bytes 786464 | tf_op jit(solution)/shard_map/ppermute | solution.py:306
  19.2 0.9 copy-done.7
  20.1 4.9 %all-to-all-start = ((bf16[4,2,512,384]{3,2,1,0:T(8,128)(2,1)}), bf16[4,2,512,384]{3,2,1,0:T(8,128)(2,1)}, u32[]{:S(2)}, u32[]{:S(2)}) async-start(bf16[4,2,512,384]{3,2,1,0:T(8,128)(2,1)} %get-tuple-element.26), calls=%async_computation | async-start | bytes 6291456 | tf_op jit(solution)/shard_map/all_to_all | solution.py:338
  25.0 0.8 copy-done.9
  25.8 1.3 %fusion = bf16[256,768]{1,0:T(8,128)(2,1)S(1)} fusion(bf16[2,256,768]{2,1,0:T(8,128)(2,1)} %copy-done.7, bf16[256,768]{1,0:T(8,128)(2,1)} %copy-done.9, bf16[256,768]{1,0:T(8,128)(2,1)} %collective-permute-done, bf16[2,512,1536]{2,1,0:T(8,128)(2,1)S(1)} %copy-done, pred[]{:T(512)S(6)} %and.18), kind=kLoop, calls=%fused_computation.2 | loop fusion | flops 786432 | bytes 1966081 | tf_op jit(solution)/shard_map/add | solution.py:312
  27.2 4.5 %collective-permute-done.6 = bf16[256,768]{1,0:T(8,128)(2,1)} collective-permute-done((bf16[256,768]{1,0:T(8,128)(2,1)}, bf16[256,768]{1,0:T(8,128)(2,1)}, u32[]{:S(2)}, u32[]{:S(2)}) %collective-permute-start.6) | collective-permute-done | bytes 393248 | tf_op jit(solution)/shard_map/ppermute | solution.py:306
  31.7 1.2 fusion.2
  32.9 0.7 copy-done.6
  33.6 0.7 slice.37
  34.3 2.0 %collective-permute-start.8 = (bf16[256,384]{1,0:T(8,128)(2,1)}, bf16[256,384]{1,0:T(8,128)(2,1)}, u32[]{:S(2)}, u32[]{:S(2)}) collective-permute-start(bf16[256,384]{1,0:T(8,128)(2,1)} %slice.37), channel_id=1, source_target_pairs={{0,1},{2,3},{4,5},{6,7},{8,9},{10,11},{12,13},{14,15},{16,17},{18,... | collective-permute-start | bytes 589832 | tf_op jit(solution)/shard_map/ppermute | solution.py:322
  36.3 0.6 broadcast_compare_fusion
  36.9 1.3 %ge.11 = pred[32,512]{1,0:T(8,128)(4,1)} reshape(pred[16384]{0:T(1024)(128)(4,1)} %broadcast_compare_fusion) | data formatting | bytes 32768 | tf_op jit(solution)/shard_map/ge | solution.py:341
  38.4 4.3 %collective-permute-start.13 = (bf16[128,384]{1,0:T(8,128)(2,1)}, bf16[128,384]{1,0:T(8,128)(2,1)S(1)}, u32[]{:S(2)}, u32[]{:S(2)}) collective-permute-start(bf16[128,384]{1,0:T(8,128)(2,1)} %param.10), channel_id=1, source_target_pairs={{0,8},{4,12},{8,0},{12,4},{16,24},{20,28},{24,16},{28,20},{1,9},{5... | collective-permute-start | bytes 294920 | tf_op jit(solution)/shard_map/ppermute | solution.py:291
  42.7 1.3 %collective-permute-start.3 = (bf16[256,384]{1,0:T(8,128)(2,1)S(1)}, bf16[256,384]{1,0:T(8,128)(2,1)S(1)}, u32[]{:S(2)}, u32[]{:S(2)}) collective-permute-start(bf16[256,384]{1,0:T(8,128)(2,1)S(1)} %slice.34), channel_id=1, source_target_pairs={{0,1},{2,3},{4,5},{6,7},{8,9},{10,11},{12,13},{14,15},{16,17},{18,... | collective-permute-start | bytes 589832 | tf_op jit(solution)/shard_map/ppermute | solution.py:322
  44.1 1.0 slice_add_fusion
  45.1 1.9 %collective-permute-start.9 = (bf16[256,384]{1,0:T(8,128)(2,1)S(1)}, bf16[256,384]{1,0:T(8,128)(2,1)S(1)}, u32[]{:S(2)}, u32[]{:S(2)}) collective-permute-start(bf16[256,384]{1,0:T(8,128)(2,1)S(1)} %slice_add_fusion), channel_id=1, source_target_pairs={{0,16},{4,20},{1,17},{5,21},{2,18},{6,22},{3,19},{7,23}} | collective-permute-start | bytes 589832 | tf_op jit(solution)/shard_map/ppermute | solution.py:326
  47.1 1.3 %collective-permute-start.4 = (bf16[256,384]{1,0:T(8,128)(2,1)S(1)}, bf16[256,384]{1,0:T(8,128)(2,1)S(1)}, u32[]{:S(2)}, u32[]{:S(2)}) collective-permute-start(bf16[256,384]{1,0:T(8,128)(2,1)S(1)} %slice_add_fusion.1), channel_id=1, source_target_pairs={{0,16},{4,20},{1,17},{5,21},{2,18},{6,22},{3,19},{7,23}} | collective-permute-start | bytes 589832 | tf_op jit(solution)/shard_map/ppermute | solution.py:326
  48.4 3.9 %collective-permute-done.9 = bf16[256,384]{1,0:T(8,128)(2,1)S(1)} collective-permute-done((bf16[256,384]{1,0:T(8,128)(2,1)S(1)}, bf16[256,384]{1,0:T(8,128)(2,1)S(1)}, u32[]{:S(2)}, u32[]{:S(2)}) %collective-permute-start.9) | collective-permute-done | bytes 196640 | tf_op jit(solution)/shard_map/ppermute | solution.py:326
  52.3 1.3 %collective-permute-start.10 = (bf16[256,384]{1,0:T(8,128)(2,1)S(1)}, bf16[256,384]{1,0:T(8,128)(2,1)S(1)}, u32[]{:S(2)}, u32[]{:S(2)}) collective-permute-start(bf16[256,384]{1,0:T(8,128)(2,1)S(1)} %add.61), channel_id=1, source_target_pairs={{0,8},{4,12},{16,24},{20,28},{1,9},{5,13},{17,25},{21,29},{2,10},{... | collective-permute-start | bytes 589832 | tf_op jit(solution)/shard_map/ppermute | solution.py:326
  53.6 0.1 fusion.5.bias_ref
  53.8 0.8 pad_maximum_fusion.1.near_ref
  54.6 1.9 %collective-permute-done.4 = bf16[256,384]{1,0:T(8,128)(2,1)S(1)} collective-permute-done((bf16[256,384]{1,0:T(8,128)(2,1)S(1)}, bf16[256,384]{1,0:T(8,128)(2,1)S(1)}, u32[]{:S(2)}, u32[]{:S(2)}) %collective-permute-start.4) | collective-permute-done | bytes 196640 | tf_op jit(solution)/shard_map/ppermute | solution.py:326
  56.5 1.3 %collective-permute-start.5 = (bf16[256,384]{1,0:T(8,128)(2,1)S(1)}, bf16[256,384]{1,0:T(8,128)(2,1)S(1)}, u32[]{:S(2)}, u32[]{:S(2)}) collective-permute-start(bf16[256,384]{1,0:T(8,128)(2,1)S(1)} %add.55), channel_id=1, source_target_pairs={{0,8},{4,12},{16,24},{20,28},{1,9},{5,13},{17,25},{21,29},{2,10},{... | collective-permute-start | bytes 589832 | tf_op jit(solution)/shard_map/ppermute | solution.py:326
  57.8 2.3 %collective-permute-done.10 = bf16[256,384]{1,0:T(8,128)(2,1)S(1)} collective-permute-done((bf16[256,384]{1,0:T(8,128)(2,1)S(1)}, bf16[256,384]{1,0:T(8,128)(2,1)S(1)}, u32[]{:S(2)}, u32[]{:S(2)}) %collective-permute-start.10) | collective-permute-done | bytes 196640 | tf_op jit(solution)/shard_map/ppermute | solution.py:326
  60.2 2.1 %collective-permute-done.5 = bf16[256,384]{1,0:T(8,128)(2,1)S(1)} collective-permute-done((bf16[256,384]{1,0:T(8,128)(2,1)S(1)}, bf16[256,384]{1,0:T(8,128)(2,1)S(1)}, u32[]{:S(2)}, u32[]{:S(2)}) %collective-permute-start.5) | collective-permute-done | bytes 196640 | tf_op jit(solution)/shard_map/ppermute | solution.py:326
  62.3 0.8 pad_maximum_fusion.refs_2_
  63.1 3.9 %collective-permute-start.12 = (bf16[2,256,384]{2,1,0:T(8,128)(2,1)}, bf16[2,256,384]{2,1,0:T(8,128)(2,1)}, u32[]{:S(2)}, u32[]{:S(2)}) collective-permute-start(bf16[2,256,384]{2,1,0:T(8,128)(2,1)} %pad_maximum_fusion.refs_2_), channel_id=1, source_target_pairs={{0,2},{1,3},{2,0},{3,1},{4,6},{5,7},{6,4},{7,5},{8,10},{9,11},{10,... | collective-permute-start | bytes 1179656 | tf_op jit(solution)/shard_map/ppermute | solution.py:291
  67.0 13.3 %suffix_attend.1 = f32[8,136,384]{2,1,0:T(8,128)S(1)} custom-call(s32[1]{0:T(128)} %bitcast.9.at_ref, bf16[4,128,384]{2,1,0:T(8,128)(2,1)} %pad_maximum_fusion.1.near_ref, bf16[4,128,384]{2,1,0:T(8,128)(2,1)} %collective-permute-done.16.far_ref, bf16[4,2,512,384]{3,2,1,0:T(8,128)(2,1)} %all-to-all-done.kv_ref, bf16[2,128,384]{2,1,0:T(8,128)(2,1)S(1)} %copy-done.5, ...), custom_call_target="tpu_custom_call" | custom-call | flops 6845104128 | bytes 7864320 | tf_op jit(solution)/shard_map/suffix_attend/pallas_call | solution.py:148
  80.4 1.0 convert_element_type.9
  81.4 5.3 %all-to-all-start.1 = ((f16[8,136,384]{2,1,0:T(8,128)(2,1)}), f16[8,136,384]{2,1,0:T(8,128)(2,1)}, u32[]{:S(2)}, u32[]{:S(2)}) async-start(f16[8,136,384]{2,1,0:T(8,128)(2,1)} %convert_element_type.9), calls=%async_computation.1 | async-start | bytes 1671168 | tf_op jit(solution)/shard_map/all_to_all | solution.py:350
  86.7 0.5 collective-permute-start.19
  87.2 1.8 %collective-permute-start.17 = (bf16[2,256,384]{2,1,0:T(8,128)(2,1)}, bf16[2,256,384]{2,1,0:T(8,128)(2,1)}, u32[]{:S(2)}, u32[]{:S(2)}) collective-permute-start(bf16[2,256,384]{2,1,0:T(8,128)(2,1)} %collective-permute-done.11.refs_3_), channel_id=1, source_target_pairs={{0,2},{1,3},{2,0},{3,1},{4,6},{5,7},{6,4},{7,5},{8,10},{9,11},{10,... | collective-permute-start | bytes 1179656 | tf_op jit(solution)/shard_map/ppermute | solution.py:291
  89.2 1.4 %copy-done.1 = bf16[512,1536]{1,0:T(8,128)(2,1)S(1)} copy-done((bf16[512,1536]{1,0:T(8,128)(2,1)S(1)}, bf16[512,1536]{1,0:T(8,128)(2,1)}, u32[]{:S(2)}) %copy-start.1) | copy-done | bytes 1572888
  90.6 5.2 %context_attend.4.refs_4_ = bf16[512,1536]{1,0:T(8,128)(2,1)} custom-call(s32[3]{0:T(128)S(1)} %add_add_fusion.2.at_ref, s32[32]{0:T(128)S(1)} %copy-done.4, f32[32,512]{1,0:T(8,128)S(1)} %fusion.5.bias_ref, bf16[512,1536]{1,0:T(8,128)(2,1)S(1)} %copy-done.1, bf16[2,512,1536]{2,1,0:T(8,128)(2,1)S(1)} %copy-done, ...), custom_call_target="tpu_custom_call" | custom-call | flops 805306368 | bytes 2359296 | tf_op jit(solution)/shard_map/context_attend/pallas_call | solution.py:262
  95.9 5.2 %context_attend.5.refs_4_ = bf16[512,1536]{1,0:T(8,128)(2,1)} custom-call(s32[3]{0:T(128)S(1)} %add_add_fusion.1.at_ref, s32[32]{0:T(128)S(1)} %copy-done.4, f32[32,512]{1,0:T(8,128)S(1)} %fusion.5.bias_ref, bf16[512,1536]{1,0:T(8,128)(2,1)S(1)} %copy-done.2, bf16[2,512,1536]{2,1,0:T(8,128)(2,1)S(1)} %copy-done, ...), custom_call_target="tpu_custom_call", output_to_operand_aliasing={{}: (7, {})} | custom-call | flops 805306368 | bytes 2359296 | tf_op jit(solution)/shard_map/context_attend/pallas_call | solution.py:262
  101.2 0.5 collective-permute-start.21
  101.7 0.1 add_add_fusion.at_ref
  101.8 1.4 %copy-done.3 = bf16[512,1536]{1,0:T(8,128)(2,1)S(1)} copy-done((bf16[512,1536]{1,0:T(8,128)(2,1)S(1)}, bf16[512,1536]{1,0:T(8,128)(2,1)}, u32[]{:S(2)}) %copy-start.3) | copy-done | bytes 1572888
  103.2 5.2 %context_attend.6.refs_4_ = bf16[512,1536]{1,0:T(8,128)(2,1)} custom-call(s32[3]{0:T(128)S(1)} %add_add_fusion.3.at_ref, s32[32]{0:T(128)S(1)} %copy-done.4, f32[32,512]{1,0:T(8,128)S(1)} %fusion.5.bias_ref, bf16[512,1536]{1,0:T(8,128)(2,1)S(1)} %copy-done.3, bf16[2,512,1536]{2,1,0:T(8,128)(2,1)S(1)} %copy-done, ...), custom_call_target="tpu_custom_call", output_to_operand_aliasing={{}: (7, {})} | custom-call | flops 805306368 | bytes 2359296 | tf_op jit(solution)/shard_map/context_attend/pallas_call | solution.py:262
  108.5 5.2 %context_attend.7 = bf16[512,1536]{1,0:T(8,128)(2,1)} custom-call(s32[3]{0:T(128)S(1)} %add_add_fusion.at_ref, s32[32]{0:T(128)S(1)} %copy-done.4, f32[32,512]{1,0:T(8,128)S(1)} %fusion.5.bias_ref, bf16[512,1536]{1,0:T(8,128)(2,1)S(1)} %copy-done.3, bf16[2,512,1536]{2,1,0:T(8,128)(2,1)S(1)} %copy-done, ...), custom_call_target="tpu_custom_call", output_to_operand_aliasing={{}: (7, {})} | custom-call | flops 805306368 | bytes 2359296 | tf_op jit(solution)/shard_map/context_attend/pallas_call | solution.py:262
  113.7 2.5 %convert_element_type.10.in_ref = f32[8,136,384]{2,1,0:T(8,128)} convert(f16[8,136,384]{2,1,0:T(8,128)(2,1)} %all-to-all-done.1) | non-fusion elementwise | flops 417792 | bytes 2506752 | tf_op jit(solution)/shard_map/convert_element_type | solution.py:366
  116.2 2.7 %combine_groups.1 = bf16[128,384]{1,0:T(8,128)(2,1)} custom-call(f32[8,136,384]{2,1,0:T(8,128)} %convert_element_type.10.in_ref), custom_call_target="tpu_custom_call" | custom-call | flops 835584 | bytes 1671168 | tf_op jit(solution)/shard_map/combine_groups/pallas_call | solution.py:192
  (55 shorter events, 0.8 us)
Async XLA Ops:
  4.5 14.7 %collective-permute-start.2 = (bf16[2,256,768]{2,1,0:T(8,128)(2,1)}, bf16[2,256,768]{2,1,0:T(8,128)(2,1)S(1)}, u32[]{:S(2)}, u32[]{:S(2)}) collective-permute-start(bf16[2,256,768]{2,1,0:T(8,128)(2,1)} %get-tuple-element.21), channel_id=1, source_target_pairs={{0,4}} | collective-permute-start | bytes 2359304 | tf_op jit(solution)/shard_map/ppermute | solution.py:306
  9.4 15.6 %collective-permute-start.1 = (bf16[256,768]{1,0:T(8,128)(2,1)}, bf16[256,768]{1,0:T(8,128)(2,1)S(1)}, u32[]{:S(2)}, u32[]{:S(2)}) collective-permute-start(bf16[256,768]{1,0:T(8,128)(2,1)} %get-tuple-element.20), channel_id=1, source_target_pairs={{0,2}} | collective-permute-start | bytes 1179656 | tf_op jit(solution)/shard_map/ppermute | solution.py:306
  10.7 15.1 %collective-permute-start = (bf16[256,768]{1,0:T(8,128)(2,1)}, bf16[256,768]{1,0:T(8,128)(2,1)}, u32[]{:S(2)}, u32[]{:S(2)}) collective-permute-start(bf16[256,768]{1,0:T(8,128)(2,1)} %get-tuple-element.19), channel_id=1, source_target_pairs={{0,6}} | collective-permute-start | bytes 1179656 | tf_op jit(solution)/shard_map/ppermute | solution.py:306
  12.8 14.4 %collective-permute-start.7 = (bf16[256,768]{1,0:T(8,128)(2,1)}, bf16[256,768]{1,0:T(8,128)(2,1)}, u32[]{:S(2)}, u32[]{:S(2)}) collective-permute-start(bf16[256,768]{1,0:T(8,128)(2,1)} %get-tuple-element.23), channel_id=1, source_target_pairs={{0,2}} | collective-permute-start | bytes 1179656 | tf_op jit(solution)/shard_map/ppermute | solution.py:306
  14.9 16.8 %collective-permute-start.6 = (bf16[256,768]{1,0:T(8,128)(2,1)}, bf16[256,768]{1,0:T(8,128)(2,1)}, u32[]{:S(2)}, u32[]{:S(2)}) collective-permute-start(bf16[256,768]{1,0:T(8,128)(2,1)} %get-tuple-element.22), channel_id=1, source_target_pairs={{0,6}} | collective-permute-start | bytes 1179656 | tf_op jit(solution)/shard_map/ppermute | solution.py:306
  19.2 0.9 copy-start.7
  20.1 5.7 %copy-start = (bf16[2,512,1536]{2,1,0:T(8,128)(2,1)S(1)}, bf16[2,512,1536]{2,1,0:T(8,128)(2,1)}, u32[]{:S(2)}) copy-start(bf16[2,512,1536]{2,1,0:T(8,128)(2,1)} %refs_1_.7) | copy-start | bytes 9437188
  20.1 43.0 %all-to-all-start = ((bf16[4,2,512,384]{3,2,1,0:T(8,128)(2,1)}), bf16[4,2,512,384]{3,2,1,0:T(8,128)(2,1)}, u32[]{:S(2)}, u32[]{:S(2)}) async-start(bf16[4,2,512,384]{3,2,1,0:T(8,128)(2,1)} %get-tuple-element.26), calls=%async_computation | async-start | bytes 6291456 | tf_op jit(solution)/shard_map/all_to_all | solution.py:338
  25.0 2.1 %copy-start.8 = (bf16[2,256,768]{2,1,0:T(8,128)(2,1)S(1)}, bf16[2,256,768]{2,1,0:T(8,128)(2,1)}, u32[]{:S(2)}) copy-start(bf16[2,256,768]{2,1,0:T(8,128)(2,1)} %copy-done.7) | copy-start | bytes 2359300
  25.0 0.8 copy-start.9
  27.1 9.2 %copy-start.11 = (s32[16384]{0:T(1024)S(1)}, s32[16384]{0:T(1024)}, u32[]{:S(2)}) copy-start(s32[16384]{0:T(1024)} %param.8) | copy-start | bytes 196612
  32.9 0.7 copy-start.6
  33.6 20.0 %copy-start.4 = (s32[32]{0:T(128)S(1)}, s32[32]{0:T(128)}, u32[]{:S(2)}) copy-start(s32[32]{0:T(128)} %len_ref.7) | copy-start | bytes 388
  34.3 9.7 %collective-permute-start.8 = (bf16[256,384]{1,0:T(8,128)(2,1)}, bf16[256,384]{1,0:T(8,128)(2,1)}, u32[]{:S(2)}, u32[]{:S(2)}) collective-permute-start(bf16[256,384]{1,0:T(8,128)(2,1)} %slice.37), channel_id=1, source_target_pairs={{0,1},{2,3},{4,5},{6,7},{8,9},{10,11},{12,13},{14,15},{16,17},{18,... | collective-permute-start | bytes 589832 | tf_op jit(solution)/shard_map/ppermute | solution.py:322
  38.3 15.4 %copy-start.12 = (pred[32,512]{1,0:T(8,128)(4,1)S(1)}, pred[32,512]{1,0:T(8,128)(4,1)}, u32[]{:S(2)}) copy-start(pred[32,512]{1,0:T(8,128)(4,1)} %ge.11) | copy-start | bytes 49156
  38.3 15.5 %copy-start.10 = (bf16[128,384]{1,0:T(8,128)(2,1)S(1)}, bf16[128,384]{1,0:T(8,128)(2,1)}, u32[]{:S(2)}) copy-start(bf16[128,384]{1,0:T(8,128)(2,1)} %param.10) | copy-start | bytes 294916
  38.3 15.4 %collective-permute-start.15 = (bf16[128,384]{1,0:T(8,128)(2,1)}, bf16[128,384]{1,0:T(8,128)(2,1)S(1)}, u32[]{:S(2)}, u32[]{:S(2)}) collective-permute-start(bf16[128,384]{1,0:T(8,128)(2,1)} %param.10), channel_id=1, source_target_pairs={{0,24},{4,28},{8,16},{12,20},{16,8},{20,12},{24,0},{28,4},{1,25},{... | collective-permute-start | bytes 294920 | tf_op jit(solution)/shard_map/ppermute | solution.py:291
  38.4 15.4 %collective-permute-start.14 = (bf16[128,384]{1,0:T(8,128)(2,1)}, bf16[128,384]{1,0:T(8,128)(2,1)S(1)}, u32[]{:S(2)}, u32[]{:S(2)}) collective-permute-start(bf16[128,384]{1,0:T(8,128)(2,1)} %param.10), channel_id=1, source_target_pairs={{0,16},{4,20},{8,24},{12,28},{16,0},{20,4},{24,8},{28,12},{1,17},{... | collective-permute-start | bytes 294920 | tf_op jit(solution)/shard_map/ppermute | solution.py:291
  38.4 15.3 %collective-permute-start.13 = (bf16[128,384]{1,0:T(8,128)(2,1)}, bf16[128,384]{1,0:T(8,128)(2,1)S(1)}, u32[]{:S(2)}, u32[]{:S(2)}) collective-permute-start(bf16[128,384]{1,0:T(8,128)(2,1)} %param.10), channel_id=1, source_target_pairs={{0,8},{4,12},{8,0},{12,4},{16,24},{20,28},{24,16},{28,20},{1,9},{5... | collective-permute-start | bytes 294920 | tf_op jit(solution)/shard_map/ppermute | solution.py:291
  42.7 4.3 %collective-permute-start.3 = (bf16[256,384]{1,0:T(8,128)(2,1)S(1)}, bf16[256,384]{1,0:T(8,128)(2,1)S(1)}, u32[]{:S(2)}, u32[]{:S(2)}) collective-permute-start(bf16[256,384]{1,0:T(8,128)(2,1)S(1)} %slice.34), channel_id=1, source_target_pairs={{0,1},{2,3},{4,5},{6,7},{8,9},{10,11},{12,13},{14,15},{16,17},{18,... | collective-permute-start | bytes 589832 | tf_op jit(solution)/shard_map/ppermute | solution.py:322
  45.1 7.2 %collective-permute-start.9 = (bf16[256,384]{1,0:T(8,128)(2,1)S(1)}, bf16[256,384]{1,0:T(8,128)(2,1)S(1)}, u32[]{:S(2)}, u32[]{:S(2)}) collective-permute-start(bf16[256,384]{1,0:T(8,128)(2,1)S(1)} %slice_add_fusion), channel_id=1, source_target_pairs={{0,16},{4,20},{1,17},{5,21},{2,18},{6,22},{3,19},{7,23}} | collective-permute-start | bytes 589832 | tf_op jit(solution)/shard_map/ppermute | solution.py:326
  47.1 9.4 %collective-permute-start.4 = (bf16[256,384]{1,0:T(8,128)(2,1)S(1)}, bf16[256,384]{1,0:T(8,128)(2,1)S(1)}, u32[]{:S(2)}, u32[]{:S(2)}) collective-permute-start(bf16[256,384]{1,0:T(8,128)(2,1)S(1)} %slice_add_fusion.1), channel_id=1, source_target_pairs={{0,16},{4,20},{1,17},{5,21},{2,18},{6,22},{3,19},{7,23}} | collective-permute-start | bytes 589832 | tf_op jit(solution)/shard_map/ppermute | solution.py:326
  52.3 7.8 %collective-permute-start.10 = (bf16[256,384]{1,0:T(8,128)(2,1)S(1)}, bf16[256,384]{1,0:T(8,128)(2,1)S(1)}, u32[]{:S(2)}, u32[]{:S(2)}) collective-permute-start(bf16[256,384]{1,0:T(8,128)(2,1)S(1)} %add.61), channel_id=1, source_target_pairs={{0,8},{4,12},{16,24},{20,28},{1,9},{5,13},{17,25},{21,29},{2,10},{... | collective-permute-start | bytes 589832 | tf_op jit(solution)/shard_map/ppermute | solution.py:326
  53.8 13.2 %copy-start.5 = (bf16[2,128,384]{2,1,0:T(8,128)(2,1)S(1)}, bf16[2,128,384]{2,1,0:T(8,128)(2,1)}, u32[]{:S(2)}) copy-start(bf16[2,128,384]{2,1,0:T(8,128)(2,1)} %sk_ref.1) | copy-start | bytes 589828
  54.6 12.4 %collective-permute-start.16 = (bf16[4,128,384]{2,1,0:T(8,128)(2,1)}, bf16[4,128,384]{2,1,0:T(8,128)(2,1)}, u32[]{:S(2)}, u32[]{:S(2)}) collective-permute-start(bf16[4,128,384]{2,1,0:T(8,128)(2,1)} %pad_maximum_fusion.1.near_ref), channel_id=1, source_target_pairs={{0,4},{4,0},{8,12},{12,8},{16,20},{20,16},{24,28},{28,24},{1,5},{5... | collective-permute-start | bytes 1179656 | tf_op jit(solution)/shard_map/ppermute | solution.py:291
  56.5 5.7 %collective-permute-start.5 = (bf16[256,384]{1,0:T(8,128)(2,1)S(1)}, bf16[256,384]{1,0:T(8,128)(2,1)S(1)}, u32[]{:S(2)}, u32[]{:S(2)}) collective-permute-start(bf16[256,384]{1,0:T(8,128)(2,1)S(1)} %add.55), channel_id=1, source_target_pairs={{0,8},{4,12},{16,24},{20,28},{1,9},{5,13},{17,25},{21,29},{2,10},{... | collective-permute-start | bytes 589832 | tf_op jit(solution)/shard_map/ppermute | solution.py:326
  63.1 17.3 %collective-permute-start.11 = (bf16[2,256,384]{2,1,0:T(8,128)(2,1)}, bf16[2,256,384]{2,1,0:T(8,128)(2,1)}, u32[]{:S(2)}, u32[]{:S(2)}) collective-permute-start(bf16[2,256,384]{2,1,0:T(8,128)(2,1)} %pad_maximum_fusion.refs_2_), channel_id=1, source_target_pairs={{0,4},{4,0},{8,12},{12,8},{16,20},{20,16},{24,28},{28,24},{1,5},{5... | collective-permute-start | bytes 1179656 | tf_op jit(solution)/shard_map/ppermute | solution.py:291
  63.1 17.3 %collective-permute-start.12 = (bf16[2,256,384]{2,1,0:T(8,128)(2,1)}, bf16[2,256,384]{2,1,0:T(8,128)(2,1)}, u32[]{:S(2)}, u32[]{:S(2)}) collective-permute-start(bf16[2,256,384]{2,1,0:T(8,128)(2,1)} %pad_maximum_fusion.refs_2_), channel_id=1, source_target_pairs={{0,2},{1,3},{2,0},{3,1},{4,6},{5,7},{6,4},{7,5},{8,10},{9,11},{10,... | collective-permute-start | bytes 1179656 | tf_op jit(solution)/shard_map/ppermute | solution.py:291
  81.4 32.3 %all-to-all-start.1 = ((f16[8,136,384]{2,1,0:T(8,128)(2,1)}), f16[8,136,384]{2,1,0:T(8,128)(2,1)}, u32[]{:S(2)}, u32[]{:S(2)}) async-start(f16[8,136,384]{2,1,0:T(8,128)(2,1)} %convert_element_type.9), calls=%async_computation.1 | async-start | bytes 1671168 | tf_op jit(solution)/shard_map/all_to_all | solution.py:350
  86.7 9.1 %collective-permute-start.18 = (bf16[2,256,384]{2,1,0:T(8,128)(2,1)}, bf16[2,256,384]{2,1,0:T(8,128)(2,1)}, u32[]{:S(2)}, u32[]{:S(2)}) collective-permute-start(bf16[2,256,384]{2,1,0:T(8,128)(2,1)} %pad_maximum_fusion.refs_2_), channel_id=1, source_target_pairs={{0,1},{1,0},{2,3},{3,2},{4,5},{5,4},{6,7},{7,6},{8,9},{9,8},{10,11... | collective-permute-start | bytes 1179656 | tf_op jit(solution)/shard_map/ppermute | solution.py:291
  86.7 9.1 %collective-permute-start.19 = (bf16[2,256,384]{2,1,0:T(8,128)(2,1)}, bf16[2,256,384]{2,1,0:T(8,128)(2,1)}, u32[]{:S(2)}, u32[]{:S(2)}) collective-permute-start(bf16[2,256,384]{2,1,0:T(8,128)(2,1)} %collective-permute-done.11.refs_3_), channel_id=1, source_target_pairs={{0,1},{1,0},{2,3},{3,2},{4,5},{5,4},{6,7},{7,6},{8,9},{9,8},{10,11... | collective-permute-start | bytes 1179656 | tf_op jit(solution)/shard_map/ppermute | solution.py:291
  87.2 13.9 %collective-permute-start.17 = (bf16[2,256,384]{2,1,0:T(8,128)(2,1)}, bf16[2,256,384]{2,1,0:T(8,128)(2,1)}, u32[]{:S(2)}, u32[]{:S(2)}) collective-permute-start(bf16[2,256,384]{2,1,0:T(8,128)(2,1)} %collective-permute-done.11.refs_3_), channel_id=1, source_target_pairs={{0,2},{1,3},{2,0},{3,1},{4,6},{5,7},{6,4},{7,5},{8,10},{9,11},{10,... | collective-permute-start | bytes 1179656 | tf_op jit(solution)/shard_map/ppermute | solution.py:291
  89.2 1.4 %copy-start.1 = (bf16[512,1536]{1,0:T(8,128)(2,1)S(1)}, bf16[512,1536]{1,0:T(8,128)(2,1)}, u32[]{:S(2)}) copy-start(bf16[512,1536]{1,0:T(8,128)(2,1)} %refs_0_.7) | copy-start | bytes 4718596
  90.6 5.3 %copy-start.2 = (bf16[512,1536]{1,0:T(8,128)(2,1)S(1)}, bf16[512,1536]{1,0:T(8,128)(2,1)}, u32[]{:S(2)}) copy-start(bf16[512,1536]{1,0:T(8,128)(2,1)} %refs_0_.7) | copy-start | bytes 4718596
  101.1 7.4 %collective-permute-start.20 = (bf16[2,256,384]{2,1,0:T(8,128)(2,1)}, bf16[2,256,384]{2,1,0:T(8,128)(2,1)}, u32[]{:S(2)}, u32[]{:S(2)}) collective-permute-start(bf16[2,256,384]{2,1,0:T(8,128)(2,1)} %collective-permute-done.12.refs_2_), channel_id=1, source_target_pairs={{0,1},{1,0},{2,3},{3,2},{4,5},{5,4},{6,7},{7,6},{8,9},{9,8},{10,11... | collective-permute-start | bytes 1179656 | tf_op jit(solution)/shard_map/ppermute | solution.py:291
  101.2 7.3 %collective-permute-start.21 = (bf16[2,256,384]{2,1,0:T(8,128)(2,1)}, bf16[2,256,384]{2,1,0:T(8,128)(2,1)}, u32[]{:S(2)}, u32[]{:S(2)}) collective-permute-start(bf16[2,256,384]{2,1,0:T(8,128)(2,1)} %collective-permute-done.17.refs_3_), channel_id=1, source_target_pairs={{0,1},{1,0},{2,3},{3,2},{4,5},{5,4},{6,7},{7,6},{8,9},{9,8},{10,11... | collective-permute-start | bytes 1179656 | tf_op jit(solution)/shard_map/ppermute | solution.py:291
  101.8 1.4 %copy-start.3 = (bf16[512,1536]{1,0:T(8,128)(2,1)S(1)}, bf16[512,1536]{1,0:T(8,128)(2,1)}, u32[]{:S(2)}) copy-start(bf16[512,1536]{1,0:T(8,128)(2,1)} %refs_0_.7) | copy-start | bytes 4718596

commit v12 on v10

--- a/solution.py
+++ b/solution.py
@@ -26,11 +26,22 @@
     return lax.dot_general(a, b, (((1,), (0,)), ((), ())), preferred_element_type=jnp.float32)
 
 
+def row_sums(x):
+    coarse = x.astype(jnp.bfloat16)
+    fine = (x - coarse.astype(jnp.float32)).astype(jnp.bfloat16)
+    ones = jnp.ones((HSZ, HSZ), jnp.bfloat16)
+    return dot(coarse, ones) + dot(fine, ones)
+
+
 def softmax(scores):
     top = functools.reduce(jnp.maximum, [jnp.max(s, axis=-1, keepdims=True) for s in scores])
     base = top * C2
     weights = [jnp.exp2(s * C2 - base) for s in scores]
-    total = functools.reduce(jnp.add, [jnp.sum(w, axis=-1, keepdims=True) for w in weights])
+    whole = [w[:, c : c + HSZ] for w in weights for c in range(0, w.shape[1] - HSZ + 1, HSZ)]
+    total = row_sums(functools.reduce(jnp.add, whole))
+    for w in weights:
+        if w.shape[1] % HSZ:
+            total = total + jnp.sum(w[:, w.shape[1] // HSZ * HSZ :], axis=-1, keepdims=True)
     return base, total, [w.astype(jnp.bfloat16) for w in weights]
 
 
@@ -326,15 +337,11 @@
     seen = (token_ids.reshape(-1, rows) >= NAMB) & (jnp.arange(rows)[None, :] < lengths[:, None])
     bias = jnp.where(seen, 0.0, NEG).astype(jnp.float32)
     suffix = functools.partial(suffix_attend, jnp.stack([host]), *gathered, swapped, suffix_kv, bias)
-    heads = suffix_queries.shape[1] // HSZ
-    early = max(1, heads - 1)
     far, other_near = swap(near, "hst", 1), swap(after(near, swapped), "grp", cores)
-    far, other_near, parts = lax.optimization_barrier((far, other_near, suffix(0, early, None)))
+    parts = suffix(0, suffix_queries.shape[1] // HSZ, None)
+    far, other_near, parts = lax.optimization_barrier((far, other_near, parts))
     other_far = swap(far, "grp", cores)
     by_core = [[swap(x, "grp", k) for x in (near, far)] for k in range(1, cores)]
-    if heads > early:
-        parts = suffix(early, heads - early, parts)
-    by_core, parts = lax.optimization_barrier((by_core, parts))
     parts = parts.astype(jnp.float16)
     coded = lax.all_to_all(parts, "hst", split_axis=0, concat_axis=0, tiled=True)
     held = {0: after([near, far], parts), cores: [other_near, other_far]}

time: 117 us -> 120 us (1.026)
  waiting for transfers between devices: 11.8 us -> 16.9 us
  starting transfers between devices: 47.1 us -> 42.9 us
  local copies, waits for them, and re-layouts: 5.93 us -> 7.35 us
    ppermute x4, starting transfers between devices: 10.3 us -> 5.84 us  [spread_anchor(): piece = piece + lax.ppermute(piece, 'hst', pairs)]
    ppermute x5, waiting for transfers between devices: 2.34 us -> 6.75 us  [scatter_anchor(): send = lambda x, to: lax.ppermute(x, BOTH, [(0, to)])]
    ppermute x4, waiting for transfers between devices: 7.1 us -> 10.1 us  [spread_anchor(): piece = piece + lax.ppermute(piece, 'hst', pairs)]
    all_to_all x1, waiting for transfers between devices: 2.37 us -> 0.01 us  [per_device(): lax.all_to_all(after(packed, down), 'grp', split_axis=0, concat_axis=0, t...]
    pallas_call x4, Pallas kernels: 19.3 us -> 20.5 us  [context_attend(): pl.pallas_call(context_kernel, grid_spec=pltpu.PrefetchScalarGridSpec(num...]
    unnamed x24 -> x26, local copies, waits for them, and re-layouts: 4.52 us -> 5.27 us
    pallas_call x2 -> x1, Pallas kernels: 14.7 us -> 14.2 us  [suffix_attend(): pl.pallas_call(suffix_kernel, grid_spec=pltpu.PrefetchScalarGridSpec(num_...]
  transfers between devices with their start and end apart: 24 -> 24, of which waited for: 5 -> 6; matrix products, arithmetic and copies ran while one was open for 6% -> 7% of each run, Pallas kernels for 29% -> 29%
where the time goes in v12:
time: 120 us; the launch traced here: 119 us
  starting transfers between devices  42.9 us (36%)
  Pallas kernels  41.3 us (34%)
  waiting for transfers between devices  16.9 us (14%)
  other arithmetic  9.81 us (8%)
  local copies, waits for them, and re-layouts  7.35 us (6%)
    pallas_call x4, Pallas kernels, context_attend(): pl.pallas_call(context_kernel, grid_spec=pltpu.PrefetchScalarGridSpec(num...  20.5 us
    pallas_call x1, Pallas kernels, suffix_attend(): pl.pallas_call(suffix_kernel, grid_spec=pltpu.PrefetchScalarGridSpec(num_...  14.2 us
    ppermute x5, starting transfers between devices, scatter_anchor(): send = lambda x, to: lax.ppermute(x, BOTH, [(0, to)])  12.4 us
    ppermute x11, starting transfers between devices, swap(): lax.ppermute(x, axis, [(i, i ^ k) for i in range(lax.axis_size(axis))])  11.2 us
    ppermute x4, waiting for transfers between devices, spread_anchor(): piece = piece + lax.ppermute(piece, 'hst', pairs)  10.1 us
    ppermute x5, waiting for transfers between devices, scatter_anchor(): send = lambda x, to: lax.ppermute(x, BOTH, [(0, to)])  6.75 us
    ppermute x4, starting transfers between devices, spread_anchor(): piece = piece + lax.ppermute(piece, 'hst', pairs)  5.84 us
    all_to_all x1, starting transfers between devices, per_device(): lax.all_to_all(parts, 'hst', split_axis=0, concat_axis=0, tiled=True)  5.32 us
  transfers between devices with their start and end apart: 24, of which 6 were waited for; matrix products, arithmetic and copies ran while one was open for 7% of the time, Pallas kernels for 29%

profile of v12, /device:TPU:0, one launch (start us, length us, event | category | flops | bytes accessed | tf_op | source)
XLA Modules:
  0.0 119.3 jit_solution(11346443154943670478)
XLA Ops:
  0.6 3.9 %pack_heads.1 = (bf16[4,2,512,384]{3,2,1,0:T(8,128)(2,1)}, bf16[2,256,768]{2,1,0:T(8,128)(2,1)}, bf16[256,768]{1,0:T(8,128)(2,1)}, bf16[256,768]{1,0:T(8,128)(2,...) custom-call(bf16[2,512,1536]{2,1,0:T(8,128)(2,1)} %kv_ref.9), custom_call_target="tpu_custom_call" | custom-call | bytes 9437184 | tf_op jit(solution)/shard_map/pack_heads/pallas_call | solution.py:77
  4.5 4.9 %collective-permute-start.2 = (bf16[2,256,768]{2,1,0:T(8,128)(2,1)}, bf16[2,256,768]{2,1,0:T(8,128)(2,1)S(1)}, u32[]{:S(2)}, u32[]{:S(2)}) collective-permute-start(bf16[2,256,768]{2,1,0:T(8,128)(2,1)} %get-tuple-element.21), channel_id=1, source_target_pairs={{0,4}} | collective-permute-start | bytes 2359304 | tf_op jit(solution)/shard_map/ppermute | solution.py:302
  9.4 1.3 %collective-permute-start.1 = (bf16[256,768]{1,0:T(8,128)(2,1)}, bf16[256,768]{1,0:T(8,128)(2,1)S(1)}, u32[]{:S(2)}, u32[]{:S(2)}) collective-permute-start(bf16[256,768]{1,0:T(8,128)(2,1)} %get-tuple-element.20), channel_id=1, source_target_pairs={{0,2}} | collective-permute-start | bytes 1179656 | tf_op jit(solution)/shard_map/ppermute | solution.py:302
  10.7 2.1 %collective-permute-start = (bf16[256,768]{1,0:T(8,128)(2,1)}, bf16[256,768]{1,0:T(8,128)(2,1)}, u32[]{:S(2)}, u32[]{:S(2)}) collective-permute-start(bf16[256,768]{1,0:T(8,128)(2,1)} %get-tuple-element.19), channel_id=1, source_target_pairs={{0,6}} | collective-permute-start | bytes 1179656 | tf_op jit(solution)/shard_map/ppermute | solution.py:302
  12.8 2.1 %collective-permute-start.7 = (bf16[256,768]{1,0:T(8,128)(2,1)}, bf16[256,768]{1,0:T(8,128)(2,1)}, u32[]{:S(2)}, u32[]{:S(2)}) collective-permute-start(bf16[256,768]{1,0:T(8,128)(2,1)} %get-tuple-element.23), channel_id=1, source_target_pairs={{0,2}} | collective-permute-start | bytes 1179656 | tf_op jit(solution)/shard_map/ppermute | solution.py:302
  14.9 2.1 %collective-permute-start.6 = (bf16[256,768]{1,0:T(8,128)(2,1)}, bf16[256,768]{1,0:T(8,128)(2,1)}, u32[]{:S(2)}, u32[]{:S(2)}) collective-permute-start(bf16[256,768]{1,0:T(8,128)(2,1)} %get-tuple-element.22), channel_id=1, source_target_pairs={{0,6}} | collective-permute-start | bytes 1179656 | tf_op jit(solution)/shard_map/ppermute | solution.py:302
  16.9 2.2 %collective-permute-done.2 = bf16[2,256,768]{2,1,0:T(8,128)(2,1)S(1)} collective-permute-done((bf16[2,256,768]{2,1,0:T(8,128)(2,1)}, bf16[2,256,768]{2,1,0:T(8,128)(2,1)S(1)}, u32[]{:S(2)}, u32[]{:S(2)}) %collective-permute-start.2) | collective-permute-done | bytes 786464 | tf_op jit(solution)/shard_map/ppermute | solution.py:302
  19.2 0.9 copy-done.7
  20.1 4.9 %all-to-all-start = ((bf16[4,2,512,384]{3,2,1,0:T(8,128)(2,1)}), bf16[4,2,512,384]{3,2,1,0:T(8,128)(2,1)}, u32[]{:S(2)}, u32[]{:S(2)}) async-start(bf16[4,2,512,384]{3,2,1,0:T(8,128)(2,1)} %get-tuple-element.26), calls=%async_computation | async-start | bytes 6291456 | tf_op jit(solution)/shard_map/all_to_all | solution.py:334
  25.0 0.8 copy-done.9
  25.8 1.3 %fusion = bf16[256,768]{1,0:T(8,128)(2,1)S(1)} fusion(bf16[2,256,768]{2,1,0:T(8,128)(2,1)} %copy-done.7, bf16[256,768]{1,0:T(8,128)(2,1)} %copy-done.9, bf16[256,768]{1,0:T(8,128)(2,1)} %collective-permute-done, bf16[2,512,1536]{2,1,0:T(8,128)(2,1)S(1)} %copy-done, pred[]{:T(512)S(6)} %and.18), kind=kLoop, calls=%fused_computation.2 | loop fusion | flops 786432 | bytes 1966081 | tf_op jit(solution)/shard_map/add | solution.py:308
  27.2 4.5 %collective-permute-done.6 = bf16[256,768]{1,0:T(8,128)(2,1)} collective-permute-done((bf16[256,768]{1,0:T(8,128)(2,1)}, bf16[256,768]{1,0:T(8,128)(2,1)}, u32[]{:S(2)}, u32[]{:S(2)}) %collective-permute-start.6) | collective-permute-done | bytes 393248 | tf_op jit(solution)/shard_map/ppermute | solution.py:302
  31.7 1.2 fusion.2
  32.9 0.7 copy-done.6
  33.6 0.7 slice.37
  34.3 2.0 %collective-permute-start.8 = (bf16[256,384]{1,0:T(8,128)(2,1)}, bf16[256,384]{1,0:T(8,128)(2,1)}, u32[]{:S(2)}, u32[]{:S(2)}) collective-permute-start(bf16[256,384]{1,0:T(8,128)(2,1)} %slice.37), channel_id=1, source_target_pairs={{0,1},{2,3},{4,5},{6,7},{8,9},{10,11},{12,13},{14,15},{16,17},{18,... | collective-permute-start | bytes 589832 | tf_op jit(solution)/shard_map/ppermute | solution.py:318
  36.3 0.6 broadcast_compare_fusion
  36.9 1.3 %ge.11 = pred[32,512]{1,0:T(8,128)(4,1)} reshape(pred[16384]{0:T(1024)(128)(4,1)} %broadcast_compare_fusion) | data formatting | bytes 32768 | tf_op jit(solution)/shard_map/ge | solution.py:337
  38.4 4.3 %collective-permute-start.13 = (bf16[128,384]{1,0:T(8,128)(2,1)}, bf16[128,384]{1,0:T(8,128)(2,1)S(1)}, u32[]{:S(2)}, u32[]{:S(2)}) collective-permute-start(bf16[128,384]{1,0:T(8,128)(2,1)} %param.10), channel_id=1, source_target_pairs={{0,8},{4,12},{8,0},{12,4},{16,24},{20,28},{24,16},{28,20},{1,9},{5... | collective-permute-start | bytes 294920 | tf_op jit(solution)/shard_map/ppermute | solution.py:287
  42.7 1.3 %collective-permute-start.3 = (bf16[256,384]{1,0:T(8,128)(2,1)S(1)}, bf16[256,384]{1,0:T(8,128)(2,1)S(1)}, u32[]{:S(2)}, u32[]{:S(2)}) collective-permute-start(bf16[256,384]{1,0:T(8,128)(2,1)S(1)} %slice.34), channel_id=1, source_target_pairs={{0,1},{2,3},{4,5},{6,7},{8,9},{10,11},{12,13},{14,15},{16,17},{18,... | collective-permute-start | bytes 589832 | tf_op jit(solution)/shard_map/ppermute | solution.py:318
  44.1 1.0 slice_add_fusion
  45.1 1.9 %collective-permute-start.9 = (bf16[256,384]{1,0:T(8,128)(2,1)S(1)}, bf16[256,384]{1,0:T(8,128)(2,1)S(1)}, u32[]{:S(2)}, u32[]{:S(2)}) collective-permute-start(bf16[256,384]{1,0:T(8,128)(2,1)S(1)} %slice_add_fusion), channel_id=1, source_target_pairs={{0,16},{4,20},{1,17},{5,21},{2,18},{6,22},{3,19},{7,23}} | collective-permute-start | bytes 589832 | tf_op jit(solution)/shard_map/ppermute | solution.py:322
  47.1 1.3 %collective-permute-start.4 = (bf16[256,384]{1,0:T(8,128)(2,1)S(1)}, bf16[256,384]{1,0:T(8,128)(2,1)S(1)}, u32[]{:S(2)}, u32[]{:S(2)}) collective-permute-start(bf16[256,384]{1,0:T(8,128)(2,1)S(1)} %slice_add_fusion.1), channel_id=1, source_target_pairs={{0,16},{4,20},{1,17},{5,21},{2,18},{6,22},{3,19},{7,23}} | collective-permute-start | bytes 589832 | tf_op jit(solution)/shard_map/ppermute | solution.py:322
  48.4 3.9 %collective-permute-done.9 = bf16[256,384]{1,0:T(8,128)(2,1)S(1)} collective-permute-done((bf16[256,384]{1,0:T(8,128)(2,1)S(1)}, bf16[256,384]{1,0:T(8,128)(2,1)S(1)}, u32[]{:S(2)}, u32[]{:S(2)}) %collective-permute-start.9) | collective-permute-done | bytes 196640 | tf_op jit(solution)/shard_map/ppermute | solution.py:322
  52.3 1.3 %collective-permute-start.10 = (bf16[256,384]{1,0:T(8,128)(2,1)S(1)}, bf16[256,384]{1,0:T(8,128)(2,1)S(1)}, u32[]{:S(2)}, u32[]{:S(2)}) collective-permute-start(bf16[256,384]{1,0:T(8,128)(2,1)S(1)} %add.61), channel_id=1, source_target_pairs={{0,8},{4,12},{16,24},{20,28},{1,9},{5,13},{17,25},{21,29},{2,10},{... | collective-permute-start | bytes 589832 | tf_op jit(solution)/shard_map/ppermute | solution.py:322
  53.6 0.1 fusion.5.bias_ref
  53.8 0.8 pad_maximum_fusion.1.near_ref
  54.6 1.9 %collective-permute-done.4 = bf16[256,384]{1,0:T(8,128)(2,1)S(1)} collective-permute-done((bf16[256,384]{1,0:T(8,128)(2,1)S(1)}, bf16[256,384]{1,0:T(8,128)(2,1)S(1)}, u32[]{:S(2)}, u32[]{:S(2)}) %collective-permute-start.4) | collective-permute-done | bytes 196640 | tf_op jit(solution)/shard_map/ppermute | solution.py:322
  56.5 1.3 %collective-permute-start.5 = (bf16[256,384]{1,0:T(8,128)(2,1)S(1)}, bf16[256,384]{1,0:T(8,128)(2,1)S(1)}, u32[]{:S(2)}, u32[]{:S(2)}) collective-permute-start(bf16[256,384]{1,0:T(8,128)(2,1)S(1)} %add.55), channel_id=1, source_target_pairs={{0,8},{4,12},{16,24},{20,28},{1,9},{5,13},{17,25},{21,29},{2,10},{... | collective-permute-start | bytes 589832 | tf_op jit(solution)/shard_map/ppermute | solution.py:322
  57.8 2.3 %collective-permute-done.10 = bf16[256,384]{1,0:T(8,128)(2,1)S(1)} collective-permute-done((bf16[256,384]{1,0:T(8,128)(2,1)S(1)}, bf16[256,384]{1,0:T(8,128)(2,1)S(1)}, u32[]{:S(2)}, u32[]{:S(2)}) %collective-permute-start.10) | collective-permute-done | bytes 196640 | tf_op jit(solution)/shard_map/ppermute | solution.py:322
  60.2 2.1 %collective-permute-done.5 = bf16[256,384]{1,0:T(8,128)(2,1)S(1)} collective-permute-done((bf16[256,384]{1,0:T(8,128)(2,1)S(1)}, bf16[256,384]{1,0:T(8,128)(2,1)S(1)}, u32[]{:S(2)}, u32[]{:S(2)}) %collective-permute-start.5) | collective-permute-done | bytes 196640 | tf_op jit(solution)/shard_map/ppermute | solution.py:322
  62.3 0.8 pad_maximum_fusion.near_ref
  63.1 3.9 %collective-permute-start.12 = (bf16[2,256,384]{2,1,0:T(8,128)(2,1)}, bf16[2,256,384]{2,1,0:T(8,128)(2,1)}, u32[]{:S(2)}, u32[]{:S(2)}) collective-permute-start(bf16[2,256,384]{2,1,0:T(8,128)(2,1)} %pad_maximum_fusion.near_ref), channel_id=1, source_target_pairs={{0,2},{1,3},{2,0},{3,1},{4,6},{5,7},{6,4},{7,5},{8,10},{9,11},{10,... | collective-permute-start | bytes 1179656 | tf_op jit(solution)/shard_map/ppermute | solution.py:287
  67.0 14.2 %suffix_attend.1 = f32[8,136,384]{2,1,0:T(8,128)S(1)} custom-call(s32[1]{0:T(128)} %bitcast.9.at_ref, bf16[4,128,384]{2,1,0:T(8,128)(2,1)} %pad_maximum_fusion.1.near_ref, bf16[4,128,384]{2,1,0:T(8,128)(2,1)} %collective-permute-done.16.far_ref, bf16[4,2,512,384]{3,2,1,0:T(8,128)(2,1)} %all-to-all-done.kv_ref, bf16[2,128,384]{2,1,0:T(8,128)(2,1)S(1)} %copy-done.5, ...), custom_call_target="tpu_custom_call" | custom-call | flops 6845104128 | bytes 7864320 | tf_op jit(solution)/shard_map/suffix_attend/pallas_call | solution.py:159
  81.2 1.0 convert_element_type.9
  82.2 5.3 %all-to-all-start.1 = ((f16[8,136,384]{2,1,0:T(8,128)(2,1)}), f16[8,136,384]{2,1,0:T(8,128)(2,1)}, u32[]{:S(2)}, u32[]{:S(2)}) async-start(f16[8,136,384]{2,1,0:T(8,128)(2,1)} %convert_element_type.9), calls=%async_computation.1 | async-start | bytes 1671168 | tf_op jit(solution)/shard_map/all_to_all | solution.py:346
  87.6 0.5 collective-permute-start.19
  88.1 1.8 %collective-permute-start.17 = (bf16[2,256,384]{2,1,0:T(8,128)(2,1)}, bf16[2,256,384]{2,1,0:T(8,128)(2,1)}, u32[]{:S(2)}, u32[]{:S(2)}) collective-permute-start(bf16[2,256,384]{2,1,0:T(8,128)(2,1)} %collective-permute-done.11.far_ref), channel_id=1, source_target_pairs={{0,2},{1,3},{2,0},{3,1},{4,6},{5,7},{6,4},{7,5},{8,10},{9,11},{10,... | collective-permute-start | bytes 1179656 | tf_op jit(solution)/shard_map/ppermute | solution.py:287
  90.0 1.4 %copy-done.1 = bf16[512,1536]{1,0:T(8,128)(2,1)S(1)} copy-done((bf16[512,1536]{1,0:T(8,128)(2,1)S(1)}, bf16[512,1536]{1,0:T(8,128)(2,1)}, u32[]{:S(2)}) %copy-start.1) | copy-done | bytes 1572888
  91.4 5.1 %context_attend.4.rest_0_ = bf16[512,1536]{1,0:T(8,128)(2,1)} custom-call(s32[3]{0:T(128)S(1)} %add_add_fusion.2.at_ref, s32[32]{0:T(128)S(1)} %copy-done.4, bf16[512,1536]{1,0:T(8,128)(2,1)S(1)} %copy-done.1, bf16[2,512,1536]{2,1,0:T(8,128)(2,1)S(1)} %copy-done, f32[32,512]{1,0:T(8,128)S(1)} %fusion.5.bias_ref, ...), custom_call_target="tpu_custom_call" | custom-call | flops 805306368 | bytes 2359296 | tf_op jit(solution)/shard_map/context_attend/pallas_call | solution.py:258
  96.6 5.1 %context_attend.5.rest_0_ = bf16[512,1536]{1,0:T(8,128)(2,1)} custom-call(s32[3]{0:T(128)S(1)} %add_add_fusion.1.at_ref, s32[32]{0:T(128)S(1)} %copy-done.4, bf16[512,1536]{1,0:T(8,128)(2,1)S(1)} %copy-done.2, bf16[2,512,1536]{2,1,0:T(8,128)(2,1)S(1)} %copy-done, f32[32,512]{1,0:T(8,128)S(1)} %fusion.5.bias_ref, ...), custom_call_target="tpu_custom_call", output_to_operand_aliasing={{}: (7, {})} | custom-call | flops 805306368 | bytes 2359296 | tf_op jit(solution)/shard_map/context_attend/pallas_call | solution.py:258
  101.7 0.5 collective-permute-start.21
  102.2 0.1 add_add_fusion.at_ref
  102.4 1.4 %copy-done.3 = bf16[512,1536]{1,0:T(8,128)(2,1)S(1)} copy-done((bf16[512,1536]{1,0:T(8,128)(2,1)S(1)}, bf16[512,1536]{1,0:T(8,128)(2,1)}, u32[]{:S(2)}) %copy-start.3) | copy-done | bytes 1572888
  103.8 5.1 %context_attend.6.rest_0_ = bf16[512,1536]{1,0:T(8,128)(2,1)} custom-call(s32[3]{0:T(128)S(1)} %add_add_fusion.3.at_ref, s32[32]{0:T(128)S(1)} %copy-done.4, bf16[512,1536]{1,0:T(8,128)(2,1)S(1)} %copy-done.3, bf16[2,512,1536]{2,1,0:T(8,128)(2,1)S(1)} %copy-done, f32[32,512]{1,0:T(8,128)S(1)} %fusion.5.bias_ref, ...), custom_call_target="tpu_custom_call", output_to_operand_aliasing={{}: (7, {})} | custom-call | flops 805306368 | bytes 2359296 | tf_op jit(solution)/shard_map/context_attend/pallas_call | solution.py:258
  108.9 5.1 %context_attend.7 = bf16[512,1536]{1,0:T(8,128)(2,1)} custom-call(s32[3]{0:T(128)S(1)} %add_add_fusion.at_ref, s32[32]{0:T(128)S(1)} %copy-done.4, bf16[512,1536]{1,0:T(8,128)(2,1)S(1)} %copy-done.3, bf16[2,512,1536]{2,1,0:T(8,128)(2,1)S(1)} %copy-done, f32[32,512]{1,0:T(8,128)S(1)} %fusion.5.bias_ref, ...), custom_call_target="tpu_custom_call", output_to_operand_aliasing={{}: (7, {})} | custom-call | flops 805306368 | bytes 2359296 | tf_op jit(solution)/shard_map/context_attend/pallas_call | solution.py:258
  114.1 2.5 %convert_element_type.10.in_ref = f32[8,136,384]{2,1,0:T(8,128)} convert(f16[8,136,384]{2,1,0:T(8,128)(2,1)} %all-to-all-done.1) | non-fusion elementwise | flops 417792 | bytes 2506752 | tf_op jit(solution)/shard_map/convert_element_type | solution.py:362
  116.5 2.7 %combine_groups.1 = bf16[128,384]{1,0:T(8,128)(2,1)} custom-call(f32[8,136,384]{2,1,0:T(8,128)} %convert_element_type.10.in_ref), custom_call_target="tpu_custom_call" | custom-call | flops 835584 | bytes 1671168 | tf_op jit(solution)/shard_map/combine_groups/pallas_call | solution.py:203
  (55 shorter events, 0.7 us)
Async XLA Ops:
  4.5 14.7 %collective-permute-start.2 = (bf16[2,256,768]{2,1,0:T(8,128)(2,1)}, bf16[2,256,768]{2,1,0:T(8,128)(2,1)S(1)}, u32[]{:S(2)}, u32[]{:S(2)}) collective-permute-start(bf16[2,256,768]{2,1,0:T(8,128)(2,1)} %get-tuple-element.21), channel_id=1, source_target_pairs={{0,4}} | collective-permute-start | bytes 2359304 | tf_op jit(solution)/shard_map/ppermute | solution.py:302
  9.4 15.6 %collective-permute-start.1 = (bf16[256,768]{1,0:T(8,128)(2,1)}, bf16[256,768]{1,0:T(8,128)(2,1)S(1)}, u32[]{:S(2)}, u32[]{:S(2)}) collective-permute-start(bf16[256,768]{1,0:T(8,128)(2,1)} %get-tuple-element.20), channel_id=1, source_target_pairs={{0,2}} | collective-permute-start | bytes 1179656 | tf_op jit(solution)/shard_map/ppermute | solution.py:302
  10.7 15.1 %collective-permute-start = (bf16[256,768]{1,0:T(8,128)(2,1)}, bf16[256,768]{1,0:T(8,128)(2,1)}, u32[]{:S(2)}, u32[]{:S(2)}) collective-permute-start(bf16[256,768]{1,0:T(8,128)(2,1)} %get-tuple-element.19), channel_id=1, source_target_pairs={{0,6}} | collective-permute-start | bytes 1179656 | tf_op jit(solution)/shard_map/ppermute | solution.py:302
  12.8 14.4 %collective-permute-start.7 = (bf16[256,768]{1,0:T(8,128)(2,1)}, bf16[256,768]{1,0:T(8,128)(2,1)}, u32[]{:S(2)}, u32[]{:S(2)}) collective-permute-start(bf16[256,768]{1,0:T(8,128)(2,1)} %get-tuple-element.23), channel_id=1, source_target_pairs={{0,2}} | collective-permute-start | bytes 1179656 | tf_op jit(solution)/shard_map/ppermute | solution.py:302
  14.9 16.8 %collective-permute-start.6 = (bf16[256,768]{1,0:T(8,128)(2,1)}, bf16[256,768]{1,0:T(8,128)(2,1)}, u32[]{:S(2)}, u32[]{:S(2)}) collective-permute-start(bf16[256,768]{1,0:T(8,128)(2,1)} %get-tuple-element.22), channel_id=1, source_target_pairs={{0,6}} | collective-permute-start | bytes 1179656 | tf_op jit(solution)/shard_map/ppermute | solution.py:302
  19.2 0.9 copy-start.7
  20.1 5.7 %copy-start = (bf16[2,512,1536]{2,1,0:T(8,128)(2,1)S(1)}, bf16[2,512,1536]{2,1,0:T(8,128)(2,1)}, u32[]{:S(2)}) copy-start(bf16[2,512,1536]{2,1,0:T(8,128)(2,1)} %kv_ref.9) | copy-start | bytes 9437188
  20.1 43.0 %all-to-all-start = ((bf16[4,2,512,384]{3,2,1,0:T(8,128)(2,1)}), bf16[4,2,512,384]{3,2,1,0:T(8,128)(2,1)}, u32[]{:S(2)}, u32[]{:S(2)}) async-start(bf16[4,2,512,384]{3,2,1,0:T(8,128)(2,1)} %get-tuple-element.26), calls=%async_computation | async-start | bytes 6291456 | tf_op jit(solution)/shard_map/all_to_all | solution.py:334
  25.0 2.1 %copy-start.8 = (bf16[2,256,768]{2,1,0:T(8,128)(2,1)S(1)}, bf16[2,256,768]{2,1,0:T(8,128)(2,1)}, u32[]{:S(2)}) copy-start(bf16[2,256,768]{2,1,0:T(8,128)(2,1)} %copy-done.7) | copy-start | bytes 2359300
  25.0 0.8 copy-start.9
  27.1 9.2 %copy-start.11 = (s32[16384]{0:T(1024)S(1)}, s32[16384]{0:T(1024)}, u32[]{:S(2)}) copy-start(s32[16384]{0:T(1024)} %param.8) | copy-start | bytes 196612
  32.9 0.7 copy-start.6
  33.6 20.0 %copy-start.4 = (s32[32]{0:T(128)S(1)}, s32[32]{0:T(128)}, u32[]{:S(2)}) copy-start(s32[32]{0:T(128)} %len_ref.7) | copy-start | bytes 388
  34.3 9.7 %collective-permute-start.8 = (bf16[256,384]{1,0:T(8,128)(2,1)}, bf16[256,384]{1,0:T(8,128)(2,1)}, u32[]{:S(2)}, u32[]{:S(2)}) collective-permute-start(bf16[256,384]{1,0:T(8,128)(2,1)} %slice.37), channel_id=1, source_target_pairs={{0,1},{2,3},{4,5},{6,7},{8,9},{10,11},{12,13},{14,15},{16,17},{18,... | collective-permute-start | bytes 589832 | tf_op jit(solution)/shard_map/ppermute | solution.py:318
  38.3 15.4 %copy-start.12 = (pred[32,512]{1,0:T(8,128)(4,1)S(1)}, pred[32,512]{1,0:T(8,128)(4,1)}, u32[]{:S(2)}) copy-start(pred[32,512]{1,0:T(8,128)(4,1)} %ge.11) | copy-start | bytes 49156
  38.3 15.5 %copy-start.10 = (bf16[128,384]{1,0:T(8,128)(2,1)S(1)}, bf16[128,384]{1,0:T(8,128)(2,1)}, u32[]{:S(2)}) copy-start(bf16[128,384]{1,0:T(8,128)(2,1)} %param.10) | copy-start | bytes 294916
  38.3 15.4 %collective-permute-start.15 = (bf16[128,384]{1,0:T(8,128)(2,1)}, bf16[128,384]{1,0:T(8,128)(2,1)S(1)}, u32[]{:S(2)}, u32[]{:S(2)}) collective-permute-start(bf16[128,384]{1,0:T(8,128)(2,1)} %param.10), channel_id=1, source_target_pairs={{0,24},{4,28},{8,16},{12,20},{16,8},{20,12},{24,0},{28,4},{1,25},{... | collective-permute-start | bytes 294920 | tf_op jit(solution)/shard_map/ppermute | solution.py:287
  38.4 15.4 %collective-permute-start.14 = (bf16[128,384]{1,0:T(8,128)(2,1)}, bf16[128,384]{1,0:T(8,128)(2,1)S(1)}, u32[]{:S(2)}, u32[]{:S(2)}) collective-permute-start(bf16[128,384]{1,0:T(8,128)(2,1)} %param.10), channel_id=1, source_target_pairs={{0,16},{4,20},{8,24},{12,28},{16,0},{20,4},{24,8},{28,12},{1,17},{... | collective-permute-start | bytes 294920 | tf_op jit(solution)/shard_map/ppermute | solution.py:287
  38.4 15.3 %collective-permute-start.13 = (bf16[128,384]{1,0:T(8,128)(2,1)}, bf16[128,384]{1,0:T(8,128)(2,1)S(1)}, u32[]{:S(2)}, u32[]{:S(2)}) collective-permute-start(bf16[128,384]{1,0:T(8,128)(2,1)} %param.10), channel_id=1, source_target_pairs={{0,8},{4,12},{8,0},{12,4},{16,24},{20,28},{24,16},{28,20},{1,9},{5... | collective-permute-start | bytes 294920 | tf_op jit(solution)/shard_map/ppermute | solution.py:287
  42.7 4.3 %collective-permute-start.3 = (bf16[256,384]{1,0:T(8,128)(2,1)S(1)}, bf16[256,384]{1,0:T(8,128)(2,1)S(1)}, u32[]{:S(2)}, u32[]{:S(2)}) collective-permute-start(bf16[256,384]{1,0:T(8,128)(2,1)S(1)} %slice.34), channel_id=1, source_target_pairs={{0,1},{2,3},{4,5},{6,7},{8,9},{10,11},{12,13},{14,15},{16,17},{18,... | collective-permute-start | bytes 589832 | tf_op jit(solution)/shard_map/ppermute | solution.py:318
  45.1 7.2 %collective-permute-start.9 = (bf16[256,384]{1,0:T(8,128)(2,1)S(1)}, bf16[256,384]{1,0:T(8,128)(2,1)S(1)}, u32[]{:S(2)}, u32[]{:S(2)}) collective-permute-start(bf16[256,384]{1,0:T(8,128)(2,1)S(1)} %slice_add_fusion), channel_id=1, source_target_pairs={{0,16},{4,20},{1,17},{5,21},{2,18},{6,22},{3,19},{7,23}} | collective-permute-start | bytes 589832 | tf_op jit(solution)/shard_map/ppermute | solution.py:322
  47.1 9.4 %collective-permute-start.4 = (bf16[256,384]{1,0:T(8,128)(2,1)S(1)}, bf16[256,384]{1,0:T(8,128)(2,1)S(1)}, u32[]{:S(2)}, u32[]{:S(2)}) collective-permute-start(bf16[256,384]{1,0:T(8,128)(2,1)S(1)} %slice_add_fusion.1), channel_id=1, source_target_pairs={{0,16},{4,20},{1,17},{5,21},{2,18},{6,22},{3,19},{7,23}} | collective-permute-start | bytes 589832 | tf_op jit(solution)/shard_map/ppermute | solution.py:322
  52.3 7.8 %collective-permute-start.10 = (bf16[256,384]{1,0:T(8,128)(2,1)S(1)}, bf16[256,384]{1,0:T(8,128)(2,1)S(1)}, u32[]{:S(2)}, u32[]{:S(2)}) collective-permute-start(bf16[256,384]{1,0:T(8,128)(2,1)S(1)} %add.61), channel_id=1, source_target_pairs={{0,8},{4,12},{16,24},{20,28},{1,9},{5,13},{17,25},{21,29},{2,10},{... | collective-permute-start | bytes 589832 | tf_op jit(solution)/shard_map/ppermute | solution.py:322
  53.8 13.2 %copy-start.5 = (bf16[2,128,384]{2,1,0:T(8,128)(2,1)S(1)}, bf16[2,128,384]{2,1,0:T(8,128)(2,1)}, u32[]{:S(2)}) copy-start(bf16[2,128,384]{2,1,0:T(8,128)(2,1)} %sk_ref.1) | copy-start | bytes 589828
  54.6 12.4 %collective-permute-start.16 = (bf16[4,128,384]{2,1,0:T(8,128)(2,1)}, bf16[4,128,384]{2,1,0:T(8,128)(2,1)}, u32[]{:S(2)}, u32[]{:S(2)}) collective-permute-start(bf16[4,128,384]{2,1,0:T(8,128)(2,1)} %pad_maximum_fusion.1.near_ref), channel_id=1, source_target_pairs={{0,4},{4,0},{8,12},{12,8},{16,20},{20,16},{24,28},{28,24},{1,5},{5... | collective-permute-start | bytes 1179656 | tf_op jit(solution)/shard_map/ppermute | solution.py:287
  56.5 5.7 %collective-permute-start.5 = (bf16[256,384]{1,0:T(8,128)(2,1)S(1)}, bf16[256,384]{1,0:T(8,128)(2,1)S(1)}, u32[]{:S(2)}, u32[]{:S(2)}) collective-permute-start(bf16[256,384]{1,0:T(8,128)(2,1)S(1)} %add.55), channel_id=1, source_target_pairs={{0,8},{4,12},{16,24},{20,28},{1,9},{5,13},{17,25},{21,29},{2,10},{... | collective-permute-start | bytes 589832 | tf_op jit(solution)/shard_map/ppermute | solution.py:322
  63.1 18.1 %collective-permute-start.11 = (bf16[2,256,384]{2,1,0:T(8,128)(2,1)}, bf16[2,256,384]{2,1,0:T(8,128)(2,1)}, u32[]{:S(2)}, u32[]{:S(2)}) collective-permute-start(bf16[2,256,384]{2,1,0:T(8,128)(2,1)} %pad_maximum_fusion.near_ref), channel_id=1, source_target_pairs={{0,4},{4,0},{8,12},{12,8},{16,20},{20,16},{24,28},{28,24},{1,5},{5... | collective-permute-start | bytes 1179656 | tf_op jit(solution)/shard_map/ppermute | solution.py:287
  63.1 18.1 %collective-permute-start.12 = (bf16[2,256,384]{2,1,0:T(8,128)(2,1)}, bf16[2,256,384]{2,1,0:T(8,128)(2,1)}, u32[]{:S(2)}, u32[]{:S(2)}) collective-permute-start(bf16[2,256,384]{2,1,0:T(8,128)(2,1)} %pad_maximum_fusion.near_ref), channel_id=1, source_target_pairs={{0,2},{1,3},{2,0},{3,1},{4,6},{5,7},{6,4},{7,5},{8,10},{9,11},{10,... | collective-permute-start | bytes 1179656 | tf_op jit(solution)/shard_map/ppermute | solution.py:287
  82.2 31.8 %all-to-all-start.1 = ((f16[8,136,384]{2,1,0:T(8,128)(2,1)}), f16[8,136,384]{2,1,0:T(8,128)(2,1)}, u32[]{:S(2)}, u32[]{:S(2)}) async-start(f16[8,136,384]{2,1,0:T(8,128)(2,1)} %convert_element_type.9), calls=%async_computation.1 | async-start | bytes 1671168 | tf_op jit(solution)/shard_map/all_to_all | solution.py:346
  87.6 9.0 %collective-permute-start.18 = (bf16[2,256,384]{2,1,0:T(8,128)(2,1)}, bf16[2,256,384]{2,1,0:T(8,128)(2,1)}, u32[]{:S(2)}, u32[]{:S(2)}) collective-permute-start(bf16[2,256,384]{2,1,0:T(8,128)(2,1)} %pad_maximum_fusion.near_ref), channel_id=1, source_target_pairs={{0,1},{1,0},{2,3},{3,2},{4,5},{5,4},{6,7},{7,6},{8,9},{9,8},{10,11... | collective-permute-start | bytes 1179656 | tf_op jit(solution)/shard_map/ppermute | solution.py:287
  87.6 9.0 %collective-permute-start.19 = (bf16[2,256,384]{2,1,0:T(8,128)(2,1)}, bf16[2,256,384]{2,1,0:T(8,128)(2,1)}, u32[]{:S(2)}, u32[]{:S(2)}) collective-permute-start(bf16[2,256,384]{2,1,0:T(8,128)(2,1)} %collective-permute-done.11.far_ref), channel_id=1, source_target_pairs={{0,1},{1,0},{2,3},{3,2},{4,5},{5,4},{6,7},{7,6},{8,9},{9,8},{10,11... | collective-permute-start | bytes 1179656 | tf_op jit(solution)/shard_map/ppermute | solution.py:287
  88.1 13.6 %collective-permute-start.17 = (bf16[2,256,384]{2,1,0:T(8,128)(2,1)}, bf16[2,256,384]{2,1,0:T(8,128)(2,1)}, u32[]{:S(2)}, u32[]{:S(2)}) collective-permute-start(bf16[2,256,384]{2,1,0:T(8,128)(2,1)} %collective-permute-done.11.far_ref), channel_id=1, source_target_pairs={{0,2},{1,3},{2,0},{3,1},{4,6},{5,7},{6,4},{7,5},{8,10},{9,11},{10,... | collective-permute-start | bytes 1179656 | tf_op jit(solution)/shard_map/ppermute | solution.py:287
  90.0 1.4 %copy-start.1 = (bf16[512,1536]{1,0:T(8,128)(2,1)S(1)}, bf16[512,1536]{1,0:T(8,128)(2,1)}, u32[]{:S(2)}) copy-start(bf16[512,1536]{1,0:T(8,128)(2,1)} %q_ref.7) | copy-start | bytes 4718596
  91.4 5.1 %copy-start.2 = (bf16[512,1536]{1,0:T(8,128)(2,1)S(1)}, bf16[512,1536]{1,0:T(8,128)(2,1)}, u32[]{:S(2)}) copy-start(bf16[512,1536]{1,0:T(8,128)(2,1)} %q_ref.7) | copy-start | bytes 4718596
  101.7 7.2 %collective-permute-start.20 = (bf16[2,256,384]{2,1,0:T(8,128)(2,1)}, bf16[2,256,384]{2,1,0:T(8,128)(2,1)}, u32[]{:S(2)}, u32[]{:S(2)}) collective-permute-start(bf16[2,256,384]{2,1,0:T(8,128)(2,1)} %collective-permute-done.12.near_ref), channel_id=1, source_target_pairs={{0,1},{1,0},{2,3},{3,2},{4,5},{5,4},{6,7},{7,6},{8,9},{9,8},{10,11... | collective-permute-start | bytes 1179656 | tf_op jit(solution)/shard_map/ppermute | solution.py:287
  101.7 7.2 %collective-permute-start.21 = (bf16[2,256,384]{2,1,0:T(8,128)(2,1)}, bf16[2,256,384]{2,1,0:T(8,128)(2,1)}, u32[]{:S(2)}, u32[]{:S(2)}) collective-permute-start(bf16[2,256,384]{2,1,0:T(8,128)(2,1)} %collective-permute-done.17.far_ref), channel_id=1, source_target_pairs={{0,1},{1,0},{2,3},{3,2},{4,5},{5,4},{6,7},{7,6},{8,9},{9,8},{10,11... | collective-permute-start | bytes 1179656 | tf_op jit(solution)/shard_map/ppermute | solution.py:287
  102.4 1.4 %copy-start.3 = (bf16[512,1536]{1,0:T(8,128)(2,1)S(1)}, bf16[512,1536]{1,0:T(8,128)(2,1)}, u32[]{:S(2)}) copy-start(bf16[512,1536]{1,0:T(8,128)(2,1)} %q_ref.7) | copy-start | bytes 4718596

commit v13 on v10

--- a/solution.py
+++ b/solution.py
@@ -34,8 +34,8 @@
     return base, total, [w.astype(jnp.bfloat16) for w in weights]
 
 
-def pack_kernel(kv_ref, out_ref, below_ref, *refs):
-    across_refs, diagonal_refs, (held, came, left) = refs[0:2], refs[2:4], refs[4:]
+def pack_kernel(kv_ref, out_ref, *refs):
+    below_refs, across_refs, diagonal_refs, (held, came, left) = refs[0:2], refs[2:4], refs[4:6], refs[6:]
     groups, _, rows, part = out_ref.shape
     few, wide, pieces = rows // 4, groups * part // 2, [(s, i) for s in range(2) for i in range(4)]
     arrive = {}
@@ -50,7 +50,7 @@
         right = held.at[s, band, pl.ds(wide, wide)]
         moves = [(right, (across_refs if i < 2 else diagonal_refs)[s].at[place])]
         if i >= 2:
-            moves.append((held.at[s, band, pl.ds(0, wide)], below_ref.at[s, place]))
+            moves.append((held.at[s, band, pl.ds(0, wide)], below_refs[s].at[place]))
         moves += [(held.at[s, band, pl.ds(g * part, part)], out_ref.at[g, s, band]) for g in range(groups)]
         for n, (source, target) in enumerate(moves):
             leave.append(pltpu.make_async_copy(source, target, left.at[s, i, n]))
@@ -63,15 +63,11 @@
     _, rows, width = kv.shape
     anywhere = pl.BlockSpec(memory_space=pl.ANY)
     half = jax.ShapeDtypeStruct((rows // 2, width // 2), kv.dtype)
-    out, below, *others = pl.pallas_call(
+    out, *quarters = pl.pallas_call(
         pack_kernel,
         in_specs=[anywhere],
-        out_specs=[anywhere] * 6,
-        out_shape=[
-            jax.ShapeDtypeStruct((groups, 2, rows, width // groups), kv.dtype),
-            jax.ShapeDtypeStruct((2, rows // 2, width // 2), kv.dtype),
-        ]
-        + [half] * 4,
+        out_specs=[anywhere] * 7,
+        out_shape=[jax.ShapeDtypeStruct((groups, 2, rows, width // groups), kv.dtype)] + [half] * 6,
         scratch_shapes=[
             pltpu.VMEM(kv.shape, kv.dtype),
             pltpu.SemaphoreType.DMA((2, 4)),
@@ -80,7 +76,7 @@
         cost_estimate=pl.CostEstimate(flops=0, bytes_accessed=6 * kv.size, transcendentals=0),
         name="pack_heads",
     )(kv)
-    return out, below, others[:2], others[2:]
+    return out, quarters[:2], quarters[2:4], quarters[4:]
 
 
 def pipelined(tasks, score, finish):
@@ -289,13 +285,17 @@
     cores = groups // 2
     first = (lax.axis_index("hst") == 0) & (lax.axis_index("grp") == 0)
     send = lambda x, to: lax.ppermute(x, BOTH, [(0, to)])
-    down = send(below, groups)
     _, rows, width = kv.shape
     slabs = []
     for s in range(2):
-        slab = jnp.where(first, kv[s, : rows // 2, : width // 2], 0.0) + send(diagonal[s], groups + cores) + send(across[s], cores)
-        slabs.append(slab + (after(down[s], slabs[0]) if s else down[s]))
-    return slabs, down
+        down = send(below[s], groups)
+        if s:
+            down = after(down, slabs[0])
+        else:
+            come = down
+        slab = jnp.where(first, kv[s, : rows // 2, : width // 2], 0.0)
+        slabs.append(slab + send(diagonal[s], groups + cores) + send(across[s], cores) + down)
+    return slabs, come
 
 
 def spread_anchor(slab, hosts, groups):
@@ -323,6 +323,7 @@
     swapped = lax.all_to_all(after(packed, down), "grp", split_axis=0, concat_axis=0, tiled=True)
     near = jnp.stack([spread_anchor(x, hosts, groups) for x in slabs])
     gathered = gather_hosts(after(suffix_queries, slabs[1]), hosts)
+    token_ids = after(token_ids, slabs[1])
     seen = (token_ids.reshape(-1, rows) >= NAMB) & (jnp.arange(rows)[None, :] < lengths[:, None])
     bias = jnp.where(seen, 0.0, NEG).astype(jnp.float32)
     suffix = functools.partial(suffix_attend, jnp.stack([host]), *gathered, swapped, suffix_kv, bias)

time: 117 us -> 122 us (1.043)
  waiting for transfers between devices: 11.8 us -> 16.2 us
  starting transfers between devices: 47.1 us -> 44.6 us
  other arithmetic: 9.61 us -> 11.9 us
    ppermute x5 -> x6, waiting for transfers between devices: 2.34 us -> 6.75 us  [scatter_anchor(): send = lambda x, to: lax.ppermute(x, BOTH, [(0, to)])]
    ppermute x4, starting transfers between devices: 10.3 us -> 6.8 us  [spread_anchor(): piece = piece + lax.ppermute(piece, 'hst', pairs)]
    ppermute x5 -> x6, starting transfers between devices: 12.8 us -> 15.5 us  [scatter_anchor(): send = lambda x, to: lax.ppermute(x, BOTH, [(0, to)])]
    ppermute x11, starting transfers between devices: 10.9 us -> 8.36 us  [swap(): lax.ppermute(x, axis, [(i, i ^ k) for i in range(lax.axis_size(axis))])]
    all_to_all x1, waiting for transfers between devices: 2.37 us -> 0.01 us  [per_device(): lax.all_to_all(after(packed, down), 'grp', split_axis=0, concat_axis=0, t...]
    add x2, other arithmetic: 0.06 us -> 1.93 us  [spread_anchor(): piece = piece + lax.ppermute(slab[:, c * wide:(c + 1) * wide], 'grp', pairs)]
    ppermute x4, waiting for transfers between devices: 7.1 us -> 8.72 us  [spread_anchor(): piece = piece + lax.ppermute(piece, 'hst', pairs)]
    slice x2, local copies, waits for them, and re-layouts: 0.04 us -> 1.39 us  [spread_anchor(): piece = piece + lax.ppermute(slab[:, c * wide:(c + 1) * wide], 'grp', pairs)]
  transfers between devices with their start and end apart: 24 -> 25, of which waited for: 5 -> 6; matrix products, arithmetic and copies ran while one was open for 6% -> 9% of each run, Pallas kernels for 29% -> 28%
where the time goes in v13:
time: 122 us; the launch traced here: 121 us
  starting transfers between devices  44.6 us (37%)
  Pallas kernels  40.6 us (33%)
  waiting for transfers between devices  16.2 us (13%)
  other arithmetic  11.9 us (10%)
  local copies, waits for them, and re-layouts  7.09 us (6%)
    pallas_call x4, Pallas kernels, context_attend(): pl.pallas_call(context_kernel, grid_spec=pltpu.PrefetchScalarGridSpec(num...  19.3 us
    ppermute x6, starting transfers between devices, scatter_anchor(): send = lambda x, to: lax.ppermute(x, BOTH, [(0, to)])  15.5 us
    pallas_call x2, Pallas kernels, suffix_attend(): pl.pallas_call(suffix_kernel, grid_spec=pltpu.PrefetchScalarGridSpec(num_...  14.7 us
    ppermute x4, waiting for transfers between devices, spread_anchor(): piece = piece + lax.ppermute(piece, 'hst', pairs)  8.72 us
    ppermute x11, starting transfers between devices, swap(): lax.ppermute(x, axis, [(i, i ^ k) for i in range(lax.axis_size(axis))])  8.36 us
    ppermute x4, starting transfers between devices, spread_anchor(): piece = piece + lax.ppermute(piece, 'hst', pairs)  6.8 us
    ppermute x6, waiting for transfers between devices, scatter_anchor(): send = lambda x, to: lax.ppermute(x, BOTH, [(0, to)])  6.75 us
    all_to_all x1, starting transfers between devices, per_device(): lax.all_to_all(parts, 'hst', split_axis=0, concat_axis=0, tiled=True)  5.64 us
  transfers between devices with their start and end apart: 25, of which 6 were waited for; matrix products, arithmetic and copies ran while one was open for 9% of the time, Pallas kernels for 28%

profile of v13, /device:TPU:0, one launch (start us, length us, event | category | flops | bytes accessed | tf_op | source)
XLA Modules:
  0.0 121.2 jit_solution(10439607052062549454)
XLA Ops:
  0.6 3.9 %pack_heads.1 = (bf16[4,2,512,384]{3,2,1,0:T(8,128)(2,1)}, bf16[256,768]{1,0:T(8,128)(2,1)}, bf16[256,768]{1,0:T(8,128)(2,1)}, bf16[256,768]{1,0:T(8,128)(2,1)},...) custom-call(bf16[2,512,1536]{2,1,0:T(8,128)(2,1)} %kv_ref.9), custom_call_target="tpu_custom_call" | custom-call | bytes 9437184 | tf_op jit(solution)/shard_map/pack_heads/pallas_call | solution.py:66
  4.5 5.6 %collective-permute-start.5 = (bf16[256,768]{1,0:T(8,128)(2,1)}, bf16[256,768]{1,0:T(8,128)(2,1)}, u32[]{:S(2)}, u32[]{:S(2)}) collective-permute-start(bf16[256,768]{1,0:T(8,128)(2,1)} %get-tuple-element.29), channel_id=1, source_target_pairs={{0,4}} | collective-permute-start | bytes 1179656 | tf_op jit(solution)/shard_map/ppermute | solution.py:287
  10.1 1.6 %collective-permute-start.3 = (bf16[256,768]{1,0:T(8,128)(2,1)}, bf16[256,768]{1,0:T(8,128)(2,1)S(1)}, u32[]{:S(2)}, u32[]{:S(2)}) collective-permute-start(bf16[256,768]{1,0:T(8,128)(2,1)} %get-tuple-element.27), channel_id=1, source_target_pairs={{0,6}} | collective-permute-start | bytes 1179656 | tf_op jit(solution)/shard_map/ppermute | solution.py:287
  11.7 2.1 %collective-permute-start.4 = (bf16[256,768]{1,0:T(8,128)(2,1)}, bf16[256,768]{1,0:T(8,128)(2,1)}, u32[]{:S(2)}, u32[]{:S(2)}) collective-permute-start(bf16[256,768]{1,0:T(8,128)(2,1)} %get-tuple-element.28), channel_id=1, source_target_pairs={{0,2}} | collective-permute-start | bytes 1179656 | tf_op jit(solution)/shard_map/ppermute | solution.py:287
  13.8 2.1 %collective-permute-start.2 = (bf16[256,768]{1,0:T(8,128)(2,1)}, bf16[256,768]{1,0:T(8,128)(2,1)}, u32[]{:S(2)}, u32[]{:S(2)}) collective-permute-start(bf16[256,768]{1,0:T(8,128)(2,1)} %get-tuple-element.26), channel_id=1, source_target_pairs={{0,4}} | collective-permute-start | bytes 1179656 | tf_op jit(solution)/shard_map/ppermute | solution.py:287
  15.9 2.0 %collective-permute-start = (bf16[256,768]{1,0:T(8,128)(2,1)}, bf16[256,768]{1,0:T(8,128)(2,1)}, u32[]{:S(2)}, u32[]{:S(2)}) collective-permute-start(bf16[256,768]{1,0:T(8,128)(2,1)} %get-tuple-element.24), channel_id=1, source_target_pairs={{0,6}} | collective-permute-start | bytes 1179656 | tf_op jit(solution)/shard_map/ppermute | solution.py:287
  17.9 2.0 %collective-permute-start.1 = (bf16[256,768]{1,0:T(8,128)(2,1)}, bf16[256,768]{1,0:T(8,128)(2,1)}, u32[]{:S(2)}, u32[]{:S(2)}) collective-permute-start(bf16[256,768]{1,0:T(8,128)(2,1)} %get-tuple-element.25), channel_id=1, source_target_pairs={{0,2}} | collective-permute-start | bytes 1179656 | tf_op jit(solution)/shard_map/ppermute | solution.py:287
  20.0 4.9 %all-to-all-start = ((bf16[4,2,512,384]{3,2,1,0:T(8,128)(2,1)}), bf16[4,2,512,384]{3,2,1,0:T(8,128)(2,1)}, u32[]{:S(2)}, u32[]{:S(2)}) async-start(bf16[4,2,512,384]{3,2,1,0:T(8,128)(2,1)} %get-tuple-element.33), calls=%async_computation | async-start | bytes 6291456 | tf_op jit(solution)/shard_map/all_to_all | solution.py:323
  24.9 0.7 copy-done.9
  25.7 1.3 %fusion.1 = bf16[256,768]{1,0:T(8,128)(2,1)S(1)} fusion(bf16[256,768]{1,0:T(8,128)(2,1)} %collective-permute-done.5, bf16[256,768]{1,0:T(8,128)(2,1)} %collective-permute-done.4, bf16[256,768]{1,0:T(8,128)(2,1)} %copy-done.9, bf16[2,512,1536]{2,1,0:T(8,128)(2,1)S(1)} %copy-done, pred[]{:T(512)S(6)} %and.17), kind=kLoop, calls=%fused_computation.4 | loop fusion | flops 786432 | bytes 1966081 | tf_op jit(solution)/shard_map/add | solution.py:297
  27.0 6.7 %collective-permute-done.1 = bf16[256,768]{1,0:T(8,128)(2,1)} collective-permute-done((bf16[256,768]{1,0:T(8,128)(2,1)}, bf16[256,768]{1,0:T(8,128)(2,1)}, u32[]{:S(2)}, u32[]{:S(2)}) %collective-permute-start.1) | collective-permute-done | bytes 393248 | tf_op jit(solution)/shard_map/ppermute | solution.py:287
  33.8 1.3 %fusion.3 = bf16[256,768]{1,0:T(8,128)(2,1)S(1)} fusion(bf16[256,768]{1,0:T(8,128)(2,1)} %collective-permute-done.2, bf16[256,768]{1,0:T(8,128)(2,1)} %collective-permute-done.1, bf16[256,768]{1,0:T(8,128)(2,1)} %collective-permute-done, bf16[2,512,1536]{2,1,0:T(8,128)(2,1)S(1)} %copy-done, pred[]{:T(512)S(6)} %and.17), kind=kLoop, calls=%fused_computation.7 | loop fusion | flops 786432 | bytes 1966081 | tf_op jit(solution)/shard_map/add | solution.py:297
  35.2 3.4 %collective-permute-start.14 = (bf16[128,384]{1,0:T(8,128)(2,1)}, bf16[128,384]{1,0:T(8,128)(2,1)}, u32[]{:S(2)}, u32[]{:S(2)}) collective-permute-start(bf16[128,384]{1,0:T(8,128)(2,1)} %param.10), channel_id=1, source_target_pairs={{0,8},{4,12},{8,0},{12,4},{16,24},{20,28},{24,16},{28,20},{1,9},{5... | collective-permute-start | bytes 294920 | tf_op jit(solution)/shard_map/ppermute | solution.py:272
  38.6 0.7 slice.25
  39.3 2.0 %collective-permute-start.6 = (bf16[256,384]{1,0:T(8,128)(2,1)}, bf16[256,384]{1,0:T(8,128)(2,1)}, u32[]{:S(2)}, u32[]{:S(2)}) collective-permute-start(bf16[256,384]{1,0:T(8,128)(2,1)} %slice.25), channel_id=1, source_target_pairs={{0,1},{2,3},{4,5},{6,7},{8,9},{10,11},{12,13},{14,15},{16,17},{18,... | collective-permute-start | bytes 589832 | tf_op jit(solution)/shard_map/ppermute | solution.py:307
  41.3 0.6 broadcast_compare_fusion
  41.9 0.7 slice.27
  42.6 1.3 %ge.11 = pred[32,512]{1,0:T(8,128)(4,1)} reshape(pred[16384]{0:T(1024)(128)(4,1)} %broadcast_compare_fusion) | data formatting | bytes 32768 | tf_op jit(solution)/shard_map/ge | solution.py:327
  44.0 1.4 %collective-permute-start.9 = (bf16[256,384]{1,0:T(8,128)(2,1)}, bf16[256,384]{1,0:T(8,128)(2,1)S(1)}, u32[]{:S(2)}, u32[]{:S(2)}) collective-permute-start(bf16[256,384]{1,0:T(8,128)(2,1)} %slice.27), channel_id=1, source_target_pairs={{0,1},{2,3},{4,5},{6,7},{8,9},{10,11},{12,13},{14,15},{16,17},{18,... | collective-permute-start | bytes 589832 | tf_op jit(solution)/shard_map/ppermute | solution.py:307
  45.4 1.0 slice_add_fusion.1
  46.4 2.9 %collective-permute-start.7 = (bf16[256,384]{1,0:T(8,128)(2,1)S(1)}, bf16[256,384]{1,0:T(8,128)(2,1)S(1)}, u32[]{:S(2)}, u32[]{:S(2)}) collective-permute-start(bf16[256,384]{1,0:T(8,128)(2,1)S(1)} %slice_add_fusion.1), channel_id=1, source_target_pairs={{0,16},{4,20},{1,17},{5,21},{2,18},{6,22},{3,19},{7,23}} | collective-permute-start | bytes 589832 | tf_op jit(solution)/shard_map/ppermute | solution.py:311
  49.3 1.0 slice_add_fusion
  50.3 1.3 %collective-permute-start.10 = (bf16[256,384]{1,0:T(8,128)(2,1)S(1)}, bf16[256,384]{1,0:T(8,128)(2,1)S(1)}, u32[]{:S(2)}, u32[]{:S(2)}) collective-permute-start(bf16[256,384]{1,0:T(8,128)(2,1)S(1)} %slice_add_fusion), channel_id=1, source_target_pairs={{0,16},{4,20},{1,17},{5,21},{2,18},{6,22},{3,19},{7,23}} | collective-permute-start | bytes 589832 | tf_op jit(solution)/shard_map/ppermute | solution.py:311
  51.6 2.4 %collective-permute-done.7 = bf16[256,384]{1,0:T(8,128)(2,1)S(1)} collective-permute-done((bf16[256,384]{1,0:T(8,128)(2,1)S(1)}, bf16[256,384]{1,0:T(8,128)(2,1)S(1)}, u32[]{:S(2)}, u32[]{:S(2)}) %collective-permute-start.7) | collective-permute-done | bytes 196640 | tf_op jit(solution)/shard_map/ppermute | solution.py:311
  54.0 1.3 %collective-permute-start.8 = (bf16[256,384]{1,0:T(8,128)(2,1)S(1)}, bf16[256,384]{1,0:T(8,128)(2,1)S(1)}, u32[]{:S(2)}, u32[]{:S(2)}) collective-permute-start(bf16[256,384]{1,0:T(8,128)(2,1)S(1)} %add.58), channel_id=1, source_target_pairs={{0,8},{4,12},{16,24},{20,28},{1,9},{5,13},{17,25},{21,29},{2,10},{... | collective-permute-start | bytes 589832 | tf_op jit(solution)/shard_map/ppermute | solution.py:311
  55.5 1.9 %pad_maximum_fusion.1.near_ref = bf16[4,128,384]{2,1,0:T(8,128)(2,1)} fusion(bf16[1,128,384]{2,1,0:T(8,128)(2,1)} %bitcast.11, bf16[1,128,384]{2,1,0:T(8,128)(2,1)} %bitcast.10, bf16[1,128,384]{2,1,0:T(8,128)(2,1)} %bitcast.9, bf16[1,128,384]{2,1,0:T(8,128)(2,1)} %bitcast.8), kind=kLoop, calls=%fused_computation.1 | loop fusion | flops 589824 | bytes 786432 | tf_op jit(solution)/shard_map/stack | solution.py:276
  57.3 0.8 collective-permute-done.10
  58.2 1.3 %collective-permute-start.11 = (bf16[256,384]{1,0:T(8,128)(2,1)S(1)}, bf16[256,384]{1,0:T(8,128)(2,1)S(1)}, u32[]{:S(2)}, u32[]{:S(2)}) collective-permute-start(bf16[256,384]{1,0:T(8,128)(2,1)S(1)} %add.61), channel_id=1, source_target_pairs={{0,8},{4,12},{16,24},{20,28},{1,9},{5,13},{17,25},{21,29},{2,10},{... | collective-permute-start | bytes 589832 | tf_op jit(solution)/shard_map/ppermute | solution.py:311
  59.5 2.8 %collective-permute-done.8 = bf16[256,384]{1,0:T(8,128)(2,1)S(1)} collective-permute-done((bf16[256,384]{1,0:T(8,128)(2,1)S(1)}, bf16[256,384]{1,0:T(8,128)(2,1)S(1)}, u32[]{:S(2)}, u32[]{:S(2)}) %collective-permute-start.8) | collective-permute-done | bytes 196640 | tf_op jit(solution)/shard_map/ppermute | solution.py:311
  62.4 2.7 %collective-permute-done.11 = bf16[256,384]{1,0:T(8,128)(2,1)S(1)} collective-permute-done((bf16[256,384]{1,0:T(8,128)(2,1)S(1)}, bf16[256,384]{1,0:T(8,128)(2,1)S(1)}, u32[]{:S(2)}, u32[]{:S(2)}) %collective-permute-start.11) | collective-permute-done | bytes 196640 | tf_op jit(solution)/shard_map/ppermute | solution.py:311
  65.1 0.8 pad_maximum_fusion.near_ref
  65.9 2.5 %collective-permute-start.13 = (bf16[2,256,384]{2,1,0:T(8,128)(2,1)}, bf16[2,256,384]{2,1,0:T(8,128)(2,1)}, u32[]{:S(2)}, u32[]{:S(2)}) collective-permute-start(bf16[2,256,384]{2,1,0:T(8,128)(2,1)} %pad_maximum_fusion.near_ref), channel_id=1, source_target_pairs={{0,2},{1,3},{2,0},{3,1},{4,6},{5,7},{6,4},{7,5},{8,10},{9,11},{10,... | collective-permute-start | bytes 1179656 | tf_op jit(solution)/shard_map/ppermute | solution.py:272
  68.5 9.3 %suffix_attend.2.rest_0_ = f32[8,136,384]{2,1,0:T(8,128)S(1)} custom-call(s32[1]{0:T(128)} %bitcast.7.at_ref, bf16[4,128,384]{2,1,0:T(8,128)(2,1)} %pad_maximum_fusion.1.near_ref, bf16[4,128,384]{2,1,0:T(8,128)(2,1)} %collective-permute-done.17.far_ref, bf16[4,2,512,384]{3,2,1,0:T(8,128)(2,1)} %all-to-all-done.kv_ref, bf16[2,128,384]{2,1,0:T(8,128)(2,1)S(1)} %copy-done.7, ...), custom_call_target="tpu_custom_call" | custom-call | flops 4563402752 | bytes 5242880 | tf_op jit(solution)/shard_map/suffix_attend/pallas_call | solution.py:144
  77.8 0.7 collective-permute-done.13.near_ref
  78.5 5.3 %suffix_attend.3 = f32[8,136,384]{2,1,0:T(8,128)S(1)} custom-call(s32[1]{0:T(128)} %bitcast.7.at_ref, bf16[4,128,384]{2,1,0:T(8,128)(2,1)} %pad_maximum_fusion.1.near_ref, bf16[4,128,384]{2,1,0:T(8,128)(2,1)} %collective-permute-done.17.far_ref, bf16[4,2,512,384]{3,2,1,0:T(8,128)(2,1)} %all-to-all-done.kv_ref, ...), custom_call_target="tpu_custom_call", output_to_operand_aliasing={{}: (6, {})} | custom-call | flops 2281701376 | bytes 2621440 | tf_op jit(solution)/shard_map/suffix_attend/pallas_call | solution.py:144
  83.9 0.8 copy-done.4
  84.6 1.0 convert_element_type.9
  85.7 5.6 %all-to-all-start.1 = ((f16[8,136,384]{2,1,0:T(8,128)(2,1)}), f16[8,136,384]{2,1,0:T(8,128)(2,1)}, u32[]{:S(2)}, u32[]{:S(2)}) async-start(f16[8,136,384]{2,1,0:T(8,128)(2,1)} %convert_element_type.9), calls=%async_computation.1 | async-start | bytes 1671168 | tf_op jit(solution)/shard_map/all_to_all | solution.py:340
  91.3 1.8 %collective-permute-start.18 = (bf16[2,256,384]{2,1,0:T(8,128)(2,1)}, bf16[2,256,384]{2,1,0:T(8,128)(2,1)}, u32[]{:S(2)}, u32[]{:S(2)}) collective-permute-start(bf16[2,256,384]{2,1,0:T(8,128)(2,1)} %collective-permute-done.12.far_ref), channel_id=1, source_target_pairs={{0,2},{1,3},{2,0},{3,1},{4,6},{5,7},{6,4},{7,5},{8,10},{9,11},{10,... | collective-permute-start | bytes 1179656 | tf_op jit(solution)/shard_map/ppermute | solution.py:272
  93.2 1.4 %copy-done.1 = bf16[512,1536]{1,0:T(8,128)(2,1)S(1)} copy-done((bf16[512,1536]{1,0:T(8,128)(2,1)S(1)}, bf16[512,1536]{1,0:T(8,128)(2,1)}, u32[]{:S(2)}) %copy-start.1) | copy-done | bytes 1572888
  94.6 4.9 %context_attend.4.rest_0_ = bf16[512,1536]{1,0:T(8,128)(2,1)} custom-call(s32[3]{0:T(128)S(1)} %add_add_fusion.2.at_ref, s32[32]{0:T(128)S(1)} %copy-done.6, bf16[512,1536]{1,0:T(8,128)(2,1)S(1)} %copy-done.1, bf16[2,512,1536]{2,1,0:T(8,128)(2,1)S(1)} %copy-done, f32[32,512]{1,0:T(8,128)S(1)} %fusion.5.bias_ref, ...), custom_call_target="tpu_custom_call" | custom-call | flops 805306368 | bytes 2359296 | tf_op jit(solution)/shard_map/context_attend/pallas_call | solution.py:243
  99.5 4.8 %context_attend.5.rest_0_ = bf16[512,1536]{1,0:T(8,128)(2,1)} custom-call(s32[3]{0:T(128)S(1)} %add_add_fusion.1.at_ref, s32[32]{0:T(128)S(1)} %copy-done.6, bf16[512,1536]{1,0:T(8,128)(2,1)S(1)} %copy-done.2, bf16[2,512,1536]{2,1,0:T(8,128)(2,1)S(1)} %copy-done, f32[32,512]{1,0:T(8,128)S(1)} %fusion.5.bias_ref, ...), custom_call_target="tpu_custom_call", output_to_operand_aliasing={{}: (7, {})} | custom-call | flops 805306368 | bytes 2359296 | tf_op jit(solution)/shard_map/context_attend/pallas_call | solution.py:243
  104.3 0.5 collective-permute-start.22
  105.0 1.4 %copy-done.3 = bf16[512,1536]{1,0:T(8,128)(2,1)S(1)} copy-done((bf16[512,1536]{1,0:T(8,128)(2,1)S(1)}, bf16[512,1536]{1,0:T(8,128)(2,1)}, u32[]{:S(2)}) %copy-start.3) | copy-done | bytes 1572888
  106.4 4.8 %context_attend.6.rest_0_ = bf16[512,1536]{1,0:T(8,128)(2,1)} custom-call(s32[3]{0:T(128)S(1)} %add_add_fusion.3.at_ref, s32[32]{0:T(128)S(1)} %copy-done.6, bf16[512,1536]{1,0:T(8,128)(2,1)S(1)} %copy-done.3, bf16[2,512,1536]{2,1,0:T(8,128)(2,1)S(1)} %copy-done, f32[32,512]{1,0:T(8,128)S(1)} %fusion.5.bias_ref, ...), custom_call_target="tpu_custom_call", output_to_operand_aliasing={{}: (7, {})} | custom-call | flops 805306368 | bytes 2359296 | tf_op jit(solution)/shard_map/context_attend/pallas_call | solution.py:243
  111.2 4.8 %context_attend.7 = bf16[512,1536]{1,0:T(8,128)(2,1)} custom-call(s32[3]{0:T(128)S(1)} %add_add_fusion.at_ref, s32[32]{0:T(128)S(1)} %copy-done.6, bf16[512,1536]{1,0:T(8,128)(2,1)S(1)} %copy-done.3, bf16[2,512,1536]{2,1,0:T(8,128)(2,1)S(1)} %copy-done, f32[32,512]{1,0:T(8,128)S(1)} %fusion.5.bias_ref, ...), custom_call_target="tpu_custom_call", output_to_operand_aliasing={{}: (7, {})} | custom-call | flops 805306368 | bytes 2359296 | tf_op jit(solution)/shard_map/context_attend/pallas_call | solution.py:243
  116.0 2.5 %convert_element_type.10.in_ref = f32[8,136,384]{2,1,0:T(8,128)} convert(f16[8,136,384]{2,1,0:T(8,128)(2,1)} %all-to-all-done.1) | non-fusion elementwise | flops 417792 | bytes 2506752 | tf_op jit(solution)/shard_map/convert_element_type | solution.py:356
  118.5 2.7 %combine_groups.1 = bf16[128,384]{1,0:T(8,128)(2,1)} custom-call(f32[8,136,384]{2,1,0:T(8,128)} %convert_element_type.10.in_ref), custom_call_target="tpu_custom_call" | custom-call | flops 835584 | bytes 1671168 | tf_op jit(solution)/shard_map/combine_groups/pallas_call | solution.py:188
  (55 shorter events, 0.8 us)
Async XLA Ops:
  4.5 13.4 %collective-permute-start.5 = (bf16[256,768]{1,0:T(8,128)(2,1)}, bf16[256,768]{1,0:T(8,128)(2,1)}, u32[]{:S(2)}, u32[]{:S(2)}) collective-permute-start(bf16[256,768]{1,0:T(8,128)(2,1)} %get-tuple-element.29), channel_id=1, source_target_pairs={{0,4}} | collective-permute-start | bytes 1179656 | tf_op jit(solution)/shard_map/ppermute | solution.py:287
  10.1 14.8 %collective-permute-start.3 = (bf16[256,768]{1,0:T(8,128)(2,1)}, bf16[256,768]{1,0:T(8,128)(2,1)S(1)}, u32[]{:S(2)}, u32[]{:S(2)}) collective-permute-start(bf16[256,768]{1,0:T(8,128)(2,1)} %get-tuple-element.27), channel_id=1, source_target_pairs={{0,6}} | collective-permute-start | bytes 1179656 | tf_op jit(solution)/shard_map/ppermute | solution.py:287
  11.7 13.9 %collective-permute-start.4 = (bf16[256,768]{1,0:T(8,128)(2,1)}, bf16[256,768]{1,0:T(8,128)(2,1)}, u32[]{:S(2)}, u32[]{:S(2)}) collective-permute-start(bf16[256,768]{1,0:T(8,128)(2,1)} %get-tuple-element.28), channel_id=1, source_target_pairs={{0,2}} | collective-permute-start | bytes 1179656 | tf_op jit(solution)/shard_map/ppermute | solution.py:287
  13.8 13.2 %collective-permute-start.2 = (bf16[256,768]{1,0:T(8,128)(2,1)}, bf16[256,768]{1,0:T(8,128)(2,1)}, u32[]{:S(2)}, u32[]{:S(2)}) collective-permute-start(bf16[256,768]{1,0:T(8,128)(2,1)} %get-tuple-element.26), channel_id=1, source_target_pairs={{0,4}} | collective-permute-start | bytes 1179656 | tf_op jit(solution)/shard_map/ppermute | solution.py:287
  15.9 11.1 %collective-permute-start = (bf16[256,768]{1,0:T(8,128)(2,1)}, bf16[256,768]{1,0:T(8,128)(2,1)}, u32[]{:S(2)}, u32[]{:S(2)}) collective-permute-start(bf16[256,768]{1,0:T(8,128)(2,1)} %get-tuple-element.24), channel_id=1, source_target_pairs={{0,6}} | collective-permute-start | bytes 1179656 | tf_op jit(solution)/shard_map/ppermute | solution.py:287
  17.9 15.8 %collective-permute-start.1 = (bf16[256,768]{1,0:T(8,128)(2,1)}, bf16[256,768]{1,0:T(8,128)(2,1)}, u32[]{:S(2)}, u32[]{:S(2)}) collective-permute-start(bf16[256,768]{1,0:T(8,128)(2,1)} %get-tuple-element.25), channel_id=1, source_target_pairs={{0,2}} | collective-permute-start | bytes 1179656 | tf_op jit(solution)/shard_map/ppermute | solution.py:287
  20.0 5.7 %copy-start = (bf16[2,512,1536]{2,1,0:T(8,128)(2,1)S(1)}, bf16[2,512,1536]{2,1,0:T(8,128)(2,1)}, u32[]{:S(2)}) copy-start(bf16[2,512,1536]{2,1,0:T(8,128)(2,1)} %kv_ref.9) | copy-start | bytes 9437188
  20.0 45.9 %all-to-all-start = ((bf16[4,2,512,384]{3,2,1,0:T(8,128)(2,1)}), bf16[4,2,512,384]{3,2,1,0:T(8,128)(2,1)}, u32[]{:S(2)}, u32[]{:S(2)}) async-start(bf16[4,2,512,384]{3,2,1,0:T(8,128)(2,1)} %get-tuple-element.33), calls=%async_computation | async-start | bytes 6291456 | tf_op jit(solution)/shard_map/all_to_all | solution.py:323
  24.9 0.7 copy-start.9
  27.0 14.3 %copy-start.10 = (s32[16384]{0:T(1024)S(1)}, s32[16384]{0:T(1024)}, u32[]{:S(2)}) copy-start(s32[16384]{0:T(1024)} %param.8) | copy-start | bytes 196612
  35.1 6.9 %copy-start.8 = (bf16[256,768]{1,0:T(8,128)(2,1)}, bf16[256,768]{1,0:T(8,128)(2,1)S(1)}, u32[]{:S(2)}) copy-start(bf16[256,768]{1,0:T(8,128)(2,1)S(1)} %fusion.3) | copy-start | bytes 1179652
  35.1 20.2 %copy-start.6 = (s32[32]{0:T(128)S(1)}, s32[32]{0:T(128)}, u32[]{:S(2)}) copy-start(s32[32]{0:T(128)} %len_ref.7) | copy-start | bytes 388
  35.1 20.3 %collective-permute-start.15 = (bf16[128,384]{1,0:T(8,128)(2,1)}, bf16[128,384]{1,0:T(8,128)(2,1)}, u32[]{:S(2)}, u32[]{:S(2)}) collective-permute-start(bf16[128,384]{1,0:T(8,128)(2,1)} %param.10), channel_id=1, source_target_pairs={{0,16},{4,20},{8,24},{12,28},{16,0},{20,4},{24,8},{28,12},{1,17},{... | collective-permute-start | bytes 294920 | tf_op jit(solution)/shard_map/ppermute | solution.py:272
  35.2 20.3 %collective-permute-start.16 = (bf16[128,384]{1,0:T(8,128)(2,1)}, bf16[128,384]{1,0:T(8,128)(2,1)}, u32[]{:S(2)}, u32[]{:S(2)}) collective-permute-start(bf16[128,384]{1,0:T(8,128)(2,1)} %param.10), channel_id=1, source_target_pairs={{0,24},{4,28},{8,16},{12,20},{16,8},{20,12},{24,0},{28,4},{1,25},{... | collective-permute-start | bytes 294920 | tf_op jit(solution)/shard_map/ppermute | solution.py:272
  35.2 20.2 %collective-permute-start.14 = (bf16[128,384]{1,0:T(8,128)(2,1)}, bf16[128,384]{1,0:T(8,128)(2,1)}, u32[]{:S(2)}, u32[]{:S(2)}) collective-permute-start(bf16[128,384]{1,0:T(8,128)(2,1)} %param.10), channel_id=1, source_target_pairs={{0,8},{4,12},{8,0},{12,4},{16,24},{20,28},{24,16},{28,20},{1,9},{5... | collective-permute-start | bytes 294920 | tf_op jit(solution)/shard_map/ppermute | solution.py:272
  39.3 6.1 %collective-permute-start.6 = (bf16[256,384]{1,0:T(8,128)(2,1)}, bf16[256,384]{1,0:T(8,128)(2,1)}, u32[]{:S(2)}, u32[]{:S(2)}) collective-permute-start(bf16[256,384]{1,0:T(8,128)(2,1)} %slice.25), channel_id=1, source_target_pairs={{0,1},{2,3},{4,5},{6,7},{8,9},{10,11},{12,13},{14,15},{16,17},{18,... | collective-permute-start | bytes 589832 | tf_op jit(solution)/shard_map/ppermute | solution.py:307
  44.0 11.3 %copy-start.11 = (pred[32,512]{1,0:T(8,128)(4,1)S(1)}, pred[32,512]{1,0:T(8,128)(4,1)}, u32[]{:S(2)}) copy-start(pred[32,512]{1,0:T(8,128)(4,1)} %ge.11) | copy-start | bytes 49156
  44.0 5.3 %collective-permute-start.9 = (bf16[256,384]{1,0:T(8,128)(2,1)}, bf16[256,384]{1,0:T(8,128)(2,1)S(1)}, u32[]{:S(2)}, u32[]{:S(2)}) collective-permute-start(bf16[256,384]{1,0:T(8,128)(2,1)} %slice.27), channel_id=1, source_target_pairs={{0,1},{2,3},{4,5},{6,7},{8,9},{10,11},{12,13},{14,15},{16,17},{18,... | collective-permute-start | bytes 589832 | tf_op jit(solution)/shard_map/ppermute | solution.py:307
  46.4 7.6 %collective-permute-start.7 = (bf16[256,384]{1,0:T(8,128)(2,1)S(1)}, bf16[256,384]{1,0:T(8,128)(2,1)S(1)}, u32[]{:S(2)}, u32[]{:S(2)}) collective-permute-start(bf16[256,384]{1,0:T(8,128)(2,1)S(1)} %slice_add_fusion.1), channel_id=1, source_target_pairs={{0,16},{4,20},{1,17},{5,21},{2,18},{6,22},{3,19},{7,23}} | collective-permute-start | bytes 589832 | tf_op jit(solution)/shard_map/ppermute | solution.py:311
  50.3 7.9 %collective-permute-start.10 = (bf16[256,384]{1,0:T(8,128)(2,1)S(1)}, bf16[256,384]{1,0:T(8,128)(2,1)S(1)}, u32[]{:S(2)}, u32[]{:S(2)}) collective-permute-start(bf16[256,384]{1,0:T(8,128)(2,1)S(1)} %slice_add_fusion), channel_id=1, source_target_pairs={{0,16},{4,20},{1,17},{5,21},{2,18},{6,22},{3,19},{7,23}} | collective-permute-start | bytes 589832 | tf_op jit(solution)/shard_map/ppermute | solution.py:311
  54.0 8.4 %collective-permute-start.8 = (bf16[256,384]{1,0:T(8,128)(2,1)S(1)}, bf16[256,384]{1,0:T(8,128)(2,1)S(1)}, u32[]{:S(2)}, u32[]{:S(2)}) collective-permute-start(bf16[256,384]{1,0:T(8,128)(2,1)S(1)} %add.58), channel_id=1, source_target_pairs={{0,8},{4,12},{16,24},{20,28},{1,9},{5,13},{17,25},{21,29},{2,10},{... | collective-permute-start | bytes 589832 | tf_op jit(solution)/shard_map/ppermute | solution.py:311
  55.4 13.0 %copy-start.7 = (bf16[2,128,384]{2,1,0:T(8,128)(2,1)S(1)}, bf16[2,128,384]{2,1,0:T(8,128)(2,1)}, u32[]{:S(2)}) copy-start(bf16[2,128,384]{2,1,0:T(8,128)(2,1)} %sk_ref.3) | copy-start | bytes 589828
  57.3 11.1 %collective-permute-start.17 = (bf16[4,128,384]{2,1,0:T(8,128)(2,1)}, bf16[4,128,384]{2,1,0:T(8,128)(2,1)}, u32[]{:S(2)}, u32[]{:S(2)}) collective-permute-start(bf16[4,128,384]{2,1,0:T(8,128)(2,1)} %pad_maximum_fusion.1.near_ref), channel_id=1, source_target_pairs={{0,4},{4,0},{8,12},{12,8},{16,20},{20,16},{24,28},{28,24},{1,5},{5... | collective-permute-start | bytes 1179656 | tf_op jit(solution)/shard_map/ppermute | solution.py:272
  58.2 6.9 %collective-permute-start.11 = (bf16[256,384]{1,0:T(8,128)(2,1)S(1)}, bf16[256,384]{1,0:T(8,128)(2,1)S(1)}, u32[]{:S(2)}, u32[]{:S(2)}) collective-permute-start(bf16[256,384]{1,0:T(8,128)(2,1)S(1)} %add.61), channel_id=1, source_target_pairs={{0,8},{4,12},{16,24},{20,28},{1,9},{5,13},{17,25},{21,29},{2,10},{... | collective-permute-start | bytes 589832 | tf_op jit(solution)/shard_map/ppermute | solution.py:311
  65.9 11.9 %collective-permute-start.12 = (bf16[2,256,384]{2,1,0:T(8,128)(2,1)}, bf16[2,256,384]{2,1,0:T(8,128)(2,1)}, u32[]{:S(2)}, u32[]{:S(2)}) collective-permute-start(bf16[2,256,384]{2,1,0:T(8,128)(2,1)} %pad_maximum_fusion.near_ref), channel_id=1, source_target_pairs={{0,4},{4,0},{8,12},{12,8},{16,20},{20,16},{24,28},{28,24},{1,5},{5... | collective-permute-start | bytes 1179656 | tf_op jit(solution)/shard_map/ppermute | solution.py:272
  65.9 18.0 %collective-permute-start.19 = (bf16[2,256,384]{2,1,0:T(8,128)(2,1)}, bf16[2,256,384]{2,1,0:T(8,128)(2,1)}, u32[]{:S(2)}, u32[]{:S(2)}) collective-permute-start(bf16[2,256,384]{2,1,0:T(8,128)(2,1)} %pad_maximum_fusion.near_ref), channel_id=1, source_target_pairs={{0,1},{1,0},{2,3},{3,2},{4,5},{5,4},{6,7},{7,6},{8,9},{9,8},{10,11... | collective-permute-start | bytes 1179656 | tf_op jit(solution)/shard_map/ppermute | solution.py:272
  65.9 12.6 %collective-permute-start.13 = (bf16[2,256,384]{2,1,0:T(8,128)(2,1)}, bf16[2,256,384]{2,1,0:T(8,128)(2,1)}, u32[]{:S(2)}, u32[]{:S(2)}) collective-permute-start(bf16[2,256,384]{2,1,0:T(8,128)(2,1)} %pad_maximum_fusion.near_ref), channel_id=1, source_target_pairs={{0,2},{1,3},{2,0},{3,1},{4,6},{5,7},{6,4},{7,5},{8,10},{9,11},{10,... | collective-permute-start | bytes 1179656 | tf_op jit(solution)/shard_map/ppermute | solution.py:272
  78.5 5.4 %collective-permute-start.20 = (bf16[2,256,384]{2,1,0:T(8,128)(2,1)}, bf16[2,256,384]{2,1,0:T(8,128)(2,1)S(1)}, u32[]{:S(2)}, u32[]{:S(2)}) collective-permute-start(bf16[2,256,384]{2,1,0:T(8,128)(2,1)} %collective-permute-done.12.far_ref), channel_id=1, source_target_pairs={{0,1},{1,0},{2,3},{3,2},{4,5},{5,4},{6,7},{7,6},{8,9},{9,8},{10,11... | collective-permute-start | bytes 1179656 | tf_op jit(solution)/shard_map/ppermute | solution.py:272
  83.9 0.8 copy-start.4
  85.7 30.4 %all-to-all-start.1 = ((f16[8,136,384]{2,1,0:T(8,128)(2,1)}), f16[8,136,384]{2,1,0:T(8,128)(2,1)}, u32[]{:S(2)}, u32[]{:S(2)}) async-start(f16[8,136,384]{2,1,0:T(8,128)(2,1)} %convert_element_type.9), calls=%async_computation.1 | async-start | bytes 1671168 | tf_op jit(solution)/shard_map/all_to_all | solution.py:340
  91.3 13.0 %collective-permute-start.18 = (bf16[2,256,384]{2,1,0:T(8,128)(2,1)}, bf16[2,256,384]{2,1,0:T(8,128)(2,1)}, u32[]{:S(2)}, u32[]{:S(2)}) collective-permute-start(bf16[2,256,384]{2,1,0:T(8,128)(2,1)} %collective-permute-done.12.far_ref), channel_id=1, source_target_pairs={{0,2},{1,3},{2,0},{3,1},{4,6},{5,7},{6,4},{7,5},{8,10},{9,11},{10,... | collective-permute-start | bytes 1179656 | tf_op jit(solution)/shard_map/ppermute | solution.py:272
  93.2 1.4 %copy-start.1 = (bf16[512,1536]{1,0:T(8,128)(2,1)S(1)}, bf16[512,1536]{1,0:T(8,128)(2,1)}, u32[]{:S(2)}) copy-start(bf16[512,1536]{1,0:T(8,128)(2,1)} %q_ref.7) | copy-start | bytes 4718596
  94.6 4.9 %copy-start.2 = (bf16[512,1536]{1,0:T(8,128)(2,1)S(1)}, bf16[512,1536]{1,0:T(8,128)(2,1)}, u32[]{:S(2)}) copy-start(bf16[512,1536]{1,0:T(8,128)(2,1)} %q_ref.7) | copy-start | bytes 4718596
  94.6 4.9 %copy-start.5 = (bf16[2,256,384]{2,1,0:T(8,128)(2,1)S(1)}, bf16[2,256,384]{2,1,0:T(8,128)(2,1)}, u32[]{:S(2)}) copy-start(bf16[2,256,384]{2,1,0:T(8,128)(2,1)} %copy-done.4) | copy-start | bytes 1179652
  104.3 6.9 %collective-permute-start.21 = (bf16[2,256,384]{2,1,0:T(8,128)(2,1)}, bf16[2,256,384]{2,1,0:T(8,128)(2,1)}, u32[]{:S(2)}, u32[]{:S(2)}) collective-permute-start(bf16[2,256,384]{2,1,0:T(8,128)(2,1)} %collective-permute-done.13.near_ref), channel_id=1, source_target_pairs={{0,1},{1,0},{2,3},{3,2},{4,5},{5,4},{6,7},{7,6},{8,9},{9,8},{10,11... | collective-permute-start | bytes 1179656 | tf_op jit(solution)/shard_map/ppermute | solution.py:272
  104.3 6.9 %collective-permute-start.22 = (bf16[2,256,384]{2,1,0:T(8,128)(2,1)}, bf16[2,256,384]{2,1,0:T(8,128)(2,1)}, u32[]{:S(2)}, u32[]{:S(2)}) collective-permute-start(bf16[2,256,384]{2,1,0:T(8,128)(2,1)} %collective-permute-done.18.far_ref), channel_id=1, source_target_pairs={{0,1},{1,0},{2,3},{3,2},{4,5},{5,4},{6,7},{7,6},{8,9},{9,8},{10,11... | collective-permute-start | bytes 1179656 | tf_op jit(solution)/shard_map/ppermute | solution.py:272
  105.0 1.4 %copy-start.3 = (bf16[512,1536]{1,0:T(8,128)(2,1)S(1)}, bf16[512,1536]{1,0:T(8,128)(2,1)}, u32[]{:S(2)}) copy-start(bf16[512,1536]{1,0:T(8,128)(2,1)} %q_ref.7) | copy-start | bytes 4718596

commit v14 on v13

--- a/solution.py
+++ b/solution.py
@@ -284,17 +284,17 @@
 def scatter_anchor(kv, across, diagonal, below, groups):
     cores = groups // 2
     first = (lax.axis_index("hst") == 0) & (lax.axis_index("grp") == 0)
-    send = lambda x, to: lax.ppermute(x, BOTH, [(0, to)])
+    send = lambda x, to: lax.ppermute(x, BOTH, [(0, to), (to, 0)])
     _, rows, width = kv.shape
-    slabs = []
+    slabs, come = [], None
     for s in range(2):
         down = send(below[s], groups)
         if s:
             down = after(down, slabs[0])
         else:
             come = down
-        slab = jnp.where(first, kv[s, : rows // 2, : width // 2], 0.0)
-        slabs.append(slab + send(diagonal[s], groups + cores) + send(across[s], cores) + down)
+        got = send(diagonal[s], groups + cores) + send(across[s], cores) + down
+        slabs.append(jnp.where(first, kv[s, : rows // 2, : width // 2], got))
     return slabs, come
 
 
@@ -305,12 +305,13 @@
     for c in range(1, cores):
         pairs = [(x, x + c) for x in (0, cores)]
         piece = piece + lax.ppermute(slab[:, c * wide : (c + 1) * wide], "grp", pairs)
+    shared = piece
     far = hosts // 2
     while far >= 2:
         pairs = [(h, h + far) for h in range(hosts) if h % (2 * far) < 2]
         piece = piece + lax.ppermute(piece, "hst", pairs)
         far //= 2
-    return piece
+    return piece, shared
 
 
 def per_device(queries, keys_values, token_ids, lengths, suffix_queries, suffix_kv):
@@ -321,9 +322,9 @@
     packed, below, across, diagonal = pack(keys_values, groups)
     slabs, down = scatter_anchor(keys_values, across, diagonal, below, groups)
     swapped = lax.all_to_all(after(packed, down), "grp", split_axis=0, concat_axis=0, tiled=True)
-    near = jnp.stack([spread_anchor(x, hosts, groups) for x in slabs])
-    gathered = gather_hosts(after(suffix_queries, slabs[1]), hosts)
-    token_ids = after(token_ids, slabs[1])
+    spread = [spread_anchor(x, hosts, groups) for x in slabs]
+    near = jnp.stack([x for x, _ in spread])
+    gathered = gather_hosts(after(suffix_queries, spread[1][1]), hosts)
     seen = (token_ids.reshape(-1, rows) >= NAMB) & (jnp.arange(rows)[None, :] < lengths[:, None])
     bias = jnp.where(seen, 0.0, NEG).astype(jnp.float32)
     suffix = functools.partial(suffix_attend, jnp.stack([host]), *gathered, swapped, suffix_kv, bias)

time: 122 us -> 117 us (0.959)
  starting transfers between devices: 44.6 us -> 42.3 us
  other arithmetic: 11.9 us -> 9.69 us
  local copies, waits for them, and re-layouts: 7.09 us -> 5 us
    ppermute x6, waiting for transfers between devices: 6.75 us -> 0.81 us  [scatter_anchor(): send = lambda x, to: lax.ppermute(x, BOTH, [(0, to), (to, 0)])]
    all_to_all x1, waiting for transfers between devices: 0.01 us -> 3.7 us  [per_device(): lax.all_to_all(after(packed, down), 'grp', split_axis=0, concat_axis=0, t...]
    ppermute x11, waiting for transfers between devices: 0.71 us -> 4.23 us  [swap(): lax.ppermute(x, axis, [(i, i ^ k) for i in range(lax.axis_size(axis))])]
    add x2 -> x0, other arithmetic: 2.61 us -> none  [scatter_anchor(): slab + send(diagonal[s], groups + cores) + send(across[s], cores) + down]
    select_n x0 -> x2, other arithmetic: none -> 2.53 us  [scatter_anchor(): slabs.append(jnp.where(first, kv[s, :rows // 2, :width // 2], got))]
    add x2, other arithmetic: 1.93 us -> 0.06 us  [spread_anchor(): piece = piece + lax.ppermute(slab[:, c * wide:(c + 1) * wide], 'grp', pairs)]
    ppermute x11, starting transfers between devices: 8.36 us -> 6.74 us  [swap(): lax.ppermute(x, axis, [(i, i ^ k) for i in range(lax.axis_size(axis))])]
    slice x2, local copies, waits for them, and re-layouts: 1.39 us -> 0.04 us  [spread_anchor(): piece = piece + lax.ppermute(slab[:, c * wide:(c + 1) * wide], 'grp', pairs)]
  transfers between devices with their start and end apart: 25 -> 25, of which waited for: 6 -> 9; matrix products, arithmetic and copies ran while one was open for 9% -> 7% of each run, Pallas kernels for 28% -> 29%
where the time goes in v14:
time: 117 us; the launch traced here: 116 us
  starting transfers between devices  42.3 us (36%)
  Pallas kernels  40.6 us (35%)
  waiting for transfers between devices  17 us (15%)
  other arithmetic  9.69 us (8%)
  local copies, waits for them, and re-layouts  5 us (4%)
    pallas_call x4, Pallas kernels, context_attend(): pl.pallas_call(context_kernel, grid_spec=pltpu.PrefetchScalarGridSpec(num...  19.3 us
    ppermute x6, starting transfers between devices, scatter_anchor(): send = lambda x, to: lax.ppermute(x, BOTH, [(0, to), (to, 0)])  15.6 us
    pallas_call x2, Pallas kernels, suffix_attend(): pl.pallas_call(suffix_kernel, grid_spec=pltpu.PrefetchScalarGridSpec(num_...  14.7 us
    ppermute x4, waiting for transfers between devices, spread_anchor(): piece = piece + lax.ppermute(piece, 'hst', pairs)  8.26 us
    ppermute x4, starting transfers between devices, spread_anchor(): piece = piece + lax.ppermute(piece, 'hst', pairs)  6.79 us
    ppermute x11, starting transfers between devices, swap(): lax.ppermute(x, axis, [(i, i ^ k) for i in range(lax.axis_size(axis))])  6.74 us
    all_to_all x1, starting transfers between devices, per_device(): lax.all_to_all(after(packed, down), 'grp', split_axis=0, concat_axis=0, t...  4.92 us
    all_to_all x1, starting transfers between devices, per_device(): lax.all_to_all(parts, 'hst', split_axis=0, concat_axis=0, tiled=True)  4.4 us
  transfers between devices with their start and end apart: 25, of which 9 were waited for; matrix products, arithmetic and copies ran while one was open for 7% of the time, Pallas kernels for 29%

profile of v14, /device:TPU:0, one launch (start us, length us, event | category | flops | bytes accessed | tf_op | source)
XLA Modules:
  0.0 115.6 jit_solution(12774527141353926867)
XLA Ops:
  0.6 3.9 %pack_heads.1 = (bf16[4,2,512,384]{3,2,1,0:T(8,128)(2,1)}, bf16[256,768]{1,0:T(8,128)(2,1)}, bf16[256,768]{1,0:T(8,128)(2,1)}, bf16[256,768]{1,0:T(8,128)(2,1)},...) custom-call(bf16[2,512,1536]{2,1,0:T(8,128)(2,1)} %kv_ref.9), custom_call_target="tpu_custom_call" | custom-call | bytes 9437184 | tf_op jit(solution)/shard_map/pack_heads/pallas_call | solution.py:66
  4.5 4.9 %collective-permute-start.2 = (bf16[256,768]{1,0:T(8,128)(2,1)}, bf16[256,768]{1,0:T(8,128)(2,1)S(1)}, u32[]{:S(2)}, u32[]{:S(2)}) collective-permute-start(bf16[256,768]{1,0:T(8,128)(2,1)} %get-tuple-element.25), channel_id=1, source_target_pairs={{0,4},{4,0}} | collective-permute-start | bytes 1179656 | tf_op jit(solution)/shard_map/ppermute | solution.py:287
  9.4 1.9 %collective-permute-start = (bf16[256,768]{1,0:T(8,128)(2,1)}, bf16[256,768]{1,0:T(8,128)(2,1)}, u32[]{:S(2)}, u32[]{:S(2)}) collective-permute-start(bf16[256,768]{1,0:T(8,128)(2,1)} %get-tuple-element.23), channel_id=1, source_target_pairs={{0,6},{6,0}} | collective-permute-start | bytes 1179656 | tf_op jit(solution)/shard_map/ppermute | solution.py:287
  11.3 1.9 %collective-permute-start.1 = (bf16[256,768]{1,0:T(8,128)(2,1)}, bf16[256,768]{1,0:T(8,128)(2,1)}, u32[]{:S(2)}, u32[]{:S(2)}) collective-permute-start(bf16[256,768]{1,0:T(8,128)(2,1)} %get-tuple-element.24), channel_id=1, source_target_pairs={{0,2},{2,0}} | collective-permute-start | bytes 1179656 | tf_op jit(solution)/shard_map/ppermute | solution.py:287
  13.2 1.9 %collective-permute-start.8 = (bf16[256,768]{1,0:T(8,128)(2,1)}, bf16[256,768]{1,0:T(8,128)(2,1)S(1)}, u32[]{:S(2)}, u32[]{:S(2)}) collective-permute-start(bf16[256,768]{1,0:T(8,128)(2,1)} %get-tuple-element.28), channel_id=1, source_target_pairs={{0,4},{4,0}} | collective-permute-start | bytes 1179656 | tf_op jit(solution)/shard_map/ppermute | solution.py:287
  15.2 3.1 %collective-permute-start.6 = (bf16[256,768]{1,0:T(8,128)(2,1)}, bf16[256,768]{1,0:T(8,128)(2,1)}, u32[]{:S(2)}, u32[]{:S(2)}) collective-permute-start(bf16[256,768]{1,0:T(8,128)(2,1)} %get-tuple-element.26), channel_id=1, source_target_pairs={{0,6},{6,0}} | collective-permute-start | bytes 1179656 | tf_op jit(solution)/shard_map/ppermute | solution.py:287
  18.3 1.9 %collective-permute-start.7 = (bf16[256,768]{1,0:T(8,128)(2,1)}, bf16[256,768]{1,0:T(8,128)(2,1)}, u32[]{:S(2)}, u32[]{:S(2)}) collective-permute-start(bf16[256,768]{1,0:T(8,128)(2,1)} %get-tuple-element.27), channel_id=1, source_target_pairs={{0,2},{2,0}} | collective-permute-start | bytes 1179656 | tf_op jit(solution)/shard_map/ppermute | solution.py:287
  20.2 4.9 %all-to-all-start = ((bf16[4,2,512,384]{3,2,1,0:T(8,128)(2,1)}), bf16[4,2,512,384]{3,2,1,0:T(8,128)(2,1)}, u32[]{:S(2)}, u32[]{:S(2)}) async-start(bf16[4,2,512,384]{3,2,1,0:T(8,128)(2,1)} %get-tuple-element.31), calls=%async_computation | async-start | bytes 6291456 | tf_op jit(solution)/shard_map/all_to_all | solution.py:324
  25.2 1.5 %broadcast_compare_fusion = pred[16384]{0:T(1024)(128)(4,1)} fusion(s32[16384]{0:T(1024)} %param.8), kind=kLoop, calls=%fused_computation.11 | loop fusion | flops 16384 | bytes 81920 | tf_op jit(solution)/shard_map/ge | solution.py:328
  26.6 1.4 %ge.11 = pred[32,512]{1,0:T(8,128)(4,1)} reshape(pred[16384]{0:T(1024)(128)(4,1)} %broadcast_compare_fusion) | data formatting | bytes 32768 | tf_op jit(solution)/shard_map/ge | solution.py:328
  28.0 1.3 %bitcast_select_fusion.1 = bf16[256,768]{1,0:T(8,128)(2,1)S(1)} fusion(bf16[256,768]{1,0:T(8,128)(2,1)} %copy-done.8, bf16[256,768]{1,0:T(8,128)(2,1)} %collective-permute-done, bf16[256,768]{1,0:T(8,128)(2,1)} %collective-permute-done.1, bf16[2,512,1536]{2,1,0:T(8,128)(2,1)S(1)} %copy-done, pred[]{:T(512)S(6)} %and.18), kind=kLoop, calls=%fused_computation.3 | loop fusion | flops 589824 | bytes 1966081 | tf_op jit(solution)/shard_map/jit(_where)/select_n | solution.py:297
  29.4 2.5 %collective-permute-start.3 = (bf16[256,384]{1,0:T(8,128)(2,1)S(1)}, bf16[256,384]{1,0:T(8,128)(2,1)S(1)}, u32[]{:S(2)}, u32[]{:S(2)}) collective-permute-start(bf16[256,384]{1,0:T(8,128)(2,1)S(1)} %slice.25), channel_id=1, source_target_pairs={{0,1},{2,3},{4,5},{6,7},{8,9},{10,11},{12,13},{14,15},{16,17},{18,... | collective-permute-start | bytes 589832 | tf_op jit(solution)/shard_map/ppermute | solution.py:307
  31.9 0.8 collective-permute-done.7
  32.7 1.2 %bitcast_select_fusion = bf16[256,768]{1,0:T(8,128)(2,1)S(1)} fusion(bf16[256,768]{1,0:T(8,128)(2,1)S(1)} %collective-permute-done.8, bf16[256,768]{1,0:T(8,128)(2,1)} %collective-permute-done.6, bf16[256,768]{1,0:T(8,128)(2,1)} %collective-permute-done.7, bf16[2,512,1536]{2,1,0:T(8,128)(2,1)S(1)} %copy-done, pred[]{:T(512)S(6)} %and.18), kind=kLoop, calls=%fused_computation.2 | loop fusion | flops 589824 | bytes 1966081 | tf_op jit(solution)/shard_map/jit(_where)/select_n | solution.py:297
  33.9 1.3 %collective-permute-start.9 = (bf16[256,384]{1,0:T(8,128)(2,1)S(1)}, bf16[256,384]{1,0:T(8,128)(2,1)S(1)}, u32[]{:S(2)}, u32[]{:S(2)}) collective-permute-start(bf16[256,384]{1,0:T(8,128)(2,1)S(1)} %slice.27), channel_id=1, source_target_pairs={{0,1},{2,3},{4,5},{6,7},{8,9},{10,11},{12,13},{14,15},{16,17},{18,... | collective-permute-start | bytes 589832 | tf_op jit(solution)/shard_map/ppermute | solution.py:307
  35.3 1.3 %collective-permute-start.4 = (bf16[256,384]{1,0:T(8,128)(2,1)S(1)}, bf16[256,384]{1,0:T(8,128)(2,1)S(1)}, u32[]{:S(2)}, u32[]{:S(2)}) collective-permute-start(bf16[256,384]{1,0:T(8,128)(2,1)S(1)} %slice_add_fusion.1), channel_id=1, source_target_pairs={{0,16},{4,20},{1,17},{5,21},{2,18},{6,22},{3,19},{7,23}} | collective-permute-start | bytes 589832 | tf_op jit(solution)/shard_map/ppermute | solution.py:312
  36.8 3.4 %collective-permute-start.14 = (bf16[128,384]{1,0:T(8,128)(2,1)S(1)}, bf16[128,384]{1,0:T(8,128)(2,1)S(1)}, u32[]{:S(2)}, u32[]{:S(2)}) collective-permute-start(bf16[128,384]{1,0:T(8,128)(2,1)S(1)} %copy-done.9), channel_id=1, source_target_pairs={{0,8},{4,12},{8,0},{12,4},{16,24},{20,28},{24,16},{28,20},{1,9},{5... | collective-permute-start | bytes 294920 | tf_op jit(solution)/shard_map/ppermute | solution.py:272
  40.2 2.9 %collective-permute-start.10 = (bf16[256,384]{1,0:T(8,128)(2,1)S(1)}, bf16[256,384]{1,0:T(8,128)(2,1)S(1)}, u32[]{:S(2)}, u32[]{:S(2)}) collective-permute-start(bf16[256,384]{1,0:T(8,128)(2,1)S(1)} %slice_add_fusion), channel_id=1, source_target_pairs={{0,16},{4,20},{1,17},{5,21},{2,18},{6,22},{3,19},{7,23}} | collective-permute-start | bytes 589832 | tf_op jit(solution)/shard_map/ppermute | solution.py:312
  43.2 1.3 %collective-permute-start.5 = (bf16[256,384]{1,0:T(8,128)(2,1)S(1)}, bf16[256,384]{1,0:T(8,128)(2,1)S(1)}, u32[]{:S(2)}, u32[]{:S(2)}) collective-permute-start(bf16[256,384]{1,0:T(8,128)(2,1)S(1)} %add.48), channel_id=1, source_target_pairs={{0,8},{4,12},{16,24},{20,28},{1,9},{5,13},{17,25},{21,29},{2,10},{... | collective-permute-start | bytes 589832 | tf_op jit(solution)/shard_map/ppermute | solution.py:312
  44.5 0.1 fusion.1.bias_ref
  44.6 0.8 collective-permute-done.15
  45.4 0.8 collective-permute-done.16
  46.2 2.1 %collective-permute-done.14 = bf16[128,384]{1,0:T(8,128)(2,1)S(1)} collective-permute-done((bf16[128,384]{1,0:T(8,128)(2,1)S(1)}, bf16[128,384]{1,0:T(8,128)(2,1)S(1)}, u32[]{:S(2)}, u32[]{:S(2)}) %collective-permute-start.14) | collective-permute-done | bytes 98336 | tf_op jit(solution)/shard_map/ppermute | solution.py:272
  48.3 0.8 pad_maximum_fusion.1.near_ref
  49.1 3.4 %collective-permute-done.10 = bf16[256,384]{1,0:T(8,128)(2,1)S(1)} collective-permute-done((bf16[256,384]{1,0:T(8,128)(2,1)S(1)}, bf16[256,384]{1,0:T(8,128)(2,1)S(1)}, u32[]{:S(2)}, u32[]{:S(2)}) %collective-permute-start.10) | collective-permute-done | bytes 196640 | tf_op jit(solution)/shard_map/ppermute | solution.py:312
  52.6 1.3 %collective-permute-start.11 = (bf16[256,384]{1,0:T(8,128)(2,1)S(1)}, bf16[256,384]{1,0:T(8,128)(2,1)S(1)}, u32[]{:S(2)}, u32[]{:S(2)}) collective-permute-start(bf16[256,384]{1,0:T(8,128)(2,1)S(1)} %add.53), channel_id=1, source_target_pairs={{0,8},{4,12},{16,24},{20,28},{1,9},{5,13},{17,25},{21,29},{2,10},{... | collective-permute-start | bytes 589832 | tf_op jit(solution)/shard_map/ppermute | solution.py:312
  53.9 2.8 %collective-permute-done.5 = bf16[256,384]{1,0:T(8,128)(2,1)S(1)} collective-permute-done((bf16[256,384]{1,0:T(8,128)(2,1)S(1)}, bf16[256,384]{1,0:T(8,128)(2,1)S(1)}, u32[]{:S(2)}, u32[]{:S(2)}) %collective-permute-start.5) | collective-permute-done | bytes 196640 | tf_op jit(solution)/shard_map/ppermute | solution.py:312
  56.7 2.1 %collective-permute-done.11 = bf16[256,384]{1,0:T(8,128)(2,1)S(1)} collective-permute-done((bf16[256,384]{1,0:T(8,128)(2,1)S(1)}, bf16[256,384]{1,0:T(8,128)(2,1)S(1)}, u32[]{:S(2)}, u32[]{:S(2)}) %collective-permute-start.11) | collective-permute-done | bytes 196640 | tf_op jit(solution)/shard_map/ppermute | solution.py:312
  58.8 0.8 pad_maximum_fusion.near_ref
  59.6 3.7 %all-to-all-done.kv_ref = bf16[4,2,512,384]{3,2,1,0:T(8,128)(2,1)} async-done(((bf16[4,2,512,384]{3,2,1,0:T(8,128)(2,1)}), bf16[4,2,512,384]{3,2,1,0:T(8,128)(2,1)}, u32[]{:S(2)}, u32[]{:S(2)}) %all-to-all-start) | async-done | bytes 3145760 | tf_op jit(solution)/shard_map/all_to_all | solution.py:324
  63.3 2.5 %collective-permute-start.13 = (bf16[2,256,384]{2,1,0:T(8,128)(2,1)}, bf16[2,256,384]{2,1,0:T(8,128)(2,1)}, u32[]{:S(2)}, u32[]{:S(2)}) collective-permute-start(bf16[2,256,384]{2,1,0:T(8,128)(2,1)} %pad_maximum_fusion.near_ref), channel_id=1, source_target_pairs={{0,2},{1,3},{2,0},{3,1},{4,6},{5,7},{6,4},{7,5},{8,10},{9,11},{10,... | collective-permute-start | bytes 1179656 | tf_op jit(solution)/shard_map/ppermute | solution.py:272
  65.8 9.3 %suffix_attend.2.rest_0_ = f32[8,136,384]{2,1,0:T(8,128)S(1)} custom-call(s32[1]{0:T(128)} %bitcast.7.at_ref, bf16[4,128,384]{2,1,0:T(8,128)(2,1)} %pad_maximum_fusion.1.near_ref, bf16[4,128,384]{2,1,0:T(8,128)(2,1)} %collective-permute-done.17.far_ref, bf16[4,2,512,384]{3,2,1,0:T(8,128)(2,1)} %all-to-all-done.kv_ref, bf16[2,128,384]{2,1,0:T(8,128)(2,1)S(1)} %copy-done.7, ...), custom_call_target="tpu_custom_call" | custom-call | flops 4563402752 | bytes 5242880 | tf_op jit(solution)/shard_map/suffix_attend/pallas_call | solution.py:144
  75.2 5.4 %suffix_attend.3 = f32[8,136,384]{2,1,0:T(8,128)S(1)} custom-call(s32[1]{0:T(128)} %bitcast.7.at_ref, bf16[4,128,384]{2,1,0:T(8,128)(2,1)} %pad_maximum_fusion.1.near_ref, bf16[4,128,384]{2,1,0:T(8,128)(2,1)} %collective-permute-done.17.far_ref, bf16[4,2,512,384]{3,2,1,0:T(8,128)(2,1)} %all-to-all-done.kv_ref, ...), custom_call_target="tpu_custom_call", output_to_operand_aliasing={{}: (6, {})} | custom-call | flops 2281701376 | bytes 2621440 | tf_op jit(solution)/shard_map/suffix_attend/pallas_call | solution.py:144
  80.6 0.7 copy-done.4
  81.4 1.0 convert_element_type.6
  82.4 4.4 %all-to-all-start.1 = ((f16[8,136,384]{2,1,0:T(8,128)(2,1)}), f16[8,136,384]{2,1,0:T(8,128)(2,1)}, u32[]{:S(2)}, u32[]{:S(2)}) async-start(f16[8,136,384]{2,1,0:T(8,128)(2,1)} %convert_element_type.6), calls=%async_computation.1 | async-start | bytes 1671168 | tf_op jit(solution)/shard_map/all_to_all | solution.py:341
  86.8 0.1 collective-permute-start.18
  86.9 0.1 add_add_fusion.2.at_ref
  87.1 1.4 %copy-done.1 = bf16[512,1536]{1,0:T(8,128)(2,1)S(1)} copy-done((bf16[512,1536]{1,0:T(8,128)(2,1)S(1)}, bf16[512,1536]{1,0:T(8,128)(2,1)}, u32[]{:S(2)}) %copy-start.1) | copy-done | bytes 1572888
  88.5 4.9 %context_attend.4.rest_0_ = bf16[512,1536]{1,0:T(8,128)(2,1)} custom-call(s32[3]{0:T(128)S(1)} %add_add_fusion.2.at_ref, s32[32]{0:T(128)S(1)} %copy-done.6, bf16[512,1536]{1,0:T(8,128)(2,1)S(1)} %copy-done.1, bf16[2,512,1536]{2,1,0:T(8,128)(2,1)S(1)} %copy-done, f32[32,512]{1,0:T(8,128)S(1)} %fusion.1.bias_ref, ...), custom_call_target="tpu_custom_call" | custom-call | flops 805306368 | bytes 2359296 | tf_op jit(solution)/shard_map/context_attend/pallas_call | solution.py:243
  93.4 4.8 %context_attend.5.rest_0_ = bf16[512,1536]{1,0:T(8,128)(2,1)} custom-call(s32[3]{0:T(128)S(1)} %add_add_fusion.1.at_ref, s32[32]{0:T(128)S(1)} %copy-done.6, bf16[512,1536]{1,0:T(8,128)(2,1)S(1)} %copy-done.2, bf16[2,512,1536]{2,1,0:T(8,128)(2,1)S(1)} %copy-done, f32[32,512]{1,0:T(8,128)S(1)} %fusion.1.bias_ref, ...), custom_call_target="tpu_custom_call", output_to_operand_aliasing={{}: (7, {})} | custom-call | flops 805306368 | bytes 2359296 | tf_op jit(solution)/shard_map/context_attend/pallas_call | solution.py:243
  98.2 0.5 collective-permute-done.18.far_ref
  98.7 0.5 collective-permute-start.22
  99.4 1.4 %copy-done.3 = bf16[512,1536]{1,0:T(8,128)(2,1)S(1)} copy-done((bf16[512,1536]{1,0:T(8,128)(2,1)S(1)}, bf16[512,1536]{1,0:T(8,128)(2,1)}, u32[]{:S(2)}) %copy-start.3) | copy-done | bytes 1572888
  100.8 4.8 %context_attend.6.rest_0_ = bf16[512,1536]{1,0:T(8,128)(2,1)} custom-call(s32[3]{0:T(128)S(1)} %add_add_fusion.3.at_ref, s32[32]{0:T(128)S(1)} %copy-done.6, bf16[512,1536]{1,0:T(8,128)(2,1)S(1)} %copy-done.3, bf16[2,512,1536]{2,1,0:T(8,128)(2,1)S(1)} %copy-done, f32[32,512]{1,0:T(8,128)S(1)} %fusion.1.bias_ref, ...), custom_call_target="tpu_custom_call", output_to_operand_aliasing={{}: (7, {})} | custom-call | flops 805306368 | bytes 2359296 | tf_op jit(solution)/shard_map/context_attend/pallas_call | solution.py:243
  105.6 4.8 %context_attend.7 = bf16[512,1536]{1,0:T(8,128)(2,1)} custom-call(s32[3]{0:T(128)S(1)} %add_add_fusion.at_ref, s32[32]{0:T(128)S(1)} %copy-done.6, bf16[512,1536]{1,0:T(8,128)(2,1)S(1)} %copy-done.3, bf16[2,512,1536]{2,1,0:T(8,128)(2,1)S(1)} %copy-done, f32[32,512]{1,0:T(8,128)S(1)} %fusion.1.bias_ref, ...), custom_call_target="tpu_custom_call", output_to_operand_aliasing={{}: (7, {})} | custom-call | flops 805306368 | bytes 2359296 | tf_op jit(solution)/shard_map/context_attend/pallas_call | solution.py:243
  110.4 2.5 %convert_element_type.7.in_ref = f32[8,136,384]{2,1,0:T(8,128)} convert(f16[8,136,384]{2,1,0:T(8,128)(2,1)} %all-to-all-done.1) | non-fusion elementwise | flops 417792 | bytes 2506752 | tf_op jit(solution)/shard_map/convert_element_type | solution.py:357
  112.9 2.7 %combine_groups.1 = bf16[128,384]{1,0:T(8,128)(2,1)} custom-call(f32[8,136,384]{2,1,0:T(8,128)} %convert_element_type.7.in_ref), custom_call_target="tpu_custom_call" | custom-call | flops 835584 | bytes 1671168 | tf_op jit(solution)/shard_map/combine_groups/pallas_call | solution.py:188
  (53 shorter events, 0.8 us)
Async XLA Ops:
  4.5 13.8 %collective-permute-start.2 = (bf16[256,768]{1,0:T(8,128)(2,1)}, bf16[256,768]{1,0:T(8,128)(2,1)S(1)}, u32[]{:S(2)}, u32[]{:S(2)}) collective-permute-start(bf16[256,768]{1,0:T(8,128)(2,1)} %get-tuple-element.25), channel_id=1, source_target_pairs={{0,4},{4,0}} | collective-permute-start | bytes 1179656 | tf_op jit(solution)/shard_map/ppermute | solution.py:287
  9.4 18.6 %collective-permute-start = (bf16[256,768]{1,0:T(8,128)(2,1)}, bf16[256,768]{1,0:T(8,128)(2,1)}, u32[]{:S(2)}, u32[]{:S(2)}) collective-permute-start(bf16[256,768]{1,0:T(8,128)(2,1)} %get-tuple-element.23), channel_id=1, source_target_pairs={{0,6},{6,0}} | collective-permute-start | bytes 1179656 | tf_op jit(solution)/shard_map/ppermute | solution.py:287
  11.3 16.7 %collective-permute-start.1 = (bf16[256,768]{1,0:T(8,128)(2,1)}, bf16[256,768]{1,0:T(8,128)(2,1)}, u32[]{:S(2)}, u32[]{:S(2)}) collective-permute-start(bf16[256,768]{1,0:T(8,128)(2,1)} %get-tuple-element.24), channel_id=1, source_target_pairs={{0,2},{2,0}} | collective-permute-start | bytes 1179656 | tf_op jit(solution)/shard_map/ppermute | solution.py:287
  13.2 16.1 %collective-permute-start.8 = (bf16[256,768]{1,0:T(8,128)(2,1)}, bf16[256,768]{1,0:T(8,128)(2,1)S(1)}, u32[]{:S(2)}, u32[]{:S(2)}) collective-permute-start(bf16[256,768]{1,0:T(8,128)(2,1)} %get-tuple-element.28), channel_id=1, source_target_pairs={{0,4},{4,0}} | collective-permute-start | bytes 1179656 | tf_op jit(solution)/shard_map/ppermute | solution.py:287
  15.2 16.7 %collective-permute-start.6 = (bf16[256,768]{1,0:T(8,128)(2,1)}, bf16[256,768]{1,0:T(8,128)(2,1)}, u32[]{:S(2)}, u32[]{:S(2)}) collective-permute-start(bf16[256,768]{1,0:T(8,128)(2,1)} %get-tuple-element.26), channel_id=1, source_target_pairs={{0,6},{6,0}} | collective-permute-start | bytes 1179656 | tf_op jit(solution)/shard_map/ppermute | solution.py:287
  18.3 1.9 %copy-start.8 = (bf16[256,768]{1,0:T(8,128)(2,1)}, bf16[256,768]{1,0:T(8,128)(2,1)S(1)}, u32[]{:S(2)}) copy-start(bf16[256,768]{1,0:T(8,128)(2,1)S(1)} %collective-permute-done.2) | copy-start | bytes 1179652
  18.3 14.4 %collective-permute-start.7 = (bf16[256,768]{1,0:T(8,128)(2,1)}, bf16[256,768]{1,0:T(8,128)(2,1)}, u32[]{:S(2)}, u32[]{:S(2)}) collective-permute-start(bf16[256,768]{1,0:T(8,128)(2,1)} %get-tuple-element.27), channel_id=1, source_target_pairs={{0,2},{2,0}} | collective-permute-start | bytes 1179656 | tf_op jit(solution)/shard_map/ppermute | solution.py:287
  20.2 7.8 %copy-start = (bf16[2,512,1536]{2,1,0:T(8,128)(2,1)S(1)}, bf16[2,512,1536]{2,1,0:T(8,128)(2,1)}, u32[]{:S(2)}) copy-start(bf16[2,512,1536]{2,1,0:T(8,128)(2,1)} %kv_ref.9) | copy-start | bytes 9437188
  20.2 43.1 %all-to-all-start = ((bf16[4,2,512,384]{3,2,1,0:T(8,128)(2,1)}), bf16[4,2,512,384]{3,2,1,0:T(8,128)(2,1)}, u32[]{:S(2)}, u32[]{:S(2)}) async-start(bf16[4,2,512,384]{3,2,1,0:T(8,128)(2,1)} %get-tuple-element.31), calls=%async_computation | async-start | bytes 6291456 | tf_op jit(solution)/shard_map/all_to_all | solution.py:324
  29.3 7.3 %copy-start.9 = (bf16[128,384]{1,0:T(8,128)(2,1)S(1)}, bf16[128,384]{1,0:T(8,128)(2,1)}, u32[]{:S(2)}) copy-start(bf16[128,384]{1,0:T(8,128)(2,1)} %param.10) | copy-start | bytes 294916
  29.3 15.1 %copy-start.6 = (s32[32]{0:T(128)S(1)}, s32[32]{0:T(128)}, u32[]{:S(2)}) copy-start(s32[32]{0:T(128)} %len_ref.7) | copy-start | bytes 388
  29.3 15.1 %copy-start.10 = (pred[32,512]{1,0:T(8,128)(4,1)S(1)}, pred[32,512]{1,0:T(8,128)(4,1)}, u32[]{:S(2)}) copy-start(pred[32,512]{1,0:T(8,128)(4,1)} %ge.11) | copy-start | bytes 49156
  29.4 5.9 %collective-permute-start.3 = (bf16[256,384]{1,0:T(8,128)(2,1)S(1)}, bf16[256,384]{1,0:T(8,128)(2,1)S(1)}, u32[]{:S(2)}, u32[]{:S(2)}) collective-permute-start(bf16[256,384]{1,0:T(8,128)(2,1)S(1)} %slice.25), channel_id=1, source_target_pairs={{0,1},{2,3},{4,5},{6,7},{8,9},{10,11},{12,13},{14,15},{16,17},{18,... | collective-permute-start | bytes 589832 | tf_op jit(solution)/shard_map/ppermute | solution.py:307
  33.9 2.7 %collective-permute-start.9 = (bf16[256,384]{1,0:T(8,128)(2,1)S(1)}, bf16[256,384]{1,0:T(8,128)(2,1)S(1)}, u32[]{:S(2)}, u32[]{:S(2)}) collective-permute-start(bf16[256,384]{1,0:T(8,128)(2,1)S(1)} %slice.27), channel_id=1, source_target_pairs={{0,1},{2,3},{4,5},{6,7},{8,9},{10,11},{12,13},{14,15},{16,17},{18,... | collective-permute-start | bytes 589832 | tf_op jit(solution)/shard_map/ppermute | solution.py:307
  35.3 7.8 %collective-permute-start.4 = (bf16[256,384]{1,0:T(8,128)(2,1)S(1)}, bf16[256,384]{1,0:T(8,128)(2,1)S(1)}, u32[]{:S(2)}, u32[]{:S(2)}) collective-permute-start(bf16[256,384]{1,0:T(8,128)(2,1)S(1)} %slice_add_fusion.1), channel_id=1, source_target_pairs={{0,16},{4,20},{1,17},{5,21},{2,18},{6,22},{3,19},{7,23}} | collective-permute-start | bytes 589832 | tf_op jit(solution)/shard_map/ppermute | solution.py:312
  36.7 8.8 %collective-permute-start.15 = (bf16[128,384]{1,0:T(8,128)(2,1)S(1)}, bf16[128,384]{1,0:T(8,128)(2,1)S(1)}, u32[]{:S(2)}, u32[]{:S(2)}) collective-permute-start(bf16[128,384]{1,0:T(8,128)(2,1)S(1)} %copy-done.9), channel_id=1, source_target_pairs={{0,16},{4,20},{8,24},{12,28},{16,0},{20,4},{24,8},{28,12},{1,17},{... | collective-permute-start | bytes 294920 | tf_op jit(solution)/shard_map/ppermute | solution.py:272
  36.7 9.5 %collective-permute-start.16 = (bf16[128,384]{1,0:T(8,128)(2,1)S(1)}, bf16[128,384]{1,0:T(8,128)(2,1)S(1)}, u32[]{:S(2)}, u32[]{:S(2)}) collective-permute-start(bf16[128,384]{1,0:T(8,128)(2,1)S(1)} %copy-done.9), channel_id=1, source_target_pairs={{0,24},{4,28},{8,16},{12,20},{16,8},{20,12},{24,0},{28,4},{1,25},{... | collective-permute-start | bytes 294920 | tf_op jit(solution)/shard_map/ppermute | solution.py:272
  36.8 11.5 %collective-permute-start.14 = (bf16[128,384]{1,0:T(8,128)(2,1)S(1)}, bf16[128,384]{1,0:T(8,128)(2,1)S(1)}, u32[]{:S(2)}, u32[]{:S(2)}) collective-permute-start(bf16[128,384]{1,0:T(8,128)(2,1)S(1)} %copy-done.9), channel_id=1, source_target_pairs={{0,8},{4,12},{8,0},{12,4},{16,24},{20,28},{24,16},{28,20},{1,9},{5... | collective-permute-start | bytes 294920 | tf_op jit(solution)/shard_map/ppermute | solution.py:272
  40.2 12.3 %collective-permute-start.10 = (bf16[256,384]{1,0:T(8,128)(2,1)S(1)}, bf16[256,384]{1,0:T(8,128)(2,1)S(1)}, u32[]{:S(2)}, u32[]{:S(2)}) collective-permute-start(bf16[256,384]{1,0:T(8,128)(2,1)S(1)} %slice_add_fusion), channel_id=1, source_target_pairs={{0,16},{4,20},{1,17},{5,21},{2,18},{6,22},{3,19},{7,23}} | collective-permute-start | bytes 589832 | tf_op jit(solution)/shard_map/ppermute | solution.py:312
  43.2 13.5 %collective-permute-start.5 = (bf16[256,384]{1,0:T(8,128)(2,1)S(1)}, bf16[256,384]{1,0:T(8,128)(2,1)S(1)}, u32[]{:S(2)}, u32[]{:S(2)}) collective-permute-start(bf16[256,384]{1,0:T(8,128)(2,1)S(1)} %add.48), channel_id=1, source_target_pairs={{0,8},{4,12},{16,24},{20,28},{1,9},{5,13},{17,25},{21,29},{2,10},{... | collective-permute-start | bytes 589832 | tf_op jit(solution)/shard_map/ppermute | solution.py:312
  48.3 17.5 %copy-start.7 = (bf16[2,128,384]{2,1,0:T(8,128)(2,1)S(1)}, bf16[2,128,384]{2,1,0:T(8,128)(2,1)}, u32[]{:S(2)}) copy-start(bf16[2,128,384]{2,1,0:T(8,128)(2,1)} %sk_ref.3) | copy-start | bytes 589828
  49.1 16.7 %collective-permute-start.17 = (bf16[4,128,384]{2,1,0:T(8,128)(2,1)}, bf16[4,128,384]{2,1,0:T(8,128)(2,1)}, u32[]{:S(2)}, u32[]{:S(2)}) collective-permute-start(bf16[4,128,384]{2,1,0:T(8,128)(2,1)} %pad_maximum_fusion.1.near_ref), channel_id=1, source_target_pairs={{0,4},{4,0},{8,12},{12,8},{16,20},{20,16},{24,28},{28,24},{1,5},{5... | collective-permute-start | bytes 1179656 | tf_op jit(solution)/shard_map/ppermute | solution.py:272
  52.6 6.2 %collective-permute-start.11 = (bf16[256,384]{1,0:T(8,128)(2,1)S(1)}, bf16[256,384]{1,0:T(8,128)(2,1)S(1)}, u32[]{:S(2)}, u32[]{:S(2)}) collective-permute-start(bf16[256,384]{1,0:T(8,128)(2,1)S(1)} %add.53), channel_id=1, source_target_pairs={{0,8},{4,12},{16,24},{20,28},{1,9},{5,13},{17,25},{21,29},{2,10},{... | collective-permute-start | bytes 589832 | tf_op jit(solution)/shard_map/ppermute | solution.py:312
  59.6 15.5 %collective-permute-start.12 = (bf16[2,256,384]{2,1,0:T(8,128)(2,1)}, bf16[2,256,384]{2,1,0:T(8,128)(2,1)}, u32[]{:S(2)}, u32[]{:S(2)}) collective-permute-start(bf16[2,256,384]{2,1,0:T(8,128)(2,1)} %pad_maximum_fusion.near_ref), channel_id=1, source_target_pairs={{0,4},{4,0},{8,12},{12,8},{16,20},{20,16},{24,28},{28,24},{1,5},{5... | collective-permute-start | bytes 1179656 | tf_op jit(solution)/shard_map/ppermute | solution.py:272
  59.6 21.0 %collective-permute-start.19 = (bf16[2,256,384]{2,1,0:T(8,128)(2,1)}, bf16[2,256,384]{2,1,0:T(8,128)(2,1)}, u32[]{:S(2)}, u32[]{:S(2)}) collective-permute-start(bf16[2,256,384]{2,1,0:T(8,128)(2,1)} %pad_maximum_fusion.near_ref), channel_id=1, source_target_pairs={{0,1},{1,0},{2,3},{3,2},{4,5},{5,4},{6,7},{7,6},{8,9},{9,8},{10,11... | collective-permute-start | bytes 1179656 | tf_op jit(solution)/shard_map/ppermute | solution.py:272
  63.3 11.8 %collective-permute-start.13 = (bf16[2,256,384]{2,1,0:T(8,128)(2,1)}, bf16[2,256,384]{2,1,0:T(8,128)(2,1)}, u32[]{:S(2)}, u32[]{:S(2)}) collective-permute-start(bf16[2,256,384]{2,1,0:T(8,128)(2,1)} %pad_maximum_fusion.near_ref), channel_id=1, source_target_pairs={{0,2},{1,3},{2,0},{3,1},{4,6},{5,7},{6,4},{7,5},{8,10},{9,11},{10,... | collective-permute-start | bytes 1179656 | tf_op jit(solution)/shard_map/ppermute | solution.py:272
  75.2 5.5 %collective-permute-start.20 = (bf16[2,256,384]{2,1,0:T(8,128)(2,1)}, bf16[2,256,384]{2,1,0:T(8,128)(2,1)S(1)}, u32[]{:S(2)}, u32[]{:S(2)}) collective-permute-start(bf16[2,256,384]{2,1,0:T(8,128)(2,1)} %collective-permute-done.12.far_ref), channel_id=1, source_target_pairs={{0,1},{1,0},{2,3},{3,2},{4,5},{5,4},{6,7},{7,6},{8,9},{9,8},{10,11... | collective-permute-start | bytes 1179656 | tf_op jit(solution)/shard_map/ppermute | solution.py:272
  80.6 0.7 copy-start.4
  82.4 28.0 %all-to-all-start.1 = ((f16[8,136,384]{2,1,0:T(8,128)(2,1)}), f16[8,136,384]{2,1,0:T(8,128)(2,1)}, u32[]{:S(2)}, u32[]{:S(2)}) async-start(f16[8,136,384]{2,1,0:T(8,128)(2,1)} %convert_element_type.6), calls=%async_computation.1 | async-start | bytes 1671168 | tf_op jit(solution)/shard_map/all_to_all | solution.py:341
  86.8 11.9 %collective-permute-start.18 = (bf16[2,256,384]{2,1,0:T(8,128)(2,1)}, bf16[2,256,384]{2,1,0:T(8,128)(2,1)}, u32[]{:S(2)}, u32[]{:S(2)}) collective-permute-start(bf16[2,256,384]{2,1,0:T(8,128)(2,1)} %collective-permute-done.12.far_ref), channel_id=1, source_target_pairs={{0,2},{1,3},{2,0},{3,1},{4,6},{5,7},{6,4},{7,5},{8,10},{9,11},{10,... | collective-permute-start | bytes 1179656 | tf_op jit(solution)/shard_map/ppermute | solution.py:272
  87.1 1.4 %copy-start.1 = (bf16[512,1536]{1,0:T(8,128)(2,1)S(1)}, bf16[512,1536]{1,0:T(8,128)(2,1)}, u32[]{:S(2)}) copy-start(bf16[512,1536]{1,0:T(8,128)(2,1)} %q_ref.7) | copy-start | bytes 4718596
  88.5 4.9 %copy-start.2 = (bf16[512,1536]{1,0:T(8,128)(2,1)S(1)}, bf16[512,1536]{1,0:T(8,128)(2,1)}, u32[]{:S(2)}) copy-start(bf16[512,1536]{1,0:T(8,128)(2,1)} %q_ref.7) | copy-start | bytes 4718596
  88.5 4.9 %copy-start.5 = (bf16[2,256,384]{2,1,0:T(8,128)(2,1)S(1)}, bf16[2,256,384]{2,1,0:T(8,128)(2,1)}, u32[]{:S(2)}) copy-start(bf16[2,256,384]{2,1,0:T(8,128)(2,1)} %copy-done.4) | copy-start | bytes 1179652
  98.7 6.9 %collective-permute-start.21 = (bf16[2,256,384]{2,1,0:T(8,128)(2,1)}, bf16[2,256,384]{2,1,0:T(8,128)(2,1)}, u32[]{:S(2)}, u32[]{:S(2)}) collective-permute-start(bf16[2,256,384]{2,1,0:T(8,128)(2,1)} %collective-permute-done.13.near_ref), channel_id=1, source_target_pairs={{0,1},{1,0},{2,3},{3,2},{4,5},{5,4},{6,7},{7,6},{8,9},{9,8},{10,11... | collective-permute-start | bytes 1179656 | tf_op jit(solution)/shard_map/ppermute | solution.py:272
  98.7 6.9 %collective-permute-start.22 = (bf16[2,256,384]{2,1,0:T(8,128)(2,1)}, bf16[2,256,384]{2,1,0:T(8,128)(2,1)}, u32[]{:S(2)}, u32[]{:S(2)}) collective-permute-start(bf16[2,256,384]{2,1,0:T(8,128)(2,1)} %collective-permute-done.18.far_ref), channel_id=1, source_target_pairs={{0,1},{1,0},{2,3},{3,2},{4,5},{5,4},{6,7},{7,6},{8,9},{9,8},{10,11... | collective-permute-start | bytes 1179656 | tf_op jit(solution)/shard_map/ppermute | solution.py:272
  99.4 1.4 %copy-start.3 = (bf16[512,1536]{1,0:T(8,128)(2,1)S(1)}, bf16[512,1536]{1,0:T(8,128)(2,1)}, u32[]{:S(2)}) copy-start(bf16[512,1536]{1,0:T(8,128)(2,1)} %q_ref.7) | copy-start | bytes 4718596

commit v15 on v14

--- a/solution.py
+++ b/solution.py
@@ -35,7 +35,7 @@
 
 
 def pack_kernel(kv_ref, out_ref, *refs):
-    below_refs, across_refs, diagonal_refs, (held, came, left) = refs[0:2], refs[2:4], refs[4:6], refs[6:]
+    below_refs, (across_ref, diagonal_ref, held, came, left) = refs[0:2], refs[2:]
     groups, _, rows, part = out_ref.shape
     few, wide, pieces = rows // 4, groups * part // 2, [(s, i) for s in range(2) for i in range(4)]
     arrive = {}
@@ -48,7 +48,7 @@
         arrive[s, i].wait()
         band, place = pl.ds(i * few, few), pl.ds(i % 2 * few, few)
         right = held.at[s, band, pl.ds(wide, wide)]
-        moves = [(right, (across_refs if i < 2 else diagonal_refs)[s].at[place])]
+        moves = [(right, (across_ref if i < 2 else diagonal_ref).at[s, place])]
         if i >= 2:
             moves.append((held.at[s, band, pl.ds(0, wide)], below_refs[s].at[place]))
         moves += [(held.at[s, band, pl.ds(g * part, part)], out_ref.at[g, s, band]) for g in range(groups)]
@@ -62,12 +62,15 @@
 def pack(kv, groups):
     _, rows, width = kv.shape
     anywhere = pl.BlockSpec(memory_space=pl.ANY)
-    half = jax.ShapeDtypeStruct((rows // 2, width // 2), kv.dtype)
+    array = lambda *shape: jax.ShapeDtypeStruct(shape, kv.dtype)
+    tall, wide = rows // 2, width // 2
     out, *quarters = pl.pallas_call(
         pack_kernel,
         in_specs=[anywhere],
-        out_specs=[anywhere] * 7,
-        out_shape=[jax.ShapeDtypeStruct((groups, 2, rows, width // groups), kv.dtype)] + [half] * 6,
+        out_specs=[anywhere] * 5,
+        out_shape=[array(groups, 2, rows, width // groups)]
+        + [array(tall, wide)] * 2
+        + [array(2, tall, wide)] * 2,
         scratch_shapes=[
             pltpu.VMEM(kv.shape, kv.dtype),
             pltpu.SemaphoreType.DMA((2, 4)),
@@ -76,7 +79,7 @@
         cost_estimate=pl.CostEstimate(flops=0, bytes_accessed=6 * kv.size, transcendentals=0),
         name="pack_heads",
     )(kv)
-    return out, quarters[:2], quarters[2:4], quarters[4:]
+    return out, quarters[:2], *quarters[2:]
 
 
 def pipelined(tasks, score, finish):
@@ -286,15 +289,11 @@
     first = (lax.axis_index("hst") == 0) & (lax.axis_index("grp") == 0)
     send = lambda x, to: lax.ppermute(x, BOTH, [(0, to), (to, 0)])
     _, rows, width = kv.shape
-    slabs, come = [], None
+    slabs, come = [], send(below[0], groups)
+    right = send(diagonal, groups + cores) + send(across, cores)
     for s in range(2):
-        down = send(below[s], groups)
-        if s:
-            down = after(down, slabs[0])
-        else:
-            come = down
-        got = send(diagonal[s], groups + cores) + send(across[s], cores) + down
-        slabs.append(jnp.where(first, kv[s, : rows // 2, : width // 2], got))
+        down = after(send(below[s], groups), slabs[0]) if s else come
+        slabs.append(jnp.where(first, kv[s, : rows // 2, : width // 2], right[s] + down))
     return slabs, come
 
 

time: 117 us -> 127 us (1.085)
  waiting for transfers between devices: 17 us -> 27.9 us
    ppermute x6 -> x4, waiting for transfers between devices: 0.81 us -> 15.3 us  [scatter_anchor(): send = lambda x, to: lax.ppermute(x, BOTH, [(0, to), (to, 0)])]
    ppermute x6 -> x4, starting transfers between devices: 15.6 us -> 10.6 us  [scatter_anchor(): send = lambda x, to: lax.ppermute(x, BOTH, [(0, to), (to, 0)])]
    ppermute x11, starting transfers between devices: 6.74 us -> 10.9 us  [swap(): lax.ppermute(x, axis, [(i, i ^ k) for i in range(lax.axis_size(axis))])]
    all_to_all x1, waiting for transfers between devices: 3.7 us -> 0.01 us  [per_device(): lax.all_to_all(after(packed, down), 'grp', split_axis=0, concat_axis=0, t...]
    ppermute x4, starting transfers between devices: 6.79 us -> 8.52 us  [spread_anchor(): piece = piece + lax.ppermute(piece, 'hst', pairs)]
    add x0 -> x1, other arithmetic: none -> 1.55 us  [scatter_anchor(): right = send(diagonal, groups + cores) + send(across, cores)]
    select_n x2, other arithmetic: 2.53 us -> 1.12 us  [scatter_anchor(): jnp.where(first, kv[s, :rows // 2, :width // 2], right[s] + down)]
    unnamed x22 -> x18, local copies, waits for them, and re-layouts: 3.6 us -> 3.58 us
  transfers between devices with their start and end apart: 25 -> 23, of which waited for: 9 -> 9; matrix products, arithmetic and copies ran while one was open for 7% -> 6% of each run, Pallas kernels for 29% -> 27%
where the time goes in v15:
time: 127 us; the launch traced here: 126 us
  starting transfers between devices  42.7 us (34%)
  Pallas kernels  40.6 us (32%)
  waiting for transfers between devices  27.9 us (22%)
  other arithmetic  9.82 us (8%)
  local copies, waits for them, and re-layouts  4.37 us (3%)
    pallas_call x4, Pallas kernels, context_attend(): pl.pallas_call(context_kernel, grid_spec=pltpu.PrefetchScalarGridSpec(num...  19.3 us
    ppermute x4, waiting for transfers between devices, scatter_anchor(): send = lambda x, to: lax.ppermute(x, BOTH, [(0, to), (to, 0)])  15.3 us
    pallas_call x2, Pallas kernels, suffix_attend(): pl.pallas_call(suffix_kernel, grid_spec=pltpu.PrefetchScalarGridSpec(num_...  14.7 us
    ppermute x11, starting transfers between devices, swap(): lax.ppermute(x, axis, [(i, i ^ k) for i in range(lax.axis_size(axis))])  10.9 us
    ppermute x4, starting transfers between devices, scatter_anchor(): send = lambda x, to: lax.ppermute(x, BOTH, [(0, to), (to, 0)])  10.6 us
    ppermute x4, starting transfers between devices, spread_anchor(): piece = piece + lax.ppermute(piece, 'hst', pairs)  8.52 us
    ppermute x4, waiting for transfers between devices, spread_anchor(): piece = piece + lax.ppermute(piece, 'hst', pairs)  7.45 us
    ppermute x11, waiting for transfers between devices, swap(): lax.ppermute(x, axis, [(i, i ^ k) for i in range(lax.axis_size(axis))])  5.13 us
  transfers between devices with their start and end apart: 23, of which 9 were waited for; matrix products, arithmetic and copies ran while one was open for 6% of the time, Pallas kernels for 27%

profile of v15, /device:TPU:0, one launch (start us, length us, event | category | flops | bytes accessed | tf_op | source)
XLA Modules:
  0.0 126.4 jit_solution(7562150357414941368)
XLA Ops:
  0.6 3.9 %pack_heads.1 = (bf16[4,2,512,384]{3,2,1,0:T(8,128)(2,1)}, bf16[256,768]{1,0:T(8,128)(2,1)}, bf16[256,768]{1,0:T(8,128)(2,1)}, bf16[2,256,768]{2,1,0:T(8,128)(2,1)}, bf16[2,256,768]{2,1,0:T(8,128)(2,1)}) custom-call(bf16[2,512,1536]{2,1,0:T(8,128)(2,1)} %kv_ref.9), custom_call_target="tpu_custom_call" | custom-call | bytes 9437184 | tf_op jit(solution)/shard_map/pack_heads/pallas_call | solution.py:67
  4.5 4.9 %collective-permute-start.2 = (bf16[256,768]{1,0:T(8,128)(2,1)}, bf16[256,768]{1,0:T(8,128)(2,1)S(1)}, u32[]{:S(2)}, u32[]{:S(2)}) collective-permute-start(bf16[256,768]{1,0:T(8,128)(2,1)} %get-tuple-element.23), channel_id=1, source_target_pairs={{0,4},{4,0}} | collective-permute-start | bytes 1179656 | tf_op jit(solution)/shard_map/ppermute | solution.py:290
  9.4 1.9 %collective-permute-start = (bf16[2,256,768]{2,1,0:T(8,128)(2,1)}, bf16[2,256,768]{2,1,0:T(8,128)(2,1)}, u32[]{:S(2)}, u32[]{:S(2)}) collective-permute-start(bf16[2,256,768]{2,1,0:T(8,128)(2,1)} %get-tuple-element.21), channel_id=1, source_target_pairs={{0,6},{6,0}} | collective-permute-start | bytes 2359304 | tf_op jit(solution)/shard_map/ppermute | solution.py:290
  11.3 1.9 %collective-permute-start.1 = (bf16[2,256,768]{2,1,0:T(8,128)(2,1)}, bf16[2,256,768]{2,1,0:T(8,128)(2,1)}, u32[]{:S(2)}, u32[]{:S(2)}) collective-permute-start(bf16[2,256,768]{2,1,0:T(8,128)(2,1)} %get-tuple-element.22), channel_id=1, source_target_pairs={{0,2},{2,0}} | collective-permute-start | bytes 2359304 | tf_op jit(solution)/shard_map/ppermute | solution.py:290
  13.2 1.9 %collective-permute-start.6 = (bf16[256,768]{1,0:T(8,128)(2,1)}, bf16[256,768]{1,0:T(8,128)(2,1)}, u32[]{:S(2)}, u32[]{:S(2)}) collective-permute-start(bf16[256,768]{1,0:T(8,128)(2,1)} %get-tuple-element.24), channel_id=1, source_target_pairs={{0,4},{4,0}} | collective-permute-start | bytes 1179656 | tf_op jit(solution)/shard_map/ppermute | solution.py:290
  15.2 0.2 collective-permute-done.2
  15.3 4.9 %all-to-all-start = ((bf16[4,2,512,384]{3,2,1,0:T(8,128)(2,1)}), bf16[4,2,512,384]{3,2,1,0:T(8,128)(2,1)}, u32[]{:S(2)}, u32[]{:S(2)}) async-start(bf16[4,2,512,384]{3,2,1,0:T(8,128)(2,1)} %get-tuple-element.27), calls=%async_computation | async-start | bytes 6291456 | tf_op jit(solution)/shard_map/all_to_all | solution.py:323
  20.3 1.5 %broadcast_compare_fusion = pred[16384]{0:T(1024)(128)(4,1)} fusion(s32[16384]{0:T(1024)} %param.8), kind=kLoop, calls=%fused_computation.15 | loop fusion | flops 16384 | bytes 81920 | tf_op jit(solution)/shard_map/ge | solution.py:327
  21.7 0.8 ge.11
  22.5 2.1 %collective-permute-done = bf16[2,256,768]{2,1,0:T(8,128)(2,1)} collective-permute-done((bf16[2,256,768]{2,1,0:T(8,128)(2,1)}, bf16[2,256,768]{2,1,0:T(8,128)(2,1)}, u32[]{:S(2)}, u32[]{:S(2)}) %collective-permute-start) | collective-permute-done | bytes 786464 | tf_op jit(solution)/shard_map/ppermute | solution.py:290
  24.6 13.0 %collective-permute-done.1 = bf16[2,256,768]{2,1,0:T(8,128)(2,1)} collective-permute-done((bf16[2,256,768]{2,1,0:T(8,128)(2,1)}, bf16[2,256,768]{2,1,0:T(8,128)(2,1)}, u32[]{:S(2)}, u32[]{:S(2)}) %collective-permute-start.1) | collective-permute-done | bytes 786464 | tf_op jit(solution)/shard_map/ppermute | solution.py:290
  37.6 1.6 %add.42 = bf16[2,256,768]{2,1,0:T(8,128)(2,1)S(1)} add(bf16[2,256,768]{2,1,0:T(8,128)(2,1)} %collective-permute-done, bf16[2,256,768]{2,1,0:T(8,128)(2,1)} %collective-permute-done.1) | non-fusion elementwise | flops 393216 | bytes 2359296 | tf_op jit(solution)/shard_map/add | solution.py:293
  39.3 1.4 %collective-permute-start.3 = (bf16[256,384]{1,0:T(8,128)(2,1)S(1)}, bf16[256,384]{1,0:T(8,128)(2,1)S(1)}, u32[]{:S(2)}, u32[]{:S(2)}) collective-permute-start(bf16[256,384]{1,0:T(8,128)(2,1)S(1)} %slice.34), channel_id=1, source_target_pairs={{0,1},{2,3},{4,5},{6,7},{8,9},{10,11},{12,13},{14,15},{16,17},{18,... | collective-permute-start | bytes 589832 | tf_op jit(solution)/shard_map/ppermute | solution.py:306
  40.7 1.1 fusion.1
  41.8 1.3 %collective-permute-start.7 = (bf16[256,384]{1,0:T(8,128)(2,1)S(1)}, bf16[256,384]{1,0:T(8,128)(2,1)S(1)}, u32[]{:S(2)}, u32[]{:S(2)}) collective-permute-start(bf16[256,384]{1,0:T(8,128)(2,1)S(1)} %slice.37), channel_id=1, source_target_pairs={{0,1},{2,3},{4,5},{6,7},{8,9},{10,11},{12,13},{14,15},{16,17},{18,... | collective-permute-start | bytes 589832 | tf_op jit(solution)/shard_map/ppermute | solution.py:306
  43.2 1.3 %collective-permute-start.4 = (bf16[256,384]{1,0:T(8,128)(2,1)S(1)}, bf16[256,384]{1,0:T(8,128)(2,1)S(1)}, u32[]{:S(2)}, u32[]{:S(2)}) collective-permute-start(bf16[256,384]{1,0:T(8,128)(2,1)S(1)} %slice_add_fusion.1), channel_id=1, source_target_pairs={{0,16},{4,20},{1,17},{5,21},{2,18},{6,22},{3,19},{7,23}} | collective-permute-start | bytes 589832 | tf_op jit(solution)/shard_map/ppermute | solution.py:311
  44.7 4.3 %collective-permute-start.14 = (bf16[128,384]{1,0:T(8,128)(2,1)S(1)}, bf16[128,384]{1,0:T(8,128)(2,1)S(1)}, u32[]{:S(2)}, u32[]{:S(2)}) collective-permute-start(bf16[128,384]{1,0:T(8,128)(2,1)S(1)} %copy-done.8), channel_id=1, source_target_pairs={{0,24},{4,28},{8,16},{12,20},{16,8},{20,12},{24,0},{28,4},{1,25},{... | collective-permute-start | bytes 294920 | tf_op jit(solution)/shard_map/ppermute | solution.py:275
  49.0 1.3 %collective-permute-start.8 = (bf16[256,384]{1,0:T(8,128)(2,1)S(1)}, bf16[256,384]{1,0:T(8,128)(2,1)S(1)}, u32[]{:S(2)}, u32[]{:S(2)}) collective-permute-start(bf16[256,384]{1,0:T(8,128)(2,1)S(1)} %slice_add_fusion), channel_id=1, source_target_pairs={{0,16},{4,20},{1,17},{5,21},{2,18},{6,22},{3,19},{7,23}} | collective-permute-start | bytes 589832 | tf_op jit(solution)/shard_map/ppermute | solution.py:311
  50.4 1.3 %collective-permute-start.5 = (bf16[256,384]{1,0:T(8,128)(2,1)S(1)}, bf16[256,384]{1,0:T(8,128)(2,1)S(1)}, u32[]{:S(2)}, u32[]{:S(2)}) collective-permute-start(bf16[256,384]{1,0:T(8,128)(2,1)S(1)} %add.45), channel_id=1, source_target_pairs={{0,8},{4,12},{16,24},{20,28},{1,9},{5,13},{17,25},{21,29},{2,10},{... | collective-permute-start | bytes 589832 | tf_op jit(solution)/shard_map/ppermute | solution.py:311
  51.7 0.1 fusion.5.bias_ref
  51.8 0.2 collective-permute-done.12
  51.9 3.6 %collective-permute-done.13 = bf16[128,384]{1,0:T(8,128)(2,1)S(1)} collective-permute-done((bf16[128,384]{1,0:T(8,128)(2,1)S(1)}, bf16[128,384]{1,0:T(8,128)(2,1)S(1)}, u32[]{:S(2)}, u32[]{:S(2)}) %collective-permute-start.13) | collective-permute-done | bytes 98336 | tf_op jit(solution)/shard_map/ppermute | solution.py:275
  55.5 0.6 collective-permute-done.14
  56.2 0.8 pad_maximum_fusion.1.near_ref
  57.0 3.4 %collective-permute-done.8 = bf16[256,384]{1,0:T(8,128)(2,1)S(1)} collective-permute-done((bf16[256,384]{1,0:T(8,128)(2,1)S(1)}, bf16[256,384]{1,0:T(8,128)(2,1)S(1)}, u32[]{:S(2)}, u32[]{:S(2)}) %collective-permute-start.8) | collective-permute-done | bytes 196640 | tf_op jit(solution)/shard_map/ppermute | solution.py:311
  60.4 4.6 %collective-permute-start.9 = (bf16[256,384]{1,0:T(8,128)(2,1)S(1)}, bf16[256,384]{1,0:T(8,128)(2,1)S(1)}, u32[]{:S(2)}, u32[]{:S(2)}) collective-permute-start(bf16[256,384]{1,0:T(8,128)(2,1)S(1)} %add.49), channel_id=1, source_target_pairs={{0,8},{4,12},{16,24},{20,28},{1,9},{5,13},{17,25},{21,29},{2,10},{... | collective-permute-start | bytes 589832 | tf_op jit(solution)/shard_map/ppermute | solution.py:311
  65.1 4.0 %collective-permute-done.9 = bf16[256,384]{1,0:T(8,128)(2,1)S(1)} collective-permute-done((bf16[256,384]{1,0:T(8,128)(2,1)S(1)}, bf16[256,384]{1,0:T(8,128)(2,1)S(1)}, u32[]{:S(2)}, u32[]{:S(2)}) %collective-permute-start.9) | collective-permute-done | bytes 196640 | tf_op jit(solution)/shard_map/ppermute | solution.py:311
  69.2 0.8 pad_maximum_fusion.near_ref
  70.0 1.7 %collective-permute-start.10 = (bf16[2,256,384]{2,1,0:T(8,128)(2,1)}, bf16[2,256,384]{2,1,0:T(8,128)(2,1)}, u32[]{:S(2)}, u32[]{:S(2)}) collective-permute-start(bf16[2,256,384]{2,1,0:T(8,128)(2,1)} %pad_maximum_fusion.near_ref), channel_id=1, source_target_pairs={{0,4},{4,0},{8,12},{12,8},{16,20},{20,16},{24,28},{28,24},{1,5},{5... | collective-permute-start | bytes 1179656 | tf_op jit(solution)/shard_map/ppermute | solution.py:275
  71.7 2.5 %collective-permute-start.11 = (bf16[2,256,384]{2,1,0:T(8,128)(2,1)}, bf16[2,256,384]{2,1,0:T(8,128)(2,1)}, u32[]{:S(2)}, u32[]{:S(2)}) collective-permute-start(bf16[2,256,384]{2,1,0:T(8,128)(2,1)} %pad_maximum_fusion.near_ref), channel_id=1, source_target_pairs={{0,2},{1,3},{2,0},{3,1},{4,6},{5,7},{6,4},{7,5},{8,10},{9,11},{10,... | collective-permute-start | bytes 1179656 | tf_op jit(solution)/shard_map/ppermute | solution.py:275
  74.2 9.3 %suffix_attend.2.rest_0_ = f32[8,136,384]{2,1,0:T(8,128)S(1)} custom-call(s32[1]{0:T(128)} %bitcast.9.at_ref, bf16[4,128,384]{2,1,0:T(8,128)(2,1)} %pad_maximum_fusion.1.near_ref, bf16[4,128,384]{2,1,0:T(8,128)(2,1)} %collective-permute-done.15.far_ref, bf16[4,2,512,384]{3,2,1,0:T(8,128)(2,1)} %all-to-all-done.kv_ref, bf16[2,128,384]{2,1,0:T(8,128)(2,1)S(1)} %copy-done.7, ...), custom_call_target="tpu_custom_call" | custom-call | flops 4563402752 | bytes 5242880 | tf_op jit(solution)/shard_map/suffix_attend/pallas_call | solution.py:147
  83.5 0.7 collective-permute-done.11.near_ref
  84.3 5.3 %suffix_attend.3 = f32[8,136,384]{2,1,0:T(8,128)S(1)} custom-call(s32[1]{0:T(128)} %bitcast.9.at_ref, bf16[4,128,384]{2,1,0:T(8,128)(2,1)} %pad_maximum_fusion.1.near_ref, bf16[4,128,384]{2,1,0:T(8,128)(2,1)} %collective-permute-done.15.far_ref, bf16[4,2,512,384]{3,2,1,0:T(8,128)(2,1)} %all-to-all-done.kv_ref, ...), custom_call_target="tpu_custom_call", output_to_operand_aliasing={{}: (6, {})} | custom-call | flops 2281701376 | bytes 2621440 | tf_op jit(solution)/shard_map/suffix_attend/pallas_call | solution.py:147
  89.7 0.7 copy-done.4
  90.4 1.0 convert_element_type.6
  91.4 5.0 %all-to-all-start.1 = ((f16[8,136,384]{2,1,0:T(8,128)(2,1)}), f16[8,136,384]{2,1,0:T(8,128)(2,1)}, u32[]{:S(2)}, u32[]{:S(2)}) async-start(f16[8,136,384]{2,1,0:T(8,128)(2,1)} %convert_element_type.6), calls=%async_computation.1 | async-start | bytes 1671168 | tf_op jit(solution)/shard_map/all_to_all | solution.py:340
  96.4 1.8 %collective-permute-start.16 = (bf16[2,256,384]{2,1,0:T(8,128)(2,1)}, bf16[2,256,384]{2,1,0:T(8,128)(2,1)}, u32[]{:S(2)}, u32[]{:S(2)}) collective-permute-start(bf16[2,256,384]{2,1,0:T(8,128)(2,1)} %collective-permute-done.10.far_ref), channel_id=1, source_target_pairs={{0,2},{1,3},{2,0},{3,1},{4,6},{5,7},{6,4},{7,5},{8,10},{9,11},{10,... | collective-permute-start | bytes 1179656 | tf_op jit(solution)/shard_map/ppermute | solution.py:275
  98.2 0.1 add_add_fusion.2.at_ref
  98.3 1.4 %copy-done.1 = bf16[512,1536]{1,0:T(8,128)(2,1)S(1)} copy-done((bf16[512,1536]{1,0:T(8,128)(2,1)S(1)}, bf16[512,1536]{1,0:T(8,128)(2,1)}, u32[]{:S(2)}) %copy-start.1) | copy-done | bytes 1572888
  99.7 4.9 %context_attend.4.rest_0_ = bf16[512,1536]{1,0:T(8,128)(2,1)} custom-call(s32[3]{0:T(128)S(1)} %add_add_fusion.2.at_ref, s32[32]{0:T(128)S(1)} %copy-done.6, bf16[512,1536]{1,0:T(8,128)(2,1)S(1)} %copy-done.1, bf16[2,512,1536]{2,1,0:T(8,128)(2,1)S(1)} %copy-done, f32[32,512]{1,0:T(8,128)S(1)} %fusion.5.bias_ref, ...), custom_call_target="tpu_custom_call" | custom-call | flops 805306368 | bytes 2359296 | tf_op jit(solution)/shard_map/context_attend/pallas_call | solution.py:246
  104.6 4.8 %context_attend.5.rest_0_ = bf16[512,1536]{1,0:T(8,128)(2,1)} custom-call(s32[3]{0:T(128)S(1)} %add_add_fusion.1.at_ref, s32[32]{0:T(128)S(1)} %copy-done.6, bf16[512,1536]{1,0:T(8,128)(2,1)S(1)} %copy-done.2, bf16[2,512,1536]{2,1,0:T(8,128)(2,1)S(1)} %copy-done, f32[32,512]{1,0:T(8,128)S(1)} %fusion.5.bias_ref, ...), custom_call_target="tpu_custom_call", output_to_operand_aliasing={{}: (7, {})} | custom-call | flops 805306368 | bytes 2359296 | tf_op jit(solution)/shard_map/context_attend/pallas_call | solution.py:246
  109.4 0.5 collective-permute-start.20
  110.0 0.1 add_add_fusion.at_ref
  110.1 1.4 %copy-done.3 = bf16[512,1536]{1,0:T(8,128)(2,1)S(1)} copy-done((bf16[512,1536]{1,0:T(8,128)(2,1)S(1)}, bf16[512,1536]{1,0:T(8,128)(2,1)}, u32[]{:S(2)}) %copy-start.3) | copy-done | bytes 1572888
  111.5 4.8 %context_attend.6.rest_0_ = bf16[512,1536]{1,0:T(8,128)(2,1)} custom-call(s32[3]{0:T(128)S(1)} %add_add_fusion.3.at_ref, s32[32]{0:T(128)S(1)} %copy-done.6, bf16[512,1536]{1,0:T(8,128)(2,1)S(1)} %copy-done.3, bf16[2,512,1536]{2,1,0:T(8,128)(2,1)S(1)} %copy-done, f32[32,512]{1,0:T(8,128)S(1)} %fusion.5.bias_ref, ...), custom_call_target="tpu_custom_call", output_to_operand_aliasing={{}: (7, {})} | custom-call | flops 805306368 | bytes 2359296 | tf_op jit(solution)/shard_map/context_attend/pallas_call | solution.py:246
  116.3 4.8 %context_attend.7 = bf16[512,1536]{1,0:T(8,128)(2,1)} custom-call(s32[3]{0:T(128)S(1)} %add_add_fusion.at_ref, s32[32]{0:T(128)S(1)} %copy-done.6, bf16[512,1536]{1,0:T(8,128)(2,1)S(1)} %copy-done.3, bf16[2,512,1536]{2,1,0:T(8,128)(2,1)S(1)} %copy-done, f32[32,512]{1,0:T(8,128)S(1)} %fusion.5.bias_ref, ...), custom_call_target="tpu_custom_call", output_to_operand_aliasing={{}: (7, {})} | custom-call | flops 805306368 | bytes 2359296 | tf_op jit(solution)/shard_map/context_attend/pallas_call | solution.py:246
  121.2 2.5 %convert_element_type.7.in_ref = f32[8,136,384]{2,1,0:T(8,128)} convert(f16[8,136,384]{2,1,0:T(8,128)(2,1)} %all-to-all-done.1) | non-fusion elementwise | flops 417792 | bytes 2506752 | tf_op jit(solution)/shard_map/convert_element_type | solution.py:356
  123.6 2.7 %combine_groups.1 = bf16[128,384]{1,0:T(8,128)(2,1)} custom-call(f32[8,136,384]{2,1,0:T(8,128)} %convert_element_type.7.in_ref), custom_call_target="tpu_custom_call" | custom-call | flops 835584 | bytes 1671168 | tf_op jit(solution)/shard_map/combine_groups/pallas_call | solution.py:191
  (46 shorter events, 0.7 us)
Async XLA Ops:
  4.5 10.8 %collective-permute-start.2 = (bf16[256,768]{1,0:T(8,128)(2,1)}, bf16[256,768]{1,0:T(8,128)(2,1)S(1)}, u32[]{:S(2)}, u32[]{:S(2)}) collective-permute-start(bf16[256,768]{1,0:T(8,128)(2,1)} %get-tuple-element.23), channel_id=1, source_target_pairs={{0,4},{4,0}} | collective-permute-start | bytes 1179656 | tf_op jit(solution)/shard_map/ppermute | solution.py:290
  9.4 15.2 %collective-permute-start = (bf16[2,256,768]{2,1,0:T(8,128)(2,1)}, bf16[2,256,768]{2,1,0:T(8,128)(2,1)}, u32[]{:S(2)}, u32[]{:S(2)}) collective-permute-start(bf16[2,256,768]{2,1,0:T(8,128)(2,1)} %get-tuple-element.21), channel_id=1, source_target_pairs={{0,6},{6,0}} | collective-permute-start | bytes 2359304 | tf_op jit(solution)/shard_map/ppermute | solution.py:290
  11.3 26.3 %collective-permute-start.1 = (bf16[2,256,768]{2,1,0:T(8,128)(2,1)}, bf16[2,256,768]{2,1,0:T(8,128)(2,1)}, u32[]{:S(2)}, u32[]{:S(2)}) collective-permute-start(bf16[2,256,768]{2,1,0:T(8,128)(2,1)} %get-tuple-element.22), channel_id=1, source_target_pairs={{0,2},{2,0}} | collective-permute-start | bytes 2359304 | tf_op jit(solution)/shard_map/ppermute | solution.py:290
  13.2 26.0 %collective-permute-start.6 = (bf16[256,768]{1,0:T(8,128)(2,1)}, bf16[256,768]{1,0:T(8,128)(2,1)}, u32[]{:S(2)}, u32[]{:S(2)}) collective-permute-start(bf16[256,768]{1,0:T(8,128)(2,1)} %get-tuple-element.24), channel_id=1, source_target_pairs={{0,4},{4,0}} | collective-permute-start | bytes 1179656 | tf_op jit(solution)/shard_map/ppermute | solution.py:290
  15.3 23.8 %copy-start = (bf16[2,512,1536]{2,1,0:T(8,128)(2,1)S(1)}, bf16[2,512,1536]{2,1,0:T(8,128)(2,1)}, u32[]{:S(2)}) copy-start(bf16[2,512,1536]{2,1,0:T(8,128)(2,1)} %kv_ref.9) | copy-start | bytes 9437188
  15.3 56.4 %all-to-all-start = ((bf16[4,2,512,384]{3,2,1,0:T(8,128)(2,1)}), bf16[4,2,512,384]{3,2,1,0:T(8,128)(2,1)}, u32[]{:S(2)}, u32[]{:S(2)}) async-start(bf16[4,2,512,384]{3,2,1,0:T(8,128)(2,1)} %get-tuple-element.27), calls=%async_computation | async-start | bytes 6291456 | tf_op jit(solution)/shard_map/all_to_all | solution.py:323
  39.3 5.3 %copy-start.8 = (bf16[128,384]{1,0:T(8,128)(2,1)S(1)}, bf16[128,384]{1,0:T(8,128)(2,1)}, u32[]{:S(2)}) copy-start(bf16[128,384]{1,0:T(8,128)(2,1)} %param.10) | copy-start | bytes 294916
  39.3 12.4 %copy-start.6 = (s32[32]{0:T(128)S(1)}, s32[32]{0:T(128)}, u32[]{:S(2)}) copy-start(s32[32]{0:T(128)} %len_ref.7) | copy-start | bytes 388
  39.3 3.8 %collective-permute-start.3 = (bf16[256,384]{1,0:T(8,128)(2,1)S(1)}, bf16[256,384]{1,0:T(8,128)(2,1)S(1)}, u32[]{:S(2)}, u32[]{:S(2)}) collective-permute-start(bf16[256,384]{1,0:T(8,128)(2,1)S(1)} %slice.34), channel_id=1, source_target_pairs={{0,1},{2,3},{4,5},{6,7},{8,9},{10,11},{12,13},{14,15},{16,17},{18,... | collective-permute-start | bytes 589832 | tf_op jit(solution)/shard_map/ppermute | solution.py:306
  41.8 2.7 %collective-permute-start.7 = (bf16[256,384]{1,0:T(8,128)(2,1)S(1)}, bf16[256,384]{1,0:T(8,128)(2,1)S(1)}, u32[]{:S(2)}, u32[]{:S(2)}) collective-permute-start(bf16[256,384]{1,0:T(8,128)(2,1)S(1)} %slice.37), channel_id=1, source_target_pairs={{0,1},{2,3},{4,5},{6,7},{8,9},{10,11},{12,13},{14,15},{16,17},{18,... | collective-permute-start | bytes 589832 | tf_op jit(solution)/shard_map/ppermute | solution.py:306
  43.2 7.1 %collective-permute-start.4 = (bf16[256,384]{1,0:T(8,128)(2,1)S(1)}, bf16[256,384]{1,0:T(8,128)(2,1)S(1)}, u32[]{:S(2)}, u32[]{:S(2)}) collective-permute-start(bf16[256,384]{1,0:T(8,128)(2,1)S(1)} %slice_add_fusion.1), channel_id=1, source_target_pairs={{0,16},{4,20},{1,17},{5,21},{2,18},{6,22},{3,19},{7,23}} | collective-permute-start | bytes 589832 | tf_op jit(solution)/shard_map/ppermute | solution.py:311
  44.6 7.4 %collective-permute-start.12 = (bf16[128,384]{1,0:T(8,128)(2,1)S(1)}, bf16[128,384]{1,0:T(8,128)(2,1)S(1)}, u32[]{:S(2)}, u32[]{:S(2)}) collective-permute-start(bf16[128,384]{1,0:T(8,128)(2,1)S(1)} %copy-done.8), channel_id=1, source_target_pairs={{0,8},{4,12},{8,0},{12,4},{16,24},{20,28},{24,16},{28,20},{1,9},{5... | collective-permute-start | bytes 294920 | tf_op jit(solution)/shard_map/ppermute | solution.py:275
  44.6 10.9 %collective-permute-start.13 = (bf16[128,384]{1,0:T(8,128)(2,1)S(1)}, bf16[128,384]{1,0:T(8,128)(2,1)S(1)}, u32[]{:S(2)}, u32[]{:S(2)}) collective-permute-start(bf16[128,384]{1,0:T(8,128)(2,1)S(1)} %copy-done.8), channel_id=1, source_target_pairs={{0,16},{4,20},{8,24},{12,28},{16,0},{20,4},{24,8},{28,12},{1,17},{... | collective-permute-start | bytes 294920 | tf_op jit(solution)/shard_map/ppermute | solution.py:275
  44.7 11.4 %collective-permute-start.14 = (bf16[128,384]{1,0:T(8,128)(2,1)S(1)}, bf16[128,384]{1,0:T(8,128)(2,1)S(1)}, u32[]{:S(2)}, u32[]{:S(2)}) collective-permute-start(bf16[128,384]{1,0:T(8,128)(2,1)S(1)} %copy-done.8), channel_id=1, source_target_pairs={{0,24},{4,28},{8,16},{12,20},{16,8},{20,12},{24,0},{28,4},{1,25},{... | collective-permute-start | bytes 294920 | tf_op jit(solution)/shard_map/ppermute | solution.py:275
  49.0 11.4 %collective-permute-start.8 = (bf16[256,384]{1,0:T(8,128)(2,1)S(1)}, bf16[256,384]{1,0:T(8,128)(2,1)S(1)}, u32[]{:S(2)}, u32[]{:S(2)}) collective-permute-start(bf16[256,384]{1,0:T(8,128)(2,1)S(1)} %slice_add_fusion), channel_id=1, source_target_pairs={{0,16},{4,20},{1,17},{5,21},{2,18},{6,22},{3,19},{7,23}} | collective-permute-start | bytes 589832 | tf_op jit(solution)/shard_map/ppermute | solution.py:311
  50.4 14.7 %collective-permute-start.5 = (bf16[256,384]{1,0:T(8,128)(2,1)S(1)}, bf16[256,384]{1,0:T(8,128)(2,1)S(1)}, u32[]{:S(2)}, u32[]{:S(2)}) collective-permute-start(bf16[256,384]{1,0:T(8,128)(2,1)S(1)} %add.45), channel_id=1, source_target_pairs={{0,8},{4,12},{16,24},{20,28},{1,9},{5,13},{17,25},{21,29},{2,10},{... | collective-permute-start | bytes 589832 | tf_op jit(solution)/shard_map/ppermute | solution.py:311
  56.2 18.0 %copy-start.7 = (bf16[2,128,384]{2,1,0:T(8,128)(2,1)S(1)}, bf16[2,128,384]{2,1,0:T(8,128)(2,1)}, u32[]{:S(2)}) copy-start(bf16[2,128,384]{2,1,0:T(8,128)(2,1)} %sk_ref.3) | copy-start | bytes 589828
  57.0 17.2 %collective-permute-start.15 = (bf16[4,128,384]{2,1,0:T(8,128)(2,1)}, bf16[4,128,384]{2,1,0:T(8,128)(2,1)}, u32[]{:S(2)}, u32[]{:S(2)}) collective-permute-start(bf16[4,128,384]{2,1,0:T(8,128)(2,1)} %pad_maximum_fusion.1.near_ref), channel_id=1, source_target_pairs={{0,4},{4,0},{8,12},{12,8},{16,20},{20,16},{24,28},{28,24},{1,5},{5... | collective-permute-start | bytes 1179656 | tf_op jit(solution)/shard_map/ppermute | solution.py:275
  60.4 8.7 %collective-permute-start.9 = (bf16[256,384]{1,0:T(8,128)(2,1)S(1)}, bf16[256,384]{1,0:T(8,128)(2,1)S(1)}, u32[]{:S(2)}, u32[]{:S(2)}) collective-permute-start(bf16[256,384]{1,0:T(8,128)(2,1)S(1)} %add.49), channel_id=1, source_target_pairs={{0,8},{4,12},{16,24},{20,28},{1,9},{5,13},{17,25},{21,29},{2,10},{... | collective-permute-start | bytes 589832 | tf_op jit(solution)/shard_map/ppermute | solution.py:311
  70.0 13.6 %collective-permute-start.10 = (bf16[2,256,384]{2,1,0:T(8,128)(2,1)}, bf16[2,256,384]{2,1,0:T(8,128)(2,1)}, u32[]{:S(2)}, u32[]{:S(2)}) collective-permute-start(bf16[2,256,384]{2,1,0:T(8,128)(2,1)} %pad_maximum_fusion.near_ref), channel_id=1, source_target_pairs={{0,4},{4,0},{8,12},{12,8},{16,20},{20,16},{24,28},{28,24},{1,5},{5... | collective-permute-start | bytes 1179656 | tf_op jit(solution)/shard_map/ppermute | solution.py:275
  71.7 18.0 %collective-permute-start.17 = (bf16[2,256,384]{2,1,0:T(8,128)(2,1)}, bf16[2,256,384]{2,1,0:T(8,128)(2,1)}, u32[]{:S(2)}, u32[]{:S(2)}) collective-permute-start(bf16[2,256,384]{2,1,0:T(8,128)(2,1)} %pad_maximum_fusion.near_ref), channel_id=1, source_target_pairs={{0,1},{1,0},{2,3},{3,2},{4,5},{5,4},{6,7},{7,6},{8,9},{9,8},{10,11... | collective-permute-start | bytes 1179656 | tf_op jit(solution)/shard_map/ppermute | solution.py:275
  71.7 12.6 %collective-permute-start.11 = (bf16[2,256,384]{2,1,0:T(8,128)(2,1)}, bf16[2,256,384]{2,1,0:T(8,128)(2,1)}, u32[]{:S(2)}, u32[]{:S(2)}) collective-permute-start(bf16[2,256,384]{2,1,0:T(8,128)(2,1)} %pad_maximum_fusion.near_ref), channel_id=1, source_target_pairs={{0,2},{1,3},{2,0},{3,1},{4,6},{5,7},{6,4},{7,5},{8,10},{9,11},{10,... | collective-permute-start | bytes 1179656 | tf_op jit(solution)/shard_map/ppermute | solution.py:275
  84.3 5.4 %collective-permute-start.18 = (bf16[2,256,384]{2,1,0:T(8,128)(2,1)}, bf16[2,256,384]{2,1,0:T(8,128)(2,1)S(1)}, u32[]{:S(2)}, u32[]{:S(2)}) collective-permute-start(bf16[2,256,384]{2,1,0:T(8,128)(2,1)} %collective-permute-done.10.far_ref), channel_id=1, source_target_pairs={{0,1},{1,0},{2,3},{3,2},{4,5},{5,4},{6,7},{7,6},{8,9},{9,8},{10,11... | collective-permute-start | bytes 1179656 | tf_op jit(solution)/shard_map/ppermute | solution.py:275
  89.7 0.7 copy-start.4
  91.4 29.7 %all-to-all-start.1 = ((f16[8,136,384]{2,1,0:T(8,128)(2,1)}), f16[8,136,384]{2,1,0:T(8,128)(2,1)}, u32[]{:S(2)}, u32[]{:S(2)}) async-start(f16[8,136,384]{2,1,0:T(8,128)(2,1)} %convert_element_type.6), calls=%async_computation.1 | async-start | bytes 1671168 | tf_op jit(solution)/shard_map/all_to_all | solution.py:340
  96.4 13.0 %collective-permute-start.16 = (bf16[2,256,384]{2,1,0:T(8,128)(2,1)}, bf16[2,256,384]{2,1,0:T(8,128)(2,1)}, u32[]{:S(2)}, u32[]{:S(2)}) collective-permute-start(bf16[2,256,384]{2,1,0:T(8,128)(2,1)} %collective-permute-done.10.far_ref), channel_id=1, source_target_pairs={{0,2},{1,3},{2,0},{3,1},{4,6},{5,7},{6,4},{7,5},{8,10},{9,11},{10,... | collective-permute-start | bytes 1179656 | tf_op jit(solution)/shard_map/ppermute | solution.py:275
  98.3 1.4 %copy-start.1 = (bf16[512,1536]{1,0:T(8,128)(2,1)S(1)}, bf16[512,1536]{1,0:T(8,128)(2,1)}, u32[]{:S(2)}) copy-start(bf16[512,1536]{1,0:T(8,128)(2,1)} %q_ref.7) | copy-start | bytes 4718596
  99.7 4.9 %copy-start.2 = (bf16[512,1536]{1,0:T(8,128)(2,1)S(1)}, bf16[512,1536]{1,0:T(8,128)(2,1)}, u32[]{:S(2)}) copy-start(bf16[512,1536]{1,0:T(8,128)(2,1)} %q_ref.7) | copy-start | bytes 4718596
  99.7 4.9 %copy-start.5 = (bf16[2,256,384]{2,1,0:T(8,128)(2,1)S(1)}, bf16[2,256,384]{2,1,0:T(8,128)(2,1)}, u32[]{:S(2)}) copy-start(bf16[2,256,384]{2,1,0:T(8,128)(2,1)} %copy-done.4) | copy-start | bytes 1179652
  109.4 6.9 %collective-permute-start.19 = (bf16[2,256,384]{2,1,0:T(8,128)(2,1)}, bf16[2,256,384]{2,1,0:T(8,128)(2,1)}, u32[]{:S(2)}, u32[]{:S(2)}) collective-permute-start(bf16[2,256,384]{2,1,0:T(8,128)(2,1)} %collective-permute-done.11.near_ref), channel_id=1, source_target_pairs={{0,1},{1,0},{2,3},{3,2},{4,5},{5,4},{6,7},{7,6},{8,9},{9,8},{10,11... | collective-permute-start | bytes 1179656 | tf_op jit(solution)/shard_map/ppermute | solution.py:275
  109.4 6.9 %collective-permute-start.20 = (bf16[2,256,384]{2,1,0:T(8,128)(2,1)}, bf16[2,256,384]{2,1,0:T(8,128)(2,1)}, u32[]{:S(2)}, u32[]{:S(2)}) collective-permute-start(bf16[2,256,384]{2,1,0:T(8,128)(2,1)} %collective-permute-done.16.far_ref), channel_id=1, source_target_pairs={{0,1},{1,0},{2,3},{3,2},{4,5},{5,4},{6,7},{7,6},{8,9},{9,8},{10,11... | collective-permute-start | bytes 1179656 | tf_op jit(solution)/shard_map/ppermute | solution.py:275
  110.1 1.4 %copy-start.3 = (bf16[512,1536]{1,0:T(8,128)(2,1)S(1)}, bf16[512,1536]{1,0:T(8,128)(2,1)}, u32[]{:S(2)}) copy-start(bf16[512,1536]{1,0:T(8,128)(2,1)} %q_ref.7) | copy-start | bytes 4718596

commit v16 on v14

--- a/solution.py
+++ b/solution.py
@@ -158,7 +158,7 @@
         ),
         out_shape=jax.ShapeDtypeStruct((hosts, share + EXTRA, width), jnp.float32),
         input_output_aliases={6: 0} if more else {},
-        compiler_params=pltpu.CompilerParams(vmem_limit_bytes=24 * 1024 * 1024),
+        compiler_params=pltpu.CompilerParams(vmem_limit_bytes=16 * 1024 * 1024),
         cost_estimate=pl.CostEstimate(
             flops=8 * count * hosts * share * seen * HSZ,
             bytes_accessed=4 * count * (groups * rows + 3 * hosts * share) * HSZ,
@@ -258,7 +258,7 @@
         ),
         out_shape=jax.ShapeDtypeStruct((rows, width), q.dtype),
         input_output_aliases={7: 0} if more else {},
-        compiler_params=pltpu.CompilerParams(vmem_limit_bytes=24 * 1024 * 1024),
+        compiler_params=pltpu.CompilerParams(vmem_limit_bytes=16 * 1024 * 1024),
         cost_estimate=pl.CostEstimate(
             flops=8 * rows * rows * wide,
             bytes_accessed=12 * rows * wide,

time: 117 us -> 117 us (level)
  no operation moved by 1% of the time
where the time goes in v16:
time: 117 us; the launch traced here: 116 us
  starting transfers between devices  42.3 us (36%)
  Pallas kernels  40.6 us (35%)
  waiting for transfers between devices  17 us (15%)
  other arithmetic  9.69 us (8%)
  local copies, waits for them, and re-layouts  5 us (4%)
    pallas_call x4, Pallas kernels, context_attend(): pl.pallas_call(context_kernel, grid_spec=pltpu.PrefetchScalarGridSpec(num...  19.3 us
    ppermute x6, starting transfers between devices, scatter_anchor(): send = lambda x, to: lax.ppermute(x, BOTH, [(0, to), (to, 0)])  15.6 us
    pallas_call x2, Pallas kernels, suffix_attend(): pl.pallas_call(suffix_kernel, grid_spec=pltpu.PrefetchScalarGridSpec(num_...  14.7 us
    ppermute x4, waiting for transfers between devices, spread_anchor(): piece = piece + lax.ppermute(piece, 'hst', pairs)  8.26 us
    ppermute x4, starting transfers between devices, spread_anchor(): piece = piece + lax.ppermute(piece, 'hst', pairs)  6.79 us
    ppermute x11, starting transfers between devices, swap(): lax.ppermute(x, axis, [(i, i ^ k) for i in range(lax.axis_size(axis))])  6.74 us
    all_to_all x1, starting transfers between devices, per_device(): lax.all_to_all(after(packed, down), 'grp', split_axis=0, concat_axis=0, t...  4.92 us
    all_to_all x1, starting transfers between devices, per_device(): lax.all_to_all(parts, 'hst', split_axis=0, concat_axis=0, tiled=True)  4.4 us
  transfers between devices with their start and end apart: 25, of which 9 were waited for; matrix products, arithmetic and copies ran while one was open for 7% of the time, Pallas kernels for 29%

profile of v16, /device:TPU:0, one launch (start us, length us, event | category | flops | bytes accessed | tf_op | source)
XLA Modules:
  0.0 115.6 jit_solution(11574588054268737707)
XLA Ops:
  0.6 3.9 %pack_heads.1 = (bf16[4,2,512,384]{3,2,1,0:T(8,128)(2,1)}, bf16[256,768]{1,0:T(8,128)(2,1)}, bf16[256,768]{1,0:T(8,128)(2,1)}, bf16[256,768]{1,0:T(8,128)(2,1)},...) custom-call(bf16[2,512,1536]{2,1,0:T(8,128)(2,1)} %kv_ref.9), custom_call_target="tpu_custom_call" | custom-call | bytes 9437184 | tf_op jit(solution)/shard_map/pack_heads/pallas_call | solution.py:66
  4.5 4.9 %collective-permute-start.2 = (bf16[256,768]{1,0:T(8,128)(2,1)}, bf16[256,768]{1,0:T(8,128)(2,1)S(1)}, u32[]{:S(2)}, u32[]{:S(2)}) collective-permute-start(bf16[256,768]{1,0:T(8,128)(2,1)} %get-tuple-element.25), channel_id=1, source_target_pairs={{0,4},{4,0}} | collective-permute-start | bytes 1179656 | tf_op jit(solution)/shard_map/ppermute | solution.py:287
  9.4 1.9 %collective-permute-start = (bf16[256,768]{1,0:T(8,128)(2,1)}, bf16[256,768]{1,0:T(8,128)(2,1)}, u32[]{:S(2)}, u32[]{:S(2)}) collective-permute-start(bf16[256,768]{1,0:T(8,128)(2,1)} %get-tuple-element.23), channel_id=1, source_target_pairs={{0,6},{6,0}} | collective-permute-start | bytes 1179656 | tf_op jit(solution)/shard_map/ppermute | solution.py:287
  11.3 1.9 %collective-permute-start.1 = (bf16[256,768]{1,0:T(8,128)(2,1)}, bf16[256,768]{1,0:T(8,128)(2,1)}, u32[]{:S(2)}, u32[]{:S(2)}) collective-permute-start(bf16[256,768]{1,0:T(8,128)(2,1)} %get-tuple-element.24), channel_id=1, source_target_pairs={{0,2},{2,0}} | collective-permute-start | bytes 1179656 | tf_op jit(solution)/shard_map/ppermute | solution.py:287
  13.2 1.9 %collective-permute-start.8 = (bf16[256,768]{1,0:T(8,128)(2,1)}, bf16[256,768]{1,0:T(8,128)(2,1)S(1)}, u32[]{:S(2)}, u32[]{:S(2)}) collective-permute-start(bf16[256,768]{1,0:T(8,128)(2,1)} %get-tuple-element.28), channel_id=1, source_target_pairs={{0,4},{4,0}} | collective-permute-start | bytes 1179656 | tf_op jit(solution)/shard_map/ppermute | solution.py:287
  15.2 3.1 %collective-permute-start.6 = (bf16[256,768]{1,0:T(8,128)(2,1)}, bf16[256,768]{1,0:T(8,128)(2,1)}, u32[]{:S(2)}, u32[]{:S(2)}) collective-permute-start(bf16[256,768]{1,0:T(8,128)(2,1)} %get-tuple-element.26), channel_id=1, source_target_pairs={{0,6},{6,0}} | collective-permute-start | bytes 1179656 | tf_op jit(solution)/shard_map/ppermute | solution.py:287
  18.3 1.9 %collective-permute-start.7 = (bf16[256,768]{1,0:T(8,128)(2,1)}, bf16[256,768]{1,0:T(8,128)(2,1)}, u32[]{:S(2)}, u32[]{:S(2)}) collective-permute-start(bf16[256,768]{1,0:T(8,128)(2,1)} %get-tuple-element.27), channel_id=1, source_target_pairs={{0,2},{2,0}} | collective-permute-start | bytes 1179656 | tf_op jit(solution)/shard_map/ppermute | solution.py:287
  20.2 4.9 %all-to-all-start = ((bf16[4,2,512,384]{3,2,1,0:T(8,128)(2,1)}), bf16[4,2,512,384]{3,2,1,0:T(8,128)(2,1)}, u32[]{:S(2)}, u32[]{:S(2)}) async-start(bf16[4,2,512,384]{3,2,1,0:T(8,128)(2,1)} %get-tuple-element.31), calls=%async_computation | async-start | bytes 6291456 | tf_op jit(solution)/shard_map/all_to_all | solution.py:324
  25.2 1.5 %broadcast_compare_fusion = pred[16384]{0:T(1024)(128)(4,1)} fusion(s32[16384]{0:T(1024)} %param.8), kind=kLoop, calls=%fused_computation.11 | loop fusion | flops 16384 | bytes 81920 | tf_op jit(solution)/shard_map/ge | solution.py:328
  26.6 1.4 %ge.11 = pred[32,512]{1,0:T(8,128)(4,1)} reshape(pred[16384]{0:T(1024)(128)(4,1)} %broadcast_compare_fusion) | data formatting | bytes 32768 | tf_op jit(solution)/shard_map/ge | solution.py:328
  28.0 1.3 %bitcast_select_fusion.1 = bf16[256,768]{1,0:T(8,128)(2,1)S(1)} fusion(bf16[256,768]{1,0:T(8,128)(2,1)} %copy-done.8, bf16[256,768]{1,0:T(8,128)(2,1)} %collective-permute-done, bf16[256,768]{1,0:T(8,128)(2,1)} %collective-permute-done.1, bf16[2,512,1536]{2,1,0:T(8,128)(2,1)S(1)} %copy-done, pred[]{:T(512)S(6)} %and.18), kind=kLoop, calls=%fused_computation.3 | loop fusion | flops 589824 | bytes 1966081 | tf_op jit(solution)/shard_map/jit(_where)/select_n | solution.py:297
  29.4 2.5 %collective-permute-start.3 = (bf16[256,384]{1,0:T(8,128)(2,1)S(1)}, bf16[256,384]{1,0:T(8,128)(2,1)S(1)}, u32[]{:S(2)}, u32[]{:S(2)}) collective-permute-start(bf16[256,384]{1,0:T(8,128)(2,1)S(1)} %slice.25), channel_id=1, source_target_pairs={{0,1},{2,3},{4,5},{6,7},{8,9},{10,11},{12,13},{14,15},{16,17},{18,... | collective-permute-start | bytes 589832 | tf_op jit(solution)/shard_map/ppermute | solution.py:307
  31.9 0.8 collective-permute-done.7
  32.7 1.2 %bitcast_select_fusion = bf16[256,768]{1,0:T(8,128)(2,1)S(1)} fusion(bf16[256,768]{1,0:T(8,128)(2,1)S(1)} %collective-permute-done.8, bf16[256,768]{1,0:T(8,128)(2,1)} %collective-permute-done.6, bf16[256,768]{1,0:T(8,128)(2,1)} %collective-permute-done.7, bf16[2,512,1536]{2,1,0:T(8,128)(2,1)S(1)} %copy-done, pred[]{:T(512)S(6)} %and.18), kind=kLoop, calls=%fused_computation.2 | loop fusion | flops 589824 | bytes 1966081 | tf_op jit(solution)/shard_map/jit(_where)/select_n | solution.py:297
  33.9 1.3 %collective-permute-start.9 = (bf16[256,384]{1,0:T(8,128)(2,1)S(1)}, bf16[256,384]{1,0:T(8,128)(2,1)S(1)}, u32[]{:S(2)}, u32[]{:S(2)}) collective-permute-start(bf16[256,384]{1,0:T(8,128)(2,1)S(1)} %slice.27), channel_id=1, source_target_pairs={{0,1},{2,3},{4,5},{6,7},{8,9},{10,11},{12,13},{14,15},{16,17},{18,... | collective-permute-start | bytes 589832 | tf_op jit(solution)/shard_map/ppermute | solution.py:307
  35.3 1.3 %collective-permute-start.4 = (bf16[256,384]{1,0:T(8,128)(2,1)S(1)}, bf16[256,384]{1,0:T(8,128)(2,1)S(1)}, u32[]{:S(2)}, u32[]{:S(2)}) collective-permute-start(bf16[256,384]{1,0:T(8,128)(2,1)S(1)} %slice_add_fusion.1), channel_id=1, source_target_pairs={{0,16},{4,20},{1,17},{5,21},{2,18},{6,22},{3,19},{7,23}} | collective-permute-start | bytes 589832 | tf_op jit(solution)/shard_map/ppermute | solution.py:312
  36.8 3.4 %collective-permute-start.14 = (bf16[128,384]{1,0:T(8,128)(2,1)S(1)}, bf16[128,384]{1,0:T(8,128)(2,1)S(1)}, u32[]{:S(2)}, u32[]{:S(2)}) collective-permute-start(bf16[128,384]{1,0:T(8,128)(2,1)S(1)} %copy-done.9), channel_id=1, source_target_pairs={{0,8},{4,12},{8,0},{12,4},{16,24},{20,28},{24,16},{28,20},{1,9},{5... | collective-permute-start | bytes 294920 | tf_op jit(solution)/shard_map/ppermute | solution.py:272
  40.2 2.9 %collective-permute-start.10 = (bf16[256,384]{1,0:T(8,128)(2,1)S(1)}, bf16[256,384]{1,0:T(8,128)(2,1)S(1)}, u32[]{:S(2)}, u32[]{:S(2)}) collective-permute-start(bf16[256,384]{1,0:T(8,128)(2,1)S(1)} %slice_add_fusion), channel_id=1, source_target_pairs={{0,16},{4,20},{1,17},{5,21},{2,18},{6,22},{3,19},{7,23}} | collective-permute-start | bytes 589832 | tf_op jit(solution)/shard_map/ppermute | solution.py:312
  43.2 1.3 %collective-permute-start.5 = (bf16[256,384]{1,0:T(8,128)(2,1)S(1)}, bf16[256,384]{1,0:T(8,128)(2,1)S(1)}, u32[]{:S(2)}, u32[]{:S(2)}) collective-permute-start(bf16[256,384]{1,0:T(8,128)(2,1)S(1)} %add.48), channel_id=1, source_target_pairs={{0,8},{4,12},{16,24},{20,28},{1,9},{5,13},{17,25},{21,29},{2,10},{... | collective-permute-start | bytes 589832 | tf_op jit(solution)/shard_map/ppermute | solution.py:312
  44.5 0.1 fusion.1.bias_ref
  44.6 0.8 collective-permute-done.15
  45.4 0.8 collective-permute-done.16
  46.2 2.1 %collective-permute-done.14 = bf16[128,384]{1,0:T(8,128)(2,1)S(1)} collective-permute-done((bf16[128,384]{1,0:T(8,128)(2,1)S(1)}, bf16[128,384]{1,0:T(8,128)(2,1)S(1)}, u32[]{:S(2)}, u32[]{:S(2)}) %collective-permute-start.14) | collective-permute-done | bytes 98336 | tf_op jit(solution)/shard_map/ppermute | solution.py:272
  48.3 0.8 pad_maximum_fusion.1.near_ref
  49.1 3.4 %collective-permute-done.10 = bf16[256,384]{1,0:T(8,128)(2,1)S(1)} collective-permute-done((bf16[256,384]{1,0:T(8,128)(2,1)S(1)}, bf16[256,384]{1,0:T(8,128)(2,1)S(1)}, u32[]{:S(2)}, u32[]{:S(2)}) %collective-permute-start.10) | collective-permute-done | bytes 196640 | tf_op jit(solution)/shard_map/ppermute | solution.py:312
  52.6 1.3 %collective-permute-start.11 = (bf16[256,384]{1,0:T(8,128)(2,1)S(1)}, bf16[256,384]{1,0:T(8,128)(2,1)S(1)}, u32[]{:S(2)}, u32[]{:S(2)}) collective-permute-start(bf16[256,384]{1,0:T(8,128)(2,1)S(1)} %add.53), channel_id=1, source_target_pairs={{0,8},{4,12},{16,24},{20,28},{1,9},{5,13},{17,25},{21,29},{2,10},{... | collective-permute-start | bytes 589832 | tf_op jit(solution)/shard_map/ppermute | solution.py:312
  53.9 2.8 %collective-permute-done.5 = bf16[256,384]{1,0:T(8,128)(2,1)S(1)} collective-permute-done((bf16[256,384]{1,0:T(8,128)(2,1)S(1)}, bf16[256,384]{1,0:T(8,128)(2,1)S(1)}, u32[]{:S(2)}, u32[]{:S(2)}) %collective-permute-start.5) | collective-permute-done | bytes 196640 | tf_op jit(solution)/shard_map/ppermute | solution.py:312
  56.7 2.1 %collective-permute-done.11 = bf16[256,384]{1,0:T(8,128)(2,1)S(1)} collective-permute-done((bf16[256,384]{1,0:T(8,128)(2,1)S(1)}, bf16[256,384]{1,0:T(8,128)(2,1)S(1)}, u32[]{:S(2)}, u32[]{:S(2)}) %collective-permute-start.11) | collective-permute-done | bytes 196640 | tf_op jit(solution)/shard_map/ppermute | solution.py:312
  58.8 0.8 pad_maximum_fusion.near_ref
  59.6 3.7 %all-to-all-done.kv_ref = bf16[4,2,512,384]{3,2,1,0:T(8,128)(2,1)} async-done(((bf16[4,2,512,384]{3,2,1,0:T(8,128)(2,1)}), bf16[4,2,512,384]{3,2,1,0:T(8,128)(2,1)}, u32[]{:S(2)}, u32[]{:S(2)}) %all-to-all-start) | async-done | bytes 3145760 | tf_op jit(solution)/shard_map/all_to_all | solution.py:324
  63.3 2.5 %collective-permute-start.13 = (bf16[2,256,384]{2,1,0:T(8,128)(2,1)}, bf16[2,256,384]{2,1,0:T(8,128)(2,1)}, u32[]{:S(2)}, u32[]{:S(2)}) collective-permute-start(bf16[2,256,384]{2,1,0:T(8,128)(2,1)} %pad_maximum_fusion.near_ref), channel_id=1, source_target_pairs={{0,2},{1,3},{2,0},{3,1},{4,6},{5,7},{6,4},{7,5},{8,10},{9,11},{10,... | collective-permute-start | bytes 1179656 | tf_op jit(solution)/shard_map/ppermute | solution.py:272
  65.8 9.3 %suffix_attend.2.rest_0_ = f32[8,136,384]{2,1,0:T(8,128)S(1)} custom-call(s32[1]{0:T(128)} %bitcast.7.at_ref, bf16[4,128,384]{2,1,0:T(8,128)(2,1)} %pad_maximum_fusion.1.near_ref, bf16[4,128,384]{2,1,0:T(8,128)(2,1)} %collective-permute-done.17.far_ref, bf16[4,2,512,384]{3,2,1,0:T(8,128)(2,1)} %all-to-all-done.kv_ref, bf16[2,128,384]{2,1,0:T(8,128)(2,1)S(1)} %copy-done.7, ...), custom_call_target="tpu_custom_call" | custom-call | flops 4563402752 | bytes 5242880 | tf_op jit(solution)/shard_map/suffix_attend/pallas_call | solution.py:144
  75.2 5.4 %suffix_attend.3 = f32[8,136,384]{2,1,0:T(8,128)S(1)} custom-call(s32[1]{0:T(128)} %bitcast.7.at_ref, bf16[4,128,384]{2,1,0:T(8,128)(2,1)} %pad_maximum_fusion.1.near_ref, bf16[4,128,384]{2,1,0:T(8,128)(2,1)} %collective-permute-done.17.far_ref, bf16[4,2,512,384]{3,2,1,0:T(8,128)(2,1)} %all-to-all-done.kv_ref, ...), custom_call_target="tpu_custom_call", output_to_operand_aliasing={{}: (6, {})} | custom-call | flops 2281701376 | bytes 2621440 | tf_op jit(solution)/shard_map/suffix_attend/pallas_call | solution.py:144
  80.6 0.7 copy-done.4
  81.4 1.0 convert_element_type.6
  82.4 4.4 %all-to-all-start.1 = ((f16[8,136,384]{2,1,0:T(8,128)(2,1)}), f16[8,136,384]{2,1,0:T(8,128)(2,1)}, u32[]{:S(2)}, u32[]{:S(2)}) async-start(f16[8,136,384]{2,1,0:T(8,128)(2,1)} %convert_element_type.6), calls=%async_computation.1 | async-start | bytes 1671168 | tf_op jit(solution)/shard_map/all_to_all | solution.py:341
  86.8 0.1 collective-permute-start.18
  86.9 0.1 add_add_fusion.2.at_ref
  87.1 1.4 %copy-done.1 = bf16[512,1536]{1,0:T(8,128)(2,1)S(1)} copy-done((bf16[512,1536]{1,0:T(8,128)(2,1)S(1)}, bf16[512,1536]{1,0:T(8,128)(2,1)}, u32[]{:S(2)}) %copy-start.1) | copy-done | bytes 1572888
  88.5 4.9 %context_attend.4.rest_0_ = bf16[512,1536]{1,0:T(8,128)(2,1)} custom-call(s32[3]{0:T(128)S(1)} %add_add_fusion.2.at_ref, s32[32]{0:T(128)S(1)} %copy-done.6, bf16[512,1536]{1,0:T(8,128)(2,1)S(1)} %copy-done.1, bf16[2,512,1536]{2,1,0:T(8,128)(2,1)S(1)} %copy-done, f32[32,512]{1,0:T(8,128)S(1)} %fusion.1.bias_ref, ...), custom_call_target="tpu_custom_call" | custom-call | flops 805306368 | bytes 2359296 | tf_op jit(solution)/shard_map/context_attend/pallas_call | solution.py:243
  93.4 4.8 %context_attend.5.rest_0_ = bf16[512,1536]{1,0:T(8,128)(2,1)} custom-call(s32[3]{0:T(128)S(1)} %add_add_fusion.1.at_ref, s32[32]{0:T(128)S(1)} %copy-done.6, bf16[512,1536]{1,0:T(8,128)(2,1)S(1)} %copy-done.2, bf16[2,512,1536]{2,1,0:T(8,128)(2,1)S(1)} %copy-done, f32[32,512]{1,0:T(8,128)S(1)} %fusion.1.bias_ref, ...), custom_call_target="tpu_custom_call", output_to_operand_aliasing={{}: (7, {})} | custom-call | flops 805306368 | bytes 2359296 | tf_op jit(solution)/shard_map/context_attend/pallas_call | solution.py:243
  98.2 0.5 collective-permute-done.18.far_ref
  98.7 0.5 collective-permute-start.22
  99.4 1.4 %copy-done.3 = bf16[512,1536]{1,0:T(8,128)(2,1)S(1)} copy-done((bf16[512,1536]{1,0:T(8,128)(2,1)S(1)}, bf16[512,1536]{1,0:T(8,128)(2,1)}, u32[]{:S(2)}) %copy-start.3) | copy-done | bytes 1572888
  100.8 4.8 %context_attend.6.rest_0_ = bf16[512,1536]{1,0:T(8,128)(2,1)} custom-call(s32[3]{0:T(128)S(1)} %add_add_fusion.3.at_ref, s32[32]{0:T(128)S(1)} %copy-done.6, bf16[512,1536]{1,0:T(8,128)(2,1)S(1)} %copy-done.3, bf16[2,512,1536]{2,1,0:T(8,128)(2,1)S(1)} %copy-done, f32[32,512]{1,0:T(8,128)S(1)} %fusion.1.bias_ref, ...), custom_call_target="tpu_custom_call", output_to_operand_aliasing={{}: (7, {})} | custom-call | flops 805306368 | bytes 2359296 | tf_op jit(solution)/shard_map/context_attend/pallas_call | solution.py:243
  105.6 4.8 %context_attend.7 = bf16[512,1536]{1,0:T(8,128)(2,1)} custom-call(s32[3]{0:T(128)S(1)} %add_add_fusion.at_ref, s32[32]{0:T(128)S(1)} %copy-done.6, bf16[512,1536]{1,0:T(8,128)(2,1)S(1)} %copy-done.3, bf16[2,512,1536]{2,1,0:T(8,128)(2,1)S(1)} %copy-done, f32[32,512]{1,0:T(8,128)S(1)} %fusion.1.bias_ref, ...), custom_call_target="tpu_custom_call", output_to_operand_aliasing={{}: (7, {})} | custom-call | flops 805306368 | bytes 2359296 | tf_op jit(solution)/shard_map/context_attend/pallas_call | solution.py:243
  110.4 2.5 %convert_element_type.7.in_ref = f32[8,136,384]{2,1,0:T(8,128)} convert(f16[8,136,384]{2,1,0:T(8,128)(2,1)} %all-to-all-done.1) | non-fusion elementwise | flops 417792 | bytes 2506752 | tf_op jit(solution)/shard_map/convert_element_type | solution.py:357
  112.9 2.7 %combine_groups.1 = bf16[128,384]{1,0:T(8,128)(2,1)} custom-call(f32[8,136,384]{2,1,0:T(8,128)} %convert_element_type.7.in_ref), custom_call_target="tpu_custom_call" | custom-call | flops 835584 | bytes 1671168 | tf_op jit(solution)/shard_map/combine_groups/pallas_call | solution.py:188
  (53 shorter events, 0.8 us)
Async XLA Ops:
  4.5 13.8 %collective-permute-start.2 = (bf16[256,768]{1,0:T(8,128)(2,1)}, bf16[256,768]{1,0:T(8,128)(2,1)S(1)}, u32[]{:S(2)}, u32[]{:S(2)}) collective-permute-start(bf16[256,768]{1,0:T(8,128)(2,1)} %get-tuple-element.25), channel_id=1, source_target_pairs={{0,4},{4,0}} | collective-permute-start | bytes 1179656 | tf_op jit(solution)/shard_map/ppermute | solution.py:287
  9.4 18.6 %collective-permute-start = (bf16[256,768]{1,0:T(8,128)(2,1)}, bf16[256,768]{1,0:T(8,128)(2,1)}, u32[]{:S(2)}, u32[]{:S(2)}) collective-permute-start(bf16[256,768]{1,0:T(8,128)(2,1)} %get-tuple-element.23), channel_id=1, source_target_pairs={{0,6},{6,0}} | collective-permute-start | bytes 1179656 | tf_op jit(solution)/shard_map/ppermute | solution.py:287
  11.3 16.7 %collective-permute-start.1 = (bf16[256,768]{1,0:T(8,128)(2,1)}, bf16[256,768]{1,0:T(8,128)(2,1)}, u32[]{:S(2)}, u32[]{:S(2)}) collective-permute-start(bf16[256,768]{1,0:T(8,128)(2,1)} %get-tuple-element.24), channel_id=1, source_target_pairs={{0,2},{2,0}} | collective-permute-start | bytes 1179656 | tf_op jit(solution)/shard_map/ppermute | solution.py:287
  13.2 16.1 %collective-permute-start.8 = (bf16[256,768]{1,0:T(8,128)(2,1)}, bf16[256,768]{1,0:T(8,128)(2,1)S(1)}, u32[]{:S(2)}, u32[]{:S(2)}) collective-permute-start(bf16[256,768]{1,0:T(8,128)(2,1)} %get-tuple-element.28), channel_id=1, source_target_pairs={{0,4},{4,0}} | collective-permute-start | bytes 1179656 | tf_op jit(solution)/shard_map/ppermute | solution.py:287
  15.2 16.7 %collective-permute-start.6 = (bf16[256,768]{1,0:T(8,128)(2,1)}, bf16[256,768]{1,0:T(8,128)(2,1)}, u32[]{:S(2)}, u32[]{:S(2)}) collective-permute-start(bf16[256,768]{1,0:T(8,128)(2,1)} %get-tuple-element.26), channel_id=1, source_target_pairs={{0,6},{6,0}} | collective-permute-start | bytes 1179656 | tf_op jit(solution)/shard_map/ppermute | solution.py:287
  18.3 1.9 %copy-start.8 = (bf16[256,768]{1,0:T(8,128)(2,1)}, bf16[256,768]{1,0:T(8,128)(2,1)S(1)}, u32[]{:S(2)}) copy-start(bf16[256,768]{1,0:T(8,128)(2,1)S(1)} %collective-permute-done.2) | copy-start | bytes 1179652
  18.3 14.4 %collective-permute-start.7 = (bf16[256,768]{1,0:T(8,128)(2,1)}, bf16[256,768]{1,0:T(8,128)(2,1)}, u32[]{:S(2)}, u32[]{:S(2)}) collective-permute-start(bf16[256,768]{1,0:T(8,128)(2,1)} %get-tuple-element.27), channel_id=1, source_target_pairs={{0,2},{2,0}} | collective-permute-start | bytes 1179656 | tf_op jit(solution)/shard_map/ppermute | solution.py:287
  20.2 7.8 %copy-start = (bf16[2,512,1536]{2,1,0:T(8,128)(2,1)S(1)}, bf16[2,512,1536]{2,1,0:T(8,128)(2,1)}, u32[]{:S(2)}) copy-start(bf16[2,512,1536]{2,1,0:T(8,128)(2,1)} %kv_ref.9) | copy-start | bytes 9437188
  20.2 43.1 %all-to-all-start = ((bf16[4,2,512,384]{3,2,1,0:T(8,128)(2,1)}), bf16[4,2,512,384]{3,2,1,0:T(8,128)(2,1)}, u32[]{:S(2)}, u32[]{:S(2)}) async-start(bf16[4,2,512,384]{3,2,1,0:T(8,128)(2,1)} %get-tuple-element.31), calls=%async_computation | async-start | bytes 6291456 | tf_op jit(solution)/shard_map/all_to_all | solution.py:324
  29.3 7.3 %copy-start.9 = (bf16[128,384]{1,0:T(8,128)(2,1)S(1)}, bf16[128,384]{1,0:T(8,128)(2,1)}, u32[]{:S(2)}) copy-start(bf16[128,384]{1,0:T(8,128)(2,1)} %param.10) | copy-start | bytes 294916
  29.3 15.1 %copy-start.6 = (s32[32]{0:T(128)S(1)}, s32[32]{0:T(128)}, u32[]{:S(2)}) copy-start(s32[32]{0:T(128)} %len_ref.7) | copy-start | bytes 388
  29.3 15.1 %copy-start.10 = (pred[32,512]{1,0:T(8,128)(4,1)S(1)}, pred[32,512]{1,0:T(8,128)(4,1)}, u32[]{:S(2)}) copy-start(pred[32,512]{1,0:T(8,128)(4,1)} %ge.11) | copy-start | bytes 49156
  29.4 5.9 %collective-permute-start.3 = (bf16[256,384]{1,0:T(8,128)(2,1)S(1)}, bf16[256,384]{1,0:T(8,128)(2,1)S(1)}, u32[]{:S(2)}, u32[]{:S(2)}) collective-permute-start(bf16[256,384]{1,0:T(8,128)(2,1)S(1)} %slice.25), channel_id=1, source_target_pairs={{0,1},{2,3},{4,5},{6,7},{8,9},{10,11},{12,13},{14,15},{16,17},{18,... | collective-permute-start | bytes 589832 | tf_op jit(solution)/shard_map/ppermute | solution.py:307
  33.9 2.7 %collective-permute-start.9 = (bf16[256,384]{1,0:T(8,128)(2,1)S(1)}, bf16[256,384]{1,0:T(8,128)(2,1)S(1)}, u32[]{:S(2)}, u32[]{:S(2)}) collective-permute-start(bf16[256,384]{1,0:T(8,128)(2,1)S(1)} %slice.27), channel_id=1, source_target_pairs={{0,1},{2,3},{4,5},{6,7},{8,9},{10,11},{12,13},{14,15},{16,17},{18,... | collective-permute-start | bytes 589832 | tf_op jit(solution)/shard_map/ppermute | solution.py:307
  35.3 7.8 %collective-permute-start.4 = (bf16[256,384]{1,0:T(8,128)(2,1)S(1)}, bf16[256,384]{1,0:T(8,128)(2,1)S(1)}, u32[]{:S(2)}, u32[]{:S(2)}) collective-permute-start(bf16[256,384]{1,0:T(8,128)(2,1)S(1)} %slice_add_fusion.1), channel_id=1, source_target_pairs={{0,16},{4,20},{1,17},{5,21},{2,18},{6,22},{3,19},{7,23}} | collective-permute-start | bytes 589832 | tf_op jit(solution)/shard_map/ppermute | solution.py:312
  36.7 8.8 %collective-permute-start.15 = (bf16[128,384]{1,0:T(8,128)(2,1)S(1)}, bf16[128,384]{1,0:T(8,128)(2,1)S(1)}, u32[]{:S(2)}, u32[]{:S(2)}) collective-permute-start(bf16[128,384]{1,0:T(8,128)(2,1)S(1)} %copy-done.9), channel_id=1, source_target_pairs={{0,16},{4,20},{8,24},{12,28},{16,0},{20,4},{24,8},{28,12},{1,17},{... | collective-permute-start | bytes 294920 | tf_op jit(solution)/shard_map/ppermute | solution.py:272
  36.7 9.5 %collective-permute-start.16 = (bf16[128,384]{1,0:T(8,128)(2,1)S(1)}, bf16[128,384]{1,0:T(8,128)(2,1)S(1)}, u32[]{:S(2)}, u32[]{:S(2)}) collective-permute-start(bf16[128,384]{1,0:T(8,128)(2,1)S(1)} %copy-done.9), channel_id=1, source_target_pairs={{0,24},{4,28},{8,16},{12,20},{16,8},{20,12},{24,0},{28,4},{1,25},{... | collective-permute-start | bytes 294920 | tf_op jit(solution)/shard_map/ppermute | solution.py:272
  36.8 11.5 %collective-permute-start.14 = (bf16[128,384]{1,0:T(8,128)(2,1)S(1)}, bf16[128,384]{1,0:T(8,128)(2,1)S(1)}, u32[]{:S(2)}, u32[]{:S(2)}) collective-permute-start(bf16[128,384]{1,0:T(8,128)(2,1)S(1)} %copy-done.9), channel_id=1, source_target_pairs={{0,8},{4,12},{8,0},{12,4},{16,24},{20,28},{24,16},{28,20},{1,9},{5... | collective-permute-start | bytes 294920 | tf_op jit(solution)/shard_map/ppermute | solution.py:272
  40.2 12.3 %collective-permute-start.10 = (bf16[256,384]{1,0:T(8,128)(2,1)S(1)}, bf16[256,384]{1,0:T(8,128)(2,1)S(1)}, u32[]{:S(2)}, u32[]{:S(2)}) collective-permute-start(bf16[256,384]{1,0:T(8,128)(2,1)S(1)} %slice_add_fusion), channel_id=1, source_target_pairs={{0,16},{4,20},{1,17},{5,21},{2,18},{6,22},{3,19},{7,23}} | collective-permute-start | bytes 589832 | tf_op jit(solution)/shard_map/ppermute | solution.py:312
  43.2 13.5 %collective-permute-start.5 = (bf16[256,384]{1,0:T(8,128)(2,1)S(1)}, bf16[256,384]{1,0:T(8,128)(2,1)S(1)}, u32[]{:S(2)}, u32[]{:S(2)}) collective-permute-start(bf16[256,384]{1,0:T(8,128)(2,1)S(1)} %add.48), channel_id=1, source_target_pairs={{0,8},{4,12},{16,24},{20,28},{1,9},{5,13},{17,25},{21,29},{2,10},{... | collective-permute-start | bytes 589832 | tf_op jit(solution)/shard_map/ppermute | solution.py:312
  48.3 17.5 %copy-start.7 = (bf16[2,128,384]{2,1,0:T(8,128)(2,1)S(1)}, bf16[2,128,384]{2,1,0:T(8,128)(2,1)}, u32[]{:S(2)}) copy-start(bf16[2,128,384]{2,1,0:T(8,128)(2,1)} %sk_ref.3) | copy-start | bytes 589828
  49.1 16.7 %collective-permute-start.17 = (bf16[4,128,384]{2,1,0:T(8,128)(2,1)}, bf16[4,128,384]{2,1,0:T(8,128)(2,1)}, u32[]{:S(2)}, u32[]{:S(2)}) collective-permute-start(bf16[4,128,384]{2,1,0:T(8,128)(2,1)} %pad_maximum_fusion.1.near_ref), channel_id=1, source_target_pairs={{0,4},{4,0},{8,12},{12,8},{16,20},{20,16},{24,28},{28,24},{1,5},{5... | collective-permute-start | bytes 1179656 | tf_op jit(solution)/shard_map/ppermute | solution.py:272
  52.6 6.2 %collective-permute-start.11 = (bf16[256,384]{1,0:T(8,128)(2,1)S(1)}, bf16[256,384]{1,0:T(8,128)(2,1)S(1)}, u32[]{:S(2)}, u32[]{:S(2)}) collective-permute-start(bf16[256,384]{1,0:T(8,128)(2,1)S(1)} %add.53), channel_id=1, source_target_pairs={{0,8},{4,12},{16,24},{20,28},{1,9},{5,13},{17,25},{21,29},{2,10},{... | collective-permute-start | bytes 589832 | tf_op jit(solution)/shard_map/ppermute | solution.py:312
  59.6 15.5 %collective-permute-start.12 = (bf16[2,256,384]{2,1,0:T(8,128)(2,1)}, bf16[2,256,384]{2,1,0:T(8,128)(2,1)}, u32[]{:S(2)}, u32[]{:S(2)}) collective-permute-start(bf16[2,256,384]{2,1,0:T(8,128)(2,1)} %pad_maximum_fusion.near_ref), channel_id=1, source_target_pairs={{0,4},{4,0},{8,12},{12,8},{16,20},{20,16},{24,28},{28,24},{1,5},{5... | collective-permute-start | bytes 1179656 | tf_op jit(solution)/shard_map/ppermute | solution.py:272
  59.6 21.0 %collective-permute-start.19 = (bf16[2,256,384]{2,1,0:T(8,128)(2,1)}, bf16[2,256,384]{2,1,0:T(8,128)(2,1)}, u32[]{:S(2)}, u32[]{:S(2)}) collective-permute-start(bf16[2,256,384]{2,1,0:T(8,128)(2,1)} %pad_maximum_fusion.near_ref), channel_id=1, source_target_pairs={{0,1},{1,0},{2,3},{3,2},{4,5},{5,4},{6,7},{7,6},{8,9},{9,8},{10,11... | collective-permute-start | bytes 1179656 | tf_op jit(solution)/shard_map/ppermute | solution.py:272
  63.3 11.8 %collective-permute-start.13 = (bf16[2,256,384]{2,1,0:T(8,128)(2,1)}, bf16[2,256,384]{2,1,0:T(8,128)(2,1)}, u32[]{:S(2)}, u32[]{:S(2)}) collective-permute-start(bf16[2,256,384]{2,1,0:T(8,128)(2,1)} %pad_maximum_fusion.near_ref), channel_id=1, source_target_pairs={{0,2},{1,3},{2,0},{3,1},{4,6},{5,7},{6,4},{7,5},{8,10},{9,11},{10,... | collective-permute-start | bytes 1179656 | tf_op jit(solution)/shard_map/ppermute | solution.py:272
  75.2 5.5 %collective-permute-start.20 = (bf16[2,256,384]{2,1,0:T(8,128)(2,1)}, bf16[2,256,384]{2,1,0:T(8,128)(2,1)S(1)}, u32[]{:S(2)}, u32[]{:S(2)}) collective-permute-start(bf16[2,256,384]{2,1,0:T(8,128)(2,1)} %collective-permute-done.12.far_ref), channel_id=1, source_target_pairs={{0,1},{1,0},{2,3},{3,2},{4,5},{5,4},{6,7},{7,6},{8,9},{9,8},{10,11... | collective-permute-start | bytes 1179656 | tf_op jit(solution)/shard_map/ppermute | solution.py:272
  80.6 0.7 copy-start.4
  82.4 28.0 %all-to-all-start.1 = ((f16[8,136,384]{2,1,0:T(8,128)(2,1)}), f16[8,136,384]{2,1,0:T(8,128)(2,1)}, u32[]{:S(2)}, u32[]{:S(2)}) async-start(f16[8,136,384]{2,1,0:T(8,128)(2,1)} %convert_element_type.6), calls=%async_computation.1 | async-start | bytes 1671168 | tf_op jit(solution)/shard_map/all_to_all | solution.py:341
  86.8 11.9 %collective-permute-start.18 = (bf16[2,256,384]{2,1,0:T(8,128)(2,1)}, bf16[2,256,384]{2,1,0:T(8,128)(2,1)}, u32[]{:S(2)}, u32[]{:S(2)}) collective-permute-start(bf16[2,256,384]{2,1,0:T(8,128)(2,1)} %collective-permute-done.12.far_ref), channel_id=1, source_target_pairs={{0,2},{1,3},{2,0},{3,1},{4,6},{5,7},{6,4},{7,5},{8,10},{9,11},{10,... | collective-permute-start | bytes 1179656 | tf_op jit(solution)/shard_map/ppermute | solution.py:272
  87.1 1.4 %copy-start.1 = (bf16[512,1536]{1,0:T(8,128)(2,1)S(1)}, bf16[512,1536]{1,0:T(8,128)(2,1)}, u32[]{:S(2)}) copy-start(bf16[512,1536]{1,0:T(8,128)(2,1)} %q_ref.7) | copy-start | bytes 4718596
  88.5 4.9 %copy-start.2 = (bf16[512,1536]{1,0:T(8,128)(2,1)S(1)}, bf16[512,1536]{1,0:T(8,128)(2,1)}, u32[]{:S(2)}) copy-start(bf16[512,1536]{1,0:T(8,128)(2,1)} %q_ref.7) | copy-start | bytes 4718596
  88.5 4.9 %copy-start.5 = (bf16[2,256,384]{2,1,0:T(8,128)(2,1)S(1)}, bf16[2,256,384]{2,1,0:T(8,128)(2,1)}, u32[]{:S(2)}) copy-start(bf16[2,256,384]{2,1,0:T(8,128)(2,1)} %copy-done.4) | copy-start | bytes 1179652
  98.7 6.9 %collective-permute-start.21 = (bf16[2,256,384]{2,1,0:T(8,128)(2,1)}, bf16[2,256,384]{2,1,0:T(8,128)(2,1)}, u32[]{:S(2)}, u32[]{:S(2)}) collective-permute-start(bf16[2,256,384]{2,1,0:T(8,128)(2,1)} %collective-permute-done.13.near_ref), channel_id=1, source_target_pairs={{0,1},{1,0},{2,3},{3,2},{4,5},{5,4},{6,7},{7,6},{8,9},{9,8},{10,11... | collective-permute-start | bytes 1179656 | tf_op jit(solution)/shard_map/ppermute | solution.py:272
  98.7 6.9 %collective-permute-start.22 = (bf16[2,256,384]{2,1,0:T(8,128)(2,1)}, bf16[2,256,384]{2,1,0:T(8,128)(2,1)}, u32[]{:S(2)}, u32[]{:S(2)}) collective-permute-start(bf16[2,256,384]{2,1,0:T(8,128)(2,1)} %collective-permute-done.18.far_ref), channel_id=1, source_target_pairs={{0,1},{1,0},{2,3},{3,2},{4,5},{5,4},{6,7},{7,6},{8,9},{9,8},{10,11... | collective-permute-start | bytes 1179656 | tf_op jit(solution)/shard_map/ppermute | solution.py:272
  99.4 1.4 %copy-start.3 = (bf16[512,1536]{1,0:T(8,128)(2,1)S(1)}, bf16[512,1536]{1,0:T(8,128)(2,1)}, u32[]{:S(2)}) copy-start(bf16[512,1536]{1,0:T(8,128)(2,1)} %q_ref.7) | copy-start | bytes 4718596

commit v17 on v16

--- a/solution.py
+++ b/solution.py
@@ -258,7 +258,7 @@
         ),
         out_shape=jax.ShapeDtypeStruct((rows, width), q.dtype),
         input_output_aliases={7: 0} if more else {},
-        compiler_params=pltpu.CompilerParams(vmem_limit_bytes=16 * 1024 * 1024),
+        compiler_params=pltpu.CompilerParams(vmem_limit_bytes=60 * 1024 * 1024),
         cost_estimate=pl.CostEstimate(
             flops=8 * rows * rows * wide,
             bytes_accessed=12 * rows * wide,

time: 117 us -> 119 us (1.017)
  local copies, waits for them, and re-layouts: 5 us -> 2.33 us
  waiting for transfers between devices: 17 us -> 19 us
  other arithmetic: 9.69 us -> 11 us
  Pallas kernels: 40.6 us -> 41.8 us
    ppermute x6, waiting for transfers between devices: 0.81 us -> 5.52 us  [scatter_anchor(): send = lambda x, to: lax.ppermute(x, BOTH, [(0, to), (to, 0)])]
    another operation x4, other arithmetic: 0.3 us -> 2.58 us  [context(): at = jnp.stack([host * groups + group, group ^ k, host % 2])]
    unnamed x22 -> x18, local copies, waits for them, and re-layouts: 3.6 us -> 1.54 us
    pallas_call x4, Pallas kernels: 19.3 us -> 21.4 us  [context_attend(): pl.pallas_call(context_kernel, grid_spec=pltpu.PrefetchScalarGridSpec(num...]
    ppermute x11, starting transfers between devices: 6.74 us -> 8.65 us  [swap(): lax.ppermute(x, axis, [(i, i ^ k) for i in range(lax.axis_size(axis))])]
    all_to_all x1, waiting for transfers between devices: 3.7 us -> 2.06 us  [per_device(): lax.all_to_all(after(packed, down), 'grp', split_axis=0, concat_axis=0, t...]
    all_to_all x1, starting transfers between devices: 4.92 us -> 3.71 us  [per_device(): lax.all_to_all(after(packed, down), 'grp', split_axis=0, concat_axis=0, t...]
  transfers between devices with their start and end apart: 25 -> 25, of which waited for: 9 -> 9; matrix products, arithmetic and copies ran while one was open for 7% -> 8% of each run, Pallas kernels for 29% -> 30%
where the time goes in v17:
time: 119 us; the launch traced here: 118 us
  starting transfers between devices  42.9 us (36%)
  Pallas kernels  41.8 us (35%)
  waiting for transfers between devices  19 us (16%)
  other arithmetic  11 us (9%)
  local copies, waits for them, and re-layouts  2.33 us (2%)
    pallas_call x4, Pallas kernels, context_attend(): pl.pallas_call(context_kernel, grid_spec=pltpu.PrefetchScalarGridSpec(num...  21.4 us
    ppermute x6, starting transfers between devices, scatter_anchor(): send = lambda x, to: lax.ppermute(x, BOTH, [(0, to), (to, 0)])  15.6 us
    pallas_call x2, Pallas kernels, suffix_attend(): pl.pallas_call(suffix_kernel, grid_spec=pltpu.PrefetchScalarGridSpec(num_...  13.9 us
    ppermute x11, starting transfers between devices, swap(): lax.ppermute(x, axis, [(i, i ^ k) for i in range(lax.axis_size(axis))])  8.65 us
    ppermute x4, waiting for transfers between devices, spread_anchor(): piece = piece + lax.ppermute(piece, 'hst', pairs)  7.8 us
    ppermute x4, starting transfers between devices, spread_anchor(): piece = piece + lax.ppermute(piece, 'hst', pairs)  6.9 us
    ppermute x6, waiting for transfers between devices, scatter_anchor(): send = lambda x, to: lax.ppermute(x, BOTH, [(0, to), (to, 0)])  5.52 us
    all_to_all x1, starting transfers between devices, per_device(): lax.all_to_all(parts, 'hst', split_axis=0, concat_axis=0, tiled=True)  5.1 us
  transfers between devices with their start and end apart: 25, of which 9 were waited for; matrix products, arithmetic and copies ran while one was open for 8% of the time, Pallas kernels for 30%

profile of v17, /device:TPU:0, one launch (start us, length us, event | category | flops | bytes accessed | tf_op | source)
XLA Modules:
  0.0 118.1 jit_solution(17318589154162182000)
XLA Ops:
  0.6 3.9 %pack_heads.1 = (bf16[4,2,512,384]{3,2,1,0:T(8,128)(2,1)}, bf16[256,768]{1,0:T(8,128)(2,1)}, bf16[256,768]{1,0:T(8,128)(2,1)}, bf16[256,768]{1,0:T(8,128)(2,1)},...) custom-call(bf16[2,512,1536]{2,1,0:T(8,128)(2,1)} %kv_ref.9), custom_call_target="tpu_custom_call" | custom-call | bytes 9437184 | tf_op jit(solution)/shard_map/pack_heads/pallas_call | solution.py:66
  4.5 4.9 %collective-permute-start.2 = (bf16[256,768]{1,0:T(8,128)(2,1)}, bf16[256,768]{1,0:T(8,128)(2,1)}, u32[]{:S(2)}, u32[]{:S(2)}) collective-permute-start(bf16[256,768]{1,0:T(8,128)(2,1)} %get-tuple-element.25), channel_id=1, source_target_pairs={{0,4},{4,0}} | collective-permute-start | bytes 1179656 | tf_op jit(solution)/shard_map/ppermute | solution.py:287
  9.4 2.3 %collective-permute-start = (bf16[256,768]{1,0:T(8,128)(2,1)}, bf16[256,768]{1,0:T(8,128)(2,1)}, u32[]{:S(2)}, u32[]{:S(2)}) collective-permute-start(bf16[256,768]{1,0:T(8,128)(2,1)} %get-tuple-element.23), channel_id=1, source_target_pairs={{0,6},{6,0}} | collective-permute-start | bytes 1179656 | tf_op jit(solution)/shard_map/ppermute | solution.py:287
  11.7 1.9 %collective-permute-start.1 = (bf16[256,768]{1,0:T(8,128)(2,1)}, bf16[256,768]{1,0:T(8,128)(2,1)}, u32[]{:S(2)}, u32[]{:S(2)}) collective-permute-start(bf16[256,768]{1,0:T(8,128)(2,1)} %get-tuple-element.24), channel_id=1, source_target_pairs={{0,2},{2,0}} | collective-permute-start | bytes 1179656 | tf_op jit(solution)/shard_map/ppermute | solution.py:287
  13.7 1.9 %collective-permute-start.8 = (bf16[256,768]{1,0:T(8,128)(2,1)}, bf16[256,768]{1,0:T(8,128)(2,1)S(1)}, u32[]{:S(2)}, u32[]{:S(2)}) collective-permute-start(bf16[256,768]{1,0:T(8,128)(2,1)} %get-tuple-element.28), channel_id=1, source_target_pairs={{0,4},{4,0}} | collective-permute-start | bytes 1179656 | tf_op jit(solution)/shard_map/ppermute | solution.py:287
  15.6 2.7 %collective-permute-start.6 = (bf16[256,768]{1,0:T(8,128)(2,1)}, bf16[256,768]{1,0:T(8,128)(2,1)}, u32[]{:S(2)}, u32[]{:S(2)}) collective-permute-start(bf16[256,768]{1,0:T(8,128)(2,1)} %get-tuple-element.26), channel_id=1, source_target_pairs={{0,6},{6,0}} | collective-permute-start | bytes 1179656 | tf_op jit(solution)/shard_map/ppermute | solution.py:287
  18.3 1.9 %collective-permute-start.7 = (bf16[256,768]{1,0:T(8,128)(2,1)}, bf16[256,768]{1,0:T(8,128)(2,1)}, u32[]{:S(2)}, u32[]{:S(2)}) collective-permute-start(bf16[256,768]{1,0:T(8,128)(2,1)} %get-tuple-element.27), channel_id=1, source_target_pairs={{0,2},{2,0}} | collective-permute-start | bytes 1179656 | tf_op jit(solution)/shard_map/ppermute | solution.py:287
  20.2 3.7 %all-to-all-start = ((bf16[4,2,512,384]{3,2,1,0:T(8,128)(2,1)}), bf16[4,2,512,384]{3,2,1,0:T(8,128)(2,1)S(1)}, u32[]{:S(2)}, u32[]{:S(2)}) async-start(bf16[4,2,512,384]{3,2,1,0:T(8,128)(2,1)} %get-tuple-element.31), calls=%async_computation | async-start | bytes 6291456 | tf_op jit(solution)/shard_map/all_to_all | solution.py:324
  23.9 1.5 %broadcast_compare_fusion = pred[16384]{0:T(1024)(128)(4,1)} fusion(s32[16384]{0:T(1024)} %param.8), kind=kLoop, calls=%fused_computation.11 | loop fusion | flops 16384 | bytes 81920 | tf_op jit(solution)/shard_map/ge | solution.py:328
  25.4 0.8 ge.11
  26.2 1.4 %bitcast_select_fusion.1 = bf16[256,768]{1,0:T(8,128)(2,1)S(1)} fusion(bf16[256,768]{1,0:T(8,128)(2,1)} %collective-permute-done.2, bf16[256,768]{1,0:T(8,128)(2,1)} %collective-permute-done, bf16[256,768]{1,0:T(8,128)(2,1)} %collective-permute-done.1, bf16[2,512,1536]{2,1,0:T(8,128)(2,1)} %kv_ref.9, pred[]{:T(512)S(6)} %and.18), kind=kLoop, calls=%fused_computation.3 | loop fusion | flops 589824 | bytes 1966081 | tf_op jit(solution)/shard_map/jit(_where)/select_n | solution.py:297
  27.7 0.9 collective-permute-done.8
  28.6 1.6 %collective-permute-start.3 = (bf16[256,384]{1,0:T(8,128)(2,1)S(1)}, bf16[256,384]{1,0:T(8,128)(2,1)S(1)}, u32[]{:S(2)}, u32[]{:S(2)}) collective-permute-start(bf16[256,384]{1,0:T(8,128)(2,1)S(1)} %slice.25), channel_id=1, source_target_pairs={{0,1},{2,3},{4,5},{6,7},{8,9},{10,11},{12,13},{14,15},{16,17},{18,... | collective-permute-start | bytes 589832 | tf_op jit(solution)/shard_map/ppermute | solution.py:307
  30.2 4.6 %collective-permute-done.7 = bf16[256,768]{1,0:T(8,128)(2,1)} collective-permute-done((bf16[256,768]{1,0:T(8,128)(2,1)}, bf16[256,768]{1,0:T(8,128)(2,1)}, u32[]{:S(2)}, u32[]{:S(2)}) %collective-permute-start.7) | collective-permute-done | bytes 393248 | tf_op jit(solution)/shard_map/ppermute | solution.py:287
  34.8 1.3 %bitcast_select_fusion = bf16[256,768]{1,0:T(8,128)(2,1)S(1)} fusion(bf16[256,768]{1,0:T(8,128)(2,1)S(1)} %collective-permute-done.8, bf16[256,768]{1,0:T(8,128)(2,1)} %collective-permute-done.6, bf16[256,768]{1,0:T(8,128)(2,1)} %collective-permute-done.7, bf16[2,512,1536]{2,1,0:T(8,128)(2,1)} %kv_ref.9, pred[]{:T(512)S(6)} %and.18), kind=kLoop, calls=%fused_computation.2 | loop fusion | flops 589824 | bytes 1966081 | tf_op jit(solution)/shard_map/jit(_where)/select_n | solution.py:297
  36.1 1.3 %collective-permute-start.9 = (bf16[256,384]{1,0:T(8,128)(2,1)S(1)}, bf16[256,384]{1,0:T(8,128)(2,1)S(1)}, u32[]{:S(2)}, u32[]{:S(2)}) collective-permute-start(bf16[256,384]{1,0:T(8,128)(2,1)S(1)} %slice.27), channel_id=1, source_target_pairs={{0,1},{2,3},{4,5},{6,7},{8,9},{10,11},{12,13},{14,15},{16,17},{18,... | collective-permute-start | bytes 589832 | tf_op jit(solution)/shard_map/ppermute | solution.py:307
  37.5 1.3 %collective-permute-start.4 = (bf16[256,384]{1,0:T(8,128)(2,1)S(1)}, bf16[256,384]{1,0:T(8,128)(2,1)S(1)}, u32[]{:S(2)}, u32[]{:S(2)}) collective-permute-start(bf16[256,384]{1,0:T(8,128)(2,1)S(1)} %slice_add_fusion.1), channel_id=1, source_target_pairs={{0,16},{4,20},{1,17},{5,21},{2,18},{6,22},{3,19},{7,23}} | collective-permute-start | bytes 589832 | tf_op jit(solution)/shard_map/ppermute | solution.py:312
  39.0 3.4 %collective-permute-start.14 = (bf16[128,384]{1,0:T(8,128)(2,1)S(1)}, bf16[128,384]{1,0:T(8,128)(2,1)S(1)}, u32[]{:S(2)}, u32[]{:S(2)}) collective-permute-start(bf16[128,384]{1,0:T(8,128)(2,1)S(1)} %copy-done.7), channel_id=1, source_target_pairs={{0,8},{4,12},{8,0},{12,4},{16,24},{20,28},{24,16},{28,20},{1,9},{5... | collective-permute-start | bytes 294920 | tf_op jit(solution)/shard_map/ppermute | solution.py:272
  42.4 2.9 %collective-permute-start.10 = (bf16[256,384]{1,0:T(8,128)(2,1)S(1)}, bf16[256,384]{1,0:T(8,128)(2,1)S(1)}, u32[]{:S(2)}, u32[]{:S(2)}) collective-permute-start(bf16[256,384]{1,0:T(8,128)(2,1)S(1)} %slice_add_fusion), channel_id=1, source_target_pairs={{0,16},{4,20},{1,17},{5,21},{2,18},{6,22},{3,19},{7,23}} | collective-permute-start | bytes 589832 | tf_op jit(solution)/shard_map/ppermute | solution.py:312
  45.3 1.3 %collective-permute-start.5 = (bf16[256,384]{1,0:T(8,128)(2,1)S(1)}, bf16[256,384]{1,0:T(8,128)(2,1)S(1)}, u32[]{:S(2)}, u32[]{:S(2)}) collective-permute-start(bf16[256,384]{1,0:T(8,128)(2,1)S(1)} %add.48), channel_id=1, source_target_pairs={{0,8},{4,12},{16,24},{20,28},{1,9},{5,13},{17,25},{21,29},{2,10},{... | collective-permute-start | bytes 589832 | tf_op jit(solution)/shard_map/ppermute | solution.py:312
  46.8 0.8 collective-permute-done.15
  47.6 0.6 collective-permute-done.16
  48.2 2.1 %collective-permute-done.14 = bf16[128,384]{1,0:T(8,128)(2,1)S(1)} collective-permute-done((bf16[128,384]{1,0:T(8,128)(2,1)S(1)}, bf16[128,384]{1,0:T(8,128)(2,1)S(1)}, u32[]{:S(2)}, u32[]{:S(2)}) %collective-permute-start.14) | collective-permute-done | bytes 98336 | tf_op jit(solution)/shard_map/ppermute | solution.py:272
  50.3 0.8 pad_maximum_fusion.1.near_ref
  51.1 3.0 %collective-permute-done.10 = bf16[256,384]{1,0:T(8,128)(2,1)S(1)} collective-permute-done((bf16[256,384]{1,0:T(8,128)(2,1)S(1)}, bf16[256,384]{1,0:T(8,128)(2,1)S(1)}, u32[]{:S(2)}, u32[]{:S(2)}) %collective-permute-start.10) | collective-permute-done | bytes 196640 | tf_op jit(solution)/shard_map/ppermute | solution.py:312
  54.2 1.4 %collective-permute-start.11 = (bf16[256,384]{1,0:T(8,128)(2,1)S(1)}, bf16[256,384]{1,0:T(8,128)(2,1)S(1)}, u32[]{:S(2)}, u32[]{:S(2)}) collective-permute-start(bf16[256,384]{1,0:T(8,128)(2,1)S(1)} %add.53), channel_id=1, source_target_pairs={{0,8},{4,12},{16,24},{20,28},{1,9},{5,13},{17,25},{21,29},{2,10},{... | collective-permute-start | bytes 589832 | tf_op jit(solution)/shard_map/ppermute | solution.py:312
  55.6 2.8 %collective-permute-done.5 = bf16[256,384]{1,0:T(8,128)(2,1)S(1)} collective-permute-done((bf16[256,384]{1,0:T(8,128)(2,1)S(1)}, bf16[256,384]{1,0:T(8,128)(2,1)S(1)}, u32[]{:S(2)}, u32[]{:S(2)}) %collective-permute-start.5) | collective-permute-done | bytes 196640 | tf_op jit(solution)/shard_map/ppermute | solution.py:312
  58.4 2.0 %collective-permute-done.11 = bf16[256,384]{1,0:T(8,128)(2,1)S(1)} collective-permute-done((bf16[256,384]{1,0:T(8,128)(2,1)S(1)}, bf16[256,384]{1,0:T(8,128)(2,1)S(1)}, u32[]{:S(2)}, u32[]{:S(2)}) %collective-permute-start.11) | collective-permute-done | bytes 196640 | tf_op jit(solution)/shard_map/ppermute | solution.py:312
  60.5 0.8 pad_maximum_fusion.near_ref
  61.6 2.1 %all-to-all-done.kv_ref = bf16[4,2,512,384]{3,2,1,0:T(8,128)(2,1)S(1)} async-done(((bf16[4,2,512,384]{3,2,1,0:T(8,128)(2,1)}), bf16[4,2,512,384]{3,2,1,0:T(8,128)(2,1)S(1)}, u32[]{:S(2)}, u32[]{:S(2)}) %all-to-all-start) | async-done | bytes 3145760 | tf_op jit(solution)/shard_map/all_to_all | solution.py:324
  63.7 2.4 %collective-permute-start.13 = (bf16[2,256,384]{2,1,0:T(8,128)(2,1)}, bf16[2,256,384]{2,1,0:T(8,128)(2,1)S(1)}, u32[]{:S(2)}, u32[]{:S(2)}) collective-permute-start(bf16[2,256,384]{2,1,0:T(8,128)(2,1)} %pad_maximum_fusion.near_ref), channel_id=1, source_target_pairs={{0,2},{1,3},{2,0},{3,1},{4,6},{5,7},{6,4},{7,5},{8,10},{9,11},{10,... | collective-permute-start | bytes 1179656 | tf_op jit(solution)/shard_map/ppermute | solution.py:272
  66.1 8.9 %suffix_attend.2.rest_0_ = f32[8,136,384]{2,1,0:T(8,128)S(1)} custom-call(s32[1]{0:T(128)} %bitcast.7.at_ref, bf16[4,128,384]{2,1,0:T(8,128)(2,1)} %pad_maximum_fusion.1.near_ref, bf16[4,128,384]{2,1,0:T(8,128)(2,1)} %collective-permute-done.17.far_ref, bf16[4,2,512,384]{3,2,1,0:T(8,128)(2,1)S(1)} %all-to-all-done.kv_ref, ...), custom_call_target="tpu_custom_call" | custom-call | flops 4563402752 | bytes 5242880 | tf_op jit(solution)/shard_map/suffix_attend/pallas_call | solution.py:144
  75.1 5.0 %suffix_attend.3 = f32[8,136,384]{2,1,0:T(8,128)S(1)} custom-call(s32[1]{0:T(128)} %bitcast.7.at_ref, bf16[4,128,384]{2,1,0:T(8,128)(2,1)} %pad_maximum_fusion.1.near_ref, bf16[4,128,384]{2,1,0:T(8,128)(2,1)} %collective-permute-done.17.far_ref, bf16[4,2,512,384]{3,2,1,0:T(8,128)(2,1)S(1)} %all-to-all-done.kv_ref, ...), custom_call_target="tpu_custom_call", output_to_operand_aliasing={{}: (6, {})} | custom-call | flops 2281701376 | bytes 2621440 | tf_op jit(solution)/shard_map/suffix_attend/pallas_call | solution.py:144
  80.1 1.0 convert_element_type.6
  81.1 5.1 %all-to-all-start.1 = ((f16[8,136,384]{2,1,0:T(8,128)(2,1)}), f16[8,136,384]{2,1,0:T(8,128)(2,1)S(1)}, u32[]{:S(2)}, u32[]{:S(2)}) async-start(f16[8,136,384]{2,1,0:T(8,128)(2,1)} %convert_element_type.6), calls=%async_computation.1 | async-start | bytes 1671168 | tf_op jit(solution)/shard_map/all_to_all | solution.py:341
  86.2 1.7 %collective-permute-start.18 = (bf16[2,256,384]{2,1,0:T(8,128)(2,1)}, bf16[2,256,384]{2,1,0:T(8,128)(2,1)S(1)}, u32[]{:S(2)}, u32[]{:S(2)}) collective-permute-start(bf16[2,256,384]{2,1,0:T(8,128)(2,1)} %collective-permute-done.12.far_ref), channel_id=1, source_target_pairs={{0,2},{1,3},{2,0},{3,1},{4,6},{5,7},{6,4},{7,5},{8,10},{9,11},{10,... | collective-permute-start | bytes 1179656 | tf_op jit(solution)/shard_map/ppermute | solution.py:272
  88.0 0.7 add_add_fusion.2.at_ref
  88.6 0.6 add_add_fusion.1.at_ref
  89.3 5.3 %context_attend.4.rest_0_ = bf16[512,1536]{1,0:T(8,128)(2,1)} custom-call(s32[3]{0:T(128)} %add_add_fusion.2.at_ref, s32[32]{0:T(128)} %len_ref.7, bf16[512,1536]{1,0:T(8,128)(2,1)} %q_ref.7, bf16[2,512,1536]{2,1,0:T(8,128)(2,1)} %kv_ref.9, f32[32,512]{1,0:T(8,128)} %copy-done, bf16[2,256,384]{2,1,0:T(8,128)(2,1)} %pad_maximum_fusion.near_ref, ...), custom_call_target="tpu_custom_call" | custom-call | flops 805306368 | bytes 2359296 | tf_op jit(solution)/shard_map/context_attend/pallas_call | solution.py:243
  94.6 5.4 %context_attend.5.rest_0_ = bf16[512,1536]{1,0:T(8,128)(2,1)} custom-call(s32[3]{0:T(128)} %add_add_fusion.1.at_ref, s32[32]{0:T(128)} %len_ref.7, bf16[512,1536]{1,0:T(8,128)(2,1)} %q_ref.7, bf16[2,512,1536]{2,1,0:T(8,128)(2,1)} %kv_ref.9, f32[32,512]{1,0:T(8,128)} %copy-done, ...), custom_call_target="tpu_custom_call", output_to_operand_aliasing={{}: (7, {})} | custom-call | flops 805306368 | bytes 2359296 | tf_op jit(solution)/shard_map/context_attend/pallas_call | solution.py:243
  100.6 0.7 add_add_fusion.3.at_ref
  101.2 0.6 add_add_fusion.at_ref
  101.9 5.3 %context_attend.6.rest_0_ = bf16[512,1536]{1,0:T(8,128)(2,1)} custom-call(s32[3]{0:T(128)} %add_add_fusion.3.at_ref, s32[32]{0:T(128)} %len_ref.7, bf16[512,1536]{1,0:T(8,128)(2,1)} %q_ref.7, bf16[2,512,1536]{2,1,0:T(8,128)(2,1)} %kv_ref.9, f32[32,512]{1,0:T(8,128)} %copy-done, bf16[2,256,384]{2,1,0:T(8,128)(2,1)} %copy-done.2, ...), custom_call_target="tpu_custom_call", output_to_operand_aliasing={{}: (7, {})} | custom-call | flops 805306368 | bytes 2359296 | tf_op jit(solution)/shard_map/context_attend/pallas_call | solution.py:243
  107.2 0.8 copy-done.5
  108.0 0.7 copy-done.6
  108.7 5.3 %context_attend.7 = bf16[512,1536]{1,0:T(8,128)(2,1)} custom-call(s32[3]{0:T(128)} %add_add_fusion.at_ref, s32[32]{0:T(128)} %len_ref.7, bf16[512,1536]{1,0:T(8,128)(2,1)} %q_ref.7, bf16[2,512,1536]{2,1,0:T(8,128)(2,1)} %kv_ref.9, f32[32,512]{1,0:T(8,128)} %copy-done, bf16[2,256,384]{2,1,0:T(8,128)(2,1)} %copy-done.5, ...), custom_call_target="tpu_custom_call", output_to_operand_aliasing={{}: (7, {})} | custom-call | flops 805306368 | bytes 2359296 | tf_op jit(solution)/shard_map/context_attend/pallas_call | solution.py:243
  114.0 1.3 %convert_element_type.7.in_ref = f32[8,136,384]{2,1,0:T(8,128)} convert(f16[8,136,384]{2,1,0:T(8,128)(2,1)S(1)} %all-to-all-done.1) | non-fusion elementwise | flops 417792 | bytes 2506752 | tf_op jit(solution)/shard_map/convert_element_type | solution.py:357
  115.3 2.7 %combine_groups.1 = bf16[128,384]{1,0:T(8,128)(2,1)} custom-call(f32[8,136,384]{2,1,0:T(8,128)} %convert_element_type.7.in_ref), custom_call_target="tpu_custom_call" | custom-call | flops 835584 | bytes 1671168 | tf_op jit(solution)/shard_map/combine_groups/pallas_call | solution.py:188
  (49 shorter events, 1.5 us)
Async XLA Ops:
  4.5 13.8 %collective-permute-start.2 = (bf16[256,768]{1,0:T(8,128)(2,1)}, bf16[256,768]{1,0:T(8,128)(2,1)}, u32[]{:S(2)}, u32[]{:S(2)}) collective-permute-start(bf16[256,768]{1,0:T(8,128)(2,1)} %get-tuple-element.25), channel_id=1, source_target_pairs={{0,4},{4,0}} | collective-permute-start | bytes 1179656 | tf_op jit(solution)/shard_map/ppermute | solution.py:287
  9.4 16.8 %collective-permute-start = (bf16[256,768]{1,0:T(8,128)(2,1)}, bf16[256,768]{1,0:T(8,128)(2,1)}, u32[]{:S(2)}, u32[]{:S(2)}) collective-permute-start(bf16[256,768]{1,0:T(8,128)(2,1)} %get-tuple-element.23), channel_id=1, source_target_pairs={{0,6},{6,0}} | collective-permute-start | bytes 1179656 | tf_op jit(solution)/shard_map/ppermute | solution.py:287
  11.7 14.4 %collective-permute-start.1 = (bf16[256,768]{1,0:T(8,128)(2,1)}, bf16[256,768]{1,0:T(8,128)(2,1)}, u32[]{:S(2)}, u32[]{:S(2)}) collective-permute-start(bf16[256,768]{1,0:T(8,128)(2,1)} %get-tuple-element.24), channel_id=1, source_target_pairs={{0,2},{2,0}} | collective-permute-start | bytes 1179656 | tf_op jit(solution)/shard_map/ppermute | solution.py:287
  13.7 14.9 %collective-permute-start.8 = (bf16[256,768]{1,0:T(8,128)(2,1)}, bf16[256,768]{1,0:T(8,128)(2,1)S(1)}, u32[]{:S(2)}, u32[]{:S(2)}) collective-permute-start(bf16[256,768]{1,0:T(8,128)(2,1)} %get-tuple-element.28), channel_id=1, source_target_pairs={{0,4},{4,0}} | collective-permute-start | bytes 1179656 | tf_op jit(solution)/shard_map/ppermute | solution.py:287
  15.6 14.6 %collective-permute-start.6 = (bf16[256,768]{1,0:T(8,128)(2,1)}, bf16[256,768]{1,0:T(8,128)(2,1)}, u32[]{:S(2)}, u32[]{:S(2)}) collective-permute-start(bf16[256,768]{1,0:T(8,128)(2,1)} %get-tuple-element.26), channel_id=1, source_target_pairs={{0,6},{6,0}} | collective-permute-start | bytes 1179656 | tf_op jit(solution)/shard_map/ppermute | solution.py:287
  18.3 16.5 %collective-permute-start.7 = (bf16[256,768]{1,0:T(8,128)(2,1)}, bf16[256,768]{1,0:T(8,128)(2,1)}, u32[]{:S(2)}, u32[]{:S(2)}) collective-permute-start(bf16[256,768]{1,0:T(8,128)(2,1)} %get-tuple-element.27), channel_id=1, source_target_pairs={{0,2},{2,0}} | collective-permute-start | bytes 1179656 | tf_op jit(solution)/shard_map/ppermute | solution.py:287
  20.2 43.5 %all-to-all-start = ((bf16[4,2,512,384]{3,2,1,0:T(8,128)(2,1)}), bf16[4,2,512,384]{3,2,1,0:T(8,128)(2,1)S(1)}, u32[]{:S(2)}, u32[]{:S(2)}) async-start(bf16[4,2,512,384]{3,2,1,0:T(8,128)(2,1)} %get-tuple-element.31), calls=%async_computation | async-start | bytes 6291456 | tf_op jit(solution)/shard_map/all_to_all | solution.py:324
  27.6 11.2 %copy-start.7 = (bf16[128,384]{1,0:T(8,128)(2,1)S(1)}, bf16[128,384]{1,0:T(8,128)(2,1)}, u32[]{:S(2)}) copy-start(bf16[128,384]{1,0:T(8,128)(2,1)} %param.10) | copy-start | bytes 294916
  27.6 19.0 %copy-start.8 = (s32[32]{0:T(128)S(1)}, s32[32]{0:T(128)}, u32[]{:S(2)}) copy-start(s32[32]{0:T(128)} %len_ref.7) | copy-start | bytes 388
  28.6 8.8 %collective-permute-start.3 = (bf16[256,384]{1,0:T(8,128)(2,1)S(1)}, bf16[256,384]{1,0:T(8,128)(2,1)S(1)}, u32[]{:S(2)}, u32[]{:S(2)}) collective-permute-start(bf16[256,384]{1,0:T(8,128)(2,1)S(1)} %slice.25), channel_id=1, source_target_pairs={{0,1},{2,3},{4,5},{6,7},{8,9},{10,11},{12,13},{14,15},{16,17},{18,... | collective-permute-start | bytes 589832 | tf_op jit(solution)/shard_map/ppermute | solution.py:307
  36.1 2.7 %collective-permute-start.9 = (bf16[256,384]{1,0:T(8,128)(2,1)S(1)}, bf16[256,384]{1,0:T(8,128)(2,1)S(1)}, u32[]{:S(2)}, u32[]{:S(2)}) collective-permute-start(bf16[256,384]{1,0:T(8,128)(2,1)S(1)} %slice.27), channel_id=1, source_target_pairs={{0,1},{2,3},{4,5},{6,7},{8,9},{10,11},{12,13},{14,15},{16,17},{18,... | collective-permute-start | bytes 589832 | tf_op jit(solution)/shard_map/ppermute | solution.py:307
  37.5 7.8 %collective-permute-start.4 = (bf16[256,384]{1,0:T(8,128)(2,1)S(1)}, bf16[256,384]{1,0:T(8,128)(2,1)S(1)}, u32[]{:S(2)}, u32[]{:S(2)}) collective-permute-start(bf16[256,384]{1,0:T(8,128)(2,1)S(1)} %slice_add_fusion.1), channel_id=1, source_target_pairs={{0,16},{4,20},{1,17},{5,21},{2,18},{6,22},{3,19},{7,23}} | collective-permute-start | bytes 589832 | tf_op jit(solution)/shard_map/ppermute | solution.py:312
  38.8 8.8 %collective-permute-start.15 = (bf16[128,384]{1,0:T(8,128)(2,1)S(1)}, bf16[128,384]{1,0:T(8,128)(2,1)S(1)}, u32[]{:S(2)}, u32[]{:S(2)}) collective-permute-start(bf16[128,384]{1,0:T(8,128)(2,1)S(1)} %copy-done.7), channel_id=1, source_target_pairs={{0,16},{4,20},{8,24},{12,28},{16,0},{20,4},{24,8},{28,12},{1,17},{... | collective-permute-start | bytes 294920 | tf_op jit(solution)/shard_map/ppermute | solution.py:272
  38.9 9.3 %collective-permute-start.16 = (bf16[128,384]{1,0:T(8,128)(2,1)S(1)}, bf16[128,384]{1,0:T(8,128)(2,1)S(1)}, u32[]{:S(2)}, u32[]{:S(2)}) collective-permute-start(bf16[128,384]{1,0:T(8,128)(2,1)S(1)} %copy-done.7), channel_id=1, source_target_pairs={{0,24},{4,28},{8,16},{12,20},{16,8},{20,12},{24,0},{28,4},{1,25},{... | collective-permute-start | bytes 294920 | tf_op jit(solution)/shard_map/ppermute | solution.py:272
  39.0 11.3 %collective-permute-start.14 = (bf16[128,384]{1,0:T(8,128)(2,1)S(1)}, bf16[128,384]{1,0:T(8,128)(2,1)S(1)}, u32[]{:S(2)}, u32[]{:S(2)}) collective-permute-start(bf16[128,384]{1,0:T(8,128)(2,1)S(1)} %copy-done.7), channel_id=1, source_target_pairs={{0,8},{4,12},{8,0},{12,4},{16,24},{20,28},{24,16},{28,20},{1,9},{5... | collective-permute-start | bytes 294920 | tf_op jit(solution)/shard_map/ppermute | solution.py:272
  42.4 11.7 %collective-permute-start.10 = (bf16[256,384]{1,0:T(8,128)(2,1)S(1)}, bf16[256,384]{1,0:T(8,128)(2,1)S(1)}, u32[]{:S(2)}, u32[]{:S(2)}) collective-permute-start(bf16[256,384]{1,0:T(8,128)(2,1)S(1)} %slice_add_fusion), channel_id=1, source_target_pairs={{0,16},{4,20},{1,17},{5,21},{2,18},{6,22},{3,19},{7,23}} | collective-permute-start | bytes 589832 | tf_op jit(solution)/shard_map/ppermute | solution.py:312
  45.3 13.0 %collective-permute-start.5 = (bf16[256,384]{1,0:T(8,128)(2,1)S(1)}, bf16[256,384]{1,0:T(8,128)(2,1)S(1)}, u32[]{:S(2)}, u32[]{:S(2)}) collective-permute-start(bf16[256,384]{1,0:T(8,128)(2,1)S(1)} %add.48), channel_id=1, source_target_pairs={{0,8},{4,12},{16,24},{20,28},{1,9},{5,13},{17,25},{21,29},{2,10},{... | collective-permute-start | bytes 589832 | tf_op jit(solution)/shard_map/ppermute | solution.py:312
  46.7 28.3 %copy-start = (f32[32,512]{1,0:T(8,128)}, f32[32,512]{1,0:T(8,128)S(1)}, u32[]{:S(2)}) copy-start(f32[32,512]{1,0:T(8,128)S(1)} %fusion.1.bias_ref) | copy-start | bytes 196612
  50.3 15.7 %copy-start.1 = (bf16[2,128,384]{2,1,0:T(8,128)(2,1)S(1)}, bf16[2,128,384]{2,1,0:T(8,128)(2,1)}, u32[]{:S(2)}) copy-start(bf16[2,128,384]{2,1,0:T(8,128)(2,1)} %sk_ref.3) | copy-start | bytes 589828
  51.1 14.9 %collective-permute-start.17 = (bf16[4,128,384]{2,1,0:T(8,128)(2,1)}, bf16[4,128,384]{2,1,0:T(8,128)(2,1)}, u32[]{:S(2)}, u32[]{:S(2)}) collective-permute-start(bf16[4,128,384]{2,1,0:T(8,128)(2,1)} %pad_maximum_fusion.1.near_ref), channel_id=1, source_target_pairs={{0,4},{4,0},{8,12},{12,8},{16,20},{20,16},{24,28},{28,24},{1,5},{5... | collective-permute-start | bytes 1179656 | tf_op jit(solution)/shard_map/ppermute | solution.py:272
  54.2 6.3 %collective-permute-start.11 = (bf16[256,384]{1,0:T(8,128)(2,1)S(1)}, bf16[256,384]{1,0:T(8,128)(2,1)S(1)}, u32[]{:S(2)}, u32[]{:S(2)}) collective-permute-start(bf16[256,384]{1,0:T(8,128)(2,1)S(1)} %add.53), channel_id=1, source_target_pairs={{0,8},{4,12},{16,24},{20,28},{1,9},{5,13},{17,25},{21,29},{2,10},{... | collective-permute-start | bytes 589832 | tf_op jit(solution)/shard_map/ppermute | solution.py:312
  61.3 13.7 %collective-permute-start.12 = (bf16[2,256,384]{2,1,0:T(8,128)(2,1)}, bf16[2,256,384]{2,1,0:T(8,128)(2,1)}, u32[]{:S(2)}, u32[]{:S(2)}) collective-permute-start(bf16[2,256,384]{2,1,0:T(8,128)(2,1)} %pad_maximum_fusion.near_ref), channel_id=1, source_target_pairs={{0,4},{4,0},{8,12},{12,8},{16,20},{20,16},{24,28},{28,24},{1,5},{5... | collective-permute-start | bytes 1179656 | tf_op jit(solution)/shard_map/ppermute | solution.py:272
  61.6 18.5 %collective-permute-start.19 = (bf16[2,256,384]{2,1,0:T(8,128)(2,1)}, bf16[2,256,384]{2,1,0:T(8,128)(2,1)}, u32[]{:S(2)}, u32[]{:S(2)}) collective-permute-start(bf16[2,256,384]{2,1,0:T(8,128)(2,1)} %pad_maximum_fusion.near_ref), channel_id=1, source_target_pairs={{0,1},{1,0},{2,3},{3,2},{4,5},{5,4},{6,7},{7,6},{8,9},{9,8},{10,11... | collective-permute-start | bytes 1179656 | tf_op jit(solution)/shard_map/ppermute | solution.py:272
  63.7 11.3 %collective-permute-start.13 = (bf16[2,256,384]{2,1,0:T(8,128)(2,1)}, bf16[2,256,384]{2,1,0:T(8,128)(2,1)S(1)}, u32[]{:S(2)}, u32[]{:S(2)}) collective-permute-start(bf16[2,256,384]{2,1,0:T(8,128)(2,1)} %pad_maximum_fusion.near_ref), channel_id=1, source_target_pairs={{0,2},{1,3},{2,0},{3,1},{4,6},{5,7},{6,4},{7,5},{8,10},{9,11},{10,... | collective-permute-start | bytes 1179656 | tf_op jit(solution)/shard_map/ppermute | solution.py:272
  75.0 5.1 %copy-start.2 = (bf16[2,256,384]{2,1,0:T(8,128)(2,1)}, bf16[2,256,384]{2,1,0:T(8,128)(2,1)S(1)}, u32[]{:S(2)}) copy-start(bf16[2,256,384]{2,1,0:T(8,128)(2,1)S(1)} %collective-permute-done.13.near_ref) | copy-start | bytes 1179652
  75.0 5.1 %collective-permute-start.20 = (bf16[2,256,384]{2,1,0:T(8,128)(2,1)}, bf16[2,256,384]{2,1,0:T(8,128)(2,1)}, u32[]{:S(2)}, u32[]{:S(2)}) collective-permute-start(bf16[2,256,384]{2,1,0:T(8,128)(2,1)} %collective-permute-done.12.far_ref), channel_id=1, source_target_pairs={{0,1},{1,0},{2,3},{3,2},{4,5},{5,4},{6,7},{7,6},{8,9},{9,8},{10,11... | collective-permute-start | bytes 1179656 | tf_op jit(solution)/shard_map/ppermute | solution.py:272
  81.1 32.9 %all-to-all-start.1 = ((f16[8,136,384]{2,1,0:T(8,128)(2,1)}), f16[8,136,384]{2,1,0:T(8,128)(2,1)S(1)}, u32[]{:S(2)}, u32[]{:S(2)}) async-start(f16[8,136,384]{2,1,0:T(8,128)(2,1)} %convert_element_type.6), calls=%async_computation.1 | async-start | bytes 1671168 | tf_op jit(solution)/shard_map/all_to_all | solution.py:341
  86.2 13.8 %collective-permute-start.18 = (bf16[2,256,384]{2,1,0:T(8,128)(2,1)}, bf16[2,256,384]{2,1,0:T(8,128)(2,1)S(1)}, u32[]{:S(2)}, u32[]{:S(2)}) collective-permute-start(bf16[2,256,384]{2,1,0:T(8,128)(2,1)} %collective-permute-done.12.far_ref), channel_id=1, source_target_pairs={{0,2},{1,3},{2,0},{3,1},{4,6},{5,7},{6,4},{7,5},{8,10},{9,11},{10,... | collective-permute-start | bytes 1179656 | tf_op jit(solution)/shard_map/ppermute | solution.py:272
  94.6 5.4 %copy-start.3 = (bf16[2,256,384]{2,1,0:T(8,128)(2,1)S(1)}, bf16[2,256,384]{2,1,0:T(8,128)(2,1)}, u32[]{:S(2)}) copy-start(bf16[2,256,384]{2,1,0:T(8,128)(2,1)} %copy-done.2) | copy-start | bytes 1179652
  100.0 1.9 %copy-start.4 = (bf16[2,256,384]{2,1,0:T(8,128)(2,1)}, bf16[2,256,384]{2,1,0:T(8,128)(2,1)S(1)}, u32[]{:S(2)}) copy-start(bf16[2,256,384]{2,1,0:T(8,128)(2,1)S(1)} %collective-permute-done.18.far_ref) | copy-start | bytes 1179652
  100.0 7.2 %collective-permute-start.21 = (bf16[2,256,384]{2,1,0:T(8,128)(2,1)S(1)}, bf16[2,256,384]{2,1,0:T(8,128)(2,1)S(1)}, u32[]{:S(2)}, u32[]{:S(2)}) collective-permute-start(bf16[2,256,384]{2,1,0:T(8,128)(2,1)S(1)} %copy-done.3), channel_id=1, source_target_pairs={{0,1},{1,0},{2,3},{3,2},{4,5},{5,4},{6,7},{7,6},{8,9},{9,8},{10,11... | collective-permute-start | bytes 1179656 | tf_op jit(solution)/shard_map/ppermute | solution.py:272
  100.1 7.1 %collective-permute-start.22 = (bf16[2,256,384]{2,1,0:T(8,128)(2,1)S(1)}, bf16[2,256,384]{2,1,0:T(8,128)(2,1)S(1)}, u32[]{:S(2)}, u32[]{:S(2)}) collective-permute-start(bf16[2,256,384]{2,1,0:T(8,128)(2,1)S(1)} %collective-permute-done.18.far_ref), channel_id=1, source_target_pairs={{0,1},{1,0},{2,3},{3,2},{4,5},{5,4},{6,7},{7,6},{8,9},{9,8},{10,11... | collective-permute-start | bytes 1179656 | tf_op jit(solution)/shard_map/ppermute | solution.py:272
  107.2 0.8 copy-start.5
  108.0 0.7 copy-start.6

commit v18 on v16

--- a/solution.py
+++ b/solution.py
@@ -336,8 +336,8 @@
     by_core = [[swap(x, "grp", k) for x in (near, far)] for k in range(1, cores)]
     if heads > early:
         parts = suffix(early, heads - early, parts)
-    by_core, parts = lax.optimization_barrier((by_core, parts))
     parts = parts.astype(jnp.float16)
+    by_core = after(by_core, parts)
     coded = lax.all_to_all(parts, "hst", split_axis=0, concat_axis=0, tiled=True)
     held = {0: after([near, far], parts), cores: [other_near, other_far]}
 

time: 117 us -> 116 us (level)
    unnamed x22 -> x18, local copies, waits for them, and re-layouts: 3.6 us -> 2.86 us
  transfers between devices with their start and end apart: 25 -> 25, of which waited for: 9 -> 9; matrix products, arithmetic and copies ran while one was open for 7% -> 7% of each run, Pallas kernels for 29% -> 25%
where the time goes in v18:
time: 116 us; the launch traced here: 115 us
  starting transfers between devices  42.7 us (37%)
  Pallas kernels  40.6 us (35%)
  waiting for transfers between devices  16.7 us (14%)
  other arithmetic  9.7 us (8%)
  local copies, waits for them, and re-layouts  4.25 us (4%)
    pallas_call x4, Pallas kernels, context_attend(): pl.pallas_call(context_kernel, grid_spec=pltpu.PrefetchScalarGridSpec(num...  19.3 us
    ppermute x6, starting transfers between devices, scatter_anchor(): send = lambda x, to: lax.ppermute(x, BOTH, [(0, to), (to, 0)])  15.6 us
    pallas_call x2, Pallas kernels, suffix_attend(): pl.pallas_call(suffix_kernel, grid_spec=pltpu.PrefetchScalarGridSpec(num_...  14.7 us
    ppermute x4, waiting for transfers between devices, spread_anchor(): piece = piece + lax.ppermute(piece, 'hst', pairs)  8.21 us
    ppermute x11, starting transfers between devices, swap(): lax.ppermute(x, axis, [(i, i ^ k) for i in range(lax.axis_size(axis))])  7.16 us
    ppermute x4, starting transfers between devices, spread_anchor(): piece = piece + lax.ppermute(piece, 'hst', pairs)  6.79 us
    all_to_all x1, starting transfers between devices, per_device(): lax.all_to_all(after(packed, down), 'grp', split_axis=0, concat_axis=0, t...  4.92 us
    all_to_all x1, starting transfers between devices, per_device(): lax.all_to_all(parts, 'hst', split_axis=0, concat_axis=0, tiled=True)  4.39 us
  transfers between devices with their start and end apart: 25, of which 9 were waited for; matrix products, arithmetic and copies ran while one was open for 7% of the time, Pallas kernels for 25%

profile of v18, /device:TPU:0, one launch (start us, length us, event | category | flops | bytes accessed | tf_op | source)
XLA Modules:
  0.0 114.9 jit_solution(16161587505771130468)
XLA Ops:
  0.6 3.9 %pack_heads.1 = (bf16[4,2,512,384]{3,2,1,0:T(8,128)(2,1)}, bf16[256,768]{1,0:T(8,128)(2,1)}, bf16[256,768]{1,0:T(8,128)(2,1)}, bf16[256,768]{1,0:T(8,128)(2,1)},...) custom-call(bf16[2,512,1536]{2,1,0:T(8,128)(2,1)} %kv_ref.9), custom_call_target="tpu_custom_call" | custom-call | bytes 9437184 | tf_op jit(solution)/shard_map/pack_heads/pallas_call | solution.py:66
  4.5 4.9 %collective-permute-start.2 = (bf16[256,768]{1,0:T(8,128)(2,1)}, bf16[256,768]{1,0:T(8,128)(2,1)S(1)}, u32[]{:S(2)}, u32[]{:S(2)}) collective-permute-start(bf16[256,768]{1,0:T(8,128)(2,1)} %get-tuple-element.24), channel_id=1, source_target_pairs={{0,4},{4,0}} | collective-permute-start | bytes 1179656 | tf_op jit(solution)/shard_map/ppermute | solution.py:287
  9.4 1.9 %collective-permute-start = (bf16[256,768]{1,0:T(8,128)(2,1)}, bf16[256,768]{1,0:T(8,128)(2,1)}, u32[]{:S(2)}, u32[]{:S(2)}) collective-permute-start(bf16[256,768]{1,0:T(8,128)(2,1)} %get-tuple-element.22), channel_id=1, source_target_pairs={{0,6},{6,0}} | collective-permute-start | bytes 1179656 | tf_op jit(solution)/shard_map/ppermute | solution.py:287
  11.3 1.9 %collective-permute-start.1 = (bf16[256,768]{1,0:T(8,128)(2,1)}, bf16[256,768]{1,0:T(8,128)(2,1)}, u32[]{:S(2)}, u32[]{:S(2)}) collective-permute-start(bf16[256,768]{1,0:T(8,128)(2,1)} %get-tuple-element.23), channel_id=1, source_target_pairs={{0,2},{2,0}} | collective-permute-start | bytes 1179656 | tf_op jit(solution)/shard_map/ppermute | solution.py:287
  13.3 1.9 %collective-permute-start.8 = (bf16[256,768]{1,0:T(8,128)(2,1)}, bf16[256,768]{1,0:T(8,128)(2,1)S(1)}, u32[]{:S(2)}, u32[]{:S(2)}) collective-permute-start(bf16[256,768]{1,0:T(8,128)(2,1)} %get-tuple-element.27), channel_id=1, source_target_pairs={{0,4},{4,0}} | collective-permute-start | bytes 1179656 | tf_op jit(solution)/shard_map/ppermute | solution.py:287
  15.2 3.1 %collective-permute-start.6 = (bf16[256,768]{1,0:T(8,128)(2,1)}, bf16[256,768]{1,0:T(8,128)(2,1)}, u32[]{:S(2)}, u32[]{:S(2)}) collective-permute-start(bf16[256,768]{1,0:T(8,128)(2,1)} %get-tuple-element.25), channel_id=1, source_target_pairs={{0,6},{6,0}} | collective-permute-start | bytes 1179656 | tf_op jit(solution)/shard_map/ppermute | solution.py:287
  18.3 1.9 %collective-permute-start.7 = (bf16[256,768]{1,0:T(8,128)(2,1)}, bf16[256,768]{1,0:T(8,128)(2,1)}, u32[]{:S(2)}, u32[]{:S(2)}) collective-permute-start(bf16[256,768]{1,0:T(8,128)(2,1)} %get-tuple-element.26), channel_id=1, source_target_pairs={{0,2},{2,0}} | collective-permute-start | bytes 1179656 | tf_op jit(solution)/shard_map/ppermute | solution.py:287
  20.2 4.9 %all-to-all-start = ((bf16[4,2,512,384]{3,2,1,0:T(8,128)(2,1)}), bf16[4,2,512,384]{3,2,1,0:T(8,128)(2,1)}, u32[]{:S(2)}, u32[]{:S(2)}) async-start(bf16[4,2,512,384]{3,2,1,0:T(8,128)(2,1)} %get-tuple-element.30), calls=%async_computation | async-start | bytes 6291456 | tf_op jit(solution)/shard_map/all_to_all | solution.py:324
  25.1 1.5 %broadcast_compare_fusion = pred[16384]{0:T(1024)(128)(4,1)} fusion(s32[16384]{0:T(1024)} %param.8), kind=kLoop, calls=%fused_computation.11 | loop fusion | flops 16384 | bytes 81920 | tf_op jit(solution)/shard_map/ge | solution.py:328
  26.6 1.3 %ge.11 = pred[32,512]{1,0:T(8,128)(4,1)} reshape(pred[16384]{0:T(1024)(128)(4,1)} %broadcast_compare_fusion) | data formatting | bytes 32768 | tf_op jit(solution)/shard_map/ge | solution.py:328
  28.0 1.3 %bitcast_select_fusion.1 = bf16[256,768]{1,0:T(8,128)(2,1)S(1)} fusion(bf16[256,768]{1,0:T(8,128)(2,1)} %copy-done.6, bf16[256,768]{1,0:T(8,128)(2,1)} %collective-permute-done, bf16[256,768]{1,0:T(8,128)(2,1)} %collective-permute-done.1, bf16[2,512,1536]{2,1,0:T(8,128)(2,1)S(1)} %copy-done, pred[]{:T(512)S(6)} %and.18), kind=kLoop, calls=%fused_computation.3 | loop fusion | flops 589824 | bytes 1966081 | tf_op jit(solution)/shard_map/jit(_where)/select_n | solution.py:297
  29.4 2.5 %collective-permute-start.3 = (bf16[256,384]{1,0:T(8,128)(2,1)S(1)}, bf16[256,384]{1,0:T(8,128)(2,1)S(1)}, u32[]{:S(2)}, u32[]{:S(2)}) collective-permute-start(bf16[256,384]{1,0:T(8,128)(2,1)S(1)} %slice.25), channel_id=1, source_target_pairs={{0,1},{2,3},{4,5},{6,7},{8,9},{10,11},{12,13},{14,15},{16,17},{18,... | collective-permute-start | bytes 589832 | tf_op jit(solution)/shard_map/ppermute | solution.py:307
  31.9 0.8 collective-permute-done.7
  32.7 1.2 %bitcast_select_fusion = bf16[256,768]{1,0:T(8,128)(2,1)S(1)} fusion(bf16[256,768]{1,0:T(8,128)(2,1)S(1)} %collective-permute-done.8, bf16[256,768]{1,0:T(8,128)(2,1)} %collective-permute-done.6, bf16[256,768]{1,0:T(8,128)(2,1)} %collective-permute-done.7, bf16[2,512,1536]{2,1,0:T(8,128)(2,1)S(1)} %copy-done, pred[]{:T(512)S(6)} %and.18), kind=kLoop, calls=%fused_computation.2 | loop fusion | flops 589824 | bytes 1966081 | tf_op jit(solution)/shard_map/jit(_where)/select_n | solution.py:297
  34.0 1.3 %collective-permute-start.9 = (bf16[256,384]{1,0:T(8,128)(2,1)S(1)}, bf16[256,384]{1,0:T(8,128)(2,1)S(1)}, u32[]{:S(2)}, u32[]{:S(2)}) collective-permute-start(bf16[256,384]{1,0:T(8,128)(2,1)S(1)} %slice.27), channel_id=1, source_target_pairs={{0,1},{2,3},{4,5},{6,7},{8,9},{10,11},{12,13},{14,15},{16,17},{18,... | collective-permute-start | bytes 589832 | tf_op jit(solution)/shard_map/ppermute | solution.py:307
  35.3 1.3 %collective-permute-start.4 = (bf16[256,384]{1,0:T(8,128)(2,1)S(1)}, bf16[256,384]{1,0:T(8,128)(2,1)S(1)}, u32[]{:S(2)}, u32[]{:S(2)}) collective-permute-start(bf16[256,384]{1,0:T(8,128)(2,1)S(1)} %slice_add_fusion.1), channel_id=1, source_target_pairs={{0,16},{4,20},{1,17},{5,21},{2,18},{6,22},{3,19},{7,23}} | collective-permute-start | bytes 589832 | tf_op jit(solution)/shard_map/ppermute | solution.py:312
  36.8 3.4 %collective-permute-start.14 = (bf16[128,384]{1,0:T(8,128)(2,1)S(1)}, bf16[128,384]{1,0:T(8,128)(2,1)S(1)}, u32[]{:S(2)}, u32[]{:S(2)}) collective-permute-start(bf16[128,384]{1,0:T(8,128)(2,1)S(1)} %copy-done.7), channel_id=1, source_target_pairs={{0,8},{4,12},{8,0},{12,4},{16,24},{20,28},{24,16},{28,20},{1,9},{5... | collective-permute-start | bytes 294920 | tf_op jit(solution)/shard_map/ppermute | solution.py:272
  40.2 2.9 %collective-permute-start.10 = (bf16[256,384]{1,0:T(8,128)(2,1)S(1)}, bf16[256,384]{1,0:T(8,128)(2,1)S(1)}, u32[]{:S(2)}, u32[]{:S(2)}) collective-permute-start(bf16[256,384]{1,0:T(8,128)(2,1)S(1)} %slice_add_fusion), channel_id=1, source_target_pairs={{0,16},{4,20},{1,17},{5,21},{2,18},{6,22},{3,19},{7,23}} | collective-permute-start | bytes 589832 | tf_op jit(solution)/shard_map/ppermute | solution.py:312
  43.2 1.3 %collective-permute-start.5 = (bf16[256,384]{1,0:T(8,128)(2,1)S(1)}, bf16[256,384]{1,0:T(8,128)(2,1)S(1)}, u32[]{:S(2)}, u32[]{:S(2)}) collective-permute-start(bf16[256,384]{1,0:T(8,128)(2,1)S(1)} %add.48), channel_id=1, source_target_pairs={{0,8},{4,12},{16,24},{20,28},{1,9},{5,13},{17,25},{21,29},{2,10},{... | collective-permute-start | bytes 589832 | tf_op jit(solution)/shard_map/ppermute | solution.py:312
  44.5 0.1 fusion.1.bias_ref
  44.6 0.8 collective-permute-done.15
  45.5 0.8 collective-permute-done.16
  46.2 2.1 %collective-permute-done.14 = bf16[128,384]{1,0:T(8,128)(2,1)S(1)} collective-permute-done((bf16[128,384]{1,0:T(8,128)(2,1)S(1)}, bf16[128,384]{1,0:T(8,128)(2,1)S(1)}, u32[]{:S(2)}, u32[]{:S(2)}) %collective-permute-start.14) | collective-permute-done | bytes 98336 | tf_op jit(solution)/shard_map/ppermute | solution.py:272
  48.3 0.8 pad_maximum_fusion.1.near_ref
  49.1 3.4 %collective-permute-done.10 = bf16[256,384]{1,0:T(8,128)(2,1)S(1)} collective-permute-done((bf16[256,384]{1,0:T(8,128)(2,1)S(1)}, bf16[256,384]{1,0:T(8,128)(2,1)S(1)}, u32[]{:S(2)}, u32[]{:S(2)}) %collective-permute-start.10) | collective-permute-done | bytes 196640 | tf_op jit(solution)/shard_map/ppermute | solution.py:312
  52.6 1.3 %collective-permute-start.11 = (bf16[256,384]{1,0:T(8,128)(2,1)S(1)}, bf16[256,384]{1,0:T(8,128)(2,1)S(1)}, u32[]{:S(2)}, u32[]{:S(2)}) collective-permute-start(bf16[256,384]{1,0:T(8,128)(2,1)S(1)} %add.53), channel_id=1, source_target_pairs={{0,8},{4,12},{16,24},{20,28},{1,9},{5,13},{17,25},{21,29},{2,10},{... | collective-permute-start | bytes 589832 | tf_op jit(solution)/shard_map/ppermute | solution.py:312
  53.9 2.7 %collective-permute-done.5 = bf16[256,384]{1,0:T(8,128)(2,1)S(1)} collective-permute-done((bf16[256,384]{1,0:T(8,128)(2,1)S(1)}, bf16[256,384]{1,0:T(8,128)(2,1)S(1)}, u32[]{:S(2)}, u32[]{:S(2)}) %collective-permute-start.5) | collective-permute-done | bytes 196640 | tf_op jit(solution)/shard_map/ppermute | solution.py:312
  56.7 2.1 %collective-permute-done.11 = bf16[256,384]{1,0:T(8,128)(2,1)S(1)} collective-permute-done((bf16[256,384]{1,0:T(8,128)(2,1)S(1)}, bf16[256,384]{1,0:T(8,128)(2,1)S(1)}, u32[]{:S(2)}, u32[]{:S(2)}) %collective-permute-start.11) | collective-permute-done | bytes 196640 | tf_op jit(solution)/shard_map/ppermute | solution.py:312
  58.8 0.8 pad_maximum_fusion.near_ref
  59.6 3.7 %all-to-all-done.kv_ref = bf16[4,2,512,384]{3,2,1,0:T(8,128)(2,1)} async-done(((bf16[4,2,512,384]{3,2,1,0:T(8,128)(2,1)}), bf16[4,2,512,384]{3,2,1,0:T(8,128)(2,1)}, u32[]{:S(2)}, u32[]{:S(2)}) %all-to-all-start) | async-done | bytes 3145760 | tf_op jit(solution)/shard_map/all_to_all | solution.py:324
  63.3 2.5 %collective-permute-start.13 = (bf16[2,256,384]{2,1,0:T(8,128)(2,1)}, bf16[2,256,384]{2,1,0:T(8,128)(2,1)}, u32[]{:S(2)}, u32[]{:S(2)}) collective-permute-start(bf16[2,256,384]{2,1,0:T(8,128)(2,1)} %pad_maximum_fusion.near_ref), channel_id=1, source_target_pairs={{0,2},{1,3},{2,0},{3,1},{4,6},{5,7},{6,4},{7,5},{8,10},{9,11},{10,... | collective-permute-start | bytes 1179656 | tf_op jit(solution)/shard_map/ppermute | solution.py:272
  65.8 9.3 %suffix_attend.2.rest_0_ = f32[8,136,384]{2,1,0:T(8,128)S(1)} custom-call(s32[1]{0:T(128)} %bitcast.7.at_ref, bf16[4,128,384]{2,1,0:T(8,128)(2,1)} %pad_maximum_fusion.1.near_ref, bf16[4,128,384]{2,1,0:T(8,128)(2,1)} %collective-permute-done.17.far_ref, bf16[4,2,512,384]{3,2,1,0:T(8,128)(2,1)} %all-to-all-done.kv_ref, bf16[2,128,384]{2,1,0:T(8,128)(2,1)S(1)} %copy-done.5, ...), custom_call_target="tpu_custom_call" | custom-call | flops 4563402752 | bytes 5242880 | tf_op jit(solution)/shard_map/suffix_attend/pallas_call | solution.py:144
  75.2 5.4 %suffix_attend.3 = f32[8,136,384]{2,1,0:T(8,128)S(1)} custom-call(s32[1]{0:T(128)} %bitcast.7.at_ref, bf16[4,128,384]{2,1,0:T(8,128)(2,1)} %pad_maximum_fusion.1.near_ref, bf16[4,128,384]{2,1,0:T(8,128)(2,1)} %collective-permute-done.17.far_ref, bf16[4,2,512,384]{3,2,1,0:T(8,128)(2,1)} %all-to-all-done.kv_ref, ...), custom_call_target="tpu_custom_call", output_to_operand_aliasing={{}: (6, {})} | custom-call | flops 2281701376 | bytes 2621440 | tf_op jit(solution)/shard_map/suffix_attend/pallas_call | solution.py:144
  80.5 1.0 convert_element_type.6
  81.6 4.4 %all-to-all-start.1 = ((f16[8,136,384]{2,1,0:T(8,128)(2,1)}), f16[8,136,384]{2,1,0:T(8,128)(2,1)}, u32[]{:S(2)}, u32[]{:S(2)}) async-start(f16[8,136,384]{2,1,0:T(8,128)(2,1)} %convert_element_type.6), calls=%async_computation.1 | async-start | bytes 1671168 | tf_op jit(solution)/shard_map/all_to_all | solution.py:341
  86.1 0.5 collective-permute-start.20
  86.6 0.1 add_add_fusion.2.at_ref
  86.6 0.1 add_add_fusion.1.at_ref
  86.7 1.4 %copy-done.1 = bf16[512,1536]{1,0:T(8,128)(2,1)S(1)} copy-done((bf16[512,1536]{1,0:T(8,128)(2,1)S(1)}, bf16[512,1536]{1,0:T(8,128)(2,1)}, u32[]{:S(2)}) %copy-start.1) | copy-done | bytes 1572888
  88.1 4.8 %context_attend.4.rest_0_ = bf16[512,1536]{1,0:T(8,128)(2,1)} custom-call(s32[3]{0:T(128)S(1)} %add_add_fusion.2.at_ref, s32[32]{0:T(128)S(1)} %copy-done.4, bf16[512,1536]{1,0:T(8,128)(2,1)S(1)} %copy-done.1, bf16[2,512,1536]{2,1,0:T(8,128)(2,1)S(1)} %copy-done, f32[32,512]{1,0:T(8,128)S(1)} %fusion.1.bias_ref, ...), custom_call_target="tpu_custom_call" | custom-call | flops 805306368 | bytes 2359296 | tf_op jit(solution)/shard_map/context_attend/pallas_call | solution.py:243
  93.0 4.8 %context_attend.5.rest_0_ = bf16[512,1536]{1,0:T(8,128)(2,1)} custom-call(s32[3]{0:T(128)S(1)} %add_add_fusion.1.at_ref, s32[32]{0:T(128)S(1)} %copy-done.4, bf16[512,1536]{1,0:T(8,128)(2,1)S(1)} %copy-done.2, bf16[2,512,1536]{2,1,0:T(8,128)(2,1)S(1)} %copy-done, f32[32,512]{1,0:T(8,128)S(1)} %fusion.1.bias_ref, ...), custom_call_target="tpu_custom_call", output_to_operand_aliasing={{}: (7, {})} | custom-call | flops 805306368 | bytes 2359296 | tf_op jit(solution)/shard_map/context_attend/pallas_call | solution.py:243
  97.8 0.2 collective-permute-done.18.far_ref
  98.0 0.5 collective-permute-start.22
  98.6 1.4 %copy-done.3 = bf16[512,1536]{1,0:T(8,128)(2,1)S(1)} copy-done((bf16[512,1536]{1,0:T(8,128)(2,1)S(1)}, bf16[512,1536]{1,0:T(8,128)(2,1)}, u32[]{:S(2)}) %copy-start.3) | copy-done | bytes 1572888
  100.0 4.8 %context_attend.6.rest_0_ = bf16[512,1536]{1,0:T(8,128)(2,1)} custom-call(s32[3]{0:T(128)S(1)} %add_add_fusion.3.at_ref, s32[32]{0:T(128)S(1)} %copy-done.4, bf16[512,1536]{1,0:T(8,128)(2,1)S(1)} %copy-done.3, bf16[2,512,1536]{2,1,0:T(8,128)(2,1)S(1)} %copy-done, f32[32,512]{1,0:T(8,128)S(1)} %fusion.1.bias_ref, ...), custom_call_target="tpu_custom_call", output_to_operand_aliasing={{}: (7, {})} | custom-call | flops 805306368 | bytes 2359296 | tf_op jit(solution)/shard_map/context_attend/pallas_call | solution.py:243
  104.9 4.8 %context_attend.7 = bf16[512,1536]{1,0:T(8,128)(2,1)} custom-call(s32[3]{0:T(128)S(1)} %add_add_fusion.at_ref, s32[32]{0:T(128)S(1)} %copy-done.4, bf16[512,1536]{1,0:T(8,128)(2,1)S(1)} %copy-done.3, bf16[2,512,1536]{2,1,0:T(8,128)(2,1)S(1)} %copy-done, f32[32,512]{1,0:T(8,128)S(1)} %fusion.1.bias_ref, ...), custom_call_target="tpu_custom_call", output_to_operand_aliasing={{}: (7, {})} | custom-call | flops 805306368 | bytes 2359296 | tf_op jit(solution)/shard_map/context_attend/pallas_call | solution.py:243
  109.7 2.5 %convert_element_type.7.in_ref = f32[8,136,384]{2,1,0:T(8,128)} convert(f16[8,136,384]{2,1,0:T(8,128)(2,1)} %all-to-all-done.1) | non-fusion elementwise | flops 417792 | bytes 2506752 | tf_op jit(solution)/shard_map/convert_element_type | solution.py:357
  112.2 2.7 %combine_groups.1 = bf16[128,384]{1,0:T(8,128)(2,1)} custom-call(f32[8,136,384]{2,1,0:T(8,128)} %convert_element_type.7.in_ref), custom_call_target="tpu_custom_call" | custom-call | flops 835584 | bytes 1671168 | tf_op jit(solution)/shard_map/combine_groups/pallas_call | solution.py:188
  (49 shorter events, 0.8 us)
Async XLA Ops:
  4.5 13.7 %collective-permute-start.2 = (bf16[256,768]{1,0:T(8,128)(2,1)}, bf16[256,768]{1,0:T(8,128)(2,1)S(1)}, u32[]{:S(2)}, u32[]{:S(2)}) collective-permute-start(bf16[256,768]{1,0:T(8,128)(2,1)} %get-tuple-element.24), channel_id=1, source_target_pairs={{0,4},{4,0}} | collective-permute-start | bytes 1179656 | tf_op jit(solution)/shard_map/ppermute | solution.py:287
  9.4 18.6 %collective-permute-start = (bf16[256,768]{1,0:T(8,128)(2,1)}, bf16[256,768]{1,0:T(8,128)(2,1)}, u32[]{:S(2)}, u32[]{:S(2)}) collective-permute-start(bf16[256,768]{1,0:T(8,128)(2,1)} %get-tuple-element.22), channel_id=1, source_target_pairs={{0,6},{6,0}} | collective-permute-start | bytes 1179656 | tf_op jit(solution)/shard_map/ppermute | solution.py:287
  11.3 16.6 %collective-permute-start.1 = (bf16[256,768]{1,0:T(8,128)(2,1)}, bf16[256,768]{1,0:T(8,128)(2,1)}, u32[]{:S(2)}, u32[]{:S(2)}) collective-permute-start(bf16[256,768]{1,0:T(8,128)(2,1)} %get-tuple-element.23), channel_id=1, source_target_pairs={{0,2},{2,0}} | collective-permute-start | bytes 1179656 | tf_op jit(solution)/shard_map/ppermute | solution.py:287
  13.3 16.1 %collective-permute-start.8 = (bf16[256,768]{1,0:T(8,128)(2,1)}, bf16[256,768]{1,0:T(8,128)(2,1)S(1)}, u32[]{:S(2)}, u32[]{:S(2)}) collective-permute-start(bf16[256,768]{1,0:T(8,128)(2,1)} %get-tuple-element.27), channel_id=1, source_target_pairs={{0,4},{4,0}} | collective-permute-start | bytes 1179656 | tf_op jit(solution)/shard_map/ppermute | solution.py:287
  15.2 16.7 %collective-permute-start.6 = (bf16[256,768]{1,0:T(8,128)(2,1)}, bf16[256,768]{1,0:T(8,128)(2,1)}, u32[]{:S(2)}, u32[]{:S(2)}) collective-permute-start(bf16[256,768]{1,0:T(8,128)(2,1)} %get-tuple-element.25), channel_id=1, source_target_pairs={{0,6},{6,0}} | collective-permute-start | bytes 1179656 | tf_op jit(solution)/shard_map/ppermute | solution.py:287
  18.3 1.9 %copy-start.6 = (bf16[256,768]{1,0:T(8,128)(2,1)}, bf16[256,768]{1,0:T(8,128)(2,1)S(1)}, u32[]{:S(2)}) copy-start(bf16[256,768]{1,0:T(8,128)(2,1)S(1)} %collective-permute-done.2) | copy-start | bytes 1179652
  18.3 14.5 %collective-permute-start.7 = (bf16[256,768]{1,0:T(8,128)(2,1)}, bf16[256,768]{1,0:T(8,128)(2,1)}, u32[]{:S(2)}, u32[]{:S(2)}) collective-permute-start(bf16[256,768]{1,0:T(8,128)(2,1)} %get-tuple-element.26), channel_id=1, source_target_pairs={{0,2},{2,0}} | collective-permute-start | bytes 1179656 | tf_op jit(solution)/shard_map/ppermute | solution.py:287
  20.2 7.8 %copy-start = (bf16[2,512,1536]{2,1,0:T(8,128)(2,1)S(1)}, bf16[2,512,1536]{2,1,0:T(8,128)(2,1)}, u32[]{:S(2)}) copy-start(bf16[2,512,1536]{2,1,0:T(8,128)(2,1)} %kv_ref.9) | copy-start | bytes 9437188
  20.2 43.1 %all-to-all-start = ((bf16[4,2,512,384]{3,2,1,0:T(8,128)(2,1)}), bf16[4,2,512,384]{3,2,1,0:T(8,128)(2,1)}, u32[]{:S(2)}, u32[]{:S(2)}) async-start(bf16[4,2,512,384]{3,2,1,0:T(8,128)(2,1)} %get-tuple-element.30), calls=%async_computation | async-start | bytes 6291456 | tf_op jit(solution)/shard_map/all_to_all | solution.py:324
  29.3 7.4 %copy-start.7 = (bf16[128,384]{1,0:T(8,128)(2,1)S(1)}, bf16[128,384]{1,0:T(8,128)(2,1)}, u32[]{:S(2)}) copy-start(bf16[128,384]{1,0:T(8,128)(2,1)} %param.10) | copy-start | bytes 294916
  29.3 15.2 %copy-start.4 = (s32[32]{0:T(128)S(1)}, s32[32]{0:T(128)}, u32[]{:S(2)}) copy-start(s32[32]{0:T(128)} %len_ref.7) | copy-start | bytes 388
  29.3 15.2 %copy-start.8 = (pred[32,512]{1,0:T(8,128)(4,1)S(1)}, pred[32,512]{1,0:T(8,128)(4,1)}, u32[]{:S(2)}) copy-start(pred[32,512]{1,0:T(8,128)(4,1)} %ge.11) | copy-start | bytes 49156
  29.4 5.9 %collective-permute-start.3 = (bf16[256,384]{1,0:T(8,128)(2,1)S(1)}, bf16[256,384]{1,0:T(8,128)(2,1)S(1)}, u32[]{:S(2)}, u32[]{:S(2)}) collective-permute-start(bf16[256,384]{1,0:T(8,128)(2,1)S(1)} %slice.25), channel_id=1, source_target_pairs={{0,1},{2,3},{4,5},{6,7},{8,9},{10,11},{12,13},{14,15},{16,17},{18,... | collective-permute-start | bytes 589832 | tf_op jit(solution)/shard_map/ppermute | solution.py:307
  34.0 2.7 %collective-permute-start.9 = (bf16[256,384]{1,0:T(8,128)(2,1)S(1)}, bf16[256,384]{1,0:T(8,128)(2,1)S(1)}, u32[]{:S(2)}, u32[]{:S(2)}) collective-permute-start(bf16[256,384]{1,0:T(8,128)(2,1)S(1)} %slice.27), channel_id=1, source_target_pairs={{0,1},{2,3},{4,5},{6,7},{8,9},{10,11},{12,13},{14,15},{16,17},{18,... | collective-permute-start | bytes 589832 | tf_op jit(solution)/shard_map/ppermute | solution.py:307
  35.3 7.8 %collective-permute-start.4 = (bf16[256,384]{1,0:T(8,128)(2,1)S(1)}, bf16[256,384]{1,0:T(8,128)(2,1)S(1)}, u32[]{:S(2)}, u32[]{:S(2)}) collective-permute-start(bf16[256,384]{1,0:T(8,128)(2,1)S(1)} %slice_add_fusion.1), channel_id=1, source_target_pairs={{0,16},{4,20},{1,17},{5,21},{2,18},{6,22},{3,19},{7,23}} | collective-permute-start | bytes 589832 | tf_op jit(solution)/shard_map/ppermute | solution.py:312
  36.7 8.8 %collective-permute-start.15 = (bf16[128,384]{1,0:T(8,128)(2,1)S(1)}, bf16[128,384]{1,0:T(8,128)(2,1)S(1)}, u32[]{:S(2)}, u32[]{:S(2)}) collective-permute-start(bf16[128,384]{1,0:T(8,128)(2,1)S(1)} %copy-done.7), channel_id=1, source_target_pairs={{0,16},{4,20},{8,24},{12,28},{16,0},{20,4},{24,8},{28,12},{1,17},{... | collective-permute-start | bytes 294920 | tf_op jit(solution)/shard_map/ppermute | solution.py:272
  36.8 9.5 %collective-permute-start.16 = (bf16[128,384]{1,0:T(8,128)(2,1)S(1)}, bf16[128,384]{1,0:T(8,128)(2,1)S(1)}, u32[]{:S(2)}, u32[]{:S(2)}) collective-permute-start(bf16[128,384]{1,0:T(8,128)(2,1)S(1)} %copy-done.7), channel_id=1, source_target_pairs={{0,24},{4,28},{8,16},{12,20},{16,8},{20,12},{24,0},{28,4},{1,25},{... | collective-permute-start | bytes 294920 | tf_op jit(solution)/shard_map/ppermute | solution.py:272
  36.8 11.5 %collective-permute-start.14 = (bf16[128,384]{1,0:T(8,128)(2,1)S(1)}, bf16[128,384]{1,0:T(8,128)(2,1)S(1)}, u32[]{:S(2)}, u32[]{:S(2)}) collective-permute-start(bf16[128,384]{1,0:T(8,128)(2,1)S(1)} %copy-done.7), channel_id=1, source_target_pairs={{0,8},{4,12},{8,0},{12,4},{16,24},{20,28},{24,16},{28,20},{1,9},{5... | collective-permute-start | bytes 294920 | tf_op jit(solution)/shard_map/ppermute | solution.py:272
  40.2 12.3 %collective-permute-start.10 = (bf16[256,384]{1,0:T(8,128)(2,1)S(1)}, bf16[256,384]{1,0:T(8,128)(2,1)S(1)}, u32[]{:S(2)}, u32[]{:S(2)}) collective-permute-start(bf16[256,384]{1,0:T(8,128)(2,1)S(1)} %slice_add_fusion), channel_id=1, source_target_pairs={{0,16},{4,20},{1,17},{5,21},{2,18},{6,22},{3,19},{7,23}} | collective-permute-start | bytes 589832 | tf_op jit(solution)/shard_map/ppermute | solution.py:312
  43.2 13.4 %collective-permute-start.5 = (bf16[256,384]{1,0:T(8,128)(2,1)S(1)}, bf16[256,384]{1,0:T(8,128)(2,1)S(1)}, u32[]{:S(2)}, u32[]{:S(2)}) collective-permute-start(bf16[256,384]{1,0:T(8,128)(2,1)S(1)} %add.48), channel_id=1, source_target_pairs={{0,8},{4,12},{16,24},{20,28},{1,9},{5,13},{17,25},{21,29},{2,10},{... | collective-permute-start | bytes 589832 | tf_op jit(solution)/shard_map/ppermute | solution.py:312
  48.3 17.5 %copy-start.5 = (bf16[2,128,384]{2,1,0:T(8,128)(2,1)S(1)}, bf16[2,128,384]{2,1,0:T(8,128)(2,1)}, u32[]{:S(2)}) copy-start(bf16[2,128,384]{2,1,0:T(8,128)(2,1)} %sk_ref.3) | copy-start | bytes 589828
  49.1 16.7 %collective-permute-start.17 = (bf16[4,128,384]{2,1,0:T(8,128)(2,1)}, bf16[4,128,384]{2,1,0:T(8,128)(2,1)}, u32[]{:S(2)}, u32[]{:S(2)}) collective-permute-start(bf16[4,128,384]{2,1,0:T(8,128)(2,1)} %pad_maximum_fusion.1.near_ref), channel_id=1, source_target_pairs={{0,4},{4,0},{8,12},{12,8},{16,20},{20,16},{24,28},{28,24},{1,5},{5... | collective-permute-start | bytes 1179656 | tf_op jit(solution)/shard_map/ppermute | solution.py:272
  52.6 6.1 %collective-permute-start.11 = (bf16[256,384]{1,0:T(8,128)(2,1)S(1)}, bf16[256,384]{1,0:T(8,128)(2,1)S(1)}, u32[]{:S(2)}, u32[]{:S(2)}) collective-permute-start(bf16[256,384]{1,0:T(8,128)(2,1)S(1)} %add.53), channel_id=1, source_target_pairs={{0,8},{4,12},{16,24},{20,28},{1,9},{5,13},{17,25},{21,29},{2,10},{... | collective-permute-start | bytes 589832 | tf_op jit(solution)/shard_map/ppermute | solution.py:312
  59.6 15.6 %collective-permute-start.12 = (bf16[2,256,384]{2,1,0:T(8,128)(2,1)}, bf16[2,256,384]{2,1,0:T(8,128)(2,1)}, u32[]{:S(2)}, u32[]{:S(2)}) collective-permute-start(bf16[2,256,384]{2,1,0:T(8,128)(2,1)} %pad_maximum_fusion.near_ref), channel_id=1, source_target_pairs={{0,4},{4,0},{8,12},{12,8},{16,20},{20,16},{24,28},{28,24},{1,5},{5... | collective-permute-start | bytes 1179656 | tf_op jit(solution)/shard_map/ppermute | solution.py:272
  63.3 11.8 %collective-permute-start.13 = (bf16[2,256,384]{2,1,0:T(8,128)(2,1)}, bf16[2,256,384]{2,1,0:T(8,128)(2,1)}, u32[]{:S(2)}, u32[]{:S(2)}) collective-permute-start(bf16[2,256,384]{2,1,0:T(8,128)(2,1)} %pad_maximum_fusion.near_ref), channel_id=1, source_target_pairs={{0,2},{1,3},{2,0},{3,1},{4,6},{5,7},{6,4},{7,5},{8,10},{9,11},{10,... | collective-permute-start | bytes 1179656 | tf_op jit(solution)/shard_map/ppermute | solution.py:272
  81.6 28.1 %all-to-all-start.1 = ((f16[8,136,384]{2,1,0:T(8,128)(2,1)}), f16[8,136,384]{2,1,0:T(8,128)(2,1)}, u32[]{:S(2)}, u32[]{:S(2)}) async-start(f16[8,136,384]{2,1,0:T(8,128)(2,1)} %convert_element_type.6), calls=%async_computation.1 | async-start | bytes 1671168 | tf_op jit(solution)/shard_map/all_to_all | solution.py:341
  86.0 7.0 %collective-permute-start.19 = (bf16[2,256,384]{2,1,0:T(8,128)(2,1)}, bf16[2,256,384]{2,1,0:T(8,128)(2,1)}, u32[]{:S(2)}, u32[]{:S(2)}) collective-permute-start(bf16[2,256,384]{2,1,0:T(8,128)(2,1)} %pad_maximum_fusion.near_ref), channel_id=1, source_target_pairs={{0,1},{1,0},{2,3},{3,2},{4,5},{5,4},{6,7},{7,6},{8,9},{9,8},{10,11... | collective-permute-start | bytes 1179656 | tf_op jit(solution)/shard_map/ppermute | solution.py:272
  86.1 6.9 %collective-permute-start.20 = (bf16[2,256,384]{2,1,0:T(8,128)(2,1)}, bf16[2,256,384]{2,1,0:T(8,128)(2,1)}, u32[]{:S(2)}, u32[]{:S(2)}) collective-permute-start(bf16[2,256,384]{2,1,0:T(8,128)(2,1)} %collective-permute-done.12.far_ref), channel_id=1, source_target_pairs={{0,1},{1,0},{2,3},{3,2},{4,5},{5,4},{6,7},{7,6},{8,9},{9,8},{10,11... | collective-permute-start | bytes 1179656 | tf_op jit(solution)/shard_map/ppermute | solution.py:272
  86.5 11.4 %collective-permute-start.18 = (bf16[2,256,384]{2,1,0:T(8,128)(2,1)}, bf16[2,256,384]{2,1,0:T(8,128)(2,1)}, u32[]{:S(2)}, u32[]{:S(2)}) collective-permute-start(bf16[2,256,384]{2,1,0:T(8,128)(2,1)} %collective-permute-done.12.far_ref), channel_id=1, source_target_pairs={{0,2},{1,3},{2,0},{3,1},{4,6},{5,7},{6,4},{7,5},{8,10},{9,11},{10,... | collective-permute-start | bytes 1179656 | tf_op jit(solution)/shard_map/ppermute | solution.py:272
  86.7 1.4 %copy-start.1 = (bf16[512,1536]{1,0:T(8,128)(2,1)S(1)}, bf16[512,1536]{1,0:T(8,128)(2,1)}, u32[]{:S(2)}) copy-start(bf16[512,1536]{1,0:T(8,128)(2,1)} %q_ref.7) | copy-start | bytes 4718596
  88.1 4.8 %copy-start.2 = (bf16[512,1536]{1,0:T(8,128)(2,1)S(1)}, bf16[512,1536]{1,0:T(8,128)(2,1)}, u32[]{:S(2)}) copy-start(bf16[512,1536]{1,0:T(8,128)(2,1)} %q_ref.7) | copy-start | bytes 4718596
  98.0 6.9 %collective-permute-start.21 = (bf16[2,256,384]{2,1,0:T(8,128)(2,1)}, bf16[2,256,384]{2,1,0:T(8,128)(2,1)}, u32[]{:S(2)}, u32[]{:S(2)}) collective-permute-start(bf16[2,256,384]{2,1,0:T(8,128)(2,1)} %collective-permute-done.13.near_ref), channel_id=1, source_target_pairs={{0,1},{1,0},{2,3},{3,2},{4,5},{5,4},{6,7},{7,6},{8,9},{9,8},{10,11... | collective-permute-start | bytes 1179656 | tf_op jit(solution)/shard_map/ppermute | solution.py:272
  98.0 6.9 %collective-permute-start.22 = (bf16[2,256,384]{2,1,0:T(8,128)(2,1)}, bf16[2,256,384]{2,1,0:T(8,128)(2,1)}, u32[]{:S(2)}, u32[]{:S(2)}) collective-permute-start(bf16[2,256,384]{2,1,0:T(8,128)(2,1)} %collective-permute-done.18.far_ref), channel_id=1, source_target_pairs={{0,1},{1,0},{2,3},{3,2},{4,5},{5,4},{6,7},{7,6},{8,9},{9,8},{10,11... | collective-permute-start | bytes 1179656 | tf_op jit(solution)/shard_map/ppermute | solution.py:272
  98.6 1.4 %copy-start.3 = (bf16[512,1536]{1,0:T(8,128)(2,1)S(1)}, bf16[512,1536]{1,0:T(8,128)(2,1)}, u32[]{:S(2)}) copy-start(bf16[512,1536]{1,0:T(8,128)(2,1)} %q_ref.7) | copy-start | bytes 4718596
